TPU v7x, 32 devices: a whole 2x2x4 slice. The times are simulated.
32 devices in a mesh: grp: 2 (over x), fsdp: 16 (over z, y, core).
Axes of the slice: x: 2, y: 2, z: 4, core: 2. Of those that a mesh axis runs over, the one named last changes fastest.
Arguments:
- token_states: bfloat16 [2, 48, 128, 4096], P('grp', 'fsdp'), may hold values from -250 to 250
- token_ids: int32 [2, 48, 128], P('grp', 'fsdp'), may hold values from 0 to 31999, as said below
- master: float32 [2, 4096, 1024], P('grp', 'fsdp'), may hold values from -0.09375 to 0.09375
- gain: float32 [4096], replicated, may hold values from 0.25 to 4.5
- cand_ids: int32 [48, 8], P('fsdp'), may hold values from 0 to 47, all different within a row
- slab_owner: int32 [48], replicated, may hold values from 0 to 15, as said below
Outputs:
- weights_out: float32 [2, 4096, 1024], P('grp', 'fsdp')
Inputs may be any that keep to these rules, and one draw needn't show every extreme that they name: `token_ids`: 0 marks padding, which only follows a sequence's tokens; every sequence has 16 or more tokens. `slab_owner`: each fsdp index owns exactly 3 slab rows; the passages of slot 1 on the device with that index are the rows it owns, in increasing order. `cand_ids`: the ids of one row differ, and every slab row is some query's candidate.
All inputs are finite; a program needn't handle non-finite values.
Results may differ from a plain program's by a relative error of at most 0.012.
The roundings to bfloat16 on the way count: a program that leaves them out, or rounds other values in their place, can miss the bound.
Values may be sent and summed in bfloat16 or wider, within the bound.
No kernel may reach another device: no remote copies, remote signals or barrier semaphores. Data moves between devices by JAX's collectives and lax.ppermute only.
A program may use at most 64 MiB of HBM per device.

v0:
```python
import jax
import jax.numpy as jnp
from jax import lax
from jax.sharding import PartitionSpec as P

sharpness = 20.0


def passed_along(shard, axis, by):
    size = lax.axis_size(axis)
    pairs = [(i, i + by) for i in range(size) if 0 <= i + by < size]
    return lax.ppermute(shard, axis, pairs)


def shards(token_states, token_ids, master, gain, cand_ids, slab_owner):
    trainer = lax.axis_index("grp") == 0
    devices_fsdp = lax.axis_size("fsdp")
    states = token_states[0]
    seq_dev, length, width = states.shape
    embedding = master.shape[2]
    shard_rows = master.shape[1]
    tokens_dev = seq_dev * length
    states_wide = states.astype(jnp.float32)
    mean_square = jnp.mean(states_wide * states_wide, axis=-1, keepdims=True)
    normed = (
        (states_wide * lax.rsqrt(mean_square + 1e-05) * gain)
        .astype(jnp.bfloat16)
        .reshape(tokens_dev, width)
    )
    weight_bf = master[0].astype(jnp.bfloat16)
    hidden = jnp.dot(
        normed,
        lax.all_gather(weight_bf, "fsdp", axis=0, tiled=True),
        preferred_element_type=jnp.float32,
    )
    copied = passed_along(weight_bf, "grp", 1)
    active = jnp.tanh(hidden).reshape(seq_dev, length, embedding)
    valid = (token_ids[0] != 0).astype(jnp.float32)
    counts = jnp.sum(valid, axis=1)
    pooled = jnp.sum(active * valid[:, :, None], axis=1) / counts[:, None]
    pooled_square = jnp.mean(pooled * pooled, axis=-1, keepdims=True)
    scale = lax.rsqrt(pooled_square + 1e-06)
    unit = pooled * scale
    stored = unit.astype(jnp.bfloat16)
    owners = jnp.arange(devices_fsdp, dtype=jnp.int32)
    onehot = (slab_owner[:, None] == owners[None, :]).astype(jnp.int32)
    ranks = jnp.sum((jnp.cumsum(onehot, axis=0) - onehot) * onehot, axis=1)
    places = slab_owner * seq_dev + ranks
    wanted = places[cand_ids]
    mine = passed_along(stored, "grp", -1)
    slab = lax.all_gather(mine, "fsdp", axis=0, tiled=True)
    chosen = slab[wanted]
    chosen_wide = chosen.astype(jnp.float32)
    logits = (
        sharpness
        / embedding
        * jnp.einsum("qe,qje->qj", unit, chosen_wide, precision=lax.Precision.HIGHEST)
    )
    exponent = jnp.exp(logits)
    probs = exponent / jnp.sum(exponent, axis=-1, keepdims=True)
    target = (jnp.arange(chosen.shape[1]) == 0).astype(jnp.float32)
    logit_grad = probs - target[None, :]
    unit_grad = (
        sharpness
        / embedding
        * jnp.einsum("qj,qje->qe", logit_grad, chosen_wide, precision=lax.Precision.HIGHEST)
    )
    inner = jnp.sum(pooled * unit_grad, axis=-1, keepdims=True)
    pooled_grad = scale * unit_grad - pooled * (scale * scale * scale) * inner / embedding
    delta = (
        (valid / counts[:, None])[:, :, None] * pooled_grad[:, None, :] * (1.0 - active * active)
    )
    delta = delta.astype(jnp.bfloat16).reshape(tokens_dev, embedding)

    def compute():
        return lax.dot_general(
            normed, delta, (((0,), (0,)), ((), ())), preferred_element_type=jnp.float32
        )

    shard = lax.psum_scatter(
        lax.cond(
            trainer,
            compute,
            lambda: jnp.zeros((lax.axis_size("fsdp") * shard_rows, embedding), jnp.float32),
        ),
        "fsdp",
        scatter_dimension=0,
        tiled=True,
    )
    row_square = jnp.mean(shard * shard, axis=1, keepdims=True)
    normalized = shard * lax.rsqrt(row_square + 1e-06)
    result = jnp.where(trainer, normalized, copied.astype(jnp.float32))
    return result[None]


def solution(mesh):
    placed = (
        P("grp", "fsdp", None, None),
        P("grp", "fsdp", None),
        P("grp", "fsdp", None),
        P(),
        P("fsdp", None),
        P(),
    )
    return jax.shard_map(
        shards, mesh=mesh, in_specs=placed, out_specs=P("grp", "fsdp", None), check_vma=False
    )
```

profile of v0, /device:TPU:0, one launch (start us, length us, event | category | flops | bytes accessed | tf_op | source)
XLA Modules:
  0.0 318.0 jit_solution(6757325037633358318)
XLA Ops:
  6.5 2.2 convert_element_type.70
  8.9 0.7 compare_convert_fusion
  9.6 0.7 compare_select_fusion.1
  10.3 0.7 fusion.13
  11.1 0.8 select_reduce_fusion
  12.0 0.7 multiply_add_fusion
  12.6 0.7 gather_fusion
  13.5 0.1 fusion.22
  13.7 0.7 multiply_reduce_fusion
  14.4 1.0 copy-done.1
  15.4 1.2 fusion.3
  16.6 70.6 %all-gather.4.cloned.1.call-done = bf16[1,4096,1024]{2,1,0:T(8,128)(2,1)} async-done(((bf16[1,256,1024]{2,1,0:T(8,128)(2,1)}), bf16[1,4096,1024]{2,1,0:T(8,128)(2,1)}) %all-gather.4.cloned.1.call-update) | async-done | bytes 8388624 | tf_op jit(solution)/shard_map/all_gather | solution.py:33
  87.2 5.8 %fusion.6 = f32[384,1024]{1,0:T(8,128)S(1)} fusion(bf16[384,4096]{1,0:T(8,128)(2,1)S(1)} %fusion.3, bf16[1,4096,1024]{2,1,0:T(8,128)(2,1)} %all-gather.4.cloned.1.call-done), kind=kOutput, calls=%fused_computation.12 | convolution fusion | flops 3221225472 | bytes 13107200 | tf_op jit(solution)/shard_map/dot_general | solution.py:31
  93.0 1.1 copy-done.2
  94.1 0.2 multiply_reduce_fusion.1
  94.3 0.2 multiply_reduce_fusion.3
  94.6 1.3 collective-permute-start
  95.9 4.2 %collective-permute-done = bf16[3,1024]{1,0:T(4,128)(2,1)S(1)} collective-permute-done((bf16[3,1024]{1,0:T(4,128)(2,1)S(1)}, bf16[3,1024]{1,0:T(4,128)(2,1)S(1)}, u32[]{:S(2)}, u32[]{:S(2)}) %collective-permute-start) | collective-permute-done | bytes 6176 | tf_op jit(solution)/shard_map/ppermute | solution.py:12
  100.2 19.0 %all-gather.1 = bf16[16,3,1024]{2,1,0:T(4,128)(2,1)S(1)} all-gather(bf16[1,3,1024]{2,1,0:T(4,128)(2,1)S(1)} %bitcast.65), channel_id=1, replica_groups=mesh['grp'=2,'fsdp'=16] {'fsdp'}, dimensions={0}, use_global_device_ids=true | all-gather | bytes 104448 | tf_op jit(solution)/shard_map/all_gather | solution.py:51
  119.3 0.6 gather_fusion.1
  119.9 0.2 fusion.9
  120.1 0.1 fusion.19
  120.3 0.2 fusion.11
  120.5 0.1 fusion.16
  120.7 2.6 fusion.5
  123.3 9.2 %conditional.1 = (f32[4096,1024]{1,0:T(8,128)}) conditional(s32[]{:T(128)} %convert_element_type.62, () %tuple.11, (bf16[384,4096]{1,0:T(8,128)(2,1)S(1)}, bf16[384,1024]{1,0:T(8,128)(2,1)}) %tuple.12), branch_computations={%region_8.9_spmd, %region_9.10_spmd} | conditional | flops 3221225472 | bytes 20709384 | solution.py:81
  123.3 9.2 %fusion.23 = f32[4096,1024]{1,0:T(8,128)} fusion(bf16[384,4096]{1,0:T(8,128)(2,1)S(1)} %get-tuple-element.12, bf16[384,1024]{1,0:T(8,128)(2,1)} %get-tuple-element.13), kind=kOutput, calls=%fused_computation.53 | convolution fusion | flops 3221225472 | bytes 20709376 | tf_op jit(solution)/shard_map/cond/branch_1_fun/dot_general | solution.py:76
  132.5 1.2 copy-done.3
  133.8 1.3 collective-permute-start.1
  135.1 172.2 %reduce-scatter.2.cloned.1.call-done = f32[256,1024]{1,0:T(8,128)} async-done(((f32[4096,1024]{1,0:T(8,128)}), f32[256,1024]{1,0:T(8,128)}) %reduce-scatter.2.cloned.1.call-update) | async-done | bytes 1048592 | tf_op jit(solution)/shard_map/reduce_scatter | solution.py:80
  307.4 1.4 multiply_reduce_fusion.2
  308.8 2.4 select_bitcast_fusion
  (33 shorter events, 0.9 us)
Async XLA Ops:
  6.5 7.0 %copy-start.5 = (s32[1,3,128]{2,0,1:T(1,128)S(1)}, s32[1,3,128]{2,0,1:T(1,128)}, u32[]{:S(2)}) copy-start(s32[1,3,128]{2,0,1:T(1,128)} %param.9) | copy-start | bytes 4612
  6.5 7.1 %copy-start = (bf16[1,3,128,4096]{3,2,1,0:T(8,128)(2,1)S(1)}, bf16[1,3,128,4096]{3,2,1,0:T(8,128)(2,1)}, u32[]{:S(2)}) copy-start(bf16[1,3,128,4096]{3,2,1,0:T(8,128)(2,1)} %param.8) | copy-start | bytes 9437188
  6.5 80.6 %all-gather.4.cloned.1.call-start = ((), (), s32[]{:S(2)}) async-start(), calls=%async_computation.2 | async-start | bytes 8912896 | tf_op jit(solution)/shard_map/all_gather | solution.py:33
  8.8 5.7 %copy-start.4 = (f32[4096]{0:T(1024)S(1)}, f32[4096]{0:T(1024)}, u32[]{:S(2)}) copy-start(f32[4096]{0:T(1024)} %param.11) | copy-start | bytes 49156
  8.8 298.6 %reduce-scatter.2.cloned.1.call-start = ((), (), s32[]{:S(2)}) async-start(), calls=%async_computation.1 | async-start | bytes 17825792 | tf_op jit(solution)/shard_map/reduce_scatter | solution.py:80
  13.5 1.9 copy-start.1
  93.0 1.2 copy-start.2
  94.6 5.5 %collective-permute-start = (bf16[3,1024]{1,0:T(4,128)(2,1)S(1)}, bf16[3,1024]{1,0:T(4,128)(2,1)S(1)}, u32[]{:S(2)}, u32[]{:S(2)}) collective-permute-start(bf16[3,1024]{1,0:T(4,128)(2,1)S(1)} %get-tuple-element.21), channel_id=1, source_target_pairs={{16,0},{17,1},{18,2},{19,3},{20,4},{21,5},{22,6},{23,7},{24,8},{25... | collective-permute-start | bytes 18440 | tf_op jit(solution)/shard_map/ppermute | solution.py:12
  132.5 1.2 copy-start.3
  133.8 175.0 %collective-permute-start.1 = (bf16[256,1024]{1,0:T(8,128)(2,1)S(1)}, bf16[256,1024]{1,0:T(8,128)(2,1)S(1)}, u32[]{:S(2)}, u32[]{:S(2)}) collective-permute-start(bf16[256,1024]{1,0:T(8,128)(2,1)S(1)} %convert_bitcast_fusion), channel_id=1, source_target_pairs={{0,16},{1,17},{2,18},{3,19},{4,20},{5,21},{6,22},{7,23},{8,24},{9,... | collective-permute-start | bytes 1572872 | tf_op jit(solution)/shard_map/ppermute | solution.py:12
Sparse Core Ops, SparseCore 0:
  9.5 77.5 all-gather.3
  132.7 174.6 reduce-scatter.1
where the time goes:
time: 318 us
  waiting for transfers between devices  247 us (78%)
  blocking collectives  19 us (6%)
  matrix products  15.4 us (5%)
  other arithmetic  15.3 us (5%)
  between operations  13.5 us (4%)
  local copies, waits for them, and re-layouts  4.98 us (2%)
    reduce_scatter x1, waiting for transfers between devices, shards(): lax.psum_scatter(lax.cond(trainer, compute, lambda: jnp.zeros((lax.axis_s...  172 us
    all_gather x1, waiting for transfers between devices, shards(): lax.all_gather(weight_bf, 'fsdp', axis=0, tiled=True)  70.6 us
    all_gather x1, blocking collectives, shards(): slab = lax.all_gather(mine, 'fsdp', axis=0, tiled=True)  19 us
    dot_general x1, matrix products, compute(): lax.dot_general(normed, delta, (((0,), (0,)), ((), ())), preferred_elemen...  9.23 us
  transfers between devices with their start and end apart: 4, of which 3 were waited for; matrix products, arithmetic and copies ran while one was open for 3% of the time, Pallas kernels for 0%

commit v1 on v0

--- a/solution.py
+++ b/solution.py
@@ -75,18 +75,18 @@
     def compute():
         return lax.dot_general(
             normed, delta, (((0,), (0,)), ((), ())), preferred_element_type=jnp.float32
-        )
+        ).astype(jnp.bfloat16)
 
     shard = lax.psum_scatter(
         lax.cond(
             trainer,
             compute,
-            lambda: jnp.zeros((lax.axis_size("fsdp") * shard_rows, embedding), jnp.float32),
+            lambda: jnp.zeros((lax.axis_size("fsdp") * shard_rows, embedding), jnp.bfloat16),
         ),
         "fsdp",
         scatter_dimension=0,
         tiled=True,
-    )
+    ).astype(jnp.float32)
     row_square = jnp.mean(shard * shard, axis=1, keepdims=True)
     normalized = shard * lax.rsqrt(row_square + 1e-06)
     result = jnp.where(trainer, normalized, copied.astype(jnp.float32))

time: 318 us -> 241 us (0.76)
  waiting for transfers between devices: 247 us -> 173 us
    reduce_scatter x1, waiting for transfers between devices: 172 us -> 98.3 us  [shards(): lax.psum_scatter(lax.cond(trainer, compute, lambda: jnp.zeros((lax.axis_s...]
  transfers between devices with their start and end apart: 4 -> 4, of which waited for: 3 -> 3; matrix products, arithmetic and copies ran while one was open for 3% -> 4% of each run, Pallas kernels for 0% -> 0%
where the time goes in v1:
time: 241 us
  waiting for transfers between devices  173 us (72%)
  blocking collectives  19 us (8%)
  matrix products  16 us (7%)
  other arithmetic  14.3 us (6%)
  between operations  13.5 us (6%)
  local copies, waits for them, and re-layouts  2.86 us (1%)
  starting transfers between devices  2.66 us (1%)
    reduce_scatter x1, waiting for transfers between devices, shards(): lax.psum_scatter(lax.cond(trainer, compute, lambda: jnp.zeros((lax.axis_s...  98.3 us
    all_gather x1, waiting for transfers between devices, shards(): lax.all_gather(weight_bf, 'fsdp', axis=0, tiled=True)  70 us
    all_gather x1, blocking collectives, shards(): slab = lax.all_gather(mine, 'fsdp', axis=0, tiled=True)  19 us
    dot_general x1, matrix products, compute(): lax.dot_general(normed, delta, (((0,), (0,)), ((), ())), preferred_elemen...  8.77 us
    dot_general x1, matrix products, shards(): jnp.dot(normed, lax.all_gather(weight_bf, 'fsdp', axis=0, tiled=True), pr...  6.79 us
  transfers between devices with their start and end apart: 4, of which 3 were waited for; matrix products, arithmetic and copies ran while one was open for 4% of the time, Pallas kernels for 0%

profile of v1, /device:TPU:0, one launch (start us, length us, event | category | flops | bytes accessed | tf_op | source)
XLA Modules:
  0.0 240.9 jit_solution(16838814864444121084)
XLA Ops:
  6.5 2.2 convert_element_type.76
  8.9 0.7 compare_convert_fusion
  9.6 0.7 compare_select_fusion.1
  10.3 0.7 fusion.16
  11.1 0.8 select_reduce_fusion
  12.0 0.7 multiply_add_fusion
  12.6 0.7 gather_fusion
  13.3 0.1 gather.9
  13.4 0.1 reshape.117
  13.5 0.1 fusion.25
  13.7 0.7 multiply_reduce_fusion
  14.4 2.8 %fusion.3 = bf16[384,4096]{1,0:T(8,128)(2,1)} fusion(f32[4096]{0:T(1024)S(1)} %copy-done.2, f32[384]{0:T(512)S(1)} %rsqrt_bitcast_fusion, bf16[1,3,128,4096]{3,2,1,0:T(8,128)(2,1)S(1)} %copy-done), kind=kLoop, calls=%fused_computation.7 | loop fusion | flops 6291456 | bytes 6309376 | tf_op jit(solution)/shard_map/convert_element_type | solution.py:27
  17.2 70.0 %all-gather.4.cloned.1.call-done = bf16[1,4096,1024]{2,1,0:T(8,128)(2,1)} async-done(((bf16[1,256,1024]{2,1,0:T(8,128)(2,1)}), bf16[1,4096,1024]{2,1,0:T(8,128)(2,1)}) %all-gather.4.cloned.1.call-update) | async-done | bytes 8388624 | tf_op jit(solution)/shard_map/all_gather | solution.py:33
  87.2 6.8 %fusion.6 = f32[384,1024]{1,0:T(8,128)S(1)} fusion(bf16[384,4096]{1,0:T(8,128)(2,1)} %fusion.3, bf16[1,4096,1024]{2,1,0:T(8,128)(2,1)} %all-gather.4.cloned.1.call-done), kind=kOutput, calls=%fused_computation.13 | convolution fusion | flops 3221225472 | bytes 13107200 | tf_op jit(solution)/shard_map/dot_general | solution.py:31
  94.0 0.2 multiply_reduce_fusion.1
  94.2 0.2 multiply_reduce_fusion.2
  94.4 1.3 collective-permute-start
  95.8 4.2 %collective-permute-done = bf16[3,1024]{1,0:T(4,128)(2,1)S(1)} collective-permute-done((bf16[3,1024]{1,0:T(4,128)(2,1)S(1)}, bf16[3,1024]{1,0:T(4,128)(2,1)S(1)}, u32[]{:S(2)}, u32[]{:S(2)}) %collective-permute-start) | collective-permute-done | bytes 6176 | tf_op jit(solution)/shard_map/ppermute | solution.py:12
  100.0 19.0 %all-gather.1 = bf16[16,3,1024]{2,1,0:T(4,128)(2,1)S(1)} all-gather(bf16[1,3,1024]{2,1,0:T(4,128)(2,1)S(1)} %bitcast.65), channel_id=1, replica_groups=mesh['grp'=2,'fsdp'=16] {'fsdp'}, dimensions={0}, use_global_device_ids=true | all-gather | bytes 104448 | tf_op jit(solution)/shard_map/all_gather | solution.py:51
  119.1 0.6 gather_fusion.1
  119.7 0.2 fusion.12
  119.9 0.1 fusion.22
  120.1 0.2 fusion.14
  120.3 0.1 fusion.19
  120.5 0.3 fusion.5
  120.8 8.8 %conditional.1 = (bf16[4096,1024]{1,0:T(8,128)(2,1)}) conditional(s32[]{:T(128)} %convert_element_type.68, () %tuple.11, (bf16[384,4096]{1,0:T(8,128)(2,1)}, bf16[384,1024]{1,0:T(8,128)(2,1)S(1)}) %tuple.12), branch_computations={%region_8.9_spmd, %region_9.10_spmd} | conditional | flops 3225419776 | bytes 12320776 | solution.py:81
  120.8 8.8 %convolution_convert_fusion = bf16[4096,1024]{1,0:T(8,128)(2,1)} fusion(bf16[384,4096]{1,0:T(8,128)(2,1)} %get-tuple-element.12, bf16[384,1024]{1,0:T(8,128)(2,1)S(1)} %get-tuple-element.13), kind=kOutput, calls=%fused_computation.2 | convolution fusion | flops 3225419776 | bytes 12320768 | tf_op jit(solution)/shard_map/cond/branch_1_fun/dot_general | solution.py:76
  129.6 1.2 copy-done.1
  130.9 1.3 collective-permute-start.1
  132.3 98.3 %reduce-scatter.2.cloned.1.call-done = bf16[256,1024]{1,0:T(8,128)(2,1)} async-done(((bf16[4096,1024]{1,0:T(8,128)(2,1)}), bf16[256,1024]{1,0:T(8,128)(2,1)}) %reduce-scatter.2.cloned.1.call-update) | async-done | bytes 524304 | tf_op jit(solution)/shard_map/reduce_scatter | solution.py:80
  230.6 1.2 fusion.9
  231.8 2.2 fusion.11
  (29 shorter events, 0.8 us)
Async XLA Ops:
  6.5 7.0 %copy-start.3 = (s32[1,3,128]{2,0,1:T(1,128)S(1)}, s32[1,3,128]{2,0,1:T(1,128)}, u32[]{:S(2)}) copy-start(s32[1,3,128]{2,0,1:T(1,128)} %param.9) | copy-start | bytes 4612
  6.5 7.1 %copy-start = (bf16[1,3,128,4096]{3,2,1,0:T(8,128)(2,1)S(1)}, bf16[1,3,128,4096]{3,2,1,0:T(8,128)(2,1)}, u32[]{:S(2)}) copy-start(bf16[1,3,128,4096]{3,2,1,0:T(8,128)(2,1)} %param.8) | copy-start | bytes 9437188
  6.5 80.6 %all-gather.4.cloned.1.call-start = ((), (), s32[]{:S(2)}) async-start(), calls=%async_computation.2 | async-start | bytes 8912896 | tf_op jit(solution)/shard_map/all_gather | solution.py:33
  8.8 5.7 %copy-start.2 = (f32[4096]{0:T(1024)S(1)}, f32[4096]{0:T(1024)}, u32[]{:S(2)}) copy-start(f32[4096]{0:T(1024)} %param.11) | copy-start | bytes 49156
  8.8 221.8 %reduce-scatter.2.cloned.1.call-start = ((), (), s32[]{:S(2)}) async-start(), calls=%async_computation.1 | async-start | bytes 8912896 | tf_op jit(solution)/shard_map/reduce_scatter | solution.py:80
  94.4 5.5 %collective-permute-start = (bf16[3,1024]{1,0:T(4,128)(2,1)S(1)}, bf16[3,1024]{1,0:T(4,128)(2,1)S(1)}, u32[]{:S(2)}, u32[]{:S(2)}) collective-permute-start(bf16[3,1024]{1,0:T(4,128)(2,1)S(1)} %get-tuple-element.21), channel_id=1, source_target_pairs={{16,0},{17,1},{18,2},{19,3},{20,4},{21,5},{22,6},{23,7},{24,8},{25... | collective-permute-start | bytes 18440 | tf_op jit(solution)/shard_map/ppermute | solution.py:12
  129.6 1.2 copy-start.1
  130.9 100.9 %collective-permute-start.1 = (bf16[256,1024]{1,0:T(8,128)(2,1)S(1)}, bf16[256,1024]{1,0:T(8,128)(2,1)S(1)}, u32[]{:S(2)}, u32[]{:S(2)}) collective-permute-start(bf16[256,1024]{1,0:T(8,128)(2,1)S(1)} %convert_bitcast_fusion), channel_id=1, source_target_pairs={{0,16},{1,17},{2,18},{3,19},{4,20},{5,21},{6,22},{7,23},{8,24},{9,... | collective-permute-start | bytes 1572872 | tf_op jit(solution)/shard_map/ppermute | solution.py:12
Sparse Core Ops, SparseCore 0:
  9.5 77.5 all-gather.3
  129.8 100.7 reduce-scatter.1

commit v2 on v0

v2 whole, which is shorter than its diff:
```python
import jax
import jax.numpy as jnp
from jax import lax
from jax.sharding import Mesh, PartitionSpec as P

sharpness = 20.0
cores = 2
longest_ring = 16


def ring_order(chips):
    return list(range(0, chips, 2)) + list(range(1, chips, 2))[::-1]


def ring_place(chip, chips):
    return jnp.where(chip % 2 == 0, chip // 2, chips - 1 - chip // 2)


def ring_chip(place, chips):
    place = lax.rem(place + 2 * chips, chips)
    return jnp.where(place < chips // 2, 2 * place, 2 * (chips - 1 - place) + 1)


def along_ring(block, by):
    order = ring_order(lax.axis_size("chip"))
    pairs = [(chip, order[(i + by) % len(order)]) for i, chip in enumerate(order)]
    return lax.ppermute(block, "chip", pairs)


def from_sibling(block):
    return lax.ppermute(block, "core", [(0, 1), (1, 0)])


def in_core_order(mine, other, core, axis=0):
    return jnp.where(
        core == 0,
        jnp.concatenate([mine, other], axis=axis),
        jnp.concatenate([other, mine], axis=axis),
    )


def shards(token_states, token_ids, master, gain, cand_ids, slab_owner):
    trainer = lax.axis_index("grp") == 0
    chips = lax.axis_size("chip")
    chip = lax.axis_index("chip")
    core = lax.axis_index("core")
    place = ring_place(chip, chips)
    states = token_states[0]
    seq_dev, length, width = states.shape
    rows, embedding = master.shape[1:]
    half = embedding // cores
    tokens_dev = seq_dev * length
    seqs = cores * seq_dev

    weight_bf = master[0].astype(jnp.bfloat16)
    own = lax.dynamic_slice(weight_bf, (0, core * half), (rows, half))
    sibling = from_sibling(lax.dynamic_slice(weight_bf, (0, (1 - core) * half), (rows, half)))
    copied = lax.ppermute(weight_bf, "grp", [(0, 1)])

    states_wide = states.astype(jnp.float32)
    mean_square = jnp.mean(states_wide * states_wide, axis=-1, keepdims=True)
    normed = (
        (states_wide * lax.rsqrt(mean_square + 1e-05) * gain)
        .astype(jnp.bfloat16)
        .reshape(tokens_dev, width)
    )
    normed = jnp.concatenate([normed, from_sibling(normed)])
    ids = jnp.concatenate([token_ids[0], cand_ids], axis=1)
    ids = jnp.concatenate([ids, from_sibling(ids)])
    valid = (ids[:, :length] != 0).astype(jnp.float32)
    counts = jnp.sum(valid, axis=1)
    weighted = valid / counts[:, None]
    cands = ids[:, length:]

    def columns(offset, part):
        first = (ring_chip(place + offset, chips) * cores + part) * rows
        return lax.dynamic_slice(normed, (0, first), (seqs * length, rows))

    def product(offset, part, block):
        return jnp.dot(columns(offset, part), block, preferred_element_type=jnp.float32)

    parts = (core, 1 - core)
    if chips <= longest_ring:
        hidden = product(0, parts[0], own) + product(0, parts[1], sibling)
        moving = {(i, by): block for by in (1, -1) for i, block in enumerate((own, sibling))}
        for step in range(1, chips // 2 + 1):
            for i, by in ((0, 1), (1, -1), (1, 1), (0, -1)):
                if step == chips // 2 and (i, by) not in ((0, 1), (1, -1)):
                    continue
                moving[i, by] = along_ring(moving[i, by], by)
                hidden = hidden + product(-by * step, parts[i], moving[i, by])
    else:
        both = in_core_order(own, sibling, core)
        gathered = lax.all_gather(both, "chip", axis=0, tiled=True)
        hidden = jnp.dot(normed, gathered, preferred_element_type=jnp.float32)

    active = jnp.tanh(hidden).reshape(seqs, length, half)
    pooled = jnp.sum(active * valid[:, :, None], axis=1) / counts[:, None]
    pooled_other = from_sibling(pooled)
    pooled_other = jnp.concatenate([pooled_other[seq_dev:], pooled_other[:seq_dev]])
    whole = in_core_order(pooled, pooled_other, core, axis=1)
    pooled_square = jnp.mean(whole * whole, axis=-1, keepdims=True)
    scale = lax.rsqrt(pooled_square + 1e-06)
    unit = whole * scale
    stored = unit.astype(jnp.bfloat16)
    stored = in_core_order(stored[:seq_dev], stored[seq_dev:], core)

    devices_fsdp = chips * cores
    owners = jnp.arange(devices_fsdp, dtype=jnp.int32)
    onehot = (slab_owner[:, None] == owners[None, :]).astype(jnp.int32)
    ranks = jnp.sum((jnp.cumsum(onehot, axis=0) - onehot) * onehot, axis=1)
    places = slab_owner * seq_dev + ranks
    wanted = places[cands]
    groups = lax.axis_size("grp")
    spread = jnp.broadcast_to(stored[None], (groups * chips,) + stored.shape)
    spread = lax.all_to_all(spread, ("grp", "chip"), 0, 0)
    slab = spread[(groups - 1) * chips :].reshape(devices_fsdp * seq_dev, embedding)

    chosen = slab[wanted].astype(jnp.float32)
    logits = (
        sharpness
        / embedding
        * jnp.einsum("qe,qje->qj", unit, chosen, precision=lax.Precision.HIGHEST)
    )
    exponent = jnp.exp(logits)
    probs = exponent / jnp.sum(exponent, axis=-1, keepdims=True)
    target = (jnp.arange(chosen.shape[1]) == 0).astype(jnp.float32)
    logit_grad = probs - target[None, :]
    unit_grad = (
        sharpness
        / embedding
        * jnp.einsum("qj,qje->qe", logit_grad, chosen, precision=lax.Precision.HIGHEST)
    )
    inner = jnp.sum(whole * unit_grad, axis=-1, keepdims=True)
    pooled_grad = scale * unit_grad - whole * (scale * scale * scale) * inner / embedding
    pooled_grad = lax.dynamic_slice(pooled_grad, (0, core * half), (seqs, half))
    delta = weighted[:, :, None] * pooled_grad[:, None, :] * (1.0 - active * active)
    delta = delta.astype(jnp.bfloat16).reshape(seqs * length, half)

    def term(offset, part):
        return lax.dot_general(
            columns(offset, part),
            delta,
            (((0,), (0,)), ((), ())),
            preferred_element_type=jnp.float32,
        )

    if chips <= longest_ring:
        arrived = {}
        for step in range(chips // 2, 0, -1):
            for i, by in ((1, -1), (0, 1), (1, 1), (0, -1)):
                if step == chips // 2 and (i, by) not in ((0, 1), (1, -1)):
                    continue
                total = term(by * step, parts[i])
                if (i, by) in arrived:
                    total = total + arrived[i, by].astype(jnp.float32)
                arrived[i, by] = along_ring(total.astype(jnp.bfloat16), by)
        mine, other = [
            term(0, parts[i])
            + arrived[i, 1].astype(jnp.float32)
            + arrived[i, -1].astype(jnp.float32)
            for i in range(2)
        ]
    else:
        grad = lax.dot_general(
            normed, delta, (((0,), (0,)), ((), ())), preferred_element_type=jnp.float32
        )
        reduced = lax.psum_scatter(grad, "chip", scatter_dimension=0, tiled=True)
        mine, other = [lax.dynamic_slice(reduced, (i * rows, 0), (rows, half)) for i in parts]
    other = from_sibling(other)
    shard = in_core_order(mine, other, core, axis=1)
    row_square = jnp.mean(shard * shard, axis=1, keepdims=True)
    normalized = shard * lax.rsqrt(row_square + 1e-06)
    result = jnp.where(trainer, normalized, copied.astype(jnp.float32))
    return result[None]


def solution(mesh):
    groups, devices_fsdp = mesh.devices.shape
    finer = Mesh(
        mesh.devices.reshape(groups, devices_fsdp // cores, cores), ("grp", "chip", "core")
    )
    fsdp = ("chip", "core")
    placed = (
        P("grp", fsdp, None, None),
        P("grp", fsdp, None),
        P("grp", fsdp, None),
        P(),
        P(fsdp, None),
        P(),
    )
    return jax.shard_map(
        shards, mesh=finer, in_specs=placed, out_specs=P("grp", fsdp, None), check_vma=False
    )
```

time: 318 us -> 161 us (0.51)
  waiting for transfers between devices: 247 us -> 61.2 us
  starting transfers between devices: 2.66 us -> 40.8 us
  blocking collectives: 19 us -> 0 us
  matrix products: 15.4 us -> 31.9 us
  between operations: 13.5 us -> 0.82 us
  other arithmetic: 15.3 us -> 19.2 us
    reduce_scatter x1 -> x0, waiting for transfers between devices: 172 us -> none  [shards(): lax.psum_scatter(lax.cond(trainer, compute, lambda: jnp.zeros((lax.axis_s...]
    all_gather x1 -> x0, waiting for transfers between devices: 70.6 us -> none  [shards(): lax.all_gather(weight_bf, 'fsdp', axis=0, tiled=True)]
    ppermute x2 -> x34, waiting for transfers between devices: 4.24 us -> 51 us  [the longest x28 39.3 us: along_ring(): return lax.ppermute(block, 'chip', pairs)]
    ppermute x2 -> x34, starting transfers between devices: 2.61 us -> 33.7 us  [the longest x28 29.8 us: along_ring(): return lax.ppermute(block, 'chip', pairs)]
    all_gather x1 -> x0, blocking collectives: 19 us -> none  [shards(): slab = lax.all_gather(mine, 'fsdp', axis=0, tiled=True)]
    dot_general x4 -> x34, matrix products: 15.4 us -> 31.9 us  [the longest x16 19.3 us: product(): jnp.dot(columns(offset, part), block, preferred_element_type=jnp.float32)]
    all_to_all x0 -> x1, waiting for transfers between devices: none -> 10.1 us  [shards(): spread = lax.all_to_all(spread, ('grp', 'chip'), 0, 0)]
    all_to_all x0 -> x1, starting transfers between devices: none -> 7.05 us  [shards(): spread = lax.all_to_all(spread, ('grp', 'chip'), 0, 0)]
  transfers between devices with their start and end apart: 4 -> 35, of which waited for: 3 -> 19; matrix products, arithmetic and copies ran while one was open for 3% -> 25% of each run, Pallas kernels for 0% -> 0%
where the time goes in v2:
time: 161 us; the launch traced here: 160 us
  waiting for transfers between devices  61.2 us (38%)
  starting transfers between devices  40.8 us (25%)
  matrix products  31.9 us (20%)
  other arithmetic  19.2 us (12%)
  local copies, waits for them, and re-layouts  5.72 us (4%)
    ppermute x28, waiting for transfers between devices, along_ring(): return lax.ppermute(block, 'chip', pairs)  39.3 us
    ppermute x28, starting transfers between devices, along_ring(): return lax.ppermute(block, 'chip', pairs)  29.8 us
    dot_general x16, matrix products, product(): jnp.dot(columns(offset, part), block, preferred_element_type=jnp.float32)  19.3 us
    dot_general x16, matrix products, term(): lax.dot_general(columns(offset, part), delta, (((0,), (0,)), ((), ())), p...  11.3 us
    ppermute x1, waiting for transfers between devices, shards(): copied = lax.ppermute(weight_bf, 'grp', [(0, 1)])  10.4 us
    all_to_all x1, waiting for transfers between devices, shards(): spread = lax.all_to_all(spread, ('grp', 'chip'), 0, 0)  10.1 us
    all_to_all x1, starting transfers between devices, shards(): spread = lax.all_to_all(spread, ('grp', 'chip'), 0, 0)  7.05 us
    concatenate x3, other arithmetic, shards(): normed = jnp.concatenate([normed, from_sibling(normed)])  4.65 us
  transfers between devices with their start and end apart: 35, of which 19 were waited for; matrix products, arithmetic and copies ran while one was open for 25% of the time, Pallas kernels for 0%

profile of v2, /device:TPU:0, one launch (start us, length us, event | category | flops | bytes accessed | tf_op | source)
XLA Modules:
  0.0 159.6 jit_solution(12039963311295958682)
XLA Ops:
  0.0 2.7 %multiply_reduce_fusion = f32[3,128]{1,0:T(4,128)S(1)} fusion(bf16[1,3,128,4096]{3,2,1,0:T(8,128)(2,1)} %param.6), kind=kLoop, calls=%fused_computation.41 | loop fusion | flops 4718208 | bytes 3147264 | tf_op jit(solution)/shard_map/reduce_sum | solution.py:61
  2.8 1.7 %fusion.1 = bf16[384,4096]{1,0:T(8,128)(2,1)S(1)} fusion(f32[4096]{0:T(1024)} %param.9, f32[384]{0:T(512)S(1)} %rsqrt_bitcast_fusion, bf16[1,3,128,4096]{3,2,1,0:T(8,128)(2,1)S(1)} %copy-done.3), kind=kLoop, calls=%fused_computation.40 | loop fusion | flops 6291456 | bytes 6309376 | tf_op jit(solution)/shard_map/convert_element_type | solution.py:64
  5.1 2.1 %convert_element_type.133 = bf16[1,256,1024]{2,1,0:T(8,128)(2,1)} convert(f32[1,256,1024]{2,1,0:T(8,128)} %param.8) | non-fusion elementwise | flops 262144 | bytes 1572864 | tf_op jit(solution)/shard_map/convert_element_type | solution.py:55
  7.2 1.8 %dynamic-slice_bitcast_fusion = (bf16[256,512]{1,0:T(8,128)(2,1)}, bf16[256,512]{1,0:T(8,128)(2,1)S(1)}) fusion(bf16[1,256,1024]{2,1,0:T(8,128)(2,1)} %convert_element_type.133, s32[]{:T(128)S(6)} %select_n.191, s32[]{:T(128)S(6)} %select_n.189), kind=kLoop, calls=%fused_computation.97 | loop fusion | bytes 1048584 | tf_op jit(solution)/shard_map/dynamic_slice | solution.py:57
  9.0 2.6 %collective-permute-start.3 = (bf16[256,512]{1,0:T(8,128)(2,1)S(1)}, bf16[256,512]{1,0:T(8,128)(2,1)}, u32[]{:S(2)}, u32[]{:S(2)}) collective-permute-start(bf16[256,512]{1,0:T(8,128)(2,1)S(1)} %get-tuple-element.24), channel_id=1, source_target_pairs={{0,4},{4,8},{8,12},{12,14},{14,10},{10,6},{6,2},{2,0},{1,5},{5,9},... | collective-permute-start | bytes 786440 | tf_op jit(solution)/shard_map/ppermute | solution.py:27
  13.5 2.0 %collective-permute-start.4 = (bf16[256,512]{1,0:T(8,128)(2,1)}, bf16[256,512]{1,0:T(8,128)(2,1)}, u32[]{:S(2)}, u32[]{:S(2)}) collective-permute-start(bf16[256,512]{1,0:T(8,128)(2,1)} %collective-permute-done.2), channel_id=1, source_target_pairs={{0,2},{4,0},{8,4},{12,8},{14,12},{10,14},{6,10},{2,6},{1,3},{5,1},... | collective-permute-start | bytes 786440 | tf_op jit(solution)/shard_map/ppermute | solution.py:27
  16.1 2.4 %collective-permute-done.3 = bf16[256,512]{1,0:T(8,128)(2,1)} collective-permute-done((bf16[256,512]{1,0:T(8,128)(2,1)S(1)}, bf16[256,512]{1,0:T(8,128)(2,1)}, u32[]{:S(2)}, u32[]{:S(2)}) %collective-permute-start.3) | collective-permute-done | bytes 262176 | tf_op jit(solution)/shard_map/ppermute | solution.py:27
  18.6 2.2 %collective-permute-start.7 = (bf16[256,512]{1,0:T(8,128)(2,1)}, bf16[256,512]{1,0:T(8,128)(2,1)}, u32[]{:S(2)}, u32[]{:S(2)}) collective-permute-start(bf16[256,512]{1,0:T(8,128)(2,1)} %collective-permute-done.3), channel_id=1, source_target_pairs={{0,4},{4,8},{8,12},{12,14},{14,10},{10,6},{6,2},{2,0},{1,5},{5,9},... | collective-permute-start | bytes 786440 | tf_op jit(solution)/shard_map/ppermute | solution.py:27
  20.8 4.9 %collective-permute-done.4 = bf16[256,512]{1,0:T(8,128)(2,1)} collective-permute-done((bf16[256,512]{1,0:T(8,128)(2,1)}, bf16[256,512]{1,0:T(8,128)(2,1)}, u32[]{:S(2)}, u32[]{:S(2)}) %collective-permute-start.4) | collective-permute-done | bytes 262176 | tf_op jit(solution)/shard_map/ppermute | solution.py:27
  26.0 1.7 %collective-permute-start.10 = (bf16[256,512]{1,0:T(8,128)(2,1)}, bf16[256,512]{1,0:T(8,128)(2,1)}, u32[]{:S(2)}, u32[]{:S(2)}) collective-permute-start(bf16[256,512]{1,0:T(8,128)(2,1)} %collective-permute-done.6), channel_id=1, source_target_pairs={{0,2},{4,0},{8,4},{12,8},{14,12},{10,14},{6,10},{2,6},{1,3},{5,1},... | collective-permute-start | bytes 786440 | tf_op jit(solution)/shard_map/ppermute | solution.py:27
  28.1 2.5 %collective-permute-done.7 = bf16[256,512]{1,0:T(8,128)(2,1)} collective-permute-done((bf16[256,512]{1,0:T(8,128)(2,1)}, bf16[256,512]{1,0:T(8,128)(2,1)}, u32[]{:S(2)}, u32[]{:S(2)}) %collective-permute-start.7) | collective-permute-done | bytes 262176 | tf_op jit(solution)/shard_map/ppermute | solution.py:27
  32.0 3.3 %collective-permute-done.8 = bf16[256,512]{1,0:T(8,128)(2,1)} collective-permute-done((bf16[256,512]{1,0:T(8,128)(2,1)}, bf16[256,512]{1,0:T(8,128)(2,1)}, u32[]{:S(2)}, u32[]{:S(2)}) %collective-permute-start.8) | collective-permute-done | bytes 262176 | tf_op jit(solution)/shard_map/ppermute | solution.py:27
  35.8 5.1 %collective-permute-done.10 = bf16[256,512]{1,0:T(8,128)(2,1)} collective-permute-done((bf16[256,512]{1,0:T(8,128)(2,1)}, bf16[256,512]{1,0:T(8,128)(2,1)}, u32[]{:S(2)}, u32[]{:S(2)}) %collective-permute-start.10) | collective-permute-done | bytes 262176 | tf_op jit(solution)/shard_map/ppermute | solution.py:27
  41.2 1.8 %collective-permute-start.13 = (bf16[256,512]{1,0:T(8,128)(2,1)}, bf16[256,512]{1,0:T(8,128)(2,1)S(1)}, u32[]{:S(2)}, u32[]{:S(2)}) collective-permute-start(bf16[256,512]{1,0:T(8,128)(2,1)} %collective-permute-done.9), channel_id=1, source_target_pairs={{0,4},{4,8},{8,12},{12,14},{14,10},{10,6},{6,2},{2,0},{1,5},{5,9},... | collective-permute-start | bytes 786440 | tf_op jit(solution)/shard_map/ppermute | solution.py:27
  42.9 1.6 collective-permute-start.15
  44.5 2.0 %collective-permute-done.12 = bf16[256,512]{1,0:T(8,128)(2,1)} collective-permute-done((bf16[256,512]{1,0:T(8,128)(2,1)}, bf16[256,512]{1,0:T(8,128)(2,1)}, u32[]{:S(2)}, u32[]{:S(2)}) %collective-permute-start.12) | collective-permute-done | bytes 262176 | tf_op jit(solution)/shard_map/ppermute | solution.py:27
  46.8 1.6 fusion.18
  48.8 2.0 %fusion.23 = (bf16[768,256]{1,0:T(8,128)(2,1)S(1)}, bf16[768,256]{1,0:T(8,128)(2,1)S(1)}, bf16[768,256]{1,0:T(8,128)(2,1)S(1)}, bf16[768,256]{1,0:T(8,128)(2,1)S...) fusion(s32[]{:T(128)S(6)} %select_n.199, bf16[384,4096]{1,0:T(8,128)(2,1)S(1)} %fusion.1, ...), kind=kLoop, calls=%fused_computation.85 | loop fusion | flops 4718592 | bytes 8650776 | tf_op jit(solution)/shard_map/concatenate | solution.py:67
  50.8 1.5 fusion.70
  65.4 1.5 fusion.68
  69.0 2.1 %add_tanh_fusion = f32[768,512]{1,0:T(8,128)S(1)} fusion(f32[768,512]{1,0:T(8,128)S(1)} %fusion.35, f32[768,512]{1,0:T(8,128)S(1)} %fusion.76, f32[768,512]{1,0:T(8,128)S(1)} %fusion.75, f32[768,512]{1,0:T(8,128)S(1)} %fusion.74, f32[768,512]{1,0:T(8,128)S(1)} %fusion.73, f32[768,512]{1,0:T(8,128)S(1)} %fusion.72, f32[768,512]{1,0:T(8,128)S(1)} %fusion.71, ...), kind=kOutput, calls=%fused_computation.46 | convolution fusion | flops 208011264 | bytes 31719428 | tf_op jit(solution)/shard_map/dot_general | solution.py:80
  75.4 7.0 %all-to-all-start = ((bf16[16,6,1024]{2,1,0:T(8,128)(2,1)}), bf16[16,6,1024]{2,1,0:T(8,128)(2,1)S(1)}, u32[]{:S(2)}, u32[]{:S(2)}) async-start(bf16[16,6,1024]{2,1,0:T(8,128)(2,1)} %broadcast_in_dim.6), calls=%async_computation | async-start | bytes 524288 | tf_op jit(solution)/shard_map/all_to_all | solution.py:116
  82.5 10.1 %all-to-all-done = bf16[16,6,1024]{2,1,0:T(8,128)(2,1)S(1)} async-done(((bf16[16,6,1024]{2,1,0:T(8,128)(2,1)}), bf16[16,6,1024]{2,1,0:T(8,128)(2,1)S(1)}, u32[]{:S(2)}, u32[]{:S(2)}) %all-to-all-start) | async-done | bytes 196640 | tf_op jit(solution)/shard_map/all_to_all | solution.py:116
  96.6 1.7 %fusion.3 = bf16[768,512]{1,0:T(8,128)(2,1)S(1)} fusion(f32[768,512]{1,0:T(8,128)} %copy-done.2, f32[6,512]{1,0:T(8,128)S(1)} %fusion.45, f32[768]{0:T(1024)S(1)} %divide_bitcast_fusion), kind=kLoop, calls=%fused_computation.44 | loop fusion | flops 1966080 | bytes 2374656 | tf_op jit(solution)/shard_map/convert_element_type | solution.py:138
  107.7 2.6 %collective-permute-done.28 = bf16[256,512]{1,0:T(8,128)(2,1)S(1)} collective-permute-done((bf16[256,512]{1,0:T(8,128)(2,1)S(1)}, bf16[256,512]{1,0:T(8,128)(2,1)S(1)}, u32[]{:S(2)}, u32[]{:S(2)}) %collective-permute-start.28) | collective-permute-done | bytes 262176 | tf_op jit(solution)/shard_map/ppermute | solution.py:27
  114.4 1.5 collective-permute-done.22
  120.0 1.5 collective-permute-done.29
  125.6 1.5 collective-permute-done.23
  129.4 3.4 %collective-permute-done.30 = bf16[256,512]{1,0:T(8,128)(2,1)S(1)} collective-permute-done((bf16[256,512]{1,0:T(8,128)(2,1)S(1)}, bf16[256,512]{1,0:T(8,128)(2,1)S(1)}, u32[]{:S(2)}, u32[]{:S(2)}) %collective-permute-start.30) | collective-permute-done | bytes 262176 | tf_op jit(solution)/shard_map/ppermute | solution.py:27
  136.3 5.0 %collective-permute-done.31 = bf16[256,512]{1,0:T(8,128)(2,1)S(1)} collective-permute-done((bf16[256,512]{1,0:T(8,128)(2,1)S(1)}, bf16[256,512]{1,0:T(8,128)(2,1)S(1)}, u32[]{:S(2)}, u32[]{:S(2)}) %collective-permute-start.31) | collective-permute-done | bytes 262176 | tf_op jit(solution)/shard_map/ppermute | solution.py:27
  143.4 2.8 %collective-permute-start.33 = (bf16[256,1024]{1,0:T(8,128)(2,1)}, bf16[256,1024]{1,0:T(8,128)(2,1)S(1)}, u32[]{:S(2)}, u32[]{:S(2)}) collective-permute-start(bf16[256,1024]{1,0:T(8,128)(2,1)} %convert_bitcast_fusion), channel_id=1, source_target_pairs={{0,16},{1,17},{2,18},{3,19},{4,20},{5,21},{6,22},{7,23},{8,24},{9,... | collective-permute-start | bytes 1572872 | tf_op jit(solution)/shard_map/ppermute | solution.py:58
  148.0 10.4 %collective-permute-done.33 = bf16[256,1024]{1,0:T(8,128)(2,1)S(1)} collective-permute-done((bf16[256,1024]{1,0:T(8,128)(2,1)}, bf16[256,1024]{1,0:T(8,128)(2,1)S(1)}, u32[]{:S(2)}, u32[]{:S(2)}) %collective-permute-start.33) | collective-permute-done | bytes 524320 | tf_op jit(solution)/shard_map/ppermute | solution.py:58
  (198 shorter events, 62.1 us)
Async XLA Ops:
  4.6 42.2 %collective-permute-start = (bf16[384,4096]{1,0:T(8,128)(2,1)S(1)}, bf16[384,4096]{1,0:T(8,128)(2,1)}, u32[]{:S(2)}, u32[]{:S(2)}) collective-permute-start(bf16[384,4096]{1,0:T(8,128)(2,1)S(1)} %fusion.1), channel_id=1, source_target_pairs={{0,1},{1,0},{2,3},{3,2},{4,5},{5,4},{6,7},{7,6},{8,9},{9,8},{10,11... | collective-permute-start | bytes 9437192 | tf_op jit(solution)/shard_map/ppermute | solution.py:31
  9.0 9.6 %collective-permute-start.3 = (bf16[256,512]{1,0:T(8,128)(2,1)S(1)}, bf16[256,512]{1,0:T(8,128)(2,1)}, u32[]{:S(2)}, u32[]{:S(2)}) collective-permute-start(bf16[256,512]{1,0:T(8,128)(2,1)S(1)} %get-tuple-element.24), channel_id=1, source_target_pairs={{0,4},{4,8},{8,12},{12,14},{14,10},{10,6},{6,2},{2,0},{1,5},{5,9},... | collective-permute-start | bytes 786440 | tf_op jit(solution)/shard_map/ppermute | solution.py:27
  11.6 14.4 %collective-permute-start.6 = (bf16[256,512]{1,0:T(8,128)(2,1)S(1)}, bf16[256,512]{1,0:T(8,128)(2,1)}, u32[]{:S(2)}, u32[]{:S(2)}) collective-permute-start(bf16[256,512]{1,0:T(8,128)(2,1)S(1)} %get-tuple-element.24), channel_id=1, source_target_pairs={{0,2},{4,0},{8,4},{12,8},{14,12},{10,14},{6,10},{2,6},{1,3},{5,1},... | collective-permute-start | bytes 786440 | tf_op jit(solution)/shard_map/ppermute | solution.py:27
  13.5 12.3 %collective-permute-start.4 = (bf16[256,512]{1,0:T(8,128)(2,1)}, bf16[256,512]{1,0:T(8,128)(2,1)}, u32[]{:S(2)}, u32[]{:S(2)}) collective-permute-start(bf16[256,512]{1,0:T(8,128)(2,1)} %collective-permute-done.2), channel_id=1, source_target_pairs={{0,2},{4,0},{8,4},{12,8},{14,12},{10,14},{6,10},{2,6},{1,3},{5,1},... | collective-permute-start | bytes 786440 | tf_op jit(solution)/shard_map/ppermute | solution.py:27
  16.0 11.7 %collective-permute-start.5 = (bf16[256,512]{1,0:T(8,128)(2,1)}, bf16[256,512]{1,0:T(8,128)(2,1)}, u32[]{:S(2)}, u32[]{:S(2)}) collective-permute-start(bf16[256,512]{1,0:T(8,128)(2,1)} %collective-permute-done.2), channel_id=1, source_target_pairs={{0,4},{4,8},{8,12},{12,14},{14,10},{10,6},{6,2},{2,0},{1,5},{5,9},... | collective-permute-start | bytes 786440 | tf_op jit(solution)/shard_map/ppermute | solution.py:27
  18.6 12.0 %collective-permute-start.7 = (bf16[256,512]{1,0:T(8,128)(2,1)}, bf16[256,512]{1,0:T(8,128)(2,1)}, u32[]{:S(2)}, u32[]{:S(2)}) collective-permute-start(bf16[256,512]{1,0:T(8,128)(2,1)} %collective-permute-done.3), channel_id=1, source_target_pairs={{0,4},{4,8},{8,12},{12,14},{14,10},{10,6},{6,2},{2,0},{1,5},{5,9},... | collective-permute-start | bytes 786440 | tf_op jit(solution)/shard_map/ppermute | solution.py:27
  25.7 9.6 %collective-permute-start.8 = (bf16[256,512]{1,0:T(8,128)(2,1)}, bf16[256,512]{1,0:T(8,128)(2,1)}, u32[]{:S(2)}, u32[]{:S(2)}) collective-permute-start(bf16[256,512]{1,0:T(8,128)(2,1)} %collective-permute-done.4), channel_id=1, source_target_pairs={{0,2},{4,0},{8,4},{12,8},{14,12},{10,14},{6,10},{2,6},{1,3},{5,1},... | collective-permute-start | bytes 786440 | tf_op jit(solution)/shard_map/ppermute | solution.py:27
  26.0 14.9 %collective-permute-start.10 = (bf16[256,512]{1,0:T(8,128)(2,1)}, bf16[256,512]{1,0:T(8,128)(2,1)}, u32[]{:S(2)}, u32[]{:S(2)}) collective-permute-start(bf16[256,512]{1,0:T(8,128)(2,1)} %collective-permute-done.6), channel_id=1, source_target_pairs={{0,2},{4,0},{8,4},{12,8},{14,12},{10,14},{6,10},{2,6},{1,3},{5,1},... | collective-permute-start | bytes 786440 | tf_op jit(solution)/shard_map/ppermute | solution.py:27
  27.8 13.4 %collective-permute-start.9 = (bf16[256,512]{1,0:T(8,128)(2,1)}, bf16[256,512]{1,0:T(8,128)(2,1)}, u32[]{:S(2)}, u32[]{:S(2)}) collective-permute-start(bf16[256,512]{1,0:T(8,128)(2,1)} %collective-permute-done.5), channel_id=1, source_target_pairs={{0,4},{4,8},{8,12},{12,14},{14,10},{10,6},{6,2},{2,0},{1,5},{5,9},... | collective-permute-start | bytes 786440 | tf_op jit(solution)/shard_map/ppermute | solution.py:27
  30.6 12.3 %collective-permute-start.11 = (bf16[256,512]{1,0:T(8,128)(2,1)}, bf16[256,512]{1,0:T(8,128)(2,1)}, u32[]{:S(2)}, u32[]{:S(2)}) collective-permute-start(bf16[256,512]{1,0:T(8,128)(2,1)} %collective-permute-done.7), channel_id=1, source_target_pairs={{0,4},{4,8},{8,12},{12,14},{14,10},{10,6},{6,2},{2,0},{1,5},{5,9},... | collective-permute-start | bytes 786440 | tf_op jit(solution)/shard_map/ppermute | solution.py:27
  35.3 11.2 %collective-permute-start.12 = (bf16[256,512]{1,0:T(8,128)(2,1)}, bf16[256,512]{1,0:T(8,128)(2,1)}, u32[]{:S(2)}, u32[]{:S(2)}) collective-permute-start(bf16[256,512]{1,0:T(8,128)(2,1)} %collective-permute-done.8), channel_id=1, source_target_pairs={{0,2},{4,0},{8,4},{12,8},{14,12},{10,14},{6,10},{2,6},{1,3},{5,1},... | collective-permute-start | bytes 786440 | tf_op jit(solution)/shard_map/ppermute | solution.py:27
  40.9 26.4 %collective-permute-start.14 = (bf16[256,512]{1,0:T(8,128)(2,1)}, bf16[256,512]{1,0:T(8,128)(2,1)S(1)}, u32[]{:S(2)}, u32[]{:S(2)}) collective-permute-start(bf16[256,512]{1,0:T(8,128)(2,1)} %collective-permute-done.10), channel_id=1, source_target_pairs={{0,2},{4,0},{8,4},{12,8},{14,12},{10,14},{6,10},{2,6},{1,3},{5,1},... | collective-permute-start | bytes 786440 | tf_op jit(solution)/shard_map/ppermute | solution.py:27
  41.2 25.8 %collective-permute-start.13 = (bf16[256,512]{1,0:T(8,128)(2,1)}, bf16[256,512]{1,0:T(8,128)(2,1)S(1)}, u32[]{:S(2)}, u32[]{:S(2)}) collective-permute-start(bf16[256,512]{1,0:T(8,128)(2,1)} %collective-permute-done.9), channel_id=1, source_target_pairs={{0,4},{4,8},{8,12},{12,14},{14,10},{10,6},{6,2},{2,0},{1,5},{5,9},... | collective-permute-start | bytes 786440 | tf_op jit(solution)/shard_map/ppermute | solution.py:27
  42.9 24.7 %collective-permute-start.15 = (bf16[256,512]{1,0:T(8,128)(2,1)}, bf16[256,512]{1,0:T(8,128)(2,1)S(1)}, u32[]{:S(2)}, u32[]{:S(2)}) collective-permute-start(bf16[256,512]{1,0:T(8,128)(2,1)} %collective-permute-done.11), channel_id=1, source_target_pairs={{0,4},{4,8},{8,12},{12,14},{14,10},{10,6},{6,2},{2,0},{1,5},{5,9},... | collective-permute-start | bytes 786440 | tf_op jit(solution)/shard_map/ppermute | solution.py:27
  46.5 22.5 %collective-permute-start.16 = (bf16[256,512]{1,0:T(8,128)(2,1)}, bf16[256,512]{1,0:T(8,128)(2,1)S(1)}, u32[]{:S(2)}, u32[]{:S(2)}) collective-permute-start(bf16[256,512]{1,0:T(8,128)(2,1)} %collective-permute-done.12), channel_id=1, source_target_pairs={{0,2},{4,0},{8,4},{12,8},{14,12},{10,14},{6,10},{2,6},{1,3},{5,1},... | collective-permute-start | bytes 786440 | tf_op jit(solution)/shard_map/ppermute | solution.py:27
  75.4 17.3 %all-to-all-start = ((bf16[16,6,1024]{2,1,0:T(8,128)(2,1)}), bf16[16,6,1024]{2,1,0:T(8,128)(2,1)S(1)}, u32[]{:S(2)}, u32[]{:S(2)}) async-start(bf16[16,6,1024]{2,1,0:T(8,128)(2,1)} %broadcast_in_dim.6), calls=%async_computation | async-start | bytes 524288 | tf_op jit(solution)/shard_map/all_to_all | solution.py:116
  98.7 7.6 %collective-permute-start.25 = (bf16[256,512]{1,0:T(8,128)(2,1)S(1)}, bf16[256,512]{1,0:T(8,128)(2,1)S(1)}, u32[]{:S(2)}, u32[]{:S(2)}) collective-permute-start(bf16[256,512]{1,0:T(8,128)(2,1)S(1)} %convolution_convert_fusion.1), channel_id=1, source_target_pairs={{0,4},{4,8},{8,12},{12,14},{14,10},{10,6},{6,2},{2,0},{1,5},{5,9},... | collective-permute-start | bytes 786440 | tf_op jit(solution)/shard_map/ppermute | solution.py:27
  101.0 9.2 %collective-permute-start.28 = (bf16[256,512]{1,0:T(8,128)(2,1)S(1)}, bf16[256,512]{1,0:T(8,128)(2,1)S(1)}, u32[]{:S(2)}, u32[]{:S(2)}) collective-permute-start(bf16[256,512]{1,0:T(8,128)(2,1)S(1)} %convolution_convert_fusion), channel_id=1, source_target_pairs={{0,2},{4,0},{8,4},{12,8},{14,12},{10,14},{6,10},{2,6},{1,3},{5,1},... | collective-permute-start | bytes 786440 | tf_op jit(solution)/shard_map/ppermute | solution.py:27
  103.7 9.3 %collective-permute-start.18 = (bf16[256,512]{1,0:T(8,128)(2,1)S(1)}, bf16[256,512]{1,0:T(8,128)(2,1)S(1)}, u32[]{:S(2)}, u32[]{:S(2)}) collective-permute-start(bf16[256,512]{1,0:T(8,128)(2,1)S(1)} %convolution_convert_fusion.3), channel_id=1, source_target_pairs={{0,4},{4,8},{8,12},{12,14},{14,10},{10,6},{6,2},{2,0},{1,5},{5,9},... | collective-permute-start | bytes 786440 | tf_op jit(solution)/shard_map/ppermute | solution.py:27
  105.1 10.8 %collective-permute-start.22 = (bf16[256,512]{1,0:T(8,128)(2,1)S(1)}, bf16[256,512]{1,0:T(8,128)(2,1)S(1)}, u32[]{:S(2)}, u32[]{:S(2)}) collective-permute-start(bf16[256,512]{1,0:T(8,128)(2,1)S(1)} %convolution_convert_fusion.2), channel_id=1, source_target_pairs={{0,2},{4,0},{8,4},{12,8},{14,12},{10,14},{6,10},{2,6},{1,3},{5,1},... | collective-permute-start | bytes 786440 | tf_op jit(solution)/shard_map/ppermute | solution.py:27
  106.7 12.0 %collective-permute-start.26 = (bf16[256,512]{1,0:T(8,128)(2,1)S(1)}, bf16[256,512]{1,0:T(8,128)(2,1)S(1)}, u32[]{:S(2)}, u32[]{:S(2)}) collective-permute-start(bf16[256,512]{1,0:T(8,128)(2,1)S(1)} %fusion.12), channel_id=1, source_target_pairs={{0,4},{4,8},{8,12},{12,14},{14,10},{10,6},{6,2},{2,0},{1,5},{5,9},... | collective-permute-start | bytes 786440 | tf_op jit(solution)/shard_map/ppermute | solution.py:27
  110.7 10.8 %collective-permute-start.29 = (bf16[256,512]{1,0:T(8,128)(2,1)S(1)}, bf16[256,512]{1,0:T(8,128)(2,1)S(1)}, u32[]{:S(2)}, u32[]{:S(2)}) collective-permute-start(bf16[256,512]{1,0:T(8,128)(2,1)S(1)} %fusion.15), channel_id=1, source_target_pairs={{0,2},{4,0},{8,4},{12,8},{14,12},{10,14},{6,10},{2,6},{1,3},{5,1},... | collective-permute-start | bytes 786440 | tf_op jit(solution)/shard_map/ppermute | solution.py:27
  113.4 10.8 %collective-permute-start.19 = (bf16[256,512]{1,0:T(8,128)(2,1)S(1)}, bf16[256,512]{1,0:T(8,128)(2,1)S(1)}, u32[]{:S(2)}, u32[]{:S(2)}) collective-permute-start(bf16[256,512]{1,0:T(8,128)(2,1)S(1)} %fusion.8), channel_id=1, source_target_pairs={{0,4},{4,8},{8,12},{12,14},{14,10},{10,6},{6,2},{2,0},{1,5},{5,9},... | collective-permute-start | bytes 786440 | tf_op jit(solution)/shard_map/ppermute | solution.py:27
  116.3 10.8 %collective-permute-start.23 = (bf16[256,512]{1,0:T(8,128)(2,1)S(1)}, bf16[256,512]{1,0:T(8,128)(2,1)S(1)}, u32[]{:S(2)}, u32[]{:S(2)}) collective-permute-start(bf16[256,512]{1,0:T(8,128)(2,1)S(1)} %fusion.10), channel_id=1, source_target_pairs={{0,2},{4,0},{8,4},{12,8},{14,12},{10,14},{6,10},{2,6},{1,3},{5,1},... | collective-permute-start | bytes 786440 | tf_op jit(solution)/shard_map/ppermute | solution.py:27
  119.1 17.3 %collective-permute-start.27 = (bf16[256,512]{1,0:T(8,128)(2,1)S(1)}, bf16[256,512]{1,0:T(8,128)(2,1)S(1)}, u32[]{:S(2)}, u32[]{:S(2)}) collective-permute-start(bf16[256,512]{1,0:T(8,128)(2,1)S(1)} %fusion.11), channel_id=1, source_target_pairs={{0,4},{4,8},{8,12},{12,14},{14,10},{10,6},{6,2},{2,0},{1,5},{5,9},... | collective-permute-start | bytes 786440 | tf_op jit(solution)/shard_map/ppermute | solution.py:27
  121.9 10.8 %collective-permute-start.30 = (bf16[256,512]{1,0:T(8,128)(2,1)S(1)}, bf16[256,512]{1,0:T(8,128)(2,1)S(1)}, u32[]{:S(2)}, u32[]{:S(2)}) collective-permute-start(bf16[256,512]{1,0:T(8,128)(2,1)S(1)} %fusion.14), channel_id=1, source_target_pairs={{0,2},{4,0},{8,4},{12,8},{14,12},{10,14},{6,10},{2,6},{1,3},{5,1},... | collective-permute-start | bytes 786440 | tf_op jit(solution)/shard_map/ppermute | solution.py:27
  124.7 9.7 %collective-permute-start.20 = (bf16[256,512]{1,0:T(8,128)(2,1)S(1)}, bf16[256,512]{1,0:T(8,128)(2,1)S(1)}, u32[]{:S(2)}, u32[]{:S(2)}) collective-permute-start(bf16[256,512]{1,0:T(8,128)(2,1)S(1)} %fusion.7), channel_id=1, source_target_pairs={{0,4},{4,8},{8,12},{12,14},{14,10},{10,6},{6,2},{2,0},{1,5},{5,9},... | collective-permute-start | bytes 786440 | tf_op jit(solution)/shard_map/ppermute | solution.py:27
  128.2 18.1 %collective-permute-start.24 = (bf16[256,512]{1,0:T(8,128)(2,1)}, bf16[256,512]{1,0:T(8,128)(2,1)}, u32[]{:S(2)}, u32[]{:S(2)}) collective-permute-start(bf16[256,512]{1,0:T(8,128)(2,1)} %fusion.9), channel_id=1, source_target_pairs={{0,2},{4,0},{8,4},{12,8},{14,12},{10,14},{6,10},{2,6},{1,3},{5,1},... | collective-permute-start | bytes 786440 | tf_op jit(solution)/shard_map/ppermute | solution.py:27
  133.2 8.2 %collective-permute-start.31 = (bf16[256,512]{1,0:T(8,128)(2,1)S(1)}, bf16[256,512]{1,0:T(8,128)(2,1)S(1)}, u32[]{:S(2)}, u32[]{:S(2)}) collective-permute-start(bf16[256,512]{1,0:T(8,128)(2,1)S(1)} %fusion.13), channel_id=1, source_target_pairs={{0,2},{4,0},{8,4},{12,8},{14,12},{10,14},{6,10},{2,6},{1,3},{5,1},... | collective-permute-start | bytes 786440 | tf_op jit(solution)/shard_map/ppermute | solution.py:27
  135.4 10.9 %collective-permute-start.21 = (bf16[256,512]{1,0:T(8,128)(2,1)}, bf16[256,512]{1,0:T(8,128)(2,1)}, u32[]{:S(2)}, u32[]{:S(2)}) collective-permute-start(bf16[256,512]{1,0:T(8,128)(2,1)} %fusion.6), channel_id=1, source_target_pairs={{0,4},{4,8},{8,12},{12,14},{14,10},{10,6},{6,2},{2,0},{1,5},{5,9},... | collective-permute-start | bytes 786440 | tf_op jit(solution)/shard_map/ppermute | solution.py:27
  142.5 5.2 %collective-permute-start.32 = (f32[256,512]{1,0:T(8,128)}, f32[256,512]{1,0:T(8,128)S(1)}, u32[]{:S(2)}, u32[]{:S(2)}) collective-permute-start(f32[256,512]{1,0:T(8,128)} %fusion.5), channel_id=1, source_target_pairs={{0,1},{1,0},{2,3},{3,2},{4,5},{5,4},{6,7},{7,6},{8,9},{9,8},{10,11... | collective-permute-start | bytes 1572872 | tf_op jit(solution)/shard_map/ppermute | solution.py:31
  143.4 15.0 %collective-permute-start.33 = (bf16[256,1024]{1,0:T(8,128)(2,1)}, bf16[256,1024]{1,0:T(8,128)(2,1)S(1)}, u32[]{:S(2)}, u32[]{:S(2)}) collective-permute-start(bf16[256,1024]{1,0:T(8,128)(2,1)} %convert_bitcast_fusion), channel_id=1, source_target_pairs={{0,16},{1,17},{2,18},{3,19},{4,20},{5,21},{6,22},{7,23},{8,24},{9,... | collective-permute-start | bytes 1572872 | tf_op jit(solution)/shard_map/ppermute | solution.py:58
  (41 other events, 307.9 us)

commit v3 on v2

--- a/solution.py
+++ b/solution.py
@@ -27,8 +27,27 @@
     return lax.ppermute(block, "chip", pairs)
 
 
+def after(first, block):
+    return lax.optimization_barrier((first, block))[1]
+
+
 def from_sibling(block):
     return lax.ppermute(block, "core", [(0, 1), (1, 0)])
+
+
+def slab_blocks(stored, chips, core):
+    order = ring_order(chips)
+    kept = []
+    for j in range(chips // cores):
+        pairs = []
+        for i, chip in enumerate(order):
+            for c in range(cores):
+                source = order[(i + j + c * (chips // cores)) % chips]
+                pairs.append(((chips + source) * cores + c, chip * cores + c))
+        kept.append(lax.ppermute(stored, ("grp", "chip", "core"), pairs))
+    kept = jnp.concatenate(kept)
+    other = from_sibling(kept)
+    return [jnp.where(core == 0, kept, other), jnp.where(core == 0, other, kept)]
 
 
 def in_core_order(mine, other, core, axis=0):
@@ -37,6 +56,12 @@
         jnp.concatenate([mine, other], axis=axis),
         jnp.concatenate([other, mine], axis=axis),
     )
+
+
+def normalize(states, gain):
+    states_wide = states.astype(jnp.float32)
+    mean_square = jnp.mean(states_wide * states_wide, axis=-1, keepdims=True)
+    return (states_wide * lax.rsqrt(mean_square + 1e-05) * gain).astype(jnp.bfloat16)
 
 
 def shards(token_states, token_ids, master, gain, cand_ids, slab_owner):
@@ -49,22 +74,19 @@
     seq_dev, length, width = states.shape
     rows, embedding = master.shape[1:]
     half = embedding // cores
-    tokens_dev = seq_dev * length
     seqs = cores * seq_dev
 
-    weight_bf = master[0].astype(jnp.bfloat16)
-    own = lax.dynamic_slice(weight_bf, (0, core * half), (rows, half))
-    sibling = from_sibling(lax.dynamic_slice(weight_bf, (0, (1 - core) * half), (rows, half)))
-    copied = lax.ppermute(weight_bf, "grp", [(0, 1)])
-
-    states_wide = states.astype(jnp.float32)
-    mean_square = jnp.mean(states_wide * states_wide, axis=-1, keepdims=True)
-    normed = (
-        (states_wide * lax.rsqrt(mean_square + 1e-05) * gain)
-        .astype(jnp.bfloat16)
-        .reshape(tokens_dev, width)
-    )
-    normed = jnp.concatenate([normed, from_sibling(normed)])
+    weights = master[0]
+    own = lax.dynamic_slice(weights, (0, core * half), (rows, half)).astype(jnp.bfloat16)
+    given = lax.dynamic_slice(weights, (0, (1 - core) * half), (rows, half))
+    given = given.astype(jnp.bfloat16)
+    sibling = from_sibling(given)
+
+    normed = normalize(states, gain)
+    normed, weights = lax.optimization_barrier((normed, weights))
+    copied = lax.ppermute(weights.astype(jnp.bfloat16), "grp", [(0, 1)])
+    normed = jnp.concatenate([normed, normalize(from_sibling(states), gain)])
+    normed = normed.reshape(seqs * length, width)
     ids = jnp.concatenate([token_ids[0], cand_ids], axis=1)
     ids = jnp.concatenate([ids, from_sibling(ids)])
     valid = (ids[:, :length] != 0).astype(jnp.float32)
@@ -81,14 +103,23 @@
 
     parts = (core, 1 - core)
     if chips <= longest_ring:
-        hidden = product(0, parts[0], own) + product(0, parts[1], sibling)
         moving = {(i, by): block for by in (1, -1) for i, block in enumerate((own, sibling))}
+        sums = [None]
         for step in range(1, chips // 2 + 1):
-            for i, by in ((0, 1), (1, -1), (1, 1), (0, -1)):
-                if step == chips // 2 and (i, by) not in ((0, 1), (1, -1)):
-                    continue
+            sent = [(0, 1), (1, -1), (1, 1), (0, -1)]
+            if step == chips // 2:
+                sent = sent[:2]
+            if step == 1:
+                total = product(0, parts[0], own) + product(0, parts[1], sibling)
+            else:
+                total = sums[-1]
+            for i, by in sent:
+                if step > 2:
+                    moving[i, by] = after(sums[step - 2], moving[i, by])
                 moving[i, by] = along_ring(moving[i, by], by)
-                hidden = hidden + product(-by * step, parts[i], moving[i, by])
+                total = total + product(-by * step, parts[i], moving[i, by])
+            sums.append(total)
+        hidden = sums[-1]
     else:
         both = in_core_order(own, sibling, core)
         gathered = lax.all_gather(both, "chip", axis=0, tiled=True)
@@ -96,6 +127,7 @@
 
     active = jnp.tanh(hidden).reshape(seqs, length, half)
     pooled = jnp.sum(active * valid[:, :, None], axis=1) / counts[:, None]
+    pooled, copied = lax.optimization_barrier((pooled, copied))
     pooled_other = from_sibling(pooled)
     pooled_other = jnp.concatenate([pooled_other[seq_dev:], pooled_other[:seq_dev]])
     whole = in_core_order(pooled, pooled_other, core, axis=1)
@@ -111,11 +143,9 @@
     ranks = jnp.sum((jnp.cumsum(onehot, axis=0) - onehot) * onehot, axis=1)
     places = slab_owner * seq_dev + ranks
     wanted = places[cands]
-    groups = lax.axis_size("grp")
-    spread = jnp.broadcast_to(stored[None], (groups * chips,) + stored.shape)
-    spread = lax.all_to_all(spread, ("grp", "chip"), 0, 0)
-    slab = spread[(groups - 1) * chips :].reshape(devices_fsdp * seq_dev, embedding)
-
+    slab = jnp.concatenate(slab_blocks(stored, chips, core))
+    seen = lax.rem(ring_place(wanted // seqs, chips) - place + chips, chips)
+    wanted = seen * seqs + lax.rem(wanted, seqs)
     chosen = slab[wanted].astype(jnp.float32)
     logits = (
         sharpness

time: 161 us -> 135 us (0.84)
  waiting for transfers between devices: 61.2 us -> 40.8 us
  matrix products: 31.9 us -> 27.7 us
    all_to_all x1 -> x0, waiting for transfers between devices: 10.1 us -> none  [shards(): spread = lax.all_to_all(spread, ('grp', 'chip'), 0, 0)]
    all_to_all x1 -> x0, starting transfers between devices: 7.05 us -> none  [shards(): spread = lax.all_to_all(spread, ('grp', 'chip'), 0, 0)]
    ppermute x28, waiting for transfers between devices: 39.3 us -> 32.8 us  [along_ring(): return lax.ppermute(block, 'chip', pairs)]
    ppermute x1 -> x5, starting transfers between devices: 2.84 us -> 9.22 us  [the longest x4 5.35 us: slab_blocks(): kept.append(lax.ppermute(stored, ('grp', 'chip', 'core'), pairs))]
    ppermute x1 -> x5, waiting for transfers between devices: 10.4 us -> 6.19 us  [the longest x4 6.19 us: slab_blocks(): kept.append(lax.ppermute(stored, ('grp', 'chip', 'core'), pairs))]
    dot_general x16, matrix products: 19.3 us -> 15.7 us  [product(): jnp.dot(columns(offset, part), block, preferred_element_type=jnp.float32)]
    reduce_sum x1 -> x2, other arithmetic: 2.73 us -> 5.17 us  [normalize(): mean_square = jnp.mean(states_wide * states_wide, axis=-1, keepdims=True)]
    concatenate x3, other arithmetic: 4.65 us -> 2.47 us  [the longest x1 2.43 us: shards(): normed = jnp.concatenate([normed, normalize(from_sibling(states), gain)])]
  transfers between devices with their start and end apart: 35 -> 39, of which waited for: 19 -> 18; matrix products, arithmetic and copies ran while one was open for 25% -> 32% of each run, Pallas kernels for 0% -> 0%
where the time goes in v3:
time: 135 us; the launch traced here: 134 us
  starting transfers between devices  41.9 us (31%)
  waiting for transfers between devices  40.8 us (30%)
  matrix products  27.7 us (21%)
  other arithmetic  18.6 us (14%)
  local copies, waits for them, and re-layouts  4.54 us (3%)
    ppermute x28, waiting for transfers between devices, along_ring(): return lax.ppermute(block, 'chip', pairs)  32.8 us
    ppermute x28, starting transfers between devices, along_ring(): return lax.ppermute(block, 'chip', pairs)  31 us
    dot_general x16, matrix products, product(): jnp.dot(columns(offset, part), block, preferred_element_type=jnp.float32)  15.7 us
    dot_general x16, matrix products, term(): lax.dot_general(columns(offset, part), delta, (((0,), (0,)), ((), ())), p...  11.5 us
    ppermute x4, waiting for transfers between devices, slab_blocks(): kept.append(lax.ppermute(stored, ('grp', 'chip', 'core'), pairs))  6.19 us
    ppermute x4, starting transfers between devices, slab_blocks(): kept.append(lax.ppermute(stored, ('grp', 'chip', 'core'), pairs))  5.35 us
    reduce_sum x2, other arithmetic, normalize(): mean_square = jnp.mean(states_wide * states_wide, axis=-1, keepdims=True)  5.17 us
    convert_element_type x1, other arithmetic, normalize(): (states_wide * lax.rsqrt(mean_square + 1e-05) * gain).astype(jnp.bfloat16)  4.78 us
  transfers between devices with their start and end apart: 39, of which 18 were waited for; matrix products, arithmetic and copies ran while one was open for 32% of the time, Pallas kernels for 0%

profile of v3, /device:TPU:0, one launch (start us, length us, event | category | flops | bytes accessed | tf_op | source)
XLA Modules:
  0.0 134.2 jit_solution(14594053024334483685)
XLA Ops:
  0.5 2.0 %fusion.95 = (bf16[256,512]{1,0:T(8,128)(2,1)}, bf16[256,512]{1,0:T(8,128)(2,1)S(1)}) fusion(f32[1,256,1024]{2,1,0:T(8,128)} %param.8, s32[]{:T(128)S(6)} %select_n.249, s32[]{:T(128)S(6)} %select_n.247), kind=kLoop, calls=%fused_computation.102 | loop fusion | bytes 1048584 | tf_op jit(solution)/shard_map/convert_element_type | solution.py:82
  2.4 2.5 %collective-permute-start.6 = (bf16[256,512]{1,0:T(8,128)(2,1)S(1)}, bf16[256,512]{1,0:T(8,128)(2,1)}, u32[]{:S(2)}, u32[]{:S(2)}) collective-permute-start(bf16[256,512]{1,0:T(8,128)(2,1)S(1)} %get-tuple-element.30), channel_id=1, source_target_pairs={{0,2},{4,0},{8,4},{12,8},{14,12},{10,14},{6,10},{2,6},{1,3},{5,1},... | collective-permute-start | bytes 786440 | tf_op jit(solution)/shard_map/ppermute | solution.py:27
  9.2 2.6 %fusion = f32[3,128]{1,0:T(4,128)S(1)} fusion(bf16[1,3,128,4096]{3,2,1,0:T(8,128)(2,1)} %param.6), kind=kLoop, calls=%fused_computation.6 | loop fusion | flops 4718208 | bytes 3147264 | tf_op jit(solution)/shard_map/reduce_sum | solution.py:63
  12.9 2.1 %collective-permute-start.5 = (bf16[256,512]{1,0:T(8,128)(2,1)}, bf16[256,512]{1,0:T(8,128)(2,1)}, u32[]{:S(2)}, u32[]{:S(2)}) collective-permute-start(bf16[256,512]{1,0:T(8,128)(2,1)} %collective-permute-done.2), channel_id=1, source_target_pairs={{0,4},{4,8},{8,12},{12,14},{14,10},{10,6},{6,2},{2,0},{1,5},{5,9},... | collective-permute-start | bytes 786440 | tf_op jit(solution)/shard_map/ppermute | solution.py:27
  15.4 2.0 %collective-permute-start.10 = (bf16[256,512]{1,0:T(8,128)(2,1)}, bf16[256,512]{1,0:T(8,128)(2,1)}, u32[]{:S(2)}, u32[]{:S(2)}) collective-permute-start(bf16[256,512]{1,0:T(8,128)(2,1)} %collective-permute-done.6), channel_id=1, source_target_pairs={{0,2},{4,0},{8,4},{12,8},{14,12},{10,14},{6,10},{2,6},{1,3},{5,1},... | collective-permute-start | bytes 786440 | tf_op jit(solution)/shard_map/ppermute | solution.py:27
  17.5 4.9 %collective-permute-done.5 = bf16[256,512]{1,0:T(8,128)(2,1)} collective-permute-done((bf16[256,512]{1,0:T(8,128)(2,1)}, bf16[256,512]{1,0:T(8,128)(2,1)}, u32[]{:S(2)}, u32[]{:S(2)}) %collective-permute-start.5) | collective-permute-done | bytes 262176 | tf_op jit(solution)/shard_map/ppermute | solution.py:27
  22.4 2.1 %collective-permute-start.9 = (bf16[256,512]{1,0:T(8,128)(2,1)}, bf16[256,512]{1,0:T(8,128)(2,1)}, u32[]{:S(2)}, u32[]{:S(2)}) collective-permute-start(bf16[256,512]{1,0:T(8,128)(2,1)} %collective-permute-done.5), channel_id=1, source_target_pairs={{0,4},{4,8},{8,12},{12,14},{14,10},{10,6},{6,2},{2,0},{1,5},{5,9},... | collective-permute-start | bytes 786440 | tf_op jit(solution)/shard_map/ppermute | solution.py:27
  24.5 2.6 %fusion.3 = f32[3,128]{1,0:T(4,128)S(1)} fusion(bf16[3,128,4096]{2,1,0:T(8,128)(2,1)} %collective-permute-done), kind=kLoop, calls=%fused_computation.9 | loop fusion | flops 4718208 | bytes 3147264 | tf_op jit(solution)/shard_map/reduce_sum | solution.py:63
  27.1 4.8 %fusion.2 = (bf16[3,128,4096]{2,1,0:T(8,128)(2,1)S(1)}, bf16[3,128,4096]{2,1,0:T(8,128)(2,1)}) fusion(f32[4096]{0:T(1024)S(1)} %copy-done.4, f32[3,128]{1,0:T(4,128)S(1)} %add_rsqrt_fusion.1, bf16[1,3,128,4096]{3,2,1,0:T(8,128)(2,1)S(1)} %copy-done.2, f32[3,128]{1,0:T(4,128)S(1)} %add_rsqrt_fusion, bf16[3,128,4096]{2,1,0:T(8,128)(2,1)} %collective-permute-done), kind=kLoop, calls=%fused_computation.8 | loop fusion | flops 12582912 | bytes 12602368 | tf_op jit(solution)/shard_map/convert_element_type | solution.py:64
  32.0 3.9 %collective-permute-start.17 = (bf16[256,1024]{1,0:T(8,128)(2,1)S(1)}, bf16[256,1024]{1,0:T(8,128)(2,1)S(1)}, u32[]{:S(2)}, u32[]{:S(2)}) collective-permute-start(bf16[256,1024]{1,0:T(8,128)(2,1)S(1)} %convert_element_type.144), channel_id=1, source_target_pairs={{0,16},{1,17},{2,18},{3,19},{4,20},{5,21},{6,22},{7,23},{8,24},{9,... | collective-permute-start | bytes 1572872 | tf_op jit(solution)/shard_map/ppermute | solution.py:87
  35.9 2.4 %pad_maximum_fusion = bf16[6,128,4096]{2,1,0:T(8,128)(2,1)S(1)} fusion(bf16[3,128,4096]{2,1,0:T(8,128)(2,1)} %get-tuple-element.40, bf16[3,128,4096]{2,1,0:T(8,128)(2,1)S(1)} %get-tuple-element.15), kind=kLoop, calls=%fused_computation.12 | loop fusion | flops 3145728 | bytes 12582912 | tf_op jit(solution)/shard_map/concatenate | solution.py:88
  44.4 1.5 %add_add_fusion.1 = f32[768,512]{1,0:T(8,128)S(1)} fusion(f32[768,512]{1,0:T(8,128)S(1)} %fusion.62, f32[768,512]{1,0:T(8,128)S(1)} %fusion.76, f32[768,512]{1,0:T(8,128)S(1)} %fusion.82, f32[768,512]{1,0:T(8,128)S(1)} %fusion.92, f32[768,512]{1,0:T(8,128)S(1)} %fusion.88, bf16[256,512]{1,0:T(8,128)(2,1)} %collective-permute-done.5, ...), kind=kOutput, calls=%fused_computation.19 | convolution fusion | flops 203292672 | bytes 10092548 | tf_op jit(solution)/shard_map/dot_general | solution.py:102
  45.9 1.6 %collective-permute-start.11 = (bf16[256,512]{1,0:T(8,128)(2,1)}, bf16[256,512]{1,0:T(8,128)(2,1)S(1)}, u32[]{:S(2)}, u32[]{:S(2)}) collective-permute-start(bf16[256,512]{1,0:T(8,128)(2,1)} %collective-permute-done.7), channel_id=1, source_target_pairs={{0,4},{4,8},{8,12},{12,14},{14,10},{10,6},{6,2},{2,0},{1,5},{5,9},... | collective-permute-start | bytes 786440 | tf_op jit(solution)/shard_map/ppermute | solution.py:27
  48.0 1.6 %collective-permute-start.13 = (bf16[256,512]{1,0:T(8,128)(2,1)}, bf16[256,512]{1,0:T(8,128)(2,1)S(1)}, u32[]{:S(2)}, u32[]{:S(2)}) collective-permute-start(bf16[256,512]{1,0:T(8,128)(2,1)} %collective-permute-done.9), channel_id=1, source_target_pairs={{0,4},{4,8},{8,12},{12,14},{14,10},{10,6},{6,2},{2,0},{1,5},{5,9},... | collective-permute-start | bytes 786440 | tf_op jit(solution)/shard_map/ppermute | solution.py:27
  54.0 1.5 %add_add_fusion = f32[768,512]{1,0:T(8,128)S(1)} fusion(f32[768,512]{1,0:T(8,128)S(1)} %fusion.36, f32[768,512]{1,0:T(8,128)S(1)} %fusion.50, f32[768,512]{1,0:T(8,128)S(1)} %add_add_fusion.1, f32[768,512]{1,0:T(8,128)S(1)} %fusion.56, bf16[256,512]{1,0:T(8,128)(2,1)} %collective-permute-done.9, bf16[768,4096]{1,0:T(8,128)(2,1)S(1)} %bitcast.88, ...), kind=kOutput, calls=%fused_computation.18 | convolution fusion | flops 202899456 | bytes 8519684 | tf_op jit(solution)/shard_map/dot_general | solution.py:102
  55.9 1.6 %collective-permute-start.15 = (bf16[256,512]{1,0:T(8,128)(2,1)S(1)}, bf16[256,512]{1,0:T(8,128)(2,1)S(1)}, u32[]{:S(2)}, u32[]{:S(2)}) collective-permute-start(bf16[256,512]{1,0:T(8,128)(2,1)S(1)} %collective-permute-done.11), channel_id=1, source_target_pairs={{0,4},{4,8},{8,12},{12,14},{14,10},{10,6},{6,2},{2,0},{1,5},{5,9},... | collective-permute-start | bytes 786440 | tf_op jit(solution)/shard_map/ppermute | solution.py:27
  58.7 2.8 %collective-permute-done.14 = bf16[256,512]{1,0:T(8,128)(2,1)S(1)} collective-permute-done((bf16[256,512]{1,0:T(8,128)(2,1)}, bf16[256,512]{1,0:T(8,128)(2,1)S(1)}, u32[]{:S(2)}, u32[]{:S(2)}) %collective-permute-start.14) | collective-permute-done | bytes 262176 | tf_op jit(solution)/shard_map/ppermute | solution.py:27
  72.2 2.9 %collective-permute-done.22 = bf16[6,1024]{1,0:T(8,128)(2,1)S(1)} collective-permute-done((bf16[6,1024]{1,0:T(8,128)(2,1)S(1)}, bf16[6,1024]{1,0:T(8,128)(2,1)S(1)}, u32[]{:S(2)}, u32[]{:S(2)}) %collective-permute-start.22) | collective-permute-done | bytes 12320 | tf_op jit(solution)/shard_map/ppermute | solution.py:47
  76.1 2.3 %collective-permute-done.19 = bf16[6,1024]{1,0:T(8,128)(2,1)S(1)} collective-permute-done((bf16[6,1024]{1,0:T(8,128)(2,1)S(1)}, bf16[6,1024]{1,0:T(8,128)(2,1)S(1)}, u32[]{:S(2)}, u32[]{:S(2)}) %collective-permute-start.19) | collective-permute-done | bytes 12320 | tf_op jit(solution)/shard_map/ppermute | solution.py:47
  81.9 1.5 %convolution_convert_fusion.1 = bf16[256,512]{1,0:T(8,128)(2,1)S(1)} fusion(bf16[768,512]{1,0:T(8,128)(2,1)S(1)} %fusion.7, bf16[768,4096]{1,0:T(8,128)(2,1)} %bitcast.95, s32[]{:T(128)S(6)} %select_n.265), kind=kOutput, calls=%fused_computation.21 | convolution fusion | flops 201457664 | bytes 1441796 | tf_op jit(solution)/shard_map/dot_general | solution.py:171
  86.8 2.1 %collective-permute-start.34 = (bf16[256,512]{1,0:T(8,128)(2,1)S(1)}, bf16[256,512]{1,0:T(8,128)(2,1)S(1)}, u32[]{:S(2)}, u32[]{:S(2)}) collective-permute-start(bf16[256,512]{1,0:T(8,128)(2,1)S(1)} %convolution_convert_fusion), channel_id=1, source_target_pairs={{0,2},{4,0},{8,4},{12,8},{14,12},{10,14},{6,10},{2,6},{1,3},{5,1},... | collective-permute-start | bytes 786440 | tf_op jit(solution)/shard_map/ppermute | solution.py:27
  91.4 4.1 %collective-permute-done.24 = bf16[256,512]{1,0:T(8,128)(2,1)S(1)} collective-permute-done((bf16[256,512]{1,0:T(8,128)(2,1)S(1)}, bf16[256,512]{1,0:T(8,128)(2,1)S(1)}, u32[]{:S(2)}, u32[]{:S(2)}) %collective-permute-start.24) | collective-permute-done | bytes 262176 | tf_op jit(solution)/shard_map/ppermute | solution.py:27
  96.5 2.0 %collective-permute-start.35 = (bf16[256,512]{1,0:T(8,128)(2,1)S(1)}, bf16[256,512]{1,0:T(8,128)(2,1)S(1)}, u32[]{:S(2)}, u32[]{:S(2)}) collective-permute-start(bf16[256,512]{1,0:T(8,128)(2,1)S(1)} %add_convert_fusion.2), channel_id=1, source_target_pairs={{0,2},{4,0},{8,4},{12,8},{14,12},{10,14},{6,10},{2,6},{1,3},{5,1},... | collective-permute-start | bytes 786440 | tf_op jit(solution)/shard_map/ppermute | solution.py:27
  98.5 3.1 %collective-permute-done.28 = bf16[256,512]{1,0:T(8,128)(2,1)S(1)} collective-permute-done((bf16[256,512]{1,0:T(8,128)(2,1)S(1)}, bf16[256,512]{1,0:T(8,128)(2,1)S(1)}, u32[]{:S(2)}, u32[]{:S(2)}) %collective-permute-start.28) | collective-permute-done | bytes 262176 | tf_op jit(solution)/shard_map/ppermute | solution.py:27
  102.1 2.1 %collective-permute-start.29 = (bf16[256,512]{1,0:T(8,128)(2,1)S(1)}, bf16[256,512]{1,0:T(8,128)(2,1)S(1)}, u32[]{:S(2)}, u32[]{:S(2)}) collective-permute-start(bf16[256,512]{1,0:T(8,128)(2,1)S(1)} %add_convert_fusion.6), channel_id=1, source_target_pairs={{0,2},{4,0},{8,4},{12,8},{14,12},{10,14},{6,10},{2,6},{1,3},{5,1},... | collective-permute-start | bytes 786440 | tf_op jit(solution)/shard_map/ppermute | solution.py:27
  105.2 2.0 %collective-permute-done.35 = bf16[256,512]{1,0:T(8,128)(2,1)S(1)} collective-permute-done((bf16[256,512]{1,0:T(8,128)(2,1)S(1)}, bf16[256,512]{1,0:T(8,128)(2,1)S(1)}, u32[]{:S(2)}, u32[]{:S(2)}) %collective-permute-start.35) | collective-permute-done | bytes 262176 | tf_op jit(solution)/shard_map/ppermute | solution.py:27
  107.7 2.1 %collective-permute-start.36 = (bf16[256,512]{1,0:T(8,128)(2,1)S(1)}, bf16[256,512]{1,0:T(8,128)(2,1)S(1)}, u32[]{:S(2)}, u32[]{:S(2)}) collective-permute-start(bf16[256,512]{1,0:T(8,128)(2,1)S(1)} %add_convert_fusion.1), channel_id=1, source_target_pairs={{0,2},{4,0},{8,4},{12,8},{14,12},{10,14},{6,10},{2,6},{1,3},{5,1},... | collective-permute-start | bytes 786440 | tf_op jit(solution)/shard_map/ppermute | solution.py:27
  110.8 1.8 %collective-permute-done.32 = bf16[256,512]{1,0:T(8,128)(2,1)S(1)} collective-permute-done((bf16[256,512]{1,0:T(8,128)(2,1)S(1)}, bf16[256,512]{1,0:T(8,128)(2,1)S(1)}, u32[]{:S(2)}, u32[]{:S(2)}) %collective-permute-start.32) | collective-permute-done | bytes 262176 | tf_op jit(solution)/shard_map/ppermute | solution.py:27
  113.4 4.6 %collective-permute-done.36 = bf16[256,512]{1,0:T(8,128)(2,1)S(1)} collective-permute-done((bf16[256,512]{1,0:T(8,128)(2,1)S(1)}, bf16[256,512]{1,0:T(8,128)(2,1)S(1)}, u32[]{:S(2)}, u32[]{:S(2)}) %collective-permute-start.36) | collective-permute-done | bytes 262176 | tf_op jit(solution)/shard_map/ppermute | solution.py:27
  118.3 1.8 %collective-permute-start.37 = (bf16[256,512]{1,0:T(8,128)(2,1)S(1)}, bf16[256,512]{1,0:T(8,128)(2,1)S(1)}, u32[]{:S(2)}, u32[]{:S(2)}) collective-permute-start(bf16[256,512]{1,0:T(8,128)(2,1)S(1)} %add_convert_fusion), channel_id=1, source_target_pairs={{0,2},{4,0},{8,4},{12,8},{14,12},{10,14},{6,10},{2,6},{1,3},{5,1},... | collective-permute-start | bytes 786440 | tf_op jit(solution)/shard_map/ppermute | solution.py:27
  123.8 4.4 %collective-permute-done.37 = bf16[256,512]{1,0:T(8,128)(2,1)S(1)} collective-permute-done((bf16[256,512]{1,0:T(8,128)(2,1)S(1)}, bf16[256,512]{1,0:T(8,128)(2,1)S(1)}, u32[]{:S(2)}, u32[]{:S(2)}) %collective-permute-start.37) | collective-permute-done | bytes 262176 | tf_op jit(solution)/shard_map/ppermute | solution.py:27
  129.8 2.9 %collective-permute-done.30 = bf16[256,512]{1,0:T(8,128)(2,1)S(1)} collective-permute-done((bf16[256,512]{1,0:T(8,128)(2,1)S(1)}, bf16[256,512]{1,0:T(8,128)(2,1)S(1)}, u32[]{:S(2)}, u32[]{:S(2)}) %collective-permute-start.30) | collective-permute-done | bytes 262176 | tf_op jit(solution)/shard_map/ppermute | solution.py:27
  (147 shorter events, 51.3 us)
Async XLA Ops:
  0.0 24.5 %collective-permute-start = (bf16[3,128,4096]{2,1,0:T(8,128)(2,1)}, bf16[3,128,4096]{2,1,0:T(8,128)(2,1)}, u32[]{:S(2)}, u32[]{:S(2)}) collective-permute-start(bf16[3,128,4096]{2,1,0:T(8,128)(2,1)} %bitcast.112), channel_id=1, source_target_pairs={{0,1},{1,0},{2,3},{3,2},{4,5},{5,4},{6,7},{7,6},{8,9},{9,8},{10,11... | collective-permute-start | bytes 9437192 | tf_op jit(solution)/shard_map/ppermute | solution.py:35
  2.4 13.0 %collective-permute-start.6 = (bf16[256,512]{1,0:T(8,128)(2,1)S(1)}, bf16[256,512]{1,0:T(8,128)(2,1)}, u32[]{:S(2)}, u32[]{:S(2)}) collective-permute-start(bf16[256,512]{1,0:T(8,128)(2,1)S(1)} %get-tuple-element.30), channel_id=1, source_target_pairs={{0,2},{4,0},{8,4},{12,8},{14,12},{10,14},{6,10},{2,6},{1,3},{5,1},... | collective-permute-start | bytes 786440 | tf_op jit(solution)/shard_map/ppermute | solution.py:27
  5.0 12.4 %collective-permute-start.3 = (bf16[256,512]{1,0:T(8,128)(2,1)S(1)}, bf16[256,512]{1,0:T(8,128)(2,1)}, u32[]{:S(2)}, u32[]{:S(2)}) collective-permute-start(bf16[256,512]{1,0:T(8,128)(2,1)S(1)} %get-tuple-element.30), channel_id=1, source_target_pairs={{0,4},{4,8},{8,12},{12,14},{14,10},{10,6},{6,2},{2,0},{1,5},{5,9},... | collective-permute-start | bytes 786440 | tf_op jit(solution)/shard_map/ppermute | solution.py:27
  12.9 9.5 %collective-permute-start.5 = (bf16[256,512]{1,0:T(8,128)(2,1)}, bf16[256,512]{1,0:T(8,128)(2,1)}, u32[]{:S(2)}, u32[]{:S(2)}) collective-permute-start(bf16[256,512]{1,0:T(8,128)(2,1)} %collective-permute-done.2), channel_id=1, source_target_pairs={{0,4},{4,8},{8,12},{12,14},{14,10},{10,6},{6,2},{2,0},{1,5},{5,9},... | collective-permute-start | bytes 786440 | tf_op jit(solution)/shard_map/ppermute | solution.py:27
  15.0 9.5 %collective-permute-start.4 = (bf16[256,512]{1,0:T(8,128)(2,1)}, bf16[256,512]{1,0:T(8,128)(2,1)}, u32[]{:S(2)}, u32[]{:S(2)}) collective-permute-start(bf16[256,512]{1,0:T(8,128)(2,1)} %collective-permute-done.2), channel_id=1, source_target_pairs={{0,2},{4,0},{8,4},{12,8},{14,12},{10,14},{6,10},{2,6},{1,3},{5,1},... | collective-permute-start | bytes 786440 | tf_op jit(solution)/shard_map/ppermute | solution.py:27
  15.4 30.5 %collective-permute-start.10 = (bf16[256,512]{1,0:T(8,128)(2,1)}, bf16[256,512]{1,0:T(8,128)(2,1)}, u32[]{:S(2)}, u32[]{:S(2)}) collective-permute-start(bf16[256,512]{1,0:T(8,128)(2,1)} %collective-permute-done.6), channel_id=1, source_target_pairs={{0,2},{4,0},{8,4},{12,8},{14,12},{10,14},{6,10},{2,6},{1,3},{5,1},... | collective-permute-start | bytes 786440 | tf_op jit(solution)/shard_map/ppermute | solution.py:27
  17.4 28.5 %collective-permute-start.7 = (bf16[256,512]{1,0:T(8,128)(2,1)}, bf16[256,512]{1,0:T(8,128)(2,1)}, u32[]{:S(2)}, u32[]{:S(2)}) collective-permute-start(bf16[256,512]{1,0:T(8,128)(2,1)} %collective-permute-done.3), channel_id=1, source_target_pairs={{0,4},{4,8},{8,12},{12,14},{14,10},{10,6},{6,2},{2,0},{1,5},{5,9},... | collective-permute-start | bytes 786440 | tf_op jit(solution)/shard_map/ppermute | solution.py:27
  22.4 23.5 %collective-permute-start.9 = (bf16[256,512]{1,0:T(8,128)(2,1)}, bf16[256,512]{1,0:T(8,128)(2,1)}, u32[]{:S(2)}, u32[]{:S(2)}) collective-permute-start(bf16[256,512]{1,0:T(8,128)(2,1)} %collective-permute-done.5), channel_id=1, source_target_pairs={{0,4},{4,8},{8,12},{12,14},{14,10},{10,6},{6,2},{2,0},{1,5},{5,9},... | collective-permute-start | bytes 786440 | tf_op jit(solution)/shard_map/ppermute | solution.py:27
  24.5 21.4 %collective-permute-start.8 = (bf16[256,512]{1,0:T(8,128)(2,1)}, bf16[256,512]{1,0:T(8,128)(2,1)}, u32[]{:S(2)}, u32[]{:S(2)}) collective-permute-start(bf16[256,512]{1,0:T(8,128)(2,1)} %collective-permute-done.4), channel_id=1, source_target_pairs={{0,2},{4,0},{8,4},{12,8},{14,12},{10,14},{6,10},{2,6},{1,3},{5,1},... | collective-permute-start | bytes 786440 | tf_op jit(solution)/shard_map/ppermute | solution.py:27
  32.0 33.4 %collective-permute-start.17 = (bf16[256,1024]{1,0:T(8,128)(2,1)S(1)}, bf16[256,1024]{1,0:T(8,128)(2,1)S(1)}, u32[]{:S(2)}, u32[]{:S(2)}) collective-permute-start(bf16[256,1024]{1,0:T(8,128)(2,1)S(1)} %convert_element_type.144), channel_id=1, source_target_pairs={{0,16},{1,17},{2,18},{3,19},{4,20},{5,21},{6,22},{7,23},{8,24},{9,... | collective-permute-start | bytes 1572872 | tf_op jit(solution)/shard_map/ppermute | solution.py:87
  45.9 9.9 %collective-permute-start.11 = (bf16[256,512]{1,0:T(8,128)(2,1)}, bf16[256,512]{1,0:T(8,128)(2,1)S(1)}, u32[]{:S(2)}, u32[]{:S(2)}) collective-permute-start(bf16[256,512]{1,0:T(8,128)(2,1)} %collective-permute-done.7), channel_id=1, source_target_pairs={{0,4},{4,8},{8,12},{12,14},{14,10},{10,6},{6,2},{2,0},{1,5},{5,9},... | collective-permute-start | bytes 786440 | tf_op jit(solution)/shard_map/ppermute | solution.py:27
  47.6 8.3 %collective-permute-start.12 = (bf16[256,512]{1,0:T(8,128)(2,1)}, bf16[256,512]{1,0:T(8,128)(2,1)S(1)}, u32[]{:S(2)}, u32[]{:S(2)}) collective-permute-start(bf16[256,512]{1,0:T(8,128)(2,1)} %collective-permute-done.8), channel_id=1, source_target_pairs={{0,2},{4,0},{8,4},{12,8},{14,12},{10,14},{6,10},{2,6},{1,3},{5,1},... | collective-permute-start | bytes 786440 | tf_op jit(solution)/shard_map/ppermute | solution.py:27
  48.0 13.8 %collective-permute-start.13 = (bf16[256,512]{1,0:T(8,128)(2,1)}, bf16[256,512]{1,0:T(8,128)(2,1)S(1)}, u32[]{:S(2)}, u32[]{:S(2)}) collective-permute-start(bf16[256,512]{1,0:T(8,128)(2,1)} %collective-permute-done.9), channel_id=1, source_target_pairs={{0,4},{4,8},{8,12},{12,14},{14,10},{10,6},{6,2},{2,0},{1,5},{5,9},... | collective-permute-start | bytes 786440 | tf_op jit(solution)/shard_map/ppermute | solution.py:27
  49.6 11.8 %collective-permute-start.14 = (bf16[256,512]{1,0:T(8,128)(2,1)}, bf16[256,512]{1,0:T(8,128)(2,1)S(1)}, u32[]{:S(2)}, u32[]{:S(2)}) collective-permute-start(bf16[256,512]{1,0:T(8,128)(2,1)} %collective-permute-done.10), channel_id=1, source_target_pairs={{0,2},{4,0},{8,4},{12,8},{14,12},{10,14},{6,10},{2,6},{1,3},{5,1},... | collective-permute-start | bytes 786440 | tf_op jit(solution)/shard_map/ppermute | solution.py:27
  55.9 7.1 %collective-permute-start.15 = (bf16[256,512]{1,0:T(8,128)(2,1)S(1)}, bf16[256,512]{1,0:T(8,128)(2,1)S(1)}, u32[]{:S(2)}, u32[]{:S(2)}) collective-permute-start(bf16[256,512]{1,0:T(8,128)(2,1)S(1)} %collective-permute-done.11), channel_id=1, source_target_pairs={{0,4},{4,8},{8,12},{12,14},{14,10},{10,6},{6,2},{2,0},{1,5},{5,9},... | collective-permute-start | bytes 786440 | tf_op jit(solution)/shard_map/ppermute | solution.py:27
  66.8 8.3 %collective-permute-start.22 = (bf16[6,1024]{1,0:T(8,128)(2,1)S(1)}, bf16[6,1024]{1,0:T(8,128)(2,1)S(1)}, u32[]{:S(2)}, u32[]{:S(2)}) collective-permute-start(bf16[6,1024]{1,0:T(8,128)(2,1)S(1)} %maximum_select_fusion.2), channel_id=1, source_target_pairs={{28,0},{19,1},{30,4},{17,5},{26,8},{21,9},{22,12},{25,13},{18,14},... | collective-permute-start | bytes 36872 | tf_op jit(solution)/shard_map/ppermute | solution.py:47
  68.1 7.5 %collective-permute-start.21 = (bf16[6,1024]{1,0:T(8,128)(2,1)S(1)}, bf16[6,1024]{1,0:T(8,128)(2,1)S(1)}, u32[]{:S(2)}, u32[]{:S(2)}) collective-permute-start(bf16[6,1024]{1,0:T(8,128)(2,1)S(1)} %maximum_select_fusion.2), channel_id=1, source_target_pairs={{24,0},{23,1},{28,4},{19,5},{30,8},{17,9},{26,12},{21,13},{22,14},... | collective-permute-start | bytes 36872 | tf_op jit(solution)/shard_map/ppermute | solution.py:47
  70.7 7.7 %collective-permute-start.19 = (bf16[6,1024]{1,0:T(8,128)(2,1)S(1)}, bf16[6,1024]{1,0:T(8,128)(2,1)S(1)}, u32[]{:S(2)}, u32[]{:S(2)}) collective-permute-start(bf16[6,1024]{1,0:T(8,128)(2,1)S(1)} %maximum_select_fusion.2), channel_id=1, source_target_pairs={{16,0},{31,1},{20,4},{27,5},{24,8},{23,9},{28,12},{19,13},{30,14},... | collective-permute-start | bytes 36872 | tf_op jit(solution)/shard_map/ppermute | solution.py:47
  86.3 9.2 %collective-permute-start.24 = (bf16[256,512]{1,0:T(8,128)(2,1)S(1)}, bf16[256,512]{1,0:T(8,128)(2,1)S(1)}, u32[]{:S(2)}, u32[]{:S(2)}) collective-permute-start(bf16[256,512]{1,0:T(8,128)(2,1)S(1)} %convolution_convert_fusion.3), channel_id=1, source_target_pairs={{0,4},{4,8},{8,12},{12,14},{14,10},{10,6},{6,2},{2,0},{1,5},{5,9},... | collective-permute-start | bytes 786440 | tf_op jit(solution)/shard_map/ppermute | solution.py:27
  86.8 9.2 %collective-permute-start.34 = (bf16[256,512]{1,0:T(8,128)(2,1)S(1)}, bf16[256,512]{1,0:T(8,128)(2,1)S(1)}, u32[]{:S(2)}, u32[]{:S(2)}) collective-permute-start(bf16[256,512]{1,0:T(8,128)(2,1)S(1)} %convolution_convert_fusion), channel_id=1, source_target_pairs={{0,2},{4,0},{8,4},{12,8},{14,12},{10,14},{6,10},{2,6},{1,3},{5,1},... | collective-permute-start | bytes 786440 | tf_op jit(solution)/shard_map/ppermute | solution.py:27
  89.3 12.3 %collective-permute-start.28 = (bf16[256,512]{1,0:T(8,128)(2,1)S(1)}, bf16[256,512]{1,0:T(8,128)(2,1)S(1)}, u32[]{:S(2)}, u32[]{:S(2)}) collective-permute-start(bf16[256,512]{1,0:T(8,128)(2,1)S(1)} %convolution_convert_fusion.2), channel_id=1, source_target_pairs={{0,2},{4,0},{8,4},{12,8},{14,12},{10,14},{6,10},{2,6},{1,3},{5,1},... | collective-permute-start | bytes 786440 | tf_op jit(solution)/shard_map/ppermute | solution.py:27
  90.7 13.4 %collective-permute-start.31 = (bf16[256,512]{1,0:T(8,128)(2,1)S(1)}, bf16[256,512]{1,0:T(8,128)(2,1)S(1)}, u32[]{:S(2)}, u32[]{:S(2)}) collective-permute-start(bf16[256,512]{1,0:T(8,128)(2,1)S(1)} %convolution_convert_fusion.1), channel_id=1, source_target_pairs={{0,4},{4,8},{8,12},{12,14},{14,10},{10,6},{6,2},{2,0},{1,5},{5,9},... | collective-permute-start | bytes 786440 | tf_op jit(solution)/shard_map/ppermute | solution.py:27
  96.0 13.8 %collective-permute-start.25 = (bf16[256,512]{1,0:T(8,128)(2,1)S(1)}, bf16[256,512]{1,0:T(8,128)(2,1)S(1)}, u32[]{:S(2)}, u32[]{:S(2)}) collective-permute-start(bf16[256,512]{1,0:T(8,128)(2,1)S(1)} %add_convert_fusion.9), channel_id=1, source_target_pairs={{0,4},{4,8},{8,12},{12,14},{14,10},{10,6},{6,2},{2,0},{1,5},{5,9},... | collective-permute-start | bytes 786440 | tf_op jit(solution)/shard_map/ppermute | solution.py:27
  96.5 10.8 %collective-permute-start.35 = (bf16[256,512]{1,0:T(8,128)(2,1)S(1)}, bf16[256,512]{1,0:T(8,128)(2,1)S(1)}, u32[]{:S(2)}, u32[]{:S(2)}) collective-permute-start(bf16[256,512]{1,0:T(8,128)(2,1)S(1)} %add_convert_fusion.2), channel_id=1, source_target_pairs={{0,2},{4,0},{8,4},{12,8},{14,12},{10,14},{6,10},{2,6},{1,3},{5,1},... | collective-permute-start | bytes 786440 | tf_op jit(solution)/shard_map/ppermute | solution.py:27
  102.1 18.0 %collective-permute-start.29 = (bf16[256,512]{1,0:T(8,128)(2,1)S(1)}, bf16[256,512]{1,0:T(8,128)(2,1)S(1)}, u32[]{:S(2)}, u32[]{:S(2)}) collective-permute-start(bf16[256,512]{1,0:T(8,128)(2,1)S(1)} %add_convert_fusion.6), channel_id=1, source_target_pairs={{0,2},{4,0},{8,4},{12,8},{14,12},{10,14},{6,10},{2,6},{1,3},{5,1},... | collective-permute-start | bytes 786440 | tf_op jit(solution)/shard_map/ppermute | solution.py:27
  104.6 8.1 %collective-permute-start.32 = (bf16[256,512]{1,0:T(8,128)(2,1)S(1)}, bf16[256,512]{1,0:T(8,128)(2,1)S(1)}, u32[]{:S(2)}, u32[]{:S(2)}) collective-permute-start(bf16[256,512]{1,0:T(8,128)(2,1)S(1)} %add_convert_fusion.4), channel_id=1, source_target_pairs={{0,4},{4,8},{8,12},{12,14},{14,10},{10,6},{6,2},{2,0},{1,5},{5,9},... | collective-permute-start | bytes 786440 | tf_op jit(solution)/shard_map/ppermute | solution.py:27
  107.7 10.3 %collective-permute-start.36 = (bf16[256,512]{1,0:T(8,128)(2,1)S(1)}, bf16[256,512]{1,0:T(8,128)(2,1)S(1)}, u32[]{:S(2)}, u32[]{:S(2)}) collective-permute-start(bf16[256,512]{1,0:T(8,128)(2,1)S(1)} %add_convert_fusion.1), channel_id=1, source_target_pairs={{0,2},{4,0},{8,4},{12,8},{14,12},{10,14},{6,10},{2,6},{1,3},{5,1},... | collective-permute-start | bytes 786440 | tf_op jit(solution)/shard_map/ppermute | solution.py:27
  110.2 11.6 %collective-permute-start.26 = (bf16[256,512]{1,0:T(8,128)(2,1)S(1)}, bf16[256,512]{1,0:T(8,128)(2,1)S(1)}, u32[]{:S(2)}, u32[]{:S(2)}) collective-permute-start(bf16[256,512]{1,0:T(8,128)(2,1)S(1)} %add_convert_fusion.8), channel_id=1, source_target_pairs={{0,4},{4,8},{8,12},{12,14},{14,10},{10,6},{6,2},{2,0},{1,5},{5,9},... | collective-permute-start | bytes 786440 | tf_op jit(solution)/shard_map/ppermute | solution.py:27
  113.1 10.7 %collective-permute-start.33 = (bf16[256,512]{1,0:T(8,128)(2,1)S(1)}, bf16[256,512]{1,0:T(8,128)(2,1)S(1)}, u32[]{:S(2)}, u32[]{:S(2)}) collective-permute-start(bf16[256,512]{1,0:T(8,128)(2,1)S(1)} %add_convert_fusion.3), channel_id=1, source_target_pairs={{0,4},{4,8},{8,12},{12,14},{14,10},{10,6},{6,2},{2,0},{1,5},{5,9},... | collective-permute-start | bytes 786440 | tf_op jit(solution)/shard_map/ppermute | solution.py:27
  118.3 9.8 %collective-permute-start.37 = (bf16[256,512]{1,0:T(8,128)(2,1)S(1)}, bf16[256,512]{1,0:T(8,128)(2,1)S(1)}, u32[]{:S(2)}, u32[]{:S(2)}) collective-permute-start(bf16[256,512]{1,0:T(8,128)(2,1)S(1)} %add_convert_fusion), channel_id=1, source_target_pairs={{0,2},{4,0},{8,4},{12,8},{14,12},{10,14},{6,10},{2,6},{1,3},{5,1},... | collective-permute-start | bytes 786440 | tf_op jit(solution)/shard_map/ppermute | solution.py:27
  120.6 12.1 %collective-permute-start.30 = (bf16[256,512]{1,0:T(8,128)(2,1)S(1)}, bf16[256,512]{1,0:T(8,128)(2,1)S(1)}, u32[]{:S(2)}, u32[]{:S(2)}) collective-permute-start(bf16[256,512]{1,0:T(8,128)(2,1)S(1)} %add_convert_fusion.5), channel_id=1, source_target_pairs={{0,2},{4,0},{8,4},{12,8},{14,12},{10,14},{6,10},{2,6},{1,3},{5,1},... | collective-permute-start | bytes 786440 | tf_op jit(solution)/shard_map/ppermute | solution.py:27
  122.9 9.8 %collective-permute-start.27 = (bf16[256,512]{1,0:T(8,128)(2,1)}, bf16[256,512]{1,0:T(8,128)(2,1)S(1)}, u32[]{:S(2)}, u32[]{:S(2)}) collective-permute-start(bf16[256,512]{1,0:T(8,128)(2,1)} %add_convert_fusion.7), channel_id=1, source_target_pairs={{0,4},{4,8},{8,12},{12,14},{14,10},{10,6},{6,2},{2,0},{1,5},{5,9},... | collective-permute-start | bytes 786440 | tf_op jit(solution)/shard_map/ppermute | solution.py:27
  (13 other events, 110.1 us)

commit v4 on v3

--- a/solution.py
+++ b/solution.py
@@ -1,11 +1,16 @@
+import functools
+
 import jax
 import jax.numpy as jnp
 from jax import lax
+from jax.experimental import pallas as pl
+from jax.experimental.pallas import tpu as pltpu
 from jax.sharding import Mesh, PartitionSpec as P
 
 sharpness = 20.0
 cores = 2
 longest_ring = 16
+vmem_limit = 32 << 20
 
 
 def ring_order(chips):
@@ -58,10 +63,104 @@
     )
 
 
-def normalize(states, gain):
-    states_wide = states.astype(jnp.float32)
-    mean_square = jnp.mean(states_wide * states_wide, axis=-1, keepdims=True)
-    return (states_wide * lax.rsqrt(mean_square + 1e-05) * gain).astype(jnp.bfloat16)
+def normalize_kernel(seqs, chunk, mine_ref, other_ref, gain_ref, out_ref):
+    length = mine_ref.shape[1]
+
+    def run(ref):
+        @pl.loop(0, length // chunk)
+        def _(i):
+            at = pl.ds(pl.multiple_of(i * chunk, chunk), chunk)
+            wide = ref[0, at, :].astype(jnp.float32)
+            mean_square = jnp.mean(wide * wide, axis=-1, keepdims=True)
+            wide = wide * lax.rsqrt(mean_square + 1e-05) * gain_ref[...]
+            out_ref[at, :] = wide.astype(jnp.bfloat16)
+
+    @pl.when(pl.program_id(0) < seqs)
+    def _():
+        run(mine_ref)
+
+    @pl.when(pl.program_id(0) >= seqs)
+    def _():
+        run(other_ref)
+
+
+def normalize_both(mine, other, gain):
+    seqs, length, width = mine.shape
+    tokens = 2 * seqs * length
+    return pl.pallas_call(
+        functools.partial(normalize_kernel, seqs, 16),
+        grid=(2 * seqs,),
+        in_specs=[
+            pl.BlockSpec((1, length, width), lambda i: (jnp.minimum(i, seqs - 1), 0, 0)),
+            pl.BlockSpec((1, length, width), lambda i: (jnp.maximum(i - seqs, 0), 0, 0)),
+            pl.BlockSpec((1, width), lambda i: (0, 0)),
+        ],
+        out_specs=pl.BlockSpec((length, width), lambda i: (i, 0)),
+        out_shape=jax.ShapeDtypeStruct((tokens, width), jnp.bfloat16),
+        compiler_params=pltpu.CompilerParams(vmem_limit_bytes=vmem_limit),
+        cost_estimate=pl.CostEstimate(
+            flops=6 * tokens * width, bytes_accessed=4 * tokens * width, transcendentals=tokens
+        ),
+    )(mine, other, gain[None])
+
+
+def blocks_kernel(amount, has_total, last, length, offsets_ref, counts_ref, *refs):
+    columns, blocks, rest = refs[:amount], refs[amount : 2 * amount], refs[2 * amount :]
+    total = None
+    for column, block in zip(columns, blocks):
+        term = jnp.dot(column[...], block[...], preferred_element_type=jnp.float32)
+        total = term if total is None else total + term
+    if has_total:
+        total = total + rest[0][...]
+        rest = rest[1:]
+    if not last:
+        rest[0][...] = total
+        return
+    slope_ref, pooled_ref = rest
+    active = jnp.tanh(total)
+    seqs = active.shape[0] // length
+    active = active.reshape(seqs, length, active.shape[1])
+    for i in range(seqs):
+        count = counts_ref[pl.program_id(0) * seqs + i]
+        there = lax.broadcasted_iota(jnp.int32, active.shape[1:], 0) < count
+        part = jnp.where(there, active[i], 0.0)
+        pooled_ref[i] = jnp.sum(part, axis=0, keepdims=True)
+        slope_ref[pl.ds(i * length, length), :] = jnp.where(there, 1.0 - part * part, 0.0)
+
+
+def add_blocks(normed, offsets, blocks, total, counts, length, last):
+    tokens = normed.shape[0]
+    rows, half = blocks[0].shape
+    amount = len(blocks)
+    tile = 2 * length if tokens % (2 * length) == 0 else length
+    in_specs = [
+        pl.BlockSpec((tile, rows), lambda i, offsets, counts, b=b: (i, offsets[b]))
+        for b in range(amount)
+    ]
+    in_specs += [pl.BlockSpec((rows, half), lambda i, offsets, counts: (0, 0))] * amount
+    operands = [normed] * amount + list(blocks)
+    whole = pl.BlockSpec((tile, half), lambda i, offsets, counts: (i, 0))
+    if total is not None:
+        in_specs.append(whole)
+        operands.append(total)
+    out_specs = whole
+    out_shape = jax.ShapeDtypeStruct((tokens, half), jnp.float32)
+    if last:
+        out_specs = [whole, pl.BlockSpec((tile // length, 1, half), lambda i, offsets, counts: (i, 0, 0))]
+        out_shape = [out_shape, jax.ShapeDtypeStruct((tokens // length, 1, half), jnp.float32)]
+    return pl.pallas_call(
+        functools.partial(blocks_kernel, amount, total is not None, last, length),
+        grid_spec=pltpu.PrefetchScalarGridSpec(
+            num_scalar_prefetch=2, grid=(tokens // tile,), in_specs=in_specs, out_specs=out_specs
+        ),
+        out_shape=out_shape,
+        compiler_params=pltpu.CompilerParams(vmem_limit_bytes=vmem_limit),
+        cost_estimate=pl.CostEstimate(
+            flops=2 * tokens * rows * half * amount,
+            bytes_accessed=2 * amount * rows * (tokens + half) + 8 * tokens * half,
+            transcendentals=tokens * half if last else 0,
+        ),
+    )(offsets, counts, *operands)
 
 
 def shards(token_states, token_ids, master, gain, cand_ids, slab_owner):
@@ -82,52 +181,51 @@
     given = given.astype(jnp.bfloat16)
     sibling = from_sibling(given)
 
-    normed = normalize(states, gain)
-    normed, weights = lax.optimization_barrier((normed, weights))
-    copied = lax.ppermute(weights.astype(jnp.bfloat16), "grp", [(0, 1)])
-    normed = jnp.concatenate([normed, normalize(from_sibling(states), gain)])
-    normed = normed.reshape(seqs * length, width)
+    normed = normalize_both(states, from_sibling(states), gain)
     ids = jnp.concatenate([token_ids[0], cand_ids], axis=1)
     ids = jnp.concatenate([ids, from_sibling(ids)])
-    valid = (ids[:, :length] != 0).astype(jnp.float32)
-    counts = jnp.sum(valid, axis=1)
-    weighted = valid / counts[:, None]
+    lengths = jnp.sum((ids[:, :length] != 0).astype(jnp.int32), axis=1)
+    counts = lengths.astype(jnp.float32)
     cands = ids[:, length:]
 
+    def first_column(offset, part):
+        return ring_chip(place + offset, chips) * cores + part
+
     def columns(offset, part):
-        first = (ring_chip(place + offset, chips) * cores + part) * rows
+        first = first_column(offset, part) * rows
         return lax.dynamic_slice(normed, (0, first), (seqs * length, rows))
-
-    def product(offset, part, block):
-        return jnp.dot(columns(offset, part), block, preferred_element_type=jnp.float32)
 
     parts = (core, 1 - core)
     if chips <= longest_ring:
         moving = {(i, by): block for by in (1, -1) for i, block in enumerate((own, sibling))}
         sums = [None]
+        blocks, offsets = [own, sibling], [first_column(0, part) for part in parts]
         for step in range(1, chips // 2 + 1):
-            sent = [(0, 1), (1, -1), (1, 1), (0, -1)]
-            if step == chips // 2:
-                sent = sent[:2]
-            if step == 1:
-                total = product(0, parts[0], own) + product(0, parts[1], sibling)
-            else:
-                total = sums[-1]
+            last = step == chips // 2
+            sent = [(0, 1), (1, -1)] if last else [(0, 1), (0, -1), (1, 1), (1, -1)]
             for i, by in sent:
-                if step > 2:
+                if step > 2 and i == 1:
                     moving[i, by] = after(sums[step - 2], moving[i, by])
                 moving[i, by] = along_ring(moving[i, by], by)
-                total = total + product(-by * step, parts[i], moving[i, by])
+                blocks.append(moving[i, by])
+                offsets.append(first_column(-by * step, parts[i]))
+            total = add_blocks(
+                normed, jnp.stack(offsets), blocks, sums[-1], lengths, length, last
+            )
             sums.append(total)
-        hidden = sums[-1]
+            blocks, offsets = [], []
+        slope, pooled = sums[-1]
+        pooled = pooled[:, 0] / counts[:, None]
     else:
         both = in_core_order(own, sibling, core)
         gathered = lax.all_gather(both, "chip", axis=0, tiled=True)
         hidden = jnp.dot(normed, gathered, preferred_element_type=jnp.float32)
-
-    active = jnp.tanh(hidden).reshape(seqs, length, half)
-    pooled = jnp.sum(active * valid[:, :, None], axis=1) / counts[:, None]
-    pooled, copied = lax.optimization_barrier((pooled, copied))
+        active = jnp.tanh(hidden).reshape(seqs, length, half)
+        there = jnp.arange(length)[None, :, None] < lengths[:, None, None]
+        active = jnp.where(there, active, 0.0)
+        pooled = jnp.sum(active, axis=1) / counts[:, None]
+        slope = jnp.where(there, 1.0 - active * active, 0.0).reshape(seqs * length, half)
+
     pooled_other = from_sibling(pooled)
     pooled_other = jnp.concatenate([pooled_other[seq_dev:], pooled_other[:seq_dev]])
     whole = in_core_order(pooled, pooled_other, core, axis=1)
@@ -137,37 +235,40 @@
     stored = unit.astype(jnp.bfloat16)
     stored = in_core_order(stored[:seq_dev], stored[seq_dev:], core)
 
-    devices_fsdp = chips * cores
-    owners = jnp.arange(devices_fsdp, dtype=jnp.int32)
-    onehot = (slab_owner[:, None] == owners[None, :]).astype(jnp.int32)
-    ranks = jnp.sum((jnp.cumsum(onehot, axis=0) - onehot) * onehot, axis=1)
-    places = slab_owner * seq_dev + ranks
-    wanted = places[cands]
     slab = jnp.concatenate(slab_blocks(stored, chips, core))
-    seen = lax.rem(ring_place(wanted // seqs, chips) - place + chips, chips)
-    wanted = seen * seqs + lax.rem(wanted, seqs)
-    chosen = slab[wanted].astype(jnp.float32)
+    slab_rows = slab.shape[0]
+    earlier = jnp.arange(slab_rows)[:, None] < jnp.arange(slab_rows)[None, :]
+    same = slab_owner[:, None] == slab_owner[None, :]
+    ranks = jnp.sum((earlier & same).astype(jnp.int32), axis=0)
+    owner_place = ring_place(slab_owner // cores, chips)
+    seen = lax.rem(owner_place - place + chips, chips)
+    slots = seen * seqs + lax.rem(slab_owner, cores) * seq_dev + ranks
+    positive, candidate = [
+        jnp.sum(
+            (slots[picked][:, :, None] == jnp.arange(slab_rows)).astype(jnp.float32), axis=1
+        )
+        for picked in (cands[:, :1], cands)
+    ]
+
+    slab_wide = slab.astype(jnp.float32)
     logits = (
-        sharpness
-        / embedding
-        * jnp.einsum("qe,qje->qj", unit, chosen, precision=lax.Precision.HIGHEST)
-    )
-    exponent = jnp.exp(logits)
+        sharpness / embedding * jnp.dot(unit, slab_wide.T, precision=lax.Precision.HIGHEST)
+    )
+    exponent = jnp.where(candidate > 0, jnp.exp(logits), 0.0)
     probs = exponent / jnp.sum(exponent, axis=-1, keepdims=True)
-    target = (jnp.arange(chosen.shape[1]) == 0).astype(jnp.float32)
-    logit_grad = probs - target[None, :]
+    logit_grad = probs - positive
     unit_grad = (
-        sharpness
-        / embedding
-        * jnp.einsum("qj,qje->qe", logit_grad, chosen, precision=lax.Precision.HIGHEST)
+        sharpness / embedding * jnp.dot(logit_grad, slab_wide, precision=lax.Precision.HIGHEST)
     )
     inner = jnp.sum(whole * unit_grad, axis=-1, keepdims=True)
     pooled_grad = scale * unit_grad - whole * (scale * scale * scale) * inner / embedding
     pooled_grad = lax.dynamic_slice(pooled_grad, (0, core * half), (seqs, half))
-    delta = weighted[:, :, None] * pooled_grad[:, None, :] * (1.0 - active * active)
+    delta = (pooled_grad / counts[:, None])[:, None, :] * slope.reshape(seqs, length, half)
     delta = delta.astype(jnp.bfloat16).reshape(seqs * length, half)
-
-    def term(offset, part):
+    delta, weights = lax.optimization_barrier((delta, weights))
+    copied = lax.ppermute(weights.astype(jnp.bfloat16), "grp", [(0, 1)])
+
+    def term(offset, part, delta):
         return lax.dot_general(
             columns(offset, part),
             delta,
@@ -177,16 +278,21 @@
 
     if chips <= longest_ring:
         arrived = {}
+        late = delta
         for step in range(chips // 2, 0, -1):
-            for i, by in ((1, -1), (0, 1), (1, 1), (0, -1)):
+            for i, by in ((0, 1), (1, -1), (1, 1), (0, -1)):
                 if step == chips // 2 and (i, by) not in ((0, 1), (1, -1)):
                     continue
-                total = term(by * step, parts[i])
+                total = term(by * step, parts[i], delta)
                 if (i, by) in arrived:
                     total = total + arrived[i, by].astype(jnp.float32)
+                if step == 1 and i == 0:
+                    total = after(copied, total)
                 arrived[i, by] = along_ring(total.astype(jnp.bfloat16), by)
+            if step == chips // 2:
+                late = after(arrived[0, 1], delta)
         mine, other = [
-            term(0, parts[i])
+            term(0, parts[i], late)
             + arrived[i, 1].astype(jnp.float32)
             + arrived[i, -1].astype(jnp.float32)
             for i in range(2)

time: 135 us -> 134 us (level)
  Pallas kernels: 0 us -> 21.6 us
  matrix products: 27.7 us -> 12 us
  other arithmetic: 18.6 us -> 6.84 us
  local copies, waits for them, and re-layouts: 4.54 us -> 14.2 us
  starting transfers between devices: 41.9 us -> 37.4 us
    pallas_call x0 -> x5, Pallas kernels: none -> 21.6 us  [the longest x4 14.4 us: add_blocks(): pl.pallas_call(functools.partial(blocks_kernel, amount, total is not None...]
    dot_general x18 -> x2, matrix products: 16.2 us -> 0.72 us  [the longest x1 0.36 us: shards(): jnp.dot(unit, slab_wide.T, precision=lax.Precision.HIGHEST)]
    unnamed x13 -> x17, local copies, waits for them, and re-layouts: 0.71 us -> 10.5 us
    reduce_sum x7 -> x3, other arithmetic: 6.56 us -> 1.03 us  [the longest x1 0.82 us: shards(): ranks = jnp.sum((earlier & same).astype(jnp.int32), axis=0)]
    convert_element_type x4 -> x2, other arithmetic: 5.51 us -> 0.08 us  [the longest x1 0.07 us: shards(): stored = unit.astype(jnp.bfloat16)]
    ppermute x1, starting transfers between devices: 3.87 us -> 1.32 us  [shards(): copied = lax.ppermute(weights.astype(jnp.bfloat16), 'grp', [(0, 1)])]
    concatenate x2 -> x0, other arithmetic: 2.44 us -> none  [the longest x1 2.43 us: shards(): normed = jnp.concatenate([normed, normalize(from_sibling(states), gain)])]
  transfers between devices with their start and end apart: 39 -> 39, of which waited for: 18 -> 15; matrix products, arithmetic and copies ran while one was open for 32% -> 14% of each run, Pallas kernels for 0% -> 14%
where the time goes in v4:
time: 134 us; the launch traced here: 133 us
  waiting for transfers between devices  40.1 us (30%)
  starting transfers between devices  37.4 us (28%)
  Pallas kernels  21.6 us (16%)
  local copies, waits for them, and re-layouts  14.2 us (11%)
  matrix products  12 us (9%)
  other arithmetic  6.84 us (5%)
    ppermute x28, waiting for transfers between devices, along_ring(): return lax.ppermute(block, 'chip', pairs)  31.5 us
    ppermute x28, starting transfers between devices, along_ring(): return lax.ppermute(block, 'chip', pairs)  29.8 us
    pallas_call x4, Pallas kernels, add_blocks(): pl.pallas_call(functools.partial(blocks_kernel, amount, total is not None...  14.4 us
    dot_general x16, matrix products, term(): lax.dot_general(columns(offset, part), delta, (((0,), (0,)), ((), ())), p...  11.3 us
    unnamed x17, local copies, waits for them, and re-layouts  10.5 us
    pallas_call x1, Pallas kernels, normalize_both(): pl.pallas_call(functools.partial(normalize_kernel, seqs, 16), grid=(2 * s...  7.2 us
    ppermute x4, waiting for transfers between devices, slab_blocks(): kept.append(lax.ppermute(stored, ('grp', 'chip', 'core'), pairs))  6.36 us
    ppermute x4, starting transfers between devices, slab_blocks(): kept.append(lax.ppermute(stored, ('grp', 'chip', 'core'), pairs))  5.16 us
  transfers between devices with their start and end apart: 39, of which 15 were waited for; matrix products, arithmetic and copies ran while one was open for 14% of the time, Pallas kernels for 14%

profile of v4, /device:TPU:0, one launch (start us, length us, event | category | flops | bytes accessed | tf_op | source)
XLA Modules:
  0.0 132.7 jit_solution(2342691371254714782)
XLA Ops:
  0.5 2.0 %fusion.30 = (bf16[256,512]{1,0:T(8,128)(2,1)}, bf16[256,512]{1,0:T(8,128)(2,1)S(1)}) fusion(f32[1,256,1024]{2,1,0:T(8,128)} %param.8, s32[]{:T(128)S(6)} %select_n.207, s32[]{:T(128)S(6)} %select_n.204), kind=kLoop, calls=%fused_computation.55 | loop fusion | bytes 1048584 | tf_op jit(solution)/shard_map/convert_element_type | solution.py:181
  2.4 2.6 %collective-permute-start.2 = (bf16[256,512]{1,0:T(8,128)(2,1)S(1)}, bf16[256,512]{1,0:T(8,128)(2,1)}, u32[]{:S(2)}, u32[]{:S(2)}) collective-permute-start(bf16[256,512]{1,0:T(8,128)(2,1)S(1)} %get-tuple-element.30.refs_6_), channel_id=1, source_target_pairs={{0,4},{4,8},{8,12},{12,14},{14,10},{10,6},{6,2},{2,0},{1,5},{5,9},... | collective-permute-start | bytes 786440 | tf_op jit(solution)/shard_map/ppermute | solution.py:32
  8.5 2.0 %collective-permute-start.11 = (bf16[256,512]{1,0:T(8,128)(2,1)}, bf16[256,512]{1,0:T(8,128)(2,1)}, u32[]{:S(2)}, u32[]{:S(2)}) collective-permute-start(bf16[256,512]{1,0:T(8,128)(2,1)} %collective-permute-done.8.refs_7_), channel_id=1, source_target_pairs={{0,2},{4,0},{8,4},{12,8},{14,12},{10,14},{6,10},{2,6},{1,3},{5,1},... | collective-permute-start | bytes 786440 | tf_op jit(solution)/shard_map/ppermute | solution.py:32
  12.0 1.9 %collective-permute-start.3 = (bf16[256,512]{1,0:T(8,128)(2,1)}, bf16[256,512]{1,0:T(8,128)(2,1)}, u32[]{:S(2)}, u32[]{:S(2)}) collective-permute-start(bf16[256,512]{1,0:T(8,128)(2,1)} %collective-permute-done.2.refs_8_), channel_id=1, source_target_pairs={{0,4},{4,8},{8,12},{12,14},{14,10},{10,6},{6,2},{2,0},{1,5},{5,9},... | collective-permute-start | bytes 786440 | tf_op jit(solution)/shard_map/ppermute | solution.py:32
  14.2 5.0 %collective-permute-done.11.refs_11_ = bf16[256,512]{1,0:T(8,128)(2,1)} collective-permute-done((bf16[256,512]{1,0:T(8,128)(2,1)}, bf16[256,512]{1,0:T(8,128)(2,1)}, u32[]{:S(2)}, u32[]{:S(2)}) %collective-permute-start.11) | collective-permute-done | bytes 262176 | tf_op jit(solution)/shard_map/ppermute | solution.py:32
  20.3 1.7 %collective-permute-start.7 = (bf16[256,512]{1,0:T(8,128)(2,1)}, bf16[256,512]{1,0:T(8,128)(2,1)}, u32[]{:S(2)}, u32[]{:S(2)}) collective-permute-start(bf16[256,512]{1,0:T(8,128)(2,1)} %collective-permute-done.6.refs_9_), channel_id=1, source_target_pairs={{0,2},{4,0},{8,4},{12,8},{14,12},{10,14},{6,10},{2,6},{1,3},{5,1},... | collective-permute-start | bytes 786440 | tf_op jit(solution)/shard_map/ppermute | solution.py:32
  22.3 2.7 %collective-permute-done.3.refs_4_ = bf16[256,512]{1,0:T(8,128)(2,1)} collective-permute-done((bf16[256,512]{1,0:T(8,128)(2,1)}, bf16[256,512]{1,0:T(8,128)(2,1)}, u32[]{:S(2)}, u32[]{:S(2)}) %collective-permute-start.3) | collective-permute-done | bytes 262176 | tf_op jit(solution)/shard_map/ppermute | solution.py:32
  25.8 1.9 %copy-done.4 = bf16[1,3,128,4096]{3,2,1,0:T(8,128)(2,1)S(1)} copy-done((bf16[1,3,128,4096]{3,2,1,0:T(8,128)(2,1)S(1)}, bf16[1,3,128,4096]{3,2,1,0:T(8,128)(2,1)}, u32[]{:S(2)}) %copy-start.4) | copy-done | bytes 3145752
  28.5 7.2 %shard_map.64.refs_0_.refs_1_.refs_2_.refs_3_.refs_4_.refs_5_ = bf16[768,4096]{1,0:T(8,128)(2,1)S(1)} custom-call(bf16[3,128,4096]{2,1,0:T(8,128)(2,1)S(1)} %bitcast.51, bf16[3,128,4096]{2,1,0:T(8,128)(2,1)S(1)} %collective-permute-done.other_ref, f32[1,4096]{1,0:T(1,128)S(1)} %bitcast.52), custom_call_target="tpu_custom_call" | custom-call | flops 18874368 | bytes 12582912 | tf_op jit(solution)/shard_map/pallas_call | solution.py:90
  35.7 4.9 %shard_map.65.refs_8_ = f32[768,512]{1,0:T(8,128)S(1)} custom-call(s32[6]{0:T(128)S(1)} %stack.74.offsets_ref, s32[6]{0:T(128)S(1)} %convert_reduce_fusion.2.counts_ref, bf16[768,4096]{1,0:T(8,128)(2,1)S(1)} %shard_map.64.refs_0_.refs_1_.refs_2_.refs_3_.refs_4_.refs_5_, bf16[768,4096]{1,0:T(8,128)(2,1)S(1)} %shard_map.64.refs_0_.refs_1_.refs_2_.refs_3_.refs_4_.refs_5_, ...), custom_call_target="tpu_custom_call" | custom-call | flops 1207959552 | bytes 7077888 | tf_op jit(solution)/shard_map/pallas_call | solution.py:151
  42.0 1.6 %collective-permute-start.15 = (bf16[256,512]{1,0:T(8,128)(2,1)}, bf16[256,512]{1,0:T(8,128)(2,1)}, u32[]{:S(2)}, u32[]{:S(2)}) collective-permute-start(bf16[256,512]{1,0:T(8,128)(2,1)} %collective-permute-done.7.refs_5_), channel_id=1, source_target_pairs={{0,2},{4,0},{8,4},{12,8},{14,12},{10,14},{6,10},{2,6},{1,3},{5,1},... | collective-permute-start | bytes 786440 | tf_op jit(solution)/shard_map/ppermute | solution.py:32
  44.9 2.8 %copy-done.1 = bf16[768,4096]{1,0:T(8,128)(2,1)S(1)} copy-done((bf16[768,4096]{1,0:T(8,128)(2,1)S(1)}, bf16[768,4096]{1,0:T(8,128)(2,1)}, u32[]{:S(2)}) %copy-start.1) | copy-done | bytes 6291480
  47.6 3.4 %shard_map.66.refs_8_ = f32[768,512]{1,0:T(8,128)S(1)} custom-call(s32[4]{0:T(128)S(1)} %pad_add_fusion.3.offsets_ref, s32[6]{0:T(128)S(1)} %convert_reduce_fusion.2.counts_ref, bf16[768,4096]{1,0:T(8,128)(2,1)S(1)} %copy-done.1, bf16[768,4096]{1,0:T(8,128)(2,1)S(1)} %copy-done.1, bf16[768,4096]{1,0:T(8,128)(2,1)S(1)} %copy-done.1, ...), custom_call_target="tpu_custom_call" | custom-call | flops 805306368 | bytes 5767168 | tf_op jit(solution)/shard_map/pallas_call | solution.py:151
  53.2 2.0 %collective-permute-done.15.refs_5_ = bf16[256,512]{1,0:T(8,128)(2,1)} collective-permute-done((bf16[256,512]{1,0:T(8,128)(2,1)}, bf16[256,512]{1,0:T(8,128)(2,1)}, u32[]{:S(2)}, u32[]{:S(2)}) %collective-permute-start.15) | collective-permute-done | bytes 262176 | tf_op jit(solution)/shard_map/ppermute | solution.py:32
  55.2 2.8 %copy-done.2 = bf16[768,4096]{1,0:T(8,128)(2,1)S(1)} copy-done((bf16[768,4096]{1,0:T(8,128)(2,1)S(1)}, bf16[768,4096]{1,0:T(8,128)(2,1)}, u32[]{:S(2)}) %copy-start.2) | copy-done | bytes 6291480
  58.0 3.3 %shard_map.67.refs_4_ = f32[768,512]{1,0:T(8,128)S(1)} custom-call(s32[4]{0:T(128)S(1)} %pad_add_fusion.4.offsets_ref, s32[6]{0:T(128)S(1)} %convert_reduce_fusion.2.counts_ref, bf16[768,4096]{1,0:T(8,128)(2,1)S(1)} %copy-done.2, bf16[768,4096]{1,0:T(8,128)(2,1)S(1)} %copy-done.2, bf16[768,4096]{1,0:T(8,128)(2,1)S(1)} %copy-done.2, ...), custom_call_target="tpu_custom_call" | custom-call | flops 805306368 | bytes 5767168 | tf_op jit(solution)/shard_map/pallas_call | solution.py:151
  63.0 2.8 %shard_map.68 = (f32[768,512]{1,0:T(8,128)S(1)}, f32[6,1,512]{2,1,0:T(1,128)S(1)}) custom-call(s32[2]{0:T(128)S(1)} %pad_add_fusion.2.offsets_ref, s32[6]{0:T(128)S(1)} %convert_reduce_fusion.2.counts_ref, bf16[768,4096]{1,0:T(8,128)(2,1)S(1)} %copy-done.2, bf16[768,4096]{1,0:T(8,128)(2,1)S(1)} %copy-done.2, ...), custom_call_target="tpu_custom_call" | custom-call | flops 402653184 | bytes 4456448 | tf_op jit(solution)/shard_map/pallas_call | solution.py:151
  73.3 2.0 %collective-permute-done.19 = bf16[6,1024]{1,0:T(8,128)(2,1)S(1)} collective-permute-done((bf16[6,1024]{1,0:T(8,128)(2,1)S(1)}, bf16[6,1024]{1,0:T(8,128)(2,1)S(1)}, u32[]{:S(2)}, u32[]{:S(2)}) %collective-permute-start.19) | collective-permute-done | bytes 12320 | tf_op jit(solution)/shard_map/ppermute | solution.py:52
  75.2 2.3 %collective-permute-done.20 = bf16[6,1024]{1,0:T(8,128)(2,1)S(1)} collective-permute-done((bf16[6,1024]{1,0:T(8,128)(2,1)S(1)}, bf16[6,1024]{1,0:T(8,128)(2,1)S(1)}, u32[]{:S(2)}, u32[]{:S(2)}) %collective-permute-start.20) | collective-permute-done | bytes 12320 | tf_op jit(solution)/shard_map/ppermute | solution.py:52
  77.5 2.1 %collective-permute-done.21 = bf16[6,1024]{1,0:T(8,128)(2,1)S(1)} collective-permute-done((bf16[6,1024]{1,0:T(8,128)(2,1)S(1)}, bf16[6,1024]{1,0:T(8,128)(2,1)S(1)}, u32[]{:S(2)}, u32[]{:S(2)}) %collective-permute-start.21) | collective-permute-done | bytes 12320 | tf_op jit(solution)/shard_map/ppermute | solution.py:52
  82.0 1.4 %convolution_convert_fusion.1 = bf16[256,512]{1,0:T(8,128)(2,1)S(1)} fusion(bf16[768,512]{1,0:T(8,128)(2,1)S(1)} %fusion, bf16[768,4096]{1,0:T(8,128)(2,1)} %copy-done, s32[]{:T(128)S(6)} %select_n.228), kind=kOutput, calls=%fused_computation.27 | convolution fusion | flops 201457664 | bytes 1441796 | tf_op jit(solution)/shard_map/dot_general | solution.py:272
  83.4 1.4 %collective-permute-start.31 = (bf16[256,512]{1,0:T(8,128)(2,1)S(1)}, bf16[256,512]{1,0:T(8,128)(2,1)S(1)}, u32[]{:S(2)}, u32[]{:S(2)}) collective-permute-start(bf16[256,512]{1,0:T(8,128)(2,1)S(1)} %convolution_convert_fusion.1), channel_id=1, source_target_pairs={{0,4},{4,8},{8,12},{12,14},{14,10},{10,6},{6,2},{2,0},{1,5},{5,9},... | collective-permute-start | bytes 786440 | tf_op jit(solution)/shard_map/ppermute | solution.py:32
  84.8 1.4 %convolution_convert_fusion = bf16[256,512]{1,0:T(8,128)(2,1)S(1)} fusion(bf16[768,512]{1,0:T(8,128)(2,1)S(1)} %fusion, bf16[768,4096]{1,0:T(8,128)(2,1)} %copy-done, s32[]{:T(128)S(6)} %select_n.232), kind=kOutput, calls=%fused_computation.26 | convolution fusion | flops 201457664 | bytes 1441796 | tf_op jit(solution)/shard_map/dot_general | solution.py:272
  88.3 1.4 %collective-permute-start.23 = (bf16[256,512]{1,0:T(8,128)(2,1)S(1)}, bf16[256,512]{1,0:T(8,128)(2,1)S(1)}, u32[]{:S(2)}, u32[]{:S(2)}) collective-permute-start(bf16[256,512]{1,0:T(8,128)(2,1)S(1)} %convolution_convert_fusion.3), channel_id=1, source_target_pairs={{0,4},{4,8},{8,12},{12,14},{14,10},{10,6},{6,2},{2,0},{1,5},{5,9},... | collective-permute-start | bytes 786440 | tf_op jit(solution)/shard_map/ppermute | solution.py:32
  96.6 1.7 %collective-permute-done.23 = bf16[256,512]{1,0:T(8,128)(2,1)S(1)} collective-permute-done((bf16[256,512]{1,0:T(8,128)(2,1)S(1)}, bf16[256,512]{1,0:T(8,128)(2,1)S(1)}, u32[]{:S(2)}, u32[]{:S(2)}) %collective-permute-start.23) | collective-permute-done | bytes 262176 | tf_op jit(solution)/shard_map/ppermute | solution.py:32
  100.0 2.0 %collective-permute-done.28 = bf16[256,512]{1,0:T(8,128)(2,1)S(1)} collective-permute-done((bf16[256,512]{1,0:T(8,128)(2,1)S(1)}, bf16[256,512]{1,0:T(8,128)(2,1)S(1)}, u32[]{:S(2)}, u32[]{:S(2)}) %collective-permute-start.28) | collective-permute-done | bytes 262176 | tf_op jit(solution)/shard_map/ppermute | solution.py:32
  103.3 4.3 %collective-permute-done.35 = bf16[256,512]{1,0:T(8,128)(2,1)S(1)} collective-permute-done((bf16[256,512]{1,0:T(8,128)(2,1)S(1)}, bf16[256,512]{1,0:T(8,128)(2,1)S(1)}, u32[]{:S(2)}, u32[]{:S(2)}) %collective-permute-start.35) | collective-permute-done | bytes 262176 | tf_op jit(solution)/shard_map/ppermute | solution.py:32
  112.0 5.1 %collective-permute-done.36 = bf16[256,512]{1,0:T(8,128)(2,1)S(1)} collective-permute-done((bf16[256,512]{1,0:T(8,128)(2,1)S(1)}, bf16[256,512]{1,0:T(8,128)(2,1)S(1)}, u32[]{:S(2)}, u32[]{:S(2)}) %collective-permute-start.36) | collective-permute-done | bytes 262176 | tf_op jit(solution)/shard_map/ppermute | solution.py:32
  119.5 1.6 %collective-permute-start.30 = (bf16[256,512]{1,0:T(8,128)(2,1)}, bf16[256,512]{1,0:T(8,128)(2,1)S(1)}, u32[]{:S(2)}, u32[]{:S(2)}) collective-permute-start(bf16[256,512]{1,0:T(8,128)(2,1)} %convolution_add_fusion.7), channel_id=1, source_target_pairs={{0,2},{4,0},{8,4},{12,8},{14,12},{10,14},{6,10},{2,6},{1,3},{5,1},... | collective-permute-start | bytes 786440 | tf_op jit(solution)/shard_map/ppermute | solution.py:32
  122.0 4.9 %collective-permute-done.37 = bf16[256,512]{1,0:T(8,128)(2,1)S(1)} collective-permute-done((bf16[256,512]{1,0:T(8,128)(2,1)S(1)}, bf16[256,512]{1,0:T(8,128)(2,1)S(1)}, u32[]{:S(2)}, u32[]{:S(2)}) %collective-permute-start.37) | collective-permute-done | bytes 262176 | tf_op jit(solution)/shard_map/ppermute | solution.py:32
  127.4 2.5 %collective-permute-done.30 = bf16[256,512]{1,0:T(8,128)(2,1)S(1)} collective-permute-done((bf16[256,512]{1,0:T(8,128)(2,1)}, bf16[256,512]{1,0:T(8,128)(2,1)S(1)}, u32[]{:S(2)}, u32[]{:S(2)}) %collective-permute-start.30) | collective-permute-done | bytes 262176 | tf_op jit(solution)/shard_map/ppermute | solution.py:32
  129.9 1.5 %fusion.1 = f32[256,512]{1,0:T(8,128)S(1)} fusion(bf16[768,512]{1,0:T(8,128)(2,1)S(1)} %fusion, bf16[256,512]{1,0:T(8,128)(2,1)S(1)} %collective-permute-done.30, bf16[256,512]{1,0:T(8,128)(2,1)} %collective-permute-done.27, bf16[768,4096]{1,0:T(8,128)(2,1)} %copy-done, s32[]{:T(128)S(6)} %select_n.194), kind=kOutput, calls=%fused_computation.16 | convolution fusion | flops 201850880 | bytes 2228228 | tf_op jit(solution)/shard_map/dot_general | solution.py:272
  (122 shorter events, 46.2 us)
Async XLA Ops:
  0.0 25.8 %collective-permute-start = (bf16[3,128,4096]{2,1,0:T(8,128)(2,1)}, bf16[3,128,4096]{2,1,0:T(8,128)(2,1)S(1)}, u32[]{:S(2)}, u32[]{:S(2)}) collective-permute-start(bf16[3,128,4096]{2,1,0:T(8,128)(2,1)} %bitcast.50), channel_id=1, source_target_pairs={{0,1},{1,0},{2,3},{3,2},{4,5},{5,4},{6,7},{7,6},{8,9},{9,8},{10,11... | collective-permute-start | bytes 9437192 | tf_op jit(solution)/shard_map/ppermute | solution.py:40
  2.4 9.6 %collective-permute-start.2 = (bf16[256,512]{1,0:T(8,128)(2,1)S(1)}, bf16[256,512]{1,0:T(8,128)(2,1)}, u32[]{:S(2)}, u32[]{:S(2)}) collective-permute-start(bf16[256,512]{1,0:T(8,128)(2,1)S(1)} %get-tuple-element.30.refs_6_), channel_id=1, source_target_pairs={{0,4},{4,8},{8,12},{12,14},{14,10},{10,6},{6,2},{2,0},{1,5},{5,9},... | collective-permute-start | bytes 786440 | tf_op jit(solution)/shard_map/ppermute | solution.py:32
  5.0 15.3 %collective-permute-start.6 = (bf16[256,512]{1,0:T(8,128)(2,1)S(1)}, bf16[256,512]{1,0:T(8,128)(2,1)}, u32[]{:S(2)}, u32[]{:S(2)}) collective-permute-start(bf16[256,512]{1,0:T(8,128)(2,1)S(1)} %get-tuple-element.30.refs_6_), channel_id=1, source_target_pairs={{0,2},{4,0},{8,4},{12,8},{14,12},{10,14},{6,10},{2,6},{1,3},{5,1},... | collective-permute-start | bytes 786440 | tf_op jit(solution)/shard_map/ppermute | solution.py:32
  8.5 10.7 %collective-permute-start.11 = (bf16[256,512]{1,0:T(8,128)(2,1)}, bf16[256,512]{1,0:T(8,128)(2,1)}, u32[]{:S(2)}, u32[]{:S(2)}) collective-permute-start(bf16[256,512]{1,0:T(8,128)(2,1)} %collective-permute-done.8.refs_7_), channel_id=1, source_target_pairs={{0,2},{4,0},{8,4},{12,8},{14,12},{10,14},{6,10},{2,6},{1,3},{5,1},... | collective-permute-start | bytes 786440 | tf_op jit(solution)/shard_map/ppermute | solution.py:32
  10.6 11.4 %collective-permute-start.9 = (bf16[256,512]{1,0:T(8,128)(2,1)}, bf16[256,512]{1,0:T(8,128)(2,1)}, u32[]{:S(2)}, u32[]{:S(2)}) collective-permute-start(bf16[256,512]{1,0:T(8,128)(2,1)} %collective-permute-done.8.refs_7_), channel_id=1, source_target_pairs={{0,4},{4,8},{8,12},{12,14},{14,10},{10,6},{6,2},{2,0},{1,5},{5,9},... | collective-permute-start | bytes 786440 | tf_op jit(solution)/shard_map/ppermute | solution.py:32
  12.0 13.0 %collective-permute-start.3 = (bf16[256,512]{1,0:T(8,128)(2,1)}, bf16[256,512]{1,0:T(8,128)(2,1)}, u32[]{:S(2)}, u32[]{:S(2)}) collective-permute-start(bf16[256,512]{1,0:T(8,128)(2,1)} %collective-permute-done.2.refs_8_), channel_id=1, source_target_pairs={{0,4},{4,8},{8,12},{12,14},{14,10},{10,6},{6,2},{2,0},{1,5},{5,9},... | collective-permute-start | bytes 786440 | tf_op jit(solution)/shard_map/ppermute | solution.py:32
  19.2 21.5 %collective-permute-start.12 = (bf16[256,512]{1,0:T(8,128)(2,1)}, bf16[256,512]{1,0:T(8,128)(2,1)}, u32[]{:S(2)}, u32[]{:S(2)}) collective-permute-start(bf16[256,512]{1,0:T(8,128)(2,1)} %collective-permute-done.11.refs_11_), channel_id=1, source_target_pairs={{0,2},{4,0},{8,4},{12,8},{14,12},{10,14},{6,10},{2,6},{1,3},{5,1},... | collective-permute-start | bytes 786440 | tf_op jit(solution)/shard_map/ppermute | solution.py:32
  20.3 21.7 %collective-permute-start.7 = (bf16[256,512]{1,0:T(8,128)(2,1)}, bf16[256,512]{1,0:T(8,128)(2,1)}, u32[]{:S(2)}, u32[]{:S(2)}) collective-permute-start(bf16[256,512]{1,0:T(8,128)(2,1)} %collective-permute-done.6.refs_9_), channel_id=1, source_target_pairs={{0,2},{4,0},{8,4},{12,8},{14,12},{10,14},{6,10},{2,6},{1,3},{5,1},... | collective-permute-start | bytes 786440 | tf_op jit(solution)/shard_map/ppermute | solution.py:32
  22.0 22.0 %collective-permute-start.10 = (bf16[256,512]{1,0:T(8,128)(2,1)}, bf16[256,512]{1,0:T(8,128)(2,1)}, u32[]{:S(2)}, u32[]{:S(2)}) collective-permute-start(bf16[256,512]{1,0:T(8,128)(2,1)} %collective-permute-done.9.refs_10_), channel_id=1, source_target_pairs={{0,4},{4,8},{8,12},{12,14},{14,10},{10,6},{6,2},{2,0},{1,5},{5,9},... | collective-permute-start | bytes 786440 | tf_op jit(solution)/shard_map/ppermute | solution.py:32
  25.0 18.6 %collective-permute-start.4 = (bf16[256,512]{1,0:T(8,128)(2,1)}, bf16[256,512]{1,0:T(8,128)(2,1)}, u32[]{:S(2)}, u32[]{:S(2)}) collective-permute-start(bf16[256,512]{1,0:T(8,128)(2,1)} %collective-permute-done.3.refs_4_), channel_id=1, source_target_pairs={{0,4},{4,8},{8,12},{12,14},{14,10},{10,6},{6,2},{2,0},{1,5},{5,9},... | collective-permute-start | bytes 786440 | tf_op jit(solution)/shard_map/ppermute | solution.py:32
  40.6 10.4 %collective-permute-start.13 = (bf16[256,512]{1,0:T(8,128)(2,1)}, bf16[256,512]{1,0:T(8,128)(2,1)S(1)}, u32[]{:S(2)}, u32[]{:S(2)}) collective-permute-start(bf16[256,512]{1,0:T(8,128)(2,1)} %collective-permute-done.12.refs_7_), channel_id=1, source_target_pairs={{0,2},{4,0},{8,4},{12,8},{14,12},{10,14},{6,10},{2,6},{1,3},{5,1},... | collective-permute-start | bytes 786440 | tf_op jit(solution)/shard_map/ppermute | solution.py:32
  42.0 13.2 %collective-permute-start.15 = (bf16[256,512]{1,0:T(8,128)(2,1)}, bf16[256,512]{1,0:T(8,128)(2,1)}, u32[]{:S(2)}, u32[]{:S(2)}) collective-permute-start(bf16[256,512]{1,0:T(8,128)(2,1)} %collective-permute-done.7.refs_5_), channel_id=1, source_target_pairs={{0,2},{4,0},{8,4},{12,8},{14,12},{10,14},{6,10},{2,6},{1,3},{5,1},... | collective-permute-start | bytes 786440 | tf_op jit(solution)/shard_map/ppermute | solution.py:32
  43.6 17.7 %collective-permute-start.5 = (bf16[256,512]{1,0:T(8,128)(2,1)}, bf16[256,512]{1,0:T(8,128)(2,1)}, u32[]{:S(2)}, u32[]{:S(2)}) collective-permute-start(bf16[256,512]{1,0:T(8,128)(2,1)} %collective-permute-done.4.refs_4_), channel_id=1, source_target_pairs={{0,4},{4,8},{8,12},{12,14},{14,10},{10,6},{6,2},{2,0},{1,5},{5,9},... | collective-permute-start | bytes 786440 | tf_op jit(solution)/shard_map/ppermute | solution.py:32
  44.0 11.2 %collective-permute-start.16 = (bf16[256,512]{1,0:T(8,128)(2,1)}, bf16[256,512]{1,0:T(8,128)(2,1)}, u32[]{:S(2)}, u32[]{:S(2)}) collective-permute-start(bf16[256,512]{1,0:T(8,128)(2,1)} %collective-permute-done.10.refs_6_), channel_id=1, source_target_pairs={{0,4},{4,8},{8,12},{12,14},{14,10},{10,6},{6,2},{2,0},{1,5},{5,9},... | collective-permute-start | bytes 786440 | tf_op jit(solution)/shard_map/ppermute | solution.py:32
  51.0 10.3 %collective-permute-start.14 = (bf16[256,512]{1,0:T(8,128)(2,1)S(1)}, bf16[256,512]{1,0:T(8,128)(2,1)S(1)}, u32[]{:S(2)}, u32[]{:S(2)}) collective-permute-start(bf16[256,512]{1,0:T(8,128)(2,1)S(1)} %collective-permute-done.13.refs_7_), channel_id=1, source_target_pairs={{0,2},{4,0},{8,4},{12,8},{14,12},{10,14},{6,10},{2,6},{1,3},{5,1},... | collective-permute-start | bytes 786440 | tf_op jit(solution)/shard_map/ppermute | solution.py:32
  70.0 7.5 %collective-permute-start.20 = (bf16[6,1024]{1,0:T(8,128)(2,1)S(1)}, bf16[6,1024]{1,0:T(8,128)(2,1)S(1)}, u32[]{:S(2)}, u32[]{:S(2)}) collective-permute-start(bf16[6,1024]{1,0:T(8,128)(2,1)S(1)} %maximum_select_fusion.2), channel_id=1, source_target_pairs={{24,0},{23,1},{28,4},{19,5},{30,8},{17,9},{26,12},{21,13},{22,14},... | collective-permute-start | bytes 36872 | tf_op jit(solution)/shard_map/ppermute | solution.py:52
  71.3 8.3 %collective-permute-start.21 = (bf16[6,1024]{1,0:T(8,128)(2,1)S(1)}, bf16[6,1024]{1,0:T(8,128)(2,1)S(1)}, u32[]{:S(2)}, u32[]{:S(2)}) collective-permute-start(bf16[6,1024]{1,0:T(8,128)(2,1)S(1)} %maximum_select_fusion.2), channel_id=1, source_target_pairs={{28,0},{19,1},{30,4},{17,5},{26,8},{21,9},{22,12},{25,13},{18,14},... | collective-permute-start | bytes 36872 | tf_op jit(solution)/shard_map/ppermute | solution.py:52
  83.4 10.2 %collective-permute-start.31 = (bf16[256,512]{1,0:T(8,128)(2,1)S(1)}, bf16[256,512]{1,0:T(8,128)(2,1)S(1)}, u32[]{:S(2)}, u32[]{:S(2)}) collective-permute-start(bf16[256,512]{1,0:T(8,128)(2,1)S(1)} %convolution_convert_fusion.1), channel_id=1, source_target_pairs={{0,4},{4,8},{8,12},{12,14},{14,10},{10,6},{6,2},{2,0},{1,5},{5,9},... | collective-permute-start | bytes 786440 | tf_op jit(solution)/shard_map/ppermute | solution.py:32
  86.2 9.1 %collective-permute-start.34 = (bf16[256,512]{1,0:T(8,128)(2,1)S(1)}, bf16[256,512]{1,0:T(8,128)(2,1)S(1)}, u32[]{:S(2)}, u32[]{:S(2)}) collective-permute-start(bf16[256,512]{1,0:T(8,128)(2,1)S(1)} %convolution_convert_fusion), channel_id=1, source_target_pairs={{0,2},{4,0},{8,4},{12,8},{14,12},{10,14},{6,10},{2,6},{1,3},{5,1},... | collective-permute-start | bytes 786440 | tf_op jit(solution)/shard_map/ppermute | solution.py:32
  88.3 9.9 %collective-permute-start.23 = (bf16[256,512]{1,0:T(8,128)(2,1)S(1)}, bf16[256,512]{1,0:T(8,128)(2,1)S(1)}, u32[]{:S(2)}, u32[]{:S(2)}) collective-permute-start(bf16[256,512]{1,0:T(8,128)(2,1)S(1)} %convolution_convert_fusion.3), channel_id=1, source_target_pairs={{0,4},{4,8},{8,12},{12,14},{14,10},{10,6},{6,2},{2,0},{1,5},{5,9},... | collective-permute-start | bytes 786440 | tf_op jit(solution)/shard_map/ppermute | solution.py:32
  91.0 28.5 %collective-permute-start.24 = (bf16[256,1024]{1,0:T(8,128)(2,1)S(1)}, bf16[256,1024]{1,0:T(8,128)(2,1)S(1)}, u32[]{:S(2)}, u32[]{:S(2)}) collective-permute-start(bf16[256,1024]{1,0:T(8,128)(2,1)S(1)} %convert_element_type.143), channel_id=1, source_target_pairs={{0,16},{1,17},{2,18},{3,19},{4,20},{5,21},{6,22},{7,23},{8,24},{9,... | collective-permute-start | bytes 1572872 | tf_op jit(solution)/shard_map/ppermute | solution.py:269
  92.8 9.3 %collective-permute-start.28 = (bf16[256,512]{1,0:T(8,128)(2,1)S(1)}, bf16[256,512]{1,0:T(8,128)(2,1)S(1)}, u32[]{:S(2)}, u32[]{:S(2)}) collective-permute-start(bf16[256,512]{1,0:T(8,128)(2,1)S(1)} %convolution_convert_fusion.2), channel_id=1, source_target_pairs={{0,2},{4,0},{8,4},{12,8},{14,12},{10,14},{6,10},{2,6},{1,3},{5,1},... | collective-permute-start | bytes 786440 | tf_op jit(solution)/shard_map/ppermute | solution.py:32
  94.0 14.9 %collective-permute-start.32 = (bf16[256,512]{1,0:T(8,128)(2,1)S(1)}, bf16[256,512]{1,0:T(8,128)(2,1)S(1)}, u32[]{:S(2)}, u32[]{:S(2)}) collective-permute-start(bf16[256,512]{1,0:T(8,128)(2,1)S(1)} %fusion.7), channel_id=1, source_target_pairs={{0,4},{4,8},{8,12},{12,14},{14,10},{10,6},{6,2},{2,0},{1,5},{5,9},... | collective-permute-start | bytes 786440 | tf_op jit(solution)/shard_map/ppermute | solution.py:32
  95.7 12.0 %collective-permute-start.35 = (bf16[256,512]{1,0:T(8,128)(2,1)S(1)}, bf16[256,512]{1,0:T(8,128)(2,1)S(1)}, u32[]{:S(2)}, u32[]{:S(2)}) collective-permute-start(bf16[256,512]{1,0:T(8,128)(2,1)S(1)} %fusion.10), channel_id=1, source_target_pairs={{0,2},{4,0},{8,4},{12,8},{14,12},{10,14},{6,10},{2,6},{1,3},{5,1},... | collective-permute-start | bytes 786440 | tf_op jit(solution)/shard_map/ppermute | solution.py:32
  98.7 12.0 %collective-permute-start.25 = (bf16[256,512]{1,0:T(8,128)(2,1)S(1)}, bf16[256,512]{1,0:T(8,128)(2,1)S(1)}, u32[]{:S(2)}, u32[]{:S(2)}) collective-permute-start(bf16[256,512]{1,0:T(8,128)(2,1)S(1)} %fusion.4), channel_id=1, source_target_pairs={{0,4},{4,8},{8,12},{12,14},{14,10},{10,6},{6,2},{2,0},{1,5},{5,9},... | collective-permute-start | bytes 786440 | tf_op jit(solution)/shard_map/ppermute | solution.py:32
  102.5 15.9 %collective-permute-start.29 = (bf16[256,512]{1,0:T(8,128)(2,1)S(1)}, bf16[256,512]{1,0:T(8,128)(2,1)S(1)}, u32[]{:S(2)}, u32[]{:S(2)}) collective-permute-start(bf16[256,512]{1,0:T(8,128)(2,1)S(1)} %fusion.5), channel_id=1, source_target_pairs={{0,2},{4,0},{8,4},{12,8},{14,12},{10,14},{6,10},{2,6},{1,3},{5,1},... | collective-permute-start | bytes 786440 | tf_op jit(solution)/shard_map/ppermute | solution.py:32
  108.1 9.1 %collective-permute-start.36 = (bf16[256,512]{1,0:T(8,128)(2,1)S(1)}, bf16[256,512]{1,0:T(8,128)(2,1)S(1)}, u32[]{:S(2)}, u32[]{:S(2)}) collective-permute-start(bf16[256,512]{1,0:T(8,128)(2,1)S(1)} %fusion.9), channel_id=1, source_target_pairs={{0,2},{4,0},{8,4},{12,8},{14,12},{10,14},{6,10},{2,6},{1,3},{5,1},... | collective-permute-start | bytes 786440 | tf_op jit(solution)/shard_map/ppermute | solution.py:32
  109.3 12.6 %collective-permute-start.33 = (bf16[256,512]{1,0:T(8,128)(2,1)S(1)}, bf16[256,512]{1,0:T(8,128)(2,1)S(1)}, u32[]{:S(2)}, u32[]{:S(2)}) collective-permute-start(bf16[256,512]{1,0:T(8,128)(2,1)S(1)} %fusion.6), channel_id=1, source_target_pairs={{0,4},{4,8},{8,12},{12,14},{14,10},{10,6},{6,2},{2,0},{1,5},{5,9},... | collective-permute-start | bytes 786440 | tf_op jit(solution)/shard_map/ppermute | solution.py:32
  111.1 10.0 %collective-permute-start.26 = (bf16[256,512]{1,0:T(8,128)(2,1)S(1)}, bf16[256,512]{1,0:T(8,128)(2,1)S(1)}, u32[]{:S(2)}, u32[]{:S(2)}) collective-permute-start(bf16[256,512]{1,0:T(8,128)(2,1)S(1)} %fusion.3), channel_id=1, source_target_pairs={{0,4},{4,8},{8,12},{12,14},{14,10},{10,6},{6,2},{2,0},{1,5},{5,9},... | collective-permute-start | bytes 786440 | tf_op jit(solution)/shard_map/ppermute | solution.py:32
  117.6 9.3 %collective-permute-start.37 = (bf16[256,512]{1,0:T(8,128)(2,1)S(1)}, bf16[256,512]{1,0:T(8,128)(2,1)S(1)}, u32[]{:S(2)}, u32[]{:S(2)}) collective-permute-start(bf16[256,512]{1,0:T(8,128)(2,1)S(1)} %fusion.8), channel_id=1, source_target_pairs={{0,2},{4,0},{8,4},{12,8},{14,12},{10,14},{6,10},{2,6},{1,3},{5,1},... | collective-permute-start | bytes 786440 | tf_op jit(solution)/shard_map/ppermute | solution.py:32
  119.5 10.4 %collective-permute-start.30 = (bf16[256,512]{1,0:T(8,128)(2,1)}, bf16[256,512]{1,0:T(8,128)(2,1)S(1)}, u32[]{:S(2)}, u32[]{:S(2)}) collective-permute-start(bf16[256,512]{1,0:T(8,128)(2,1)} %convolution_add_fusion.7), channel_id=1, source_target_pairs={{0,2},{4,0},{8,4},{12,8},{14,12},{10,14},{6,10},{2,6},{1,3},{5,1},... | collective-permute-start | bytes 786440 | tf_op jit(solution)/shard_map/ppermute | solution.py:32
  121.5 8.3 %collective-permute-start.27 = (bf16[256,512]{1,0:T(8,128)(2,1)S(1)}, bf16[256,512]{1,0:T(8,128)(2,1)}, u32[]{:S(2)}, u32[]{:S(2)}) collective-permute-start(bf16[256,512]{1,0:T(8,128)(2,1)S(1)} %convolution_add_fusion.10), channel_id=1, source_target_pairs={{0,4},{4,8},{8,12},{12,14},{14,10},{10,6},{6,2},{2,0},{1,5},{5,9},... | collective-permute-start | bytes 786440 | tf_op jit(solution)/shard_map/ppermute | solution.py:32
  (15 other events, 60.3 us)

commit v5 on v4

--- a/solution.py
+++ b/solution.py
@@ -10,7 +10,7 @@
 sharpness = 20.0
 cores = 2
 longest_ring = 16
-vmem_limit = 32 << 20
+vmem_limit = 60 << 20
 
 
 def ring_order(chips):
@@ -63,45 +63,71 @@
     )
 
 
-def normalize_kernel(seqs, chunk, mine_ref, other_ref, gain_ref, out_ref):
-    length = mine_ref.shape[1]
-
-    def run(ref):
-        @pl.loop(0, length // chunk)
-        def _(i):
-            at = pl.ds(pl.multiple_of(i * chunk, chunk), chunk)
-            wide = ref[0, at, :].astype(jnp.float32)
-            mean_square = jnp.mean(wide * wide, axis=-1, keepdims=True)
-            wide = wide * lax.rsqrt(mean_square + 1e-05) * gain_ref[...]
-            out_ref[at, :] = wide.astype(jnp.bfloat16)
-
-    @pl.when(pl.program_id(0) < seqs)
-    def _():
-        run(mine_ref)
-
-    @pl.when(pl.program_id(0) >= seqs)
-    def _():
-        run(other_ref)
-
-
-def normalize_both(mine, other, gain):
-    seqs, length, width = mine.shape
-    tokens = 2 * seqs * length
+def halves_kernel(core_ref, own_ref, other_ref, own_out, other_out):
+    own_out[...] = own_ref[...].astype(jnp.bfloat16)
+    other_out[...] = other_ref[...].astype(jnp.bfloat16)
+
+
+def cut_halves(weights, core):
+    rows, embedding = weights.shape
+    half = embedding // cores
+    tile = rows // 4 if rows % 64 == 0 else rows
+    read = (tile, half)
+    written = pl.BlockSpec((tile, half), lambda i, core: (i, 0))
     return pl.pallas_call(
-        functools.partial(normalize_kernel, seqs, 16),
-        grid=(2 * seqs,),
-        in_specs=[
-            pl.BlockSpec((1, length, width), lambda i: (jnp.minimum(i, seqs - 1), 0, 0)),
-            pl.BlockSpec((1, length, width), lambda i: (jnp.maximum(i - seqs, 0), 0, 0)),
-            pl.BlockSpec((1, width), lambda i: (0, 0)),
-        ],
-        out_specs=pl.BlockSpec((length, width), lambda i: (i, 0)),
-        out_shape=jax.ShapeDtypeStruct((tokens, width), jnp.bfloat16),
+        halves_kernel,
+        grid_spec=pltpu.PrefetchScalarGridSpec(
+            num_scalar_prefetch=1,
+            grid=(rows // tile,),
+            in_specs=[
+                pl.BlockSpec(read, lambda i, core: (i, core[0])),
+                pl.BlockSpec(read, lambda i, core: (i, 1 - core[0])),
+            ],
+            out_specs=[written, written],
+        ),
+        out_shape=[jax.ShapeDtypeStruct((rows, half), jnp.bfloat16)] * 2,
+        compiler_params=pltpu.CompilerParams(vmem_limit_bytes=vmem_limit),
+        cost_estimate=pl.CostEstimate(
+            flops=0, bytes_accessed=6 * rows * embedding, transcendentals=0
+        ),
+    )(core[None].astype(jnp.int32), weights, weights)
+
+
+def normalize_kernel(chunk, states_ref, gain_ref, *refs):
+    out_ref = refs[-1]
+
+    @pl.loop(0, states_ref.shape[1] // chunk)
+    def _(i):
+        at = pl.ds(pl.multiple_of(i * chunk, chunk), chunk)
+        wide = states_ref[0, at, :].astype(jnp.float32)
+        mean_square = jnp.mean(wide * wide, axis=-1, keepdims=True)
+        wide = wide * lax.rsqrt(mean_square + 1e-05) * gain_ref[...]
+        out_ref[at, :] = wide.astype(jnp.bfloat16)
+
+
+def normalize(states, gain, part, filled=None):
+    seqs, length, width = states.shape
+    tokens = seqs * length
+    in_specs = [
+        pl.BlockSpec((1, length, width), lambda i: (i, 0, 0)),
+        pl.BlockSpec((1, width), lambda i: (0, 0)),
+    ]
+    operands = [states, gain[None]]
+    if filled is not None:
+        in_specs.append(pl.BlockSpec(memory_space=pl.ANY))
+        operands.append(filled)
+    return pl.pallas_call(
+        functools.partial(normalize_kernel, 16),
+        grid=(seqs,),
+        in_specs=in_specs,
+        out_specs=pl.BlockSpec((length, width), lambda i: (part * seqs + i, 0)),
+        out_shape=jax.ShapeDtypeStruct((cores * tokens, width), jnp.bfloat16),
+        input_output_aliases={} if filled is None else {2: 0},
         compiler_params=pltpu.CompilerParams(vmem_limit_bytes=vmem_limit),
         cost_estimate=pl.CostEstimate(
             flops=6 * tokens * width, bytes_accessed=4 * tokens * width, transcendentals=tokens
         ),
-    )(mine, other, gain[None])
+    )(*operands)
 
 
 def blocks_kernel(amount, has_total, last, length, offsets_ref, counts_ref, *refs):
@@ -176,13 +202,14 @@
     seqs = cores * seq_dev
 
     weights = master[0]
-    own = lax.dynamic_slice(weights, (0, core * half), (rows, half)).astype(jnp.bfloat16)
-    given = lax.dynamic_slice(weights, (0, (1 - core) * half), (rows, half))
-    given = given.astype(jnp.bfloat16)
+    own, given = cut_halves(weights, core)
     sibling = from_sibling(given)
 
-    normed = normalize_both(states, from_sibling(states), gain)
-    ids = jnp.concatenate([token_ids[0], cand_ids], axis=1)
+    normed = normalize(states, gain, 0)
+    normed = normalize(from_sibling(states), gain, 1, normed)
+    first_sent = along_ring(own, 1)
+    ids, cand_ids = token_ids[0], after(first_sent, cand_ids)
+    ids = jnp.concatenate([ids, cand_ids], axis=1)
     ids = jnp.concatenate([ids, from_sibling(ids)])
     lengths = jnp.sum((ids[:, :length] != 0).astype(jnp.int32), axis=1)
     counts = lengths.astype(jnp.float32)
@@ -198,23 +225,28 @@
     parts = (core, 1 - core)
     if chips <= longest_ring:
         moving = {(i, by): block for by in (1, -1) for i, block in enumerate((own, sibling))}
-        sums = [None]
+        total, first = None, None
         blocks, offsets = [own, sibling], [first_column(0, part) for part in parts]
         for step in range(1, chips // 2 + 1):
             last = step == chips // 2
             sent = [(0, 1), (1, -1)] if last else [(0, 1), (0, -1), (1, 1), (1, -1)]
             for i, by in sent:
-                if step > 2 and i == 1:
-                    moving[i, by] = after(sums[step - 2], moving[i, by])
-                moving[i, by] = along_ring(moving[i, by], by)
+                if (step, i, by) == (1, 0, 1):
+                    moving[i, by] = first_sent
+                else:
+                    if last and i == 1:
+                        moving[i, by] = after(first, moving[i, by])
+                    elif step == 3 and i == 0:
+                        moving[i, by] = after(normed, moving[i, by])
+                    moving[i, by] = along_ring(moving[i, by], by)
                 blocks.append(moving[i, by])
                 offsets.append(first_column(-by * step, parts[i]))
-            total = add_blocks(
-                normed, jnp.stack(offsets), blocks, sums[-1], lengths, length, last
-            )
-            sums.append(total)
+            if step == 1:
+                continue
+            total = add_blocks(normed, jnp.stack(offsets), blocks, total, lengths, length, last)
+            first = total if first is None else first
             blocks, offsets = [], []
-        slope, pooled = sums[-1]
+        slope, pooled = total
         pooled = pooled[:, 0] / counts[:, None]
     else:
         both = in_core_order(own, sibling, core)

time: 134 us -> 148 us (1.10)
  Pallas kernels: 21.6 us -> 33.7 us
  local copies, waits for them, and re-layouts: 14.2 us -> 7.34 us
  waiting for transfers between devices: 40.1 us -> 43.7 us
  matrix products: 12 us -> 14.8 us
  starting transfers between devices: 37.4 us -> 38.9 us
    pallas_call x1 -> x3, Pallas kernels: 7.2 us -> 15.7 us  [the longest x2 12.4 us: normalize(): pl.pallas_call(functools.partial(normalize_kernel, 16), grid=(seqs,), in_...]
    unnamed x17 -> x27, local copies, waits for them, and re-layouts: 10.5 us -> 5.17 us
    pallas_call x4 -> x3, Pallas kernels: 14.4 us -> 18 us  [add_blocks(): pl.pallas_call(functools.partial(blocks_kernel, amount, total is not None...]
    ppermute x28, waiting for transfers between devices: 31.5 us -> 34.7 us  [along_ring(): return lax.ppermute(block, 'chip', pairs)]
    dot_general x16, matrix products: 11.3 us -> 14.1 us  [term(): lax.dot_general(columns(offset, part), delta, (((0,), (0,)), ((), ())), p...]
    convert_element_type x1 -> x0, local copies, waits for them, and re-layouts: 1.97 us -> none  [shards(): given = given.astype(jnp.bfloat16)]
  transfers between devices with their start and end apart: 39 -> 39, of which waited for: 15 -> 18; matrix products, arithmetic and copies ran while one was open for 14% -> 14% of each run, Pallas kernels for 14% -> 19%
where the time goes in v5:
time: 148 us; the launch traced here: 147 us
  waiting for transfers between devices  43.7 us (30%)
  starting transfers between devices  38.9 us (26%)
  Pallas kernels  33.7 us (23%)
  matrix products  14.8 us (10%)
  other arithmetic  8.06 us (5%)
  local copies, waits for them, and re-layouts  7.34 us (5%)
    ppermute x28, waiting for transfers between devices, along_ring(): return lax.ppermute(block, 'chip', pairs)  34.7 us
    ppermute x28, starting transfers between devices, along_ring(): return lax.ppermute(block, 'chip', pairs)  30.9 us
    pallas_call x3, Pallas kernels, add_blocks(): pl.pallas_call(functools.partial(blocks_kernel, amount, total is not None...  18 us
    dot_general x16, matrix products, term(): lax.dot_general(columns(offset, part), delta, (((0,), (0,)), ((), ())), p...  14.1 us
    pallas_call x2, Pallas kernels, normalize(): pl.pallas_call(functools.partial(normalize_kernel, 16), grid=(seqs,), in_...  12.4 us
    ppermute x4, waiting for transfers between devices, slab_blocks(): kept.append(lax.ppermute(stored, ('grp', 'chip', 'core'), pairs))  6.68 us
    unnamed x27, local copies, waits for them, and re-layouts  5.17 us
    ppermute x4, starting transfers between devices, slab_blocks(): kept.append(lax.ppermute(stored, ('grp', 'chip', 'core'), pairs))  5.16 us
  transfers between devices with their start and end apart: 39, of which 18 were waited for; matrix products, arithmetic and copies ran while one was open for 14% of the time, Pallas kernels for 19%

profile of v5, /device:TPU:0, one launch (start us, length us, event | category | flops | bytes accessed | tf_op | source)
XLA Modules:
  0.0 147.0 jit_solution(10712651767218717556)
XLA Ops:
  0.5 3.3 %shard_map.66 = (bf16[256,512]{1,0:T(8,128)(2,1)}, bf16[256,512]{1,0:T(8,128)(2,1)}) custom-call(s32[1]{0:T(128)} %bitcast.2.core_ref, f32[256,1024]{1,0:T(8,128)} %bitcast.49, f32[256,1024]{1,0:T(8,128)} %bitcast.50), custom_call_target="tpu_custom_call" | custom-call | bytes 1572864 | tf_op jit(solution)/shard_map/pallas_call | solution.py:77
  3.7 2.6 %collective-permute-start.1 = (bf16[256,512]{1,0:T(8,128)(2,1)}, bf16[256,512]{1,0:T(8,128)(2,1)S(1)}, u32[]{:S(2)}, u32[]{:S(2)}) collective-permute-start(bf16[256,512]{1,0:T(8,128)(2,1)} %get-tuple-element.18.refs_10_), channel_id=1, source_target_pairs={{0,4},{4,8},{8,12},{12,14},{14,10},{10,6},{6,2},{2,0},{1,5},{5,9},... | collective-permute-start | bytes 786440 | tf_op jit(solution)/shard_map/ppermute | solution.py:32
  8.2 2.0 %collective-permute-start.9 = (bf16[256,512]{1,0:T(8,128)(2,1)}, bf16[256,512]{1,0:T(8,128)(2,1)}, u32[]{:S(2)}, u32[]{:S(2)}) collective-permute-start(bf16[256,512]{1,0:T(8,128)(2,1)} %collective-permute-done.6.refs_11_), channel_id=1, source_target_pairs={{0,2},{4,0},{8,4},{12,8},{14,12},{10,14},{6,10},{2,6},{1,3},{5,1},... | collective-permute-start | bytes 786440 | tf_op jit(solution)/shard_map/ppermute | solution.py:32
  14.7 6.2 %shard_map.64.refs_0_ = bf16[768,4096]{1,0:T(8,128)(2,1)} custom-call(bf16[3,128,4096]{2,1,0:T(8,128)(2,1)} %bitcast.53, f32[1,4096]{1,0:T(1,128)} %bitcast.54), custom_call_target="tpu_custom_call" | custom-call | flops 9437184 | bytes 6291456 | tf_op jit(solution)/shard_map/pallas_call | solution.py:119
  20.9 2.2 %collective-permute-start.3 = (bf16[256,512]{1,0:T(8,128)(2,1)S(1)}, bf16[256,512]{1,0:T(8,128)(2,1)}, u32[]{:S(2)}, u32[]{:S(2)}) collective-permute-start(bf16[256,512]{1,0:T(8,128)(2,1)S(1)} %collective-permute-done.1.refs_12_), channel_id=1, source_target_pairs={{0,4},{4,8},{8,12},{12,14},{14,10},{10,6},{6,2},{2,0},{1,5},{5,9},... | collective-permute-start | bytes 786440 | tf_op jit(solution)/shard_map/ppermute | solution.py:32
  23.1 1.6 %collective-permute-start.12 = (bf16[256,512]{1,0:T(8,128)(2,1)}, bf16[256,512]{1,0:T(8,128)(2,1)}, u32[]{:S(2)}, u32[]{:S(2)}) collective-permute-start(bf16[256,512]{1,0:T(8,128)(2,1)} %collective-permute-done.9.refs_15_), channel_id=1, source_target_pairs={{0,2},{4,0},{8,4},{12,8},{14,12},{10,14},{6,10},{2,6},{1,3},{5,1},... | collective-permute-start | bytes 786440 | tf_op jit(solution)/shard_map/ppermute | solution.py:32
  25.3 12.2 %collective-permute-done.12.refs_19_ = bf16[256,512]{1,0:T(8,128)(2,1)} collective-permute-done((bf16[256,512]{1,0:T(8,128)(2,1)}, bf16[256,512]{1,0:T(8,128)(2,1)}, u32[]{:S(2)}, u32[]{:S(2)}) %collective-permute-start.12) | collective-permute-done | bytes 262176 | tf_op jit(solution)/shard_map/ppermute | solution.py:32
  37.7 1.7 %copy-done.2 = bf16[3,128,4096]{2,1,0:T(8,128)(2,1)} copy-done((bf16[3,128,4096]{2,1,0:T(8,128)(2,1)}, bf16[3,128,4096]{2,1,0:T(8,128)(2,1)S(1)}, u32[]{:S(2)}) %copy-start.2) | copy-done | bytes 3145752
  39.4 6.2 %shard_map.65.refs_0_.refs_1_.refs_2_.refs_3_.refs_4_.refs_5_.refs_6_.refs_7_.refs_8_.refs_9_ = bf16[768,4096]{1,0:T(8,128)(2,1)} custom-call(bf16[3,128,4096]{2,1,0:T(8,128)(2,1)} %copy-done.2, f32[1,4096]{1,0:T(1,128)} %bitcast.55, bf16[768,4096]{1,0:T(8,128)(2,1)} %shard_map.64.refs_0_), custom_call_target="tpu_custom_call", output_to_operand_aliasing={{}: (2, {})} | custom-call | flops 9437184 | bytes 6291456 | tf_op jit(solution)/shard_map/pallas_call | solution.py:119
  45.7 1.8 %collective-permute-start.4 = (bf16[256,512]{1,0:T(8,128)(2,1)}, bf16[256,512]{1,0:T(8,128)(2,1)S(1)}, u32[]{:S(2)}, u32[]{:S(2)}) collective-permute-start(bf16[256,512]{1,0:T(8,128)(2,1)} %collective-permute-done.3.refs_16_), channel_id=1, source_target_pairs={{0,4},{4,8},{8,12},{12,14},{14,10},{10,6},{6,2},{2,0},{1,5},{5,9},... | collective-permute-start | bytes 786440 | tf_op jit(solution)/shard_map/ppermute | solution.py:32
  47.7 1.6 %collective-permute-start.16 = (bf16[256,512]{1,0:T(8,128)(2,1)}, bf16[256,512]{1,0:T(8,128)(2,1)S(1)}, u32[]{:S(2)}, u32[]{:S(2)}) collective-permute-start(bf16[256,512]{1,0:T(8,128)(2,1)} %collective-permute-done.11.refs_18_), channel_id=1, source_target_pairs={{0,4},{4,8},{8,12},{12,14},{14,10},{10,6},{6,2},{2,0},{1,5},{5,9},... | collective-permute-start | bytes 786440 | tf_op jit(solution)/shard_map/ppermute | solution.py:32
  49.7 7.1 %shard_map.67.refs_8_ = f32[768,512]{1,0:T(8,128)} custom-call(s32[10]{0:T(128)} %stack.70.offsets_ref, s32[6]{0:T(128)} %copy-done.10, bf16[768,4096]{1,0:T(8,128)(2,1)} %shard_map.65.refs_0_.refs_1_.refs_2_.refs_3_.refs_4_.refs_5_.refs_6_.refs_7_.refs_8_.refs_9_, ...), custom_call_target="tpu_custom_call" | custom-call | flops 2013265920 | bytes 9699328 | tf_op jit(solution)/shard_map/pallas_call | solution.py:177
  57.1 1.7 %collective-permute-start.5 = (bf16[256,512]{1,0:T(8,128)(2,1)S(1)}, bf16[256,512]{1,0:T(8,128)(2,1)S(1)}, u32[]{:S(2)}, u32[]{:S(2)}) collective-permute-start(bf16[256,512]{1,0:T(8,128)(2,1)S(1)} %collective-permute-done.4.refs_4_), channel_id=1, source_target_pairs={{0,4},{4,8},{8,12},{12,14},{14,10},{10,6},{6,2},{2,0},{1,5},{5,9},... | collective-permute-start | bytes 786440 | tf_op jit(solution)/shard_map/ppermute | solution.py:32
  61.7 5.8 %shard_map.68.refs_4_ = f32[768,512]{1,0:T(8,128)} custom-call(s32[4]{0:T(128)} %pad_add_fusion.3.offsets_ref, s32[6]{0:T(128)} %copy-done.10, bf16[768,4096]{1,0:T(8,128)(2,1)} %shard_map.65.refs_0_.refs_1_.refs_2_.refs_3_.refs_4_.refs_5_.refs_6_.refs_7_.refs_8_.refs_9_, ...), custom_call_target="tpu_custom_call" | custom-call | flops 805306368 | bytes 5767168 | tf_op jit(solution)/shard_map/pallas_call | solution.py:177
  68.8 5.2 %shard_map.69 = (f32[768,512]{1,0:T(8,128)}, f32[6,1,512]{2,1,0:T(1,128)}) custom-call(s32[2]{0:T(128)} %pad_add_fusion.2.offsets_ref, s32[6]{0:T(128)} %copy-done.10, bf16[768,4096]{1,0:T(8,128)(2,1)} %shard_map.65.refs_0_.refs_1_.refs_2_.refs_3_.refs_4_.refs_5_.refs_6_.refs_7_.refs_8_.refs_9_, ...), custom_call_target="tpu_custom_call" | custom-call | flops 402653184 | bytes 4456448 | tf_op jit(solution)/shard_map/pallas_call | solution.py:177
  82.2 2.5 %collective-permute-done.21 = bf16[6,1024]{1,0:T(8,128)(2,1)S(1)} collective-permute-done((bf16[6,1024]{1,0:T(8,128)(2,1)S(1)}, bf16[6,1024]{1,0:T(8,128)(2,1)S(1)}, u32[]{:S(2)}, u32[]{:S(2)}) %collective-permute-start.21) | collective-permute-done | bytes 12320 | tf_op jit(solution)/shard_map/ppermute | solution.py:52
  86.3 2.6 %collective-permute-done.18 = bf16[6,1024]{1,0:T(8,128)(2,1)S(1)} collective-permute-done((bf16[6,1024]{1,0:T(8,128)(2,1)S(1)}, bf16[6,1024]{1,0:T(8,128)(2,1)S(1)}, u32[]{:S(2)}, u32[]{:S(2)}) %collective-permute-start.18) | collective-permute-done | bytes 12320 | tf_op jit(solution)/shard_map/ppermute | solution.py:52
  91.0 1.6 %fusion = bf16[768,512]{1,0:T(8,128)(2,1)S(1)} fusion(f32[768,512]{1,0:T(8,128)} %get-tuple-element.25, f32[6,512]{1,0:T(8,128)S(1)} %fusion.33), kind=kLoop, calls=%fused_computation.3 | loop fusion | flops 786432 | bytes 2371584 | tf_op jit(solution)/shard_map/convert_element_type | solution.py:299
  92.7 2.1 %collective-permute-start.24 = (bf16[256,1024]{1,0:T(8,128)(2,1)S(1)}, bf16[256,1024]{1,0:T(8,128)(2,1)S(1)}, u32[]{:S(2)}, u32[]{:S(2)}) collective-permute-start(bf16[256,1024]{1,0:T(8,128)(2,1)S(1)} %convert_element_type.128), channel_id=1, source_target_pairs={{0,16},{1,17},{2,18},{3,19},{4,20},{5,21},{6,22},{7,23},{8,24},{9,... | collective-permute-start | bytes 1572872 | tf_op jit(solution)/shard_map/ppermute | solution.py:301
  97.8 1.9 %collective-permute-start.28 = (bf16[256,512]{1,0:T(8,128)(2,1)S(1)}, bf16[256,512]{1,0:T(8,128)(2,1)S(1)}, u32[]{:S(2)}, u32[]{:S(2)}) collective-permute-start(bf16[256,512]{1,0:T(8,128)(2,1)S(1)} %convolution_convert_fusion.2), channel_id=1, source_target_pairs={{0,2},{4,0},{8,4},{12,8},{14,12},{10,14},{6,10},{2,6},{1,3},{5,1},... | collective-permute-start | bytes 786440 | tf_op jit(solution)/shard_map/ppermute | solution.py:32
  101.1 1.4 collective-permute-start.34
  104.6 2.5 %collective-permute-done.28 = bf16[256,512]{1,0:T(8,128)(2,1)S(1)} collective-permute-done((bf16[256,512]{1,0:T(8,128)(2,1)S(1)}, bf16[256,512]{1,0:T(8,128)(2,1)S(1)}, u32[]{:S(2)}, u32[]{:S(2)}) %collective-permute-start.28) | collective-permute-done | bytes 262176 | tf_op jit(solution)/shard_map/ppermute | solution.py:32
  108.5 1.9 %collective-permute-start.29 = (bf16[256,512]{1,0:T(8,128)(2,1)S(1)}, bf16[256,512]{1,0:T(8,128)(2,1)S(1)}, u32[]{:S(2)}, u32[]{:S(2)}) collective-permute-start(bf16[256,512]{1,0:T(8,128)(2,1)S(1)} %fusion.5), channel_id=1, source_target_pairs={{0,2},{4,0},{8,4},{12,8},{14,12},{10,14},{6,10},{2,6},{1,3},{5,1},... | collective-permute-start | bytes 786440 | tf_op jit(solution)/shard_map/ppermute | solution.py:32
  110.4 2.3 %collective-permute-done.34 = bf16[256,512]{1,0:T(8,128)(2,1)S(1)} collective-permute-done((bf16[256,512]{1,0:T(8,128)(2,1)S(1)}, bf16[256,512]{1,0:T(8,128)(2,1)S(1)}, u32[]{:S(2)}, u32[]{:S(2)}) %collective-permute-start.34) | collective-permute-done | bytes 262176 | tf_op jit(solution)/shard_map/ppermute | solution.py:32
  113.1 1.9 %collective-permute-start.35 = (bf16[256,512]{1,0:T(8,128)(2,1)S(1)}, bf16[256,512]{1,0:T(8,128)(2,1)S(1)}, u32[]{:S(2)}, u32[]{:S(2)}) collective-permute-start(bf16[256,512]{1,0:T(8,128)(2,1)S(1)} %fusion.10), channel_id=1, source_target_pairs={{0,2},{4,0},{8,4},{12,8},{14,12},{10,14},{6,10},{2,6},{1,3},{5,1},... | collective-permute-start | bytes 786440 | tf_op jit(solution)/shard_map/ppermute | solution.py:32
  117.3 5.5 %collective-permute-done.35 = bf16[256,512]{1,0:T(8,128)(2,1)S(1)} collective-permute-done((bf16[256,512]{1,0:T(8,128)(2,1)S(1)}, bf16[256,512]{1,0:T(8,128)(2,1)S(1)}, u32[]{:S(2)}, u32[]{:S(2)}) %collective-permute-start.35) | collective-permute-done | bytes 262176 | tf_op jit(solution)/shard_map/ppermute | solution.py:32
  123.2 1.7 %collective-permute-start.36 = (bf16[256,512]{1,0:T(8,128)(2,1)S(1)}, bf16[256,512]{1,0:T(8,128)(2,1)S(1)}, u32[]{:S(2)}, u32[]{:S(2)}) collective-permute-start(bf16[256,512]{1,0:T(8,128)(2,1)S(1)} %fusion.9), channel_id=1, source_target_pairs={{0,2},{4,0},{8,4},{12,8},{14,12},{10,14},{6,10},{2,6},{1,3},{5,1},... | collective-permute-start | bytes 786440 | tf_op jit(solution)/shard_map/ppermute | solution.py:32
  128.0 2.9 %collective-permute-done.36 = bf16[256,512]{1,0:T(8,128)(2,1)S(1)} collective-permute-done((bf16[256,512]{1,0:T(8,128)(2,1)S(1)}, bf16[256,512]{1,0:T(8,128)(2,1)S(1)}, u32[]{:S(2)}, u32[]{:S(2)}) %collective-permute-start.36) | collective-permute-done | bytes 262176 | tf_op jit(solution)/shard_map/ppermute | solution.py:32
  136.5 2.7 %collective-permute-done.33 = bf16[256,512]{1,0:T(8,128)(2,1)S(1)} collective-permute-done((bf16[256,512]{1,0:T(8,128)(2,1)S(1)}, bf16[256,512]{1,0:T(8,128)(2,1)S(1)}, u32[]{:S(2)}, u32[]{:S(2)}) %collective-permute-start.33) | collective-permute-done | bytes 262176 | tf_op jit(solution)/shard_map/ppermute | solution.py:32
  139.2 1.4 collective-permute-done.37
  141.1 2.7 %collective-permute-done.30 = bf16[256,512]{1,0:T(8,128)(2,1)S(1)} collective-permute-done((bf16[256,512]{1,0:T(8,128)(2,1)}, bf16[256,512]{1,0:T(8,128)(2,1)S(1)}, u32[]{:S(2)}, u32[]{:S(2)}) %collective-permute-start.30) | collective-permute-done | bytes 262176 | tf_op jit(solution)/shard_map/ppermute | solution.py:32
  143.9 1.7 %fusion.1 = f32[256,512]{1,0:T(8,128)S(1)} fusion(bf16[768,512]{1,0:T(8,128)(2,1)} %copy-done.1, bf16[256,512]{1,0:T(8,128)(2,1)S(1)} %collective-permute-done.30, bf16[256,512]{1,0:T(8,128)(2,1)} %collective-permute-done.27, bf16[768,4096]{1,0:T(8,128)(2,1)} %shard_map.65.refs_0_.refs_1_.refs_2_.refs_3_.refs_4_.refs_5_.refs_6_.refs_7_.refs_8_.refs_9_, ...), kind=kOutput, calls=%fused_computation.16 | convolution fusion | flops 201850880 | bytes 2228228 | tf_op jit(solution)/shard_map/dot_general | solution.py:304
  (132 shorter events, 46.3 us)
Async XLA Ops:
  0.0 37.7 %collective-permute-start = (bf16[3,128,4096]{2,1,0:T(8,128)(2,1)}, bf16[3,128,4096]{2,1,0:T(8,128)(2,1)S(1)}, u32[]{:S(2)}, u32[]{:S(2)}) collective-permute-start(bf16[3,128,4096]{2,1,0:T(8,128)(2,1)} %bitcast.52), channel_id=1, source_target_pairs={{0,1},{1,0},{2,3},{3,2},{4,5},{5,4},{6,7},{7,6},{8,9},{9,8},{10,11... | collective-permute-start | bytes 9437192 | tf_op jit(solution)/shard_map/ppermute | solution.py:40
  3.7 9.7 %collective-permute-start.1 = (bf16[256,512]{1,0:T(8,128)(2,1)}, bf16[256,512]{1,0:T(8,128)(2,1)S(1)}, u32[]{:S(2)}, u32[]{:S(2)}) collective-permute-start(bf16[256,512]{1,0:T(8,128)(2,1)} %get-tuple-element.18.refs_10_), channel_id=1, source_target_pairs={{0,4},{4,8},{8,12},{12,14},{14,10},{10,6},{6,2},{2,0},{1,5},{5,9},... | collective-permute-start | bytes 786440 | tf_op jit(solution)/shard_map/ppermute | solution.py:32
  6.3 14.6 %collective-permute-start.7 = (bf16[256,512]{1,0:T(8,128)(2,1)}, bf16[256,512]{1,0:T(8,128)(2,1)}, u32[]{:S(2)}, u32[]{:S(2)}) collective-permute-start(bf16[256,512]{1,0:T(8,128)(2,1)} %get-tuple-element.18.refs_10_), channel_id=1, source_target_pairs={{0,2},{4,0},{8,4},{12,8},{14,12},{10,14},{6,10},{2,6},{1,3},{5,1},... | collective-permute-start | bytes 786440 | tf_op jit(solution)/shard_map/ppermute | solution.py:32
  8.2 14.9 %collective-permute-start.9 = (bf16[256,512]{1,0:T(8,128)(2,1)}, bf16[256,512]{1,0:T(8,128)(2,1)}, u32[]{:S(2)}, u32[]{:S(2)}) collective-permute-start(bf16[256,512]{1,0:T(8,128)(2,1)} %collective-permute-done.6.refs_11_), channel_id=1, source_target_pairs={{0,2},{4,0},{8,4},{12,8},{14,12},{10,14},{6,10},{2,6},{1,3},{5,1},... | collective-permute-start | bytes 786440 | tf_op jit(solution)/shard_map/ppermute | solution.py:32
  10.8 13.9 %collective-permute-start.8 = (bf16[256,512]{1,0:T(8,128)(2,1)}, bf16[256,512]{1,0:T(8,128)(2,1)}, u32[]{:S(2)}, u32[]{:S(2)}) collective-permute-start(bf16[256,512]{1,0:T(8,128)(2,1)} %collective-permute-done.6.refs_11_), channel_id=1, source_target_pairs={{0,4},{4,8},{8,12},{12,14},{14,10},{10,6},{6,2},{2,0},{1,5},{5,9},... | collective-permute-start | bytes 786440 | tf_op jit(solution)/shard_map/ppermute | solution.py:32
  14.1 9.0 %collective-permute-start.2 = (s32[3,136]{1,0:T(4,128)S(1)}, s32[3,136]{1,0:T(4,128)S(1)}, u32[]{:S(2)}, u32[]{:S(2)}) collective-permute-start(s32[3,136]{1,0:T(4,128)S(1)} %pad_add_fusion.1), channel_id=1, source_target_pairs={{0,1},{1,0},{2,3},{3,2},{4,5},{5,4},{6,7},{7,6},{8,9},{9,8},{10,11... | collective-permute-start | bytes 4904 | tf_op jit(solution)/shard_map/ppermute | solution.py:40
  20.9 24.8 %collective-permute-start.3 = (bf16[256,512]{1,0:T(8,128)(2,1)S(1)}, bf16[256,512]{1,0:T(8,128)(2,1)}, u32[]{:S(2)}, u32[]{:S(2)}) collective-permute-start(bf16[256,512]{1,0:T(8,128)(2,1)S(1)} %collective-permute-done.1.refs_12_), channel_id=1, source_target_pairs={{0,4},{4,8},{8,12},{12,14},{14,10},{10,6},{6,2},{2,0},{1,5},{5,9},... | collective-permute-start | bytes 786440 | tf_op jit(solution)/shard_map/ppermute | solution.py:32
  23.1 26.2 %collective-permute-start.10 = (bf16[256,512]{1,0:T(8,128)(2,1)}, bf16[256,512]{1,0:T(8,128)(2,1)}, u32[]{:S(2)}, u32[]{:S(2)}) collective-permute-start(bf16[256,512]{1,0:T(8,128)(2,1)} %collective-permute-done.7.refs_13_), channel_id=1, source_target_pairs={{0,2},{4,0},{8,4},{12,8},{14,12},{10,14},{6,10},{2,6},{1,3},{5,1},... | collective-permute-start | bytes 786440 | tf_op jit(solution)/shard_map/ppermute | solution.py:32
  23.1 14.4 %collective-permute-start.12 = (bf16[256,512]{1,0:T(8,128)(2,1)}, bf16[256,512]{1,0:T(8,128)(2,1)}, u32[]{:S(2)}, u32[]{:S(2)}) collective-permute-start(bf16[256,512]{1,0:T(8,128)(2,1)} %collective-permute-done.9.refs_15_), channel_id=1, source_target_pairs={{0,2},{4,0},{8,4},{12,8},{14,12},{10,14},{6,10},{2,6},{1,3},{5,1},... | collective-permute-start | bytes 786440 | tf_op jit(solution)/shard_map/ppermute | solution.py:32
  24.7 23.0 %collective-permute-start.11 = (bf16[256,512]{1,0:T(8,128)(2,1)}, bf16[256,512]{1,0:T(8,128)(2,1)}, u32[]{:S(2)}, u32[]{:S(2)}) collective-permute-start(bf16[256,512]{1,0:T(8,128)(2,1)} %collective-permute-done.8.refs_14_), channel_id=1, source_target_pairs={{0,4},{4,8},{8,12},{12,14},{14,10},{10,6},{6,2},{2,0},{1,5},{5,9},... | collective-permute-start | bytes 786440 | tf_op jit(solution)/shard_map/ppermute | solution.py:32
  37.5 19.3 %collective-permute-start.13 = (bf16[256,512]{1,0:T(8,128)(2,1)}, bf16[256,512]{1,0:T(8,128)(2,1)}, u32[]{:S(2)}, u32[]{:S(2)}) collective-permute-start(bf16[256,512]{1,0:T(8,128)(2,1)} %collective-permute-done.12.refs_19_), channel_id=1, source_target_pairs={{0,2},{4,0},{8,4},{12,8},{14,12},{10,14},{6,10},{2,6},{1,3},{5,1},... | collective-permute-start | bytes 786440 | tf_op jit(solution)/shard_map/ppermute | solution.py:32
  45.7 11.5 %collective-permute-start.4 = (bf16[256,512]{1,0:T(8,128)(2,1)}, bf16[256,512]{1,0:T(8,128)(2,1)S(1)}, u32[]{:S(2)}, u32[]{:S(2)}) collective-permute-start(bf16[256,512]{1,0:T(8,128)(2,1)} %collective-permute-done.3.refs_16_), channel_id=1, source_target_pairs={{0,4},{4,8},{8,12},{12,14},{14,10},{10,6},{6,2},{2,0},{1,5},{5,9},... | collective-permute-start | bytes 786440 | tf_op jit(solution)/shard_map/ppermute | solution.py:32
  47.7 12.6 %collective-permute-start.16 = (bf16[256,512]{1,0:T(8,128)(2,1)}, bf16[256,512]{1,0:T(8,128)(2,1)S(1)}, u32[]{:S(2)}, u32[]{:S(2)}) collective-permute-start(bf16[256,512]{1,0:T(8,128)(2,1)} %collective-permute-done.11.refs_18_), channel_id=1, source_target_pairs={{0,4},{4,8},{8,12},{12,14},{14,10},{10,6},{6,2},{2,0},{1,5},{5,9},... | collective-permute-start | bytes 786440 | tf_op jit(solution)/shard_map/ppermute | solution.py:32
  49.3 11.0 %collective-permute-start.15 = (bf16[256,512]{1,0:T(8,128)(2,1)}, bf16[256,512]{1,0:T(8,128)(2,1)S(1)}, u32[]{:S(2)}, u32[]{:S(2)}) collective-permute-start(bf16[256,512]{1,0:T(8,128)(2,1)} %collective-permute-done.10.refs_17_), channel_id=1, source_target_pairs={{0,2},{4,0},{8,4},{12,8},{14,12},{10,14},{6,10},{2,6},{1,3},{5,1},... | collective-permute-start | bytes 786440 | tf_op jit(solution)/shard_map/ppermute | solution.py:32
  56.8 10.7 %collective-permute-start.14 = (bf16[256,512]{1,0:T(8,128)(2,1)}, bf16[256,512]{1,0:T(8,128)(2,1)S(1)}, u32[]{:S(2)}, u32[]{:S(2)}) collective-permute-start(bf16[256,512]{1,0:T(8,128)(2,1)} %collective-permute-done.13.refs_7_), channel_id=1, source_target_pairs={{0,2},{4,0},{8,4},{12,8},{14,12},{10,14},{6,10},{2,6},{1,3},{5,1},... | collective-permute-start | bytes 786440 | tf_op jit(solution)/shard_map/ppermute | solution.py:32
  57.1 10.3 %collective-permute-start.5 = (bf16[256,512]{1,0:T(8,128)(2,1)S(1)}, bf16[256,512]{1,0:T(8,128)(2,1)S(1)}, u32[]{:S(2)}, u32[]{:S(2)}) collective-permute-start(bf16[256,512]{1,0:T(8,128)(2,1)S(1)} %collective-permute-done.4.refs_4_), channel_id=1, source_target_pairs={{0,4},{4,8},{8,12},{12,14},{14,10},{10,6},{6,2},{2,0},{1,5},{5,9},... | collective-permute-start | bytes 786440 | tf_op jit(solution)/shard_map/ppermute | solution.py:32
  76.3 8.3 %collective-permute-start.21 = (bf16[6,1024]{1,0:T(8,128)(2,1)S(1)}, bf16[6,1024]{1,0:T(8,128)(2,1)S(1)}, u32[]{:S(2)}, u32[]{:S(2)}) collective-permute-start(bf16[6,1024]{1,0:T(8,128)(2,1)S(1)} %maximum_select_fusion.2), channel_id=1, source_target_pairs={{28,0},{19,1},{30,4},{17,5},{26,8},{21,9},{22,12},{25,13},{18,14},... | collective-permute-start | bytes 36872 | tf_op jit(solution)/shard_map/ppermute | solution.py:52
  80.2 8.7 %collective-permute-start.18 = (bf16[6,1024]{1,0:T(8,128)(2,1)S(1)}, bf16[6,1024]{1,0:T(8,128)(2,1)S(1)}, u32[]{:S(2)}, u32[]{:S(2)}) collective-permute-start(bf16[6,1024]{1,0:T(8,128)(2,1)S(1)} %maximum_select_fusion.2), channel_id=1, source_target_pairs={{16,0},{31,1},{20,4},{27,5},{24,8},{23,9},{28,12},{19,13},{30,14},... | collective-permute-start | bytes 36872 | tf_op jit(solution)/shard_map/ppermute | solution.py:52
  92.7 40.6 %collective-permute-start.24 = (bf16[256,1024]{1,0:T(8,128)(2,1)S(1)}, bf16[256,1024]{1,0:T(8,128)(2,1)S(1)}, u32[]{:S(2)}, u32[]{:S(2)}) collective-permute-start(bf16[256,1024]{1,0:T(8,128)(2,1)S(1)} %convert_element_type.128), channel_id=1, source_target_pairs={{0,16},{1,17},{2,18},{3,19},{4,20},{5,21},{6,22},{7,23},{8,24},{9,... | collective-permute-start | bytes 1572872 | tf_op jit(solution)/shard_map/ppermute | solution.py:301
  96.2 8.4 %collective-permute-start.23 = (bf16[256,512]{1,0:T(8,128)(2,1)S(1)}, bf16[256,512]{1,0:T(8,128)(2,1)S(1)}, u32[]{:S(2)}, u32[]{:S(2)}) collective-permute-start(bf16[256,512]{1,0:T(8,128)(2,1)S(1)} %convolution_convert_fusion.3), channel_id=1, source_target_pairs={{0,4},{4,8},{8,12},{12,14},{14,10},{10,6},{6,2},{2,0},{1,5},{5,9},... | collective-permute-start | bytes 786440 | tf_op jit(solution)/shard_map/ppermute | solution.py:32
  97.8 9.3 %collective-permute-start.28 = (bf16[256,512]{1,0:T(8,128)(2,1)S(1)}, bf16[256,512]{1,0:T(8,128)(2,1)S(1)}, u32[]{:S(2)}, u32[]{:S(2)}) collective-permute-start(bf16[256,512]{1,0:T(8,128)(2,1)S(1)} %convolution_convert_fusion.2), channel_id=1, source_target_pairs={{0,2},{4,0},{8,4},{12,8},{14,12},{10,14},{6,10},{2,6},{1,3},{5,1},... | collective-permute-start | bytes 786440 | tf_op jit(solution)/shard_map/ppermute | solution.py:32
  101.1 11.6 %collective-permute-start.34 = (bf16[256,512]{1,0:T(8,128)(2,1)S(1)}, bf16[256,512]{1,0:T(8,128)(2,1)S(1)}, u32[]{:S(2)}, u32[]{:S(2)}) collective-permute-start(bf16[256,512]{1,0:T(8,128)(2,1)S(1)} %convolution_convert_fusion), channel_id=1, source_target_pairs={{0,2},{4,0},{8,4},{12,8},{14,12},{10,14},{6,10},{2,6},{1,3},{5,1},... | collective-permute-start | bytes 786440 | tf_op jit(solution)/shard_map/ppermute | solution.py:32
  103.9 11.8 %collective-permute-start.31 = (bf16[256,512]{1,0:T(8,128)(2,1)S(1)}, bf16[256,512]{1,0:T(8,128)(2,1)S(1)}, u32[]{:S(2)}, u32[]{:S(2)}) collective-permute-start(bf16[256,512]{1,0:T(8,128)(2,1)S(1)} %convolution_convert_fusion.1), channel_id=1, source_target_pairs={{0,4},{4,8},{8,12},{12,14},{14,10},{10,6},{6,2},{2,0},{1,5},{5,9},... | collective-permute-start | bytes 786440 | tf_op jit(solution)/shard_map/ppermute | solution.py:32
  108.5 23.8 %collective-permute-start.29 = (bf16[256,512]{1,0:T(8,128)(2,1)S(1)}, bf16[256,512]{1,0:T(8,128)(2,1)S(1)}, u32[]{:S(2)}, u32[]{:S(2)}) collective-permute-start(bf16[256,512]{1,0:T(8,128)(2,1)S(1)} %fusion.5), channel_id=1, source_target_pairs={{0,2},{4,0},{8,4},{12,8},{14,12},{10,14},{6,10},{2,6},{1,3},{5,1},... | collective-permute-start | bytes 786440 | tf_op jit(solution)/shard_map/ppermute | solution.py:32
  113.1 9.6 %collective-permute-start.35 = (bf16[256,512]{1,0:T(8,128)(2,1)S(1)}, bf16[256,512]{1,0:T(8,128)(2,1)S(1)}, u32[]{:S(2)}, u32[]{:S(2)}) collective-permute-start(bf16[256,512]{1,0:T(8,128)(2,1)S(1)} %fusion.10), channel_id=1, source_target_pairs={{0,2},{4,0},{8,4},{12,8},{14,12},{10,14},{6,10},{2,6},{1,3},{5,1},... | collective-permute-start | bytes 786440 | tf_op jit(solution)/shard_map/ppermute | solution.py:32
  115.5 9.4 %collective-permute-start.25 = (bf16[256,512]{1,0:T(8,128)(2,1)S(1)}, bf16[256,512]{1,0:T(8,128)(2,1)S(1)}, u32[]{:S(2)}, u32[]{:S(2)}) collective-permute-start(bf16[256,512]{1,0:T(8,128)(2,1)S(1)} %fusion.4), channel_id=1, source_target_pairs={{0,4},{4,8},{8,12},{12,14},{14,10},{10,6},{6,2},{2,0},{1,5},{5,9},... | collective-permute-start | bytes 786440 | tf_op jit(solution)/shard_map/ppermute | solution.py:32
  116.1 10.2 %collective-permute-start.32 = (bf16[256,512]{1,0:T(8,128)(2,1)S(1)}, bf16[256,512]{1,0:T(8,128)(2,1)S(1)}, u32[]{:S(2)}, u32[]{:S(2)}) collective-permute-start(bf16[256,512]{1,0:T(8,128)(2,1)S(1)} %fusion.7), channel_id=1, source_target_pairs={{0,4},{4,8},{8,12},{12,14},{14,10},{10,6},{6,2},{2,0},{1,5},{5,9},... | collective-permute-start | bytes 786440 | tf_op jit(solution)/shard_map/ppermute | solution.py:32
  125.3 9.5 %collective-permute-start.26 = (bf16[256,512]{1,0:T(8,128)(2,1)S(1)}, bf16[256,512]{1,0:T(8,128)(2,1)S(1)}, u32[]{:S(2)}, u32[]{:S(2)}) collective-permute-start(bf16[256,512]{1,0:T(8,128)(2,1)S(1)} %fusion.3), channel_id=1, source_target_pairs={{0,4},{4,8},{8,12},{12,14},{14,10},{10,6},{6,2},{2,0},{1,5},{5,9},... | collective-permute-start | bytes 786440 | tf_op jit(solution)/shard_map/ppermute | solution.py:32
  126.7 12.5 %collective-permute-start.33 = (bf16[256,512]{1,0:T(8,128)(2,1)S(1)}, bf16[256,512]{1,0:T(8,128)(2,1)S(1)}, u32[]{:S(2)}, u32[]{:S(2)}) collective-permute-start(bf16[256,512]{1,0:T(8,128)(2,1)S(1)} %fusion.6), channel_id=1, source_target_pairs={{0,4},{4,8},{8,12},{12,14},{14,10},{10,6},{6,2},{2,0},{1,5},{5,9},... | collective-permute-start | bytes 786440 | tf_op jit(solution)/shard_map/ppermute | solution.py:32
  131.3 9.3 %collective-permute-start.37 = (bf16[256,512]{1,0:T(8,128)(2,1)S(1)}, bf16[256,512]{1,0:T(8,128)(2,1)S(1)}, u32[]{:S(2)}, u32[]{:S(2)}) collective-permute-start(bf16[256,512]{1,0:T(8,128)(2,1)S(1)} %fusion.8), channel_id=1, source_target_pairs={{0,2},{4,0},{8,4},{12,8},{14,12},{10,14},{6,10},{2,6},{1,3},{5,1},... | collective-permute-start | bytes 786440 | tf_op jit(solution)/shard_map/ppermute | solution.py:32
  133.4 10.5 %collective-permute-start.30 = (bf16[256,512]{1,0:T(8,128)(2,1)}, bf16[256,512]{1,0:T(8,128)(2,1)S(1)}, u32[]{:S(2)}, u32[]{:S(2)}) collective-permute-start(bf16[256,512]{1,0:T(8,128)(2,1)} %convolution_add_fusion.7), channel_id=1, source_target_pairs={{0,2},{4,0},{8,4},{12,8},{14,12},{10,14},{6,10},{2,6},{1,3},{5,1},... | collective-permute-start | bytes 786440 | tf_op jit(solution)/shard_map/ppermute | solution.py:32
  135.9 8.0 %collective-permute-start.27 = (bf16[256,512]{1,0:T(8,128)(2,1)}, bf16[256,512]{1,0:T(8,128)(2,1)}, u32[]{:S(2)}, u32[]{:S(2)}) collective-permute-start(bf16[256,512]{1,0:T(8,128)(2,1)} %convolution_add_fusion.10), channel_id=1, source_target_pairs={{0,4},{4,8},{8,12},{12,14},{14,10},{10,6},{6,2},{2,0},{1,5},{5,9},... | collective-permute-start | bytes 786440 | tf_op jit(solution)/shard_map/ppermute | solution.py:32
  (20 other events, 222.7 us)

commit v6 on v5

--- a/solution.py
+++ b/solution.py
@@ -10,7 +10,7 @@
 sharpness = 20.0
 cores = 2
 longest_ring = 16
-vmem_limit = 60 << 20
+vmem_limit = 63 << 20
 
 
 def ring_order(chips):
@@ -63,43 +63,13 @@
     )
 
 
-def halves_kernel(core_ref, own_ref, other_ref, own_out, other_out):
-    own_out[...] = own_ref[...].astype(jnp.bfloat16)
-    other_out[...] = other_ref[...].astype(jnp.bfloat16)
-
-
-def cut_halves(weights, core):
-    rows, embedding = weights.shape
-    half = embedding // cores
-    tile = rows // 4 if rows % 64 == 0 else rows
-    read = (tile, half)
-    written = pl.BlockSpec((tile, half), lambda i, core: (i, 0))
-    return pl.pallas_call(
-        halves_kernel,
-        grid_spec=pltpu.PrefetchScalarGridSpec(
-            num_scalar_prefetch=1,
-            grid=(rows // tile,),
-            in_specs=[
-                pl.BlockSpec(read, lambda i, core: (i, core[0])),
-                pl.BlockSpec(read, lambda i, core: (i, 1 - core[0])),
-            ],
-            out_specs=[written, written],
-        ),
-        out_shape=[jax.ShapeDtypeStruct((rows, half), jnp.bfloat16)] * 2,
-        compiler_params=pltpu.CompilerParams(vmem_limit_bytes=vmem_limit),
-        cost_estimate=pl.CostEstimate(
-            flops=0, bytes_accessed=6 * rows * embedding, transcendentals=0
-        ),
-    )(core[None].astype(jnp.int32), weights, weights)
-
-
 def normalize_kernel(chunk, states_ref, gain_ref, *refs):
     out_ref = refs[-1]
 
-    @pl.loop(0, states_ref.shape[1] // chunk)
+    @pl.loop(0, states_ref.shape[0] // chunk)
     def _(i):
         at = pl.ds(pl.multiple_of(i * chunk, chunk), chunk)
-        wide = states_ref[0, at, :].astype(jnp.float32)
+        wide = states_ref[at, :].astype(jnp.float32)
         mean_square = jnp.mean(wide * wide, axis=-1, keepdims=True)
         wide = wide * lax.rsqrt(mean_square + 1e-05) * gain_ref[...]
         out_ref[at, :] = wide.astype(jnp.bfloat16)
@@ -108,19 +78,21 @@
 def normalize(states, gain, part, filled=None):
     seqs, length, width = states.shape
     tokens = seqs * length
+    tile = 32 if length % 32 == 0 else length
+    steps = tokens // tile
     in_specs = [
-        pl.BlockSpec((1, length, width), lambda i: (i, 0, 0)),
+        pl.BlockSpec((tile, width), lambda i: (i, 0)),
         pl.BlockSpec((1, width), lambda i: (0, 0)),
     ]
-    operands = [states, gain[None]]
+    operands = [states.reshape(tokens, width), gain[None]]
     if filled is not None:
         in_specs.append(pl.BlockSpec(memory_space=pl.ANY))
         operands.append(filled)
     return pl.pallas_call(
         functools.partial(normalize_kernel, 16),
-        grid=(seqs,),
+        grid=(steps,),
         in_specs=in_specs,
-        out_specs=pl.BlockSpec((length, width), lambda i: (part * seqs + i, 0)),
+        out_specs=pl.BlockSpec((tile, width), lambda i: (part * steps + i, 0)),
         out_shape=jax.ShapeDtypeStruct((cores * tokens, width), jnp.bfloat16),
         input_output_aliases={} if filled is None else {2: 0},
         compiler_params=pltpu.CompilerParams(vmem_limit_bytes=vmem_limit),
@@ -130,11 +102,16 @@
     )(*operands)
 
 
-def blocks_kernel(amount, has_total, last, length, offsets_ref, counts_ref, *refs):
-    columns, blocks, rest = refs[:amount], refs[amount : 2 * amount], refs[2 * amount :]
+def blocks_kernel(sources, chips, has_total, last, where_ref, counts_ref, normed_ref, *refs):
+    blocks, rest = refs[: len(sources)], refs[len(sources) :]
+    rows = blocks[0].shape[0]
+    place, core = where_ref[0], where_ref[1]
     total = None
-    for column, block in zip(columns, blocks):
-        term = jnp.dot(column[...], block[...], preferred_element_type=jnp.float32)
+    for (offset, part), block in zip(sources, blocks):
+        part = core if part == 0 else 1 - core
+        first = (ring_chip(place + offset, chips) * cores + part) * rows
+        columns = normed_ref[:, pl.ds(pl.multiple_of(first, rows), rows)]
+        term = jnp.dot(columns, block[...], preferred_element_type=jnp.float32)
         total = term if total is None else total + term
     if has_total:
         total = total + rest[0][...]
@@ -143,50 +120,40 @@
         rest[0][...] = total
         return
     slope_ref, pooled_ref = rest
-    active = jnp.tanh(total)
-    seqs = active.shape[0] // length
-    active = active.reshape(seqs, length, active.shape[1])
-    for i in range(seqs):
-        count = counts_ref[pl.program_id(0) * seqs + i]
-        there = lax.broadcasted_iota(jnp.int32, active.shape[1:], 0) < count
-        part = jnp.where(there, active[i], 0.0)
-        pooled_ref[i] = jnp.sum(part, axis=0, keepdims=True)
-        slope_ref[pl.ds(i * length, length), :] = jnp.where(there, 1.0 - part * part, 0.0)
-
-
-def add_blocks(normed, offsets, blocks, total, counts, length, last):
-    tokens = normed.shape[0]
+    there = lax.broadcasted_iota(jnp.int32, total.shape, 0) < counts_ref[pl.program_id(0)]
+    active = jnp.where(there, jnp.tanh(total), 0.0)
+    pooled_ref[0] = jnp.sum(active, axis=0, keepdims=True)
+    slope_ref[...] = jnp.where(there, 1.0 - active * active, 0.0)
+
+
+def add_blocks(normed, where, sources, blocks, total, counts, chips, length, last):
+    tokens, width = normed.shape
     rows, half = blocks[0].shape
-    amount = len(blocks)
-    tile = 2 * length if tokens % (2 * length) == 0 else length
-    in_specs = [
-        pl.BlockSpec((tile, rows), lambda i, offsets, counts, b=b: (i, offsets[b]))
-        for b in range(amount)
-    ]
-    in_specs += [pl.BlockSpec((rows, half), lambda i, offsets, counts: (0, 0))] * amount
-    operands = [normed] * amount + list(blocks)
-    whole = pl.BlockSpec((tile, half), lambda i, offsets, counts: (i, 0))
+    whole = pl.BlockSpec((length, half), lambda i, where, counts: (i, 0))
+    in_specs = [pl.BlockSpec((length, width), lambda i, where, counts: (i, 0))]
+    in_specs += [pl.BlockSpec((rows, half), lambda i, where, counts: (0, 0))] * len(blocks)
+    operands = [normed] + list(blocks)
     if total is not None:
         in_specs.append(whole)
         operands.append(total)
     out_specs = whole
     out_shape = jax.ShapeDtypeStruct((tokens, half), jnp.float32)
     if last:
-        out_specs = [whole, pl.BlockSpec((tile // length, 1, half), lambda i, offsets, counts: (i, 0, 0))]
+        out_specs = [whole, pl.BlockSpec((1, 1, half), lambda i, where, counts: (i, 0, 0))]
         out_shape = [out_shape, jax.ShapeDtypeStruct((tokens // length, 1, half), jnp.float32)]
     return pl.pallas_call(
-        functools.partial(blocks_kernel, amount, total is not None, last, length),
+        functools.partial(blocks_kernel, sources, chips, total is not None, last),
         grid_spec=pltpu.PrefetchScalarGridSpec(
-            num_scalar_prefetch=2, grid=(tokens // tile,), in_specs=in_specs, out_specs=out_specs
+            num_scalar_prefetch=2, grid=(tokens // length,), in_specs=in_specs, out_specs=out_specs
         ),
         out_shape=out_shape,
         compiler_params=pltpu.CompilerParams(vmem_limit_bytes=vmem_limit),
         cost_estimate=pl.CostEstimate(
-            flops=2 * tokens * rows * half * amount,
-            bytes_accessed=2 * amount * rows * (tokens + half) + 8 * tokens * half,
+            flops=2 * tokens * rows * half * len(blocks),
+            bytes_accessed=2 * tokens * width + 2 * len(blocks) * rows * half + 8 * tokens * half,
             transcendentals=tokens * half if last else 0,
         ),
-    )(offsets, counts, *operands)
+    )(where, counts, *operands)
 
 
 def shards(token_states, token_ids, master, gain, cand_ids, slab_owner):
@@ -202,7 +169,9 @@
     seqs = cores * seq_dev
 
     weights = master[0]
-    own, given = cut_halves(weights, core)
+    own = lax.dynamic_slice(weights, (0, core * half), (rows, half)).astype(jnp.bfloat16)
+    given = lax.dynamic_slice(weights, (0, (1 - core) * half), (rows, half))
+    given = given.astype(jnp.bfloat16)
     sibling = from_sibling(given)
 
     normed = normalize(states, gain, 0)
@@ -215,18 +184,16 @@
     counts = lengths.astype(jnp.float32)
     cands = ids[:, length:]
 
-    def first_column(offset, part):
-        return ring_chip(place + offset, chips) * cores + part
-
     def columns(offset, part):
-        first = first_column(offset, part) * rows
+        first = (ring_chip(place + offset, chips) * cores + part) * rows
         return lax.dynamic_slice(normed, (0, first), (seqs * length, rows))
 
     parts = (core, 1 - core)
     if chips <= longest_ring:
         moving = {(i, by): block for by in (1, -1) for i, block in enumerate((own, sibling))}
         total, first = None, None
-        blocks, offsets = [own, sibling], [first_column(0, part) for part in parts]
+        where = jnp.stack([place, core]).astype(jnp.int32)
+        blocks, sources = [own, sibling], [(0, 0), (0, 1)]
         for step in range(1, chips // 2 + 1):
             last = step == chips // 2
             sent = [(0, 1), (1, -1)] if last else [(0, 1), (0, -1), (1, 1), (1, -1)]
@@ -234,18 +201,19 @@
                 if (step, i, by) == (1, 0, 1):
                     moving[i, by] = first_sent
                 else:
-                    if last and i == 1:
+                    if last and i == 1 and first is not None:
                         moving[i, by] = after(first, moving[i, by])
                     elif step == 3 and i == 0:
                         moving[i, by] = after(normed, moving[i, by])
                     moving[i, by] = along_ring(moving[i, by], by)
                 blocks.append(moving[i, by])
-                offsets.append(first_column(-by * step, parts[i]))
-            if step == 1:
-                continue
-            total = add_blocks(normed, jnp.stack(offsets), blocks, total, lengths, length, last)
-            first = total if first is None else first
-            blocks, offsets = [], []
+                sources.append((-by * step, i))
+            if last or step == chips // 2 - 2:
+                total = add_blocks(
+                    normed, where, sources, blocks, total, lengths, chips, length, last
+                )
+                first = total
+                blocks, sources = [], []
         slope, pooled = total
         pooled = pooled[:, 0] / counts[:, None]
     else:

time: 148 us -> 147 us (level)
  waiting for transfers between devices: 43.7 us -> 38.8 us
  local copies, waits for them, and re-layouts: 7.34 us -> 3.58 us
  starting transfers between devices: 38.9 us -> 42.5 us
  other arithmetic: 8.06 us -> 10.3 us
  Pallas kernels: 33.7 us -> 35.3 us
    ppermute x28, waiting for transfers between devices: 34.7 us -> 28.6 us  [along_ring(): return lax.ppermute(block, 'chip', pairs)]
    unnamed x27 -> x23, local copies, waits for them, and re-layouts: 5.17 us -> 0.73 us
    ppermute x28, starting transfers between devices: 30.9 us -> 34.6 us  [along_ring(): return lax.ppermute(block, 'chip', pairs)]
    pallas_call x6 -> x4, Pallas kernels: 33.7 us -> 35.3 us  [the longest x2 18.8 us: normalize(): pl.pallas_call(functools.partial(normalize_kernel, 16), grid=(steps,), in...]
  transfers between devices with their start and end apart: 39 -> 39, of which waited for: 18 -> 20; matrix products, arithmetic and copies ran while one was open for 14% -> 15% of each run, Pallas kernels for 19% -> 19%
where the time goes in v6:
time: 147 us; the launch traced here: 146 us
  starting transfers between devices  42.5 us (29%)
  waiting for transfers between devices  38.8 us (26%)
  Pallas kernels  35.3 us (24%)
  matrix products  14.7 us (10%)
  other arithmetic  10.3 us (7%)
  local copies, waits for them, and re-layouts  3.58 us (2%)
    ppermute x28, starting transfers between devices, along_ring(): return lax.ppermute(block, 'chip', pairs)  34.6 us
    ppermute x28, waiting for transfers between devices, along_ring(): return lax.ppermute(block, 'chip', pairs)  28.6 us
    pallas_call x2, Pallas kernels, normalize(): pl.pallas_call(functools.partial(normalize_kernel, 16), grid=(steps,), in...  18.8 us
    pallas_call x2, Pallas kernels, add_blocks(): pl.pallas_call(functools.partial(blocks_kernel, sources, chips, total is...  16.5 us
    dot_general x16, matrix products, term(): lax.dot_general(columns(offset, part), delta, (((0,), (0,)), ((), ())), p...  14 us
    ppermute x4, waiting for transfers between devices, slab_blocks(): kept.append(lax.ppermute(stored, ('grp', 'chip', 'core'), pairs))  6.71 us
    ppermute x4, starting transfers between devices, slab_blocks(): kept.append(lax.ppermute(stored, ('grp', 'chip', 'core'), pairs))  5.16 us
    ppermute x6, waiting for transfers between devices, from_sibling(): return lax.ppermute(block, 'core', [(0, 1), (1, 0)])  3.51 us
  transfers between devices with their start and end apart: 39, of which 20 were waited for; matrix products, arithmetic and copies ran while one was open for 15% of the time, Pallas kernels for 19%

profile of v6, /device:TPU:0, one launch (start us, length us, event | category | flops | bytes accessed | tf_op | source)
XLA Modules:
  0.0 145.6 jit_solution(15025304572205298259)
XLA Ops:
  1.9 3.0 %collective-permute-start.1 = (bf16[256,512]{1,0:T(8,128)(2,1)S(1)}, bf16[256,512]{1,0:T(8,128)(2,1)S(1)}, u32[]{:S(2)}, u32[]{:S(2)}) collective-permute-start(bf16[256,512]{1,0:T(8,128)(2,1)S(1)} %get-tuple-element.32.refs_0_), channel_id=1, source_target_pairs={{0,4},{4,8},{8,12},{12,14},{14,10},{10,6},{6,2},{2,0},{1,5},{5,9},... | collective-permute-start | bytes 786440 | tf_op jit(solution)/shard_map/ppermute | solution.py:32
  6.1 2.9 %collective-permute-start.12 = (bf16[256,512]{1,0:T(8,128)(2,1)S(1)}, bf16[256,512]{1,0:T(8,128)(2,1)}, u32[]{:S(2)}, u32[]{:S(2)}) collective-permute-start(bf16[256,512]{1,0:T(8,128)(2,1)S(1)} %collective-permute-done.8.refs_1_), channel_id=1, source_target_pairs={{0,2},{4,0},{8,4},{12,8},{14,12},{10,14},{6,10},{2,6},{1,3},{5,1},... | collective-permute-start | bytes 786440 | tf_op jit(solution)/shard_map/ppermute | solution.py:32
  11.4 1.8 %collective-permute-start.9 = (bf16[256,512]{1,0:T(8,128)(2,1)S(1)}, bf16[256,512]{1,0:T(8,128)(2,1)}, u32[]{:S(2)}, u32[]{:S(2)}) collective-permute-start(bf16[256,512]{1,0:T(8,128)(2,1)S(1)} %collective-permute-done.8.refs_1_), channel_id=1, source_target_pairs={{0,4},{4,8},{8,12},{12,14},{14,10},{10,6},{6,2},{2,0},{1,5},{5,9},... | collective-permute-start | bytes 786440 | tf_op jit(solution)/shard_map/ppermute | solution.py:32
  14.2 1.6 %collective-permute-start.3 = (bf16[256,512]{1,0:T(8,128)(2,1)S(1)}, bf16[256,512]{1,0:T(8,128)(2,1)}, u32[]{:S(2)}, u32[]{:S(2)}) collective-permute-start(bf16[256,512]{1,0:T(8,128)(2,1)S(1)} %collective-permute-done.1.refs_2_), channel_id=1, source_target_pairs={{0,4},{4,8},{8,12},{12,14},{14,10},{10,6},{6,2},{2,0},{1,5},{5,9},... | collective-permute-start | bytes 786440 | tf_op jit(solution)/shard_map/ppermute | solution.py:32
  15.8 2.8 %collective-permute-done.12.refs_5_ = bf16[256,512]{1,0:T(8,128)(2,1)} collective-permute-done((bf16[256,512]{1,0:T(8,128)(2,1)S(1)}, bf16[256,512]{1,0:T(8,128)(2,1)}, u32[]{:S(2)}, u32[]{:S(2)}) %collective-permute-start.12) | collective-permute-done | bytes 262176 | tf_op jit(solution)/shard_map/ppermute | solution.py:32
  19.6 1.7 %collective-permute-start.6 = (bf16[256,512]{1,0:T(8,128)(2,1)}, bf16[256,512]{1,0:T(8,128)(2,1)}, u32[]{:S(2)}, u32[]{:S(2)}) collective-permute-start(bf16[256,512]{1,0:T(8,128)(2,1)} %collective-permute-done.5.refs_3_), channel_id=1, source_target_pairs={{0,2},{4,0},{8,4},{12,8},{14,12},{10,14},{6,10},{2,6},{1,3},{5,1},... | collective-permute-start | bytes 786440 | tf_op jit(solution)/shard_map/ppermute | solution.py:32
  23.2 9.4 %shard_map.64.refs_0_ = bf16[768,4096]{1,0:T(8,128)(2,1)} custom-call(bf16[384,4096]{1,0:T(8,128)(2,1)} %bitcast.41, f32[1,4096]{1,0:T(1,128)} %bitcast.43), custom_call_target="tpu_custom_call" | custom-call | flops 9437184 | bytes 6291456 | tf_op jit(solution)/shard_map/pallas_call | solution.py:91
  33.4 9.4 %shard_map.65.normed_ref = bf16[768,4096]{1,0:T(8,128)(2,1)} custom-call(bf16[384,4096]{1,0:T(8,128)(2,1)} %bitcast.1.states_ref, f32[1,4096]{1,0:T(1,128)} %bitcast.44, bf16[768,4096]{1,0:T(8,128)(2,1)} %shard_map.64.refs_0_), custom_call_target="tpu_custom_call", output_to_operand_aliasing={{}: (2, {})} | custom-call | flops 9437184 | bytes 6291456 | tf_op jit(solution)/shard_map/pallas_call | solution.py:91
  44.8 1.6 %collective-permute-start.11 = (bf16[256,512]{1,0:T(8,128)(2,1)}, bf16[256,512]{1,0:T(8,128)(2,1)S(1)}, u32[]{:S(2)}, u32[]{:S(2)}) collective-permute-start(bf16[256,512]{1,0:T(8,128)(2,1)} %collective-permute-done.10.refs_8_), channel_id=1, source_target_pairs={{0,4},{4,8},{8,12},{12,14},{14,10},{10,6},{6,2},{2,0},{1,5},{5,9},... | collective-permute-start | bytes 786440 | tf_op jit(solution)/shard_map/ppermute | solution.py:32
  46.8 8.4 %shard_map.66.refs_6_ = f32[768,512]{1,0:T(8,128)} custom-call(s32[2]{0:T(128)} %pad_add_fusion.2.where_ref, s32[6]{0:T(128)} %convert_reduce_fusion.2.counts_ref, bf16[768,4096]{1,0:T(8,128)(2,1)} %shard_map.65.normed_ref, bf16[256,512]{1,0:T(8,128)(2,1)} %copy-done, bf16[256,512]{1,0:T(8,128)(2,1)} %copy-done.2, bf16[256,512]{1,0:T(8,128)(2,1)} %copy-done.3, ...), custom_call_target="tpu_custom_call" | custom-call | flops 2013265920 | bytes 12058624 | tf_op jit(solution)/shard_map/pallas_call | solution.py:144
  58.4 3.6 %collective-permute-done.16.refs_5_ = bf16[256,512]{1,0:T(8,128)(2,1)} collective-permute-done((bf16[256,512]{1,0:T(8,128)(2,1)}, bf16[256,512]{1,0:T(8,128)(2,1)}, u32[]{:S(2)}, u32[]{:S(2)}) %collective-permute-start.16) | collective-permute-done | bytes 262176 | tf_op jit(solution)/shard_map/ppermute | solution.py:32
  62.6 8.1 %shard_map.67 = (f32[768,512]{1,0:T(8,128)}, f32[6,1,512]{2,1,0:T(1,128)}) custom-call(s32[2]{0:T(128)} %pad_add_fusion.2.where_ref, s32[6]{0:T(128)} %convert_reduce_fusion.2.counts_ref, bf16[768,4096]{1,0:T(8,128)(2,1)} %shard_map.65.normed_ref, bf16[256,512]{1,0:T(8,128)(2,1)} %copy-done.4, bf16[256,512]{1,0:T(8,128)(2,1)} %copy-done.6, ...), custom_call_target="tpu_custom_call" | custom-call | flops 1207959552 | bytes 11010048 | tf_op jit(solution)/shard_map/pallas_call | solution.py:144
  78.8 2.5 %collective-permute-done.21 = bf16[6,1024]{1,0:T(8,128)(2,1)S(1)} collective-permute-done((bf16[6,1024]{1,0:T(8,128)(2,1)S(1)}, bf16[6,1024]{1,0:T(8,128)(2,1)S(1)}, u32[]{:S(2)}, u32[]{:S(2)}) %collective-permute-start.21) | collective-permute-done | bytes 12320 | tf_op jit(solution)/shard_map/ppermute | solution.py:52
  81.3 1.5 %collective-permute-done.20 = bf16[6,1024]{1,0:T(8,128)(2,1)S(1)} collective-permute-done((bf16[6,1024]{1,0:T(8,128)(2,1)S(1)}, bf16[6,1024]{1,0:T(8,128)(2,1)S(1)}, u32[]{:S(2)}, u32[]{:S(2)}) %collective-permute-start.20) | collective-permute-done | bytes 12320 | tf_op jit(solution)/shard_map/ppermute | solution.py:52
  83.2 2.3 %collective-permute-done.18 = bf16[6,1024]{1,0:T(8,128)(2,1)S(1)} collective-permute-done((bf16[6,1024]{1,0:T(8,128)(2,1)S(1)}, bf16[6,1024]{1,0:T(8,128)(2,1)S(1)}, u32[]{:S(2)}, u32[]{:S(2)}) %collective-permute-start.18) | collective-permute-done | bytes 12320 | tf_op jit(solution)/shard_map/ppermute | solution.py:52
  87.7 1.6 %fusion = bf16[768,512]{1,0:T(8,128)(2,1)S(1)} fusion(f32[768,512]{1,0:T(8,128)} %get-tuple-element.21, f32[6,512]{1,0:T(8,128)S(1)} %fusion.35), kind=kLoop, calls=%fused_computation.3 | loop fusion | flops 786432 | bytes 2371584 | tf_op jit(solution)/shard_map/convert_element_type | solution.py:267
  90.6 2.1 %collective-permute-start.24 = (bf16[256,1024]{1,0:T(8,128)(2,1)S(1)}, bf16[256,1024]{1,0:T(8,128)(2,1)S(1)}, u32[]{:S(2)}, u32[]{:S(2)}) collective-permute-start(bf16[256,1024]{1,0:T(8,128)(2,1)S(1)} %convert_element_type.143), channel_id=1, source_target_pairs={{0,16},{1,17},{2,18},{3,19},{4,20},{5,21},{6,22},{7,23},{8,24},{9,... | collective-permute-start | bytes 1572872 | tf_op jit(solution)/shard_map/ppermute | solution.py:269
  92.7 1.4 convolution_convert_fusion.3
  94.2 1.4 convolution_convert_fusion.2
  95.5 2.1 %collective-permute-start.28 = (bf16[256,512]{1,0:T(8,128)(2,1)S(1)}, bf16[256,512]{1,0:T(8,128)(2,1)S(1)}, u32[]{:S(2)}, u32[]{:S(2)}) collective-permute-start(bf16[256,512]{1,0:T(8,128)(2,1)S(1)} %convolution_convert_fusion.2), channel_id=1, source_target_pairs={{0,2},{4,0},{8,4},{12,8},{14,12},{10,14},{6,10},{2,6},{1,3},{5,1},... | collective-permute-start | bytes 786440 | tf_op jit(solution)/shard_map/ppermute | solution.py:32
  102.5 2.3 %collective-permute-done.28 = bf16[256,512]{1,0:T(8,128)(2,1)S(1)} collective-permute-done((bf16[256,512]{1,0:T(8,128)(2,1)S(1)}, bf16[256,512]{1,0:T(8,128)(2,1)S(1)}, u32[]{:S(2)}, u32[]{:S(2)}) %collective-permute-start.28) | collective-permute-done | bytes 262176 | tf_op jit(solution)/shard_map/ppermute | solution.py:32
  104.8 1.4 fusion.5
  106.2 2.1 %collective-permute-start.29 = (bf16[256,512]{1,0:T(8,128)(2,1)S(1)}, bf16[256,512]{1,0:T(8,128)(2,1)S(1)}, u32[]{:S(2)}, u32[]{:S(2)}) collective-permute-start(bf16[256,512]{1,0:T(8,128)(2,1)S(1)} %fusion.5), channel_id=1, source_target_pairs={{0,2},{4,0},{8,4},{12,8},{14,12},{10,14},{6,10},{2,6},{1,3},{5,1},... | collective-permute-start | bytes 786440 | tf_op jit(solution)/shard_map/ppermute | solution.py:32
  108.3 2.1 %collective-permute-done.34 = bf16[256,512]{1,0:T(8,128)(2,1)S(1)} collective-permute-done((bf16[256,512]{1,0:T(8,128)(2,1)S(1)}, bf16[256,512]{1,0:T(8,128)(2,1)S(1)}, u32[]{:S(2)}, u32[]{:S(2)}) %collective-permute-start.34) | collective-permute-done | bytes 262176 | tf_op jit(solution)/shard_map/ppermute | solution.py:32
  110.8 2.1 %collective-permute-start.35 = (bf16[256,512]{1,0:T(8,128)(2,1)S(1)}, bf16[256,512]{1,0:T(8,128)(2,1)S(1)}, u32[]{:S(2)}, u32[]{:S(2)}) collective-permute-start(bf16[256,512]{1,0:T(8,128)(2,1)S(1)} %fusion.10), channel_id=1, source_target_pairs={{0,2},{4,0},{8,4},{12,8},{14,12},{10,14},{6,10},{2,6},{1,3},{5,1},... | collective-permute-start | bytes 786440 | tf_op jit(solution)/shard_map/ppermute | solution.py:32
  114.9 5.6 %collective-permute-done.35 = bf16[256,512]{1,0:T(8,128)(2,1)S(1)} collective-permute-done((bf16[256,512]{1,0:T(8,128)(2,1)S(1)}, bf16[256,512]{1,0:T(8,128)(2,1)S(1)}, u32[]{:S(2)}, u32[]{:S(2)}) %collective-permute-start.35) | collective-permute-done | bytes 262176 | tf_op jit(solution)/shard_map/ppermute | solution.py:32
  121.0 1.8 %collective-permute-start.36 = (bf16[256,512]{1,0:T(8,128)(2,1)S(1)}, bf16[256,512]{1,0:T(8,128)(2,1)S(1)}, u32[]{:S(2)}, u32[]{:S(2)}) collective-permute-start(bf16[256,512]{1,0:T(8,128)(2,1)S(1)} %fusion.9), channel_id=1, source_target_pairs={{0,2},{4,0},{8,4},{12,8},{14,12},{10,14},{6,10},{2,6},{1,3},{5,1},... | collective-permute-start | bytes 786440 | tf_op jit(solution)/shard_map/ppermute | solution.py:32
  125.7 2.9 %collective-permute-done.36 = bf16[256,512]{1,0:T(8,128)(2,1)S(1)} collective-permute-done((bf16[256,512]{1,0:T(8,128)(2,1)S(1)}, bf16[256,512]{1,0:T(8,128)(2,1)S(1)}, u32[]{:S(2)}, u32[]{:S(2)}) %collective-permute-start.36) | collective-permute-done | bytes 262176 | tf_op jit(solution)/shard_map/ppermute | solution.py:32
  134.4 2.7 %collective-permute-done.33 = bf16[256,512]{1,0:T(8,128)(2,1)S(1)} collective-permute-done((bf16[256,512]{1,0:T(8,128)(2,1)S(1)}, bf16[256,512]{1,0:T(8,128)(2,1)S(1)}, u32[]{:S(2)}, u32[]{:S(2)}) %collective-permute-start.33) | collective-permute-done | bytes 262176 | tf_op jit(solution)/shard_map/ppermute | solution.py:32
  138.8 2.8 %collective-permute-done.30 = bf16[256,512]{1,0:T(8,128)(2,1)} collective-permute-done((bf16[256,512]{1,0:T(8,128)(2,1)}, bf16[256,512]{1,0:T(8,128)(2,1)}, u32[]{:S(2)}, u32[]{:S(2)}) %collective-permute-start.30) | collective-permute-done | bytes 262176 | tf_op jit(solution)/shard_map/ppermute | solution.py:32
  141.6 1.5 %fusion.1 = f32[256,512]{1,0:T(8,128)S(1)} fusion(bf16[768,512]{1,0:T(8,128)(2,1)S(1)} %fusion, bf16[256,512]{1,0:T(8,128)(2,1)} %collective-permute-done.30, bf16[256,512]{1,0:T(8,128)(2,1)} %collective-permute-done.27, bf16[768,4096]{1,0:T(8,128)(2,1)} %shard_map.65.normed_ref, s32[]{:T(128)S(6)} %select_n.178), kind=kOutput, calls=%fused_computation.16 | convolution fusion | flops 201850880 | bytes 2228228 | tf_op jit(solution)/shard_map/dot_general | solution.py:272
  143.3 2.3 %select_bitcast_fusion = f32[1,256,1024]{2,1,0:T(8,128)} fusion(bf16[256,1024]{1,0:T(8,128)(2,1)} %copy-done.1, f32[256,512]{1,0:T(8,128)S(1)} %fusion.1, f32[256,512]{1,0:T(8,128)S(1)} %collective-permute-done.38, f32[256]{0:T(256)S(1)} %add_rsqrt_fusion, pred[]{:T(512)S(6)} %eq.66, pred[]{:T(512)S(6)} %eq.65), kind=kLoop, calls=%fused_computation.34 | loop fusion | flops 1572864 | bytes 2622466 | tf_op jit(solution)/shard_map/broadcast_in_dim | solution.py:311
  (125 shorter events, 46.6 us)
Async XLA Ops:
  0.0 33.4 %collective-permute-start = (bf16[3,128,4096]{2,1,0:T(8,128)(2,1)}, bf16[3,128,4096]{2,1,0:T(8,128)(2,1)}, u32[]{:S(2)}, u32[]{:S(2)}) collective-permute-start(bf16[3,128,4096]{2,1,0:T(8,128)(2,1)} %bitcast.40), channel_id=1, source_target_pairs={{0,1},{1,0},{2,3},{3,2},{4,5},{5,4},{6,7},{7,6},{8,9},{9,8},{10,11... | collective-permute-start | bytes 9437192 | tf_op jit(solution)/shard_map/ppermute | solution.py:40
  1.9 9.5 %collective-permute-start.1 = (bf16[256,512]{1,0:T(8,128)(2,1)S(1)}, bf16[256,512]{1,0:T(8,128)(2,1)S(1)}, u32[]{:S(2)}, u32[]{:S(2)}) collective-permute-start(bf16[256,512]{1,0:T(8,128)(2,1)S(1)} %get-tuple-element.32.refs_0_), channel_id=1, source_target_pairs={{0,4},{4,8},{8,12},{12,14},{14,10},{10,6},{6,2},{2,0},{1,5},{5,9},... | collective-permute-start | bytes 786440 | tf_op jit(solution)/shard_map/ppermute | solution.py:32
  4.9 9.3 %collective-permute-start.5 = (bf16[256,512]{1,0:T(8,128)(2,1)S(1)}, bf16[256,512]{1,0:T(8,128)(2,1)}, u32[]{:S(2)}, u32[]{:S(2)}) collective-permute-start(bf16[256,512]{1,0:T(8,128)(2,1)S(1)} %get-tuple-element.32.refs_0_), channel_id=1, source_target_pairs={{0,2},{4,0},{8,4},{12,8},{14,12},{10,14},{6,10},{2,6},{1,3},{5,1},... | collective-permute-start | bytes 786440 | tf_op jit(solution)/shard_map/ppermute | solution.py:32
  6.1 12.5 %collective-permute-start.12 = (bf16[256,512]{1,0:T(8,128)(2,1)S(1)}, bf16[256,512]{1,0:T(8,128)(2,1)}, u32[]{:S(2)}, u32[]{:S(2)}) collective-permute-start(bf16[256,512]{1,0:T(8,128)(2,1)S(1)} %collective-permute-done.8.refs_1_), channel_id=1, source_target_pairs={{0,2},{4,0},{8,4},{12,8},{14,12},{10,14},{6,10},{2,6},{1,3},{5,1},... | collective-permute-start | bytes 786440 | tf_op jit(solution)/shard_map/ppermute | solution.py:32
  11.4 10.0 %collective-permute-start.9 = (bf16[256,512]{1,0:T(8,128)(2,1)S(1)}, bf16[256,512]{1,0:T(8,128)(2,1)}, u32[]{:S(2)}, u32[]{:S(2)}) collective-permute-start(bf16[256,512]{1,0:T(8,128)(2,1)S(1)} %collective-permute-done.8.refs_1_), channel_id=1, source_target_pairs={{0,4},{4,8},{8,12},{12,14},{14,10},{10,6},{6,2},{2,0},{1,5},{5,9},... | collective-permute-start | bytes 786440 | tf_op jit(solution)/shard_map/ppermute | solution.py:32
  14.2 28.7 %collective-permute-start.3 = (bf16[256,512]{1,0:T(8,128)(2,1)S(1)}, bf16[256,512]{1,0:T(8,128)(2,1)}, u32[]{:S(2)}, u32[]{:S(2)}) collective-permute-start(bf16[256,512]{1,0:T(8,128)(2,1)S(1)} %collective-permute-done.1.refs_2_), channel_id=1, source_target_pairs={{0,4},{4,8},{8,12},{12,14},{14,10},{10,6},{6,2},{2,0},{1,5},{5,9},... | collective-permute-start | bytes 786440 | tf_op jit(solution)/shard_map/ppermute | solution.py:32
  18.6 13.9 %collective-permute-start.13 = (bf16[256,512]{1,0:T(8,128)(2,1)}, bf16[256,512]{1,0:T(8,128)(2,1)}, u32[]{:S(2)}, u32[]{:S(2)}) collective-permute-start(bf16[256,512]{1,0:T(8,128)(2,1)} %collective-permute-done.12.refs_5_), channel_id=1, source_target_pairs={{0,2},{4,0},{8,4},{12,8},{14,12},{10,14},{6,10},{2,6},{1,3},{5,1},... | collective-permute-start | bytes 786440 | tf_op jit(solution)/shard_map/ppermute | solution.py:32
  19.6 26.8 %collective-permute-start.6 = (bf16[256,512]{1,0:T(8,128)(2,1)}, bf16[256,512]{1,0:T(8,128)(2,1)}, u32[]{:S(2)}, u32[]{:S(2)}) collective-permute-start(bf16[256,512]{1,0:T(8,128)(2,1)} %collective-permute-done.5.refs_3_), channel_id=1, source_target_pairs={{0,2},{4,0},{8,4},{12,8},{14,12},{10,14},{6,10},{2,6},{1,3},{5,1},... | collective-permute-start | bytes 786440 | tf_op jit(solution)/shard_map/ppermute | solution.py:32
  21.3 23.4 %collective-permute-start.10 = (bf16[256,512]{1,0:T(8,128)(2,1)}, bf16[256,512]{1,0:T(8,128)(2,1)}, u32[]{:S(2)}, u32[]{:S(2)}) collective-permute-start(bf16[256,512]{1,0:T(8,128)(2,1)} %collective-permute-done.9.refs_4_), channel_id=1, source_target_pairs={{0,4},{4,8},{8,12},{12,14},{14,10},{10,6},{6,2},{2,0},{1,5},{5,9},... | collective-permute-start | bytes 786440 | tf_op jit(solution)/shard_map/ppermute | solution.py:32
  32.6 22.7 %collective-permute-start.14 = (bf16[256,512]{1,0:T(8,128)(2,1)}, bf16[256,512]{1,0:T(8,128)(2,1)}, u32[]{:S(2)}, u32[]{:S(2)}) collective-permute-start(bf16[256,512]{1,0:T(8,128)(2,1)} %collective-permute-done.13.refs_9_), channel_id=1, source_target_pairs={{0,2},{4,0},{8,4},{12,8},{14,12},{10,14},{6,10},{2,6},{1,3},{5,1},... | collective-permute-start | bytes 786440 | tf_op jit(solution)/shard_map/ppermute | solution.py:32
  42.9 13.3 %collective-permute-start.4 = (bf16[256,512]{1,0:T(8,128)(2,1)}, bf16[256,512]{1,0:T(8,128)(2,1)S(1)}, u32[]{:S(2)}, u32[]{:S(2)}) collective-permute-start(bf16[256,512]{1,0:T(8,128)(2,1)} %collective-permute-done.3.refs_6_), channel_id=1, source_target_pairs={{0,4},{4,8},{8,12},{12,14},{14,10},{10,6},{6,2},{2,0},{1,5},{5,9},... | collective-permute-start | bytes 786440 | tf_op jit(solution)/shard_map/ppermute | solution.py:32
  44.8 13.6 %collective-permute-start.11 = (bf16[256,512]{1,0:T(8,128)(2,1)}, bf16[256,512]{1,0:T(8,128)(2,1)S(1)}, u32[]{:S(2)}, u32[]{:S(2)}) collective-permute-start(bf16[256,512]{1,0:T(8,128)(2,1)} %collective-permute-done.10.refs_8_), channel_id=1, source_target_pairs={{0,4},{4,8},{8,12},{12,14},{14,10},{10,6},{6,2},{2,0},{1,5},{5,9},... | collective-permute-start | bytes 786440 | tf_op jit(solution)/shard_map/ppermute | solution.py:32
  46.4 12.0 %collective-permute-start.7 = (bf16[256,512]{1,0:T(8,128)(2,1)}, bf16[256,512]{1,0:T(8,128)(2,1)S(1)}, u32[]{:S(2)}, u32[]{:S(2)}) collective-permute-start(bf16[256,512]{1,0:T(8,128)(2,1)} %collective-permute-done.6.refs_7_), channel_id=1, source_target_pairs={{0,2},{4,0},{8,4},{12,8},{14,12},{10,14},{6,10},{2,6},{1,3},{5,1},... | collective-permute-start | bytes 786440 | tf_op jit(solution)/shard_map/ppermute | solution.py:32
  73.0 8.3 %collective-permute-start.21 = (bf16[6,1024]{1,0:T(8,128)(2,1)S(1)}, bf16[6,1024]{1,0:T(8,128)(2,1)S(1)}, u32[]{:S(2)}, u32[]{:S(2)}) collective-permute-start(bf16[6,1024]{1,0:T(8,128)(2,1)S(1)} %maximum_select_fusion.2), channel_id=1, source_target_pairs={{28,0},{19,1},{30,4},{17,5},{26,8},{21,9},{22,12},{25,13},{18,14},... | collective-permute-start | bytes 36872 | tf_op jit(solution)/shard_map/ppermute | solution.py:52
  74.3 8.5 %collective-permute-start.20 = (bf16[6,1024]{1,0:T(8,128)(2,1)S(1)}, bf16[6,1024]{1,0:T(8,128)(2,1)S(1)}, u32[]{:S(2)}, u32[]{:S(2)}) collective-permute-start(bf16[6,1024]{1,0:T(8,128)(2,1)S(1)} %maximum_select_fusion.2), channel_id=1, source_target_pairs={{24,0},{23,1},{28,4},{19,5},{30,8},{17,9},{26,12},{21,13},{22,14},... | collective-permute-start | bytes 36872 | tf_op jit(solution)/shard_map/ppermute | solution.py:52
  75.6 7.7 %collective-permute-start.19 = (bf16[6,1024]{1,0:T(8,128)(2,1)S(1)}, bf16[6,1024]{1,0:T(8,128)(2,1)S(1)}, u32[]{:S(2)}, u32[]{:S(2)}) collective-permute-start(bf16[6,1024]{1,0:T(8,128)(2,1)S(1)} %maximum_select_fusion.2), channel_id=1, source_target_pairs={{20,0},{27,1},{24,4},{23,5},{28,8},{19,9},{30,12},{17,13},{26,14},... | collective-permute-start | bytes 36872 | tf_op jit(solution)/shard_map/ppermute | solution.py:52
  76.9 8.7 %collective-permute-start.18 = (bf16[6,1024]{1,0:T(8,128)(2,1)S(1)}, bf16[6,1024]{1,0:T(8,128)(2,1)S(1)}, u32[]{:S(2)}, u32[]{:S(2)}) collective-permute-start(bf16[6,1024]{1,0:T(8,128)(2,1)S(1)} %maximum_select_fusion.2), channel_id=1, source_target_pairs={{16,0},{31,1},{20,4},{27,5},{24,8},{23,9},{28,12},{19,13},{30,14},... | collective-permute-start | bytes 36872 | tf_op jit(solution)/shard_map/ppermute | solution.py:52
  90.6 40.6 %collective-permute-start.24 = (bf16[256,1024]{1,0:T(8,128)(2,1)S(1)}, bf16[256,1024]{1,0:T(8,128)(2,1)S(1)}, u32[]{:S(2)}, u32[]{:S(2)}) collective-permute-start(bf16[256,1024]{1,0:T(8,128)(2,1)S(1)} %convert_element_type.143), channel_id=1, source_target_pairs={{0,16},{1,17},{2,18},{3,19},{4,20},{5,21},{6,22},{7,23},{8,24},{9,... | collective-permute-start | bytes 1572872 | tf_op jit(solution)/shard_map/ppermute | solution.py:269
  94.1 8.4 %collective-permute-start.23 = (bf16[256,512]{1,0:T(8,128)(2,1)S(1)}, bf16[256,512]{1,0:T(8,128)(2,1)S(1)}, u32[]{:S(2)}, u32[]{:S(2)}) collective-permute-start(bf16[256,512]{1,0:T(8,128)(2,1)S(1)} %convolution_convert_fusion.3), channel_id=1, source_target_pairs={{0,4},{4,8},{8,12},{12,14},{14,10},{10,6},{6,2},{2,0},{1,5},{5,9},... | collective-permute-start | bytes 786440 | tf_op jit(solution)/shard_map/ppermute | solution.py:32
  95.5 9.2 %collective-permute-start.28 = (bf16[256,512]{1,0:T(8,128)(2,1)S(1)}, bf16[256,512]{1,0:T(8,128)(2,1)S(1)}, u32[]{:S(2)}, u32[]{:S(2)}) collective-permute-start(bf16[256,512]{1,0:T(8,128)(2,1)S(1)} %convolution_convert_fusion.2), channel_id=1, source_target_pairs={{0,2},{4,0},{8,4},{12,8},{14,12},{10,14},{6,10},{2,6},{1,3},{5,1},... | collective-permute-start | bytes 786440 | tf_op jit(solution)/shard_map/ppermute | solution.py:32
  99.0 11.4 %collective-permute-start.34 = (bf16[256,512]{1,0:T(8,128)(2,1)S(1)}, bf16[256,512]{1,0:T(8,128)(2,1)S(1)}, u32[]{:S(2)}, u32[]{:S(2)}) collective-permute-start(bf16[256,512]{1,0:T(8,128)(2,1)S(1)} %convolution_convert_fusion), channel_id=1, source_target_pairs={{0,2},{4,0},{8,4},{12,8},{14,12},{10,14},{6,10},{2,6},{1,3},{5,1},... | collective-permute-start | bytes 786440 | tf_op jit(solution)/shard_map/ppermute | solution.py:32
  101.4 12.0 %collective-permute-start.31 = (bf16[256,512]{1,0:T(8,128)(2,1)S(1)}, bf16[256,512]{1,0:T(8,128)(2,1)S(1)}, u32[]{:S(2)}, u32[]{:S(2)}) collective-permute-start(bf16[256,512]{1,0:T(8,128)(2,1)S(1)} %convolution_convert_fusion.1), channel_id=1, source_target_pairs={{0,4},{4,8},{8,12},{12,14},{14,10},{10,6},{6,2},{2,0},{1,5},{5,9},... | collective-permute-start | bytes 786440 | tf_op jit(solution)/shard_map/ppermute | solution.py:32
  106.2 23.9 %collective-permute-start.29 = (bf16[256,512]{1,0:T(8,128)(2,1)S(1)}, bf16[256,512]{1,0:T(8,128)(2,1)S(1)}, u32[]{:S(2)}, u32[]{:S(2)}) collective-permute-start(bf16[256,512]{1,0:T(8,128)(2,1)S(1)} %fusion.5), channel_id=1, source_target_pairs={{0,2},{4,0},{8,4},{12,8},{14,12},{10,14},{6,10},{2,6},{1,3},{5,1},... | collective-permute-start | bytes 786440 | tf_op jit(solution)/shard_map/ppermute | solution.py:32
  110.8 9.7 %collective-permute-start.35 = (bf16[256,512]{1,0:T(8,128)(2,1)S(1)}, bf16[256,512]{1,0:T(8,128)(2,1)S(1)}, u32[]{:S(2)}, u32[]{:S(2)}) collective-permute-start(bf16[256,512]{1,0:T(8,128)(2,1)S(1)} %fusion.10), channel_id=1, source_target_pairs={{0,2},{4,0},{8,4},{12,8},{14,12},{10,14},{6,10},{2,6},{1,3},{5,1},... | collective-permute-start | bytes 786440 | tf_op jit(solution)/shard_map/ppermute | solution.py:32
  113.3 9.4 %collective-permute-start.25 = (bf16[256,512]{1,0:T(8,128)(2,1)S(1)}, bf16[256,512]{1,0:T(8,128)(2,1)S(1)}, u32[]{:S(2)}, u32[]{:S(2)}) collective-permute-start(bf16[256,512]{1,0:T(8,128)(2,1)S(1)} %fusion.4), channel_id=1, source_target_pairs={{0,4},{4,8},{8,12},{12,14},{14,10},{10,6},{6,2},{2,0},{1,5},{5,9},... | collective-permute-start | bytes 786440 | tf_op jit(solution)/shard_map/ppermute | solution.py:32
  113.9 10.4 %collective-permute-start.32 = (bf16[256,512]{1,0:T(8,128)(2,1)S(1)}, bf16[256,512]{1,0:T(8,128)(2,1)S(1)}, u32[]{:S(2)}, u32[]{:S(2)}) collective-permute-start(bf16[256,512]{1,0:T(8,128)(2,1)S(1)} %fusion.7), channel_id=1, source_target_pairs={{0,4},{4,8},{8,12},{12,14},{14,10},{10,6},{6,2},{2,0},{1,5},{5,9},... | collective-permute-start | bytes 786440 | tf_op jit(solution)/shard_map/ppermute | solution.py:32
  121.0 7.6 %collective-permute-start.36 = (bf16[256,512]{1,0:T(8,128)(2,1)S(1)}, bf16[256,512]{1,0:T(8,128)(2,1)S(1)}, u32[]{:S(2)}, u32[]{:S(2)}) collective-permute-start(bf16[256,512]{1,0:T(8,128)(2,1)S(1)} %fusion.9), channel_id=1, source_target_pairs={{0,2},{4,0},{8,4},{12,8},{14,12},{10,14},{6,10},{2,6},{1,3},{5,1},... | collective-permute-start | bytes 786440 | tf_op jit(solution)/shard_map/ppermute | solution.py:32
  123.2 9.4 %collective-permute-start.26 = (bf16[256,512]{1,0:T(8,128)(2,1)S(1)}, bf16[256,512]{1,0:T(8,128)(2,1)S(1)}, u32[]{:S(2)}, u32[]{:S(2)}) collective-permute-start(bf16[256,512]{1,0:T(8,128)(2,1)S(1)} %fusion.3), channel_id=1, source_target_pairs={{0,4},{4,8},{8,12},{12,14},{14,10},{10,6},{6,2},{2,0},{1,5},{5,9},... | collective-permute-start | bytes 786440 | tf_op jit(solution)/shard_map/ppermute | solution.py:32
  124.6 12.4 %collective-permute-start.33 = (bf16[256,512]{1,0:T(8,128)(2,1)S(1)}, bf16[256,512]{1,0:T(8,128)(2,1)S(1)}, u32[]{:S(2)}, u32[]{:S(2)}) collective-permute-start(bf16[256,512]{1,0:T(8,128)(2,1)S(1)} %fusion.6), channel_id=1, source_target_pairs={{0,4},{4,8},{8,12},{12,14},{14,10},{10,6},{6,2},{2,0},{1,5},{5,9},... | collective-permute-start | bytes 786440 | tf_op jit(solution)/shard_map/ppermute | solution.py:32
  129.0 9.3 %collective-permute-start.37 = (bf16[256,512]{1,0:T(8,128)(2,1)S(1)}, bf16[256,512]{1,0:T(8,128)(2,1)S(1)}, u32[]{:S(2)}, u32[]{:S(2)}) collective-permute-start(bf16[256,512]{1,0:T(8,128)(2,1)S(1)} %fusion.8), channel_id=1, source_target_pairs={{0,2},{4,0},{8,4},{12,8},{14,12},{10,14},{6,10},{2,6},{1,3},{5,1},... | collective-permute-start | bytes 786440 | tf_op jit(solution)/shard_map/ppermute | solution.py:32
  131.2 10.3 %collective-permute-start.30 = (bf16[256,512]{1,0:T(8,128)(2,1)}, bf16[256,512]{1,0:T(8,128)(2,1)}, u32[]{:S(2)}, u32[]{:S(2)}) collective-permute-start(bf16[256,512]{1,0:T(8,128)(2,1)} %convolution_add_fusion.7), channel_id=1, source_target_pairs={{0,2},{4,0},{8,4},{12,8},{14,12},{10,14},{6,10},{2,6},{1,3},{5,1},... | collective-permute-start | bytes 786440 | tf_op jit(solution)/shard_map/ppermute | solution.py:32
  133.6 7.9 %collective-permute-start.27 = (bf16[256,512]{1,0:T(8,128)(2,1)}, bf16[256,512]{1,0:T(8,128)(2,1)}, u32[]{:S(2)}, u32[]{:S(2)}) collective-permute-start(bf16[256,512]{1,0:T(8,128)(2,1)} %convolution_add_fusion.10), channel_id=1, source_target_pairs={{0,4},{4,8},{8,12},{12,14},{14,10},{10,6},{6,2},{2,0},{1,5},{5,9},... | collective-permute-start | bytes 786440 | tf_op jit(solution)/shard_map/ppermute | solution.py:32
  (18 other events, 259.1 us)

commit v7 on v6

v7 whole, which is shorter than its diff:
```python
import functools

import jax
import jax.numpy as jnp
from jax import lax
from jax.experimental import pallas as pl
from jax.experimental.pallas import tpu as pltpu
from jax.sharding import Mesh, PartitionSpec as P

sharpness = 20.0
cores = 2
longest_ring = 16
vmem_limit = 20 << 20


def ring_order(chips):
    return list(range(0, chips, 2)) + list(range(1, chips, 2))[::-1]


def ring_place(chip, chips):
    return jnp.where(chip % 2 == 0, chip // 2, chips - 1 - chip // 2)


def ring_chip(place, chips):
    place = lax.rem(place + 2 * chips, chips)
    return jnp.where(place < chips // 2, 2 * place, 2 * (chips - 1 - place) + 1)


def along_ring(block, by):
    order = ring_order(lax.axis_size("chip"))
    pairs = [(chip, order[(i + by) % len(order)]) for i, chip in enumerate(order)]
    return lax.ppermute(block, "chip", pairs)


def after(first, block):
    return lax.optimization_barrier((first, block))[1]


def from_sibling(block):
    return lax.ppermute(block, "core", [(0, 1), (1, 0)])


def slab_blocks(stored, chips, core):
    order = ring_order(chips)
    kept = []
    for j in range(chips // cores):
        pairs = []
        for i, chip in enumerate(order):
            for c in range(cores):
                source = order[(i + j + c * (chips // cores)) % chips]
                pairs.append(((chips + source) * cores + c, chip * cores + c))
        kept.append(lax.ppermute(stored, ("grp", "chip", "core"), pairs))
    kept = jnp.concatenate(kept)
    other = from_sibling(kept)
    return [jnp.where(core == 0, kept, other), jnp.where(core == 0, other, kept)]


def in_core_order(mine, other, core, axis=0):
    return jnp.where(
        core == 0,
        jnp.concatenate([mine, other], axis=axis),
        jnp.concatenate([other, mine], axis=axis),
    )


def normalize_kernel(chunk, split, *refs):
    states_refs, gain_ref, out_ref = refs[:split], refs[split], refs[-1]

    def run(states_ref):
        @pl.loop(0, states_ref.shape[1] // chunk)
        def _(i):
            at = pl.ds(pl.multiple_of(i * chunk, chunk), chunk)
            wide = states_ref[0, at, :].astype(jnp.float32)
            mean_square = jnp.mean(wide * wide, axis=-1, keepdims=True)
            wide = wide * lax.rsqrt(mean_square + 1e-05) * gain_ref[...]
            out_ref[at, :] = wide.astype(jnp.bfloat16)

    if split == 1:
        run(states_refs[0])
        return
    for part, states_ref in enumerate(states_refs):
        pl.when(pl.program_id(0) == part)(functools.partial(run, states_ref))


def normalize(parts, gain, place, filled=None):
    length, width = parts[0].shape[1:]
    split = len(parts)
    seqs = parts[0].shape[0] if split == 1 else split
    tokens = seqs * length
    block = (1, length, width)
    if split == 1:
        in_specs = [pl.BlockSpec(block, lambda i: (i, 0, 0))]
    else:
        in_specs = [pl.BlockSpec(block, lambda i: (0, 0, 0))] * split
    in_specs.append(pl.BlockSpec((1, width), lambda i: (0, 0)))
    operands = [*parts, gain[None]]
    if filled is not None:
        in_specs.append(pl.BlockSpec(memory_space=pl.ANY))
        operands.append(filled)
    return pl.pallas_call(
        functools.partial(normalize_kernel, 16, split),
        grid=(seqs,),
        in_specs=in_specs,
        out_specs=pl.BlockSpec((length, width), lambda i: (place * seqs + i, 0)),
        out_shape=jax.ShapeDtypeStruct((cores * tokens, width), jnp.bfloat16),
        input_output_aliases={} if filled is None else {len(operands) - 1: 0},
        compiler_params=pltpu.CompilerParams(vmem_limit_bytes=vmem_limit),
        cost_estimate=pl.CostEstimate(
            flops=6 * tokens * width, bytes_accessed=4 * tokens * width, transcendentals=tokens
        ),
    )(*operands)


def shards(token_states, token_ids, master, gain, cand_ids, slab_owner):
    trainer = lax.axis_index("grp") == 0
    chips = lax.axis_size("chip")
    chip = lax.axis_index("chip")
    core = lax.axis_index("core")
    place = ring_place(chip, chips)
    states = token_states[0]
    seq_dev, length, width = states.shape
    rows, embedding = master.shape[1:]
    half = embedding // cores
    seqs = cores * seq_dev

    weights = master[0]
    own = lax.dynamic_slice(weights, (0, core * half), (rows, half)).astype(jnp.bfloat16)
    given = lax.dynamic_slice(weights, (0, (1 - core) * half), (rows, half))
    given = given.astype(jnp.bfloat16)
    sibling = from_sibling(given)

    normed = normalize([states], gain, 0)
    other_states = [from_sibling(states[i : i + 1]) for i in range(seq_dev)]
    first_sent = along_ring(own, 1)
    ids, cand_ids = token_ids[0], after(first_sent, cand_ids)
    ids = jnp.concatenate([ids, cand_ids], axis=1)
    ids = jnp.concatenate([ids, from_sibling(ids)])
    lengths = jnp.sum((ids[:, :length] != 0).astype(jnp.int32), axis=1)
    counts = lengths.astype(jnp.float32)
    cands = ids[:, length:]

    def columns(offset, part):
        first = (ring_chip(place + offset, chips) * cores + part) * rows
        return lax.dynamic_slice(normed, (0, first), (seqs * length, rows))

    parts = (core, 1 - core)
    if chips <= longest_ring:
        moving = {(i, by): block for by in (1, -1) for i, block in enumerate((own, sibling))}
        total, first = None, None
        waiting = [(0, parts[0], own), (0, parts[1], sibling)]
        for step in range(1, chips // 2 + 1):
            last = step == chips // 2
            sent = [(0, 1), (0, -1), (1, 1), (1, -1)]
            for i, by in [(0, 1), (1, -1)] if last else sent:
                if (step, i, by) == (1, 0, 1):
                    moving[i, by] = first_sent
                else:
                    if last and step > 2:
                        moving[i, by] = after(normed if i == 0 else first, moving[i, by])
                    moving[i, by] = along_ring(moving[i, by], by)
                waiting.append((-by * step, parts[i], moving[i, by]))
            if step == min(2, chips // 2):
                for key in sent:
                    other_states[0] = after(moving[key], other_states[0])
                normed = normalize(other_states, gain, 1, normed)
            if step < min(2, chips // 2):
                continue
            for offset, part, block in waiting:
                term = jnp.dot(columns(offset, part), block, preferred_element_type=jnp.float32)
                total = term if total is None else total + term
                if first is None and abs(offset) == 1 and part is parts[1]:
                    first = total
            waiting = []
        active = jnp.tanh(total).reshape(seqs, length, half)
    else:
        normed = normalize(other_states, gain, 1, normed)
        both = in_core_order(own, sibling, core)
        gathered = lax.all_gather(both, "chip", axis=0, tiled=True)
        hidden = jnp.dot(normed, gathered, preferred_element_type=jnp.float32)
        active = jnp.tanh(hidden).reshape(seqs, length, half)

    there = jnp.arange(length)[None, :, None] < lengths[:, None, None]
    pooled = jnp.sum(jnp.where(there, active, 0.0), axis=1) / counts[:, None]
    pooled_other = from_sibling(pooled)
    pooled_other = jnp.concatenate([pooled_other[seq_dev:], pooled_other[:seq_dev]])
    whole = in_core_order(pooled, pooled_other, core, axis=1)
    pooled_square = jnp.mean(whole * whole, axis=-1, keepdims=True)
    scale = lax.rsqrt(pooled_square + 1e-06)
    unit = whole * scale
    stored = unit.astype(jnp.bfloat16)
    stored = in_core_order(stored[:seq_dev], stored[seq_dev:], core)

    cut = {}
    if chips <= longest_ring:
        steps = [(chips // 2, 0, 1), (chips // 2, 1, -1), (chips // 2 - 1, 1, 1)]
        steps += [(chips // 2 - 1, 0, -1)]
        cut = {(by * step, i): columns(by * step, parts[i]) for step, i, by in steps}
        stored, *cuts = lax.optimization_barrier([stored, *cut.values()])
        cut = dict(zip(cut, cuts))
    slab = jnp.concatenate(slab_blocks(stored, chips, core))
    slab_rows = slab.shape[0]
    earlier = jnp.arange(slab_rows)[:, None] < jnp.arange(slab_rows)[None, :]
    same = slab_owner[:, None] == slab_owner[None, :]
    ranks = jnp.sum((earlier & same).astype(jnp.int32), axis=0)
    owner_place = ring_place(slab_owner // cores, chips)
    seen = lax.rem(owner_place - place + chips, chips)
    slots = seen * seqs + lax.rem(slab_owner, cores) * seq_dev + ranks
    positive, candidate = [
        jnp.sum(
            (slots[picked][:, :, None] == jnp.arange(slab_rows)).astype(jnp.float32), axis=1
        )
        for picked in (cands[:, :1], cands)
    ]

    slab_wide = slab.astype(jnp.float32)
    logits = (
        sharpness / embedding * jnp.dot(unit, slab_wide.T, precision=lax.Precision.HIGHEST)
    )
    exponent = jnp.where(candidate > 0, jnp.exp(logits), 0.0)
    probs = exponent / jnp.sum(exponent, axis=-1, keepdims=True)
    logit_grad = probs - positive
    unit_grad = (
        sharpness / embedding * jnp.dot(logit_grad, slab_wide, precision=lax.Precision.HIGHEST)
    )
    inner = jnp.sum(whole * unit_grad, axis=-1, keepdims=True)
    pooled_grad = scale * unit_grad - whole * (scale * scale * scale) * inner / embedding
    pooled_grad = lax.dynamic_slice(pooled_grad, (0, core * half), (seqs, half))
    slope = jnp.where(there, 1.0 - active * active, 0.0)
    delta = (pooled_grad / counts[:, None])[:, None, :] * slope
    delta = delta.astype(jnp.bfloat16).reshape(seqs * length, half)
    delta, weights = lax.optimization_barrier((delta, weights))
    copied = lax.ppermute(weights.astype(jnp.bfloat16), "grp", [(0, 1)])

    def term(offset, i, delta):
        return lax.dot_general(
            cut[offset, i] if (offset, i) in cut else columns(offset, parts[i]),
            delta,
            (((0,), (0,)), ((), ())),
            preferred_element_type=jnp.float32,
        )

    if chips <= longest_ring:
        arrived = {}
        late = delta
        for step in range(chips // 2, 0, -1):
            for i, by in ((0, 1), (1, -1), (1, 1), (0, -1)):
                if step == chips // 2 and (i, by) not in ((0, 1), (1, -1)):
                    continue
                total = term(by * step, i, delta)
                if (i, by) in arrived:
                    total = total + arrived[i, by].astype(jnp.float32)
                if step == 1 and i == 0:
                    total = after(copied, total)
                arrived[i, by] = along_ring(total.astype(jnp.bfloat16), by)
            if step == chips // 2:
                late = after(arrived[0, 1], delta)
        mine, other = [
            term(0, i, late)
            + arrived[i, 1].astype(jnp.float32)
            + arrived[i, -1].astype(jnp.float32)
            for i in range(2)
        ]
    else:
        grad = lax.dot_general(
            normed, delta, (((0,), (0,)), ((), ())), preferred_element_type=jnp.float32
        )
        reduced = lax.psum_scatter(grad, "chip", scatter_dimension=0, tiled=True)
        mine, other = [lax.dynamic_slice(reduced, (i * rows, 0), (rows, half)) for i in parts]
    other = from_sibling(other)
    shard = in_core_order(mine, other, core, axis=1)
    row_square = jnp.mean(shard * shard, axis=1, keepdims=True)
    normalized = shard * lax.rsqrt(row_square + 1e-06)
    result = jnp.where(trainer, normalized, copied.astype(jnp.float32))
    return result[None]


def solution(mesh):
    groups, devices_fsdp = mesh.devices.shape
    finer = Mesh(
        mesh.devices.reshape(groups, devices_fsdp // cores, cores), ("grp", "chip", "core")
    )
    fsdp = ("chip", "core")
    placed = (
        P("grp", fsdp, None, None),
        P("grp", fsdp, None),
        P("grp", fsdp, None),
        P(),
        P(fsdp, None),
        P(),
    )
    return jax.shard_map(
        shards, mesh=finer, in_specs=placed, out_specs=P("grp", fsdp, None), check_vma=False
    )
```

time: 147 us -> 144 us (0.980)
  Pallas kernels: 35.3 us -> 8.76 us
  waiting for transfers between devices: 38.8 us -> 53.3 us
  local copies, waits for them, and re-layouts: 3.58 us -> 13.9 us
  matrix products: 14.7 us -> 20.7 us
  other arithmetic: 10.3 us -> 6.03 us
  starting transfers between devices: 42.5 us -> 40 us
    pallas_call x4 -> x2, Pallas kernels: 35.3 us -> 8.76 us  [normalize(): pl.pallas_call(functools.partial(normalize_kernel, 16, split), grid=(seqs...]
    ppermute x28, waiting for transfers between devices: 28.6 us -> 45.8 us  [along_ring(): return lax.ppermute(block, 'chip', pairs)]
    dot_general x16 -> x32, matrix products: 14 us -> 20 us  [the longest x16 11 us: shards(): jnp.dot(columns(offset, part), block, preferred_element_type=jnp.float32)]
    unnamed x23 -> x35, local copies, waits for them, and re-layouts: 0.73 us -> 5.52 us
    slice x0 -> x1, local copies, waits for them, and re-layouts: none -> 3.77 us  [shards(): other_states = [from_sibling(states[i:i + 1]) for i in range(seq_dev)]]
    ppermute x28, starting transfers between devices: 34.6 us -> 31.1 us  [along_ring(): return lax.ppermute(block, 'chip', pairs)]
    reduce_sum x0 -> x1, other arithmetic: none -> 1.76 us  [shards(): pooled = jnp.sum(jnp.where(there, active, 0.0), axis=1) / counts[:, None]]
    ppermute x6 -> x8, waiting for transfers between devices: 3.51 us -> 1.95 us  [from_sibling(): return lax.ppermute(block, 'core', [(0, 1), (1, 0)])]
  transfers between devices with their start and end apart: 39 -> 41, of which waited for: 20 -> 24; matrix products, arithmetic and copies ran while one was open for 15% -> 17% of each run, Pallas kernels for 19% -> 6%
where the time goes in v7:
time: 144 us; the launch traced here: 143 us
  waiting for transfers between devices  53.3 us (37%)
  starting transfers between devices  40 us (28%)
  matrix products  20.7 us (14%)
  local copies, waits for them, and re-layouts  13.9 us (10%)
  Pallas kernels  8.76 us (6%)
  other arithmetic  6.03 us (4%)
    ppermute x28, waiting for transfers between devices, along_ring(): return lax.ppermute(block, 'chip', pairs)  45.8 us
    ppermute x28, starting transfers between devices, along_ring(): return lax.ppermute(block, 'chip', pairs)  31.1 us
    dot_general x16, matrix products, shards(): jnp.dot(columns(offset, part), block, preferred_element_type=jnp.float32)  11 us
    dot_general x16, matrix products, term(): lax.dot_general(cut[offset, i] if (offset, i) in cut else columns(offset,...  9.01 us
    pallas_call x2, Pallas kernels, normalize(): pl.pallas_call(functools.partial(normalize_kernel, 16, split), grid=(seqs...  8.76 us
    ppermute x4, waiting for transfers between devices, slab_blocks(): kept.append(lax.ppermute(stored, ('grp', 'chip', 'core'), pairs))  5.54 us
    unnamed x35, local copies, waits for them, and re-layouts  5.52 us
    ppermute x4, starting transfers between devices, slab_blocks(): kept.append(lax.ppermute(stored, ('grp', 'chip', 'core'), pairs))  5.16 us
  transfers between devices with their start and end apart: 41, of which 24 were waited for; matrix products, arithmetic and copies ran while one was open for 17% of the time, Pallas kernels for 6%

profile of v7, /device:TPU:0, one launch (start us, length us, event | category | flops | bytes accessed | tf_op | source)
XLA Modules:
  0.0 143.4 jit_solution(3964310063521709263)
XLA Ops:
  0.0 2.0 %fusion.52 = (bf16[256,512]{1,0:T(8,128)(2,1)}, bf16[256,512]{1,0:T(8,128)(2,1)S(1)}) fusion(f32[1,256,1024]{2,1,0:T(8,128)} %param.8, s32[]{:T(128)S(6)} %select_n.218, s32[]{:T(128)S(6)} %select_n.219), kind=kLoop, calls=%fused_computation.83 | loop fusion | bytes 1048584 | tf_op jit(solution)/shard_map/convert_element_type | solution.py:129
  2.4 2.6 %collective-permute-start.7 = (bf16[256,512]{1,0:T(8,128)(2,1)S(1)}, bf16[256,512]{1,0:T(8,128)(2,1)}, u32[]{:S(2)}, u32[]{:S(2)}) collective-permute-start(bf16[256,512]{1,0:T(8,128)(2,1)S(1)} %get-tuple-element.51), channel_id=1, source_target_pairs={{0,4},{4,8},{8,12},{12,14},{14,10},{10,6},{6,2},{2,0},{1,5},{5,9},... | collective-permute-start | bytes 786440 | tf_op jit(solution)/shard_map/ppermute | solution.py:32
  5.1 3.8 %slice_bitcast_fusion = (bf16[1,128,4096]{2,1,0:T(8,128)(2,1)}, bf16[1,128,4096]{2,1,0:T(8,128)(2,1)}, bf16[1,128,4096]{2,1,0:T(8,128)(2,1)}) fusion(bf16[1,3,128,4096]{3,2,1,0:T(8,128)(2,1)} %param.6), kind=kLoop, calls=%fused_computation.39 | loop fusion | bytes 6291456 | tf_op jit(solution)/shard_map/slice | solution.py:133
  9.5 2.6 %collective-permute-done.7 = bf16[256,512]{1,0:T(8,128)(2,1)} collective-permute-done((bf16[256,512]{1,0:T(8,128)(2,1)S(1)}, bf16[256,512]{1,0:T(8,128)(2,1)}, u32[]{:S(2)}, u32[]{:S(2)}) %collective-permute-start.7) | collective-permute-done | bytes 262176 | tf_op jit(solution)/shard_map/ppermute | solution.py:32
  12.2 3.6 %shard_map.64.refs_4_ = bf16[768,4096]{1,0:T(8,128)(2,1)S(1)} custom-call(bf16[3,128,4096]{2,1,0:T(8,128)(2,1)S(1)} %bitcast.65, f32[1,4096]{1,0:T(1,128)S(1)} %bitcast.66), custom_call_target="tpu_custom_call" | custom-call | flops 9437184 | bytes 6291456 | tf_op jit(solution)/shard_map/pallas_call | solution.py:100
  15.9 2.7 %copy-done = bf16[768,4096]{1,0:T(8,128)(2,1)} copy-done((bf16[768,4096]{1,0:T(8,128)(2,1)}, bf16[768,4096]{1,0:T(8,128)(2,1)S(1)}, u32[]{:S(2)}) %copy-start) | copy-done | bytes 6291480
  18.9 1.7 %collective-permute-start.1 = (bf16[256,512]{1,0:T(8,128)(2,1)}, bf16[256,512]{1,0:T(8,128)(2,1)S(1)}, u32[]{:S(2)}, u32[]{:S(2)}) collective-permute-start(bf16[256,512]{1,0:T(8,128)(2,1)} %collective-permute-done), channel_id=1, source_target_pairs={{0,2},{4,0},{8,4},{12,8},{14,12},{10,14},{6,10},{2,6},{1,3},{5,1},... | collective-permute-start | bytes 786440 | tf_op jit(solution)/shard_map/ppermute | solution.py:32
  21.1 6.4 %collective-permute-done.1 = bf16[256,512]{1,0:T(8,128)(2,1)S(1)} collective-permute-done((bf16[256,512]{1,0:T(8,128)(2,1)}, bf16[256,512]{1,0:T(8,128)(2,1)S(1)}, u32[]{:S(2)}, u32[]{:S(2)}) %collective-permute-start.1) | collective-permute-done | bytes 262176 | tf_op jit(solution)/shard_map/ppermute | solution.py:32
  27.5 1.7 %collective-permute-start.8 = (bf16[256,512]{1,0:T(8,128)(2,1)}, bf16[256,512]{1,0:T(8,128)(2,1)S(1)}, u32[]{:S(2)}, u32[]{:S(2)}) collective-permute-start(bf16[256,512]{1,0:T(8,128)(2,1)} %collective-permute-done.7), channel_id=1, source_target_pairs={{0,4},{4,8},{8,12},{12,14},{14,10},{10,6},{6,2},{2,0},{1,5},{5,9},... | collective-permute-start | bytes 786440 | tf_op jit(solution)/shard_map/ppermute | solution.py:32
  30.7 4.6 %collective-permute-done.8 = bf16[256,512]{1,0:T(8,128)(2,1)S(1)} collective-permute-done((bf16[256,512]{1,0:T(8,128)(2,1)}, bf16[256,512]{1,0:T(8,128)(2,1)S(1)}, u32[]{:S(2)}, u32[]{:S(2)}) %collective-permute-start.8) | collective-permute-done | bytes 262176 | tf_op jit(solution)/shard_map/ppermute | solution.py:32
  35.3 1.6 %collective-permute-start.2 = (bf16[256,512]{1,0:T(8,128)(2,1)S(1)}, bf16[256,512]{1,0:T(8,128)(2,1)S(1)}, u32[]{:S(2)}, u32[]{:S(2)}) collective-permute-start(bf16[256,512]{1,0:T(8,128)(2,1)S(1)} %collective-permute-done.1), channel_id=1, source_target_pairs={{0,2},{4,0},{8,4},{12,8},{14,12},{10,14},{6,10},{2,6},{1,3},{5,1},... | collective-permute-start | bytes 786440 | tf_op jit(solution)/shard_map/ppermute | solution.py:32
  37.5 1.7 %collective-permute-done.6 = bf16[256,512]{1,0:T(8,128)(2,1)S(1)} collective-permute-done((bf16[256,512]{1,0:T(8,128)(2,1)}, bf16[256,512]{1,0:T(8,128)(2,1)S(1)}, u32[]{:S(2)}, u32[]{:S(2)}) %collective-permute-start.6) | collective-permute-done | bytes 262176 | tf_op jit(solution)/shard_map/ppermute | solution.py:32
  40.8 2.6 %collective-permute-done.2 = bf16[256,512]{1,0:T(8,128)(2,1)S(1)} collective-permute-done((bf16[256,512]{1,0:T(8,128)(2,1)S(1)}, bf16[256,512]{1,0:T(8,128)(2,1)S(1)}, u32[]{:S(2)}, u32[]{:S(2)}) %collective-permute-start.2) | collective-permute-done | bytes 262176 | tf_op jit(solution)/shard_map/ppermute | solution.py:32
  43.7 2.4 %collective-permute-done.4 = bf16[256,512]{1,0:T(8,128)(2,1)S(1)} collective-permute-done((bf16[256,512]{1,0:T(8,128)(2,1)S(1)}, bf16[256,512]{1,0:T(8,128)(2,1)S(1)}, u32[]{:S(2)}, u32[]{:S(2)}) %collective-permute-start.4) | collective-permute-done | bytes 262176 | tf_op jit(solution)/shard_map/ppermute | solution.py:32
  46.1 1.6 %collective-permute-start.16 = (bf16[256,512]{1,0:T(8,128)(2,1)S(1)}, bf16[256,512]{1,0:T(8,128)(2,1)S(1)}, u32[]{:S(2)}, u32[]{:S(2)}) collective-permute-start(bf16[256,512]{1,0:T(8,128)(2,1)S(1)} %collective-permute-done.2), channel_id=1, source_target_pairs={{0,2},{4,0},{8,4},{12,8},{14,12},{10,14},{6,10},{2,6},{1,3},{5,1},... | collective-permute-start | bytes 786440 | tf_op jit(solution)/shard_map/ppermute | solution.py:32
  48.2 2.8 %copy-done.1 = bf16[768,4096]{1,0:T(8,128)(2,1)S(1)} copy-done((bf16[768,4096]{1,0:T(8,128)(2,1)S(1)}, bf16[768,4096]{1,0:T(8,128)(2,1)}, u32[]{:S(2)}) %copy-start.1) | copy-done | bytes 6291480
  51.0 5.2 %shard_map.65 = bf16[768,4096]{1,0:T(8,128)(2,1)S(1)} custom-call(bf16[1,128,4096]{2,1,0:T(8,128)(2,1)} %collective-permute-done.9.refs_0_, bf16[1,128,4096]{2,1,0:T(8,128)(2,1)} %collective-permute-done.10.refs_1_, bf16[1,128,4096]{2,1,0:T(8,128)(2,1)S(1)} %collective-permute-done.11.refs_2_, ...), custom_call_target="tpu_custom_call", output_to_operand_aliasing={{}: (4, {})} | custom-call | flops 9437184 | bytes 6291456 | tf_op jit(solution)/shard_map/pallas_call | solution.py:100
  61.4 1.6 %collective-permute-start.18 = (bf16[256,512]{1,0:T(8,128)(2,1)S(1)}, bf16[256,512]{1,0:T(8,128)(2,1)S(1)}, u32[]{:S(2)}, u32[]{:S(2)}) collective-permute-start(bf16[256,512]{1,0:T(8,128)(2,1)S(1)} %collective-permute-done.16), channel_id=1, source_target_pairs={{0,2},{4,0},{8,4},{12,8},{14,12},{10,14},{6,10},{2,6},{1,3},{5,1},... | collective-permute-start | bytes 786440 | tf_op jit(solution)/shard_map/ppermute | solution.py:32
  69.8 2.1 %add_tanh_fusion = f32[768,512]{1,0:T(8,128)} fusion(f32[768,512]{1,0:T(8,128)S(1)} %fusion.13, f32[768,512]{1,0:T(8,128)S(1)} %fusion.15, f32[768,512]{1,0:T(8,128)S(1)} %fusion.18, f32[768,512]{1,0:T(8,128)S(1)} %fusion.21, f32[768,512]{1,0:T(8,128)S(1)} %fusion.104, f32[768,512]{1,0:T(8,128)S(1)} %fusion.24, f32[768,512]{1,0:T(8,128)S(1)} %fusion.27, ...), kind=kOutput, calls=%fused_computation.5 | convolution fusion | flops 205651968 | bytes 19529728 | tf_op jit(solution)/shard_map/dot_general | solution.py:169
  71.9 1.8 %select_reduce_fusion = f32[6,512]{1,0:T(8,128)S(1)} fusion(f32[6,128,512]{2,1,0:T(8,128)} %bitcast.7, pred[6,128]{1,0:T(8,128)(4,1)S(1)} %get-tuple-element.59), kind=kLoop, calls=%fused_computation.4 | loop fusion | flops 783360 | bytes 1585920 | tf_op jit(solution)/shard_map/reduce_sum | solution.py:183
  81.1 2.6 %collective-permute-done.23 = bf16[6,1024]{1,0:T(8,128)(2,1)S(1)} collective-permute-done((bf16[6,1024]{1,0:T(8,128)(2,1)S(1)}, bf16[6,1024]{1,0:T(8,128)(2,1)S(1)}, u32[]{:S(2)}, u32[]{:S(2)}) %collective-permute-start.23) | collective-permute-done | bytes 12320 | tf_op jit(solution)/shard_map/ppermute | solution.py:52
  89.3 1.7 %fusion = bf16[768,512]{1,0:T(8,128)(2,1)S(1)} fusion(f32[768,512]{1,0:T(8,128)} %add_tanh_fusion, f32[6,512]{1,0:T(8,128)S(1)} %fusion.58, pred[768]{0:T(1024)(128)(4,1)S(1)} %get-tuple-element.58), kind=kLoop, calls=%fused_computation.3 | loop fusion | flops 1966080 | bytes 2372352 | tf_op jit(solution)/shard_map/convert_element_type | solution.py:230
  91.2 1.6 %collective-permute-start.26 = (bf16[256,1024]{1,0:T(8,128)(2,1)S(1)}, bf16[256,1024]{1,0:T(8,128)(2,1)S(1)}, u32[]{:S(2)}, u32[]{:S(2)}) collective-permute-start(bf16[256,1024]{1,0:T(8,128)(2,1)S(1)} %convert_element_type.144), channel_id=1, source_target_pairs={{0,16},{1,17},{2,18},{3,19},{4,20},{5,21},{6,22},{7,23},{8,24},{9,... | collective-permute-start | bytes 1572872 | tf_op jit(solution)/shard_map/ppermute | solution.py:232
  98.6 3.7 %collective-permute-done.25 = bf16[256,512]{1,0:T(8,128)(2,1)S(1)} collective-permute-done((bf16[256,512]{1,0:T(8,128)(2,1)S(1)}, bf16[256,512]{1,0:T(8,128)(2,1)S(1)}, u32[]{:S(2)}, u32[]{:S(2)}) %collective-permute-start.25) | collective-permute-done | bytes 262176 | tf_op jit(solution)/shard_map/ppermute | solution.py:32
  105.3 3.7 %collective-permute-done.36 = bf16[256,512]{1,0:T(8,128)(2,1)S(1)} collective-permute-done((bf16[256,512]{1,0:T(8,128)(2,1)S(1)}, bf16[256,512]{1,0:T(8,128)(2,1)S(1)}, u32[]{:S(2)}, u32[]{:S(2)}) %collective-permute-start.36) | collective-permute-done | bytes 262176 | tf_op jit(solution)/shard_map/ppermute | solution.py:32
  109.5 1.7 %collective-permute-start.37 = (bf16[256,512]{1,0:T(8,128)(2,1)S(1)}, bf16[256,512]{1,0:T(8,128)(2,1)S(1)}, u32[]{:S(2)}, u32[]{:S(2)}) collective-permute-start(bf16[256,512]{1,0:T(8,128)(2,1)S(1)} %fusion.10), channel_id=1, source_target_pairs={{0,2},{4,0},{8,4},{12,8},{14,12},{10,14},{6,10},{2,6},{1,3},{5,1},... | collective-permute-start | bytes 786440 | tf_op jit(solution)/shard_map/ppermute | solution.py:32
  114.0 5.0 %collective-permute-done.37 = bf16[256,512]{1,0:T(8,128)(2,1)S(1)} collective-permute-done((bf16[256,512]{1,0:T(8,128)(2,1)S(1)}, bf16[256,512]{1,0:T(8,128)(2,1)S(1)}, u32[]{:S(2)}, u32[]{:S(2)}) %collective-permute-start.37) | collective-permute-done | bytes 262176 | tf_op jit(solution)/shard_map/ppermute | solution.py:32
  119.5 1.8 %collective-permute-start.38 = (bf16[256,512]{1,0:T(8,128)(2,1)S(1)}, bf16[256,512]{1,0:T(8,128)(2,1)S(1)}, u32[]{:S(2)}, u32[]{:S(2)}) collective-permute-start(bf16[256,512]{1,0:T(8,128)(2,1)S(1)} %fusion.9), channel_id=1, source_target_pairs={{0,2},{4,0},{8,4},{12,8},{14,12},{10,14},{6,10},{2,6},{1,3},{5,1},... | collective-permute-start | bytes 786440 | tf_op jit(solution)/shard_map/ppermute | solution.py:32
  124.3 2.3 %collective-permute-done.38 = bf16[256,512]{1,0:T(8,128)(2,1)S(1)} collective-permute-done((bf16[256,512]{1,0:T(8,128)(2,1)S(1)}, bf16[256,512]{1,0:T(8,128)(2,1)S(1)}, u32[]{:S(2)}, u32[]{:S(2)}) %collective-permute-start.38) | collective-permute-done | bytes 262176 | tf_op jit(solution)/shard_map/ppermute | solution.py:32
  127.1 2.1 %collective-permute-start.39 = (bf16[256,512]{1,0:T(8,128)(2,1)S(1)}, bf16[256,512]{1,0:T(8,128)(2,1)S(1)}, u32[]{:S(2)}, u32[]{:S(2)}) collective-permute-start(bf16[256,512]{1,0:T(8,128)(2,1)S(1)} %fusion.8), channel_id=1, source_target_pairs={{0,2},{4,0},{8,4},{12,8},{14,12},{10,14},{6,10},{2,6},{1,3},{5,1},... | collective-permute-start | bytes 786440 | tf_op jit(solution)/shard_map/ppermute | solution.py:32
  133.4 2.5 %collective-permute-done.35 = bf16[256,512]{1,0:T(8,128)(2,1)S(1)} collective-permute-done((bf16[256,512]{1,0:T(8,128)(2,1)S(1)}, bf16[256,512]{1,0:T(8,128)(2,1)S(1)}, u32[]{:S(2)}, u32[]{:S(2)}) %collective-permute-start.35) | collective-permute-done | bytes 262176 | tf_op jit(solution)/shard_map/ppermute | solution.py:32
  136.6 2.7 %collective-permute-done.32 = bf16[256,512]{1,0:T(8,128)(2,1)} collective-permute-done((bf16[256,512]{1,0:T(8,128)(2,1)}, bf16[256,512]{1,0:T(8,128)(2,1)}, u32[]{:S(2)}, u32[]{:S(2)}) %collective-permute-start.32) | collective-permute-done | bytes 262176 | tf_op jit(solution)/shard_map/ppermute | solution.py:32
  (158 shorter events, 56.2 us)
Async XLA Ops:
  2.0 16.6 %collective-permute-start = (bf16[256,512]{1,0:T(8,128)(2,1)}, bf16[256,512]{1,0:T(8,128)(2,1)}, u32[]{:S(2)}, u32[]{:S(2)}) collective-permute-start(bf16[256,512]{1,0:T(8,128)(2,1)} %get-tuple-element.50), channel_id=1, source_target_pairs={{0,1},{1,0},{2,3},{3,2},{4,5},{5,4},{6,7},{7,6},{8,9},{9,8},{10,11... | collective-permute-start | bytes 786440 | tf_op jit(solution)/shard_map/ppermute | solution.py:40
  2.4 9.7 %collective-permute-start.7 = (bf16[256,512]{1,0:T(8,128)(2,1)S(1)}, bf16[256,512]{1,0:T(8,128)(2,1)}, u32[]{:S(2)}, u32[]{:S(2)}) collective-permute-start(bf16[256,512]{1,0:T(8,128)(2,1)S(1)} %get-tuple-element.51), channel_id=1, source_target_pairs={{0,4},{4,8},{8,12},{12,14},{14,10},{10,6},{6,2},{2,0},{1,5},{5,9},... | collective-permute-start | bytes 786440 | tf_op jit(solution)/shard_map/ppermute | solution.py:32
  8.8 28.0 %collective-permute-start.9 = (bf16[1,128,4096]{2,1,0:T(8,128)(2,1)}, bf16[1,128,4096]{2,1,0:T(8,128)(2,1)}, u32[]{:S(2)}, u32[]{:S(2)}) collective-permute-start(bf16[1,128,4096]{2,1,0:T(8,128)(2,1)} %get-tuple-element.49), channel_id=1, source_target_pairs={{0,1},{1,0},{2,3},{3,2},{4,5},{5,4},{6,7},{7,6},{8,9},{9,8},{10,11... | collective-permute-start | bytes 3145736 | tf_op jit(solution)/shard_map/ppermute | solution.py:40
  9.1 11.7 %collective-permute-start.5 = (bf16[256,512]{1,0:T(8,128)(2,1)S(1)}, bf16[256,512]{1,0:T(8,128)(2,1)}, u32[]{:S(2)}, u32[]{:S(2)}) collective-permute-start(bf16[256,512]{1,0:T(8,128)(2,1)S(1)} %get-tuple-element.51), channel_id=1, source_target_pairs={{0,2},{4,0},{8,4},{12,8},{14,12},{10,14},{6,10},{2,6},{1,3},{5,1},... | collective-permute-start | bytes 786440 | tf_op jit(solution)/shard_map/ppermute | solution.py:32
  9.3 38.4 %collective-permute-start.10 = (bf16[1,128,4096]{2,1,0:T(8,128)(2,1)}, bf16[1,128,4096]{2,1,0:T(8,128)(2,1)}, u32[]{:S(2)}, u32[]{:S(2)}) collective-permute-start(bf16[1,128,4096]{2,1,0:T(8,128)(2,1)} %get-tuple-element.48), channel_id=1, source_target_pairs={{0,1},{1,0},{2,3},{3,2},{4,5},{5,4},{6,7},{7,6},{8,9},{9,8},{10,11... | collective-permute-start | bytes 3145736 | tf_op jit(solution)/shard_map/ppermute | solution.py:40
  18.5 29.6 %collective-permute-start.11 = (bf16[1,128,4096]{2,1,0:T(8,128)(2,1)}, bf16[1,128,4096]{2,1,0:T(8,128)(2,1)S(1)}, u32[]{:S(2)}, u32[]{:S(2)}) collective-permute-start(bf16[1,128,4096]{2,1,0:T(8,128)(2,1)} %get-tuple-element.47), channel_id=1, source_target_pairs={{0,1},{1,0},{2,3},{3,2},{4,5},{5,4},{6,7},{7,6},{8,9},{9,8},{10,11... | collective-permute-start | bytes 3145736 | tf_op jit(solution)/shard_map/ppermute | solution.py:40
  18.9 8.6 %collective-permute-start.1 = (bf16[256,512]{1,0:T(8,128)(2,1)}, bf16[256,512]{1,0:T(8,128)(2,1)S(1)}, u32[]{:S(2)}, u32[]{:S(2)}) collective-permute-start(bf16[256,512]{1,0:T(8,128)(2,1)} %collective-permute-done), channel_id=1, source_target_pairs={{0,2},{4,0},{8,4},{12,8},{14,12},{10,14},{6,10},{2,6},{1,3},{5,1},... | collective-permute-start | bytes 786440 | tf_op jit(solution)/shard_map/ppermute | solution.py:32
  20.7 9.6 %collective-permute-start.3 = (bf16[256,512]{1,0:T(8,128)(2,1)}, bf16[256,512]{1,0:T(8,128)(2,1)S(1)}, u32[]{:S(2)}, u32[]{:S(2)}) collective-permute-start(bf16[256,512]{1,0:T(8,128)(2,1)} %collective-permute-done), channel_id=1, source_target_pairs={{0,4},{4,8},{8,12},{12,14},{14,10},{10,6},{6,2},{2,0},{1,5},{5,9},... | collective-permute-start | bytes 786440 | tf_op jit(solution)/shard_map/ppermute | solution.py:32
  27.5 7.7 %collective-permute-start.8 = (bf16[256,512]{1,0:T(8,128)(2,1)}, bf16[256,512]{1,0:T(8,128)(2,1)S(1)}, u32[]{:S(2)}, u32[]{:S(2)}) collective-permute-start(bf16[256,512]{1,0:T(8,128)(2,1)} %collective-permute-done.7), channel_id=1, source_target_pairs={{0,4},{4,8},{8,12},{12,14},{14,10},{10,6},{6,2},{2,0},{1,5},{5,9},... | collective-permute-start | bytes 786440 | tf_op jit(solution)/shard_map/ppermute | solution.py:32
  30.3 8.9 %collective-permute-start.6 = (bf16[256,512]{1,0:T(8,128)(2,1)}, bf16[256,512]{1,0:T(8,128)(2,1)S(1)}, u32[]{:S(2)}, u32[]{:S(2)}) collective-permute-start(bf16[256,512]{1,0:T(8,128)(2,1)} %collective-permute-done.5), channel_id=1, source_target_pairs={{0,2},{4,0},{8,4},{12,8},{14,12},{10,14},{6,10},{2,6},{1,3},{5,1},... | collective-permute-start | bytes 786440 | tf_op jit(solution)/shard_map/ppermute | solution.py:32
  35.3 8.1 %collective-permute-start.2 = (bf16[256,512]{1,0:T(8,128)(2,1)S(1)}, bf16[256,512]{1,0:T(8,128)(2,1)S(1)}, u32[]{:S(2)}, u32[]{:S(2)}) collective-permute-start(bf16[256,512]{1,0:T(8,128)(2,1)S(1)} %collective-permute-done.1), channel_id=1, source_target_pairs={{0,2},{4,0},{8,4},{12,8},{14,12},{10,14},{6,10},{2,6},{1,3},{5,1},... | collective-permute-start | bytes 786440 | tf_op jit(solution)/shard_map/ppermute | solution.py:32
  36.9 9.2 %collective-permute-start.4 = (bf16[256,512]{1,0:T(8,128)(2,1)S(1)}, bf16[256,512]{1,0:T(8,128)(2,1)S(1)}, u32[]{:S(2)}, u32[]{:S(2)}) collective-permute-start(bf16[256,512]{1,0:T(8,128)(2,1)S(1)} %collective-permute-done.3), channel_id=1, source_target_pairs={{0,4},{4,8},{8,12},{12,14},{14,10},{10,6},{6,2},{2,0},{1,5},{5,9},... | collective-permute-start | bytes 786440 | tf_op jit(solution)/shard_map/ppermute | solution.py:32
  39.2 23.8 %collective-permute-start.13 = (bf16[256,512]{1,0:T(8,128)(2,1)S(1)}, bf16[256,512]{1,0:T(8,128)(2,1)S(1)}, u32[]{:S(2)}, u32[]{:S(2)}) collective-permute-start(bf16[256,512]{1,0:T(8,128)(2,1)S(1)} %collective-permute-done.8), channel_id=1, source_target_pairs={{0,4},{4,8},{8,12},{12,14},{14,10},{10,6},{6,2},{2,0},{1,5},{5,9},... | collective-permute-start | bytes 786440 | tf_op jit(solution)/shard_map/ppermute | solution.py:32
  43.4 23.8 %collective-permute-start.14 = (bf16[256,512]{1,0:T(8,128)(2,1)S(1)}, bf16[256,512]{1,0:T(8,128)(2,1)S(1)}, u32[]{:S(2)}, u32[]{:S(2)}) collective-permute-start(bf16[256,512]{1,0:T(8,128)(2,1)S(1)} %collective-permute-done.6), channel_id=1, source_target_pairs={{0,2},{4,0},{8,4},{12,8},{14,12},{10,14},{6,10},{2,6},{1,3},{5,1},... | collective-permute-start | bytes 786440 | tf_op jit(solution)/shard_map/ppermute | solution.py:32
  46.1 15.3 %collective-permute-start.16 = (bf16[256,512]{1,0:T(8,128)(2,1)S(1)}, bf16[256,512]{1,0:T(8,128)(2,1)S(1)}, u32[]{:S(2)}, u32[]{:S(2)}) collective-permute-start(bf16[256,512]{1,0:T(8,128)(2,1)S(1)} %collective-permute-done.2), channel_id=1, source_target_pairs={{0,2},{4,0},{8,4},{12,8},{14,12},{10,14},{6,10},{2,6},{1,3},{5,1},... | collective-permute-start | bytes 786440 | tf_op jit(solution)/shard_map/ppermute | solution.py:32
  47.7 19.1 %collective-permute-start.15 = (bf16[256,512]{1,0:T(8,128)(2,1)S(1)}, bf16[256,512]{1,0:T(8,128)(2,1)S(1)}, u32[]{:S(2)}, u32[]{:S(2)}) collective-permute-start(bf16[256,512]{1,0:T(8,128)(2,1)S(1)} %collective-permute-done.4), channel_id=1, source_target_pairs={{0,4},{4,8},{8,12},{12,14},{14,10},{10,6},{6,2},{2,0},{1,5},{5,9},... | collective-permute-start | bytes 786440 | tf_op jit(solution)/shard_map/ppermute | solution.py:32
  75.3 8.4 %collective-permute-start.23 = (bf16[6,1024]{1,0:T(8,128)(2,1)S(1)}, bf16[6,1024]{1,0:T(8,128)(2,1)S(1)}, u32[]{:S(2)}, u32[]{:S(2)}) collective-permute-start(bf16[6,1024]{1,0:T(8,128)(2,1)S(1)} %maximum_select_fusion.2), channel_id=1, source_target_pairs={{28,0},{19,1},{30,4},{17,5},{26,8},{21,9},{22,12},{25,13},{18,14},... | collective-permute-start | bytes 36872 | tf_op jit(solution)/shard_map/ppermute | solution.py:52
  76.5 8.5 %collective-permute-start.22 = (bf16[6,1024]{1,0:T(8,128)(2,1)S(1)}, bf16[6,1024]{1,0:T(8,128)(2,1)S(1)}, u32[]{:S(2)}, u32[]{:S(2)}) collective-permute-start(bf16[6,1024]{1,0:T(8,128)(2,1)S(1)} %maximum_select_fusion.2), channel_id=1, source_target_pairs={{24,0},{23,1},{28,4},{19,5},{30,8},{17,9},{26,12},{21,13},{22,14},... | collective-permute-start | bytes 36872 | tf_op jit(solution)/shard_map/ppermute | solution.py:52
  91.2 39.1 %collective-permute-start.26 = (bf16[256,1024]{1,0:T(8,128)(2,1)S(1)}, bf16[256,1024]{1,0:T(8,128)(2,1)S(1)}, u32[]{:S(2)}, u32[]{:S(2)}) collective-permute-start(bf16[256,1024]{1,0:T(8,128)(2,1)S(1)} %convert_element_type.144), channel_id=1, source_target_pairs={{0,16},{1,17},{2,18},{3,19},{4,20},{5,21},{6,22},{7,23},{8,24},{9,... | collective-permute-start | bytes 1572872 | tf_op jit(solution)/shard_map/ppermute | solution.py:232
  93.2 9.2 %collective-permute-start.25 = (bf16[256,512]{1,0:T(8,128)(2,1)S(1)}, bf16[256,512]{1,0:T(8,128)(2,1)S(1)}, u32[]{:S(2)}, u32[]{:S(2)}) collective-permute-start(bf16[256,512]{1,0:T(8,128)(2,1)S(1)} %convolution_convert_fusion.3), channel_id=1, source_target_pairs={{0,4},{4,8},{8,12},{12,14},{14,10},{10,6},{6,2},{2,0},{1,5},{5,9},... | collective-permute-start | bytes 786440 | tf_op jit(solution)/shard_map/ppermute | solution.py:32
  94.2 9.3 %collective-permute-start.30 = (bf16[256,512]{1,0:T(8,128)(2,1)S(1)}, bf16[256,512]{1,0:T(8,128)(2,1)S(1)}, u32[]{:S(2)}, u32[]{:S(2)}) collective-permute-start(bf16[256,512]{1,0:T(8,128)(2,1)S(1)} %convolution_convert_fusion.2), channel_id=1, source_target_pairs={{0,2},{4,0},{8,4},{12,8},{14,12},{10,14},{6,10},{2,6},{1,3},{5,1},... | collective-permute-start | bytes 786440 | tf_op jit(solution)/shard_map/ppermute | solution.py:32
  96.1 13.0 %collective-permute-start.36 = (bf16[256,512]{1,0:T(8,128)(2,1)S(1)}, bf16[256,512]{1,0:T(8,128)(2,1)S(1)}, u32[]{:S(2)}, u32[]{:S(2)}) collective-permute-start(bf16[256,512]{1,0:T(8,128)(2,1)S(1)} %convolution_convert_fusion), channel_id=1, source_target_pairs={{0,2},{4,0},{8,4},{12,8},{14,12},{10,14},{6,10},{2,6},{1,3},{5,1},... | collective-permute-start | bytes 786440 | tf_op jit(solution)/shard_map/ppermute | solution.py:32
  98.0 14.2 %collective-permute-start.33 = (bf16[256,512]{1,0:T(8,128)(2,1)S(1)}, bf16[256,512]{1,0:T(8,128)(2,1)S(1)}, u32[]{:S(2)}, u32[]{:S(2)}) collective-permute-start(bf16[256,512]{1,0:T(8,128)(2,1)S(1)} %convolution_convert_fusion.1), channel_id=1, source_target_pairs={{0,4},{4,8},{8,12},{12,14},{14,10},{10,6},{6,2},{2,0},{1,5},{5,9},... | collective-permute-start | bytes 786440 | tf_op jit(solution)/shard_map/ppermute | solution.py:32
  103.9 25.3 %collective-permute-start.31 = (bf16[256,512]{1,0:T(8,128)(2,1)S(1)}, bf16[256,512]{1,0:T(8,128)(2,1)S(1)}, u32[]{:S(2)}, u32[]{:S(2)}) collective-permute-start(bf16[256,512]{1,0:T(8,128)(2,1)S(1)} %fusion.5), channel_id=1, source_target_pairs={{0,2},{4,0},{8,4},{12,8},{14,12},{10,14},{6,10},{2,6},{1,3},{5,1},... | collective-permute-start | bytes 786440 | tf_op jit(solution)/shard_map/ppermute | solution.py:32
  109.5 9.6 %collective-permute-start.37 = (bf16[256,512]{1,0:T(8,128)(2,1)S(1)}, bf16[256,512]{1,0:T(8,128)(2,1)S(1)}, u32[]{:S(2)}, u32[]{:S(2)}) collective-permute-start(bf16[256,512]{1,0:T(8,128)(2,1)S(1)} %fusion.10), channel_id=1, source_target_pairs={{0,2},{4,0},{8,4},{12,8},{14,12},{10,14},{6,10},{2,6},{1,3},{5,1},... | collective-permute-start | bytes 786440 | tf_op jit(solution)/shard_map/ppermute | solution.py:32
  111.5 9.8 %collective-permute-start.27 = (bf16[256,512]{1,0:T(8,128)(2,1)S(1)}, bf16[256,512]{1,0:T(8,128)(2,1)S(1)}, u32[]{:S(2)}, u32[]{:S(2)}) collective-permute-start(bf16[256,512]{1,0:T(8,128)(2,1)S(1)} %fusion.4), channel_id=1, source_target_pairs={{0,4},{4,8},{8,12},{12,14},{14,10},{10,6},{6,2},{2,0},{1,5},{5,9},... | collective-permute-start | bytes 786440 | tf_op jit(solution)/shard_map/ppermute | solution.py:32
  112.6 11.0 %collective-permute-start.34 = (bf16[256,512]{1,0:T(8,128)(2,1)S(1)}, bf16[256,512]{1,0:T(8,128)(2,1)S(1)}, u32[]{:S(2)}, u32[]{:S(2)}) collective-permute-start(bf16[256,512]{1,0:T(8,128)(2,1)S(1)} %fusion.7), channel_id=1, source_target_pairs={{0,4},{4,8},{8,12},{12,14},{14,10},{10,6},{6,2},{2,0},{1,5},{5,9},... | collective-permute-start | bytes 786440 | tf_op jit(solution)/shard_map/ppermute | solution.py:32
  121.7 10.1 %collective-permute-start.28 = (bf16[256,512]{1,0:T(8,128)(2,1)S(1)}, bf16[256,512]{1,0:T(8,128)(2,1)S(1)}, u32[]{:S(2)}, u32[]{:S(2)}) collective-permute-start(bf16[256,512]{1,0:T(8,128)(2,1)S(1)} %fusion.3), channel_id=1, source_target_pairs={{0,4},{4,8},{8,12},{12,14},{14,10},{10,6},{6,2},{2,0},{1,5},{5,9},... | collective-permute-start | bytes 786440 | tf_op jit(solution)/shard_map/ppermute | solution.py:32
  124.0 11.9 %collective-permute-start.35 = (bf16[256,512]{1,0:T(8,128)(2,1)S(1)}, bf16[256,512]{1,0:T(8,128)(2,1)S(1)}, u32[]{:S(2)}, u32[]{:S(2)}) collective-permute-start(bf16[256,512]{1,0:T(8,128)(2,1)S(1)} %fusion.6), channel_id=1, source_target_pairs={{0,4},{4,8},{8,12},{12,14},{14,10},{10,6},{6,2},{2,0},{1,5},{5,9},... | collective-permute-start | bytes 786440 | tf_op jit(solution)/shard_map/ppermute | solution.py:32
  127.1 8.9 %collective-permute-start.39 = (bf16[256,512]{1,0:T(8,128)(2,1)S(1)}, bf16[256,512]{1,0:T(8,128)(2,1)S(1)}, u32[]{:S(2)}, u32[]{:S(2)}) collective-permute-start(bf16[256,512]{1,0:T(8,128)(2,1)S(1)} %fusion.8), channel_id=1, source_target_pairs={{0,2},{4,0},{8,4},{12,8},{14,12},{10,14},{6,10},{2,6},{1,3},{5,1},... | collective-permute-start | bytes 786440 | tf_op jit(solution)/shard_map/ppermute | solution.py:32
  130.3 9.0 %collective-permute-start.32 = (bf16[256,512]{1,0:T(8,128)(2,1)}, bf16[256,512]{1,0:T(8,128)(2,1)}, u32[]{:S(2)}, u32[]{:S(2)}) collective-permute-start(bf16[256,512]{1,0:T(8,128)(2,1)} %convolution_add_fusion.7), channel_id=1, source_target_pairs={{0,2},{4,0},{8,4},{12,8},{14,12},{10,14},{6,10},{2,6},{1,3},{5,1},... | collective-permute-start | bytes 786440 | tf_op jit(solution)/shard_map/ppermute | solution.py:32
  132.9 7.5 %collective-permute-start.29 = (bf16[256,512]{1,0:T(8,128)(2,1)}, bf16[256,512]{1,0:T(8,128)(2,1)}, u32[]{:S(2)}, u32[]{:S(2)}) collective-permute-start(bf16[256,512]{1,0:T(8,128)(2,1)} %convolution_add_fusion.10), channel_id=1, source_target_pairs={{0,4},{4,8},{8,12},{12,14},{14,10},{10,6},{6,2},{2,0},{1,5},{5,9},... | collective-permute-start | bytes 786440 | tf_op jit(solution)/shard_map/ppermute | solution.py:32
  (26 other events, 192.9 us)

commit v8 on v7

--- a/solution.py
+++ b/solution.py
@@ -63,10 +63,8 @@
     )
 
 
-def normalize_kernel(chunk, split, *refs):
-    states_refs, gain_ref, out_ref = refs[:split], refs[split], refs[-1]
-
-    def run(states_ref):
+def normalize_kernel(chunk, states_ref, gain_ref, *out_refs):
+    def run(out_ref):
         @pl.loop(0, states_ref.shape[1] // chunk)
         def _(i):
             at = pl.ds(pl.multiple_of(i * chunk, chunk), chunk)
@@ -75,40 +73,27 @@
             wide = wide * lax.rsqrt(mean_square + 1e-05) * gain_ref[...]
             out_ref[at, :] = wide.astype(jnp.bfloat16)
 
-    if split == 1:
-        run(states_refs[0])
-        return
-    for part, states_ref in enumerate(states_refs):
-        pl.when(pl.program_id(0) == part)(functools.partial(run, states_ref))
-
-
-def normalize(parts, gain, place, filled=None):
-    length, width = parts[0].shape[1:]
-    split = len(parts)
-    seqs = parts[0].shape[0] if split == 1 else split
+    for part, out_ref in enumerate(out_refs):
+        pl.when(pl.program_id(0) == part)(functools.partial(run, out_ref))
+
+
+def normalize(states, gain):
+    seqs, length, width = states.shape
     tokens = seqs * length
-    block = (1, length, width)
-    if split == 1:
-        in_specs = [pl.BlockSpec(block, lambda i: (i, 0, 0))]
-    else:
-        in_specs = [pl.BlockSpec(block, lambda i: (0, 0, 0))] * split
-    in_specs.append(pl.BlockSpec((1, width), lambda i: (0, 0)))
-    operands = [*parts, gain[None]]
-    if filled is not None:
-        in_specs.append(pl.BlockSpec(memory_space=pl.ANY))
-        operands.append(filled)
     return pl.pallas_call(
-        functools.partial(normalize_kernel, 16, split),
+        functools.partial(normalize_kernel, 16),
         grid=(seqs,),
-        in_specs=in_specs,
-        out_specs=pl.BlockSpec((length, width), lambda i: (place * seqs + i, 0)),
-        out_shape=jax.ShapeDtypeStruct((cores * tokens, width), jnp.bfloat16),
-        input_output_aliases={} if filled is None else {len(operands) - 1: 0},
+        in_specs=[
+            pl.BlockSpec((1, length, width), lambda i: (i, 0, 0)),
+            pl.BlockSpec((1, width), lambda i: (0, 0)),
+        ],
+        out_specs=[pl.BlockSpec((length, width), lambda i: (0, 0))] * seqs,
+        out_shape=[jax.ShapeDtypeStruct((length, width), jnp.bfloat16)] * seqs,
         compiler_params=pltpu.CompilerParams(vmem_limit_bytes=vmem_limit),
         cost_estimate=pl.CostEstimate(
             flops=6 * tokens * width, bytes_accessed=4 * tokens * width, transcendentals=tokens
         ),
-    )(*operands)
+    )(states, gain[None])
 
 
 def shards(token_states, token_ids, master, gain, cand_ids, slab_owner):
@@ -129,8 +114,8 @@
     given = given.astype(jnp.bfloat16)
     sibling = from_sibling(given)
 
-    normed = normalize([states], gain, 0)
-    other_states = [from_sibling(states[i : i + 1]) for i in range(seq_dev)]
+    normed = list(normalize(after(sibling, states), gain))
+    normed = jnp.concatenate(normed + [from_sibling(part) for part in normed])
     first_sent = along_ring(own, 1)
     ids, cand_ids = token_ids[0], after(first_sent, cand_ids)
     ids = jnp.concatenate([ids, cand_ids], axis=1)
@@ -143,11 +128,14 @@
         first = (ring_chip(place + offset, chips) * cores + part) * rows
         return lax.dynamic_slice(normed, (0, first), (seqs * length, rows))
 
+    def product(offset, part, block):
+        return jnp.dot(columns(offset, part), block, preferred_element_type=jnp.float32)
+
     parts = (core, 1 - core)
     if chips <= longest_ring:
         moving = {(i, by): block for by in (1, -1) for i, block in enumerate((own, sibling))}
-        total, first = None, None
-        waiting = [(0, parts[0], own), (0, parts[1], sibling)]
+        total = product(0, parts[0], own) + product(0, parts[1], sibling)
+        first = None
         for step in range(1, chips // 2 + 1):
             last = step == chips // 2
             sent = [(0, 1), (0, -1), (1, 1), (1, -1)]
@@ -155,25 +143,13 @@
                 if (step, i, by) == (1, 0, 1):
                     moving[i, by] = first_sent
                 else:
-                    if last and step > 2:
-                        moving[i, by] = after(normed if i == 0 else first, moving[i, by])
+                    if last and i == 1 and first is not None:
+                        moving[i, by] = after(first, moving[i, by])
                     moving[i, by] = along_ring(moving[i, by], by)
-                waiting.append((-by * step, parts[i], moving[i, by]))
-            if step == min(2, chips // 2):
-                for key in sent:
-                    other_states[0] = after(moving[key], other_states[0])
-                normed = normalize(other_states, gain, 1, normed)
-            if step < min(2, chips // 2):
-                continue
-            for offset, part, block in waiting:
-                term = jnp.dot(columns(offset, part), block, preferred_element_type=jnp.float32)
-                total = term if total is None else total + term
-                if first is None and abs(offset) == 1 and part is parts[1]:
-                    first = total
-            waiting = []
+                total = total + product(-by * step, parts[i], moving[i, by])
+            first = total if first is None else first
         active = jnp.tanh(total).reshape(seqs, length, half)
     else:
-        normed = normalize(other_states, gain, 1, normed)
         both = in_core_order(own, sibling, core)
         gathered = lax.all_gather(both, "chip", axis=0, tiled=True)
         hidden = jnp.dot(normed, gathered, preferred_element_type=jnp.float32)

time: 144 us -> 149 us (1.035)
  matrix products: 20.7 us -> 39.6 us
  waiting for transfers between devices: 53.3 us -> 38.6 us
  Pallas kernels: 8.76 us -> 3.61 us
  starting transfers between devices: 40 us -> 43.5 us
  local copies, waits for them, and re-layouts: 13.9 us -> 16.8 us
  other arithmetic: 6.03 us -> 4.4 us
    ppermute x28, waiting for transfers between devices: 45.8 us -> 29.6 us  [along_ring(): return lax.ppermute(block, 'chip', pairs)]
    dot_general x16, matrix products: 11 us -> 20.8 us  [product(): jnp.dot(columns(offset, part), block, preferred_element_type=jnp.float32)]
    dot_general x16, matrix products: 9.01 us -> 18.1 us  [term(): lax.dot_general(cut[offset, i] if (offset, i) in cut else columns(offset,...]
    pallas_call x2 -> x1, Pallas kernels: 8.76 us -> 3.61 us  [normalize(): pl.pallas_call(functools.partial(normalize_kernel, 16), grid=(seqs,), in_...]
    unnamed x35 -> x26, local copies, waits for them, and re-layouts: 5.52 us -> 10.6 us
    ppermute x28, starting transfers between devices: 31.1 us -> 35.3 us  [along_ring(): return lax.ppermute(block, 'chip', pairs)]
    slice x1 -> x0, local copies, waits for them, and re-layouts: 3.77 us -> none  [shards(): other_states = [from_sibling(states[i:i + 1]) for i in range(seq_dev)]]
    reduce_sum x1, other arithmetic: 1.76 us -> 0.21 us  [shards(): pooled = jnp.sum(jnp.where(there, active, 0.0), axis=1) / counts[:, None]]
  transfers between devices with their start and end apart: 41 -> 41, of which waited for: 24 -> 20; matrix products, arithmetic and copies ran while one was open for 17% -> 36% of each run, Pallas kernels for 6% -> 2%
where the time goes in v8:
time: 149 us; the launch traced here: 147 us
  starting transfers between devices  43.5 us (29%)
  matrix products  39.6 us (27%)
  waiting for transfers between devices  38.6 us (26%)
  local copies, waits for them, and re-layouts  16.8 us (11%)
  other arithmetic  4.4 us (3%)
  Pallas kernels  3.61 us (2%)
    ppermute x28, starting transfers between devices, along_ring(): return lax.ppermute(block, 'chip', pairs)  35.3 us
    ppermute x28, waiting for transfers between devices, along_ring(): return lax.ppermute(block, 'chip', pairs)  29.6 us
    dot_general x16, matrix products, product(): jnp.dot(columns(offset, part), block, preferred_element_type=jnp.float32)  20.8 us
    dot_general x16, matrix products, term(): lax.dot_general(cut[offset, i] if (offset, i) in cut else columns(offset,...  18.1 us
    unnamed x26, local copies, waits for them, and re-layouts  10.6 us
    ppermute x4, waiting for transfers between devices, slab_blocks(): kept.append(lax.ppermute(stored, ('grp', 'chip', 'core'), pairs))  6.66 us
    ppermute x4, starting transfers between devices, slab_blocks(): kept.append(lax.ppermute(stored, ('grp', 'chip', 'core'), pairs))  5.16 us
    pallas_call x1, Pallas kernels, normalize(): pl.pallas_call(functools.partial(normalize_kernel, 16), grid=(seqs,), in_...  3.61 us
  transfers between devices with their start and end apart: 41, of which 20 were waited for; matrix products, arithmetic and copies ran while one was open for 36% of the time, Pallas kernels for 2%

profile of v8, /device:TPU:0, one launch (start us, length us, event | category | flops | bytes accessed | tf_op | source)
XLA Modules:
  0.0 147.3 jit_solution(12200786770794918183)
XLA Ops:
  1.3 3.0 %collective-permute-start.6 = (bf16[256,512]{1,0:T(8,128)(2,1)S(1)}, bf16[256,512]{1,0:T(8,128)(2,1)}, u32[]{:S(2)}, u32[]{:S(2)}) collective-permute-start(bf16[256,512]{1,0:T(8,128)(2,1)S(1)} %get-tuple-element.45), channel_id=1, source_target_pairs={{0,2},{4,0},{8,4},{12,8},{14,12},{10,14},{6,10},{2,6},{1,3},{5,1},... | collective-permute-start | bytes 786440 | tf_op jit(solution)/shard_map/ppermute | solution.py:32
  6.9 1.9 %copy-done = bf16[1,3,128,4096]{3,2,1,0:T(8,128)(2,1)S(1)} copy-done((bf16[1,3,128,4096]{3,2,1,0:T(8,128)(2,1)S(1)}, bf16[1,3,128,4096]{3,2,1,0:T(8,128)(2,1)}, u32[]{:S(2)}) %copy-start) | copy-done | bytes 3145752
  8.8 3.6 %shard_map.64 = (bf16[128,4096]{1,0:T(8,128)(2,1)S(1)}, bf16[128,4096]{1,0:T(8,128)(2,1)S(1)}, bf16[128,4096]{1,0:T(8,128)(2,1)S(1)}) custom-call(bf16[3,128,4096]{2,1,0:T(8,128)(2,1)S(1)} %bitcast.57, f32[1,4096]{1,0:T(1,128)S(1)} %bitcast.58), custom_call_target="tpu_custom_call" | custom-call | flops 9437184 | bytes 6291456 | tf_op jit(solution)/shard_map/pallas_call | solution.py:83
  16.6 2.0 %collective-permute-start.7 = (bf16[256,512]{1,0:T(8,128)(2,1)}, bf16[256,512]{1,0:T(8,128)(2,1)}, u32[]{:S(2)}, u32[]{:S(2)}) collective-permute-start(bf16[256,512]{1,0:T(8,128)(2,1)} %collective-permute-done), channel_id=1, source_target_pairs={{0,4},{4,8},{8,12},{12,14},{14,10},{10,6},{6,2},{2,0},{1,5},{5,9},... | collective-permute-start | bytes 786440 | tf_op jit(solution)/shard_map/ppermute | solution.py:32
  21.7 4.4 %collective-permute-done.7 = bf16[256,512]{1,0:T(8,128)(2,1)} collective-permute-done((bf16[256,512]{1,0:T(8,128)(2,1)}, bf16[256,512]{1,0:T(8,128)(2,1)}, u32[]{:S(2)}, u32[]{:S(2)}) %collective-permute-start.7) | collective-permute-done | bytes 262176 | tf_op jit(solution)/shard_map/ppermute | solution.py:32
  26.1 1.9 %collective-permute-start.10 = (bf16[256,512]{1,0:T(8,128)(2,1)}, bf16[256,512]{1,0:T(8,128)(2,1)S(1)}, u32[]{:S(2)}, u32[]{:S(2)}) collective-permute-start(bf16[256,512]{1,0:T(8,128)(2,1)} %collective-permute-done.6), channel_id=1, source_target_pairs={{0,2},{4,0},{8,4},{12,8},{14,12},{10,14},{6,10},{2,6},{1,3},{5,1},... | collective-permute-start | bytes 786440 | tf_op jit(solution)/shard_map/ppermute | solution.py:32
  28.2 4.9 %collective-permute-done.10 = bf16[256,512]{1,0:T(8,128)(2,1)S(1)} collective-permute-done((bf16[256,512]{1,0:T(8,128)(2,1)}, bf16[256,512]{1,0:T(8,128)(2,1)S(1)}, u32[]{:S(2)}, u32[]{:S(2)}) %collective-permute-start.10) | collective-permute-done | bytes 262176 | tf_op jit(solution)/shard_map/ppermute | solution.py:32
  33.1 1.6 %collective-permute-start.12 = (bf16[256,512]{1,0:T(8,128)(2,1)}, bf16[256,512]{1,0:T(8,128)(2,1)S(1)}, u32[]{:S(2)}, u32[]{:S(2)}) collective-permute-start(bf16[256,512]{1,0:T(8,128)(2,1)} %collective-permute-done.8), channel_id=1, source_target_pairs={{0,2},{4,0},{8,4},{12,8},{14,12},{10,14},{6,10},{2,6},{1,3},{5,1},... | collective-permute-start | bytes 786440 | tf_op jit(solution)/shard_map/ppermute | solution.py:32
  35.2 1.6 %collective-permute-start.13 = (bf16[256,512]{1,0:T(8,128)(2,1)S(1)}, bf16[256,512]{1,0:T(8,128)(2,1)S(1)}, u32[]{:S(2)}, u32[]{:S(2)}) collective-permute-start(bf16[256,512]{1,0:T(8,128)(2,1)S(1)} %collective-permute-done.9), channel_id=1, source_target_pairs={{0,4},{4,8},{8,12},{12,14},{14,10},{10,6},{6,2},{2,0},{1,5},{5,9},... | collective-permute-start | bytes 786440 | tf_op jit(solution)/shard_map/ppermute | solution.py:32
  36.8 2.3 %constant_dynamic-update-slice_fusion.2 = bf16[768,4096]{1,0:T(8,128)(2,1)} fusion(bf16[768,4096]{1,0:T(8,128)(2,1)} %constant_dynamic-update-slice_fusion.3, bf16[128,4096]{1,0:T(8,128)(2,1)} %collective-permute-done.1), kind=kLoop, calls=%fused_computation.108 | loop fusion | bytes 2097152
  40.5 1.9 %collective-permute-start.14 = (bf16[256,512]{1,0:T(8,128)(2,1)S(1)}, bf16[256,512]{1,0:T(8,128)(2,1)S(1)}, u32[]{:S(2)}, u32[]{:S(2)}) collective-permute-start(bf16[256,512]{1,0:T(8,128)(2,1)S(1)} %collective-permute-done.10), channel_id=1, source_target_pairs={{0,2},{4,0},{8,4},{12,8},{14,12},{10,14},{6,10},{2,6},{1,3},{5,1},... | collective-permute-start | bytes 786440 | tf_op jit(solution)/shard_map/ppermute | solution.py:32
  42.9 1.6 %collective-permute-start.16 = (bf16[256,512]{1,0:T(8,128)(2,1)S(1)}, bf16[256,512]{1,0:T(8,128)(2,1)S(1)}, u32[]{:S(2)}, u32[]{:S(2)}) collective-permute-start(bf16[256,512]{1,0:T(8,128)(2,1)S(1)} %collective-permute-done.12), channel_id=1, source_target_pairs={{0,2},{4,0},{8,4},{12,8},{14,12},{10,14},{6,10},{2,6},{1,3},{5,1},... | collective-permute-start | bytes 786440 | tf_op jit(solution)/shard_map/ppermute | solution.py:32
  44.5 2.5 %collective-permute-done.13 = bf16[256,512]{1,0:T(8,128)(2,1)S(1)} collective-permute-done((bf16[256,512]{1,0:T(8,128)(2,1)S(1)}, bf16[256,512]{1,0:T(8,128)(2,1)S(1)}, u32[]{:S(2)}, u32[]{:S(2)}) %collective-permute-start.13) | collective-permute-done | bytes 262176 | tf_op jit(solution)/shard_map/ppermute | solution.py:32
  47.5 1.6 %collective-permute-start.17 = (bf16[256,512]{1,0:T(8,128)(2,1)S(1)}, bf16[256,512]{1,0:T(8,128)(2,1)S(1)}, u32[]{:S(2)}, u32[]{:S(2)}) collective-permute-start(bf16[256,512]{1,0:T(8,128)(2,1)S(1)} %collective-permute-done.13), channel_id=1, source_target_pairs={{0,4},{4,8},{8,12},{12,14},{14,10},{10,6},{6,2},{2,0},{1,5},{5,9},... | collective-permute-start | bytes 786440 | tf_op jit(solution)/shard_map/ppermute | solution.py:32
  49.1 2.4 %constant_dynamic-update-slice_fusion.1 = bf16[768,4096]{1,0:T(8,128)(2,1)} fusion(bf16[768,4096]{1,0:T(8,128)(2,1)} %constant_dynamic-update-slice_fusion.2, bf16[128,4096]{1,0:T(8,128)(2,1)} %collective-permute-done.2), kind=kLoop, calls=%fused_computation.107 | loop fusion | bytes 2097152
  59.6 1.6 %add_add_fusion = f32[768,512]{1,0:T(8,128)S(1)} fusion(f32[768,512]{1,0:T(8,128)S(1)} %fusion.43, f32[768,512]{1,0:T(8,128)S(1)} %fusion.46, f32[768,512]{1,0:T(8,128)S(1)} %fusion.49, f32[768,512]{1,0:T(8,128)S(1)} %fusion.55, f32[768,512]{1,0:T(8,128)S(1)} %fusion.52, bf16[256,512]{1,0:T(8,128)(2,1)} %collective-permute-done.8, ...), kind=kOutput, calls=%fused_computation.6 | convolution fusion | flops 203292672 | bytes 10092548 | tf_op jit(solution)/shard_map/dot_general | solution.py:132
  61.7 2.4 %constant_dynamic-slice_fusion = (bf16[768,256]{1,0:T(8,128)(2,1)}, bf16[768,256]{1,0:T(8,128)(2,1)}, bf16[768,256]{1,0:T(8,128)(2,1)S(1)}, bf16[768,256]{1,0:T(8,128)(2,1)S(1)}) fusion(bf16[768,4096]{1,0:T(8,128)(2,1)} %constant_dynamic-update-slice_fusion, s32[]{:T(128)S(6)} %select_n.253, s32[]{:T(128)S(6)} %select_n.252, s32[]{:T(128)S(6)} %select_n.244, ...), kind=kLoop, calls=%fused_computation.128 | loop fusion | bytes 3145744 | tf_op jit(solution)/shard_map/dynamic_slice | solution.py:129
  74.5 1.8 %add_tanh_fusion = f32[768,512]{1,0:T(8,128)S(1)} fusion(f32[768,512]{1,0:T(8,128)S(1)} %fusion.13, f32[768,512]{1,0:T(8,128)S(1)} %fusion.110, f32[768,512]{1,0:T(8,128)S(1)} %fusion.20, f32[768,512]{1,0:T(8,128)S(1)} %fusion.23, f32[768,512]{1,0:T(8,128)S(1)} %fusion.109, f32[768,512]{1,0:T(8,128)S(1)} %fusion.26, f32[768,512]{1,0:T(8,128)S(1)} %fusion.29, ...), kind=kOutput, calls=%fused_computation.5 | convolution fusion | flops 205258752 | bytes 17956868 | tf_op jit(solution)/shard_map/dot_general | solution.py:132
  84.0 2.5 %collective-permute-done.23 = bf16[6,1024]{1,0:T(8,128)(2,1)S(1)} collective-permute-done((bf16[6,1024]{1,0:T(8,128)(2,1)S(1)}, bf16[6,1024]{1,0:T(8,128)(2,1)S(1)}, u32[]{:S(2)}, u32[]{:S(2)}) %collective-permute-start.23) | collective-permute-done | bytes 12320 | tf_op jit(solution)/shard_map/ppermute | solution.py:52
  86.5 1.6 %collective-permute-done.22 = bf16[6,1024]{1,0:T(8,128)(2,1)S(1)} collective-permute-done((bf16[6,1024]{1,0:T(8,128)(2,1)S(1)}, bf16[6,1024]{1,0:T(8,128)(2,1)S(1)}, u32[]{:S(2)}, u32[]{:S(2)}) %collective-permute-start.22) | collective-permute-done | bytes 12320 | tf_op jit(solution)/shard_map/ppermute | solution.py:52
  88.4 2.3 %collective-permute-done.20 = bf16[6,1024]{1,0:T(8,128)(2,1)S(1)} collective-permute-done((bf16[6,1024]{1,0:T(8,128)(2,1)S(1)}, bf16[6,1024]{1,0:T(8,128)(2,1)S(1)}, u32[]{:S(2)}, u32[]{:S(2)}) %collective-permute-start.20) | collective-permute-done | bytes 12320 | tf_op jit(solution)/shard_map/ppermute | solution.py:52
  93.3 1.8 %collective-permute-start.26 = (bf16[256,1024]{1,0:T(8,128)(2,1)S(1)}, bf16[256,1024]{1,0:T(8,128)(2,1)S(1)}, u32[]{:S(2)}, u32[]{:S(2)}) collective-permute-start(bf16[256,1024]{1,0:T(8,128)(2,1)S(1)} %convert_element_type.144), channel_id=1, source_target_pairs={{0,16},{1,17},{2,18},{3,19},{4,20},{5,21},{6,22},{7,23},{8,24},{9,... | collective-permute-start | bytes 1572872 | tf_op jit(solution)/shard_map/ppermute | solution.py:208
  96.5 1.5 %collective-permute-start.30 = (bf16[256,512]{1,0:T(8,128)(2,1)S(1)}, bf16[256,512]{1,0:T(8,128)(2,1)S(1)}, u32[]{:S(2)}, u32[]{:S(2)}) collective-permute-start(bf16[256,512]{1,0:T(8,128)(2,1)S(1)} %convolution_convert_fusion.2), channel_id=1, source_target_pairs={{0,2},{4,0},{8,4},{12,8},{14,12},{10,14},{6,10},{2,6},{1,3},{5,1},... | collective-permute-start | bytes 786440 | tf_op jit(solution)/shard_map/ppermute | solution.py:32
  98.4 1.6 %collective-permute-start.36 = (bf16[256,512]{1,0:T(8,128)(2,1)S(1)}, bf16[256,512]{1,0:T(8,128)(2,1)S(1)}, u32[]{:S(2)}, u32[]{:S(2)}) collective-permute-start(bf16[256,512]{1,0:T(8,128)(2,1)S(1)} %convolution_convert_fusion), channel_id=1, source_target_pairs={{0,2},{4,0},{8,4},{12,8},{14,12},{10,14},{6,10},{2,6},{1,3},{5,1},... | collective-permute-start | bytes 786440 | tf_op jit(solution)/shard_map/ppermute | solution.py:32
  100.9 3.8 %collective-permute-done.25 = bf16[256,512]{1,0:T(8,128)(2,1)S(1)} collective-permute-done((bf16[256,512]{1,0:T(8,128)(2,1)S(1)}, bf16[256,512]{1,0:T(8,128)(2,1)S(1)}, u32[]{:S(2)}, u32[]{:S(2)}) %collective-permute-start.25) | collective-permute-done | bytes 262176 | tf_op jit(solution)/shard_map/ppermute | solution.py:32
  107.1 1.5 %collective-permute-start.31 = (bf16[256,512]{1,0:T(8,128)(2,1)S(1)}, bf16[256,512]{1,0:T(8,128)(2,1)S(1)}, u32[]{:S(2)}, u32[]{:S(2)}) collective-permute-start(bf16[256,512]{1,0:T(8,128)(2,1)S(1)} %fusion.5), channel_id=1, source_target_pairs={{0,2},{4,0},{8,4},{12,8},{14,12},{10,14},{6,10},{2,6},{1,3},{5,1},... | collective-permute-start | bytes 786440 | tf_op jit(solution)/shard_map/ppermute | solution.py:32
  108.7 2.7 %collective-permute-done.36 = bf16[256,512]{1,0:T(8,128)(2,1)S(1)} collective-permute-done((bf16[256,512]{1,0:T(8,128)(2,1)S(1)}, bf16[256,512]{1,0:T(8,128)(2,1)S(1)}, u32[]{:S(2)}, u32[]{:S(2)}) %collective-permute-start.36) | collective-permute-done | bytes 262176 | tf_op jit(solution)/shard_map/ppermute | solution.py:32
  112.8 1.5 %collective-permute-start.37 = (bf16[256,512]{1,0:T(8,128)(2,1)S(1)}, bf16[256,512]{1,0:T(8,128)(2,1)S(1)}, u32[]{:S(2)}, u32[]{:S(2)}) collective-permute-start(bf16[256,512]{1,0:T(8,128)(2,1)S(1)} %fusion.10), channel_id=1, source_target_pairs={{0,2},{4,0},{8,4},{12,8},{14,12},{10,14},{6,10},{2,6},{1,3},{5,1},... | collective-permute-start | bytes 786440 | tf_op jit(solution)/shard_map/ppermute | solution.py:32
  119.0 2.4 %collective-permute-done.37 = bf16[256,512]{1,0:T(8,128)(2,1)S(1)} collective-permute-done((bf16[256,512]{1,0:T(8,128)(2,1)S(1)}, bf16[256,512]{1,0:T(8,128)(2,1)S(1)}, u32[]{:S(2)}, u32[]{:S(2)}) %collective-permute-start.37) | collective-permute-done | bytes 262176 | tf_op jit(solution)/shard_map/ppermute | solution.py:32
  122.8 1.5 %collective-permute-start.38 = (bf16[256,512]{1,0:T(8,128)(2,1)S(1)}, bf16[256,512]{1,0:T(8,128)(2,1)S(1)}, u32[]{:S(2)}, u32[]{:S(2)}) collective-permute-start(bf16[256,512]{1,0:T(8,128)(2,1)S(1)} %fusion.9), channel_id=1, source_target_pairs={{0,2},{4,0},{8,4},{12,8},{14,12},{10,14},{6,10},{2,6},{1,3},{5,1},... | collective-permute-start | bytes 786440 | tf_op jit(solution)/shard_map/ppermute | solution.py:32
  137.8 2.1 %collective-permute-done.35 = bf16[256,512]{1,0:T(8,128)(2,1)S(1)} collective-permute-done((bf16[256,512]{1,0:T(8,128)(2,1)S(1)}, bf16[256,512]{1,0:T(8,128)(2,1)S(1)}, u32[]{:S(2)}, u32[]{:S(2)}) %collective-permute-start.35) | collective-permute-done | bytes 262176 | tf_op jit(solution)/shard_map/ppermute | solution.py:32
  142.7 1.7 %collective-permute-done.32 = bf16[256,512]{1,0:T(8,128)(2,1)S(1)} collective-permute-done((bf16[256,512]{1,0:T(8,128)(2,1)S(1)}, bf16[256,512]{1,0:T(8,128)(2,1)S(1)}, u32[]{:S(2)}, u32[]{:S(2)}) %collective-permute-start.32) | collective-permute-done | bytes 262176 | tf_op jit(solution)/shard_map/ppermute | solution.py:32
  (147 shorter events, 75.0 us)
Async XLA Ops:
  1.3 19.5 %collective-permute-start.6 = (bf16[256,512]{1,0:T(8,128)(2,1)S(1)}, bf16[256,512]{1,0:T(8,128)(2,1)}, u32[]{:S(2)}, u32[]{:S(2)}) collective-permute-start(bf16[256,512]{1,0:T(8,128)(2,1)S(1)} %get-tuple-element.45), channel_id=1, source_target_pairs={{0,2},{4,0},{8,4},{12,8},{14,12},{10,14},{6,10},{2,6},{1,3},{5,1},... | collective-permute-start | bytes 786440 | tf_op jit(solution)/shard_map/ppermute | solution.py:32
  4.3 10.7 %collective-permute-start.4 = (bf16[256,512]{1,0:T(8,128)(2,1)S(1)}, bf16[256,512]{1,0:T(8,128)(2,1)}, u32[]{:S(2)}, u32[]{:S(2)}) collective-permute-start(bf16[256,512]{1,0:T(8,128)(2,1)S(1)} %get-tuple-element.45), channel_id=1, source_target_pairs={{0,4},{4,8},{8,12},{12,14},{14,10},{10,6},{6,2},{2,0},{1,5},{5,9},... | collective-permute-start | bytes 786440 | tf_op jit(solution)/shard_map/ppermute | solution.py:32
  13.5 21.7 %collective-permute-start.1 = (bf16[128,4096]{1,0:T(8,128)(2,1)S(1)}, bf16[128,4096]{1,0:T(8,128)(2,1)}, u32[]{:S(2)}, u32[]{:S(2)}) collective-permute-start(bf16[128,4096]{1,0:T(8,128)(2,1)S(1)} %get-tuple-element.22), channel_id=1, source_target_pairs={{0,1},{1,0},{2,3},{3,2},{4,5},{5,4},{6,7},{7,6},{8,9},{9,8},{10,11... | collective-permute-start | bytes 3145736 | tf_op jit(solution)/shard_map/ppermute | solution.py:40
  14.0 33.5 %collective-permute-start.2 = (bf16[128,4096]{1,0:T(8,128)(2,1)S(1)}, bf16[128,4096]{1,0:T(8,128)(2,1)}, u32[]{:S(2)}, u32[]{:S(2)}) collective-permute-start(bf16[128,4096]{1,0:T(8,128)(2,1)S(1)} %get-tuple-element.23), channel_id=1, source_target_pairs={{0,1},{1,0},{2,3},{3,2},{4,5},{5,4},{6,7},{7,6},{8,9},{9,8},{10,11... | collective-permute-start | bytes 3145736 | tf_op jit(solution)/shard_map/ppermute | solution.py:40
  16.6 9.5 %collective-permute-start.7 = (bf16[256,512]{1,0:T(8,128)(2,1)}, bf16[256,512]{1,0:T(8,128)(2,1)}, u32[]{:S(2)}, u32[]{:S(2)}) collective-permute-start(bf16[256,512]{1,0:T(8,128)(2,1)} %collective-permute-done), channel_id=1, source_target_pairs={{0,4},{4,8},{8,12},{12,14},{14,10},{10,6},{6,2},{2,0},{1,5},{5,9},... | collective-permute-start | bytes 786440 | tf_op jit(solution)/shard_map/ppermute | solution.py:32
  18.6 9.5 %collective-permute-start.8 = (bf16[256,512]{1,0:T(8,128)(2,1)}, bf16[256,512]{1,0:T(8,128)(2,1)}, u32[]{:S(2)}, u32[]{:S(2)}) collective-permute-start(bf16[256,512]{1,0:T(8,128)(2,1)} %collective-permute-done), channel_id=1, source_target_pairs={{0,2},{4,0},{8,4},{12,8},{14,12},{10,14},{6,10},{2,6},{1,3},{5,1},... | collective-permute-start | bytes 786440 | tf_op jit(solution)/shard_map/ppermute | solution.py:32
  20.8 13.9 %collective-permute-start.9 = (bf16[256,512]{1,0:T(8,128)(2,1)}, bf16[256,512]{1,0:T(8,128)(2,1)S(1)}, u32[]{:S(2)}, u32[]{:S(2)}) collective-permute-start(bf16[256,512]{1,0:T(8,128)(2,1)} %collective-permute-done.4), channel_id=1, source_target_pairs={{0,4},{4,8},{8,12},{12,14},{14,10},{10,6},{6,2},{2,0},{1,5},{5,9},... | collective-permute-start | bytes 786440 | tf_op jit(solution)/shard_map/ppermute | solution.py:32
  28.1 23.3 %collective-permute-start.3 = (bf16[128,4096]{1,0:T(8,128)(2,1)S(1)}, bf16[128,4096]{1,0:T(8,128)(2,1)S(1)}, u32[]{:S(2)}, u32[]{:S(2)}) collective-permute-start(bf16[128,4096]{1,0:T(8,128)(2,1)S(1)} %get-tuple-element.24), channel_id=1, source_target_pairs={{0,1},{1,0},{2,3},{3,2},{4,5},{5,4},{6,7},{7,6},{8,9},{9,8},{10,11... | collective-permute-start | bytes 3145736 | tf_op jit(solution)/shard_map/ppermute | solution.py:40
  34.7 8.3 %collective-permute-start.11 = (bf16[256,512]{1,0:T(8,128)(2,1)}, bf16[256,512]{1,0:T(8,128)(2,1)S(1)}, u32[]{:S(2)}, u32[]{:S(2)}) collective-permute-start(bf16[256,512]{1,0:T(8,128)(2,1)} %collective-permute-done.7), channel_id=1, source_target_pairs={{0,4},{4,8},{8,12},{12,14},{14,10},{10,6},{6,2},{2,0},{1,5},{5,9},... | collective-permute-start | bytes 786440 | tf_op jit(solution)/shard_map/ppermute | solution.py:32
  35.2 11.8 %collective-permute-start.13 = (bf16[256,512]{1,0:T(8,128)(2,1)S(1)}, bf16[256,512]{1,0:T(8,128)(2,1)S(1)}, u32[]{:S(2)}, u32[]{:S(2)}) collective-permute-start(bf16[256,512]{1,0:T(8,128)(2,1)S(1)} %collective-permute-done.9), channel_id=1, source_target_pairs={{0,4},{4,8},{8,12},{12,14},{14,10},{10,6},{6,2},{2,0},{1,5},{5,9},... | collective-permute-start | bytes 786440 | tf_op jit(solution)/shard_map/ppermute | solution.py:32
  40.5 31.3 %collective-permute-start.14 = (bf16[256,512]{1,0:T(8,128)(2,1)S(1)}, bf16[256,512]{1,0:T(8,128)(2,1)S(1)}, u32[]{:S(2)}, u32[]{:S(2)}) collective-permute-start(bf16[256,512]{1,0:T(8,128)(2,1)S(1)} %collective-permute-done.10), channel_id=1, source_target_pairs={{0,2},{4,0},{8,4},{12,8},{14,12},{10,14},{6,10},{2,6},{1,3},{5,1},... | collective-permute-start | bytes 786440 | tf_op jit(solution)/shard_map/ppermute | solution.py:32
  42.9 18.3 %collective-permute-start.16 = (bf16[256,512]{1,0:T(8,128)(2,1)S(1)}, bf16[256,512]{1,0:T(8,128)(2,1)S(1)}, u32[]{:S(2)}, u32[]{:S(2)}) collective-permute-start(bf16[256,512]{1,0:T(8,128)(2,1)S(1)} %collective-permute-done.12), channel_id=1, source_target_pairs={{0,2},{4,0},{8,4},{12,8},{14,12},{10,14},{6,10},{2,6},{1,3},{5,1},... | collective-permute-start | bytes 786440 | tf_op jit(solution)/shard_map/ppermute | solution.py:32
  47.0 23.4 %collective-permute-start.15 = (bf16[256,512]{1,0:T(8,128)(2,1)S(1)}, bf16[256,512]{1,0:T(8,128)(2,1)S(1)}, u32[]{:S(2)}, u32[]{:S(2)}) collective-permute-start(bf16[256,512]{1,0:T(8,128)(2,1)S(1)} %collective-permute-done.11), channel_id=1, source_target_pairs={{0,4},{4,8},{8,12},{12,14},{14,10},{10,6},{6,2},{2,0},{1,5},{5,9},... | collective-permute-start | bytes 786440 | tf_op jit(solution)/shard_map/ppermute | solution.py:32
  47.5 27.1 %collective-permute-start.17 = (bf16[256,512]{1,0:T(8,128)(2,1)S(1)}, bf16[256,512]{1,0:T(8,128)(2,1)S(1)}, u32[]{:S(2)}, u32[]{:S(2)}) collective-permute-start(bf16[256,512]{1,0:T(8,128)(2,1)S(1)} %collective-permute-done.13), channel_id=1, source_target_pairs={{0,4},{4,8},{8,12},{12,14},{14,10},{10,6},{6,2},{2,0},{1,5},{5,9},... | collective-permute-start | bytes 786440 | tf_op jit(solution)/shard_map/ppermute | solution.py:32
  61.2 11.9 %collective-permute-start.18 = (bf16[256,512]{1,0:T(8,128)(2,1)S(1)}, bf16[256,512]{1,0:T(8,128)(2,1)S(1)}, u32[]{:S(2)}, u32[]{:S(2)}) collective-permute-start(bf16[256,512]{1,0:T(8,128)(2,1)S(1)} %collective-permute-done.16), channel_id=1, source_target_pairs={{0,2},{4,0},{8,4},{12,8},{14,12},{10,14},{6,10},{2,6},{1,3},{5,1},... | collective-permute-start | bytes 786440 | tf_op jit(solution)/shard_map/ppermute | solution.py:32
  78.2 8.3 %collective-permute-start.23 = (bf16[6,1024]{1,0:T(8,128)(2,1)S(1)}, bf16[6,1024]{1,0:T(8,128)(2,1)S(1)}, u32[]{:S(2)}, u32[]{:S(2)}) collective-permute-start(bf16[6,1024]{1,0:T(8,128)(2,1)S(1)} %maximum_select_fusion.2), channel_id=1, source_target_pairs={{28,0},{19,1},{30,4},{17,5},{26,8},{21,9},{22,12},{25,13},{18,14},... | collective-permute-start | bytes 36872 | tf_op jit(solution)/shard_map/ppermute | solution.py:52
  79.5 8.6 %collective-permute-start.22 = (bf16[6,1024]{1,0:T(8,128)(2,1)S(1)}, bf16[6,1024]{1,0:T(8,128)(2,1)S(1)}, u32[]{:S(2)}, u32[]{:S(2)}) collective-permute-start(bf16[6,1024]{1,0:T(8,128)(2,1)S(1)} %maximum_select_fusion.2), channel_id=1, source_target_pairs={{24,0},{23,1},{28,4},{19,5},{30,8},{17,9},{26,12},{21,13},{22,14},... | collective-permute-start | bytes 36872 | tf_op jit(solution)/shard_map/ppermute | solution.py:52
  82.1 8.6 %collective-permute-start.20 = (bf16[6,1024]{1,0:T(8,128)(2,1)S(1)}, bf16[6,1024]{1,0:T(8,128)(2,1)S(1)}, u32[]{:S(2)}, u32[]{:S(2)}) collective-permute-start(bf16[6,1024]{1,0:T(8,128)(2,1)S(1)} %maximum_select_fusion.2), channel_id=1, source_target_pairs={{16,0},{31,1},{20,4},{27,5},{24,8},{23,9},{28,12},{19,13},{30,14},... | collective-permute-start | bytes 36872 | tf_op jit(solution)/shard_map/ppermute | solution.py:52
  93.3 41.0 %collective-permute-start.26 = (bf16[256,1024]{1,0:T(8,128)(2,1)S(1)}, bf16[256,1024]{1,0:T(8,128)(2,1)S(1)}, u32[]{:S(2)}, u32[]{:S(2)}) collective-permute-start(bf16[256,1024]{1,0:T(8,128)(2,1)S(1)} %convert_element_type.144), channel_id=1, source_target_pairs={{0,16},{1,17},{2,18},{3,19},{4,20},{5,21},{6,22},{7,23},{8,24},{9,... | collective-permute-start | bytes 1572872 | tf_op jit(solution)/shard_map/ppermute | solution.py:208
  95.5 9.2 %collective-permute-start.25 = (bf16[256,512]{1,0:T(8,128)(2,1)S(1)}, bf16[256,512]{1,0:T(8,128)(2,1)S(1)}, u32[]{:S(2)}, u32[]{:S(2)}) collective-permute-start(bf16[256,512]{1,0:T(8,128)(2,1)S(1)} %convolution_convert_fusion.3), channel_id=1, source_target_pairs={{0,4},{4,8},{8,12},{12,14},{14,10},{10,6},{6,2},{2,0},{1,5},{5,9},... | collective-permute-start | bytes 786440 | tf_op jit(solution)/shard_map/ppermute | solution.py:32
  96.5 9.3 %collective-permute-start.30 = (bf16[256,512]{1,0:T(8,128)(2,1)S(1)}, bf16[256,512]{1,0:T(8,128)(2,1)S(1)}, u32[]{:S(2)}, u32[]{:S(2)}) collective-permute-start(bf16[256,512]{1,0:T(8,128)(2,1)S(1)} %convolution_convert_fusion.2), channel_id=1, source_target_pairs={{0,2},{4,0},{8,4},{12,8},{14,12},{10,14},{6,10},{2,6},{1,3},{5,1},... | collective-permute-start | bytes 786440 | tf_op jit(solution)/shard_map/ppermute | solution.py:32
  98.4 13.0 %collective-permute-start.36 = (bf16[256,512]{1,0:T(8,128)(2,1)S(1)}, bf16[256,512]{1,0:T(8,128)(2,1)S(1)}, u32[]{:S(2)}, u32[]{:S(2)}) collective-permute-start(bf16[256,512]{1,0:T(8,128)(2,1)S(1)} %convolution_convert_fusion), channel_id=1, source_target_pairs={{0,2},{4,0},{8,4},{12,8},{14,12},{10,14},{6,10},{2,6},{1,3},{5,1},... | collective-permute-start | bytes 786440 | tf_op jit(solution)/shard_map/ppermute | solution.py:32
  100.5 16.0 %collective-permute-start.33 = (bf16[256,512]{1,0:T(8,128)(2,1)S(1)}, bf16[256,512]{1,0:T(8,128)(2,1)S(1)}, u32[]{:S(2)}, u32[]{:S(2)}) collective-permute-start(bf16[256,512]{1,0:T(8,128)(2,1)S(1)} %convolution_convert_fusion.1), channel_id=1, source_target_pairs={{0,4},{4,8},{8,12},{12,14},{14,10},{10,6},{6,2},{2,0},{1,5},{5,9},... | collective-permute-start | bytes 786440 | tf_op jit(solution)/shard_map/ppermute | solution.py:32
  107.1 25.7 %collective-permute-start.31 = (bf16[256,512]{1,0:T(8,128)(2,1)S(1)}, bf16[256,512]{1,0:T(8,128)(2,1)S(1)}, u32[]{:S(2)}, u32[]{:S(2)}) collective-permute-start(bf16[256,512]{1,0:T(8,128)(2,1)S(1)} %fusion.5), channel_id=1, source_target_pairs={{0,2},{4,0},{8,4},{12,8},{14,12},{10,14},{6,10},{2,6},{1,3},{5,1},... | collective-permute-start | bytes 786440 | tf_op jit(solution)/shard_map/ppermute | solution.py:32
  112.8 8.6 %collective-permute-start.37 = (bf16[256,512]{1,0:T(8,128)(2,1)S(1)}, bf16[256,512]{1,0:T(8,128)(2,1)S(1)}, u32[]{:S(2)}, u32[]{:S(2)}) collective-permute-start(bf16[256,512]{1,0:T(8,128)(2,1)S(1)} %fusion.10), channel_id=1, source_target_pairs={{0,2},{4,0},{8,4},{12,8},{14,12},{10,14},{6,10},{2,6},{1,3},{5,1},... | collective-permute-start | bytes 786440 | tf_op jit(solution)/shard_map/ppermute | solution.py:32
  115.7 8.7 %collective-permute-start.27 = (bf16[256,512]{1,0:T(8,128)(2,1)S(1)}, bf16[256,512]{1,0:T(8,128)(2,1)S(1)}, u32[]{:S(2)}, u32[]{:S(2)}) collective-permute-start(bf16[256,512]{1,0:T(8,128)(2,1)S(1)} %fusion.4), channel_id=1, source_target_pairs={{0,4},{4,8},{8,12},{12,14},{14,10},{10,6},{6,2},{2,0},{1,5},{5,9},... | collective-permute-start | bytes 786440 | tf_op jit(solution)/shard_map/ppermute | solution.py:32
  117.9 9.4 %collective-permute-start.34 = (bf16[256,512]{1,0:T(8,128)(2,1)S(1)}, bf16[256,512]{1,0:T(8,128)(2,1)S(1)}, u32[]{:S(2)}, u32[]{:S(2)}) collective-permute-start(bf16[256,512]{1,0:T(8,128)(2,1)S(1)} %fusion.7), channel_id=1, source_target_pairs={{0,4},{4,8},{8,12},{12,14},{14,10},{10,6},{6,2},{2,0},{1,5},{5,9},... | collective-permute-start | bytes 786440 | tf_op jit(solution)/shard_map/ppermute | solution.py:32
  122.8 7.8 %collective-permute-start.38 = (bf16[256,512]{1,0:T(8,128)(2,1)S(1)}, bf16[256,512]{1,0:T(8,128)(2,1)S(1)}, u32[]{:S(2)}, u32[]{:S(2)}) collective-permute-start(bf16[256,512]{1,0:T(8,128)(2,1)S(1)} %fusion.9), channel_id=1, source_target_pairs={{0,2},{4,0},{8,4},{12,8},{14,12},{10,14},{6,10},{2,6},{1,3},{5,1},... | collective-permute-start | bytes 786440 | tf_op jit(solution)/shard_map/ppermute | solution.py:32
  125.7 9.8 %collective-permute-start.28 = (bf16[256,512]{1,0:T(8,128)(2,1)S(1)}, bf16[256,512]{1,0:T(8,128)(2,1)S(1)}, u32[]{:S(2)}, u32[]{:S(2)}) collective-permute-start(bf16[256,512]{1,0:T(8,128)(2,1)S(1)} %fusion.3), channel_id=1, source_target_pairs={{0,4},{4,8},{8,12},{12,14},{14,10},{10,6},{6,2},{2,0},{1,5},{5,9},... | collective-permute-start | bytes 786440 | tf_op jit(solution)/shard_map/ppermute | solution.py:32
  128.7 11.3 %collective-permute-start.35 = (bf16[256,512]{1,0:T(8,128)(2,1)S(1)}, bf16[256,512]{1,0:T(8,128)(2,1)S(1)}, u32[]{:S(2)}, u32[]{:S(2)}) collective-permute-start(bf16[256,512]{1,0:T(8,128)(2,1)S(1)} %fusion.6), channel_id=1, source_target_pairs={{0,4},{4,8},{8,12},{12,14},{14,10},{10,6},{6,2},{2,0},{1,5},{5,9},... | collective-permute-start | bytes 786440 | tf_op jit(solution)/shard_map/ppermute | solution.py:32
  132.0 9.3 %collective-permute-start.39 = (bf16[256,512]{1,0:T(8,128)(2,1)S(1)}, bf16[256,512]{1,0:T(8,128)(2,1)S(1)}, u32[]{:S(2)}, u32[]{:S(2)}) collective-permute-start(bf16[256,512]{1,0:T(8,128)(2,1)S(1)} %fusion.8), channel_id=1, source_target_pairs={{0,2},{4,0},{8,4},{12,8},{14,12},{10,14},{6,10},{2,6},{1,3},{5,1},... | collective-permute-start | bytes 786440 | tf_op jit(solution)/shard_map/ppermute | solution.py:32
  134.3 10.2 %collective-permute-start.32 = (bf16[256,512]{1,0:T(8,128)(2,1)S(1)}, bf16[256,512]{1,0:T(8,128)(2,1)S(1)}, u32[]{:S(2)}, u32[]{:S(2)}) collective-permute-start(bf16[256,512]{1,0:T(8,128)(2,1)S(1)} %convolution_add_fusion.7), channel_id=1, source_target_pairs={{0,2},{4,0},{8,4},{12,8},{14,12},{10,14},{6,10},{2,6},{1,3},{5,1},... | collective-permute-start | bytes 786440 | tf_op jit(solution)/shard_map/ppermute | solution.py:32
  (19 other events, 77.0 us)

commit v9 on v8

--- a/solution.py
+++ b/solution.py
@@ -63,18 +63,14 @@
     )
 
 
-def normalize_kernel(chunk, states_ref, gain_ref, *out_refs):
-    def run(out_ref):
-        @pl.loop(0, states_ref.shape[1] // chunk)
-        def _(i):
-            at = pl.ds(pl.multiple_of(i * chunk, chunk), chunk)
-            wide = states_ref[0, at, :].astype(jnp.float32)
-            mean_square = jnp.mean(wide * wide, axis=-1, keepdims=True)
-            wide = wide * lax.rsqrt(mean_square + 1e-05) * gain_ref[...]
-            out_ref[at, :] = wide.astype(jnp.bfloat16)
-
-    for part, out_ref in enumerate(out_refs):
-        pl.when(pl.program_id(0) == part)(functools.partial(run, out_ref))
+def normalize_kernel(chunk, states_ref, gain_ref, out_ref):
+    @pl.loop(0, states_ref.shape[1] // chunk)
+    def _(i):
+        at = pl.ds(pl.multiple_of(i * chunk, chunk), chunk)
+        wide = states_ref[0, at, :].astype(jnp.float32)
+        mean_square = jnp.mean(wide * wide, axis=-1, keepdims=True)
+        wide = wide * lax.rsqrt(mean_square + 1e-05) * gain_ref[...]
+        out_ref[at, :] = wide.astype(jnp.bfloat16)
 
 
 def normalize(states, gain):
@@ -87,8 +83,8 @@
             pl.BlockSpec((1, length, width), lambda i: (i, 0, 0)),
             pl.BlockSpec((1, width), lambda i: (0, 0)),
         ],
-        out_specs=[pl.BlockSpec((length, width), lambda i: (0, 0))] * seqs,
-        out_shape=[jax.ShapeDtypeStruct((length, width), jnp.bfloat16)] * seqs,
+        out_specs=pl.BlockSpec((length, width), lambda i: (i, 0)),
+        out_shape=jax.ShapeDtypeStruct((tokens, width), jnp.bfloat16),
         compiler_params=pltpu.CompilerParams(vmem_limit_bytes=vmem_limit),
         cost_estimate=pl.CostEstimate(
             flops=6 * tokens * width, bytes_accessed=4 * tokens * width, transcendentals=tokens
@@ -114,8 +110,8 @@
     given = given.astype(jnp.bfloat16)
     sibling = from_sibling(given)
 
-    normed = list(normalize(after(sibling, states), gain))
-    normed = jnp.concatenate(normed + [from_sibling(part) for part in normed])
+    normed = normalize(after(sibling, states), gain)
+    normed = [normed, from_sibling(normed)]
     first_sent = along_ring(own, 1)
     ids, cand_ids = token_ids[0], after(first_sent, cand_ids)
     ids = jnp.concatenate([ids, cand_ids], axis=1)
@@ -124,18 +120,22 @@
     counts = lengths.astype(jnp.float32)
     cands = ids[:, length:]
 
-    def columns(offset, part):
+    def columns(offset, part, whose):
         first = (ring_chip(place + offset, chips) * cores + part) * rows
-        return lax.dynamic_slice(normed, (0, first), (seqs * length, rows))
-
-    def product(offset, part, block):
-        return jnp.dot(columns(offset, part), block, preferred_element_type=jnp.float32)
+        return lax.dynamic_slice(normed[whose], (0, first), (seq_dev * length, rows))
+
+    def added(totals, whose, blocks):
+        for offset, part, block in blocks:
+            term = jnp.dot(
+                columns(offset, part, whose), block, preferred_element_type=jnp.float32
+            )
+            totals[whose] = term if totals[whose] is None else totals[whose] + term
 
     parts = (core, 1 - core)
     if chips <= longest_ring:
         moving = {(i, by): block for by in (1, -1) for i, block in enumerate((own, sibling))}
-        total = product(0, parts[0], own) + product(0, parts[1], sibling)
-        first = None
+        totals, sums = [None, None], {}
+        waiting = [(0, parts[0], own), (0, parts[1], sibling)]
         for step in range(1, chips // 2 + 1):
             last = step == chips // 2
             sent = [(0, 1), (0, -1), (1, 1), (1, -1)]
@@ -143,20 +143,26 @@
                 if (step, i, by) == (1, 0, 1):
                     moving[i, by] = first_sent
                 else:
-                    if last and i == 1 and first is not None:
-                        moving[i, by] = after(first, moving[i, by])
+                    if last and step > 2:
+                        moving[i, by] = after(sums[step - 2 + i][1], moving[i, by])
+                    elif step > 2:
+                        moving[i, by] = after(sums[step - 2][0], moving[i, by])
                     moving[i, by] = along_ring(moving[i, by], by)
-                total = total + product(-by * step, parts[i], moving[i, by])
-            first = total if first is None else first
-        active = jnp.tanh(total).reshape(seqs, length, half)
+                waiting.append((-by * step, parts[i], moving[i, by]))
+            for whose in range(2):
+                added(totals, whose, waiting)
+            sums[step] = list(totals)
+            waiting = []
     else:
         both = in_core_order(own, sibling, core)
         gathered = lax.all_gather(both, "chip", axis=0, tiled=True)
-        hidden = jnp.dot(normed, gathered, preferred_element_type=jnp.float32)
-        active = jnp.tanh(hidden).reshape(seqs, length, half)
+        totals = [jnp.dot(n, gathered, preferred_element_type=jnp.float32) for n in normed]
 
     there = jnp.arange(length)[None, :, None] < lengths[:, None, None]
-    pooled = jnp.sum(jnp.where(there, active, 0.0), axis=1) / counts[:, None]
+    there = [there[:seq_dev], there[seq_dev:]]
+    active = [jnp.tanh(total).reshape(seq_dev, length, half) for total in totals]
+    pooled = [jnp.sum(jnp.where(there[w], active[w], 0.0), axis=1) for w in range(2)]
+    pooled = jnp.concatenate(pooled) / counts[:, None]
     pooled_other = from_sibling(pooled)
     pooled_other = jnp.concatenate([pooled_other[seq_dev:], pooled_other[:seq_dev]])
     whole = in_core_order(pooled, pooled_other, core, axis=1)
@@ -170,7 +176,11 @@
     if chips <= longest_ring:
         steps = [(chips // 2, 0, 1), (chips // 2, 1, -1), (chips // 2 - 1, 1, 1)]
         steps += [(chips // 2 - 1, 0, -1)]
-        cut = {(by * step, i): columns(by * step, parts[i]) for step, i, by in steps}
+        cut = {
+            (by * step, i, w): columns(by * step, parts[i], w)
+            for step, i, by in steps
+            for w in range(2)
+        }
         stored, *cuts = lax.optimization_barrier([stored, *cut.values()])
         cut = dict(zip(cut, cuts))
     slab = jnp.concatenate(slab_blocks(stored, chips, core))
@@ -201,19 +211,29 @@
     inner = jnp.sum(whole * unit_grad, axis=-1, keepdims=True)
     pooled_grad = scale * unit_grad - whole * (scale * scale * scale) * inner / embedding
     pooled_grad = lax.dynamic_slice(pooled_grad, (0, core * half), (seqs, half))
-    slope = jnp.where(there, 1.0 - active * active, 0.0)
-    delta = (pooled_grad / counts[:, None])[:, None, :] * slope
-    delta = delta.astype(jnp.bfloat16).reshape(seqs * length, half)
-    delta, weights = lax.optimization_barrier((delta, weights))
+    weighted = pooled_grad / counts[:, None]
+    weighted = [weighted[:seq_dev], weighted[seq_dev:]]
+    delta = [
+        jnp.where(there[w], weighted[w][:, None, :] * (1.0 - active[w] * active[w]), 0.0)
+        .astype(jnp.bfloat16)
+        .reshape(seq_dev * length, half)
+        for w in range(2)
+    ]
+    *delta, weights = lax.optimization_barrier((*delta, weights))
     copied = lax.ppermute(weights.astype(jnp.bfloat16), "grp", [(0, 1)])
 
     def term(offset, i, delta):
-        return lax.dot_general(
-            cut[offset, i] if (offset, i) in cut else columns(offset, parts[i]),
-            delta,
-            (((0,), (0,)), ((), ())),
-            preferred_element_type=jnp.float32,
-        )
+        total = None
+        for w in range(2):
+            key = (offset, i, w)
+            term = lax.dot_general(
+                cut[key] if key in cut else columns(offset, parts[i], w),
+                delta[w],
+                (((0,), (0,)), ((), ())),
+                preferred_element_type=jnp.float32,
+            )
+            total = term if total is None else total + term
+        return total
 
     if chips <= longest_ring:
         arrived = {}
@@ -222,14 +242,14 @@
             for i, by in ((0, 1), (1, -1), (1, 1), (0, -1)):
                 if step == chips // 2 and (i, by) not in ((0, 1), (1, -1)):
                     continue
-                total = term(by * step, i, delta)
+                total = term(by * step, i, delta if step > chips // 2 - 2 else late)
                 if (i, by) in arrived:
                     total = total + arrived[i, by].astype(jnp.float32)
                 if step == 1 and i == 0:
                     total = after(copied, total)
                 arrived[i, by] = along_ring(total.astype(jnp.bfloat16), by)
             if step == chips // 2:
-                late = after(arrived[0, 1], delta)
+                late = [after(arrived[0, 1], part) for part in delta]
         mine, other = [
             term(0, i, late)
             + arrived[i, 1].astype(jnp.float32)
@@ -237,8 +257,11 @@
             for i in range(2)
         ]
     else:
-        grad = lax.dot_general(
-            normed, delta, (((0,), (0,)), ((), ())), preferred_element_type=jnp.float32
+        grad = sum(
+            lax.dot_general(
+                n, d, (((0,), (0,)), ((), ())), preferred_element_type=jnp.float32
+            )
+            for n, d in zip(normed, delta)
         )
         reduced = lax.psum_scatter(grad, "chip", scatter_dimension=0, tiled=True)
         mine, other = [lax.dynamic_slice(reduced, (i * rows, 0), (rows, half)) for i in parts]

time: 149 us -> 163 us (1.094)
  matrix products: 39.6 us -> 57.3 us
  local copies, waits for them, and re-layouts: 16.8 us -> 10.5 us
  starting transfers between devices: 43.5 us -> 38.6 us
  other arithmetic: 4.4 us -> 8.29 us
  waiting for transfers between devices: 38.6 us -> 42.2 us
    dot_general x32 -> x64, matrix products: 38.9 us -> 56.6 us  [the longest x32 30.6 us: added(): jnp.dot(columns(offset, part, whose), block, preferred_element_type=jnp.f...]
    unnamed x26 -> x41, local copies, waits for them, and re-layouts: 10.6 us -> 4.66 us
    ppermute x28, starting transfers between devices: 35.3 us -> 31.2 us  [along_ring(): return lax.ppermute(block, 'chip', pairs)]
    ppermute x28, waiting for transfers between devices: 29.6 us -> 33.4 us  [along_ring(): return lax.ppermute(block, 'chip', pairs)]
  transfers between devices with their start and end apart: 41 -> 39, of which waited for: 20 -> 13; matrix products, arithmetic and copies ran while one was open for 36% -> 36% of each run, Pallas kernels for 2% -> 2%
where the time goes in v9:
time: 163 us; the launch traced here: 162 us
  matrix products  57.3 us (35%)
  waiting for transfers between devices  42.2 us (26%)
  starting transfers between devices  38.6 us (24%)
  local copies, waits for them, and re-layouts  10.5 us (6%)
  other arithmetic  8.29 us (5%)
  Pallas kernels  3.58 us (2%)
    ppermute x28, waiting for transfers between devices, along_ring(): return lax.ppermute(block, 'chip', pairs)  33.4 us
    ppermute x28, starting transfers between devices, along_ring(): return lax.ppermute(block, 'chip', pairs)  31.2 us
    dot_general x32, matrix products, added(): jnp.dot(columns(offset, part, whose), block, preferred_element_type=jnp.f...  30.6 us
    dot_general x32, matrix products, term(): lax.dot_general(cut[key] if key in cut else columns(offset, parts[i], w),...  26 us
    ppermute x4, waiting for transfers between devices, slab_blocks(): kept.append(lax.ppermute(stored, ('grp', 'chip', 'core'), pairs))  6.63 us
    ppermute x4, starting transfers between devices, slab_blocks(): kept.append(lax.ppermute(stored, ('grp', 'chip', 'core'), pairs))  5.16 us
    unnamed x41, local copies, waits for them, and re-layouts  4.66 us
    pallas_call x1, Pallas kernels, normalize(): pl.pallas_call(functools.partial(normalize_kernel, 16), grid=(seqs,), in_...  3.58 us
  transfers between devices with their start and end apart: 39, of which 13 were waited for; matrix products, arithmetic and copies ran while one was open for 36% of the time, Pallas kernels for 2%

profile of v9, /device:TPU:0, one launch (start us, length us, event | category | flops | bytes accessed | tf_op | source)
XLA Modules:
  0.0 161.6 jit_solution(5449999384001737598)
XLA Ops:
  1.3 3.0 %collective-permute-start.3 = (bf16[256,512]{1,0:T(8,128)(2,1)S(1)}, bf16[256,512]{1,0:T(8,128)(2,1)}, u32[]{:S(2)}, u32[]{:S(2)}) collective-permute-start(bf16[256,512]{1,0:T(8,128)(2,1)S(1)} %get-tuple-element.65), channel_id=1, source_target_pairs={{0,2},{4,0},{8,4},{12,8},{14,12},{10,14},{6,10},{2,6},{1,3},{5,1},... | collective-permute-start | bytes 786440 | tf_op jit(solution)/shard_map/ppermute | solution.py:32
  6.9 1.9 %copy-done = bf16[1,3,128,4096]{3,2,1,0:T(8,128)(2,1)S(1)} copy-done((bf16[1,3,128,4096]{3,2,1,0:T(8,128)(2,1)S(1)}, bf16[1,3,128,4096]{3,2,1,0:T(8,128)(2,1)}, u32[]{:S(2)}) %copy-start) | copy-done | bytes 3145752
  9.5 3.6 %shard_map.64 = bf16[384,4096]{1,0:T(8,128)(2,1)S(1)} custom-call(bf16[3,128,4096]{2,1,0:T(8,128)(2,1)S(1)} %bitcast.110, f32[1,4096]{1,0:T(1,128)S(1)} %bitcast.111), custom_call_target="tpu_custom_call" | custom-call | flops 9437184 | bytes 6291456 | tf_op jit(solution)/shard_map/pallas_call | solution.py:79
  14.7 1.9 %collective-permute-start.5 = (bf16[256,512]{1,0:T(8,128)(2,1)}, bf16[256,512]{1,0:T(8,128)(2,1)}, u32[]{:S(2)}, u32[]{:S(2)}) collective-permute-start(bf16[256,512]{1,0:T(8,128)(2,1)} %collective-permute-done), channel_id=1, source_target_pairs={{0,2},{4,0},{8,4},{12,8},{14,12},{10,14},{6,10},{2,6},{1,3},{5,1},... | collective-permute-start | bytes 786440 | tf_op jit(solution)/shard_map/ppermute | solution.py:32
  17.0 2.0 %collective-permute-start.7 = (bf16[256,512]{1,0:T(8,128)(2,1)}, bf16[256,512]{1,0:T(8,128)(2,1)}, u32[]{:S(2)}, u32[]{:S(2)}) collective-permute-start(bf16[256,512]{1,0:T(8,128)(2,1)} %collective-permute-done.3), channel_id=1, source_target_pairs={{0,2},{4,0},{8,4},{12,8},{14,12},{10,14},{6,10},{2,6},{1,3},{5,1},... | collective-permute-start | bytes 786440 | tf_op jit(solution)/shard_map/ppermute | solution.py:32
  21.4 2.1 %fusion.21 = f32[384,512]{1,0:T(8,128)} fusion(f32[384,512]{1,0:T(8,128)S(1)} %fusion.130, f32[384,512]{1,0:T(8,128)S(1)} %convolution_add_fusion.9, bf16[256,512]{1,0:T(8,128)(2,1)} %collective-permute-done.1, bf16[384,4096]{1,0:T(8,128)(2,1)S(1)} %shard_map.64, s32[]{:T(128)S(6)} %select_n.299), kind=kOutput, calls=%fused_computation.32 | convolution fusion | flops 101056512 | bytes 2818052 | tf_op jit(solution)/shard_map/dot_general | solution.py:129
  26.1 1.5 fusion.20
  27.6 4.0 %collective-permute-done.6 = bf16[256,512]{1,0:T(8,128)(2,1)} collective-permute-done((bf16[256,512]{1,0:T(8,128)(2,1)}, bf16[256,512]{1,0:T(8,128)(2,1)}, u32[]{:S(2)}, u32[]{:S(2)}) %collective-permute-start.6) | collective-permute-done | bytes 262176 | tf_op jit(solution)/shard_map/ppermute | solution.py:32
  32.0 1.7 %collective-permute-start.11 = (bf16[256,512]{1,0:T(8,128)(2,1)}, bf16[256,512]{1,0:T(8,128)(2,1)S(1)}, u32[]{:S(2)}, u32[]{:S(2)}) collective-permute-start(bf16[256,512]{1,0:T(8,128)(2,1)} %collective-permute-done.7), channel_id=1, source_target_pairs={{0,2},{4,0},{8,4},{12,8},{14,12},{10,14},{6,10},{2,6},{1,3},{5,1},... | collective-permute-start | bytes 786440 | tf_op jit(solution)/shard_map/ppermute | solution.py:32
  34.0 1.7 %collective-permute-start.9 = (bf16[256,512]{1,0:T(8,128)(2,1)}, bf16[256,512]{1,0:T(8,128)(2,1)S(1)}, u32[]{:S(2)}, u32[]{:S(2)}) collective-permute-start(bf16[256,512]{1,0:T(8,128)(2,1)} %collective-permute-done.5), channel_id=1, source_target_pairs={{0,2},{4,0},{8,4},{12,8},{14,12},{10,14},{6,10},{2,6},{1,3},{5,1},... | collective-permute-start | bytes 786440 | tf_op jit(solution)/shard_map/ppermute | solution.py:32
  38.2 6.2 %collective-permute-done.8 = bf16[256,512]{1,0:T(8,128)(2,1)S(1)} collective-permute-done((bf16[256,512]{1,0:T(8,128)(2,1)}, bf16[256,512]{1,0:T(8,128)(2,1)S(1)}, u32[]{:S(2)}, u32[]{:S(2)}) %collective-permute-start.8) | collective-permute-done | bytes 262176 | tf_op jit(solution)/shard_map/ppermute | solution.py:32
  47.3 4.1 %collective-permute-done.13 = bf16[256,512]{1,0:T(8,128)(2,1)S(1)} collective-permute-done((bf16[256,512]{1,0:T(8,128)(2,1)S(1)}, bf16[256,512]{1,0:T(8,128)(2,1)S(1)}, u32[]{:S(2)}, u32[]{:S(2)}) %collective-permute-start.13) | collective-permute-done | bytes 262176 | tf_op jit(solution)/shard_map/ppermute | solution.py:32
  64.6 1.5 collective-permute-start.15
  67.3 2.1 %constant_dynamic-slice_fusion = (bf16[384,256]{1,0:T(8,128)(2,1)}, bf16[384,256]{1,0:T(8,128)(2,1)}, bf16[384,256]{1,0:T(8,128)(2,1)S(1)}, bf16[384,256]{1,0:T(8,128)(2,1)S(1)}) fusion(bf16[384,4096]{1,0:T(8,128)(2,1)} %collective-permute-done.14, s32[]{:T(128)S(6)} %select_n.325, s32[]{:T(128)S(6)} %select_n.324, s32[]{:T(128)S(6)} %select_n.315, ...), kind=kLoop, calls=%fused_computation.227 | loop fusion | bytes 1572880 | tf_op jit(solution)/shard_map/dynamic_slice | solution.py:125
  72.7 5.3 %collective-permute-done.16 = bf16[256,512]{1,0:T(8,128)(2,1)S(1)} collective-permute-done((bf16[256,512]{1,0:T(8,128)(2,1)S(1)}, bf16[256,512]{1,0:T(8,128)(2,1)S(1)}, u32[]{:S(2)}, u32[]{:S(2)}) %collective-permute-start.16) | collective-permute-done | bytes 262176 | tf_op jit(solution)/shard_map/ppermute | solution.py:32
  89.9 2.1 %collective-permute-done.19 = bf16[6,1024]{1,0:T(8,128)(2,1)S(1)} collective-permute-done((bf16[6,1024]{1,0:T(8,128)(2,1)S(1)}, bf16[6,1024]{1,0:T(8,128)(2,1)S(1)}, u32[]{:S(2)}, u32[]{:S(2)}) %collective-permute-start.19) | collective-permute-done | bytes 12320 | tf_op jit(solution)/shard_map/ppermute | solution.py:52
  92.0 2.3 %collective-permute-done.20 = bf16[6,1024]{1,0:T(8,128)(2,1)S(1)} collective-permute-done((bf16[6,1024]{1,0:T(8,128)(2,1)S(1)}, bf16[6,1024]{1,0:T(8,128)(2,1)S(1)}, u32[]{:S(2)}, u32[]{:S(2)}) %collective-permute-start.20) | collective-permute-done | bytes 12320 | tf_op jit(solution)/shard_map/ppermute | solution.py:52
  94.3 2.3 %collective-permute-done.21 = bf16[6,1024]{1,0:T(8,128)(2,1)S(1)} collective-permute-done((bf16[6,1024]{1,0:T(8,128)(2,1)S(1)}, bf16[6,1024]{1,0:T(8,128)(2,1)S(1)}, u32[]{:S(2)}, u32[]{:S(2)}) %collective-permute-start.21) | collective-permute-done | bytes 12320 | tf_op jit(solution)/shard_map/ppermute | solution.py:52
  98.8 1.7 %fusion.51 = (bf16[384,512]{1,0:T(8,128)(2,1)S(1)}, bf16[384,512]{1,0:T(8,128)(2,1)S(1)}) fusion(f32[384,512]{1,0:T(8,128)} %copy-done.3, f32[3,512]{1,0:T(4,128)S(1)} %get-tuple-element.69, pred[384]{0:T(512)(128)(4,1)S(1)} %get-tuple-element.75, f32[384,512]{1,0:T(8,128)} %copy-done.4, f32[3,512]{1,0:T(4,128)S(1)} %get-tuple-element.70, ...), kind=kLoop, calls=%fused_computation.84 | loop fusion | flops 1966080 | bytes 2372352 | tf_op jit(solution)/shard_map/convert_element_type | solution.py:218
  102.8 1.5 collective-permute-start.31
  106.3 1.5 collective-permute-start.34
  110.6 6.2 %collective-permute-done.23 = bf16[256,512]{1,0:T(8,128)(2,1)S(1)} collective-permute-done((bf16[256,512]{1,0:T(8,128)(2,1)S(1)}, bf16[256,512]{1,0:T(8,128)(2,1)S(1)}, u32[]{:S(2)}, u32[]{:S(2)}) %collective-permute-start.23) | collective-permute-done | bytes 262176 | tf_op jit(solution)/shard_map/ppermute | solution.py:32
  118.4 1.5 collective-permute-start.32
  123.1 1.5 collective-permute-start.25
  136.9 1.6 collective-permute-start.33
  138.8 1.5 collective-permute-start.26
  140.3 2.1 %collective-permute-done.36 = bf16[256,512]{1,0:T(8,128)(2,1)S(1)} collective-permute-done((bf16[256,512]{1,0:T(8,128)(2,1)S(1)}, bf16[256,512]{1,0:T(8,128)(2,1)S(1)}, u32[]{:S(2)}, u32[]{:S(2)}) %collective-permute-start.36) | collective-permute-done | bytes 262176 | tf_op jit(solution)/shard_map/ppermute | solution.py:32
  145.8 2.9 %collective-permute-done.26 = bf16[256,512]{1,0:T(8,128)(2,1)S(1)} collective-permute-done((bf16[256,512]{1,0:T(8,128)(2,1)S(1)}, bf16[256,512]{1,0:T(8,128)(2,1)S(1)}, u32[]{:S(2)}, u32[]{:S(2)}) %collective-permute-start.26) | collective-permute-done | bytes 262176 | tf_op jit(solution)/shard_map/ppermute | solution.py:32
  149.7 1.5 collective-permute-start.27
  152.4 1.5 fusion.103
  153.9 2.5 %collective-permute-done.27 = bf16[256,512]{1,0:T(8,128)(2,1)} collective-permute-done((bf16[256,512]{1,0:T(8,128)(2,1)}, bf16[256,512]{1,0:T(8,128)(2,1)}, u32[]{:S(2)}, u32[]{:S(2)}) %collective-permute-start.27) | collective-permute-done | bytes 262176 | tf_op jit(solution)/shard_map/ppermute | solution.py:32
  159.2 2.4 %select_bitcast_fusion = f32[1,256,1024]{2,1,0:T(8,128)} fusion(bf16[256,1024]{1,0:T(8,128)(2,1)S(1)} %copy-done.18, f32[256,512]{1,0:T(8,128)S(1)} %fusion.35, f32[256,512]{1,0:T(8,128)} %collective-permute-done.38, f32[256]{0:T(256)S(1)} %add_rsqrt_fusion, pred[]{:T(512)S(6)} %eq.66, pred[]{:T(512)S(6)} %eq.65), kind=kLoop, calls=%fused_computation.80 | loop fusion | flops 1572864 | bytes 2622466 | tf_op jit(solution)/shard_map/broadcast_in_dim | solution.py:273
  (193 shorter events, 81.4 us)
Async XLA Ops:
  1.3 15.7 %collective-permute-start.3 = (bf16[256,512]{1,0:T(8,128)(2,1)S(1)}, bf16[256,512]{1,0:T(8,128)(2,1)}, u32[]{:S(2)}, u32[]{:S(2)}) collective-permute-start(bf16[256,512]{1,0:T(8,128)(2,1)S(1)} %get-tuple-element.65), channel_id=1, source_target_pairs={{0,2},{4,0},{8,4},{12,8},{14,12},{10,14},{6,10},{2,6},{1,3},{5,1},... | collective-permute-start | bytes 786440 | tf_op jit(solution)/shard_map/ppermute | solution.py:32
  4.3 9.4 %collective-permute-start.1 = (bf16[256,512]{1,0:T(8,128)(2,1)S(1)}, bf16[256,512]{1,0:T(8,128)(2,1)}, u32[]{:S(2)}, u32[]{:S(2)}) collective-permute-start(bf16[256,512]{1,0:T(8,128)(2,1)S(1)} %get-tuple-element.65), channel_id=1, source_target_pairs={{0,4},{4,8},{8,12},{12,14},{14,10},{10,6},{6,2},{2,0},{1,5},{5,9},... | collective-permute-start | bytes 786440 | tf_op jit(solution)/shard_map/ppermute | solution.py:32
  13.1 38.6 %collective-permute-start.14 = (bf16[384,4096]{1,0:T(8,128)(2,1)S(1)}, bf16[384,4096]{1,0:T(8,128)(2,1)}, u32[]{:S(2)}, u32[]{:S(2)}) collective-permute-start(bf16[384,4096]{1,0:T(8,128)(2,1)S(1)} %shard_map.64), channel_id=1, source_target_pairs={{0,1},{1,0},{2,3},{3,2},{4,5},{5,4},{6,7},{7,6},{8,9},{9,8},{10,11... | collective-permute-start | bytes 9437192 | tf_op jit(solution)/shard_map/ppermute | solution.py:40
  13.7 9.8 %collective-permute-start.2 = (s32[3,136]{1,0:T(4,128)S(1)}, s32[3,136]{1,0:T(4,128)S(1)}, u32[]{:S(2)}, u32[]{:S(2)}) collective-permute-start(s32[3,136]{1,0:T(4,128)S(1)} %pad_add_fusion.1), channel_id=1, source_target_pairs={{0,1},{1,0},{2,3},{3,2},{4,5},{5,4},{6,7},{7,6},{8,9},{9,8},{10,11... | collective-permute-start | bytes 4904 | tf_op jit(solution)/shard_map/ppermute | solution.py:40
  14.7 10.2 %collective-permute-start.5 = (bf16[256,512]{1,0:T(8,128)(2,1)}, bf16[256,512]{1,0:T(8,128)(2,1)}, u32[]{:S(2)}, u32[]{:S(2)}) collective-permute-start(bf16[256,512]{1,0:T(8,128)(2,1)} %collective-permute-done), channel_id=1, source_target_pairs={{0,2},{4,0},{8,4},{12,8},{14,12},{10,14},{6,10},{2,6},{1,3},{5,1},... | collective-permute-start | bytes 786440 | tf_op jit(solution)/shard_map/ppermute | solution.py:32
  16.6 9.6 %collective-permute-start.4 = (bf16[256,512]{1,0:T(8,128)(2,1)}, bf16[256,512]{1,0:T(8,128)(2,1)}, u32[]{:S(2)}, u32[]{:S(2)}) collective-permute-start(bf16[256,512]{1,0:T(8,128)(2,1)} %collective-permute-done), channel_id=1, source_target_pairs={{0,4},{4,8},{8,12},{12,14},{14,10},{10,6},{6,2},{2,0},{1,5},{5,9},... | collective-permute-start | bytes 786440 | tf_op jit(solution)/shard_map/ppermute | solution.py:32
  17.0 15.0 %collective-permute-start.7 = (bf16[256,512]{1,0:T(8,128)(2,1)}, bf16[256,512]{1,0:T(8,128)(2,1)}, u32[]{:S(2)}, u32[]{:S(2)}) collective-permute-start(bf16[256,512]{1,0:T(8,128)(2,1)} %collective-permute-done.3), channel_id=1, source_target_pairs={{0,2},{4,0},{8,4},{12,8},{14,12},{10,14},{6,10},{2,6},{1,3},{5,1},... | collective-permute-start | bytes 786440 | tf_op jit(solution)/shard_map/ppermute | solution.py:32
  23.5 8.2 %collective-permute-start.6 = (bf16[256,512]{1,0:T(8,128)(2,1)}, bf16[256,512]{1,0:T(8,128)(2,1)}, u32[]{:S(2)}, u32[]{:S(2)}) collective-permute-start(bf16[256,512]{1,0:T(8,128)(2,1)} %collective-permute-done.1), channel_id=1, source_target_pairs={{0,4},{4,8},{8,12},{12,14},{14,10},{10,6},{6,2},{2,0},{1,5},{5,9},... | collective-permute-start | bytes 786440 | tf_op jit(solution)/shard_map/ppermute | solution.py:32
  31.7 15.3 %collective-permute-start.10 = (bf16[256,512]{1,0:T(8,128)(2,1)}, bf16[256,512]{1,0:T(8,128)(2,1)S(1)}, u32[]{:S(2)}, u32[]{:S(2)}) collective-permute-start(bf16[256,512]{1,0:T(8,128)(2,1)} %collective-permute-done.6), channel_id=1, source_target_pairs={{0,4},{4,8},{8,12},{12,14},{14,10},{10,6},{6,2},{2,0},{1,5},{5,9},... | collective-permute-start | bytes 786440 | tf_op jit(solution)/shard_map/ppermute | solution.py:32
  32.0 14.7 %collective-permute-start.11 = (bf16[256,512]{1,0:T(8,128)(2,1)}, bf16[256,512]{1,0:T(8,128)(2,1)S(1)}, u32[]{:S(2)}, u32[]{:S(2)}) collective-permute-start(bf16[256,512]{1,0:T(8,128)(2,1)} %collective-permute-done.7), channel_id=1, source_target_pairs={{0,2},{4,0},{8,4},{12,8},{14,12},{10,14},{6,10},{2,6},{1,3},{5,1},... | collective-permute-start | bytes 786440 | tf_op jit(solution)/shard_map/ppermute | solution.py:32
  33.7 10.7 %collective-permute-start.8 = (bf16[256,512]{1,0:T(8,128)(2,1)}, bf16[256,512]{1,0:T(8,128)(2,1)S(1)}, u32[]{:S(2)}, u32[]{:S(2)}) collective-permute-start(bf16[256,512]{1,0:T(8,128)(2,1)} %collective-permute-done.4), channel_id=1, source_target_pairs={{0,4},{4,8},{8,12},{12,14},{14,10},{10,6},{6,2},{2,0},{1,5},{5,9},... | collective-permute-start | bytes 786440 | tf_op jit(solution)/shard_map/ppermute | solution.py:32
  34.0 11.0 %collective-permute-start.9 = (bf16[256,512]{1,0:T(8,128)(2,1)}, bf16[256,512]{1,0:T(8,128)(2,1)S(1)}, u32[]{:S(2)}, u32[]{:S(2)}) collective-permute-start(bf16[256,512]{1,0:T(8,128)(2,1)} %collective-permute-done.5), channel_id=1, source_target_pairs={{0,2},{4,0},{8,4},{12,8},{14,12},{10,14},{6,10},{2,6},{1,3},{5,1},... | collective-permute-start | bytes 786440 | tf_op jit(solution)/shard_map/ppermute | solution.py:32
  44.4 25.7 %collective-permute-start.12 = (bf16[256,512]{1,0:T(8,128)(2,1)S(1)}, bf16[256,512]{1,0:T(8,128)(2,1)S(1)}, u32[]{:S(2)}, u32[]{:S(2)}) collective-permute-start(bf16[256,512]{1,0:T(8,128)(2,1)S(1)} %collective-permute-done.8), channel_id=1, source_target_pairs={{0,4},{4,8},{8,12},{12,14},{14,10},{10,6},{6,2},{2,0},{1,5},{5,9},... | collective-permute-start | bytes 786440 | tf_op jit(solution)/shard_map/ppermute | solution.py:32
  64.6 7.8 %collective-permute-start.15 = (bf16[256,512]{1,0:T(8,128)(2,1)S(1)}, bf16[256,512]{1,0:T(8,128)(2,1)S(1)}, u32[]{:S(2)}, u32[]{:S(2)}) collective-permute-start(bf16[256,512]{1,0:T(8,128)(2,1)S(1)} %collective-permute-done.10), channel_id=1, source_target_pairs={{0,4},{4,8},{8,12},{12,14},{14,10},{10,6},{6,2},{2,0},{1,5},{5,9},... | collective-permute-start | bytes 786440 | tf_op jit(solution)/shard_map/ppermute | solution.py:32
  85.4 6.6 %collective-permute-start.19 = (bf16[6,1024]{1,0:T(8,128)(2,1)S(1)}, bf16[6,1024]{1,0:T(8,128)(2,1)S(1)}, u32[]{:S(2)}, u32[]{:S(2)}) collective-permute-start(bf16[6,1024]{1,0:T(8,128)(2,1)S(1)} %maximum_select_fusion.2), channel_id=1, source_target_pairs={{20,0},{27,1},{24,4},{23,5},{28,8},{19,9},{30,12},{17,13},{26,14},... | collective-permute-start | bytes 36872 | tf_op jit(solution)/shard_map/ppermute | solution.py:52
  86.7 7.6 %collective-permute-start.20 = (bf16[6,1024]{1,0:T(8,128)(2,1)S(1)}, bf16[6,1024]{1,0:T(8,128)(2,1)S(1)}, u32[]{:S(2)}, u32[]{:S(2)}) collective-permute-start(bf16[6,1024]{1,0:T(8,128)(2,1)S(1)} %maximum_select_fusion.2), channel_id=1, source_target_pairs={{24,0},{23,1},{28,4},{19,5},{30,8},{17,9},{26,12},{21,13},{22,14},... | collective-permute-start | bytes 36872 | tf_op jit(solution)/shard_map/ppermute | solution.py:52
  88.0 8.6 %collective-permute-start.21 = (bf16[6,1024]{1,0:T(8,128)(2,1)S(1)}, bf16[6,1024]{1,0:T(8,128)(2,1)S(1)}, u32[]{:S(2)}, u32[]{:S(2)}) collective-permute-start(bf16[6,1024]{1,0:T(8,128)(2,1)S(1)} %maximum_select_fusion.2), channel_id=1, source_target_pairs={{28,0},{19,1},{30,4},{17,5},{26,8},{21,9},{22,12},{25,13},{18,14},... | collective-permute-start | bytes 36872 | tf_op jit(solution)/shard_map/ppermute | solution.py:52
  102.8 15.3 %collective-permute-start.31 = (bf16[256,512]{1,0:T(8,128)(2,1)S(1)}, bf16[256,512]{1,0:T(8,128)(2,1)S(1)}, u32[]{:S(2)}, u32[]{:S(2)}) collective-permute-start(bf16[256,512]{1,0:T(8,128)(2,1)S(1)} %fusion.46), channel_id=1, source_target_pairs={{0,4},{4,8},{8,12},{12,14},{14,10},{10,6},{6,2},{2,0},{1,5},{5,9},... | collective-permute-start | bytes 786440 | tf_op jit(solution)/shard_map/ppermute | solution.py:32
  105.0 11.9 %collective-permute-start.23 = (bf16[256,512]{1,0:T(8,128)(2,1)S(1)}, bf16[256,512]{1,0:T(8,128)(2,1)S(1)}, u32[]{:S(2)}, u32[]{:S(2)}) collective-permute-start(bf16[256,512]{1,0:T(8,128)(2,1)S(1)} %fusion.44), channel_id=1, source_target_pairs={{0,4},{4,8},{8,12},{12,14},{14,10},{10,6},{6,2},{2,0},{1,5},{5,9},... | collective-permute-start | bytes 786440 | tf_op jit(solution)/shard_map/ppermute | solution.py:32
  106.3 13.7 %collective-permute-start.34 = (bf16[256,512]{1,0:T(8,128)(2,1)S(1)}, bf16[256,512]{1,0:T(8,128)(2,1)S(1)}, u32[]{:S(2)}, u32[]{:S(2)}) collective-permute-start(bf16[256,512]{1,0:T(8,128)(2,1)S(1)} %fusion.47), channel_id=1, source_target_pairs={{0,2},{4,0},{8,4},{12,8},{14,12},{10,14},{6,10},{2,6},{1,3},{5,1},... | collective-permute-start | bytes 786440 | tf_op jit(solution)/shard_map/ppermute | solution.py:32
  107.9 36.6 %collective-permute-start.24 = (bf16[256,1024]{1,0:T(8,128)(2,1)S(1)}, bf16[256,1024]{1,0:T(8,128)(2,1)S(1)}, u32[]{:S(2)}, u32[]{:S(2)}) collective-permute-start(bf16[256,1024]{1,0:T(8,128)(2,1)S(1)} %convert_element_type.149), channel_id=1, source_target_pairs={{0,16},{1,17},{2,18},{3,19},{4,20},{5,21},{6,22},{7,23},{8,24},{9,... | collective-permute-start | bytes 1572872 | tf_op jit(solution)/shard_map/ppermute | solution.py:223
  109.8 16.0 %collective-permute-start.28 = (bf16[256,512]{1,0:T(8,128)(2,1)S(1)}, bf16[256,512]{1,0:T(8,128)(2,1)S(1)}, u32[]{:S(2)}, u32[]{:S(2)}) collective-permute-start(bf16[256,512]{1,0:T(8,128)(2,1)S(1)} %fusion.45), channel_id=1, source_target_pairs={{0,2},{4,0},{8,4},{12,8},{14,12},{10,14},{6,10},{2,6},{1,3},{5,1},... | collective-permute-start | bytes 786440 | tf_op jit(solution)/shard_map/ppermute | solution.py:32
  118.4 18.1 %collective-permute-start.32 = (bf16[256,512]{1,0:T(8,128)(2,1)S(1)}, bf16[256,512]{1,0:T(8,128)(2,1)S(1)}, u32[]{:S(2)}, u32[]{:S(2)}) collective-permute-start(bf16[256,512]{1,0:T(8,128)(2,1)S(1)} %fusion.40), channel_id=1, source_target_pairs={{0,4},{4,8},{8,12},{12,14},{14,10},{10,6},{6,2},{2,0},{1,5},{5,9},... | collective-permute-start | bytes 786440 | tf_op jit(solution)/shard_map/ppermute | solution.py:32
  121.2 14.4 %collective-permute-start.35 = (bf16[256,512]{1,0:T(8,128)(2,1)S(1)}, bf16[256,512]{1,0:T(8,128)(2,1)S(1)}, u32[]{:S(2)}, u32[]{:S(2)}) collective-permute-start(bf16[256,512]{1,0:T(8,128)(2,1)S(1)} %fusion.43), channel_id=1, source_target_pairs={{0,2},{4,0},{8,4},{12,8},{14,12},{10,14},{6,10},{2,6},{1,3},{5,1},... | collective-permute-start | bytes 786440 | tf_op jit(solution)/shard_map/ppermute | solution.py:32
  123.1 15.4 %collective-permute-start.25 = (bf16[256,512]{1,0:T(8,128)(2,1)S(1)}, bf16[256,512]{1,0:T(8,128)(2,1)S(1)}, u32[]{:S(2)}, u32[]{:S(2)}) collective-permute-start(bf16[256,512]{1,0:T(8,128)(2,1)S(1)} %fusion.37), channel_id=1, source_target_pairs={{0,4},{4,8},{8,12},{12,14},{14,10},{10,6},{6,2},{2,0},{1,5},{5,9},... | collective-permute-start | bytes 786440 | tf_op jit(solution)/shard_map/ppermute | solution.py:32
  126.2 17.1 %collective-permute-start.29 = (bf16[256,512]{1,0:T(8,128)(2,1)S(1)}, bf16[256,512]{1,0:T(8,128)(2,1)S(1)}, u32[]{:S(2)}, u32[]{:S(2)}) collective-permute-start(bf16[256,512]{1,0:T(8,128)(2,1)S(1)} %fusion.38), channel_id=1, source_target_pairs={{0,2},{4,0},{8,4},{12,8},{14,12},{10,14},{6,10},{2,6},{1,3},{5,1},... | collective-permute-start | bytes 786440 | tf_op jit(solution)/shard_map/ppermute | solution.py:32
  136.0 6.5 %collective-permute-start.36 = (bf16[256,512]{1,0:T(8,128)(2,1)S(1)}, bf16[256,512]{1,0:T(8,128)(2,1)S(1)}, u32[]{:S(2)}, u32[]{:S(2)}) collective-permute-start(bf16[256,512]{1,0:T(8,128)(2,1)S(1)} %fusion.42), channel_id=1, source_target_pairs={{0,2},{4,0},{8,4},{12,8},{14,12},{10,14},{6,10},{2,6},{1,3},{5,1},... | collective-permute-start | bytes 786440 | tf_op jit(solution)/shard_map/ppermute | solution.py:32
  136.9 14.4 %collective-permute-start.33 = (bf16[256,512]{1,0:T(8,128)(2,1)S(1)}, bf16[256,512]{1,0:T(8,128)(2,1)S(1)}, u32[]{:S(2)}, u32[]{:S(2)}) collective-permute-start(bf16[256,512]{1,0:T(8,128)(2,1)S(1)} %fusion.39), channel_id=1, source_target_pairs={{0,4},{4,8},{8,12},{12,14},{14,10},{10,6},{6,2},{2,0},{1,5},{5,9},... | collective-permute-start | bytes 786440 | tf_op jit(solution)/shard_map/ppermute | solution.py:32
  138.8 9.9 %collective-permute-start.26 = (bf16[256,512]{1,0:T(8,128)(2,1)S(1)}, bf16[256,512]{1,0:T(8,128)(2,1)S(1)}, u32[]{:S(2)}, u32[]{:S(2)}) collective-permute-start(bf16[256,512]{1,0:T(8,128)(2,1)S(1)} %fusion.36), channel_id=1, source_target_pairs={{0,4},{4,8},{8,12},{12,14},{14,10},{10,6},{6,2},{2,0},{1,5},{5,9},... | collective-permute-start | bytes 786440 | tf_op jit(solution)/shard_map/ppermute | solution.py:32
  142.8 8.5 %collective-permute-start.37 = (bf16[256,512]{1,0:T(8,128)(2,1)S(1)}, bf16[256,512]{1,0:T(8,128)(2,1)S(1)}, u32[]{:S(2)}, u32[]{:S(2)}) collective-permute-start(bf16[256,512]{1,0:T(8,128)(2,1)S(1)} %fusion.41), channel_id=1, source_target_pairs={{0,2},{4,0},{8,4},{12,8},{14,12},{10,14},{6,10},{2,6},{1,3},{5,1},... | collective-permute-start | bytes 786440 | tf_op jit(solution)/shard_map/ppermute | solution.py:32
  144.4 9.5 %collective-permute-start.30 = (bf16[256,512]{1,0:T(8,128)(2,1)}, bf16[256,512]{1,0:T(8,128)(2,1)}, u32[]{:S(2)}, u32[]{:S(2)}) collective-permute-start(bf16[256,512]{1,0:T(8,128)(2,1)} %fusion.30), channel_id=1, source_target_pairs={{0,2},{4,0},{8,4},{12,8},{14,12},{10,14},{6,10},{2,6},{1,3},{5,1},... | collective-permute-start | bytes 786440 | tf_op jit(solution)/shard_map/ppermute | solution.py:32
  149.7 6.7 %collective-permute-start.27 = (bf16[256,512]{1,0:T(8,128)(2,1)}, bf16[256,512]{1,0:T(8,128)(2,1)}, u32[]{:S(2)}, u32[]{:S(2)}) collective-permute-start(bf16[256,512]{1,0:T(8,128)(2,1)} %fusion.33), channel_id=1, source_target_pairs={{0,4},{4,8},{8,12},{12,14},{14,10},{10,6},{6,2},{2,0},{1,5},{5,9},... | collective-permute-start | bytes 786440 | tf_op jit(solution)/shard_map/ppermute | solution.py:32
  (27 other events, 166.3 us)

commit v10 on v8

--- a/solution.py
+++ b/solution.py
@@ -1,16 +1,11 @@
-import functools
-
 import jax
 import jax.numpy as jnp
 from jax import lax
-from jax.experimental import pallas as pl
-from jax.experimental.pallas import tpu as pltpu
 from jax.sharding import Mesh, PartitionSpec as P
 
 sharpness = 20.0
 cores = 2
 longest_ring = 16
-vmem_limit = 20 << 20
 
 
 def ring_order(chips):
@@ -40,7 +35,7 @@
     return lax.ppermute(block, "core", [(0, 1), (1, 0)])
 
 
-def slab_blocks(stored, chips, core):
+def slab_blocks(stored, chips):
     order = ring_order(chips)
     kept = []
     for j in range(chips // cores):
@@ -50,9 +45,7 @@
                 source = order[(i + j + c * (chips // cores)) % chips]
                 pairs.append(((chips + source) * cores + c, chip * cores + c))
         kept.append(lax.ppermute(stored, ("grp", "chip", "core"), pairs))
-    kept = jnp.concatenate(kept)
-    other = from_sibling(kept)
-    return [jnp.where(core == 0, kept, other), jnp.where(core == 0, other, kept)]
+    return kept
 
 
 def in_core_order(mine, other, core, axis=0):
@@ -63,37 +56,10 @@
     )
 
 
-def normalize_kernel(chunk, states_ref, gain_ref, *out_refs):
-    def run(out_ref):
-        @pl.loop(0, states_ref.shape[1] // chunk)
-        def _(i):
-            at = pl.ds(pl.multiple_of(i * chunk, chunk), chunk)
-            wide = states_ref[0, at, :].astype(jnp.float32)
-            mean_square = jnp.mean(wide * wide, axis=-1, keepdims=True)
-            wide = wide * lax.rsqrt(mean_square + 1e-05) * gain_ref[...]
-            out_ref[at, :] = wide.astype(jnp.bfloat16)
-
-    for part, out_ref in enumerate(out_refs):
-        pl.when(pl.program_id(0) == part)(functools.partial(run, out_ref))
-
-
 def normalize(states, gain):
-    seqs, length, width = states.shape
-    tokens = seqs * length
-    return pl.pallas_call(
-        functools.partial(normalize_kernel, 16),
-        grid=(seqs,),
-        in_specs=[
-            pl.BlockSpec((1, length, width), lambda i: (i, 0, 0)),
-            pl.BlockSpec((1, width), lambda i: (0, 0)),
-        ],
-        out_specs=[pl.BlockSpec((length, width), lambda i: (0, 0))] * seqs,
-        out_shape=[jax.ShapeDtypeStruct((length, width), jnp.bfloat16)] * seqs,
-        compiler_params=pltpu.CompilerParams(vmem_limit_bytes=vmem_limit),
-        cost_estimate=pl.CostEstimate(
-            flops=6 * tokens * width, bytes_accessed=4 * tokens * width, transcendentals=tokens
-        ),
-    )(states, gain[None])
+    states_wide = states.astype(jnp.float32)
+    mean_square = jnp.mean(states_wide * states_wide, axis=-1, keepdims=True)
+    return (states_wide * lax.rsqrt(mean_square + 1e-05) * gain).astype(jnp.bfloat16)
 
 
 def shards(token_states, token_ids, master, gain, cand_ids, slab_owner):
@@ -114,10 +80,13 @@
     given = given.astype(jnp.bfloat16)
     sibling = from_sibling(given)
 
-    normed = list(normalize(after(sibling, states), gain))
-    normed = jnp.concatenate(normed + [from_sibling(part) for part in normed])
     first_sent = along_ring(own, 1)
+    other_states = from_sibling(states)
+    states = after(first_sent, states)
     ids, cand_ids = token_ids[0], after(first_sent, cand_ids)
+    slab_owner = after(first_sent, slab_owner)
+    normed = jnp.concatenate([normalize(states, gain), normalize(other_states, gain)])
+    normed = normed.reshape(seqs * length, width)
     ids = jnp.concatenate([ids, cand_ids], axis=1)
     ids = jnp.concatenate([ids, from_sibling(ids)])
     lengths = jnp.sum((ids[:, :length] != 0).astype(jnp.int32), axis=1)
@@ -135,7 +104,7 @@
     if chips <= longest_ring:
         moving = {(i, by): block for by in (1, -1) for i, block in enumerate((own, sibling))}
         total = product(0, parts[0], own) + product(0, parts[1], sibling)
-        first = None
+        sums = {}
         for step in range(1, chips // 2 + 1):
             last = step == chips // 2
             sent = [(0, 1), (0, -1), (1, 1), (1, -1)]
@@ -143,20 +112,23 @@
                 if (step, i, by) == (1, 0, 1):
                     moving[i, by] = first_sent
                 else:
-                    if last and i == 1 and first is not None:
-                        moving[i, by] = after(first, moving[i, by])
+                    if last and i == 1 and step > 2:
+                        moving[i, by] = after(sums[1], moving[i, by])
                     moving[i, by] = along_ring(moving[i, by], by)
                 total = total + product(-by * step, parts[i], moving[i, by])
-            first = total if first is None else first
-        active = jnp.tanh(total).reshape(seqs, length, half)
+            sums[step] = total
+            if step == 1:
+                weights = after(moving[1, 1], weights)
     else:
         both = in_core_order(own, sibling, core)
         gathered = lax.all_gather(both, "chip", axis=0, tiled=True)
-        hidden = jnp.dot(normed, gathered, preferred_element_type=jnp.float32)
-        active = jnp.tanh(hidden).reshape(seqs, length, half)
-
+        total = jnp.dot(normed, gathered, preferred_element_type=jnp.float32)
+
+    copied = lax.ppermute(weights.astype(jnp.bfloat16), "grp", [(0, 1)])
+    active = jnp.tanh(total).reshape(seqs, length, half)
     there = jnp.arange(length)[None, :, None] < lengths[:, None, None]
     pooled = jnp.sum(jnp.where(there, active, 0.0), axis=1) / counts[:, None]
+    pooled, copied = lax.optimization_barrier((pooled, copied))
     pooled_other = from_sibling(pooled)
     pooled_other = jnp.concatenate([pooled_other[seq_dev:], pooled_other[:seq_dev]])
     whole = in_core_order(pooled, pooled_other, core, axis=1)
@@ -166,14 +138,9 @@
     stored = unit.astype(jnp.bfloat16)
     stored = in_core_order(stored[:seq_dev], stored[seq_dev:], core)
 
-    cut = {}
-    if chips <= longest_ring:
-        steps = [(chips // 2, 0, 1), (chips // 2, 1, -1), (chips // 2 - 1, 1, 1)]
-        steps += [(chips // 2 - 1, 0, -1)]
-        cut = {(by * step, i): columns(by * step, parts[i]) for step, i, by in steps}
-        stored, *cuts = lax.optimization_barrier([stored, *cut.values()])
-        cut = dict(zip(cut, cuts))
-    slab = jnp.concatenate(slab_blocks(stored, chips, core))
+    kept = slab_blocks(stored, chips)
+    kept = jnp.concatenate(kept)
+    slab = in_core_order(kept, from_sibling(kept), core)
     slab_rows = slab.shape[0]
     earlier = jnp.arange(slab_rows)[:, None] < jnp.arange(slab_rows)[None, :]
     same = slab_owner[:, None] == slab_owner[None, :]
@@ -201,15 +168,13 @@
     inner = jnp.sum(whole * unit_grad, axis=-1, keepdims=True)
     pooled_grad = scale * unit_grad - whole * (scale * scale * scale) * inner / embedding
     pooled_grad = lax.dynamic_slice(pooled_grad, (0, core * half), (seqs, half))
-    slope = jnp.where(there, 1.0 - active * active, 0.0)
-    delta = (pooled_grad / counts[:, None])[:, None, :] * slope
+    delta = (pooled_grad / counts[:, None])[:, None, :] * (1.0 - active * active)
+    delta = jnp.where(there, delta, 0.0)
     delta = delta.astype(jnp.bfloat16).reshape(seqs * length, half)
-    delta, weights = lax.optimization_barrier((delta, weights))
-    copied = lax.ppermute(weights.astype(jnp.bfloat16), "grp", [(0, 1)])
-
-    def term(offset, i, delta):
+
+    def term(offset, part, delta):
         return lax.dot_general(
-            cut[offset, i] if (offset, i) in cut else columns(offset, parts[i]),
+            columns(offset, part),
             delta,
             (((0,), (0,)), ((), ())),
             preferred_element_type=jnp.float32,
@@ -222,7 +187,7 @@
             for i, by in ((0, 1), (1, -1), (1, 1), (0, -1)):
                 if step == chips // 2 and (i, by) not in ((0, 1), (1, -1)):
                     continue
-                total = term(by * step, i, delta)
+                total = term(by * step, parts[i], delta)
                 if (i, by) in arrived:
                     total = total + arrived[i, by].astype(jnp.float32)
                 if step == 1 and i == 0:
@@ -230,10 +195,11 @@
                 arrived[i, by] = along_ring(total.astype(jnp.bfloat16), by)
             if step == chips // 2:
                 late = after(arrived[0, 1], delta)
+        owns = [term(0, parts[i], late) for i in range(2)]
+        arrived[1, 1] = after(owns, arrived[1, 1])
+        arrived[0, -1] = after(owns, arrived[0, -1])
         mine, other = [
-            term(0, i, late)
-            + arrived[i, 1].astype(jnp.float32)
-            + arrived[i, -1].astype(jnp.float32)
+            owns[i] + arrived[i, 1].astype(jnp.float32) + arrived[i, -1].astype(jnp.float32)
             for i in range(2)
         ]
     else:

time: 149 us -> 147 us (0.987)
  other arithmetic: 4.4 us -> 19.2 us
  local copies, waits for them, and re-layouts: 16.8 us -> 4.05 us
  waiting for transfers between devices: 38.6 us -> 50.2 us
  matrix products: 39.6 us -> 30.8 us
  Pallas kernels: 3.61 us -> 0 us
  starting transfers between devices: 43.5 us -> 41 us
    ppermute x28, waiting for transfers between devices: 29.6 us -> 41.5 us  [along_ring(): return lax.ppermute(block, 'chip', pairs)]
    unnamed x26 -> x13, local copies, waits for them, and re-layouts: 10.6 us -> 0.71 us
    dot_general x16, matrix products: 18.1 us -> 9.78 us  [term(): lax.dot_general(columns(offset, part), delta, (((0,), (0,)), ((), ())), p...]
    reduce_sum x0 -> x2, other arithmetic: none -> 5.16 us  [normalize(): mean_square = jnp.mean(states_wide * states_wide, axis=-1, keepdims=True)]
    ppermute x28, starting transfers between devices: 35.3 us -> 30.5 us  [along_ring(): return lax.ppermute(block, 'chip', pairs)]
    convert_element_type x0 -> x1, other arithmetic: none -> 4.68 us  [normalize(): (states_wide * lax.rsqrt(mean_square + 1e-05) * gain).astype(jnp.bfloat16)]
    pallas_call x1 -> x0, Pallas kernels: 3.61 us -> none  [normalize(): pl.pallas_call(functools.partial(normalize_kernel, 16), grid=(seqs,), in_...]
    concatenate x1 -> x2, other arithmetic: 0.03 us -> 2.46 us  [the longest x1 2.43 us: shards(): jnp.concatenate([normalize(states, gain), normalize(other_states, gain)])]
  transfers between devices with their start and end apart: 41 -> 39, of which waited for: 20 -> 18; matrix products, arithmetic and copies ran while one was open for 36% -> 32% of each run, Pallas kernels for 2% -> 0%
where the time goes in v10:
time: 147 us; the launch traced here: 146 us
  waiting for transfers between devices  50.2 us (34%)
  starting transfers between devices  41 us (28%)
  matrix products  30.8 us (21%)
  other arithmetic  19.2 us (13%)
  local copies, waits for them, and re-layouts  4.05 us (3%)
    ppermute x28, waiting for transfers between devices, along_ring(): return lax.ppermute(block, 'chip', pairs)  41.5 us
    ppermute x28, starting transfers between devices, along_ring(): return lax.ppermute(block, 'chip', pairs)  30.5 us
    dot_general x16, matrix products, product(): jnp.dot(columns(offset, part), block, preferred_element_type=jnp.float32)  20.3 us
    dot_general x16, matrix products, term(): lax.dot_general(columns(offset, part), delta, (((0,), (0,)), ((), ())), p...  9.78 us
    ppermute x4, waiting for transfers between devices, slab_blocks(): kept.append(lax.ppermute(stored, ('grp', 'chip', 'core'), pairs))  6.47 us
    ppermute x4, starting transfers between devices, slab_blocks(): kept.append(lax.ppermute(stored, ('grp', 'chip', 'core'), pairs))  5.34 us
    reduce_sum x2, other arithmetic, normalize(): mean_square = jnp.mean(states_wide * states_wide, axis=-1, keepdims=True)  5.16 us
    convert_element_type x1, other arithmetic, normalize(): (states_wide * lax.rsqrt(mean_square + 1e-05) * gain).astype(jnp.bfloat16)  4.68 us
  transfers between devices with their start and end apart: 39, of which 18 were waited for; matrix products, arithmetic and copies ran while one was open for 32% of the time, Pallas kernels for 0%

profile of v10, /device:TPU:0, one launch (start us, length us, event | category | flops | bytes accessed | tf_op | source)
XLA Modules:
  0.0 145.7 jit_solution(7032542689378854104)
XLA Ops:
  1.7 2.6 %collective-permute-start = (bf16[256,512]{1,0:T(8,128)(2,1)S(1)}, bf16[256,512]{1,0:T(8,128)(2,1)}, u32[]{:S(2)}, u32[]{:S(2)}) collective-permute-start(bf16[256,512]{1,0:T(8,128)(2,1)S(1)} %get-tuple-element.33), channel_id=1, source_target_pairs={{0,4},{4,8},{8,12},{12,14},{14,10},{10,6},{6,2},{2,0},{1,5},{5,9},... | collective-permute-start | bytes 786440 | tf_op jit(solution)/shard_map/ppermute | solution.py:27
  5.3 6.1 %collective-permute-done = bf16[256,512]{1,0:T(8,128)(2,1)} collective-permute-done((bf16[256,512]{1,0:T(8,128)(2,1)S(1)}, bf16[256,512]{1,0:T(8,128)(2,1)}, u32[]{:S(2)}, u32[]{:S(2)}) %collective-permute-start) | collective-permute-done | bytes 262176 | tf_op jit(solution)/shard_map/ppermute | solution.py:27
  12.1 2.6 %fusion = f32[3,128]{1,0:T(4,128)S(1)} fusion(bf16[3,128,4096]{2,1,0:T(8,128)(2,1)} %bitcast.87), kind=kLoop, calls=%fused_computation.6 | loop fusion | flops 4718208 | bytes 3147264 | tf_op jit(solution)/shard_map/reduce_sum | solution.py:61
  14.8 1.8 %collective-permute-start.5 = (bf16[256,512]{1,0:T(8,128)(2,1)}, bf16[256,512]{1,0:T(8,128)(2,1)}, u32[]{:S(2)}, u32[]{:S(2)}) collective-permute-start(bf16[256,512]{1,0:T(8,128)(2,1)} %collective-permute-done.3), channel_id=1, source_target_pairs={{0,4},{4,8},{8,12},{12,14},{14,10},{10,6},{6,2},{2,0},{1,5},{5,9},... | collective-permute-start | bytes 786440 | tf_op jit(solution)/shard_map/ppermute | solution.py:27
  16.9 1.8 %collective-permute-start.7 = (bf16[256,512]{1,0:T(8,128)(2,1)}, bf16[256,512]{1,0:T(8,128)(2,1)}, u32[]{:S(2)}, u32[]{:S(2)}) collective-permute-start(bf16[256,512]{1,0:T(8,128)(2,1)} %collective-permute-done), channel_id=1, source_target_pairs={{0,4},{4,8},{8,12},{12,14},{14,10},{10,6},{6,2},{2,0},{1,5},{5,9},... | collective-permute-start | bytes 786440 | tf_op jit(solution)/shard_map/ppermute | solution.py:27
  20.0 6.1 %collective-permute-done.6 = bf16[256,512]{1,0:T(8,128)(2,1)} collective-permute-done((bf16[256,512]{1,0:T(8,128)(2,1)}, bf16[256,512]{1,0:T(8,128)(2,1)}, u32[]{:S(2)}, u32[]{:S(2)}) %collective-permute-start.6) | collective-permute-done | bytes 262176 | tf_op jit(solution)/shard_map/ppermute | solution.py:27
  26.3 1.8 %collective-permute-start.9 = (bf16[256,512]{1,0:T(8,128)(2,1)}, bf16[256,512]{1,0:T(8,128)(2,1)}, u32[]{:S(2)}, u32[]{:S(2)}) collective-permute-start(bf16[256,512]{1,0:T(8,128)(2,1)} %collective-permute-done.5), channel_id=1, source_target_pairs={{0,4},{4,8},{8,12},{12,14},{14,10},{10,6},{6,2},{2,0},{1,5},{5,9},... | collective-permute-start | bytes 786440 | tf_op jit(solution)/shard_map/ppermute | solution.py:27
  28.1 1.8 %collective-permute-done.7 = bf16[256,512]{1,0:T(8,128)(2,1)} collective-permute-done((bf16[256,512]{1,0:T(8,128)(2,1)}, bf16[256,512]{1,0:T(8,128)(2,1)}, u32[]{:S(2)}, u32[]{:S(2)}) %collective-permute-start.7) | collective-permute-done | bytes 262176 | tf_op jit(solution)/shard_map/ppermute | solution.py:27
  29.9 1.8 %collective-permute-start.11 = (bf16[256,512]{1,0:T(8,128)(2,1)}, bf16[256,512]{1,0:T(8,128)(2,1)}, u32[]{:S(2)}, u32[]{:S(2)}) collective-permute-start(bf16[256,512]{1,0:T(8,128)(2,1)} %collective-permute-done.7), channel_id=1, source_target_pairs={{0,4},{4,8},{8,12},{12,14},{14,10},{10,6},{6,2},{2,0},{1,5},{5,9},... | collective-permute-start | bytes 786440 | tf_op jit(solution)/shard_map/ppermute | solution.py:27
  31.9 2.1 %convert_element_type.156 = bf16[256,1024]{1,0:T(8,128)(2,1)} convert(f32[256,1024]{1,0:T(8,128)} %bitcast.89) | non-fusion elementwise | flops 262144 | bytes 1572864 | tf_op jit(solution)/shard_map/convert_element_type | solution.py:127
  34.0 4.2 %collective-permute-start.17 = (bf16[256,1024]{1,0:T(8,128)(2,1)}, bf16[256,1024]{1,0:T(8,128)(2,1)}, u32[]{:S(2)}, u32[]{:S(2)}) collective-permute-start(bf16[256,1024]{1,0:T(8,128)(2,1)} %convert_element_type.156), channel_id=1, source_target_pairs={{0,16},{1,17},{2,18},{3,19},{4,20},{5,21},{6,22},{7,23},{8,24},{9,... | collective-permute-start | bytes 1572872 | tf_op jit(solution)/shard_map/ppermute | solution.py:127
  40.7 1.8 %collective-permute-start.13 = (bf16[256,512]{1,0:T(8,128)(2,1)}, bf16[256,512]{1,0:T(8,128)(2,1)}, u32[]{:S(2)}, u32[]{:S(2)}) collective-permute-start(bf16[256,512]{1,0:T(8,128)(2,1)} %collective-permute-done.9), channel_id=1, source_target_pairs={{0,4},{4,8},{8,12},{12,14},{14,10},{10,6},{6,2},{2,0},{1,5},{5,9},... | collective-permute-start | bytes 786440 | tf_op jit(solution)/shard_map/ppermute | solution.py:27
  42.5 1.6 %collective-permute-start.15 = (bf16[256,512]{1,0:T(8,128)(2,1)}, bf16[256,512]{1,0:T(8,128)(2,1)}, u32[]{:S(2)}, u32[]{:S(2)}) collective-permute-start(bf16[256,512]{1,0:T(8,128)(2,1)} %collective-permute-done.11), channel_id=1, source_target_pairs={{0,4},{4,8},{8,12},{12,14},{14,10},{10,6},{6,2},{2,0},{1,5},{5,9},... | collective-permute-start | bytes 786440 | tf_op jit(solution)/shard_map/ppermute | solution.py:27
  44.1 2.6 %fusion.3 = f32[3,128]{1,0:T(4,128)S(1)} fusion(bf16[3,128,4096]{2,1,0:T(8,128)(2,1)} %collective-permute-done.1), kind=kLoop, calls=%fused_computation.9 | loop fusion | flops 4718208 | bytes 3147264 | tf_op jit(solution)/shard_map/reduce_sum | solution.py:61
  46.7 4.7 %fusion.2 = (bf16[3,128,4096]{2,1,0:T(8,128)(2,1)S(1)}, bf16[3,128,4096]{2,1,0:T(8,128)(2,1)}) fusion(bf16[3,128,4096]{2,1,0:T(8,128)(2,1)S(1)} %bitcast.88, f32[4096]{0:T(1024)S(1)} %copy-done.3, f32[3,128]{1,0:T(4,128)S(1)} %add_rsqrt_fusion.1, f32[3,128]{1,0:T(4,128)S(1)} %add_rsqrt_fusion, bf16[3,128,4096]{2,1,0:T(8,128)(2,1)} %collective-permute-done.1), kind=kLoop, calls=%fused_computation.8 | loop fusion | flops 12582912 | bytes 12602368 | tf_op jit(solution)/shard_map/convert_element_type | solution.py:62
  51.4 2.4 %pad_maximum_fusion = bf16[6,128,4096]{2,1,0:T(8,128)(2,1)S(1)} fusion(bf16[3,128,4096]{2,1,0:T(8,128)(2,1)} %get-tuple-element.40, bf16[3,128,4096]{2,1,0:T(8,128)(2,1)S(1)} %get-tuple-element.39), kind=kLoop, calls=%fused_computation.12 | loop fusion | flops 3145728 | bytes 12582912 | tf_op jit(solution)/shard_map/concatenate | solution.py:88
  59.9 1.6 %add_add_fusion = f32[768,512]{1,0:T(8,128)S(1)} fusion(f32[768,512]{1,0:T(8,128)S(1)} %fusion.70, f32[768,512]{1,0:T(8,128)S(1)} %fusion.76, f32[768,512]{1,0:T(8,128)S(1)} %fusion.82, f32[768,512]{1,0:T(8,128)S(1)} %fusion.92, f32[768,512]{1,0:T(8,128)S(1)} %fusion.88, bf16[256,512]{1,0:T(8,128)(2,1)} %collective-permute-done.6, ...), kind=kOutput, calls=%fused_computation.18 | convolution fusion | flops 203292672 | bytes 10092548 | tf_op jit(solution)/shard_map/dot_general | solution.py:101
  73.0 1.8 %add_tanh_fusion = f32[768,512]{1,0:T(8,128)S(1)} fusion(f32[768,512]{1,0:T(8,128)S(1)} %fusion.11, f32[768,512]{1,0:T(8,128)S(1)} %fusion.19, f32[768,512]{1,0:T(8,128)S(1)} %fusion.23, f32[768,512]{1,0:T(8,128)S(1)} %fusion.29, f32[768,512]{1,0:T(8,128)S(1)} %fusion.34, f32[768,512]{1,0:T(8,128)S(1)} %fusion.38, f32[768,512]{1,0:T(8,128)S(1)} %fusion.44, ...), kind=kOutput, calls=%fused_computation.17 | convolution fusion | flops 205258752 | bytes 17956868 | tf_op jit(solution)/shard_map/dot_general | solution.py:101
  82.7 1.9 %collective-permute-done.20 = bf16[6,1024]{1,0:T(8,128)(2,1)S(1)} collective-permute-done((bf16[6,1024]{1,0:T(8,128)(2,1)S(1)}, bf16[6,1024]{1,0:T(8,128)(2,1)S(1)}, u32[]{:S(2)}, u32[]{:S(2)}) %collective-permute-start.20) | collective-permute-done | bytes 12320 | tf_op jit(solution)/shard_map/ppermute | solution.py:47
  84.6 2.3 %collective-permute-done.21 = bf16[6,1024]{1,0:T(8,128)(2,1)S(1)} collective-permute-done((bf16[6,1024]{1,0:T(8,128)(2,1)S(1)}, bf16[6,1024]{1,0:T(8,128)(2,1)S(1)}, u32[]{:S(2)}, u32[]{:S(2)}) %collective-permute-start.21) | collective-permute-done | bytes 12320 | tf_op jit(solution)/shard_map/ppermute | solution.py:47
  86.9 2.3 %collective-permute-done.22 = bf16[6,1024]{1,0:T(8,128)(2,1)S(1)} collective-permute-done((bf16[6,1024]{1,0:T(8,128)(2,1)S(1)}, bf16[6,1024]{1,0:T(8,128)(2,1)S(1)}, u32[]{:S(2)}, u32[]{:S(2)}) %collective-permute-start.22) | collective-permute-done | bytes 12320 | tf_op jit(solution)/shard_map/ppermute | solution.py:47
  92.0 1.5 %convolution_convert_fusion.2 = bf16[256,512]{1,0:T(8,128)(2,1)S(1)} fusion(bf16[768,512]{1,0:T(8,128)(2,1)S(1)} %fusion.7, bf16[768,4096]{1,0:T(8,128)(2,1)} %bitcast.69, s32[]{:T(128)S(6)} %select_n.243), kind=kOutput, calls=%fused_computation.21 | convolution fusion | flops 201457664 | bytes 1441796 | tf_op jit(solution)/shard_map/dot_general | solution.py:176
  99.6 1.5 %collective-permute-start.31 = (bf16[256,512]{1,0:T(8,128)(2,1)S(1)}, bf16[256,512]{1,0:T(8,128)(2,1)S(1)}, u32[]{:S(2)}, u32[]{:S(2)}) collective-permute-start(bf16[256,512]{1,0:T(8,128)(2,1)S(1)} %convolution_convert_fusion.1), channel_id=1, source_target_pairs={{0,4},{4,8},{8,12},{12,14},{14,10},{10,6},{6,2},{2,0},{1,5},{5,9},... | collective-permute-start | bytes 786440 | tf_op jit(solution)/shard_map/ppermute | solution.py:27
  101.1 3.2 %collective-permute-done.24 = bf16[256,512]{1,0:T(8,128)(2,1)S(1)} collective-permute-done((bf16[256,512]{1,0:T(8,128)(2,1)S(1)}, bf16[256,512]{1,0:T(8,128)(2,1)S(1)}, u32[]{:S(2)}, u32[]{:S(2)}) %collective-permute-start.24) | collective-permute-done | bytes 262176 | tf_op jit(solution)/shard_map/ppermute | solution.py:27
  104.7 2.5 %collective-permute-done.28 = bf16[256,512]{1,0:T(8,128)(2,1)S(1)} collective-permute-done((bf16[256,512]{1,0:T(8,128)(2,1)S(1)}, bf16[256,512]{1,0:T(8,128)(2,1)S(1)}, u32[]{:S(2)}, u32[]{:S(2)}) %collective-permute-start.28) | collective-permute-done | bytes 262176 | tf_op jit(solution)/shard_map/ppermute | solution.py:27
  108.7 4.2 %collective-permute-done.34 = bf16[256,512]{1,0:T(8,128)(2,1)S(1)} collective-permute-done((bf16[256,512]{1,0:T(8,128)(2,1)S(1)}, bf16[256,512]{1,0:T(8,128)(2,1)S(1)}, u32[]{:S(2)}, u32[]{:S(2)}) %collective-permute-start.34) | collective-permute-done | bytes 262176 | tf_op jit(solution)/shard_map/ppermute | solution.py:27
  114.3 1.5 %collective-permute-start.25 = (bf16[256,512]{1,0:T(8,128)(2,1)S(1)}, bf16[256,512]{1,0:T(8,128)(2,1)S(1)}, u32[]{:S(2)}, u32[]{:S(2)}) collective-permute-start(bf16[256,512]{1,0:T(8,128)(2,1)S(1)} %add_convert_fusion.7), channel_id=1, source_target_pairs={{0,4},{4,8},{8,12},{12,14},{14,10},{10,6},{6,2},{2,0},{1,5},{5,9},... | collective-permute-start | bytes 786440 | tf_op jit(solution)/shard_map/ppermute | solution.py:27
  117.3 5.7 %collective-permute-done.35 = bf16[256,512]{1,0:T(8,128)(2,1)S(1)} collective-permute-done((bf16[256,512]{1,0:T(8,128)(2,1)S(1)}, bf16[256,512]{1,0:T(8,128)(2,1)S(1)}, u32[]{:S(2)}, u32[]{:S(2)}) %collective-permute-start.35) | collective-permute-done | bytes 262176 | tf_op jit(solution)/shard_map/ppermute | solution.py:27
  127.8 2.9 %collective-permute-done.36 = bf16[256,512]{1,0:T(8,128)(2,1)S(1)} collective-permute-done((bf16[256,512]{1,0:T(8,128)(2,1)S(1)}, bf16[256,512]{1,0:T(8,128)(2,1)S(1)}, u32[]{:S(2)}, u32[]{:S(2)}) %collective-permute-start.36) | collective-permute-done | bytes 262176 | tf_op jit(solution)/shard_map/ppermute | solution.py:27
  135.7 3.7 %collective-permute-done.33 = bf16[256,512]{1,0:T(8,128)(2,1)S(1)} collective-permute-done((bf16[256,512]{1,0:T(8,128)(2,1)S(1)}, bf16[256,512]{1,0:T(8,128)(2,1)S(1)}, u32[]{:S(2)}, u32[]{:S(2)}) %collective-permute-start.33) | collective-permute-done | bytes 262176 | tf_op jit(solution)/shard_map/ppermute | solution.py:27
  140.6 2.6 %collective-permute-done.30 = bf16[256,512]{1,0:T(8,128)(2,1)S(1)} collective-permute-done((bf16[256,512]{1,0:T(8,128)(2,1)S(1)}, bf16[256,512]{1,0:T(8,128)(2,1)S(1)}, u32[]{:S(2)}, u32[]{:S(2)}) %collective-permute-start.30) | collective-permute-done | bytes 262176 | tf_op jit(solution)/shard_map/ppermute | solution.py:27
  143.5 2.2 %select_bitcast_fusion = f32[1,256,1024]{2,1,0:T(8,128)} fusion(bf16[256,1024]{1,0:T(8,128)(2,1)} %collective-permute-done.17, f32[256,512]{1,0:T(8,128)S(1)} %convert_add_fusion.1, f32[256,512]{1,0:T(8,128)S(1)} %collective-permute-done.38, f32[256]{0:T(256)S(1)} %add_rsqrt_fusion.2, pred[]{:T(512)S(6)} %eq.65, pred[]{:T(512)S(6)} %eq.64), kind=kLoop, calls=%fused_computation.27 | loop fusion | flops 1572864 | bytes 2622466 | tf_op jit(solution)/shard_map/broadcast_in_dim | solution.py:216
  (136 shorter events, 57.9 us)
Async XLA Ops:
  0.0 42.5 %collective-permute-start.1 = (bf16[3,128,4096]{2,1,0:T(8,128)(2,1)}, bf16[3,128,4096]{2,1,0:T(8,128)(2,1)}, u32[]{:S(2)}, u32[]{:S(2)}) collective-permute-start(bf16[3,128,4096]{2,1,0:T(8,128)(2,1)} %bitcast.86), channel_id=1, source_target_pairs={{0,1},{1,0},{2,3},{3,2},{4,5},{5,4},{6,7},{7,6},{8,9},{9,8},{10,11... | collective-permute-start | bytes 9437192 | tf_op jit(solution)/shard_map/ppermute | solution.py:35
  1.7 9.7 %collective-permute-start = (bf16[256,512]{1,0:T(8,128)(2,1)S(1)}, bf16[256,512]{1,0:T(8,128)(2,1)}, u32[]{:S(2)}, u32[]{:S(2)}) collective-permute-start(bf16[256,512]{1,0:T(8,128)(2,1)S(1)} %get-tuple-element.33), channel_id=1, source_target_pairs={{0,4},{4,8},{8,12},{12,14},{14,10},{10,6},{6,2},{2,0},{1,5},{5,9},... | collective-permute-start | bytes 786440 | tf_op jit(solution)/shard_map/ppermute | solution.py:27
  4.4 12.5 %collective-permute-start.4 = (bf16[256,512]{1,0:T(8,128)(2,1)S(1)}, bf16[256,512]{1,0:T(8,128)(2,1)}, u32[]{:S(2)}, u32[]{:S(2)}) collective-permute-start(bf16[256,512]{1,0:T(8,128)(2,1)S(1)} %get-tuple-element.33), channel_id=1, source_target_pairs={{0,2},{4,0},{8,4},{12,8},{14,12},{10,14},{6,10},{2,6},{1,3},{5,1},... | collective-permute-start | bytes 786440 | tf_op jit(solution)/shard_map/ppermute | solution.py:27
  4.4 10.4 %collective-permute-start.3 = (bf16[256,512]{1,0:T(8,128)(2,1)S(1)}, bf16[256,512]{1,0:T(8,128)(2,1)}, u32[]{:S(2)}, u32[]{:S(2)}) collective-permute-start(bf16[256,512]{1,0:T(8,128)(2,1)S(1)} %get-tuple-element.34), channel_id=1, source_target_pairs={{0,1},{1,0},{2,3},{3,2},{4,5},{5,4},{6,7},{7,6},{8,9},{9,8},{10,11... | collective-permute-start | bytes 786440 | tf_op jit(solution)/shard_map/ppermute | solution.py:35
  14.8 11.5 %collective-permute-start.5 = (bf16[256,512]{1,0:T(8,128)(2,1)}, bf16[256,512]{1,0:T(8,128)(2,1)}, u32[]{:S(2)}, u32[]{:S(2)}) collective-permute-start(bf16[256,512]{1,0:T(8,128)(2,1)} %collective-permute-done.3), channel_id=1, source_target_pairs={{0,4},{4,8},{8,12},{12,14},{14,10},{10,6},{6,2},{2,0},{1,5},{5,9},... | collective-permute-start | bytes 786440 | tf_op jit(solution)/shard_map/ppermute | solution.py:27
  16.7 9.5 %collective-permute-start.6 = (bf16[256,512]{1,0:T(8,128)(2,1)}, bf16[256,512]{1,0:T(8,128)(2,1)}, u32[]{:S(2)}, u32[]{:S(2)}) collective-permute-start(bf16[256,512]{1,0:T(8,128)(2,1)} %collective-permute-done.3), channel_id=1, source_target_pairs={{0,2},{4,0},{8,4},{12,8},{14,12},{10,14},{6,10},{2,6},{1,3},{5,1},... | collective-permute-start | bytes 786440 | tf_op jit(solution)/shard_map/ppermute | solution.py:27
  16.9 13.0 %collective-permute-start.7 = (bf16[256,512]{1,0:T(8,128)(2,1)}, bf16[256,512]{1,0:T(8,128)(2,1)}, u32[]{:S(2)}, u32[]{:S(2)}) collective-permute-start(bf16[256,512]{1,0:T(8,128)(2,1)} %collective-permute-done), channel_id=1, source_target_pairs={{0,4},{4,8},{8,12},{12,14},{14,10},{10,6},{6,2},{2,0},{1,5},{5,9},... | collective-permute-start | bytes 786440 | tf_op jit(solution)/shard_map/ppermute | solution.py:27
  18.7 15.3 %collective-permute-start.8 = (bf16[256,512]{1,0:T(8,128)(2,1)}, bf16[256,512]{1,0:T(8,128)(2,1)}, u32[]{:S(2)}, u32[]{:S(2)}) collective-permute-start(bf16[256,512]{1,0:T(8,128)(2,1)} %collective-permute-done.4), channel_id=1, source_target_pairs={{0,2},{4,0},{8,4},{12,8},{14,12},{10,14},{6,10},{2,6},{1,3},{5,1},... | collective-permute-start | bytes 786440 | tf_op jit(solution)/shard_map/ppermute | solution.py:27
  26.1 12.1 %collective-permute-start.10 = (bf16[256,512]{1,0:T(8,128)(2,1)}, bf16[256,512]{1,0:T(8,128)(2,1)}, u32[]{:S(2)}, u32[]{:S(2)}) collective-permute-start(bf16[256,512]{1,0:T(8,128)(2,1)} %collective-permute-done.6), channel_id=1, source_target_pairs={{0,2},{4,0},{8,4},{12,8},{14,12},{10,14},{6,10},{2,6},{1,3},{5,1},... | collective-permute-start | bytes 786440 | tf_op jit(solution)/shard_map/ppermute | solution.py:27
  26.3 12.3 %collective-permute-start.9 = (bf16[256,512]{1,0:T(8,128)(2,1)}, bf16[256,512]{1,0:T(8,128)(2,1)}, u32[]{:S(2)}, u32[]{:S(2)}) collective-permute-start(bf16[256,512]{1,0:T(8,128)(2,1)} %collective-permute-done.5), channel_id=1, source_target_pairs={{0,4},{4,8},{8,12},{12,14},{14,10},{10,6},{6,2},{2,0},{1,5},{5,9},... | collective-permute-start | bytes 786440 | tf_op jit(solution)/shard_map/ppermute | solution.py:27
  29.9 10.9 %collective-permute-start.11 = (bf16[256,512]{1,0:T(8,128)(2,1)}, bf16[256,512]{1,0:T(8,128)(2,1)}, u32[]{:S(2)}, u32[]{:S(2)}) collective-permute-start(bf16[256,512]{1,0:T(8,128)(2,1)} %collective-permute-done.7), channel_id=1, source_target_pairs={{0,4},{4,8},{8,12},{12,14},{14,10},{10,6},{6,2},{2,0},{1,5},{5,9},... | collective-permute-start | bytes 786440 | tf_op jit(solution)/shard_map/ppermute | solution.py:27
  34.0 41.1 %collective-permute-start.17 = (bf16[256,1024]{1,0:T(8,128)(2,1)}, bf16[256,1024]{1,0:T(8,128)(2,1)}, u32[]{:S(2)}, u32[]{:S(2)}) collective-permute-start(bf16[256,1024]{1,0:T(8,128)(2,1)} %convert_element_type.156), channel_id=1, source_target_pairs={{0,16},{1,17},{2,18},{3,19},{4,20},{5,21},{6,22},{7,23},{8,24},{9,... | collective-permute-start | bytes 1572872 | tf_op jit(solution)/shard_map/ppermute | solution.py:127
  38.2 33.1 %collective-permute-start.12 = (bf16[256,512]{1,0:T(8,128)(2,1)}, bf16[256,512]{1,0:T(8,128)(2,1)}, u32[]{:S(2)}, u32[]{:S(2)}) collective-permute-start(bf16[256,512]{1,0:T(8,128)(2,1)} %collective-permute-done.8), channel_id=1, source_target_pairs={{0,2},{4,0},{8,4},{12,8},{14,12},{10,14},{6,10},{2,6},{1,3},{5,1},... | collective-permute-start | bytes 786440 | tf_op jit(solution)/shard_map/ppermute | solution.py:27
  38.6 22.9 %collective-permute-start.14 = (bf16[256,512]{1,0:T(8,128)(2,1)}, bf16[256,512]{1,0:T(8,128)(2,1)}, u32[]{:S(2)}, u32[]{:S(2)}) collective-permute-start(bf16[256,512]{1,0:T(8,128)(2,1)} %collective-permute-done.10), channel_id=1, source_target_pairs={{0,2},{4,0},{8,4},{12,8},{14,12},{10,14},{6,10},{2,6},{1,3},{5,1},... | collective-permute-start | bytes 786440 | tf_op jit(solution)/shard_map/ppermute | solution.py:27
  40.7 29.2 %collective-permute-start.13 = (bf16[256,512]{1,0:T(8,128)(2,1)}, bf16[256,512]{1,0:T(8,128)(2,1)}, u32[]{:S(2)}, u32[]{:S(2)}) collective-permute-start(bf16[256,512]{1,0:T(8,128)(2,1)} %collective-permute-done.9), channel_id=1, source_target_pairs={{0,4},{4,8},{8,12},{12,14},{14,10},{10,6},{6,2},{2,0},{1,5},{5,9},... | collective-permute-start | bytes 786440 | tf_op jit(solution)/shard_map/ppermute | solution.py:27
  42.5 30.5 %collective-permute-start.15 = (bf16[256,512]{1,0:T(8,128)(2,1)}, bf16[256,512]{1,0:T(8,128)(2,1)}, u32[]{:S(2)}, u32[]{:S(2)}) collective-permute-start(bf16[256,512]{1,0:T(8,128)(2,1)} %collective-permute-done.11), channel_id=1, source_target_pairs={{0,4},{4,8},{8,12},{12,14},{14,10},{10,6},{6,2},{2,0},{1,5},{5,9},... | collective-permute-start | bytes 786440 | tf_op jit(solution)/shard_map/ppermute | solution.py:27
  61.5 11.1 %collective-permute-start.16 = (bf16[256,512]{1,0:T(8,128)(2,1)}, bf16[256,512]{1,0:T(8,128)(2,1)S(1)}, u32[]{:S(2)}, u32[]{:S(2)}) collective-permute-start(bf16[256,512]{1,0:T(8,128)(2,1)} %collective-permute-done.14), channel_id=1, source_target_pairs={{0,2},{4,0},{8,4},{12,8},{14,12},{10,14},{6,10},{2,6},{1,3},{5,1},... | collective-permute-start | bytes 786440 | tf_op jit(solution)/shard_map/ppermute | solution.py:27
  79.2 7.6 %collective-permute-start.21 = (bf16[6,1024]{1,0:T(8,128)(2,1)S(1)}, bf16[6,1024]{1,0:T(8,128)(2,1)S(1)}, u32[]{:S(2)}, u32[]{:S(2)}) collective-permute-start(bf16[6,1024]{1,0:T(8,128)(2,1)S(1)} %maximum_select_fusion.2), channel_id=1, source_target_pairs={{24,0},{23,1},{28,4},{19,5},{30,8},{17,9},{26,12},{21,13},{22,14},... | collective-permute-start | bytes 36872 | tf_op jit(solution)/shard_map/ppermute | solution.py:47
  80.5 8.6 %collective-permute-start.22 = (bf16[6,1024]{1,0:T(8,128)(2,1)S(1)}, bf16[6,1024]{1,0:T(8,128)(2,1)S(1)}, u32[]{:S(2)}, u32[]{:S(2)}) collective-permute-start(bf16[6,1024]{1,0:T(8,128)(2,1)S(1)} %maximum_select_fusion.2), channel_id=1, source_target_pairs={{28,0},{19,1},{30,4},{17,5},{26,8},{21,9},{22,12},{25,13},{18,14},... | collective-permute-start | bytes 36872 | tf_op jit(solution)/shard_map/ppermute | solution.py:47
  95.1 9.2 %collective-permute-start.24 = (bf16[256,512]{1,0:T(8,128)(2,1)S(1)}, bf16[256,512]{1,0:T(8,128)(2,1)S(1)}, u32[]{:S(2)}, u32[]{:S(2)}) collective-permute-start(bf16[256,512]{1,0:T(8,128)(2,1)S(1)} %convolution_convert_fusion.3), channel_id=1, source_target_pairs={{0,4},{4,8},{8,12},{12,14},{14,10},{10,6},{6,2},{2,0},{1,5},{5,9},... | collective-permute-start | bytes 786440 | tf_op jit(solution)/shard_map/ppermute | solution.py:27
  98.0 9.2 %collective-permute-start.28 = (bf16[256,512]{1,0:T(8,128)(2,1)S(1)}, bf16[256,512]{1,0:T(8,128)(2,1)S(1)}, u32[]{:S(2)}, u32[]{:S(2)}) collective-permute-start(bf16[256,512]{1,0:T(8,128)(2,1)S(1)} %convolution_convert_fusion.2), channel_id=1, source_target_pairs={{0,2},{4,0},{8,4},{12,8},{14,12},{10,14},{6,10},{2,6},{1,3},{5,1},... | collective-permute-start | bytes 786440 | tf_op jit(solution)/shard_map/ppermute | solution.py:27
  99.0 13.8 %collective-permute-start.34 = (bf16[256,512]{1,0:T(8,128)(2,1)S(1)}, bf16[256,512]{1,0:T(8,128)(2,1)S(1)}, u32[]{:S(2)}, u32[]{:S(2)}) collective-permute-start(bf16[256,512]{1,0:T(8,128)(2,1)S(1)} %convolution_convert_fusion), channel_id=1, source_target_pairs={{0,2},{4,0},{8,4},{12,8},{14,12},{10,14},{6,10},{2,6},{1,3},{5,1},... | collective-permute-start | bytes 786440 | tf_op jit(solution)/shard_map/ppermute | solution.py:27
  99.6 16.2 %collective-permute-start.31 = (bf16[256,512]{1,0:T(8,128)(2,1)S(1)}, bf16[256,512]{1,0:T(8,128)(2,1)S(1)}, u32[]{:S(2)}, u32[]{:S(2)}) collective-permute-start(bf16[256,512]{1,0:T(8,128)(2,1)S(1)} %convolution_convert_fusion.1), channel_id=1, source_target_pairs={{0,4},{4,8},{8,12},{12,14},{14,10},{10,6},{6,2},{2,0},{1,5},{5,9},... | collective-permute-start | bytes 786440 | tf_op jit(solution)/shard_map/ppermute | solution.py:27
  107.7 24.1 %collective-permute-start.29 = (bf16[256,512]{1,0:T(8,128)(2,1)S(1)}, bf16[256,512]{1,0:T(8,128)(2,1)S(1)}, u32[]{:S(2)}, u32[]{:S(2)}) collective-permute-start(bf16[256,512]{1,0:T(8,128)(2,1)S(1)} %add_convert_fusion.5), channel_id=1, source_target_pairs={{0,2},{4,0},{8,4},{12,8},{14,12},{10,14},{6,10},{2,6},{1,3},{5,1},... | collective-permute-start | bytes 786440 | tf_op jit(solution)/shard_map/ppermute | solution.py:27
  113.3 9.7 %collective-permute-start.35 = (bf16[256,512]{1,0:T(8,128)(2,1)S(1)}, bf16[256,512]{1,0:T(8,128)(2,1)S(1)}, u32[]{:S(2)}, u32[]{:S(2)}) collective-permute-start(bf16[256,512]{1,0:T(8,128)(2,1)S(1)} %add_convert_fusion.2), channel_id=1, source_target_pairs={{0,2},{4,0},{8,4},{12,8},{14,12},{10,14},{6,10},{2,6},{1,3},{5,1},... | collective-permute-start | bytes 786440 | tf_op jit(solution)/shard_map/ppermute | solution.py:27
  114.3 9.7 %collective-permute-start.25 = (bf16[256,512]{1,0:T(8,128)(2,1)S(1)}, bf16[256,512]{1,0:T(8,128)(2,1)S(1)}, u32[]{:S(2)}, u32[]{:S(2)}) collective-permute-start(bf16[256,512]{1,0:T(8,128)(2,1)S(1)} %add_convert_fusion.7), channel_id=1, source_target_pairs={{0,4},{4,8},{8,12},{12,14},{14,10},{10,6},{6,2},{2,0},{1,5},{5,9},... | collective-permute-start | bytes 786440 | tf_op jit(solution)/shard_map/ppermute | solution.py:27
  116.3 9.7 %collective-permute-start.32 = (bf16[256,512]{1,0:T(8,128)(2,1)S(1)}, bf16[256,512]{1,0:T(8,128)(2,1)S(1)}, u32[]{:S(2)}, u32[]{:S(2)}) collective-permute-start(bf16[256,512]{1,0:T(8,128)(2,1)S(1)} %add_convert_fusion.4), channel_id=1, source_target_pairs={{0,4},{4,8},{8,12},{12,14},{14,10},{10,6},{6,2},{2,0},{1,5},{5,9},... | collective-permute-start | bytes 786440 | tf_op jit(solution)/shard_map/ppermute | solution.py:27
  124.5 9.3 %collective-permute-start.26 = (bf16[256,512]{1,0:T(8,128)(2,1)S(1)}, bf16[256,512]{1,0:T(8,128)(2,1)S(1)}, u32[]{:S(2)}, u32[]{:S(2)}) collective-permute-start(bf16[256,512]{1,0:T(8,128)(2,1)S(1)} %add_convert_fusion.6), channel_id=1, source_target_pairs={{0,4},{4,8},{8,12},{12,14},{14,10},{10,6},{6,2},{2,0},{1,5},{5,9},... | collective-permute-start | bytes 786440 | tf_op jit(solution)/shard_map/ppermute | solution.py:27
  126.4 13.0 %collective-permute-start.33 = (bf16[256,512]{1,0:T(8,128)(2,1)S(1)}, bf16[256,512]{1,0:T(8,128)(2,1)S(1)}, u32[]{:S(2)}, u32[]{:S(2)}) collective-permute-start(bf16[256,512]{1,0:T(8,128)(2,1)S(1)} %add_convert_fusion.3), channel_id=1, source_target_pairs={{0,4},{4,8},{8,12},{12,14},{14,10},{10,6},{6,2},{2,0},{1,5},{5,9},... | collective-permute-start | bytes 786440 | tf_op jit(solution)/shard_map/ppermute | solution.py:27
  131.1 9.2 %collective-permute-start.37 = (bf16[256,512]{1,0:T(8,128)(2,1)S(1)}, bf16[256,512]{1,0:T(8,128)(2,1)S(1)}, u32[]{:S(2)}, u32[]{:S(2)}) collective-permute-start(bf16[256,512]{1,0:T(8,128)(2,1)S(1)} %add_convert_fusion), channel_id=1, source_target_pairs={{0,2},{4,0},{8,4},{12,8},{14,12},{10,14},{6,10},{2,6},{1,3},{5,1},... | collective-permute-start | bytes 786440 | tf_op jit(solution)/shard_map/ppermute | solution.py:27
  132.1 11.0 %collective-permute-start.30 = (bf16[256,512]{1,0:T(8,128)(2,1)S(1)}, bf16[256,512]{1,0:T(8,128)(2,1)S(1)}, u32[]{:S(2)}, u32[]{:S(2)}) collective-permute-start(bf16[256,512]{1,0:T(8,128)(2,1)S(1)} %convert_add_fusion.2), channel_id=1, source_target_pairs={{0,2},{4,0},{8,4},{12,8},{14,12},{10,14},{6,10},{2,6},{1,3},{5,1},... | collective-permute-start | bytes 786440 | tf_op jit(solution)/shard_map/ppermute | solution.py:27
  134.2 9.0 %collective-permute-start.27 = (bf16[256,512]{1,0:T(8,128)(2,1)S(1)}, bf16[256,512]{1,0:T(8,128)(2,1)S(1)}, u32[]{:S(2)}, u32[]{:S(2)}) collective-permute-start(bf16[256,512]{1,0:T(8,128)(2,1)S(1)} %convert_add_fusion.3), channel_id=1, source_target_pairs={{0,4},{4,8},{8,12},{12,14},{14,10},{10,6},{6,2},{2,0},{1,5},{5,9},... | collective-permute-start | bytes 786440 | tf_op jit(solution)/shard_map/ppermute | solution.py:27
  (13 other events, 145.3 us)

commit v11 on v10

--- a/solution.py
+++ b/solution.py
@@ -29,6 +29,10 @@
 
 def after(first, block):
     return lax.optimization_barrier((first, block))[1]
+
+
+def passed_on(weights):
+    return lax.ppermute(weights.astype(jnp.bfloat16), "grp", [(0, 1)])
 
 
 def from_sibling(block):
@@ -82,10 +86,11 @@
 
     first_sent = along_ring(own, 1)
     other_states = from_sibling(states)
-    states = after(first_sent, states)
+    normed_own = normalize(after(first_sent, states), gain)
+    normed_other = normalize(after(normed_own, other_states), gain)
     ids, cand_ids = token_ids[0], after(first_sent, cand_ids)
     slab_owner = after(first_sent, slab_owner)
-    normed = jnp.concatenate([normalize(states, gain), normalize(other_states, gain)])
+    normed = jnp.concatenate([normed_own, normed_other])
     normed = normed.reshape(seqs * length, width)
     ids = jnp.concatenate([ids, cand_ids], axis=1)
     ids = jnp.concatenate([ids, from_sibling(ids)])
@@ -112,23 +117,22 @@
                 if (step, i, by) == (1, 0, 1):
                     moving[i, by] = first_sent
                 else:
-                    if last and i == 1 and step > 2:
-                        moving[i, by] = after(sums[1], moving[i, by])
+                    if last and step > 2:
+                        moving[i, by] = after(sums[1 + i], moving[i, by])
+                    elif step in (2, 3) and i == 1:
+                        norms = normed_own if step == 2 else normed_other
+                        moving[i, by] = after(norms, moving[i, by])
                     moving[i, by] = along_ring(moving[i, by], by)
                 total = total + product(-by * step, parts[i], moving[i, by])
             sums[step] = total
-            if step == 1:
-                weights = after(moving[1, 1], weights)
     else:
         both = in_core_order(own, sibling, core)
         gathered = lax.all_gather(both, "chip", axis=0, tiled=True)
         total = jnp.dot(normed, gathered, preferred_element_type=jnp.float32)
 
-    copied = lax.ppermute(weights.astype(jnp.bfloat16), "grp", [(0, 1)])
     active = jnp.tanh(total).reshape(seqs, length, half)
     there = jnp.arange(length)[None, :, None] < lengths[:, None, None]
     pooled = jnp.sum(jnp.where(there, active, 0.0), axis=1) / counts[:, None]
-    pooled, copied = lax.optimization_barrier((pooled, copied))
     pooled_other = from_sibling(pooled)
     pooled_other = jnp.concatenate([pooled_other[seq_dev:], pooled_other[:seq_dev]])
     whole = in_core_order(pooled, pooled_other, core, axis=1)
@@ -140,30 +144,38 @@
 
     kept = slab_blocks(stored, chips)
     kept = jnp.concatenate(kept)
-    slab = in_core_order(kept, from_sibling(kept), core)
-    slab_rows = slab.shape[0]
+    slab = [kept, from_sibling(kept)]
+    slab_rows = slab_owner.shape[0]
     earlier = jnp.arange(slab_rows)[:, None] < jnp.arange(slab_rows)[None, :]
     same = slab_owner[:, None] == slab_owner[None, :]
     ranks = jnp.sum((earlier & same).astype(jnp.int32), axis=0)
     owner_place = ring_place(slab_owner // cores, chips)
-    seen = lax.rem(owner_place - place + chips, chips)
+    seen = lax.rem(owner_place - place - core * (chips // cores) + 2 * chips, chips)
     slots = seen * seqs + lax.rem(slab_owner, cores) * seq_dev + ranks
-    positive, candidate = [
-        jnp.sum(
-            (slots[picked][:, :, None] == jnp.arange(slab_rows)).astype(jnp.float32), axis=1
-        )
-        for picked in (cands[:, :1], cands)
-    ]
-
-    slab_wide = slab.astype(jnp.float32)
-    logits = (
-        sharpness / embedding * jnp.dot(unit, slab_wide.T, precision=lax.Precision.HIGHEST)
-    )
-    exponent = jnp.where(candidate > 0, jnp.exp(logits), 0.0)
-    probs = exponent / jnp.sum(exponent, axis=-1, keepdims=True)
-    logit_grad = probs - positive
+    moved = (slots[:, None] == jnp.arange(slab_rows)[None, :]).astype(jnp.float32)
+    picked = (cands[:, :, None] == jnp.arange(slab_rows)).astype(jnp.float32)
+    positive = jnp.dot(picked[:, 0], moved)
+    candidate = jnp.dot(jnp.sum(picked, axis=1), moved)
+    piece = slab_rows // cores
+    pieces = [slice(i * piece, (i + 1) * piece) for i in range(cores)]
+
+    slab_wide = [rows_in.astype(jnp.float32) for rows_in in slab]
+    exponent = []
+    for rows_in, at in zip(slab_wide, pieces):
+        logits = (
+            sharpness / embedding * jnp.dot(unit, rows_in.T, precision=lax.Precision.HIGHEST)
+        )
+        exponent.append(jnp.where(candidate[:, at] > 0.5, jnp.exp(logits), 0.0))
+    denominator = sum(jnp.sum(part, axis=-1, keepdims=True) for part in exponent)
     unit_grad = (
-        sharpness / embedding * jnp.dot(logit_grad, slab_wide, precision=lax.Precision.HIGHEST)
+        sharpness
+        / embedding
+        * sum(
+            jnp.dot(
+                part / denominator - positive[:, at], rows_in, precision=lax.Precision.HIGHEST
+            )
+            for part, rows_in, at in zip(exponent, slab_wide, pieces)
+        )
     )
     inner = jnp.sum(whole * unit_grad, axis=-1, keepdims=True)
     pooled_grad = scale * unit_grad - whole * (scale * scale * scale) * inner / embedding
@@ -194,7 +206,8 @@
                     total = after(copied, total)
                 arrived[i, by] = along_ring(total.astype(jnp.bfloat16), by)
             if step == chips // 2:
-                late = after(arrived[0, 1], delta)
+                late, weights = after(arrived[0, 1], (delta, weights))
+                copied = passed_on(weights)
         owns = [term(0, parts[i], late) for i in range(2)]
         arrived[1, 1] = after(owns, arrived[1, 1])
         arrived[0, -1] = after(owns, arrived[0, -1])
@@ -206,6 +219,7 @@
         grad = lax.dot_general(
             normed, delta, (((0,), (0,)), ((), ())), preferred_element_type=jnp.float32
         )
+        copied = passed_on(weights)
         reduced = lax.psum_scatter(grad, "chip", scatter_dimension=0, tiled=True)
         mine, other = [lax.dynamic_slice(reduced, (i * rows, 0), (rows, half)) for i in parts]
     other = from_sibling(other)

time: 147 us -> 136 us (0.925)
  matrix products: 30.8 us -> 26.8 us
  other arithmetic: 19.2 us -> 16.3 us
  starting transfers between devices: 41 us -> 38.1 us
    dot_general x16, matrix products: 20.3 us -> 17.2 us  [product(): jnp.dot(columns(offset, part), block, preferred_element_type=jnp.float32)]
    ppermute x1, starting transfers between devices: 4.18 us -> 1.32 us  [passed_on(): return lax.ppermute(weights.astype(jnp.bfloat16), 'grp', [(0, 1)])]
    convert_element_type x1, other arithmetic: 2.1 us -> 0.07 us  [passed_on(): return lax.ppermute(weights.astype(jnp.bfloat16), 'grp', [(0, 1)])]
    concatenate x1, other arithmetic: 2.43 us -> 0.54 us  [shards(): normed = jnp.concatenate([normed_own, normed_other])]
    dot_general x16, matrix products: 9.78 us -> 7.99 us  [term(): lax.dot_general(columns(offset, part), delta, (((0,), (0,)), ((), ())), p...]
    gather x3 -> x0, local copies, waits for them, and re-layouts: 1.5 us -> none  [shards(): slots[picked][:, :, None] == jnp.arange(slab_rows)]
    convert_element_type x1 -> x2, other arithmetic: 4.68 us -> 5.84 us  [normalize(): (states_wide * lax.rsqrt(mean_square + 1e-05) * gain).astype(jnp.bfloat16)]
  transfers between devices with their start and end apart: 39 -> 39, of which waited for: 18 -> 16; matrix products, arithmetic and copies ran while one was open for 32% -> 28% of each run, Pallas kernels for 0% -> 0%
where the time goes in v11:
time: 136 us
  waiting for transfers between devices  50.2 us (37%)
  starting transfers between devices  38.1 us (28%)
  matrix products  26.8 us (20%)
  other arithmetic  16.3 us (12%)
  local copies, waits for them, and re-layouts  3.63 us (3%)
    ppermute x28, waiting for transfers between devices, along_ring(): return lax.ppermute(block, 'chip', pairs)  41.2 us
    ppermute x28, starting transfers between devices, along_ring(): return lax.ppermute(block, 'chip', pairs)  30.7 us
    dot_general x16, matrix products, product(): jnp.dot(columns(offset, part), block, preferred_element_type=jnp.float32)  17.2 us
    dot_general x16, matrix products, term(): lax.dot_general(columns(offset, part), delta, (((0,), (0,)), ((), ())), p...  7.99 us
    ppermute x4, waiting for transfers between devices, slab_blocks(): kept.append(lax.ppermute(stored, ('grp', 'chip', 'core'), pairs))  7.29 us
    convert_element_type x2, other arithmetic, normalize(): (states_wide * lax.rsqrt(mean_square + 1e-05) * gain).astype(jnp.bfloat16)  5.84 us
    ppermute x4, starting transfers between devices, slab_blocks(): kept.append(lax.ppermute(stored, ('grp', 'chip', 'core'), pairs))  5.34 us
    reduce_sum x2, other arithmetic, normalize(): mean_square = jnp.mean(states_wide * states_wide, axis=-1, keepdims=True)  5.17 us
  transfers between devices with their start and end apart: 39, of which 16 were waited for; matrix products, arithmetic and copies ran while one was open for 28% of the time, Pallas kernels for 0%

profile of v11, /device:TPU:0, one launch (start us, length us, event | category | flops | bytes accessed | tf_op | source)
XLA Modules:
  0.0 135.6 jit_solution(1922414517993946840)
XLA Ops:
  0.0 2.1 %fusion.87 = (bf16[256,512]{1,0:T(8,128)(2,1)}, bf16[256,512]{1,0:T(8,128)(2,1)S(1)}) fusion(f32[1,256,1024]{2,1,0:T(8,128)} %param.8, s32[]{:T(128)S(6)} %select_n.217, s32[]{:T(128)S(6)} %select_n.203), kind=kLoop, calls=%fused_computation.107 | loop fusion | bytes 1048584 | tf_op jit(solution)/shard_map/convert_element_type | solution.py:84
  2.1 3.0 %collective-permute-start = (bf16[256,512]{1,0:T(8,128)(2,1)S(1)}, bf16[256,512]{1,0:T(8,128)(2,1)}, u32[]{:S(2)}, u32[]{:S(2)}) collective-permute-start(bf16[256,512]{1,0:T(8,128)(2,1)S(1)} %get-tuple-element.42), channel_id=1, source_target_pairs={{0,4},{4,8},{8,12},{12,14},{14,10},{10,6},{6,2},{2,0},{1,5},{5,9},... | collective-permute-start | bytes 786440 | tf_op jit(solution)/shard_map/ppermute | solution.py:27
  6.3 5.2 %collective-permute-done = bf16[256,512]{1,0:T(8,128)(2,1)} collective-permute-done((bf16[256,512]{1,0:T(8,128)(2,1)S(1)}, bf16[256,512]{1,0:T(8,128)(2,1)}, u32[]{:S(2)}, u32[]{:S(2)}) %collective-permute-start) | collective-permute-done | bytes 262176 | tf_op jit(solution)/shard_map/ppermute | solution.py:27
  12.2 2.6 %fusion = f32[3,128]{1,0:T(4,128)S(1)} fusion(bf16[3,128,4096]{2,1,0:T(8,128)(2,1)} %bitcast.95), kind=kLoop, calls=%fused_computation.4 | loop fusion | flops 4718208 | bytes 3147264 | tf_op jit(solution)/shard_map/reduce_sum | solution.py:65
  14.8 2.7 %fusion.2 = bf16[3,128,4096]{2,1,0:T(8,128)(2,1)} fusion(bf16[3,128,4096]{2,1,0:T(8,128)(2,1)S(1)} %bitcast.96, f32[4096]{0:T(1024)S(1)} %copy-done.4, f32[3,128]{1,0:T(4,128)S(1)} %add_rsqrt_fusion.1), kind=kLoop, calls=%fused_computation.6 | loop fusion | flops 6291456 | bytes 6309376 | tf_op jit(solution)/shard_map/convert_element_type | solution.py:66
  17.7 1.9 %collective-permute-start.5 = (bf16[256,512]{1,0:T(8,128)(2,1)}, bf16[256,512]{1,0:T(8,128)(2,1)}, u32[]{:S(2)}, u32[]{:S(2)}) collective-permute-start(bf16[256,512]{1,0:T(8,128)(2,1)} %collective-permute-done.3), channel_id=1, source_target_pairs={{0,4},{4,8},{8,12},{12,14},{14,10},{10,6},{6,2},{2,0},{1,5},{5,9},... | collective-permute-start | bytes 786440 | tf_op jit(solution)/shard_map/ppermute | solution.py:27
  19.8 1.8 %collective-permute-start.7 = (bf16[256,512]{1,0:T(8,128)(2,1)}, bf16[256,512]{1,0:T(8,128)(2,1)}, u32[]{:S(2)}, u32[]{:S(2)}) collective-permute-start(bf16[256,512]{1,0:T(8,128)(2,1)} %collective-permute-done), channel_id=1, source_target_pairs={{0,4},{4,8},{8,12},{12,14},{14,10},{10,6},{6,2},{2,0},{1,5},{5,9},... | collective-permute-start | bytes 786440 | tf_op jit(solution)/shard_map/ppermute | solution.py:27
  22.5 4.7 %collective-permute-done.5 = bf16[256,512]{1,0:T(8,128)(2,1)} collective-permute-done((bf16[256,512]{1,0:T(8,128)(2,1)}, bf16[256,512]{1,0:T(8,128)(2,1)}, u32[]{:S(2)}, u32[]{:S(2)}) %collective-permute-start.5) | collective-permute-done | bytes 262176 | tf_op jit(solution)/shard_map/ppermute | solution.py:27
  27.2 1.8 %collective-permute-start.9 = (bf16[256,512]{1,0:T(8,128)(2,1)}, bf16[256,512]{1,0:T(8,128)(2,1)}, u32[]{:S(2)}, u32[]{:S(2)}) collective-permute-start(bf16[256,512]{1,0:T(8,128)(2,1)} %collective-permute-done.5), channel_id=1, source_target_pairs={{0,4},{4,8},{8,12},{12,14},{14,10},{10,6},{6,2},{2,0},{1,5},{5,9},... | collective-permute-start | bytes 786440 | tf_op jit(solution)/shard_map/ppermute | solution.py:27
  29.2 3.6 %collective-permute-done.7 = bf16[256,512]{1,0:T(8,128)(2,1)} collective-permute-done((bf16[256,512]{1,0:T(8,128)(2,1)}, bf16[256,512]{1,0:T(8,128)(2,1)}, u32[]{:S(2)}, u32[]{:S(2)}) %collective-permute-start.7) | collective-permute-done | bytes 262176 | tf_op jit(solution)/shard_map/ppermute | solution.py:27
  32.8 1.8 %collective-permute-start.11 = (bf16[256,512]{1,0:T(8,128)(2,1)}, bf16[256,512]{1,0:T(8,128)(2,1)}, u32[]{:S(2)}, u32[]{:S(2)}) collective-permute-start(bf16[256,512]{1,0:T(8,128)(2,1)} %collective-permute-done.7), channel_id=1, source_target_pairs={{0,4},{4,8},{8,12},{12,14},{14,10},{10,6},{6,2},{2,0},{1,5},{5,9},... | collective-permute-start | bytes 786440 | tf_op jit(solution)/shard_map/ppermute | solution.py:27
  34.8 2.6 %fusion.3 = f32[3,128]{1,0:T(4,128)S(1)} fusion(bf16[3,128,4096]{2,1,0:T(8,128)(2,1)} %collective-permute-done.1), kind=kLoop, calls=%fused_computation.7 | loop fusion | flops 4718208 | bytes 3147264 | tf_op jit(solution)/shard_map/reduce_sum | solution.py:65
  37.4 3.1 %fusion.5 = bf16[3,128,4096]{2,1,0:T(8,128)(2,1)S(1)} fusion(bf16[3,128,4096]{2,1,0:T(8,128)(2,1)} %collective-permute-done.1, f32[3,128]{1,0:T(4,128)S(1)} %add_rsqrt_fusion, f32[4096]{0:T(1024)S(1)} %copy-done.4), kind=kLoop, calls=%fused_computation.9 | loop fusion | flops 6291456 | bytes 6309376 | tf_op jit(solution)/shard_map/convert_element_type | solution.py:66
  41.1 1.9 %collective-permute-start.13 = (bf16[256,512]{1,0:T(8,128)(2,1)}, bf16[256,512]{1,0:T(8,128)(2,1)S(1)}, u32[]{:S(2)}, u32[]{:S(2)}) collective-permute-start(bf16[256,512]{1,0:T(8,128)(2,1)} %collective-permute-done.9), channel_id=1, source_target_pairs={{0,4},{4,8},{8,12},{12,14},{14,10},{10,6},{6,2},{2,0},{1,5},{5,9},... | collective-permute-start | bytes 786440 | tf_op jit(solution)/shard_map/ppermute | solution.py:27
  48.9 1.6 %add_add_fusion.1 = f32[768,512]{1,0:T(8,128)S(1)} fusion(f32[768,512]{1,0:T(8,128)S(1)} %fusion.68, f32[768,512]{1,0:T(8,128)S(1)} %fusion.72, f32[768,512]{1,0:T(8,128)S(1)} %fusion.76, f32[768,512]{1,0:T(8,128)S(1)} %fusion.84, f32[768,512]{1,0:T(8,128)S(1)} %fusion.80, bf16[256,512]{1,0:T(8,128)(2,1)} %collective-permute-done.6, ...), kind=kOutput, calls=%fused_computation.17 | convolution fusion | flops 203292672 | bytes 10092548 | tf_op jit(solution)/shard_map/dot_general | solution.py:106
  50.5 1.9 %collective-permute-start.15 = (bf16[256,512]{1,0:T(8,128)(2,1)}, bf16[256,512]{1,0:T(8,128)(2,1)S(1)}, u32[]{:S(2)}, u32[]{:S(2)}) collective-permute-start(bf16[256,512]{1,0:T(8,128)(2,1)} %collective-permute-done.11), channel_id=1, source_target_pairs={{0,4},{4,8},{8,12},{12,14},{14,10},{10,6},{6,2},{2,0},{1,5},{5,9},... | collective-permute-start | bytes 786440 | tf_op jit(solution)/shard_map/ppermute | solution.py:27
  56.3 1.5 %add_add_fusion = f32[768,512]{1,0:T(8,128)S(1)} fusion(f32[768,512]{1,0:T(8,128)S(1)} %fusion.40, f32[768,512]{1,0:T(8,128)S(1)} %fusion.46, f32[768,512]{1,0:T(8,128)S(1)} %add_add_fusion.1, f32[768,512]{1,0:T(8,128)S(1)} %fusion.56, bf16[256,512]{1,0:T(8,128)(2,1)} %collective-permute-done.8, bf16[768,4096]{1,0:T(8,128)(2,1)S(1)} %bitcast.70, ...), kind=kOutput, calls=%fused_computation.16 | convolution fusion | flops 202899456 | bytes 8519684 | tf_op jit(solution)/shard_map/dot_general | solution.py:106
  60.6 5.0 %collective-permute-done.16 = bf16[256,512]{1,0:T(8,128)(2,1)S(1)} collective-permute-done((bf16[256,512]{1,0:T(8,128)(2,1)S(1)}, bf16[256,512]{1,0:T(8,128)(2,1)S(1)}, u32[]{:S(2)}, u32[]{:S(2)}) %collective-permute-start.16) | collective-permute-done | bytes 262176 | tf_op jit(solution)/shard_map/ppermute | solution.py:27
  66.0 1.7 %add_tanh_fusion = f32[768,512]{1,0:T(8,128)S(1)} fusion(f32[768,512]{1,0:T(8,128)S(1)} %fusion.13, f32[768,512]{1,0:T(8,128)S(1)} %fusion.15, f32[768,512]{1,0:T(8,128)S(1)} %fusion.19, f32[768,512]{1,0:T(8,128)S(1)} %fusion.23, f32[768,512]{1,0:T(8,128)S(1)} %add_add_fusion, f32[768,512]{1,0:T(8,128)S(1)} %fusion.36, ...), kind=kOutput, calls=%fused_computation.15 | convolution fusion | flops 203685888 | bytes 11665412 | tf_op jit(solution)/shard_map/dot_general | solution.py:106
  75.1 2.3 %collective-permute-done.19 = bf16[6,1024]{1,0:T(8,128)(2,1)S(1)} collective-permute-done((bf16[6,1024]{1,0:T(8,128)(2,1)S(1)}, bf16[6,1024]{1,0:T(8,128)(2,1)S(1)}, u32[]{:S(2)}, u32[]{:S(2)}) %collective-permute-start.19) | collective-permute-done | bytes 12320 | tf_op jit(solution)/shard_map/ppermute | solution.py:51
  77.4 2.5 %collective-permute-done.20 = bf16[6,1024]{1,0:T(8,128)(2,1)S(1)} collective-permute-done((bf16[6,1024]{1,0:T(8,128)(2,1)S(1)}, bf16[6,1024]{1,0:T(8,128)(2,1)S(1)}, u32[]{:S(2)}, u32[]{:S(2)}) %collective-permute-start.20) | collective-permute-done | bytes 12320 | tf_op jit(solution)/shard_map/ppermute | solution.py:51
  79.9 2.3 %collective-permute-done.21 = bf16[6,1024]{1,0:T(8,128)(2,1)S(1)} collective-permute-done((bf16[6,1024]{1,0:T(8,128)(2,1)S(1)}, bf16[6,1024]{1,0:T(8,128)(2,1)S(1)}, u32[]{:S(2)}, u32[]{:S(2)}) %collective-permute-start.21) | collective-permute-done | bytes 12320 | tf_op jit(solution)/shard_map/ppermute | solution.py:51
  88.4 1.7 %collective-permute-start.34 = (bf16[256,512]{1,0:T(8,128)(2,1)S(1)}, bf16[256,512]{1,0:T(8,128)(2,1)S(1)}, u32[]{:S(2)}, u32[]{:S(2)}) collective-permute-start(bf16[256,512]{1,0:T(8,128)(2,1)S(1)} %convolution_convert_fusion), channel_id=1, source_target_pairs={{0,2},{4,0},{8,4},{12,8},{14,12},{10,14},{6,10},{2,6},{1,3},{5,1},... | collective-permute-start | bytes 786440 | tf_op jit(solution)/shard_map/ppermute | solution.py:27
  90.6 4.2 %collective-permute-done.31 = bf16[256,512]{1,0:T(8,128)(2,1)S(1)} collective-permute-done((bf16[256,512]{1,0:T(8,128)(2,1)S(1)}, bf16[256,512]{1,0:T(8,128)(2,1)S(1)}, u32[]{:S(2)}, u32[]{:S(2)}) %collective-permute-start.31) | collective-permute-done | bytes 262176 | tf_op jit(solution)/shard_map/ppermute | solution.py:27
  96.7 3.7 %collective-permute-done.23 = bf16[256,512]{1,0:T(8,128)(2,1)S(1)} collective-permute-done((bf16[256,512]{1,0:T(8,128)(2,1)S(1)}, bf16[256,512]{1,0:T(8,128)(2,1)S(1)}, u32[]{:S(2)}, u32[]{:S(2)}) %collective-permute-start.23) | collective-permute-done | bytes 262176 | tf_op jit(solution)/shard_map/ppermute | solution.py:27
  102.6 1.6 %collective-permute-start.25 = (bf16[256,512]{1,0:T(8,128)(2,1)S(1)}, bf16[256,512]{1,0:T(8,128)(2,1)S(1)}, u32[]{:S(2)}, u32[]{:S(2)}) collective-permute-start(bf16[256,512]{1,0:T(8,128)(2,1)S(1)} %add_convert_fusion.7), channel_id=1, source_target_pairs={{0,4},{4,8},{8,12},{12,14},{14,10},{10,6},{6,2},{2,0},{1,5},{5,9},... | collective-permute-start | bytes 786440 | tf_op jit(solution)/shard_map/ppermute | solution.py:27
  106.9 3.3 %collective-permute-done.35 = bf16[256,512]{1,0:T(8,128)(2,1)S(1)} collective-permute-done((bf16[256,512]{1,0:T(8,128)(2,1)S(1)}, bf16[256,512]{1,0:T(8,128)(2,1)S(1)}, u32[]{:S(2)}, u32[]{:S(2)}) %collective-permute-start.35) | collective-permute-done | bytes 262176 | tf_op jit(solution)/shard_map/ppermute | solution.py:27
  111.5 1.7 %collective-permute-start.33 = (bf16[256,512]{1,0:T(8,128)(2,1)S(1)}, bf16[256,512]{1,0:T(8,128)(2,1)S(1)}, u32[]{:S(2)}, u32[]{:S(2)}) collective-permute-start(bf16[256,512]{1,0:T(8,128)(2,1)S(1)} %add_convert_fusion.3), channel_id=1, source_target_pairs={{0,4},{4,8},{8,12},{12,14},{14,10},{10,6},{6,2},{2,0},{1,5},{5,9},... | collective-permute-start | bytes 786440 | tf_op jit(solution)/shard_map/ppermute | solution.py:27
  113.6 1.8 %collective-permute-start.26 = (bf16[256,512]{1,0:T(8,128)(2,1)S(1)}, bf16[256,512]{1,0:T(8,128)(2,1)S(1)}, u32[]{:S(2)}, u32[]{:S(2)}) collective-permute-start(bf16[256,512]{1,0:T(8,128)(2,1)S(1)} %add_convert_fusion.6), channel_id=1, source_target_pairs={{0,4},{4,8},{8,12},{12,14},{14,10},{10,6},{6,2},{2,0},{1,5},{5,9},... | collective-permute-start | bytes 786440 | tf_op jit(solution)/shard_map/ppermute | solution.py:27
  115.4 4.3 %collective-permute-done.36 = bf16[256,512]{1,0:T(8,128)(2,1)S(1)} collective-permute-done((bf16[256,512]{1,0:T(8,128)(2,1)S(1)}, bf16[256,512]{1,0:T(8,128)(2,1)S(1)}, u32[]{:S(2)}, u32[]{:S(2)}) %collective-permute-start.36) | collective-permute-done | bytes 262176 | tf_op jit(solution)/shard_map/ppermute | solution.py:27
  125.1 4.4 %collective-permute-done.37 = bf16[256,512]{1,0:T(8,128)(2,1)S(1)} collective-permute-done((bf16[256,512]{1,0:T(8,128)(2,1)S(1)}, bf16[256,512]{1,0:T(8,128)(2,1)S(1)}, u32[]{:S(2)}, u32[]{:S(2)}) %collective-permute-start.37) | collective-permute-done | bytes 262176 | tf_op jit(solution)/shard_map/ppermute | solution.py:27
  129.6 2.8 %collective-permute-done.30 = bf16[256,512]{1,0:T(8,128)(2,1)S(1)} collective-permute-done((bf16[256,512]{1,0:T(8,128)(2,1)}, bf16[256,512]{1,0:T(8,128)(2,1)S(1)}, u32[]{:S(2)}, u32[]{:S(2)}) %collective-permute-start.30) | collective-permute-done | bytes 262176 | tf_op jit(solution)/shard_map/ppermute | solution.py:27
  (137 shorter events, 48.2 us)
Async XLA Ops:
  2.1 9.4 %collective-permute-start = (bf16[256,512]{1,0:T(8,128)(2,1)S(1)}, bf16[256,512]{1,0:T(8,128)(2,1)}, u32[]{:S(2)}, u32[]{:S(2)}) collective-permute-start(bf16[256,512]{1,0:T(8,128)(2,1)S(1)} %get-tuple-element.42), channel_id=1, source_target_pairs={{0,4},{4,8},{8,12},{12,14},{14,10},{10,6},{6,2},{2,0},{1,5},{5,9},... | collective-permute-start | bytes 786440 | tf_op jit(solution)/shard_map/ppermute | solution.py:27
  5.1 29.7 %collective-permute-start.1 = (bf16[3,128,4096]{2,1,0:T(8,128)(2,1)}, bf16[3,128,4096]{2,1,0:T(8,128)(2,1)}, u32[]{:S(2)}, u32[]{:S(2)}) collective-permute-start(bf16[3,128,4096]{2,1,0:T(8,128)(2,1)} %bitcast.94), channel_id=1, source_target_pairs={{0,1},{1,0},{2,3},{3,2},{4,5},{5,4},{6,7},{7,6},{8,9},{9,8},{10,11... | collective-permute-start | bytes 9437192 | tf_op jit(solution)/shard_map/ppermute | solution.py:39
  5.2 14.6 %collective-permute-start.4 = (bf16[256,512]{1,0:T(8,128)(2,1)S(1)}, bf16[256,512]{1,0:T(8,128)(2,1)}, u32[]{:S(2)}, u32[]{:S(2)}) collective-permute-start(bf16[256,512]{1,0:T(8,128)(2,1)S(1)} %get-tuple-element.42), channel_id=1, source_target_pairs={{0,2},{4,0},{8,4},{12,8},{14,12},{10,14},{6,10},{2,6},{1,3},{5,1},... | collective-permute-start | bytes 786440 | tf_op jit(solution)/shard_map/ppermute | solution.py:27
  5.2 12.5 %collective-permute-start.3 = (bf16[256,512]{1,0:T(8,128)(2,1)}, bf16[256,512]{1,0:T(8,128)(2,1)}, u32[]{:S(2)}, u32[]{:S(2)}) collective-permute-start(bf16[256,512]{1,0:T(8,128)(2,1)} %get-tuple-element.41), channel_id=1, source_target_pairs={{0,1},{1,0},{2,3},{3,2},{4,5},{5,4},{6,7},{7,6},{8,9},{9,8},{10,11... | collective-permute-start | bytes 786440 | tf_op jit(solution)/shard_map/ppermute | solution.py:39
  12.2 9.4 %collective-permute-start.2 = (s32[3,136]{1,0:T(4,128)S(1)}, s32[3,136]{1,0:T(4,128)S(1)}, u32[]{:S(2)}, u32[]{:S(2)}) collective-permute-start(s32[3,136]{1,0:T(4,128)S(1)} %pad_add_fusion.1), channel_id=1, source_target_pairs={{0,1},{1,0},{2,3},{3,2},{4,5},{5,4},{6,7},{7,6},{8,9},{9,8},{10,11... | collective-permute-start | bytes 4904 | tf_op jit(solution)/shard_map/ppermute | solution.py:39
  17.7 9.5 %collective-permute-start.5 = (bf16[256,512]{1,0:T(8,128)(2,1)}, bf16[256,512]{1,0:T(8,128)(2,1)}, u32[]{:S(2)}, u32[]{:S(2)}) collective-permute-start(bf16[256,512]{1,0:T(8,128)(2,1)} %collective-permute-done.3), channel_id=1, source_target_pairs={{0,4},{4,8},{8,12},{12,14},{14,10},{10,6},{6,2},{2,0},{1,5},{5,9},... | collective-permute-start | bytes 786440 | tf_op jit(solution)/shard_map/ppermute | solution.py:27
  19.6 9.5 %collective-permute-start.6 = (bf16[256,512]{1,0:T(8,128)(2,1)}, bf16[256,512]{1,0:T(8,128)(2,1)}, u32[]{:S(2)}, u32[]{:S(2)}) collective-permute-start(bf16[256,512]{1,0:T(8,128)(2,1)} %collective-permute-done.3), channel_id=1, source_target_pairs={{0,2},{4,0},{8,4},{12,8},{14,12},{10,14},{6,10},{2,6},{1,3},{5,1},... | collective-permute-start | bytes 786440 | tf_op jit(solution)/shard_map/ppermute | solution.py:27
  19.8 13.0 %collective-permute-start.7 = (bf16[256,512]{1,0:T(8,128)(2,1)}, bf16[256,512]{1,0:T(8,128)(2,1)}, u32[]{:S(2)}, u32[]{:S(2)}) collective-permute-start(bf16[256,512]{1,0:T(8,128)(2,1)} %collective-permute-done), channel_id=1, source_target_pairs={{0,4},{4,8},{8,12},{12,14},{14,10},{10,6},{6,2},{2,0},{1,5},{5,9},... | collective-permute-start | bytes 786440 | tf_op jit(solution)/shard_map/ppermute | solution.py:27
  21.6 13.0 %collective-permute-start.8 = (bf16[256,512]{1,0:T(8,128)(2,1)}, bf16[256,512]{1,0:T(8,128)(2,1)}, u32[]{:S(2)}, u32[]{:S(2)}) collective-permute-start(bf16[256,512]{1,0:T(8,128)(2,1)} %collective-permute-done.4), channel_id=1, source_target_pairs={{0,2},{4,0},{8,4},{12,8},{14,12},{10,14},{6,10},{2,6},{1,3},{5,1},... | collective-permute-start | bytes 786440 | tf_op jit(solution)/shard_map/ppermute | solution.py:27
  27.2 13.9 %collective-permute-start.9 = (bf16[256,512]{1,0:T(8,128)(2,1)}, bf16[256,512]{1,0:T(8,128)(2,1)}, u32[]{:S(2)}, u32[]{:S(2)}) collective-permute-start(bf16[256,512]{1,0:T(8,128)(2,1)} %collective-permute-done.5), channel_id=1, source_target_pairs={{0,4},{4,8},{8,12},{12,14},{14,10},{10,6},{6,2},{2,0},{1,5},{5,9},... | collective-permute-start | bytes 786440 | tf_op jit(solution)/shard_map/ppermute | solution.py:27
  29.0 14.0 %collective-permute-start.10 = (bf16[256,512]{1,0:T(8,128)(2,1)}, bf16[256,512]{1,0:T(8,128)(2,1)}, u32[]{:S(2)}, u32[]{:S(2)}) collective-permute-start(bf16[256,512]{1,0:T(8,128)(2,1)} %collective-permute-done.6), channel_id=1, source_target_pairs={{0,2},{4,0},{8,4},{12,8},{14,12},{10,14},{6,10},{2,6},{1,3},{5,1},... | collective-permute-start | bytes 786440 | tf_op jit(solution)/shard_map/ppermute | solution.py:27
  32.8 17.7 %collective-permute-start.11 = (bf16[256,512]{1,0:T(8,128)(2,1)}, bf16[256,512]{1,0:T(8,128)(2,1)}, u32[]{:S(2)}, u32[]{:S(2)}) collective-permute-start(bf16[256,512]{1,0:T(8,128)(2,1)} %collective-permute-done.7), channel_id=1, source_target_pairs={{0,4},{4,8},{8,12},{12,14},{14,10},{10,6},{6,2},{2,0},{1,5},{5,9},... | collective-permute-start | bytes 786440 | tf_op jit(solution)/shard_map/ppermute | solution.py:27
  34.6 31.3 %collective-permute-start.12 = (bf16[256,512]{1,0:T(8,128)(2,1)}, bf16[256,512]{1,0:T(8,128)(2,1)}, u32[]{:S(2)}, u32[]{:S(2)}) collective-permute-start(bf16[256,512]{1,0:T(8,128)(2,1)} %collective-permute-done.8), channel_id=1, source_target_pairs={{0,2},{4,0},{8,4},{12,8},{14,12},{10,14},{6,10},{2,6},{1,3},{5,1},... | collective-permute-start | bytes 786440 | tf_op jit(solution)/shard_map/ppermute | solution.py:27
  41.1 18.7 %collective-permute-start.13 = (bf16[256,512]{1,0:T(8,128)(2,1)}, bf16[256,512]{1,0:T(8,128)(2,1)S(1)}, u32[]{:S(2)}, u32[]{:S(2)}) collective-permute-start(bf16[256,512]{1,0:T(8,128)(2,1)} %collective-permute-done.9), channel_id=1, source_target_pairs={{0,4},{4,8},{8,12},{12,14},{14,10},{10,6},{6,2},{2,0},{1,5},{5,9},... | collective-permute-start | bytes 786440 | tf_op jit(solution)/shard_map/ppermute | solution.py:27
  43.0 16.2 %collective-permute-start.14 = (bf16[256,512]{1,0:T(8,128)(2,1)}, bf16[256,512]{1,0:T(8,128)(2,1)S(1)}, u32[]{:S(2)}, u32[]{:S(2)}) collective-permute-start(bf16[256,512]{1,0:T(8,128)(2,1)} %collective-permute-done.10), channel_id=1, source_target_pairs={{0,2},{4,0},{8,4},{12,8},{14,12},{10,14},{6,10},{2,6},{1,3},{5,1},... | collective-permute-start | bytes 786440 | tf_op jit(solution)/shard_map/ppermute | solution.py:27
  50.5 9.7 %collective-permute-start.15 = (bf16[256,512]{1,0:T(8,128)(2,1)}, bf16[256,512]{1,0:T(8,128)(2,1)S(1)}, u32[]{:S(2)}, u32[]{:S(2)}) collective-permute-start(bf16[256,512]{1,0:T(8,128)(2,1)} %collective-permute-done.11), channel_id=1, source_target_pairs={{0,4},{4,8},{8,12},{12,14},{14,10},{10,6},{6,2},{2,0},{1,5},{5,9},... | collective-permute-start | bytes 786440 | tf_op jit(solution)/shard_map/ppermute | solution.py:27
  73.6 8.6 %collective-permute-start.21 = (bf16[6,1024]{1,0:T(8,128)(2,1)S(1)}, bf16[6,1024]{1,0:T(8,128)(2,1)S(1)}, u32[]{:S(2)}, u32[]{:S(2)}) collective-permute-start(bf16[6,1024]{1,0:T(8,128)(2,1)S(1)} %maximum_select_fusion.2), channel_id=1, source_target_pairs={{28,0},{19,1},{30,4},{17,5},{26,8},{21,9},{22,12},{25,13},{18,14},... | collective-permute-start | bytes 36872 | tf_op jit(solution)/shard_map/ppermute | solution.py:51
  85.6 9.2 %collective-permute-start.31 = (bf16[256,512]{1,0:T(8,128)(2,1)S(1)}, bf16[256,512]{1,0:T(8,128)(2,1)S(1)}, u32[]{:S(2)}, u32[]{:S(2)}) collective-permute-start(bf16[256,512]{1,0:T(8,128)(2,1)S(1)} %convolution_convert_fusion.1), channel_id=1, source_target_pairs={{0,4},{4,8},{8,12},{12,14},{14,10},{10,6},{6,2},{2,0},{1,5},{5,9},... | collective-permute-start | bytes 786440 | tf_op jit(solution)/shard_map/ppermute | solution.py:27
  87.5 12.9 %collective-permute-start.23 = (bf16[256,512]{1,0:T(8,128)(2,1)S(1)}, bf16[256,512]{1,0:T(8,128)(2,1)S(1)}, u32[]{:S(2)}, u32[]{:S(2)}) collective-permute-start(bf16[256,512]{1,0:T(8,128)(2,1)S(1)} %convolution_convert_fusion.3), channel_id=1, source_target_pairs={{0,4},{4,8},{8,12},{12,14},{14,10},{10,6},{6,2},{2,0},{1,5},{5,9},... | collective-permute-start | bytes 786440 | tf_op jit(solution)/shard_map/ppermute | solution.py:27
  88.4 12.9 %collective-permute-start.34 = (bf16[256,512]{1,0:T(8,128)(2,1)S(1)}, bf16[256,512]{1,0:T(8,128)(2,1)S(1)}, u32[]{:S(2)}, u32[]{:S(2)}) collective-permute-start(bf16[256,512]{1,0:T(8,128)(2,1)S(1)} %convolution_convert_fusion), channel_id=1, source_target_pairs={{0,2},{4,0},{8,4},{12,8},{14,12},{10,14},{6,10},{2,6},{1,3},{5,1},... | collective-permute-start | bytes 786440 | tf_op jit(solution)/shard_map/ppermute | solution.py:27
  90.1 15.6 %collective-permute-start.28 = (bf16[256,512]{1,0:T(8,128)(2,1)S(1)}, bf16[256,512]{1,0:T(8,128)(2,1)S(1)}, u32[]{:S(2)}, u32[]{:S(2)}) collective-permute-start(bf16[256,512]{1,0:T(8,128)(2,1)S(1)} %convolution_convert_fusion.2), channel_id=1, source_target_pairs={{0,2},{4,0},{8,4},{12,8},{14,12},{10,14},{6,10},{2,6},{1,3},{5,1},... | collective-permute-start | bytes 786440 | tf_op jit(solution)/shard_map/ppermute | solution.py:27
  95.2 15.9 %collective-permute-start.32 = (bf16[256,512]{1,0:T(8,128)(2,1)S(1)}, bf16[256,512]{1,0:T(8,128)(2,1)S(1)}, u32[]{:S(2)}, u32[]{:S(2)}) collective-permute-start(bf16[256,512]{1,0:T(8,128)(2,1)S(1)} %add_convert_fusion.4), channel_id=1, source_target_pairs={{0,4},{4,8},{8,12},{12,14},{14,10},{10,6},{6,2},{2,0},{1,5},{5,9},... | collective-permute-start | bytes 786440 | tf_op jit(solution)/shard_map/ppermute | solution.py:27
  101.7 8.5 %collective-permute-start.35 = (bf16[256,512]{1,0:T(8,128)(2,1)S(1)}, bf16[256,512]{1,0:T(8,128)(2,1)S(1)}, u32[]{:S(2)}, u32[]{:S(2)}) collective-permute-start(bf16[256,512]{1,0:T(8,128)(2,1)S(1)} %add_convert_fusion.2), channel_id=1, source_target_pairs={{0,2},{4,0},{8,4},{12,8},{14,12},{10,14},{6,10},{2,6},{1,3},{5,1},... | collective-permute-start | bytes 786440 | tf_op jit(solution)/shard_map/ppermute | solution.py:27
  102.6 10.6 %collective-permute-start.25 = (bf16[256,512]{1,0:T(8,128)(2,1)S(1)}, bf16[256,512]{1,0:T(8,128)(2,1)S(1)}, u32[]{:S(2)}, u32[]{:S(2)}) collective-permute-start(bf16[256,512]{1,0:T(8,128)(2,1)S(1)} %add_convert_fusion.7), channel_id=1, source_target_pairs={{0,4},{4,8},{8,12},{12,14},{14,10},{10,6},{6,2},{2,0},{1,5},{5,9},... | collective-permute-start | bytes 786440 | tf_op jit(solution)/shard_map/ppermute | solution.py:27
  104.3 17.6 %collective-permute-start.24 = (bf16[256,1024]{1,0:T(8,128)(2,1)S(1)}, bf16[256,1024]{1,0:T(8,128)(2,1)S(1)}, u32[]{:S(2)}, u32[]{:S(2)}) collective-permute-start(bf16[256,1024]{1,0:T(8,128)(2,1)S(1)} %convert_element_type.155), channel_id=1, source_target_pairs={{0,16},{1,17},{2,18},{3,19},{4,20},{5,21},{6,22},{7,23},{8,24},{9,... | collective-permute-start | bytes 1572872 | tf_op jit(solution)/shard_map/ppermute | solution.py:35
  106.1 14.8 %collective-permute-start.29 = (bf16[256,512]{1,0:T(8,128)(2,1)S(1)}, bf16[256,512]{1,0:T(8,128)(2,1)S(1)}, u32[]{:S(2)}, u32[]{:S(2)}) collective-permute-start(bf16[256,512]{1,0:T(8,128)(2,1)S(1)} %add_convert_fusion.5), channel_id=1, source_target_pairs={{0,2},{4,0},{8,4},{12,8},{14,12},{10,14},{6,10},{2,6},{1,3},{5,1},... | collective-permute-start | bytes 786440 | tf_op jit(solution)/shard_map/ppermute | solution.py:27
  110.6 9.1 %collective-permute-start.36 = (bf16[256,512]{1,0:T(8,128)(2,1)S(1)}, bf16[256,512]{1,0:T(8,128)(2,1)S(1)}, u32[]{:S(2)}, u32[]{:S(2)}) collective-permute-start(bf16[256,512]{1,0:T(8,128)(2,1)S(1)} %add_convert_fusion.1), channel_id=1, source_target_pairs={{0,2},{4,0},{8,4},{12,8},{14,12},{10,14},{6,10},{2,6},{1,3},{5,1},... | collective-permute-start | bytes 786440 | tf_op jit(solution)/shard_map/ppermute | solution.py:27
  111.5 11.6 %collective-permute-start.33 = (bf16[256,512]{1,0:T(8,128)(2,1)S(1)}, bf16[256,512]{1,0:T(8,128)(2,1)S(1)}, u32[]{:S(2)}, u32[]{:S(2)}) collective-permute-start(bf16[256,512]{1,0:T(8,128)(2,1)S(1)} %add_convert_fusion.3), channel_id=1, source_target_pairs={{0,4},{4,8},{8,12},{12,14},{14,10},{10,6},{6,2},{2,0},{1,5},{5,9},... | collective-permute-start | bytes 786440 | tf_op jit(solution)/shard_map/ppermute | solution.py:27
  113.6 9.5 %collective-permute-start.26 = (bf16[256,512]{1,0:T(8,128)(2,1)S(1)}, bf16[256,512]{1,0:T(8,128)(2,1)S(1)}, u32[]{:S(2)}, u32[]{:S(2)}) collective-permute-start(bf16[256,512]{1,0:T(8,128)(2,1)S(1)} %add_convert_fusion.6), channel_id=1, source_target_pairs={{0,4},{4,8},{8,12},{12,14},{14,10},{10,6},{6,2},{2,0},{1,5},{5,9},... | collective-permute-start | bytes 786440 | tf_op jit(solution)/shard_map/ppermute | solution.py:27
  120.2 9.3 %collective-permute-start.37 = (bf16[256,512]{1,0:T(8,128)(2,1)S(1)}, bf16[256,512]{1,0:T(8,128)(2,1)S(1)}, u32[]{:S(2)}, u32[]{:S(2)}) collective-permute-start(bf16[256,512]{1,0:T(8,128)(2,1)S(1)} %add_convert_fusion), channel_id=1, source_target_pairs={{0,2},{4,0},{8,4},{12,8},{14,12},{10,14},{6,10},{2,6},{1,3},{5,1},... | collective-permute-start | bytes 786440 | tf_op jit(solution)/shard_map/ppermute | solution.py:27
  122.0 10.5 %collective-permute-start.30 = (bf16[256,512]{1,0:T(8,128)(2,1)}, bf16[256,512]{1,0:T(8,128)(2,1)S(1)}, u32[]{:S(2)}, u32[]{:S(2)}) collective-permute-start(bf16[256,512]{1,0:T(8,128)(2,1)} %convert_add_fusion.2), channel_id=1, source_target_pairs={{0,2},{4,0},{8,4},{12,8},{14,12},{10,14},{6,10},{2,6},{1,3},{5,1},... | collective-permute-start | bytes 786440 | tf_op jit(solution)/shard_map/ppermute | solution.py:27
  124.3 8.9 %collective-permute-start.27 = (bf16[256,512]{1,0:T(8,128)(2,1)}, bf16[256,512]{1,0:T(8,128)(2,1)S(1)}, u32[]{:S(2)}, u32[]{:S(2)}) collective-permute-start(bf16[256,512]{1,0:T(8,128)(2,1)} %convert_add_fusion.3), channel_id=1, source_target_pairs={{0,4},{4,8},{8,12},{12,14},{14,10},{10,6},{6,2},{2,0},{1,5},{5,9},... | collective-permute-start | bytes 786440 | tf_op jit(solution)/shard_map/ppermute | solution.py:27
  (14 other events, 80.6 us)

commit v12 on v11

--- a/solution.py
+++ b/solution.py
@@ -1,11 +1,16 @@
+import functools
+
 import jax
 import jax.numpy as jnp
 from jax import lax
+from jax.experimental import pallas as pl
+from jax.experimental.pallas import tpu as pltpu
 from jax.sharding import Mesh, PartitionSpec as P
 
 sharpness = 20.0
 cores = 2
 longest_ring = 16
+vmem_limit = 16 << 20
 
 
 def ring_order(chips):
@@ -60,10 +65,45 @@
     )
 
 
-def normalize(states, gain):
-    states_wide = states.astype(jnp.float32)
-    mean_square = jnp.mean(states_wide * states_wide, axis=-1, keepdims=True)
-    return (states_wide * lax.rsqrt(mean_square + 1e-05) * gain).astype(jnp.bfloat16)
+def normalize_kernel(seqs, chunk, mine_ref, other_ref, gain_ref, out_ref):
+    length = mine_ref.shape[1]
+
+    def run(ref):
+        @pl.loop(0, length // chunk)
+        def _(i):
+            at = pl.ds(pl.multiple_of(i * chunk, chunk), chunk)
+            wide = ref[0, at, :].astype(jnp.float32)
+            mean_square = jnp.mean(wide * wide, axis=-1, keepdims=True)
+            wide = wide * lax.rsqrt(mean_square + 1e-05) * gain_ref[...]
+            out_ref[at, :] = wide.astype(jnp.bfloat16)
+
+    @pl.when(pl.program_id(0) < seqs)
+    def _():
+        run(mine_ref)
+
+    @pl.when(pl.program_id(0) >= seqs)
+    def _():
+        run(other_ref)
+
+
+def normalize_both(mine, other, gain):
+    seqs, length, width = mine.shape
+    tokens = 2 * seqs * length
+    return pl.pallas_call(
+        functools.partial(normalize_kernel, seqs, 16),
+        grid=(2 * seqs,),
+        in_specs=[
+            pl.BlockSpec((1, length, width), lambda i: (jnp.minimum(i, seqs - 1), 0, 0)),
+            pl.BlockSpec((1, length, width), lambda i: (jnp.maximum(i - seqs, 0), 0, 0)),
+            pl.BlockSpec((1, width), lambda i: (0, 0)),
+        ],
+        out_specs=pl.BlockSpec((length, width), lambda i: (i, 0)),
+        out_shape=jax.ShapeDtypeStruct((tokens, width), jnp.bfloat16),
+        compiler_params=pltpu.CompilerParams(vmem_limit_bytes=vmem_limit),
+        cost_estimate=pl.CostEstimate(
+            flops=6 * tokens * width, bytes_accessed=4 * tokens * width, transcendentals=tokens
+        ),
+    )(mine, other, gain[None])
 
 
 def shards(token_states, token_ids, master, gain, cand_ids, slab_owner):
@@ -84,14 +124,14 @@
     given = given.astype(jnp.bfloat16)
     sibling = from_sibling(given)
 
-    first_sent = along_ring(own, 1)
     other_states = from_sibling(states)
-    normed_own = normalize(after(first_sent, states), gain)
-    normed_other = normalize(after(normed_own, other_states), gain)
-    ids, cand_ids = token_ids[0], after(first_sent, cand_ids)
-    slab_owner = after(first_sent, slab_owner)
-    normed = jnp.concatenate([normed_own, normed_other])
-    normed = normed.reshape(seqs * length, width)
+    parts = (core, 1 - core)
+    sent = [(0, 1), (0, -1), (1, 1), (1, -1)]
+    ids = token_ids[0]
+    if chips <= longest_ring:
+        moving = {(i, by): along_ring((own, sibling)[i], by) for i, by in sent}
+        states, cand_ids, slab_owner = after(moving[1, 1], (states, cand_ids, slab_owner))
+    normed = normalize_both(states, other_states, gain)
     ids = jnp.concatenate([ids, cand_ids], axis=1)
     ids = jnp.concatenate([ids, from_sibling(ids)])
     lengths = jnp.sum((ids[:, :length] != 0).astype(jnp.int32), axis=1)
@@ -105,23 +145,17 @@
     def product(offset, part, block):
         return jnp.dot(columns(offset, part), block, preferred_element_type=jnp.float32)
 
-    parts = (core, 1 - core)
     if chips <= longest_ring:
-        moving = {(i, by): block for by in (1, -1) for i, block in enumerate((own, sibling))}
         total = product(0, parts[0], own) + product(0, parts[1], sibling)
         sums = {}
         for step in range(1, chips // 2 + 1):
             last = step == chips // 2
-            sent = [(0, 1), (0, -1), (1, 1), (1, -1)]
             for i, by in [(0, 1), (1, -1)] if last else sent:
-                if (step, i, by) == (1, 0, 1):
-                    moving[i, by] = first_sent
-                else:
+                if step > 1:
                     if last and step > 2:
                         moving[i, by] = after(sums[1 + i], moving[i, by])
-                    elif step in (2, 3) and i == 1:
-                        norms = normed_own if step == 2 else normed_other
-                        moving[i, by] = after(norms, moving[i, by])
+                    elif step == 3 and i == 1:
+                        moving[i, by] = after(normed, moving[i, by])
                     moving[i, by] = along_ring(moving[i, by], by)
                 total = total + product(-by * step, parts[i], moving[i, by])
             sums[step] = total

time: 136 us -> 131 us (0.963)
  other arithmetic: 16.3 us -> 5.14 us
  Pallas kernels: 0 us -> 7.2 us
  waiting for transfers between devices: 50.2 us -> 47.3 us
  starting transfers between devices: 38.1 us -> 39.6 us
    pallas_call x0 -> x1, Pallas kernels: none -> 7.2 us  [normalize_both(): pl.pallas_call(functools.partial(normalize_kernel, seqs, 16), grid=(2 * s...]
    convert_element_type x2 -> x0, other arithmetic: 5.84 us -> none  [normalize(): (states_wide * lax.rsqrt(mean_square + 1e-05) * gain).astype(jnp.bfloat16)]
    reduce_sum x2 -> x0, other arithmetic: 5.17 us -> none  [normalize(): mean_square = jnp.mean(states_wide * states_wide, axis=-1, keepdims=True)]
    ppermute x4, waiting for transfers between devices: 7.29 us -> 5.23 us  [slab_blocks(): kept.append(lax.ppermute(stored, ('grp', 'chip', 'core'), pairs))]
    ppermute x28, waiting for transfers between devices: 41.2 us -> 39.1 us  [along_ring(): return lax.ppermute(block, 'chip', pairs)]
    ppermute x6, starting transfers between devices: 0.78 us -> 2.42 us  [from_sibling(): return lax.ppermute(block, 'core', [(0, 1), (1, 0)])]
  transfers between devices with their start and end apart: 39 -> 39, of which waited for: 16 -> 23; matrix products, arithmetic and copies ran while one was open for 28% -> 21% of each run, Pallas kernels for 0% -> 6%
where the time goes in v12:
time: 131 us; the launch traced here: 130 us
  waiting for transfers between devices  47.3 us (36%)
  starting transfers between devices  39.6 us (30%)
  matrix products  26.1 us (20%)
  Pallas kernels  7.2 us (5%)
  other arithmetic  5.14 us (4%)
  local copies, waits for them, and re-layouts  3.96 us (3%)
    ppermute x28, waiting for transfers between devices, along_ring(): return lax.ppermute(block, 'chip', pairs)  39.1 us
    ppermute x28, starting transfers between devices, along_ring(): return lax.ppermute(block, 'chip', pairs)  30.7 us
    dot_general x16, matrix products, product(): jnp.dot(columns(offset, part), block, preferred_element_type=jnp.float32)  17.3 us
    dot_general x16, matrix products, term(): lax.dot_general(columns(offset, part), delta, (((0,), (0,)), ((), ())), p...  7.28 us
    pallas_call x1, Pallas kernels, normalize_both(): pl.pallas_call(functools.partial(normalize_kernel, seqs, 16), grid=(2 * s...  7.2 us
    ppermute x4, waiting for transfers between devices, slab_blocks(): kept.append(lax.ppermute(stored, ('grp', 'chip', 'core'), pairs))  5.23 us
    ppermute x4, starting transfers between devices, slab_blocks(): kept.append(lax.ppermute(stored, ('grp', 'chip', 'core'), pairs))  5.16 us
    ppermute x6, waiting for transfers between devices, from_sibling(): return lax.ppermute(block, 'core', [(0, 1), (1, 0)])  2.91 us
  transfers between devices with their start and end apart: 39, of which 23 were waited for; matrix products, arithmetic and copies ran while one was open for 21% of the time, Pallas kernels for 6%

profile of v12, /device:TPU:0, one launch (start us, length us, event | category | flops | bytes accessed | tf_op | source)
XLA Modules:
  0.0 129.8 jit_solution(8709178057763476814)
XLA Ops:
  1.8 3.0 %collective-permute-start.5 = (bf16[256,512]{1,0:T(8,128)(2,1)S(1)}, bf16[256,512]{1,0:T(8,128)(2,1)}, u32[]{:S(2)}, u32[]{:S(2)}) collective-permute-start(bf16[256,512]{1,0:T(8,128)(2,1)S(1)} %get-tuple-element.35), channel_id=1, source_target_pairs={{0,2},{4,0},{8,4},{12,8},{14,12},{10,14},{6,10},{2,6},{1,3},{5,1},... | collective-permute-start | bytes 786440 | tf_op jit(solution)/shard_map/ppermute | solution.py:32
  4.9 1.4 %collective-permute-done = bf16[256,512]{1,0:T(8,128)(2,1)} collective-permute-done((bf16[256,512]{1,0:T(8,128)(2,1)S(1)}, bf16[256,512]{1,0:T(8,128)(2,1)}, u32[]{:S(2)}, u32[]{:S(2)}) %collective-permute-start) | collective-permute-done | bytes 262176 | tf_op jit(solution)/shard_map/ppermute | solution.py:44
  6.3 2.9 %collective-permute-start.1 = (bf16[256,512]{1,0:T(8,128)(2,1)}, bf16[256,512]{1,0:T(8,128)(2,1)}, u32[]{:S(2)}, u32[]{:S(2)}) collective-permute-start(bf16[256,512]{1,0:T(8,128)(2,1)} %collective-permute-done), channel_id=1, source_target_pairs={{0,4},{4,8},{8,12},{12,14},{14,10},{10,6},{6,2},{2,0},{1,5},{5,9},... | collective-permute-start | bytes 786440 | tf_op jit(solution)/shard_map/ppermute | solution.py:32
  9.9 1.6 %collective-permute-done.5 = bf16[256,512]{1,0:T(8,128)(2,1)} collective-permute-done((bf16[256,512]{1,0:T(8,128)(2,1)S(1)}, bf16[256,512]{1,0:T(8,128)(2,1)}, u32[]{:S(2)}, u32[]{:S(2)}) %collective-permute-start.5) | collective-permute-done | bytes 262176 | tf_op jit(solution)/shard_map/ppermute | solution.py:32
  11.5 1.9 %collective-permute-start.8 = (bf16[256,512]{1,0:T(8,128)(2,1)}, bf16[256,512]{1,0:T(8,128)(2,1)}, u32[]{:S(2)}, u32[]{:S(2)}) collective-permute-start(bf16[256,512]{1,0:T(8,128)(2,1)} %collective-permute-done.5), channel_id=1, source_target_pairs={{0,2},{4,0},{8,4},{12,8},{14,12},{10,14},{6,10},{2,6},{1,3},{5,1},... | collective-permute-start | bytes 786440 | tf_op jit(solution)/shard_map/ppermute | solution.py:32
  14.1 5.6 %collective-permute-done.1 = bf16[256,512]{1,0:T(8,128)(2,1)} collective-permute-done((bf16[256,512]{1,0:T(8,128)(2,1)}, bf16[256,512]{1,0:T(8,128)(2,1)}, u32[]{:S(2)}, u32[]{:S(2)}) %collective-permute-start.1) | collective-permute-done | bytes 262176 | tf_op jit(solution)/shard_map/ppermute | solution.py:32
  21.9 1.9 %collective-permute-done.8 = bf16[256,512]{1,0:T(8,128)(2,1)} collective-permute-done((bf16[256,512]{1,0:T(8,128)(2,1)}, bf16[256,512]{1,0:T(8,128)(2,1)}, u32[]{:S(2)}, u32[]{:S(2)}) %collective-permute-start.8) | collective-permute-done | bytes 262176 | tf_op jit(solution)/shard_map/ppermute | solution.py:32
  23.9 1.6 %collective-permute-start.9 = (bf16[256,512]{1,0:T(8,128)(2,1)}, bf16[256,512]{1,0:T(8,128)(2,1)}, u32[]{:S(2)}, u32[]{:S(2)}) collective-permute-start(bf16[256,512]{1,0:T(8,128)(2,1)} %collective-permute-done.1), channel_id=1, source_target_pairs={{0,4},{4,8},{8,12},{12,14},{14,10},{10,6},{6,2},{2,0},{1,5},{5,9},... | collective-permute-start | bytes 786440 | tf_op jit(solution)/shard_map/ppermute | solution.py:32
  25.9 1.6 %collective-permute-start.11 = (bf16[256,512]{1,0:T(8,128)(2,1)}, bf16[256,512]{1,0:T(8,128)(2,1)}, u32[]{:S(2)}, u32[]{:S(2)}) collective-permute-start(bf16[256,512]{1,0:T(8,128)(2,1)} %collective-permute-done.7), channel_id=1, source_target_pairs={{0,4},{4,8},{8,12},{12,14},{14,10},{10,6},{6,2},{2,0},{1,5},{5,9},... | collective-permute-start | bytes 786440 | tf_op jit(solution)/shard_map/ppermute | solution.py:32
  28.6 1.9 %copy-done = bf16[1,3,128,4096]{3,2,1,0:T(8,128)(2,1)S(1)} copy-done((bf16[1,3,128,4096]{3,2,1,0:T(8,128)(2,1)S(1)}, bf16[1,3,128,4096]{3,2,1,0:T(8,128)(2,1)}, u32[]{:S(2)}) %copy-start) | copy-done | bytes 3145752
  30.5 7.2 %shard_map.64 = bf16[768,4096]{1,0:T(8,128)(2,1)S(1)} custom-call(bf16[3,128,4096]{2,1,0:T(8,128)(2,1)S(1)} %bitcast.62, bf16[3,128,4096]{2,1,0:T(8,128)(2,1)S(1)} %collective-permute-done.2.other_ref, f32[1,4096]{1,0:T(1,128)S(1)} %bitcast.63), custom_call_target="tpu_custom_call" | custom-call | flops 18874368 | bytes 12582912 | tf_op jit(solution)/shard_map/pallas_call | solution.py:92
  44.0 1.6 %add_add_fusion.1 = f32[768,512]{1,0:T(8,128)S(1)} fusion(f32[768,512]{1,0:T(8,128)S(1)} %fusion.54, f32[768,512]{1,0:T(8,128)S(1)} %fusion.57, f32[768,512]{1,0:T(8,128)S(1)} %fusion.60, f32[768,512]{1,0:T(8,128)S(1)} %fusion.68, f32[768,512]{1,0:T(8,128)S(1)} %fusion.64, bf16[256,512]{1,0:T(8,128)(2,1)} %collective-permute-done.6, ...), kind=kOutput, calls=%fused_computation.6 | convolution fusion | flops 203292672 | bytes 10092548 | tf_op jit(solution)/shard_map/dot_general | solution.py:146
  45.6 1.5 %collective-permute-start.15 = (bf16[256,512]{1,0:T(8,128)(2,1)}, bf16[256,512]{1,0:T(8,128)(2,1)S(1)}, u32[]{:S(2)}, u32[]{:S(2)}) collective-permute-start(bf16[256,512]{1,0:T(8,128)(2,1)} %collective-permute-done.11), channel_id=1, source_target_pairs={{0,4},{4,8},{8,12},{12,14},{14,10},{10,6},{6,2},{2,0},{1,5},{5,9},... | collective-permute-start | bytes 786440 | tf_op jit(solution)/shard_map/ppermute | solution.py:32
  47.1 1.6 %collective-permute-start.13 = (bf16[256,512]{1,0:T(8,128)(2,1)}, bf16[256,512]{1,0:T(8,128)(2,1)S(1)}, u32[]{:S(2)}, u32[]{:S(2)}) collective-permute-start(bf16[256,512]{1,0:T(8,128)(2,1)} %collective-permute-done.9), channel_id=1, source_target_pairs={{0,4},{4,8},{8,12},{12,14},{14,10},{10,6},{6,2},{2,0},{1,5},{5,9},... | collective-permute-start | bytes 786440 | tf_op jit(solution)/shard_map/ppermute | solution.py:32
  52.7 1.6 %add_add_fusion = f32[768,512]{1,0:T(8,128)S(1)} fusion(f32[768,512]{1,0:T(8,128)S(1)} %fusion.40, f32[768,512]{1,0:T(8,128)S(1)} %fusion.43, f32[768,512]{1,0:T(8,128)S(1)} %add_add_fusion.1, f32[768,512]{1,0:T(8,128)S(1)} %fusion.46, bf16[256,512]{1,0:T(8,128)(2,1)} %collective-permute-done.10, bf16[768,4096]{1,0:T(8,128)(2,1)S(1)} %shard_map.64, ...), kind=kOutput, calls=%fused_computation.5 | convolution fusion | flops 202899456 | bytes 8519684 | tf_op jit(solution)/shard_map/dot_general | solution.py:146
  58.3 3.7 %collective-permute-done.16 = bf16[256,512]{1,0:T(8,128)(2,1)S(1)} collective-permute-done((bf16[256,512]{1,0:T(8,128)(2,1)S(1)}, bf16[256,512]{1,0:T(8,128)(2,1)S(1)}, u32[]{:S(2)}, u32[]{:S(2)}) %collective-permute-start.16) | collective-permute-done | bytes 262176 | tf_op jit(solution)/shard_map/ppermute | solution.py:32
  62.4 1.7 %add_tanh_fusion = f32[768,512]{1,0:T(8,128)S(1)} fusion(f32[768,512]{1,0:T(8,128)S(1)} %fusion.15, f32[768,512]{1,0:T(8,128)S(1)} %fusion.17, f32[768,512]{1,0:T(8,128)S(1)} %fusion.21, f32[768,512]{1,0:T(8,128)S(1)} %fusion.24, f32[768,512]{1,0:T(8,128)S(1)} %add_add_fusion, f32[768,512]{1,0:T(8,128)S(1)} %fusion.32, ...), kind=kOutput, calls=%fused_computation.4 | convolution fusion | flops 203685888 | bytes 11665412 | tf_op jit(solution)/shard_map/dot_general | solution.py:146
  71.1 3.1 %collective-permute-done.21 = bf16[6,1024]{1,0:T(8,128)(2,1)S(1)} collective-permute-done((bf16[6,1024]{1,0:T(8,128)(2,1)S(1)}, bf16[6,1024]{1,0:T(8,128)(2,1)S(1)}, u32[]{:S(2)}, u32[]{:S(2)}) %collective-permute-start.21) | collective-permute-done | bytes 12320 | tf_op jit(solution)/shard_map/ppermute | solution.py:56
  76.4 1.8 %collective-permute-start.22 = (bf16[24,1024]{1,0:T(8,128)(2,1)S(1)}, bf16[24,1024]{1,0:T(8,128)(2,1)S(1)}, u32[]{:S(2)}, u32[]{:S(2)}) collective-permute-start(bf16[24,1024]{1,0:T(8,128)(2,1)S(1)} %pad_maximum_fusion), channel_id=1, source_target_pairs={{0,1},{1,0},{2,3},{3,2},{4,5},{5,4},{6,7},{7,6},{8,9},{9,8},{10,11... | collective-permute-start | bytes 147464 | tf_op jit(solution)/shard_map/ppermute | solution.py:44
  81.6 2.1 %collective-permute-start.28 = (bf16[256,512]{1,0:T(8,128)(2,1)S(1)}, bf16[256,512]{1,0:T(8,128)(2,1)S(1)}, u32[]{:S(2)}, u32[]{:S(2)}) collective-permute-start(bf16[256,512]{1,0:T(8,128)(2,1)S(1)} %convolution_convert_fusion.2), channel_id=1, source_target_pairs={{0,2},{4,0},{8,4},{12,8},{14,12},{10,14},{6,10},{2,6},{1,3},{5,1},... | collective-permute-start | bytes 786440 | tf_op jit(solution)/shard_map/ppermute | solution.py:32
  84.6 1.6 %collective-permute-start.31 = (bf16[256,512]{1,0:T(8,128)(2,1)S(1)}, bf16[256,512]{1,0:T(8,128)(2,1)S(1)}, u32[]{:S(2)}, u32[]{:S(2)}) collective-permute-start(bf16[256,512]{1,0:T(8,128)(2,1)S(1)} %convolution_convert_fusion.1), channel_id=1, source_target_pairs={{0,4},{4,8},{8,12},{12,14},{14,10},{10,6},{6,2},{2,0},{1,5},{5,9},... | collective-permute-start | bytes 786440 | tf_op jit(solution)/shard_map/ppermute | solution.py:32
  86.2 4.1 %collective-permute-done.23 = bf16[256,512]{1,0:T(8,128)(2,1)S(1)} collective-permute-done((bf16[256,512]{1,0:T(8,128)(2,1)S(1)}, bf16[256,512]{1,0:T(8,128)(2,1)S(1)}, u32[]{:S(2)}, u32[]{:S(2)}) %collective-permute-start.23) | collective-permute-done | bytes 262176 | tf_op jit(solution)/shard_map/ppermute | solution.py:32
  93.8 2.7 %collective-permute-done.34 = bf16[256,512]{1,0:T(8,128)(2,1)S(1)} collective-permute-done((bf16[256,512]{1,0:T(8,128)(2,1)S(1)}, bf16[256,512]{1,0:T(8,128)(2,1)S(1)}, u32[]{:S(2)}, u32[]{:S(2)}) %collective-permute-start.34) | collective-permute-done | bytes 262176 | tf_op jit(solution)/shard_map/ppermute | solution.py:32
  96.9 2.1 %collective-permute-start.35 = (bf16[256,512]{1,0:T(8,128)(2,1)S(1)}, bf16[256,512]{1,0:T(8,128)(2,1)S(1)}, u32[]{:S(2)}, u32[]{:S(2)}) collective-permute-start(bf16[256,512]{1,0:T(8,128)(2,1)S(1)} %fusion.9), channel_id=1, source_target_pairs={{0,2},{4,0},{8,4},{12,8},{14,12},{10,14},{6,10},{2,6},{1,3},{5,1},... | collective-permute-start | bytes 786440 | tf_op jit(solution)/shard_map/ppermute | solution.py:32
  100.1 1.7 %collective-permute-start.32 = (bf16[256,512]{1,0:T(8,128)(2,1)S(1)}, bf16[256,512]{1,0:T(8,128)(2,1)S(1)}, u32[]{:S(2)}, u32[]{:S(2)}) collective-permute-start(bf16[256,512]{1,0:T(8,128)(2,1)S(1)} %fusion.6), channel_id=1, source_target_pairs={{0,4},{4,8},{8,12},{12,14},{14,10},{10,6},{6,2},{2,0},{1,5},{5,9},... | collective-permute-start | bytes 786440 | tf_op jit(solution)/shard_map/ppermute | solution.py:32
  101.8 5.3 %collective-permute-done.35 = bf16[256,512]{1,0:T(8,128)(2,1)S(1)} collective-permute-done((bf16[256,512]{1,0:T(8,128)(2,1)S(1)}, bf16[256,512]{1,0:T(8,128)(2,1)S(1)}, u32[]{:S(2)}, u32[]{:S(2)}) %collective-permute-start.35) | collective-permute-done | bytes 262176 | tf_op jit(solution)/shard_map/ppermute | solution.py:32
  107.5 1.8 %collective-permute-start.36 = (bf16[256,512]{1,0:T(8,128)(2,1)S(1)}, bf16[256,512]{1,0:T(8,128)(2,1)S(1)}, u32[]{:S(2)}, u32[]{:S(2)}) collective-permute-start(bf16[256,512]{1,0:T(8,128)(2,1)S(1)} %fusion.8), channel_id=1, source_target_pairs={{0,2},{4,0},{8,4},{12,8},{14,12},{10,14},{6,10},{2,6},{1,3},{5,1},... | collective-permute-start | bytes 786440 | tf_op jit(solution)/shard_map/ppermute | solution.py:32
  110.1 1.5 %collective-permute-done.32 = bf16[256,512]{1,0:T(8,128)(2,1)S(1)} collective-permute-done((bf16[256,512]{1,0:T(8,128)(2,1)S(1)}, bf16[256,512]{1,0:T(8,128)(2,1)S(1)}, u32[]{:S(2)}, u32[]{:S(2)}) %collective-permute-start.32) | collective-permute-done | bytes 262176 | tf_op jit(solution)/shard_map/ppermute | solution.py:32
  112.7 2.6 %collective-permute-done.36 = bf16[256,512]{1,0:T(8,128)(2,1)S(1)} collective-permute-done((bf16[256,512]{1,0:T(8,128)(2,1)S(1)}, bf16[256,512]{1,0:T(8,128)(2,1)S(1)}, u32[]{:S(2)}, u32[]{:S(2)}) %collective-permute-start.36) | collective-permute-done | bytes 262176 | tf_op jit(solution)/shard_map/ppermute | solution.py:32
  115.7 1.5 %collective-permute-start.37 = (bf16[256,512]{1,0:T(8,128)(2,1)S(1)}, bf16[256,512]{1,0:T(8,128)(2,1)S(1)}, u32[]{:S(2)}, u32[]{:S(2)}) collective-permute-start(bf16[256,512]{1,0:T(8,128)(2,1)S(1)} %fusion.7), channel_id=1, source_target_pairs={{0,2},{4,0},{8,4},{12,8},{14,12},{10,14},{6,10},{2,6},{1,3},{5,1},... | collective-permute-start | bytes 786440 | tf_op jit(solution)/shard_map/ppermute | solution.py:32
  120.8 3.8 %collective-permute-done.33 = bf16[256,512]{1,0:T(8,128)(2,1)S(1)} collective-permute-done((bf16[256,512]{1,0:T(8,128)(2,1)S(1)}, bf16[256,512]{1,0:T(8,128)(2,1)S(1)}, u32[]{:S(2)}, u32[]{:S(2)}) %collective-permute-start.33) | collective-permute-done | bytes 262176 | tf_op jit(solution)/shard_map/ppermute | solution.py:32
  125.2 3.0 %collective-permute-done.30 = bf16[256,512]{1,0:T(8,128)(2,1)S(1)} collective-permute-done((bf16[256,512]{1,0:T(8,128)(2,1)S(1)}, bf16[256,512]{1,0:T(8,128)(2,1)S(1)}, u32[]{:S(2)}, u32[]{:S(2)}) %collective-permute-start.30) | collective-permute-done | bytes 262176 | tf_op jit(solution)/shard_map/ppermute | solution.py:32
  (129 shorter events, 48.4 us)
Async XLA Ops:
  0.0 28.6 %collective-permute-start.2 = (bf16[3,128,4096]{2,1,0:T(8,128)(2,1)}, bf16[3,128,4096]{2,1,0:T(8,128)(2,1)S(1)}, u32[]{:S(2)}, u32[]{:S(2)}) collective-permute-start(bf16[3,128,4096]{2,1,0:T(8,128)(2,1)} %bitcast.61), channel_id=1, source_target_pairs={{0,1},{1,0},{2,3},{3,2},{4,5},{5,4},{6,7},{7,6},{8,9},{9,8},{10,11... | collective-permute-start | bytes 9437192 | tf_op jit(solution)/shard_map/ppermute | solution.py:44
  1.8 9.7 %collective-permute-start.5 = (bf16[256,512]{1,0:T(8,128)(2,1)S(1)}, bf16[256,512]{1,0:T(8,128)(2,1)}, u32[]{:S(2)}, u32[]{:S(2)}) collective-permute-start(bf16[256,512]{1,0:T(8,128)(2,1)S(1)} %get-tuple-element.35), channel_id=1, source_target_pairs={{0,2},{4,0},{8,4},{12,8},{14,12},{10,14},{6,10},{2,6},{1,3},{5,1},... | collective-permute-start | bytes 786440 | tf_op jit(solution)/shard_map/ppermute | solution.py:32
  4.8 9.3 %collective-permute-start.4 = (bf16[256,512]{1,0:T(8,128)(2,1)S(1)}, bf16[256,512]{1,0:T(8,128)(2,1)}, u32[]{:S(2)}, u32[]{:S(2)}) collective-permute-start(bf16[256,512]{1,0:T(8,128)(2,1)S(1)} %get-tuple-element.35), channel_id=1, source_target_pairs={{0,4},{4,8},{8,12},{12,14},{14,10},{10,6},{6,2},{2,0},{1,5},{5,9},... | collective-permute-start | bytes 786440 | tf_op jit(solution)/shard_map/ppermute | solution.py:32
  6.3 13.5 %collective-permute-start.1 = (bf16[256,512]{1,0:T(8,128)(2,1)}, bf16[256,512]{1,0:T(8,128)(2,1)}, u32[]{:S(2)}, u32[]{:S(2)}) collective-permute-start(bf16[256,512]{1,0:T(8,128)(2,1)} %collective-permute-done), channel_id=1, source_target_pairs={{0,4},{4,8},{8,12},{12,14},{14,10},{10,6},{6,2},{2,0},{1,5},{5,9},... | collective-permute-start | bytes 786440 | tf_op jit(solution)/shard_map/ppermute | solution.py:32
  9.9 15.6 %collective-permute-start.6 = (bf16[256,512]{1,0:T(8,128)(2,1)}, bf16[256,512]{1,0:T(8,128)(2,1)}, u32[]{:S(2)}, u32[]{:S(2)}) collective-permute-start(bf16[256,512]{1,0:T(8,128)(2,1)} %collective-permute-done), channel_id=1, source_target_pairs={{0,2},{4,0},{8,4},{12,8},{14,12},{10,14},{6,10},{2,6},{1,3},{5,1},... | collective-permute-start | bytes 786440 | tf_op jit(solution)/shard_map/ppermute | solution.py:32
  11.5 12.4 %collective-permute-start.8 = (bf16[256,512]{1,0:T(8,128)(2,1)}, bf16[256,512]{1,0:T(8,128)(2,1)}, u32[]{:S(2)}, u32[]{:S(2)}) collective-permute-start(bf16[256,512]{1,0:T(8,128)(2,1)} %collective-permute-done.5), channel_id=1, source_target_pairs={{0,2},{4,0},{8,4},{12,8},{14,12},{10,14},{6,10},{2,6},{1,3},{5,1},... | collective-permute-start | bytes 786440 | tf_op jit(solution)/shard_map/ppermute | solution.py:32
  14.1 11.8 %collective-permute-start.7 = (bf16[256,512]{1,0:T(8,128)(2,1)}, bf16[256,512]{1,0:T(8,128)(2,1)}, u32[]{:S(2)}, u32[]{:S(2)}) collective-permute-start(bf16[256,512]{1,0:T(8,128)(2,1)} %collective-permute-done.4), channel_id=1, source_target_pairs={{0,4},{4,8},{8,12},{12,14},{14,10},{10,6},{6,2},{2,0},{1,5},{5,9},... | collective-permute-start | bytes 786440 | tf_op jit(solution)/shard_map/ppermute | solution.py:32
  20.4 7.1 %collective-permute-start.3 = (s32[3,136]{1,0:T(4,128)S(1)}, s32[3,136]{1,0:T(4,128)S(1)}, u32[]{:S(2)}, u32[]{:S(2)}) collective-permute-start(s32[3,136]{1,0:T(4,128)S(1)} %pad_add_fusion.1), channel_id=1, source_target_pairs={{0,1},{1,0},{2,3},{3,2},{4,5},{5,4},{6,7},{7,6},{8,9},{9,8},{10,11... | collective-permute-start | bytes 4904 | tf_op jit(solution)/shard_map/ppermute | solution.py:44
  23.9 23.2 %collective-permute-start.9 = (bf16[256,512]{1,0:T(8,128)(2,1)}, bf16[256,512]{1,0:T(8,128)(2,1)}, u32[]{:S(2)}, u32[]{:S(2)}) collective-permute-start(bf16[256,512]{1,0:T(8,128)(2,1)} %collective-permute-done.1), channel_id=1, source_target_pairs={{0,4},{4,8},{8,12},{12,14},{14,10},{10,6},{6,2},{2,0},{1,5},{5,9},... | collective-permute-start | bytes 786440 | tf_op jit(solution)/shard_map/ppermute | solution.py:32
  25.5 12.6 %collective-permute-start.10 = (bf16[256,512]{1,0:T(8,128)(2,1)}, bf16[256,512]{1,0:T(8,128)(2,1)}, u32[]{:S(2)}, u32[]{:S(2)}) collective-permute-start(bf16[256,512]{1,0:T(8,128)(2,1)} %collective-permute-done.6), channel_id=1, source_target_pairs={{0,2},{4,0},{8,4},{12,8},{14,12},{10,14},{6,10},{2,6},{1,3},{5,1},... | collective-permute-start | bytes 786440 | tf_op jit(solution)/shard_map/ppermute | solution.py:32
  25.9 19.7 %collective-permute-start.11 = (bf16[256,512]{1,0:T(8,128)(2,1)}, bf16[256,512]{1,0:T(8,128)(2,1)}, u32[]{:S(2)}, u32[]{:S(2)}) collective-permute-start(bf16[256,512]{1,0:T(8,128)(2,1)} %collective-permute-done.7), channel_id=1, source_target_pairs={{0,4},{4,8},{8,12},{12,14},{14,10},{10,6},{6,2},{2,0},{1,5},{5,9},... | collective-permute-start | bytes 786440 | tf_op jit(solution)/shard_map/ppermute | solution.py:32
  27.5 34.9 %collective-permute-start.12 = (bf16[256,512]{1,0:T(8,128)(2,1)}, bf16[256,512]{1,0:T(8,128)(2,1)}, u32[]{:S(2)}, u32[]{:S(2)}) collective-permute-start(bf16[256,512]{1,0:T(8,128)(2,1)} %collective-permute-done.8), channel_id=1, source_target_pairs={{0,2},{4,0},{8,4},{12,8},{14,12},{10,14},{6,10},{2,6},{1,3},{5,1},... | collective-permute-start | bytes 786440 | tf_op jit(solution)/shard_map/ppermute | solution.py:32
  38.1 17.5 %collective-permute-start.14 = (bf16[256,512]{1,0:T(8,128)(2,1)}, bf16[256,512]{1,0:T(8,128)(2,1)S(1)}, u32[]{:S(2)}, u32[]{:S(2)}) collective-permute-start(bf16[256,512]{1,0:T(8,128)(2,1)} %collective-permute-done.10), channel_id=1, source_target_pairs={{0,2},{4,0},{8,4},{12,8},{14,12},{10,14},{6,10},{2,6},{1,3},{5,1},... | collective-permute-start | bytes 786440 | tf_op jit(solution)/shard_map/ppermute | solution.py:32
  45.6 10.9 %collective-permute-start.15 = (bf16[256,512]{1,0:T(8,128)(2,1)}, bf16[256,512]{1,0:T(8,128)(2,1)S(1)}, u32[]{:S(2)}, u32[]{:S(2)}) collective-permute-start(bf16[256,512]{1,0:T(8,128)(2,1)} %collective-permute-done.11), channel_id=1, source_target_pairs={{0,4},{4,8},{8,12},{12,14},{14,10},{10,6},{6,2},{2,0},{1,5},{5,9},... | collective-permute-start | bytes 786440 | tf_op jit(solution)/shard_map/ppermute | solution.py:32
  47.1 10.8 %collective-permute-start.13 = (bf16[256,512]{1,0:T(8,128)(2,1)}, bf16[256,512]{1,0:T(8,128)(2,1)S(1)}, u32[]{:S(2)}, u32[]{:S(2)}) collective-permute-start(bf16[256,512]{1,0:T(8,128)(2,1)} %collective-permute-done.9), channel_id=1, source_target_pairs={{0,4},{4,8},{8,12},{12,14},{14,10},{10,6},{6,2},{2,0},{1,5},{5,9},... | collective-permute-start | bytes 786440 | tf_op jit(solution)/shard_map/ppermute | solution.py:32
  65.9 8.3 %collective-permute-start.21 = (bf16[6,1024]{1,0:T(8,128)(2,1)S(1)}, bf16[6,1024]{1,0:T(8,128)(2,1)S(1)}, u32[]{:S(2)}, u32[]{:S(2)}) collective-permute-start(bf16[6,1024]{1,0:T(8,128)(2,1)S(1)} %maximum_select_fusion.2), channel_id=1, source_target_pairs={{28,0},{19,1},{30,4},{17,5},{26,8},{21,9},{22,12},{25,13},{18,14},... | collective-permute-start | bytes 36872 | tf_op jit(solution)/shard_map/ppermute | solution.py:56
  67.2 7.4 %collective-permute-start.20 = (bf16[6,1024]{1,0:T(8,128)(2,1)S(1)}, bf16[6,1024]{1,0:T(8,128)(2,1)S(1)}, u32[]{:S(2)}, u32[]{:S(2)}) collective-permute-start(bf16[6,1024]{1,0:T(8,128)(2,1)S(1)} %maximum_select_fusion.2), channel_id=1, source_target_pairs={{24,0},{23,1},{28,4},{19,5},{30,8},{17,9},{26,12},{21,13},{22,14},... | collective-permute-start | bytes 36872 | tf_op jit(solution)/shard_map/ppermute | solution.py:56
  81.1 9.2 %collective-permute-start.23 = (bf16[256,512]{1,0:T(8,128)(2,1)S(1)}, bf16[256,512]{1,0:T(8,128)(2,1)S(1)}, u32[]{:S(2)}, u32[]{:S(2)}) collective-permute-start(bf16[256,512]{1,0:T(8,128)(2,1)S(1)} %convolution_convert_fusion.3), channel_id=1, source_target_pairs={{0,4},{4,8},{8,12},{12,14},{14,10},{10,6},{6,2},{2,0},{1,5},{5,9},... | collective-permute-start | bytes 786440 | tf_op jit(solution)/shard_map/ppermute | solution.py:32
  81.6 10.5 %collective-permute-start.28 = (bf16[256,512]{1,0:T(8,128)(2,1)S(1)}, bf16[256,512]{1,0:T(8,128)(2,1)S(1)}, u32[]{:S(2)}, u32[]{:S(2)}) collective-permute-start(bf16[256,512]{1,0:T(8,128)(2,1)S(1)} %convolution_convert_fusion.2), channel_id=1, source_target_pairs={{0,2},{4,0},{8,4},{12,8},{14,12},{10,14},{6,10},{2,6},{1,3},{5,1},... | collective-permute-start | bytes 786440 | tf_op jit(solution)/shard_map/ppermute | solution.py:32
  84.1 12.3 %collective-permute-start.34 = (bf16[256,512]{1,0:T(8,128)(2,1)S(1)}, bf16[256,512]{1,0:T(8,128)(2,1)S(1)}, u32[]{:S(2)}, u32[]{:S(2)}) collective-permute-start(bf16[256,512]{1,0:T(8,128)(2,1)S(1)} %convolution_convert_fusion), channel_id=1, source_target_pairs={{0,2},{4,0},{8,4},{12,8},{14,12},{10,14},{6,10},{2,6},{1,3},{5,1},... | collective-permute-start | bytes 786440 | tf_op jit(solution)/shard_map/ppermute | solution.py:32
  84.6 15.0 %collective-permute-start.31 = (bf16[256,512]{1,0:T(8,128)(2,1)S(1)}, bf16[256,512]{1,0:T(8,128)(2,1)S(1)}, u32[]{:S(2)}, u32[]{:S(2)}) collective-permute-start(bf16[256,512]{1,0:T(8,128)(2,1)S(1)} %convolution_convert_fusion.1), channel_id=1, source_target_pairs={{0,4},{4,8},{8,12},{12,14},{14,10},{10,6},{6,2},{2,0},{1,5},{5,9},... | collective-permute-start | bytes 786440 | tf_op jit(solution)/shard_map/ppermute | solution.py:32
  90.4 27.2 %collective-permute-start.24 = (bf16[256,1024]{1,0:T(8,128)(2,1)S(1)}, bf16[256,1024]{1,0:T(8,128)(2,1)S(1)}, u32[]{:S(2)}, u32[]{:S(2)}) collective-permute-start(bf16[256,1024]{1,0:T(8,128)(2,1)S(1)} %convert_element_type.139), channel_id=1, source_target_pairs={{0,16},{1,17},{2,18},{3,19},{4,20},{5,21},{6,22},{7,23},{8,24},{9,... | collective-permute-start | bytes 1572872 | tf_op jit(solution)/shard_map/ppermute | solution.py:40
  92.6 24.6 %collective-permute-start.29 = (bf16[256,512]{1,0:T(8,128)(2,1)S(1)}, bf16[256,512]{1,0:T(8,128)(2,1)S(1)}, u32[]{:S(2)}, u32[]{:S(2)}) collective-permute-start(bf16[256,512]{1,0:T(8,128)(2,1)S(1)} %fusion.4), channel_id=1, source_target_pairs={{0,2},{4,0},{8,4},{12,8},{14,12},{10,14},{6,10},{2,6},{1,3},{5,1},... | collective-permute-start | bytes 786440 | tf_op jit(solution)/shard_map/ppermute | solution.py:32
  96.9 10.2 %collective-permute-start.35 = (bf16[256,512]{1,0:T(8,128)(2,1)S(1)}, bf16[256,512]{1,0:T(8,128)(2,1)S(1)}, u32[]{:S(2)}, u32[]{:S(2)}) collective-permute-start(bf16[256,512]{1,0:T(8,128)(2,1)S(1)} %fusion.9), channel_id=1, source_target_pairs={{0,2},{4,0},{8,4},{12,8},{14,12},{10,14},{6,10},{2,6},{1,3},{5,1},... | collective-permute-start | bytes 786440 | tf_op jit(solution)/shard_map/ppermute | solution.py:32
  99.4 9.9 %collective-permute-start.25 = (bf16[256,512]{1,0:T(8,128)(2,1)S(1)}, bf16[256,512]{1,0:T(8,128)(2,1)S(1)}, u32[]{:S(2)}, u32[]{:S(2)}) collective-permute-start(bf16[256,512]{1,0:T(8,128)(2,1)S(1)} %fusion.3), channel_id=1, source_target_pairs={{0,4},{4,8},{8,12},{12,14},{14,10},{10,6},{6,2},{2,0},{1,5},{5,9},... | collective-permute-start | bytes 786440 | tf_op jit(solution)/shard_map/ppermute | solution.py:32
  100.1 11.5 %collective-permute-start.32 = (bf16[256,512]{1,0:T(8,128)(2,1)S(1)}, bf16[256,512]{1,0:T(8,128)(2,1)S(1)}, u32[]{:S(2)}, u32[]{:S(2)}) collective-permute-start(bf16[256,512]{1,0:T(8,128)(2,1)S(1)} %fusion.6), channel_id=1, source_target_pairs={{0,4},{4,8},{8,12},{12,14},{14,10},{10,6},{6,2},{2,0},{1,5},{5,9},... | collective-permute-start | bytes 786440 | tf_op jit(solution)/shard_map/ppermute | solution.py:32
  107.5 7.8 %collective-permute-start.36 = (bf16[256,512]{1,0:T(8,128)(2,1)S(1)}, bf16[256,512]{1,0:T(8,128)(2,1)S(1)}, u32[]{:S(2)}, u32[]{:S(2)}) collective-permute-start(bf16[256,512]{1,0:T(8,128)(2,1)S(1)} %fusion.8), channel_id=1, source_target_pairs={{0,2},{4,0},{8,4},{12,8},{14,12},{10,14},{6,10},{2,6},{1,3},{5,1},... | collective-permute-start | bytes 786440 | tf_op jit(solution)/shard_map/ppermute | solution.py:32
  109.7 9.3 %collective-permute-start.26 = (bf16[256,512]{1,0:T(8,128)(2,1)S(1)}, bf16[256,512]{1,0:T(8,128)(2,1)S(1)}, u32[]{:S(2)}, u32[]{:S(2)}) collective-permute-start(bf16[256,512]{1,0:T(8,128)(2,1)S(1)} %fusion.2), channel_id=1, source_target_pairs={{0,4},{4,8},{8,12},{12,14},{14,10},{10,6},{6,2},{2,0},{1,5},{5,9},... | collective-permute-start | bytes 786440 | tf_op jit(solution)/shard_map/ppermute | solution.py:32
  112.0 12.6 %collective-permute-start.33 = (bf16[256,512]{1,0:T(8,128)(2,1)S(1)}, bf16[256,512]{1,0:T(8,128)(2,1)S(1)}, u32[]{:S(2)}, u32[]{:S(2)}) collective-permute-start(bf16[256,512]{1,0:T(8,128)(2,1)S(1)} %fusion.5), channel_id=1, source_target_pairs={{0,4},{4,8},{8,12},{12,14},{14,10},{10,6},{6,2},{2,0},{1,5},{5,9},... | collective-permute-start | bytes 786440 | tf_op jit(solution)/shard_map/ppermute | solution.py:32
  115.7 9.3 %collective-permute-start.37 = (bf16[256,512]{1,0:T(8,128)(2,1)S(1)}, bf16[256,512]{1,0:T(8,128)(2,1)S(1)}, u32[]{:S(2)}, u32[]{:S(2)}) collective-permute-start(bf16[256,512]{1,0:T(8,128)(2,1)S(1)} %fusion.7), channel_id=1, source_target_pairs={{0,2},{4,0},{8,4},{12,8},{14,12},{10,14},{6,10},{2,6},{1,3},{5,1},... | collective-permute-start | bytes 786440 | tf_op jit(solution)/shard_map/ppermute | solution.py:32
  117.6 10.6 %collective-permute-start.30 = (bf16[256,512]{1,0:T(8,128)(2,1)S(1)}, bf16[256,512]{1,0:T(8,128)(2,1)S(1)}, u32[]{:S(2)}, u32[]{:S(2)}) collective-permute-start(bf16[256,512]{1,0:T(8,128)(2,1)S(1)} %convolution_add_fusion.6), channel_id=1, source_target_pairs={{0,2},{4,0},{8,4},{12,8},{14,12},{10,14},{6,10},{2,6},{1,3},{5,1},... | collective-permute-start | bytes 786440 | tf_op jit(solution)/shard_map/ppermute | solution.py:32
  120.1 8.2 %collective-permute-start.27 = (bf16[256,512]{1,0:T(8,128)(2,1)}, bf16[256,512]{1,0:T(8,128)(2,1)S(1)}, u32[]{:S(2)}, u32[]{:S(2)}) collective-permute-start(bf16[256,512]{1,0:T(8,128)(2,1)} %convolution_add_fusion.9), channel_id=1, source_target_pairs={{0,4},{4,8},{8,12},{12,14},{14,10},{10,6},{6,2},{2,0},{1,5},{5,9},... | collective-permute-start | bytes 786440 | tf_op jit(solution)/shard_map/ppermute | solution.py:32
  (13 other events, 109.7 us)

commit v13 on v12

--- a/solution.py
+++ b/solution.py
@@ -38,6 +38,14 @@
 
 def passed_on(weights):
     return lax.ppermute(weights.astype(jnp.bfloat16), "grp", [(0, 1)])
+
+
+def cut(array, axis, start, size):
+    starts = [0] * array.ndim
+    starts[axis] = start
+    sizes = list(array.shape)
+    sizes[axis] = size
+    return lax.dynamic_slice(array, starts, sizes, allow_negative_indices=False)
 
 
 def from_sibling(block):
@@ -57,9 +65,9 @@
     return kept
 
 
-def in_core_order(mine, other, core, axis=0):
+def in_core_order(mine, other, first_core, axis=0):
     return jnp.where(
-        core == 0,
+        first_core,
         jnp.concatenate([mine, other], axis=axis),
         jnp.concatenate([other, mine], axis=axis),
     )
@@ -118,35 +126,50 @@
     half = embedding // cores
     seqs = cores * seq_dev
 
-    weights = master[0]
-    own = lax.dynamic_slice(weights, (0, core * half), (rows, half)).astype(jnp.bfloat16)
-    given = lax.dynamic_slice(weights, (0, (1 - core) * half), (rows, half))
-    given = given.astype(jnp.bfloat16)
+    first_core = core == 0
+    shift = place + core * (chips // cores)
+    own_columns, given_columns = core * half, (1 - core) * half
+    parts = (core, 1 - core)
+    span = chips // 2 if chips <= longest_ring else 0
+    starts = {
+        (offset, i): (ring_chip(place + offset, chips) * cores + parts[i]) * rows
+        for offset in range(-span, span + 1)
+        for i in range(2)
+    }
+    scalars = [first_core, shift, own_columns, given_columns, trainer, *starts.values()]
+    weights, *scalars = lax.optimization_barrier([master[0], *scalars])
+    first_core, shift, own_columns, given_columns, trainer, *firsts = scalars
+    starts = dict(zip(starts, firsts))
+    own = cut(weights, 1, own_columns, half).astype(jnp.bfloat16)
+    given = cut(weights, 1, given_columns, half).astype(jnp.bfloat16)
     sibling = from_sibling(given)
 
     other_states = from_sibling(states)
-    parts = (core, 1 - core)
     sent = [(0, 1), (0, -1), (1, 1), (1, -1)]
     ids = token_ids[0]
     if chips <= longest_ring:
         moving = {(i, by): along_ring((own, sibling)[i], by) for i, by in sent}
-        states, cand_ids, slab_owner = after(moving[1, 1], (states, cand_ids, slab_owner))
+        cand_ids, slab_owner = after(moving[1, 1], (cand_ids, slab_owner))
     normed = normalize_both(states, other_states, gain)
-    ids = jnp.concatenate([ids, cand_ids], axis=1)
+    slab_rows = slab_owner.shape[0]
+    slab_ids = jnp.arange(slab_rows, dtype=jnp.int32)[None, :]
+    picked = [
+        (cand_ids[:, j : j + 1] == slab_ids).astype(jnp.int32) for j in range(cand_ids.shape[1])
+    ]
+    ids = jnp.concatenate([ids, sum(picked), picked[0]], axis=1)
     ids = jnp.concatenate([ids, from_sibling(ids)])
     lengths = jnp.sum((ids[:, :length] != 0).astype(jnp.int32), axis=1)
     counts = lengths.astype(jnp.float32)
-    cands = ids[:, length:]
-
-    def columns(offset, part):
-        first = (ring_chip(place + offset, chips) * cores + part) * rows
-        return lax.dynamic_slice(normed, (0, first), (seqs * length, rows))
-
-    def product(offset, part, block):
-        return jnp.dot(columns(offset, part), block, preferred_element_type=jnp.float32)
+    masks = ids[:, length:].astype(jnp.float32)
+
+    def columns(offset, i):
+        return cut(normed, 1, starts[offset, i], rows)
+
+    def product(offset, i, block):
+        return jnp.dot(columns(offset, i), block, preferred_element_type=jnp.float32)
 
     if chips <= longest_ring:
-        total = product(0, parts[0], own) + product(0, parts[1], sibling)
+        total = product(0, 0, own) + product(0, 1, sibling)
         sums = {}
         for step in range(1, chips // 2 + 1):
             last = step == chips // 2
@@ -157,10 +180,10 @@
                     elif step == 3 and i == 1:
                         moving[i, by] = after(normed, moving[i, by])
                     moving[i, by] = along_ring(moving[i, by], by)
-                total = total + product(-by * step, parts[i], moving[i, by])
+                total = total + product(-by * step, i, moving[i, by])
             sums[step] = total
     else:
-        both = in_core_order(own, sibling, core)
+        both = in_core_order(own, sibling, first_core)
         gathered = lax.all_gather(both, "chip", axis=0, tiled=True)
         total = jnp.dot(normed, gathered, preferred_element_type=jnp.float32)
 
@@ -169,27 +192,25 @@
     pooled = jnp.sum(jnp.where(there, active, 0.0), axis=1) / counts[:, None]
     pooled_other = from_sibling(pooled)
     pooled_other = jnp.concatenate([pooled_other[seq_dev:], pooled_other[:seq_dev]])
-    whole = in_core_order(pooled, pooled_other, core, axis=1)
+    whole = in_core_order(pooled, pooled_other, first_core, axis=1)
     pooled_square = jnp.mean(whole * whole, axis=-1, keepdims=True)
     scale = lax.rsqrt(pooled_square + 1e-06)
     unit = whole * scale
     stored = unit.astype(jnp.bfloat16)
-    stored = in_core_order(stored[:seq_dev], stored[seq_dev:], core)
+    stored = in_core_order(stored[:seq_dev], stored[seq_dev:], first_core)
 
     kept = slab_blocks(stored, chips)
     kept = jnp.concatenate(kept)
     slab = [kept, from_sibling(kept)]
-    slab_rows = slab_owner.shape[0]
     earlier = jnp.arange(slab_rows)[:, None] < jnp.arange(slab_rows)[None, :]
     same = slab_owner[:, None] == slab_owner[None, :]
     ranks = jnp.sum((earlier & same).astype(jnp.int32), axis=0)
     owner_place = ring_place(slab_owner // cores, chips)
-    seen = lax.rem(owner_place - place - core * (chips // cores) + 2 * chips, chips)
+    seen = lax.rem(owner_place - shift + 2 * chips, chips)
     slots = seen * seqs + lax.rem(slab_owner, cores) * seq_dev + ranks
     moved = (slots[:, None] == jnp.arange(slab_rows)[None, :]).astype(jnp.float32)
-    picked = (cands[:, :, None] == jnp.arange(slab_rows)).astype(jnp.float32)
-    positive = jnp.dot(picked[:, 0], moved)
-    candidate = jnp.dot(jnp.sum(picked, axis=1), moved)
+    candidate = jnp.dot(masks[:, :slab_rows], moved)
+    positive = jnp.dot(masks[:, slab_rows:], moved)
     piece = slab_rows // cores
     pieces = [slice(i * piece, (i + 1) * piece) for i in range(cores)]
 
@@ -213,14 +234,14 @@
     )
     inner = jnp.sum(whole * unit_grad, axis=-1, keepdims=True)
     pooled_grad = scale * unit_grad - whole * (scale * scale * scale) * inner / embedding
-    pooled_grad = lax.dynamic_slice(pooled_grad, (0, core * half), (seqs, half))
+    pooled_grad = cut(pooled_grad, 1, own_columns, half)
     delta = (pooled_grad / counts[:, None])[:, None, :] * (1.0 - active * active)
     delta = jnp.where(there, delta, 0.0)
     delta = delta.astype(jnp.bfloat16).reshape(seqs * length, half)
 
-    def term(offset, part, delta):
+    def term(offset, i, delta):
         return lax.dot_general(
-            columns(offset, part),
+            columns(offset, i),
             delta,
             (((0,), (0,)), ((), ())),
             preferred_element_type=jnp.float32,
@@ -233,7 +254,7 @@
             for i, by in ((0, 1), (1, -1), (1, 1), (0, -1)):
                 if step == chips // 2 and (i, by) not in ((0, 1), (1, -1)):
                     continue
-                total = term(by * step, parts[i], delta)
+                total = term(by * step, i, delta)
                 if (i, by) in arrived:
                     total = total + arrived[i, by].astype(jnp.float32)
                 if step == 1 and i == 0:
@@ -242,7 +263,7 @@
             if step == chips // 2:
                 late, weights = after(arrived[0, 1], (delta, weights))
                 copied = passed_on(weights)
-        owns = [term(0, parts[i], late) for i in range(2)]
+        owns = [term(0, i, late) for i in range(2)]
         arrived[1, 1] = after(owns, arrived[1, 1])
         arrived[0, -1] = after(owns, arrived[0, -1])
         mine, other = [
@@ -255,9 +276,9 @@
         )
         copied = passed_on(weights)
         reduced = lax.psum_scatter(grad, "chip", scatter_dimension=0, tiled=True)
-        mine, other = [lax.dynamic_slice(reduced, (i * rows, 0), (rows, half)) for i in parts]
+        mine, other = [cut(reduced, 0, part * rows, rows) for part in parts]
     other = from_sibling(other)
-    shard = in_core_order(mine, other, core, axis=1)
+    shard = in_core_order(mine, other, first_core, axis=1)
     row_square = jnp.mean(shard * shard, axis=1, keepdims=True)
     normalized = shard * lax.rsqrt(row_square + 1e-06)
     result = jnp.where(trainer, normalized, copied.astype(jnp.float32))

time: 131 us -> 122 us (0.931)
  matrix products: 26.1 us -> 18.6 us
  waiting for transfers between devices: 47.3 us -> 45.7 us
  local copies, waits for them, and re-layouts: 3.96 us -> 5.34 us
    dot_general x34, matrix products: 24.9 us -> 17.4 us  [the longest x16 9.31 us: term(): lax.dot_general(columns(offset, i), delta, (((0,), (0,)), ((), ())), pref...]
    ppermute x28, waiting for transfers between devices: 39.1 us -> 35.6 us  [along_ring(): return lax.ppermute(block, 'chip', pairs)]
    ppermute x4, waiting for transfers between devices: 5.23 us -> 7.29 us  [slab_blocks(): kept.append(lax.ppermute(stored, ('grp', 'chip', 'core'), pairs))]
    ppermute x28, starting transfers between devices: 30.7 us -> 32.4 us  [along_ring(): return lax.ppermute(block, 'chip', pairs)]
    ppermute x6, starting transfers between devices: 2.42 us -> 0.88 us  [from_sibling(): return lax.ppermute(block, 'core', [(0, 1), (1, 0)])]
  transfers between devices with their start and end apart: 39 -> 39, of which waited for: 23 -> 19; matrix products, arithmetic and copies ran while one was open for 21% -> 18% of each run, Pallas kernels for 6% -> 6%
where the time goes in v13:
time: 122 us
  waiting for transfers between devices  45.7 us (37%)
  starting transfers between devices  39.7 us (33%)
  matrix products  18.6 us (15%)
  Pallas kernels  7.2 us (6%)
  local copies, waits for them, and re-layouts  5.34 us (4%)
  other arithmetic  4.63 us (4%)
    ppermute x28, waiting for transfers between devices, along_ring(): return lax.ppermute(block, 'chip', pairs)  35.6 us
    ppermute x28, starting transfers between devices, along_ring(): return lax.ppermute(block, 'chip', pairs)  32.4 us
    dot_general x16, matrix products, term(): lax.dot_general(columns(offset, i), delta, (((0,), (0,)), ((), ())), pref...  9.31 us
    dot_general x16, matrix products, product(): jnp.dot(columns(offset, i), block, preferred_element_type=jnp.float32)  7.73 us
    ppermute x4, waiting for transfers between devices, slab_blocks(): kept.append(lax.ppermute(stored, ('grp', 'chip', 'core'), pairs))  7.29 us
    pallas_call x1, Pallas kernels, normalize_both(): pl.pallas_call(functools.partial(normalize_kernel, seqs, 16), grid=(2 * s...  7.2 us
    ppermute x4, starting transfers between devices, slab_blocks(): kept.append(lax.ppermute(stored, ('grp', 'chip', 'core'), pairs))  5.16 us
    ppermute x6, waiting for transfers between devices, from_sibling(): return lax.ppermute(block, 'core', [(0, 1), (1, 0)])  2.8 us
  transfers between devices with their start and end apart: 39, of which 19 were waited for; matrix products, arithmetic and copies ran while one was open for 18% of the time, Pallas kernels for 6%

profile of v13, /device:TPU:0, one launch (start us, length us, event | category | flops | bytes accessed | tf_op | source)
XLA Modules:
  0.0 121.7 jit_solution(14094631291812412264)
XLA Ops:
  0.5 1.5 %dynamic-slice_convert_fusion = (bf16[256,512]{1,0:T(8,128)(2,1)S(1)}, bf16[256,512]{1,0:T(8,128)(2,1)S(1)}) fusion(f32[256,1024]{1,0:T(8,128)} %bitcast.57, s32[]{:T(128)S(6)} %mul.280, s32[]{:T(128)S(6)} %mul.281), kind=kLoop, calls=%fused_computation.41 | loop fusion | bytes 1048584 | tf_op jit(solution)/shard_map/convert_element_type | solution.py:143
  2.1 3.0 %collective-permute-start.4 = (bf16[256,512]{1,0:T(8,128)(2,1)S(1)}, bf16[256,512]{1,0:T(8,128)(2,1)S(1)}, u32[]{:S(2)}, u32[]{:S(2)}) collective-permute-start(bf16[256,512]{1,0:T(8,128)(2,1)S(1)} %get-tuple-element.89), channel_id=1, source_target_pairs={{0,4},{4,8},{8,12},{12,14},{14,10},{10,6},{6,2},{2,0},{1,5},{5,9},... | collective-permute-start | bytes 786440 | tf_op jit(solution)/shard_map/ppermute | solution.py:32
  6.1 2.9 %collective-permute-start.2 = (bf16[256,512]{1,0:T(8,128)(2,1)S(1)}, bf16[256,512]{1,0:T(8,128)(2,1)S(1)}, u32[]{:S(2)}, u32[]{:S(2)}) collective-permute-start(bf16[256,512]{1,0:T(8,128)(2,1)S(1)} %collective-permute-done.1), channel_id=1, source_target_pairs={{0,4},{4,8},{8,12},{12,14},{14,10},{10,6},{6,2},{2,0},{1,5},{5,9},... | collective-permute-start | bytes 786440 | tf_op jit(solution)/shard_map/ppermute | solution.py:32
  9.7 2.4 %collective-permute-done.4 = bf16[256,512]{1,0:T(8,128)(2,1)S(1)} collective-permute-done((bf16[256,512]{1,0:T(8,128)(2,1)S(1)}, bf16[256,512]{1,0:T(8,128)(2,1)S(1)}, u32[]{:S(2)}, u32[]{:S(2)}) %collective-permute-start.4) | collective-permute-done | bytes 262176 | tf_op jit(solution)/shard_map/ppermute | solution.py:32
  12.1 2.1 %collective-permute-start.7 = (bf16[256,512]{1,0:T(8,128)(2,1)S(1)}, bf16[256,512]{1,0:T(8,128)(2,1)S(1)}, u32[]{:S(2)}, u32[]{:S(2)}) collective-permute-start(bf16[256,512]{1,0:T(8,128)(2,1)S(1)} %collective-permute-done.4), channel_id=1, source_target_pairs={{0,4},{4,8},{8,12},{12,14},{14,10},{10,6},{6,2},{2,0},{1,5},{5,9},... | collective-permute-start | bytes 786440 | tf_op jit(solution)/shard_map/ppermute | solution.py:32
  14.3 3.5 %collective-permute-done.2 = bf16[256,512]{1,0:T(8,128)(2,1)S(1)} collective-permute-done((bf16[256,512]{1,0:T(8,128)(2,1)S(1)}, bf16[256,512]{1,0:T(8,128)(2,1)S(1)}, u32[]{:S(2)}, u32[]{:S(2)}) %collective-permute-start.2) | collective-permute-done | bytes 262176 | tf_op jit(solution)/shard_map/ppermute | solution.py:32
  20.8 2.2 %collective-permute-start.9 = (bf16[256,512]{1,0:T(8,128)(2,1)S(1)}, bf16[256,512]{1,0:T(8,128)(2,1)S(1)}, u32[]{:S(2)}, u32[]{:S(2)}) collective-permute-start(bf16[256,512]{1,0:T(8,128)(2,1)S(1)} %collective-permute-done.2), channel_id=1, source_target_pairs={{0,4},{4,8},{8,12},{12,14},{14,10},{10,6},{6,2},{2,0},{1,5},{5,9},... | collective-permute-start | bytes 786440 | tf_op jit(solution)/shard_map/ppermute | solution.py:32
  23.0 1.6 %collective-permute-start.11 = (bf16[256,512]{1,0:T(8,128)(2,1)S(1)}, bf16[256,512]{1,0:T(8,128)(2,1)S(1)}, u32[]{:S(2)}, u32[]{:S(2)}) collective-permute-start(bf16[256,512]{1,0:T(8,128)(2,1)S(1)} %collective-permute-done.7), channel_id=1, source_target_pairs={{0,4},{4,8},{8,12},{12,14},{14,10},{10,6},{6,2},{2,0},{1,5},{5,9},... | collective-permute-start | bytes 786440 | tf_op jit(solution)/shard_map/ppermute | solution.py:32
  25.0 1.6 %collective-permute-start.12 = (bf16[256,512]{1,0:T(8,128)(2,1)S(1)}, bf16[256,512]{1,0:T(8,128)(2,1)S(1)}, u32[]{:S(2)}, u32[]{:S(2)}) collective-permute-start(bf16[256,512]{1,0:T(8,128)(2,1)S(1)} %collective-permute-done.8), channel_id=1, source_target_pairs={{0,2},{4,0},{8,4},{12,8},{14,12},{10,14},{6,10},{2,6},{1,3},{5,1},... | collective-permute-start | bytes 786440 | tf_op jit(solution)/shard_map/ppermute | solution.py:32
  27.0 1.9 %copy-done = bf16[1,3,128,4096]{3,2,1,0:T(8,128)(2,1)S(1)} copy-done((bf16[1,3,128,4096]{3,2,1,0:T(8,128)(2,1)S(1)}, bf16[1,3,128,4096]{3,2,1,0:T(8,128)(2,1)}, u32[]{:S(2)}) %copy-start) | copy-done | bytes 3145752
  28.9 7.2 %shard_map.64 = bf16[768,4096]{1,0:T(8,128)(2,1)S(1)} custom-call(bf16[3,128,4096]{2,1,0:T(8,128)(2,1)S(1)} %bitcast.54, bf16[3,128,4096]{2,1,0:T(8,128)(2,1)S(1)} %collective-permute-done.other_ref, f32[1,4096]{1,0:T(1,128)S(1)} %bitcast.55), custom_call_target="tpu_custom_call" | custom-call | flops 18874368 | bytes 12582912 | tf_op jit(solution)/shard_map/pallas_call | solution.py:100
  39.5 1.6 %collective-permute-start.14 = (bf16[256,512]{1,0:T(8,128)(2,1)S(1)}, bf16[256,512]{1,0:T(8,128)(2,1)S(1)}, u32[]{:S(2)}, u32[]{:S(2)}) collective-permute-start(bf16[256,512]{1,0:T(8,128)(2,1)S(1)} %collective-permute-done.10), channel_id=1, source_target_pairs={{0,2},{4,0},{8,4},{12,8},{14,12},{10,14},{6,10},{2,6},{1,3},{5,1},... | collective-permute-start | bytes 786440 | tf_op jit(solution)/shard_map/ppermute | solution.py:32
  43.9 2.9 %collective-permute-done.14 = bf16[256,512]{1,0:T(8,128)(2,1)S(1)} collective-permute-done((bf16[256,512]{1,0:T(8,128)(2,1)S(1)}, bf16[256,512]{1,0:T(8,128)(2,1)S(1)}, u32[]{:S(2)}, u32[]{:S(2)}) %collective-permute-start.14) | collective-permute-done | bytes 262176 | tf_op jit(solution)/shard_map/ppermute | solution.py:32
  48.7 2.6 %collective-permute-done.13 = bf16[256,512]{1,0:T(8,128)(2,1)S(1)} collective-permute-done((bf16[256,512]{1,0:T(8,128)(2,1)S(1)}, bf16[256,512]{1,0:T(8,128)(2,1)S(1)}, u32[]{:S(2)}, u32[]{:S(2)}) %collective-permute-start.13) | collective-permute-done | bytes 262176 | tf_op jit(solution)/shard_map/ppermute | solution.py:32
  51.8 1.4 %collective-permute-done.16 = bf16[256,512]{1,0:T(8,128)(2,1)S(1)} collective-permute-done((bf16[256,512]{1,0:T(8,128)(2,1)S(1)}, bf16[256,512]{1,0:T(8,128)(2,1)S(1)}, u32[]{:S(2)}, u32[]{:S(2)}) %collective-permute-start.16) | collective-permute-done | bytes 262176 | tf_op jit(solution)/shard_map/ppermute | solution.py:32
  61.9 2.3 %collective-permute-done.19 = bf16[6,1024]{1,0:T(8,128)(2,1)S(1)} collective-permute-done((bf16[6,1024]{1,0:T(8,128)(2,1)S(1)}, bf16[6,1024]{1,0:T(8,128)(2,1)S(1)}, u32[]{:S(2)}, u32[]{:S(2)}) %collective-permute-start.19) | collective-permute-done | bytes 12320 | tf_op jit(solution)/shard_map/ppermute | solution.py:64
  64.2 2.3 %collective-permute-done.20 = bf16[6,1024]{1,0:T(8,128)(2,1)S(1)} collective-permute-done((bf16[6,1024]{1,0:T(8,128)(2,1)S(1)}, bf16[6,1024]{1,0:T(8,128)(2,1)S(1)}, u32[]{:S(2)}, u32[]{:S(2)}) %collective-permute-start.20) | collective-permute-done | bytes 12320 | tf_op jit(solution)/shard_map/ppermute | solution.py:64
  66.5 2.2 %collective-permute-done.21 = bf16[6,1024]{1,0:T(8,128)(2,1)S(1)} collective-permute-done((bf16[6,1024]{1,0:T(8,128)(2,1)S(1)}, bf16[6,1024]{1,0:T(8,128)(2,1)S(1)}, u32[]{:S(2)}, u32[]{:S(2)}) %collective-permute-start.21) | collective-permute-done | bytes 12320 | tf_op jit(solution)/shard_map/ppermute | solution.py:64
  72.5 1.5 %collective-permute-start.31 = (bf16[256,512]{1,0:T(8,128)(2,1)S(1)}, bf16[256,512]{1,0:T(8,128)(2,1)S(1)}, u32[]{:S(2)}, u32[]{:S(2)}) collective-permute-start(bf16[256,512]{1,0:T(8,128)(2,1)S(1)} %convolution_convert_fusion.1), channel_id=1, source_target_pairs={{0,4},{4,8},{8,12},{12,14},{14,10},{10,6},{6,2},{2,0},{1,5},{5,9},... | collective-permute-start | bytes 786440 | tf_op jit(solution)/shard_map/ppermute | solution.py:32
  75.8 1.5 %collective-permute-start.34 = (bf16[256,512]{1,0:T(8,128)(2,1)S(1)}, bf16[256,512]{1,0:T(8,128)(2,1)S(1)}, u32[]{:S(2)}, u32[]{:S(2)}) collective-permute-start(bf16[256,512]{1,0:T(8,128)(2,1)S(1)} %convolution_convert_fusion), channel_id=1, source_target_pairs={{0,2},{4,0},{8,4},{12,8},{14,12},{10,14},{6,10},{2,6},{1,3},{5,1},... | collective-permute-start | bytes 786440 | tf_op jit(solution)/shard_map/ppermute | solution.py:32
  77.9 3.8 %collective-permute-done.31 = bf16[256,512]{1,0:T(8,128)(2,1)S(1)} collective-permute-done((bf16[256,512]{1,0:T(8,128)(2,1)S(1)}, bf16[256,512]{1,0:T(8,128)(2,1)S(1)}, u32[]{:S(2)}, u32[]{:S(2)}) %collective-permute-start.31) | collective-permute-done | bytes 262176 | tf_op jit(solution)/shard_map/ppermute | solution.py:32
  82.3 1.5 %collective-permute-start.32 = (bf16[256,512]{1,0:T(8,128)(2,1)S(1)}, bf16[256,512]{1,0:T(8,128)(2,1)S(1)}, u32[]{:S(2)}, u32[]{:S(2)}) collective-permute-start(bf16[256,512]{1,0:T(8,128)(2,1)S(1)} %fusion.6), channel_id=1, source_target_pairs={{0,4},{4,8},{8,12},{12,14},{14,10},{10,6},{6,2},{2,0},{1,5},{5,9},... | collective-permute-start | bytes 786440 | tf_op jit(solution)/shard_map/ppermute | solution.py:32
  83.8 3.5 %collective-permute-done.23 = bf16[256,512]{1,0:T(8,128)(2,1)S(1)} collective-permute-done((bf16[256,512]{1,0:T(8,128)(2,1)S(1)}, bf16[256,512]{1,0:T(8,128)(2,1)S(1)}, u32[]{:S(2)}, u32[]{:S(2)}) %collective-permute-start.23) | collective-permute-done | bytes 262176 | tf_op jit(solution)/shard_map/ppermute | solution.py:32
  90.3 1.6 %collective-permute-start.25 = (bf16[256,512]{1,0:T(8,128)(2,1)S(1)}, bf16[256,512]{1,0:T(8,128)(2,1)S(1)}, u32[]{:S(2)}, u32[]{:S(2)}) collective-permute-start(bf16[256,512]{1,0:T(8,128)(2,1)S(1)} %fusion.3), channel_id=1, source_target_pairs={{0,4},{4,8},{8,12},{12,14},{14,10},{10,6},{6,2},{2,0},{1,5},{5,9},... | collective-permute-start | bytes 786440 | tf_op jit(solution)/shard_map/ppermute | solution.py:32
  91.9 1.3 %collective-permute-start.24 = (bf16[256,1024]{1,0:T(8,128)(2,1)S(1)}, bf16[256,1024]{1,0:T(8,128)(2,1)S(1)}, u32[]{:S(2)}, u32[]{:S(2)}) collective-permute-start(bf16[256,1024]{1,0:T(8,128)(2,1)S(1)} %convert_element_type.163), channel_id=1, source_target_pairs={{0,16},{1,17},{2,18},{3,19},{4,20},{5,21},{6,22},{7,23},{8,24},{9,... | collective-permute-start | bytes 1572872 | tf_op jit(solution)/shard_map/ppermute | solution.py:40
  95.0 2.3 %collective-permute-done.35 = bf16[256,512]{1,0:T(8,128)(2,1)S(1)} collective-permute-done((bf16[256,512]{1,0:T(8,128)(2,1)S(1)}, bf16[256,512]{1,0:T(8,128)(2,1)S(1)}, u32[]{:S(2)}, u32[]{:S(2)}) %collective-permute-start.35) | collective-permute-done | bytes 262176 | tf_op jit(solution)/shard_map/ppermute | solution.py:32
  98.7 1.9 %collective-permute-start.33 = (bf16[256,512]{1,0:T(8,128)(2,1)S(1)}, bf16[256,512]{1,0:T(8,128)(2,1)S(1)}, u32[]{:S(2)}, u32[]{:S(2)}) collective-permute-start(bf16[256,512]{1,0:T(8,128)(2,1)S(1)} %fusion.5), channel_id=1, source_target_pairs={{0,4},{4,8},{8,12},{12,14},{14,10},{10,6},{6,2},{2,0},{1,5},{5,9},... | collective-permute-start | bytes 786440 | tf_op jit(solution)/shard_map/ppermute | solution.py:32
  101.2 1.6 %collective-permute-start.26 = (bf16[256,512]{1,0:T(8,128)(2,1)S(1)}, bf16[256,512]{1,0:T(8,128)(2,1)S(1)}, u32[]{:S(2)}, u32[]{:S(2)}) collective-permute-start(bf16[256,512]{1,0:T(8,128)(2,1)S(1)} %fusion.2), channel_id=1, source_target_pairs={{0,4},{4,8},{8,12},{12,14},{14,10},{10,6},{6,2},{2,0},{1,5},{5,9},... | collective-permute-start | bytes 786440 | tf_op jit(solution)/shard_map/ppermute | solution.py:32
  102.8 4.4 %collective-permute-done.36 = bf16[256,512]{1,0:T(8,128)(2,1)S(1)} collective-permute-done((bf16[256,512]{1,0:T(8,128)(2,1)S(1)}, bf16[256,512]{1,0:T(8,128)(2,1)S(1)}, u32[]{:S(2)}, u32[]{:S(2)}) %collective-permute-start.36) | collective-permute-done | bytes 262176 | tf_op jit(solution)/shard_map/ppermute | solution.py:32
  108.9 1.7 %collective-permute-start.30 = (bf16[256,512]{1,0:T(8,128)(2,1)S(1)}, bf16[256,512]{1,0:T(8,128)(2,1)S(1)}, u32[]{:S(2)}, u32[]{:S(2)}) collective-permute-start(bf16[256,512]{1,0:T(8,128)(2,1)S(1)} %convolution_add_fusion.6), channel_id=1, source_target_pairs={{0,2},{4,0},{8,4},{12,8},{14,12},{10,14},{6,10},{2,6},{1,3},{5,1},... | collective-permute-start | bytes 786440 | tf_op jit(solution)/shard_map/ppermute | solution.py:32
  111.6 5.4 %collective-permute-done.37 = bf16[256,512]{1,0:T(8,128)(2,1)S(1)} collective-permute-done((bf16[256,512]{1,0:T(8,128)(2,1)S(1)}, bf16[256,512]{1,0:T(8,128)(2,1)S(1)}, u32[]{:S(2)}, u32[]{:S(2)}) %collective-permute-start.37) | collective-permute-done | bytes 262176 | tf_op jit(solution)/shard_map/ppermute | solution.py:32
  117.2 2.9 %collective-permute-done.30 = bf16[256,512]{1,0:T(8,128)(2,1)S(1)} collective-permute-done((bf16[256,512]{1,0:T(8,128)(2,1)S(1)}, bf16[256,512]{1,0:T(8,128)(2,1)S(1)}, u32[]{:S(2)}, u32[]{:S(2)}) %collective-permute-start.30) | collective-permute-done | bytes 262176 | tf_op jit(solution)/shard_map/ppermute | solution.py:32
  (123 shorter events, 41.1 us)
Async XLA Ops:
  0.0 27.0 %collective-permute-start = (bf16[3,128,4096]{2,1,0:T(8,128)(2,1)}, bf16[3,128,4096]{2,1,0:T(8,128)(2,1)S(1)}, u32[]{:S(2)}, u32[]{:S(2)}) collective-permute-start(bf16[3,128,4096]{2,1,0:T(8,128)(2,1)} %bitcast.53), channel_id=1, source_target_pairs={{0,1},{1,0},{2,3},{3,2},{4,5},{5,4},{6,7},{7,6},{8,9},{9,8},{10,11... | collective-permute-start | bytes 9437192 | tf_op jit(solution)/shard_map/ppermute | solution.py:52
  2.1 10.1 %collective-permute-start.4 = (bf16[256,512]{1,0:T(8,128)(2,1)S(1)}, bf16[256,512]{1,0:T(8,128)(2,1)S(1)}, u32[]{:S(2)}, u32[]{:S(2)}) collective-permute-start(bf16[256,512]{1,0:T(8,128)(2,1)S(1)} %get-tuple-element.89), channel_id=1, source_target_pairs={{0,4},{4,8},{8,12},{12,14},{14,10},{10,6},{6,2},{2,0},{1,5},{5,9},... | collective-permute-start | bytes 786440 | tf_op jit(solution)/shard_map/ppermute | solution.py:32
  5.1 9.2 %collective-permute-start.5 = (bf16[256,512]{1,0:T(8,128)(2,1)S(1)}, bf16[256,512]{1,0:T(8,128)(2,1)S(1)}, u32[]{:S(2)}, u32[]{:S(2)}) collective-permute-start(bf16[256,512]{1,0:T(8,128)(2,1)S(1)} %get-tuple-element.89), channel_id=1, source_target_pairs={{0,2},{4,0},{8,4},{12,8},{14,12},{10,14},{6,10},{2,6},{1,3},{5,1},... | collective-permute-start | bytes 786440 | tf_op jit(solution)/shard_map/ppermute | solution.py:32
  6.1 11.6 %collective-permute-start.2 = (bf16[256,512]{1,0:T(8,128)(2,1)S(1)}, bf16[256,512]{1,0:T(8,128)(2,1)S(1)}, u32[]{:S(2)}, u32[]{:S(2)}) collective-permute-start(bf16[256,512]{1,0:T(8,128)(2,1)S(1)} %collective-permute-done.1), channel_id=1, source_target_pairs={{0,4},{4,8},{8,12},{12,14},{14,10},{10,6},{6,2},{2,0},{1,5},{5,9},... | collective-permute-start | bytes 786440 | tf_op jit(solution)/shard_map/ppermute | solution.py:32
  9.7 11.0 %collective-permute-start.6 = (bf16[256,512]{1,0:T(8,128)(2,1)S(1)}, bf16[256,512]{1,0:T(8,128)(2,1)S(1)}, u32[]{:S(2)}, u32[]{:S(2)}) collective-permute-start(bf16[256,512]{1,0:T(8,128)(2,1)S(1)} %collective-permute-done.1), channel_id=1, source_target_pairs={{0,2},{4,0},{8,4},{12,8},{14,12},{10,14},{6,10},{2,6},{1,3},{5,1},... | collective-permute-start | bytes 786440 | tf_op jit(solution)/shard_map/ppermute | solution.py:32
  12.1 10.8 %collective-permute-start.7 = (bf16[256,512]{1,0:T(8,128)(2,1)S(1)}, bf16[256,512]{1,0:T(8,128)(2,1)S(1)}, u32[]{:S(2)}, u32[]{:S(2)}) collective-permute-start(bf16[256,512]{1,0:T(8,128)(2,1)S(1)} %collective-permute-done.4), channel_id=1, source_target_pairs={{0,4},{4,8},{8,12},{12,14},{14,10},{10,6},{6,2},{2,0},{1,5},{5,9},... | collective-permute-start | bytes 786440 | tf_op jit(solution)/shard_map/ppermute | solution.py:32
  14.2 10.4 %collective-permute-start.8 = (bf16[256,512]{1,0:T(8,128)(2,1)S(1)}, bf16[256,512]{1,0:T(8,128)(2,1)S(1)}, u32[]{:S(2)}, u32[]{:S(2)}) collective-permute-start(bf16[256,512]{1,0:T(8,128)(2,1)S(1)} %collective-permute-done.5), channel_id=1, source_target_pairs={{0,2},{4,0},{8,4},{12,8},{14,12},{10,14},{6,10},{2,6},{1,3},{5,1},... | collective-permute-start | bytes 786440 | tf_op jit(solution)/shard_map/ppermute | solution.py:32
  20.8 20.3 %collective-permute-start.9 = (bf16[256,512]{1,0:T(8,128)(2,1)S(1)}, bf16[256,512]{1,0:T(8,128)(2,1)S(1)}, u32[]{:S(2)}, u32[]{:S(2)}) collective-permute-start(bf16[256,512]{1,0:T(8,128)(2,1)S(1)} %collective-permute-done.2), channel_id=1, source_target_pairs={{0,4},{4,8},{8,12},{12,14},{14,10},{10,6},{6,2},{2,0},{1,5},{5,9},... | collective-permute-start | bytes 786440 | tf_op jit(solution)/shard_map/ppermute | solution.py:32
  23.0 16.0 %collective-permute-start.11 = (bf16[256,512]{1,0:T(8,128)(2,1)S(1)}, bf16[256,512]{1,0:T(8,128)(2,1)S(1)}, u32[]{:S(2)}, u32[]{:S(2)}) collective-permute-start(bf16[256,512]{1,0:T(8,128)(2,1)S(1)} %collective-permute-done.7), channel_id=1, source_target_pairs={{0,4},{4,8},{8,12},{12,14},{14,10},{10,6},{6,2},{2,0},{1,5},{5,9},... | collective-permute-start | bytes 786440 | tf_op jit(solution)/shard_map/ppermute | solution.py:32
  24.6 14.9 %collective-permute-start.10 = (bf16[256,512]{1,0:T(8,128)(2,1)S(1)}, bf16[256,512]{1,0:T(8,128)(2,1)S(1)}, u32[]{:S(2)}, u32[]{:S(2)}) collective-permute-start(bf16[256,512]{1,0:T(8,128)(2,1)S(1)} %collective-permute-done.6), channel_id=1, source_target_pairs={{0,2},{4,0},{8,4},{12,8},{14,12},{10,14},{6,10},{2,6},{1,3},{5,1},... | collective-permute-start | bytes 786440 | tf_op jit(solution)/shard_map/ppermute | solution.py:32
  25.0 28.6 %collective-permute-start.12 = (bf16[256,512]{1,0:T(8,128)(2,1)S(1)}, bf16[256,512]{1,0:T(8,128)(2,1)S(1)}, u32[]{:S(2)}, u32[]{:S(2)}) collective-permute-start(bf16[256,512]{1,0:T(8,128)(2,1)S(1)} %collective-permute-done.8), channel_id=1, source_target_pairs={{0,2},{4,0},{8,4},{12,8},{14,12},{10,14},{6,10},{2,6},{1,3},{5,1},... | collective-permute-start | bytes 786440 | tf_op jit(solution)/shard_map/ppermute | solution.py:32
  39.0 9.3 %collective-permute-start.15 = (bf16[256,512]{1,0:T(8,128)(2,1)S(1)}, bf16[256,512]{1,0:T(8,128)(2,1)S(1)}, u32[]{:S(2)}, u32[]{:S(2)}) collective-permute-start(bf16[256,512]{1,0:T(8,128)(2,1)S(1)} %collective-permute-done.11), channel_id=1, source_target_pairs={{0,4},{4,8},{8,12},{12,14},{14,10},{10,6},{6,2},{2,0},{1,5},{5,9},... | collective-permute-start | bytes 786440 | tf_op jit(solution)/shard_map/ppermute | solution.py:32
  39.5 7.3 %collective-permute-start.14 = (bf16[256,512]{1,0:T(8,128)(2,1)S(1)}, bf16[256,512]{1,0:T(8,128)(2,1)S(1)}, u32[]{:S(2)}, u32[]{:S(2)}) collective-permute-start(bf16[256,512]{1,0:T(8,128)(2,1)S(1)} %collective-permute-done.10), channel_id=1, source_target_pairs={{0,2},{4,0},{8,4},{12,8},{14,12},{10,14},{6,10},{2,6},{1,3},{5,1},... | collective-permute-start | bytes 786440 | tf_op jit(solution)/shard_map/ppermute | solution.py:32
  41.1 10.2 %collective-permute-start.13 = (bf16[256,512]{1,0:T(8,128)(2,1)S(1)}, bf16[256,512]{1,0:T(8,128)(2,1)S(1)}, u32[]{:S(2)}, u32[]{:S(2)}) collective-permute-start(bf16[256,512]{1,0:T(8,128)(2,1)S(1)} %collective-permute-done.9), channel_id=1, source_target_pairs={{0,4},{4,8},{8,12},{12,14},{14,10},{10,6},{6,2},{2,0},{1,5},{5,9},... | collective-permute-start | bytes 786440 | tf_op jit(solution)/shard_map/ppermute | solution.py:32
  57.5 6.6 %collective-permute-start.19 = (bf16[6,1024]{1,0:T(8,128)(2,1)S(1)}, bf16[6,1024]{1,0:T(8,128)(2,1)S(1)}, u32[]{:S(2)}, u32[]{:S(2)}) collective-permute-start(bf16[6,1024]{1,0:T(8,128)(2,1)S(1)} %maximum_select_fusion.2), channel_id=1, source_target_pairs={{20,0},{27,1},{24,4},{23,5},{28,8},{19,9},{30,12},{17,13},{26,14},... | collective-permute-start | bytes 36872 | tf_op jit(solution)/shard_map/ppermute | solution.py:64
  58.8 7.7 %collective-permute-start.20 = (bf16[6,1024]{1,0:T(8,128)(2,1)S(1)}, bf16[6,1024]{1,0:T(8,128)(2,1)S(1)}, u32[]{:S(2)}, u32[]{:S(2)}) collective-permute-start(bf16[6,1024]{1,0:T(8,128)(2,1)S(1)} %maximum_select_fusion.2), channel_id=1, source_target_pairs={{24,0},{23,1},{28,4},{19,5},{30,8},{17,9},{26,12},{21,13},{22,14},... | collective-permute-start | bytes 36872 | tf_op jit(solution)/shard_map/ppermute | solution.py:64
  60.1 8.6 %collective-permute-start.21 = (bf16[6,1024]{1,0:T(8,128)(2,1)S(1)}, bf16[6,1024]{1,0:T(8,128)(2,1)S(1)}, u32[]{:S(2)}, u32[]{:S(2)}) collective-permute-start(bf16[6,1024]{1,0:T(8,128)(2,1)S(1)} %maximum_select_fusion.2), channel_id=1, source_target_pairs={{28,0},{19,1},{30,4},{17,5},{26,8},{21,9},{22,12},{25,13},{18,14},... | collective-permute-start | bytes 36872 | tf_op jit(solution)/shard_map/ppermute | solution.py:64
  72.5 9.2 %collective-permute-start.31 = (bf16[256,512]{1,0:T(8,128)(2,1)S(1)}, bf16[256,512]{1,0:T(8,128)(2,1)S(1)}, u32[]{:S(2)}, u32[]{:S(2)}) collective-permute-start(bf16[256,512]{1,0:T(8,128)(2,1)S(1)} %convolution_convert_fusion.1), channel_id=1, source_target_pairs={{0,4},{4,8},{8,12},{12,14},{14,10},{10,6},{6,2},{2,0},{1,5},{5,9},... | collective-permute-start | bytes 786440 | tf_op jit(solution)/shard_map/ppermute | solution.py:32
  74.6 12.7 %collective-permute-start.23 = (bf16[256,512]{1,0:T(8,128)(2,1)S(1)}, bf16[256,512]{1,0:T(8,128)(2,1)S(1)}, u32[]{:S(2)}, u32[]{:S(2)}) collective-permute-start(bf16[256,512]{1,0:T(8,128)(2,1)S(1)} %convolution_convert_fusion.3), channel_id=1, source_target_pairs={{0,4},{4,8},{8,12},{12,14},{14,10},{10,6},{6,2},{2,0},{1,5},{5,9},... | collective-permute-start | bytes 786440 | tf_op jit(solution)/shard_map/ppermute | solution.py:32
  75.8 12.7 %collective-permute-start.34 = (bf16[256,512]{1,0:T(8,128)(2,1)S(1)}, bf16[256,512]{1,0:T(8,128)(2,1)S(1)}, u32[]{:S(2)}, u32[]{:S(2)}) collective-permute-start(bf16[256,512]{1,0:T(8,128)(2,1)S(1)} %convolution_convert_fusion), channel_id=1, source_target_pairs={{0,2},{4,0},{8,4},{12,8},{14,12},{10,14},{6,10},{2,6},{1,3},{5,1},... | collective-permute-start | bytes 786440 | tf_op jit(solution)/shard_map/ppermute | solution.py:32
  77.3 15.9 %collective-permute-start.28 = (bf16[256,512]{1,0:T(8,128)(2,1)S(1)}, bf16[256,512]{1,0:T(8,128)(2,1)S(1)}, u32[]{:S(2)}, u32[]{:S(2)}) collective-permute-start(bf16[256,512]{1,0:T(8,128)(2,1)S(1)} %convolution_convert_fusion.2), channel_id=1, source_target_pairs={{0,2},{4,0},{8,4},{12,8},{14,12},{10,14},{6,10},{2,6},{1,3},{5,1},... | collective-permute-start | bytes 786440 | tf_op jit(solution)/shard_map/ppermute | solution.py:32
  82.3 15.8 %collective-permute-start.32 = (bf16[256,512]{1,0:T(8,128)(2,1)S(1)}, bf16[256,512]{1,0:T(8,128)(2,1)S(1)}, u32[]{:S(2)}, u32[]{:S(2)}) collective-permute-start(bf16[256,512]{1,0:T(8,128)(2,1)S(1)} %fusion.6), channel_id=1, source_target_pairs={{0,4},{4,8},{8,12},{12,14},{14,10},{10,6},{6,2},{2,0},{1,5},{5,9},... | collective-permute-start | bytes 786440 | tf_op jit(solution)/shard_map/ppermute | solution.py:32
  89.1 8.2 %collective-permute-start.35 = (bf16[256,512]{1,0:T(8,128)(2,1)S(1)}, bf16[256,512]{1,0:T(8,128)(2,1)S(1)}, u32[]{:S(2)}, u32[]{:S(2)}) collective-permute-start(bf16[256,512]{1,0:T(8,128)(2,1)S(1)} %fusion.9), channel_id=1, source_target_pairs={{0,2},{4,0},{8,4},{12,8},{14,12},{10,14},{6,10},{2,6},{1,3},{5,1},... | collective-permute-start | bytes 786440 | tf_op jit(solution)/shard_map/ppermute | solution.py:32
  90.3 10.3 %collective-permute-start.25 = (bf16[256,512]{1,0:T(8,128)(2,1)S(1)}, bf16[256,512]{1,0:T(8,128)(2,1)S(1)}, u32[]{:S(2)}, u32[]{:S(2)}) collective-permute-start(bf16[256,512]{1,0:T(8,128)(2,1)S(1)} %fusion.3), channel_id=1, source_target_pairs={{0,4},{4,8},{8,12},{12,14},{14,10},{10,6},{6,2},{2,0},{1,5},{5,9},... | collective-permute-start | bytes 786440 | tf_op jit(solution)/shard_map/ppermute | solution.py:32
  91.9 17.0 %collective-permute-start.24 = (bf16[256,1024]{1,0:T(8,128)(2,1)S(1)}, bf16[256,1024]{1,0:T(8,128)(2,1)S(1)}, u32[]{:S(2)}, u32[]{:S(2)}) collective-permute-start(bf16[256,1024]{1,0:T(8,128)(2,1)S(1)} %convert_element_type.163), channel_id=1, source_target_pairs={{0,16},{1,17},{2,18},{3,19},{4,20},{5,21},{6,22},{7,23},{8,24},{9,... | collective-permute-start | bytes 1572872 | tf_op jit(solution)/shard_map/ppermute | solution.py:40
  93.9 14.5 %collective-permute-start.29 = (bf16[256,512]{1,0:T(8,128)(2,1)S(1)}, bf16[256,512]{1,0:T(8,128)(2,1)S(1)}, u32[]{:S(2)}, u32[]{:S(2)}) collective-permute-start(bf16[256,512]{1,0:T(8,128)(2,1)S(1)} %fusion.4), channel_id=1, source_target_pairs={{0,2},{4,0},{8,4},{12,8},{14,12},{10,14},{6,10},{2,6},{1,3},{5,1},... | collective-permute-start | bytes 786440 | tf_op jit(solution)/shard_map/ppermute | solution.py:32
  97.9 9.3 %collective-permute-start.36 = (bf16[256,512]{1,0:T(8,128)(2,1)S(1)}, bf16[256,512]{1,0:T(8,128)(2,1)S(1)}, u32[]{:S(2)}, u32[]{:S(2)}) collective-permute-start(bf16[256,512]{1,0:T(8,128)(2,1)S(1)} %fusion.8), channel_id=1, source_target_pairs={{0,2},{4,0},{8,4},{12,8},{14,12},{10,14},{6,10},{2,6},{1,3},{5,1},... | collective-permute-start | bytes 786440 | tf_op jit(solution)/shard_map/ppermute | solution.py:32
  98.7 11.9 %collective-permute-start.33 = (bf16[256,512]{1,0:T(8,128)(2,1)S(1)}, bf16[256,512]{1,0:T(8,128)(2,1)S(1)}, u32[]{:S(2)}, u32[]{:S(2)}) collective-permute-start(bf16[256,512]{1,0:T(8,128)(2,1)S(1)} %fusion.5), channel_id=1, source_target_pairs={{0,4},{4,8},{8,12},{12,14},{14,10},{10,6},{6,2},{2,0},{1,5},{5,9},... | collective-permute-start | bytes 786440 | tf_op jit(solution)/shard_map/ppermute | solution.py:32
  101.2 9.4 %collective-permute-start.26 = (bf16[256,512]{1,0:T(8,128)(2,1)S(1)}, bf16[256,512]{1,0:T(8,128)(2,1)S(1)}, u32[]{:S(2)}, u32[]{:S(2)}) collective-permute-start(bf16[256,512]{1,0:T(8,128)(2,1)S(1)} %fusion.2), channel_id=1, source_target_pairs={{0,4},{4,8},{8,12},{12,14},{14,10},{10,6},{6,2},{2,0},{1,5},{5,9},... | collective-permute-start | bytes 786440 | tf_op jit(solution)/shard_map/ppermute | solution.py:32
  107.8 9.3 %collective-permute-start.37 = (bf16[256,512]{1,0:T(8,128)(2,1)S(1)}, bf16[256,512]{1,0:T(8,128)(2,1)S(1)}, u32[]{:S(2)}, u32[]{:S(2)}) collective-permute-start(bf16[256,512]{1,0:T(8,128)(2,1)S(1)} %fusion.7), channel_id=1, source_target_pairs={{0,2},{4,0},{8,4},{12,8},{14,12},{10,14},{6,10},{2,6},{1,3},{5,1},... | collective-permute-start | bytes 786440 | tf_op jit(solution)/shard_map/ppermute | solution.py:32
  108.9 11.2 %collective-permute-start.30 = (bf16[256,512]{1,0:T(8,128)(2,1)S(1)}, bf16[256,512]{1,0:T(8,128)(2,1)S(1)}, u32[]{:S(2)}, u32[]{:S(2)}) collective-permute-start(bf16[256,512]{1,0:T(8,128)(2,1)S(1)} %convolution_add_fusion.6), channel_id=1, source_target_pairs={{0,2},{4,0},{8,4},{12,8},{14,12},{10,14},{6,10},{2,6},{1,3},{5,1},... | collective-permute-start | bytes 786440 | tf_op jit(solution)/shard_map/ppermute | solution.py:32
  111.2 8.9 %collective-permute-start.27 = (bf16[256,512]{1,0:T(8,128)(2,1)S(1)}, bf16[256,512]{1,0:T(8,128)(2,1)S(1)}, u32[]{:S(2)}, u32[]{:S(2)}) collective-permute-start(bf16[256,512]{1,0:T(8,128)(2,1)S(1)} %convolution_add_fusion.9), channel_id=1, source_target_pairs={{0,4},{4,8},{8,12},{12,14},{14,10},{10,6},{6,2},{2,0},{1,5},{5,9},... | collective-permute-start | bytes 786440 | tf_op jit(solution)/shard_map/ppermute | solution.py:32
  (10 other events, 59.8 us)

commit v14 on v13

--- a/solution.py
+++ b/solution.py
@@ -10,7 +10,7 @@
 sharpness = 20.0
 cores = 2
 longest_ring = 16
-vmem_limit = 16 << 20
+vmem_limit = 12 << 20
 
 
 def ring_order(chips):
@@ -73,45 +73,41 @@
     )
 
 
-def normalize_kernel(seqs, chunk, mine_ref, other_ref, gain_ref, out_ref):
-    length = mine_ref.shape[1]
-
-    def run(ref):
-        @pl.loop(0, length // chunk)
-        def _(i):
-            at = pl.ds(pl.multiple_of(i * chunk, chunk), chunk)
-            wide = ref[0, at, :].astype(jnp.float32)
-            mean_square = jnp.mean(wide * wide, axis=-1, keepdims=True)
-            wide = wide * lax.rsqrt(mean_square + 1e-05) * gain_ref[...]
-            out_ref[at, :] = wide.astype(jnp.bfloat16)
-
-    @pl.when(pl.program_id(0) < seqs)
-    def _():
-        run(mine_ref)
-
-    @pl.when(pl.program_id(0) >= seqs)
-    def _():
-        run(other_ref)
-
-
-def normalize_both(mine, other, gain):
-    seqs, length, width = mine.shape
-    tokens = 2 * seqs * length
+def normalize_kernel(chunk, states_ref, gain_ref, *refs):
+    out_ref = refs[-1]
+
+    @pl.loop(0, states_ref.shape[1] // chunk)
+    def _(i):
+        at = pl.ds(pl.multiple_of(i * chunk, chunk), chunk)
+        wide = states_ref[0, at, :].astype(jnp.float32)
+        mean_square = jnp.mean(wide * wide, axis=-1, keepdims=True)
+        wide = wide * lax.rsqrt(mean_square + 1e-05) * gain_ref[...]
+        out_ref[at, :] = wide.astype(jnp.bfloat16)
+
+
+def normalize(states, gain, part, filled=None):
+    seqs, length, width = states.shape
+    tokens = seqs * length
+    in_specs = [
+        pl.BlockSpec((1, length, width), lambda i: (i, 0, 0)),
+        pl.BlockSpec((1, width), lambda i: (0, 0)),
+    ]
+    operands = [states, gain[None]]
+    if filled is not None:
+        in_specs.append(pl.BlockSpec(memory_space=pl.ANY))
+        operands.append(filled)
     return pl.pallas_call(
-        functools.partial(normalize_kernel, seqs, 16),
-        grid=(2 * seqs,),
-        in_specs=[
-            pl.BlockSpec((1, length, width), lambda i: (jnp.minimum(i, seqs - 1), 0, 0)),
-            pl.BlockSpec((1, length, width), lambda i: (jnp.maximum(i - seqs, 0), 0, 0)),
-            pl.BlockSpec((1, width), lambda i: (0, 0)),
-        ],
-        out_specs=pl.BlockSpec((length, width), lambda i: (i, 0)),
-        out_shape=jax.ShapeDtypeStruct((tokens, width), jnp.bfloat16),
+        functools.partial(normalize_kernel, 16),
+        grid=(seqs,),
+        in_specs=in_specs,
+        out_specs=pl.BlockSpec((length, width), lambda i: (part * seqs + i, 0)),
+        out_shape=jax.ShapeDtypeStruct((cores * tokens, width), jnp.bfloat16),
+        input_output_aliases={} if filled is None else {2: 0},
         compiler_params=pltpu.CompilerParams(vmem_limit_bytes=vmem_limit),
         cost_estimate=pl.CostEstimate(
             flops=6 * tokens * width, bytes_accessed=4 * tokens * width, transcendentals=tokens
         ),
-    )(mine, other, gain[None])
+    )(*operands)
 
 
 def shards(token_states, token_ids, master, gain, cand_ids, slab_owner):
@@ -146,21 +142,10 @@
 
     other_states = from_sibling(states)
     sent = [(0, 1), (0, -1), (1, 1), (1, -1)]
-    ids = token_ids[0]
+    normed_own = normalize(states, gain, 0)
+    normed = normalize(other_states, gain, 1, normed_own)
     if chips <= longest_ring:
         moving = {(i, by): along_ring((own, sibling)[i], by) for i, by in sent}
-        cand_ids, slab_owner = after(moving[1, 1], (cand_ids, slab_owner))
-    normed = normalize_both(states, other_states, gain)
-    slab_rows = slab_owner.shape[0]
-    slab_ids = jnp.arange(slab_rows, dtype=jnp.int32)[None, :]
-    picked = [
-        (cand_ids[:, j : j + 1] == slab_ids).astype(jnp.int32) for j in range(cand_ids.shape[1])
-    ]
-    ids = jnp.concatenate([ids, sum(picked), picked[0]], axis=1)
-    ids = jnp.concatenate([ids, from_sibling(ids)])
-    lengths = jnp.sum((ids[:, :length] != 0).astype(jnp.int32), axis=1)
-    counts = lengths.astype(jnp.float32)
-    masks = ids[:, length:].astype(jnp.float32)
 
     def columns(offset, i):
         return cut(normed, 1, starts[offset, i], rows)
@@ -177,15 +162,28 @@
                 if step > 1:
                     if last and step > 2:
                         moving[i, by] = after(sums[1 + i], moving[i, by])
-                    elif step == 3 and i == 1:
-                        moving[i, by] = after(normed, moving[i, by])
+                    elif step in (2, 3) and i == 1:
+                        moving[i, by] = after((normed_own, normed)[step - 2], moving[i, by])
                     moving[i, by] = along_ring(moving[i, by], by)
                 total = total + product(-by * step, i, moving[i, by])
             sums[step] = total
+            if step == chips // 2 - 1:
+                cand_ids, slab_owner = after(sums[1], (cand_ids, slab_owner))
     else:
         both = in_core_order(own, sibling, first_core)
         gathered = lax.all_gather(both, "chip", axis=0, tiled=True)
         total = jnp.dot(normed, gathered, preferred_element_type=jnp.float32)
+
+    slab_rows = slab_owner.shape[0]
+    slab_ids = jnp.arange(slab_rows, dtype=jnp.int32)[None, :]
+    picked = [
+        (cand_ids[:, j : j + 1] == slab_ids).astype(jnp.int32) for j in range(cand_ids.shape[1])
+    ]
+    ids = jnp.concatenate([token_ids[0], sum(picked), picked[0]], axis=1)
+    ids = jnp.concatenate([ids, from_sibling(ids)])
+    lengths = jnp.sum((ids[:, :length] != 0).astype(jnp.int32), axis=1)
+    counts = lengths.astype(jnp.float32)
+    masks = ids[:, length:].astype(jnp.float32)
 
     active = jnp.tanh(total).reshape(seqs, length, half)
     there = jnp.arange(length)[None, :, None] < lengths[:, None, None]
@@ -250,6 +248,7 @@
     if chips <= longest_ring:
         arrived = {}
         late = delta
+        early = delta
         for step in range(chips // 2, 0, -1):
             for i, by in ((0, 1), (1, -1), (1, 1), (0, -1)):
                 if step == chips // 2 and (i, by) not in ((0, 1), (1, -1)):
@@ -259,7 +258,10 @@
                     total = total + arrived[i, by].astype(jnp.float32)
                 if step == 1 and i == 0:
                     total = after(copied, total)
-                arrived[i, by] = along_ring(total.astype(jnp.bfloat16), by)
+                total = total.astype(jnp.bfloat16)
+                if step == chips // 2:
+                    early = after(total, early)
+                arrived[i, by] = along_ring(total, by)
             if step == chips // 2:
                 late, weights = after(arrived[0, 1], (delta, weights))
                 copied = passed_on(weights)

time: 122 us -> 119 us (0.975)
  other arithmetic: 4.63 us -> 3.25 us
    unnamed x7 -> x11, local copies, waits for them, and re-layouts: 2.59 us -> 3.31 us
    pallas_call x1 -> x2, Pallas kernels: 7.2 us -> 7.18 us  [normalize(): pl.pallas_call(functools.partial(normalize_kernel, 16), grid=(seqs,), in_...]
  transfers between devices with their start and end apart: 39 -> 39, of which waited for: 19 -> 18; matrix products, arithmetic and copies ran while one was open for 18% -> 16% of each run, Pallas kernels for 6% -> 6%
where the time goes in v14:
time: 119 us
  waiting for transfers between devices  45 us (38%)
  starting transfers between devices  39.4 us (33%)
  matrix products  18.7 us (16%)
  Pallas kernels  7.18 us (6%)
  local copies, waits for them, and re-layouts  5.08 us (4%)
  other arithmetic  3.25 us (3%)
    ppermute x28, waiting for transfers between devices, along_ring(): return lax.ppermute(block, 'chip', pairs)  34.8 us
    ppermute x28, starting transfers between devices, along_ring(): return lax.ppermute(block, 'chip', pairs)  32.1 us
    dot_general x16, matrix products, term(): lax.dot_general(columns(offset, i), delta, (((0,), (0,)), ((), ())), pref...  9.3 us
    dot_general x16, matrix products, product(): jnp.dot(columns(offset, i), block, preferred_element_type=jnp.float32)  7.77 us
    ppermute x4, waiting for transfers between devices, slab_blocks(): kept.append(lax.ppermute(stored, ('grp', 'chip', 'core'), pairs))  7.31 us
    pallas_call x2, Pallas kernels, normalize(): pl.pallas_call(functools.partial(normalize_kernel, 16), grid=(seqs,), in_...  7.18 us
    ppermute x4, starting transfers between devices, slab_blocks(): kept.append(lax.ppermute(stored, ('grp', 'chip', 'core'), pairs))  5.16 us
    unnamed x11, local copies, waits for them, and re-layouts  3.31 us
  transfers between devices with their start and end apart: 39, of which 18 were waited for; matrix products, arithmetic and copies ran while one was open for 16% of the time, Pallas kernels for 6%

profile of v14, /device:TPU:0, one launch (start us, length us, event | category | flops | bytes accessed | tf_op | source)
XLA Modules:
  0.0 119.0 jit_solution(2653877968394535744)
XLA Ops:
  0.5 1.5 %dynamic-slice_convert_fusion.1 = (bf16[256,512]{1,0:T(8,128)(2,1)S(1)}, bf16[256,512]{1,0:T(8,128)(2,1)S(1)}) fusion(f32[256,1024]{1,0:T(8,128)} %bitcast.58, s32[]{:T(128)S(6)} %mul.280, s32[]{:T(128)S(6)} %mul.281), kind=kLoop, calls=%fused_computation.42 | loop fusion | bytes 1048584 | tf_op jit(solution)/shard_map/convert_element_type | solution.py:139
  2.1 3.0 %collective-permute-start.2 = (bf16[256,512]{1,0:T(8,128)(2,1)S(1)}, bf16[256,512]{1,0:T(8,128)(2,1)S(1)}, u32[]{:S(2)}, u32[]{:S(2)}) collective-permute-start(bf16[256,512]{1,0:T(8,128)(2,1)S(1)} %get-tuple-element.93), channel_id=1, source_target_pairs={{0,4},{4,8},{8,12},{12,14},{14,10},{10,6},{6,2},{2,0},{1,5},{5,9},... | collective-permute-start | bytes 786440 | tf_op jit(solution)/shard_map/ppermute | solution.py:32
  6.1 2.9 %collective-permute-start.5 = (bf16[256,512]{1,0:T(8,128)(2,1)S(1)}, bf16[256,512]{1,0:T(8,128)(2,1)S(1)}, u32[]{:S(2)}, u32[]{:S(2)}) collective-permute-start(bf16[256,512]{1,0:T(8,128)(2,1)S(1)} %collective-permute-done.1), channel_id=1, source_target_pairs={{0,2},{4,0},{8,4},{12,8},{14,12},{10,14},{6,10},{2,6},{1,3},{5,1},... | collective-permute-start | bytes 786440 | tf_op jit(solution)/shard_map/ppermute | solution.py:32
  9.1 2.7 %collective-permute-done.2 = bf16[256,512]{1,0:T(8,128)(2,1)S(1)} collective-permute-done((bf16[256,512]{1,0:T(8,128)(2,1)S(1)}, bf16[256,512]{1,0:T(8,128)(2,1)S(1)}, u32[]{:S(2)}, u32[]{:S(2)}) %collective-permute-start.2) | collective-permute-done | bytes 262176 | tf_op jit(solution)/shard_map/ppermute | solution.py:32
  11.8 2.5 %collective-permute-start.7 = (bf16[256,512]{1,0:T(8,128)(2,1)S(1)}, bf16[256,512]{1,0:T(8,128)(2,1)S(1)}, u32[]{:S(2)}, u32[]{:S(2)}) collective-permute-start(bf16[256,512]{1,0:T(8,128)(2,1)S(1)} %collective-permute-done.2), channel_id=1, source_target_pairs={{0,4},{4,8},{8,12},{12,14},{14,10},{10,6},{6,2},{2,0},{1,5},{5,9},... | collective-permute-start | bytes 786440 | tf_op jit(solution)/shard_map/ppermute | solution.py:32
  15.0 1.9 %copy-done = bf16[1,3,128,4096]{3,2,1,0:T(8,128)(2,1)S(1)} copy-done((bf16[1,3,128,4096]{3,2,1,0:T(8,128)(2,1)S(1)}, bf16[1,3,128,4096]{3,2,1,0:T(8,128)(2,1)}, u32[]{:S(2)}) %copy-start) | copy-done | bytes 3145752
  17.6 3.6 %shard_map.64.refs_0_ = bf16[768,4096]{1,0:T(8,128)(2,1)S(1)} custom-call(bf16[3,128,4096]{2,1,0:T(8,128)(2,1)S(1)} %bitcast.54, f32[1,4096]{1,0:T(1,128)S(1)} %bitcast.55), custom_call_target="tpu_custom_call" | custom-call | flops 9437184 | bytes 6291456 | tf_op jit(solution)/shard_map/pallas_call | solution.py:99
  21.2 2.1 %collective-permute-start.9 = (bf16[256,512]{1,0:T(8,128)(2,1)S(1)}, bf16[256,512]{1,0:T(8,128)(2,1)S(1)}, u32[]{:S(2)}, u32[]{:S(2)}) collective-permute-start(bf16[256,512]{1,0:T(8,128)(2,1)S(1)} %collective-permute-done.4), channel_id=1, source_target_pairs={{0,4},{4,8},{8,12},{12,14},{14,10},{10,6},{6,2},{2,0},{1,5},{5,9},... | collective-permute-start | bytes 786440 | tf_op jit(solution)/shard_map/ppermute | solution.py:32
  23.4 2.1 %collective-permute-start.11 = (bf16[256,512]{1,0:T(8,128)(2,1)S(1)}, bf16[256,512]{1,0:T(8,128)(2,1)S(1)}, u32[]{:S(2)}, u32[]{:S(2)}) collective-permute-start(bf16[256,512]{1,0:T(8,128)(2,1)S(1)} %collective-permute-done.7), channel_id=1, source_target_pairs={{0,4},{4,8},{8,12},{12,14},{14,10},{10,6},{6,2},{2,0},{1,5},{5,9},... | collective-permute-start | bytes 786440 | tf_op jit(solution)/shard_map/ppermute | solution.py:32
  25.5 3.6 %shard_map.65 = bf16[768,4096]{1,0:T(8,128)(2,1)S(1)} custom-call(bf16[3,128,4096]{2,1,0:T(8,128)(2,1)S(1)} %collective-permute-done.states_ref, f32[1,4096]{1,0:T(1,128)S(1)} %bitcast.56, bf16[768,4096]{1,0:T(8,128)(2,1)S(1)} %shard_map.64.refs_0_), custom_call_target="tpu_custom_call", output_to_operand_aliasing={{}: (2, {})} | custom-call | flops 9437184 | bytes 6291456 | tf_op jit(solution)/shard_map/pallas_call | solution.py:99
  32.6 2.1 %collective-permute-start.13 = (bf16[256,512]{1,0:T(8,128)(2,1)S(1)}, bf16[256,512]{1,0:T(8,128)(2,1)S(1)}, u32[]{:S(2)}, u32[]{:S(2)}) collective-permute-start(bf16[256,512]{1,0:T(8,128)(2,1)S(1)} %collective-permute-done.9), channel_id=1, source_target_pairs={{0,4},{4,8},{8,12},{12,14},{14,10},{10,6},{6,2},{2,0},{1,5},{5,9},... | collective-permute-start | bytes 786440 | tf_op jit(solution)/shard_map/ppermute | solution.py:32
  34.7 2.0 %collective-permute-start.15 = (bf16[256,512]{1,0:T(8,128)(2,1)S(1)}, bf16[256,512]{1,0:T(8,128)(2,1)S(1)}, u32[]{:S(2)}, u32[]{:S(2)}) collective-permute-start(bf16[256,512]{1,0:T(8,128)(2,1)S(1)} %collective-permute-done.11), channel_id=1, source_target_pairs={{0,4},{4,8},{8,12},{12,14},{14,10},{10,6},{6,2},{2,0},{1,5},{5,9},... | collective-permute-start | bytes 786440 | tf_op jit(solution)/shard_map/ppermute | solution.py:32
  39.7 3.3 %collective-permute-done.14 = bf16[256,512]{1,0:T(8,128)(2,1)S(1)} collective-permute-done((bf16[256,512]{1,0:T(8,128)(2,1)S(1)}, bf16[256,512]{1,0:T(8,128)(2,1)S(1)}, u32[]{:S(2)}, u32[]{:S(2)}) %collective-permute-start.14) | collective-permute-done | bytes 262176 | tf_op jit(solution)/shard_map/ppermute | solution.py:32
  44.2 2.9 %collective-permute-done.15 = bf16[256,512]{1,0:T(8,128)(2,1)S(1)} collective-permute-done((bf16[256,512]{1,0:T(8,128)(2,1)S(1)}, bf16[256,512]{1,0:T(8,128)(2,1)S(1)}, u32[]{:S(2)}, u32[]{:S(2)}) %collective-permute-start.15) | collective-permute-done | bytes 262176 | tf_op jit(solution)/shard_map/ppermute | solution.py:32
  47.5 3.0 %collective-permute-done.16 = bf16[256,512]{1,0:T(8,128)(2,1)S(1)} collective-permute-done((bf16[256,512]{1,0:T(8,128)(2,1)S(1)}, bf16[256,512]{1,0:T(8,128)(2,1)S(1)}, u32[]{:S(2)}, u32[]{:S(2)}) %collective-permute-start.16) | collective-permute-done | bytes 262176 | tf_op jit(solution)/shard_map/ppermute | solution.py:32
  59.2 2.3 %collective-permute-done.19 = bf16[6,1024]{1,0:T(8,128)(2,1)S(1)} collective-permute-done((bf16[6,1024]{1,0:T(8,128)(2,1)S(1)}, bf16[6,1024]{1,0:T(8,128)(2,1)S(1)}, u32[]{:S(2)}, u32[]{:S(2)}) %collective-permute-start.19) | collective-permute-done | bytes 12320 | tf_op jit(solution)/shard_map/ppermute | solution.py:64
  61.5 2.3 %collective-permute-done.20 = bf16[6,1024]{1,0:T(8,128)(2,1)S(1)} collective-permute-done((bf16[6,1024]{1,0:T(8,128)(2,1)S(1)}, bf16[6,1024]{1,0:T(8,128)(2,1)S(1)}, u32[]{:S(2)}, u32[]{:S(2)}) %collective-permute-start.20) | collective-permute-done | bytes 12320 | tf_op jit(solution)/shard_map/ppermute | solution.py:64
  63.8 2.3 %collective-permute-done.21 = bf16[6,1024]{1,0:T(8,128)(2,1)S(1)} collective-permute-done((bf16[6,1024]{1,0:T(8,128)(2,1)S(1)}, bf16[6,1024]{1,0:T(8,128)(2,1)S(1)}, u32[]{:S(2)}, u32[]{:S(2)}) %collective-permute-start.21) | collective-permute-done | bytes 12320 | tf_op jit(solution)/shard_map/ppermute | solution.py:64
  69.9 1.5 %collective-permute-start.31 = (bf16[256,512]{1,0:T(8,128)(2,1)S(1)}, bf16[256,512]{1,0:T(8,128)(2,1)S(1)}, u32[]{:S(2)}, u32[]{:S(2)}) collective-permute-start(bf16[256,512]{1,0:T(8,128)(2,1)S(1)} %convolution_convert_fusion.1), channel_id=1, source_target_pairs={{0,4},{4,8},{8,12},{12,14},{14,10},{10,6},{6,2},{2,0},{1,5},{5,9},... | collective-permute-start | bytes 786440 | tf_op jit(solution)/shard_map/ppermute | solution.py:32
  73.2 1.5 %collective-permute-start.34 = (bf16[256,512]{1,0:T(8,128)(2,1)S(1)}, bf16[256,512]{1,0:T(8,128)(2,1)S(1)}, u32[]{:S(2)}, u32[]{:S(2)}) collective-permute-start(bf16[256,512]{1,0:T(8,128)(2,1)S(1)} %convolution_convert_fusion), channel_id=1, source_target_pairs={{0,2},{4,0},{8,4},{12,8},{14,12},{10,14},{6,10},{2,6},{1,3},{5,1},... | collective-permute-start | bytes 786440 | tf_op jit(solution)/shard_map/ppermute | solution.py:32
  75.3 3.8 %collective-permute-done.31 = bf16[256,512]{1,0:T(8,128)(2,1)S(1)} collective-permute-done((bf16[256,512]{1,0:T(8,128)(2,1)S(1)}, bf16[256,512]{1,0:T(8,128)(2,1)S(1)}, u32[]{:S(2)}, u32[]{:S(2)}) %collective-permute-start.31) | collective-permute-done | bytes 262176 | tf_op jit(solution)/shard_map/ppermute | solution.py:32
  79.7 1.5 %collective-permute-start.32 = (bf16[256,512]{1,0:T(8,128)(2,1)S(1)}, bf16[256,512]{1,0:T(8,128)(2,1)S(1)}, u32[]{:S(2)}, u32[]{:S(2)}) collective-permute-start(bf16[256,512]{1,0:T(8,128)(2,1)S(1)} %fusion.6), channel_id=1, source_target_pairs={{0,4},{4,8},{8,12},{12,14},{14,10},{10,6},{6,2},{2,0},{1,5},{5,9},... | collective-permute-start | bytes 786440 | tf_op jit(solution)/shard_map/ppermute | solution.py:32
  81.2 3.5 %collective-permute-done.23 = bf16[256,512]{1,0:T(8,128)(2,1)S(1)} collective-permute-done((bf16[256,512]{1,0:T(8,128)(2,1)S(1)}, bf16[256,512]{1,0:T(8,128)(2,1)S(1)}, u32[]{:S(2)}, u32[]{:S(2)}) %collective-permute-start.23) | collective-permute-done | bytes 262176 | tf_op jit(solution)/shard_map/ppermute | solution.py:32
  87.6 1.6 %collective-permute-start.25 = (bf16[256,512]{1,0:T(8,128)(2,1)S(1)}, bf16[256,512]{1,0:T(8,128)(2,1)S(1)}, u32[]{:S(2)}, u32[]{:S(2)}) collective-permute-start(bf16[256,512]{1,0:T(8,128)(2,1)S(1)} %fusion.3), channel_id=1, source_target_pairs={{0,4},{4,8},{8,12},{12,14},{14,10},{10,6},{6,2},{2,0},{1,5},{5,9},... | collective-permute-start | bytes 786440 | tf_op jit(solution)/shard_map/ppermute | solution.py:32
  89.3 1.3 %collective-permute-start.24 = (bf16[256,1024]{1,0:T(8,128)(2,1)S(1)}, bf16[256,1024]{1,0:T(8,128)(2,1)S(1)}, u32[]{:S(2)}, u32[]{:S(2)}) collective-permute-start(bf16[256,1024]{1,0:T(8,128)(2,1)S(1)} %convert_element_type.163), channel_id=1, source_target_pairs={{0,16},{1,17},{2,18},{3,19},{4,20},{5,21},{6,22},{7,23},{8,24},{9,... | collective-permute-start | bytes 1572872 | tf_op jit(solution)/shard_map/ppermute | solution.py:40
  92.0 2.6 %collective-permute-done.35 = bf16[256,512]{1,0:T(8,128)(2,1)S(1)} collective-permute-done((bf16[256,512]{1,0:T(8,128)(2,1)S(1)}, bf16[256,512]{1,0:T(8,128)(2,1)S(1)}, u32[]{:S(2)}, u32[]{:S(2)}) %collective-permute-start.35) | collective-permute-done | bytes 262176 | tf_op jit(solution)/shard_map/ppermute | solution.py:32
  96.0 2.0 %collective-permute-start.33 = (bf16[256,512]{1,0:T(8,128)(2,1)S(1)}, bf16[256,512]{1,0:T(8,128)(2,1)S(1)}, u32[]{:S(2)}, u32[]{:S(2)}) collective-permute-start(bf16[256,512]{1,0:T(8,128)(2,1)S(1)} %fusion.5), channel_id=1, source_target_pairs={{0,4},{4,8},{8,12},{12,14},{14,10},{10,6},{6,2},{2,0},{1,5},{5,9},... | collective-permute-start | bytes 786440 | tf_op jit(solution)/shard_map/ppermute | solution.py:32
  98.6 1.6 %collective-permute-start.26 = (bf16[256,512]{1,0:T(8,128)(2,1)S(1)}, bf16[256,512]{1,0:T(8,128)(2,1)S(1)}, u32[]{:S(2)}, u32[]{:S(2)}) collective-permute-start(bf16[256,512]{1,0:T(8,128)(2,1)S(1)} %fusion.2), channel_id=1, source_target_pairs={{0,4},{4,8},{8,12},{12,14},{14,10},{10,6},{6,2},{2,0},{1,5},{5,9},... | collective-permute-start | bytes 786440 | tf_op jit(solution)/shard_map/ppermute | solution.py:32
  100.2 4.4 %collective-permute-done.36 = bf16[256,512]{1,0:T(8,128)(2,1)S(1)} collective-permute-done((bf16[256,512]{1,0:T(8,128)(2,1)S(1)}, bf16[256,512]{1,0:T(8,128)(2,1)S(1)}, u32[]{:S(2)}, u32[]{:S(2)}) %collective-permute-start.36) | collective-permute-done | bytes 262176 | tf_op jit(solution)/shard_map/ppermute | solution.py:32
  106.3 1.4 %collective-permute-start.30 = (bf16[256,512]{1,0:T(8,128)(2,1)S(1)}, bf16[256,512]{1,0:T(8,128)(2,1)S(1)}, u32[]{:S(2)}, u32[]{:S(2)}) collective-permute-start(bf16[256,512]{1,0:T(8,128)(2,1)S(1)} %convolution_add_fusion.6), channel_id=1, source_target_pairs={{0,2},{4,0},{8,4},{12,8},{14,12},{10,14},{6,10},{2,6},{1,3},{5,1},... | collective-permute-start | bytes 786440 | tf_op jit(solution)/shard_map/ppermute | solution.py:32
  109.0 5.4 %collective-permute-done.37 = bf16[256,512]{1,0:T(8,128)(2,1)S(1)} collective-permute-done((bf16[256,512]{1,0:T(8,128)(2,1)S(1)}, bf16[256,512]{1,0:T(8,128)(2,1)S(1)}, u32[]{:S(2)}, u32[]{:S(2)}) %collective-permute-start.37) | collective-permute-done | bytes 262176 | tf_op jit(solution)/shard_map/ppermute | solution.py:32
  114.6 2.9 %collective-permute-done.30 = bf16[256,512]{1,0:T(8,128)(2,1)S(1)} collective-permute-done((bf16[256,512]{1,0:T(8,128)(2,1)S(1)}, bf16[256,512]{1,0:T(8,128)(2,1)S(1)}, u32[]{:S(2)}, u32[]{:S(2)}) %collective-permute-start.30) | collective-permute-done | bytes 262176 | tf_op jit(solution)/shard_map/ppermute | solution.py:32
  (128 shorter events, 37.5 us)
Async XLA Ops:
  0.0 25.5 %collective-permute-start = (bf16[3,128,4096]{2,1,0:T(8,128)(2,1)}, bf16[3,128,4096]{2,1,0:T(8,128)(2,1)S(1)}, u32[]{:S(2)}, u32[]{:S(2)}) collective-permute-start(bf16[3,128,4096]{2,1,0:T(8,128)(2,1)} %bitcast.53), channel_id=1, source_target_pairs={{0,1},{1,0},{2,3},{3,2},{4,5},{5,4},{6,7},{7,6},{8,9},{9,8},{10,11... | collective-permute-start | bytes 9437192 | tf_op jit(solution)/shard_map/ppermute | solution.py:52
  2.1 9.7 %collective-permute-start.2 = (bf16[256,512]{1,0:T(8,128)(2,1)S(1)}, bf16[256,512]{1,0:T(8,128)(2,1)S(1)}, u32[]{:S(2)}, u32[]{:S(2)}) collective-permute-start(bf16[256,512]{1,0:T(8,128)(2,1)S(1)} %get-tuple-element.93), channel_id=1, source_target_pairs={{0,4},{4,8},{8,12},{12,14},{14,10},{10,6},{6,2},{2,0},{1,5},{5,9},... | collective-permute-start | bytes 786440 | tf_op jit(solution)/shard_map/ppermute | solution.py:32
  5.1 9.2 %collective-permute-start.3 = (bf16[256,512]{1,0:T(8,128)(2,1)S(1)}, bf16[256,512]{1,0:T(8,128)(2,1)S(1)}, u32[]{:S(2)}, u32[]{:S(2)}) collective-permute-start(bf16[256,512]{1,0:T(8,128)(2,1)S(1)} %get-tuple-element.93), channel_id=1, source_target_pairs={{0,2},{4,0},{8,4},{12,8},{14,12},{10,14},{6,10},{2,6},{1,3},{5,1},... | collective-permute-start | bytes 786440 | tf_op jit(solution)/shard_map/ppermute | solution.py:32
  6.1 15.0 %collective-permute-start.5 = (bf16[256,512]{1,0:T(8,128)(2,1)S(1)}, bf16[256,512]{1,0:T(8,128)(2,1)S(1)}, u32[]{:S(2)}, u32[]{:S(2)}) collective-permute-start(bf16[256,512]{1,0:T(8,128)(2,1)S(1)} %collective-permute-done.1), channel_id=1, source_target_pairs={{0,2},{4,0},{8,4},{12,8},{14,12},{10,14},{6,10},{2,6},{1,3},{5,1},... | collective-permute-start | bytes 786440 | tf_op jit(solution)/shard_map/ppermute | solution.py:32
  9.0 12.2 %collective-permute-start.4 = (bf16[256,512]{1,0:T(8,128)(2,1)S(1)}, bf16[256,512]{1,0:T(8,128)(2,1)S(1)}, u32[]{:S(2)}, u32[]{:S(2)}) collective-permute-start(bf16[256,512]{1,0:T(8,128)(2,1)S(1)} %collective-permute-done.1), channel_id=1, source_target_pairs={{0,4},{4,8},{8,12},{12,14},{14,10},{10,6},{6,2},{2,0},{1,5},{5,9},... | collective-permute-start | bytes 786440 | tf_op jit(solution)/shard_map/ppermute | solution.py:32
  11.8 11.6 %collective-permute-start.7 = (bf16[256,512]{1,0:T(8,128)(2,1)S(1)}, bf16[256,512]{1,0:T(8,128)(2,1)S(1)}, u32[]{:S(2)}, u32[]{:S(2)}) collective-permute-start(bf16[256,512]{1,0:T(8,128)(2,1)S(1)} %collective-permute-done.2), channel_id=1, source_target_pairs={{0,4},{4,8},{8,12},{12,14},{14,10},{10,6},{6,2},{2,0},{1,5},{5,9},... | collective-permute-start | bytes 786440 | tf_op jit(solution)/shard_map/ppermute | solution.py:32
  14.3 11.2 %collective-permute-start.8 = (bf16[256,512]{1,0:T(8,128)(2,1)S(1)}, bf16[256,512]{1,0:T(8,128)(2,1)S(1)}, u32[]{:S(2)}, u32[]{:S(2)}) collective-permute-start(bf16[256,512]{1,0:T(8,128)(2,1)S(1)} %collective-permute-done.3), channel_id=1, source_target_pairs={{0,2},{4,0},{8,4},{12,8},{14,12},{10,14},{6,10},{2,6},{1,3},{5,1},... | collective-permute-start | bytes 786440 | tf_op jit(solution)/shard_map/ppermute | solution.py:32
  21.2 11.4 %collective-permute-start.9 = (bf16[256,512]{1,0:T(8,128)(2,1)S(1)}, bf16[256,512]{1,0:T(8,128)(2,1)S(1)}, u32[]{:S(2)}, u32[]{:S(2)}) collective-permute-start(bf16[256,512]{1,0:T(8,128)(2,1)S(1)} %collective-permute-done.4), channel_id=1, source_target_pairs={{0,4},{4,8},{8,12},{12,14},{14,10},{10,6},{6,2},{2,0},{1,5},{5,9},... | collective-permute-start | bytes 786440 | tf_op jit(solution)/shard_map/ppermute | solution.py:32
  23.3 11.3 %collective-permute-start.10 = (bf16[256,512]{1,0:T(8,128)(2,1)S(1)}, bf16[256,512]{1,0:T(8,128)(2,1)S(1)}, u32[]{:S(2)}, u32[]{:S(2)}) collective-permute-start(bf16[256,512]{1,0:T(8,128)(2,1)S(1)} %collective-permute-done.5), channel_id=1, source_target_pairs={{0,2},{4,0},{8,4},{12,8},{14,12},{10,14},{6,10},{2,6},{1,3},{5,1},... | collective-permute-start | bytes 786440 | tf_op jit(solution)/shard_map/ppermute | solution.py:32
  23.4 11.3 %collective-permute-start.11 = (bf16[256,512]{1,0:T(8,128)(2,1)S(1)}, bf16[256,512]{1,0:T(8,128)(2,1)S(1)}, u32[]{:S(2)}, u32[]{:S(2)}) collective-permute-start(bf16[256,512]{1,0:T(8,128)(2,1)S(1)} %collective-permute-done.7), channel_id=1, source_target_pairs={{0,4},{4,8},{8,12},{12,14},{14,10},{10,6},{6,2},{2,0},{1,5},{5,9},... | collective-permute-start | bytes 786440 | tf_op jit(solution)/shard_map/ppermute | solution.py:32
  25.5 25.5 %collective-permute-start.12 = (bf16[256,512]{1,0:T(8,128)(2,1)S(1)}, bf16[256,512]{1,0:T(8,128)(2,1)S(1)}, u32[]{:S(2)}, u32[]{:S(2)}) collective-permute-start(bf16[256,512]{1,0:T(8,128)(2,1)S(1)} %collective-permute-done.8), channel_id=1, source_target_pairs={{0,2},{4,0},{8,4},{12,8},{14,12},{10,14},{6,10},{2,6},{1,3},{5,1},... | collective-permute-start | bytes 786440 | tf_op jit(solution)/shard_map/ppermute | solution.py:32
  32.6 11.2 %collective-permute-start.13 = (bf16[256,512]{1,0:T(8,128)(2,1)S(1)}, bf16[256,512]{1,0:T(8,128)(2,1)S(1)}, u32[]{:S(2)}, u32[]{:S(2)}) collective-permute-start(bf16[256,512]{1,0:T(8,128)(2,1)S(1)} %collective-permute-done.9), channel_id=1, source_target_pairs={{0,4},{4,8},{8,12},{12,14},{14,10},{10,6},{6,2},{2,0},{1,5},{5,9},... | collective-permute-start | bytes 786440 | tf_op jit(solution)/shard_map/ppermute | solution.py:32
  34.6 8.4 %collective-permute-start.14 = (bf16[256,512]{1,0:T(8,128)(2,1)S(1)}, bf16[256,512]{1,0:T(8,128)(2,1)S(1)}, u32[]{:S(2)}, u32[]{:S(2)}) collective-permute-start(bf16[256,512]{1,0:T(8,128)(2,1)S(1)} %collective-permute-done.10), channel_id=1, source_target_pairs={{0,2},{4,0},{8,4},{12,8},{14,12},{10,14},{6,10},{2,6},{1,3},{5,1},... | collective-permute-start | bytes 786440 | tf_op jit(solution)/shard_map/ppermute | solution.py:32
  34.7 12.3 %collective-permute-start.15 = (bf16[256,512]{1,0:T(8,128)(2,1)S(1)}, bf16[256,512]{1,0:T(8,128)(2,1)S(1)}, u32[]{:S(2)}, u32[]{:S(2)}) collective-permute-start(bf16[256,512]{1,0:T(8,128)(2,1)S(1)} %collective-permute-done.11), channel_id=1, source_target_pairs={{0,4},{4,8},{8,12},{12,14},{14,10},{10,6},{6,2},{2,0},{1,5},{5,9},... | collective-permute-start | bytes 786440 | tf_op jit(solution)/shard_map/ppermute | solution.py:32
  43.0 7.5 %collective-permute-start.16 = (bf16[256,512]{1,0:T(8,128)(2,1)S(1)}, bf16[256,512]{1,0:T(8,128)(2,1)S(1)}, u32[]{:S(2)}, u32[]{:S(2)}) collective-permute-start(bf16[256,512]{1,0:T(8,128)(2,1)S(1)} %collective-permute-done.14), channel_id=1, source_target_pairs={{0,2},{4,0},{8,4},{12,8},{14,12},{10,14},{6,10},{2,6},{1,3},{5,1},... | collective-permute-start | bytes 786440 | tf_op jit(solution)/shard_map/ppermute | solution.py:32
  56.2 7.7 %collective-permute-start.20 = (bf16[6,1024]{1,0:T(8,128)(2,1)S(1)}, bf16[6,1024]{1,0:T(8,128)(2,1)S(1)}, u32[]{:S(2)}, u32[]{:S(2)}) collective-permute-start(bf16[6,1024]{1,0:T(8,128)(2,1)S(1)} %maximum_select_fusion.2), channel_id=1, source_target_pairs={{24,0},{23,1},{28,4},{19,5},{30,8},{17,9},{26,12},{21,13},{22,14},... | collective-permute-start | bytes 36872 | tf_op jit(solution)/shard_map/ppermute | solution.py:64
  57.5 8.6 %collective-permute-start.21 = (bf16[6,1024]{1,0:T(8,128)(2,1)S(1)}, bf16[6,1024]{1,0:T(8,128)(2,1)S(1)}, u32[]{:S(2)}, u32[]{:S(2)}) collective-permute-start(bf16[6,1024]{1,0:T(8,128)(2,1)S(1)} %maximum_select_fusion.2), channel_id=1, source_target_pairs={{28,0},{19,1},{30,4},{17,5},{26,8},{21,9},{22,12},{25,13},{18,14},... | collective-permute-start | bytes 36872 | tf_op jit(solution)/shard_map/ppermute | solution.py:64
  69.9 9.2 %collective-permute-start.31 = (bf16[256,512]{1,0:T(8,128)(2,1)S(1)}, bf16[256,512]{1,0:T(8,128)(2,1)S(1)}, u32[]{:S(2)}, u32[]{:S(2)}) collective-permute-start(bf16[256,512]{1,0:T(8,128)(2,1)S(1)} %convolution_convert_fusion.1), channel_id=1, source_target_pairs={{0,4},{4,8},{8,12},{12,14},{14,10},{10,6},{6,2},{2,0},{1,5},{5,9},... | collective-permute-start | bytes 786440 | tf_op jit(solution)/shard_map/ppermute | solution.py:32
  72.0 12.7 %collective-permute-start.23 = (bf16[256,512]{1,0:T(8,128)(2,1)S(1)}, bf16[256,512]{1,0:T(8,128)(2,1)S(1)}, u32[]{:S(2)}, u32[]{:S(2)}) collective-permute-start(bf16[256,512]{1,0:T(8,128)(2,1)S(1)} %convolution_convert_fusion.3), channel_id=1, source_target_pairs={{0,4},{4,8},{8,12},{12,14},{14,10},{10,6},{6,2},{2,0},{1,5},{5,9},... | collective-permute-start | bytes 786440 | tf_op jit(solution)/shard_map/ppermute | solution.py:32
  73.2 12.7 %collective-permute-start.34 = (bf16[256,512]{1,0:T(8,128)(2,1)S(1)}, bf16[256,512]{1,0:T(8,128)(2,1)S(1)}, u32[]{:S(2)}, u32[]{:S(2)}) collective-permute-start(bf16[256,512]{1,0:T(8,128)(2,1)S(1)} %convolution_convert_fusion), channel_id=1, source_target_pairs={{0,2},{4,0},{8,4},{12,8},{14,12},{10,14},{6,10},{2,6},{1,3},{5,1},... | collective-permute-start | bytes 786440 | tf_op jit(solution)/shard_map/ppermute | solution.py:32
  74.7 15.9 %collective-permute-start.28 = (bf16[256,512]{1,0:T(8,128)(2,1)S(1)}, bf16[256,512]{1,0:T(8,128)(2,1)S(1)}, u32[]{:S(2)}, u32[]{:S(2)}) collective-permute-start(bf16[256,512]{1,0:T(8,128)(2,1)S(1)} %convolution_convert_fusion.2), channel_id=1, source_target_pairs={{0,2},{4,0},{8,4},{12,8},{14,12},{10,14},{6,10},{2,6},{1,3},{5,1},... | collective-permute-start | bytes 786440 | tf_op jit(solution)/shard_map/ppermute | solution.py:32
  79.7 15.7 %collective-permute-start.32 = (bf16[256,512]{1,0:T(8,128)(2,1)S(1)}, bf16[256,512]{1,0:T(8,128)(2,1)S(1)}, u32[]{:S(2)}, u32[]{:S(2)}) collective-permute-start(bf16[256,512]{1,0:T(8,128)(2,1)S(1)} %fusion.6), channel_id=1, source_target_pairs={{0,4},{4,8},{8,12},{12,14},{14,10},{10,6},{6,2},{2,0},{1,5},{5,9},... | collective-permute-start | bytes 786440 | tf_op jit(solution)/shard_map/ppermute | solution.py:32
  86.5 8.2 %collective-permute-start.35 = (bf16[256,512]{1,0:T(8,128)(2,1)S(1)}, bf16[256,512]{1,0:T(8,128)(2,1)S(1)}, u32[]{:S(2)}, u32[]{:S(2)}) collective-permute-start(bf16[256,512]{1,0:T(8,128)(2,1)S(1)} %fusion.9), channel_id=1, source_target_pairs={{0,2},{4,0},{8,4},{12,8},{14,12},{10,14},{6,10},{2,6},{1,3},{5,1},... | collective-permute-start | bytes 786440 | tf_op jit(solution)/shard_map/ppermute | solution.py:32
  87.6 10.4 %collective-permute-start.25 = (bf16[256,512]{1,0:T(8,128)(2,1)S(1)}, bf16[256,512]{1,0:T(8,128)(2,1)S(1)}, u32[]{:S(2)}, u32[]{:S(2)}) collective-permute-start(bf16[256,512]{1,0:T(8,128)(2,1)S(1)} %fusion.3), channel_id=1, source_target_pairs={{0,4},{4,8},{8,12},{12,14},{14,10},{10,6},{6,2},{2,0},{1,5},{5,9},... | collective-permute-start | bytes 786440 | tf_op jit(solution)/shard_map/ppermute | solution.py:32
  89.3 17.0 %collective-permute-start.24 = (bf16[256,1024]{1,0:T(8,128)(2,1)S(1)}, bf16[256,1024]{1,0:T(8,128)(2,1)S(1)}, u32[]{:S(2)}, u32[]{:S(2)}) collective-permute-start(bf16[256,1024]{1,0:T(8,128)(2,1)S(1)} %convert_element_type.163), channel_id=1, source_target_pairs={{0,16},{1,17},{2,18},{3,19},{4,20},{5,21},{6,22},{7,23},{8,24},{9,... | collective-permute-start | bytes 1572872 | tf_op jit(solution)/shard_map/ppermute | solution.py:40
  91.2 14.5 %collective-permute-start.29 = (bf16[256,512]{1,0:T(8,128)(2,1)S(1)}, bf16[256,512]{1,0:T(8,128)(2,1)S(1)}, u32[]{:S(2)}, u32[]{:S(2)}) collective-permute-start(bf16[256,512]{1,0:T(8,128)(2,1)S(1)} %fusion.4), channel_id=1, source_target_pairs={{0,2},{4,0},{8,4},{12,8},{14,12},{10,14},{6,10},{2,6},{1,3},{5,1},... | collective-permute-start | bytes 786440 | tf_op jit(solution)/shard_map/ppermute | solution.py:32
  95.3 9.3 %collective-permute-start.36 = (bf16[256,512]{1,0:T(8,128)(2,1)S(1)}, bf16[256,512]{1,0:T(8,128)(2,1)S(1)}, u32[]{:S(2)}, u32[]{:S(2)}) collective-permute-start(bf16[256,512]{1,0:T(8,128)(2,1)S(1)} %fusion.8), channel_id=1, source_target_pairs={{0,2},{4,0},{8,4},{12,8},{14,12},{10,14},{6,10},{2,6},{1,3},{5,1},... | collective-permute-start | bytes 786440 | tf_op jit(solution)/shard_map/ppermute | solution.py:32
  96.0 11.6 %collective-permute-start.33 = (bf16[256,512]{1,0:T(8,128)(2,1)S(1)}, bf16[256,512]{1,0:T(8,128)(2,1)S(1)}, u32[]{:S(2)}, u32[]{:S(2)}) collective-permute-start(bf16[256,512]{1,0:T(8,128)(2,1)S(1)} %fusion.5), channel_id=1, source_target_pairs={{0,4},{4,8},{8,12},{12,14},{14,10},{10,6},{6,2},{2,0},{1,5},{5,9},... | collective-permute-start | bytes 786440 | tf_op jit(solution)/shard_map/ppermute | solution.py:32
  98.6 9.1 %collective-permute-start.26 = (bf16[256,512]{1,0:T(8,128)(2,1)S(1)}, bf16[256,512]{1,0:T(8,128)(2,1)S(1)}, u32[]{:S(2)}, u32[]{:S(2)}) collective-permute-start(bf16[256,512]{1,0:T(8,128)(2,1)S(1)} %fusion.2), channel_id=1, source_target_pairs={{0,4},{4,8},{8,12},{12,14},{14,10},{10,6},{6,2},{2,0},{1,5},{5,9},... | collective-permute-start | bytes 786440 | tf_op jit(solution)/shard_map/ppermute | solution.py:32
  105.1 9.3 %collective-permute-start.37 = (bf16[256,512]{1,0:T(8,128)(2,1)S(1)}, bf16[256,512]{1,0:T(8,128)(2,1)S(1)}, u32[]{:S(2)}, u32[]{:S(2)}) collective-permute-start(bf16[256,512]{1,0:T(8,128)(2,1)S(1)} %fusion.7), channel_id=1, source_target_pairs={{0,2},{4,0},{8,4},{12,8},{14,12},{10,14},{6,10},{2,6},{1,3},{5,1},... | collective-permute-start | bytes 786440 | tf_op jit(solution)/shard_map/ppermute | solution.py:32
  106.3 11.2 %collective-permute-start.30 = (bf16[256,512]{1,0:T(8,128)(2,1)S(1)}, bf16[256,512]{1,0:T(8,128)(2,1)S(1)}, u32[]{:S(2)}, u32[]{:S(2)}) collective-permute-start(bf16[256,512]{1,0:T(8,128)(2,1)S(1)} %convolution_add_fusion.6), channel_id=1, source_target_pairs={{0,2},{4,0},{8,4},{12,8},{14,12},{10,14},{6,10},{2,6},{1,3},{5,1},... | collective-permute-start | bytes 786440 | tf_op jit(solution)/shard_map/ppermute | solution.py:32
  108.3 9.2 %collective-permute-start.27 = (bf16[256,512]{1,0:T(8,128)(2,1)S(1)}, bf16[256,512]{1,0:T(8,128)(2,1)S(1)}, u32[]{:S(2)}, u32[]{:S(2)}) collective-permute-start(bf16[256,512]{1,0:T(8,128)(2,1)S(1)} %convolution_add_fusion.9), channel_id=1, source_target_pairs={{0,4},{4,8},{8,12},{12,14},{14,10},{10,6},{6,2},{2,0},{1,5},{5,9},... | collective-permute-start | bytes 786440 | tf_op jit(solution)/shard_map/ppermute | solution.py:32
  (12 other events, 38.8 us)

commit v15 on v14

--- a/solution.py
+++ b/solution.py
@@ -36,8 +36,78 @@
     return lax.optimization_barrier((first, block))[1]
 
 
+def to_refresher(block):
+    return lax.ppermute(block, "grp", [(0, 1)])
+
+
 def passed_on(weights):
-    return lax.ppermute(weights.astype(jnp.bfloat16), "grp", [(0, 1)])
+    return to_refresher(weights.astype(jnp.bfloat16))
+
+
+def odd_columns_kernel(rows, normed_ref, out_ref, sems):
+    tokens = out_ref.shape[0]
+    copies = []
+    for i in range(out_ref.shape[1] // rows):
+        source = normed_ref.at[pl.ds(0, tokens), pl.ds((cores * i + 1) * rows, rows)]
+        target = out_ref.at[:, pl.ds(i * rows, rows)]
+        copies.append(pltpu.make_async_copy(source, target, sems.at[i]))
+    for copy in copies:
+        copy.start()
+    for copy in copies:
+        copy.wait()
+
+
+def odd_columns(normed, rows):
+    tokens, width = normed.shape[0] // cores, normed.shape[1]
+    return pl.pallas_call(
+        functools.partial(odd_columns_kernel, rows),
+        in_specs=[pl.BlockSpec(memory_space=pl.ANY)],
+        out_specs=pl.BlockSpec(memory_space=pl.ANY),
+        out_shape=jax.ShapeDtypeStruct((tokens, width // cores), jnp.bfloat16),
+        scratch_shapes=[pltpu.SemaphoreType.DMA((width // (cores * rows),))],
+        compiler_params=pltpu.CompilerParams(vmem_limit_bytes=vmem_limit),
+        cost_estimate=pl.CostEstimate(
+            flops=0, bytes_accessed=2 * tokens * width, transcendentals=0
+        ),
+    )(normed)
+
+
+def shares_kernel(rows, flag_ref, normed_ref, own_ref, other_ref, out_ref, sems):
+    tokens = own_ref.shape[0]
+    copies = []
+    for i in range(out_ref.shape[1] // rows):
+        source = normed_ref.at[:, pl.ds(cores * i * rows, rows)]
+        target = out_ref.at[:, pl.ds(i * rows, rows)]
+        copies.append(pltpu.make_async_copy(source, target, sems.at[i]))
+    received = [
+        pltpu.make_async_copy(ref, out_ref.at[pl.ds(i * tokens, tokens), :], sems.at[i])
+        for i, ref in enumerate((own_ref, other_ref))
+    ]
+
+    def run(group):
+        for copy in group:
+            copy.start()
+        for copy in group:
+            copy.wait()
+
+    pl.when(flag_ref[0] == 1)(functools.partial(run, copies))
+    pl.when(flag_ref[0] != 1)(functools.partial(run, received))
+
+
+def shares(normed, own, other, flag, rows):
+    tokens, width = normed.shape
+    anywhere = pl.BlockSpec(memory_space=pl.ANY)
+    return pl.pallas_call(
+        functools.partial(shares_kernel, rows),
+        in_specs=[pl.BlockSpec(memory_space=pltpu.SMEM)] + [anywhere] * 3,
+        out_specs=anywhere,
+        out_shape=jax.ShapeDtypeStruct((tokens, width // cores), jnp.bfloat16),
+        scratch_shapes=[pltpu.SemaphoreType.DMA((width // (cores * rows),))],
+        compiler_params=pltpu.CompilerParams(vmem_limit_bytes=vmem_limit),
+        cost_estimate=pl.CostEstimate(
+            flops=0, bytes_accessed=2 * tokens * width, transcendentals=0
+        ),
+    )(flag, normed, own, other)
 
 
 def cut(array, axis, start, size):
@@ -132,10 +202,16 @@
         for offset in range(-span, span + 1)
         for i in range(2)
     }
-    scalars = [first_core, shift, own_columns, given_columns, trainer, *starts.values()]
-    weights, *scalars = lax.optimization_barrier([master[0], *scalars])
-    first_core, shift, own_columns, given_columns, trainer, *firsts = scalars
-    starts = dict(zip(starts, firsts))
+    share_starts = {
+        offset: ring_chip(place + offset, chips) * rows for offset in range(-span, span + 1)
+    }
+    flag = trainer.astype(jnp.int32)[None]
+    scalars = [first_core, shift, own_columns, given_columns, trainer, flag]
+    tables = [list(starts.values()), list(share_starts.values())]
+    weights, scalars, tables = lax.optimization_barrier((master[0], scalars, tables))
+    first_core, shift, own_columns, given_columns, trainer, flag = scalars
+    starts = dict(zip(starts, tables[0]))
+    share_starts = dict(zip(share_starts, tables[1]))
     own = cut(weights, 1, own_columns, half).astype(jnp.bfloat16)
     given = cut(weights, 1, given_columns, half).astype(jnp.bfloat16)
     sibling = from_sibling(given)
@@ -143,7 +219,9 @@
     other_states = from_sibling(states)
     sent = [(0, 1), (0, -1), (1, 1), (1, -1)]
     normed_own = normalize(states, gain, 0)
-    normed = normalize(other_states, gain, 1, normed_own)
+    odd = odd_columns(normed_own, rows)
+    normed = normalize(other_states, gain, 1, filled=after(odd, normed_own))
+    odd = to_refresher(odd)
     if chips <= longest_ring:
         moving = {(i, by): along_ring((own, sibling)[i], by) for i, by in sent}
 
@@ -188,6 +266,9 @@
     active = jnp.tanh(total).reshape(seqs, length, half)
     there = jnp.arange(length)[None, :, None] < lengths[:, None, None]
     pooled = jnp.sum(jnp.where(there, active, 0.0), axis=1) / counts[:, None]
+    slope = jnp.where(there, 1.0 - active * active, 0.0).reshape(seqs * length, half)
+    slope_sent = to_refresher(slope.astype(jnp.bfloat16))
+    odd = after(pooled, odd)
     pooled_other = from_sibling(pooled)
     pooled_other = jnp.concatenate([pooled_other[seq_dev:], pooled_other[:seq_dev]])
     whole = in_core_order(pooled, pooled_other, first_core, axis=1)
@@ -233,27 +314,30 @@
     inner = jnp.sum(whole * unit_grad, axis=-1, keepdims=True)
     pooled_grad = scale * unit_grad - whole * (scale * scale * scale) * inner / embedding
     pooled_grad = cut(pooled_grad, 1, own_columns, half)
-    delta = (pooled_grad / counts[:, None])[:, None, :] * (1.0 - active * active)
-    delta = jnp.where(there, delta, 0.0)
-    delta = delta.astype(jnp.bfloat16).reshape(seqs * length, half)
-
-    def term(offset, i, delta):
-        return lax.dot_general(
-            columns(offset, i),
-            delta,
-            (((0,), (0,)), ((), ())),
-            preferred_element_type=jnp.float32,
-        )
-
+    weighted = pooled_grad / counts[:, None]
     if chips <= longest_ring:
+        share = shares(normed, odd, from_sibling(odd), flag, rows)
+        weighted = jnp.where(trainer, weighted, to_refresher(weighted))
+        slope = jnp.where(trainer, slope, slope_sent.astype(jnp.float32))
+        delta = weighted[:, None, :] * slope.reshape(seqs, length, half)
+        delta = delta.astype(jnp.bfloat16).reshape(seqs * length, half)
+        sub = half // 2
+
+        def term(offset, i, delta):
+            return lax.dot_general(
+                cut(share, 1, share_starts[offset], rows),
+                delta[:, i * sub : (i + 1) * sub],
+                (((0,), (0,)), ((), ())),
+                preferred_element_type=jnp.float32,
+            )
+
         arrived = {}
-        late = delta
-        early = delta
+        early = late = delta
         for step in range(chips // 2, 0, -1):
             for i, by in ((0, 1), (1, -1), (1, 1), (0, -1)):
                 if step == chips // 2 and (i, by) not in ((0, 1), (1, -1)):
                     continue
-                total = term(by * step, i, delta)
+                total = term(by * step, i, early if step > chips // 2 - 2 else late)
                 if (i, by) in arrived:
                     total = total + arrived[i, by].astype(jnp.float32)
                 if step == 1 and i == 0:
@@ -265,22 +349,35 @@
             if step == chips // 2:
                 late, weights = after(arrived[0, 1], (delta, weights))
                 copied = passed_on(weights)
-        owns = [term(0, i, late) for i in range(2)]
-        arrived[1, 1] = after(owns, arrived[1, 1])
-        arrived[0, -1] = after(owns, arrived[0, -1])
-        mine, other = [
-            owns[i] + arrived[i, 1].astype(jnp.float32) + arrived[i, -1].astype(jnp.float32)
-            for i in range(2)
-        ]
+        mine = jnp.concatenate(
+            [
+                term(0, i, late)
+                + arrived[i, 1].astype(jnp.float32)
+                + arrived[i, -1].astype(jnp.float32)
+                for i in range(2)
+            ],
+            axis=1,
+        )
+        sent = mine.astype(jnp.bfloat16)
+        to_first = [(2 * k + 1, 2 * k) for k in range(chips)]
+        to_first += [(2 * (chips + k), 2 * k + 1) for k in range(chips)]
+        to_second = [(2 * (chips + k) + 1, 2 * k + 1) for k in range(chips)]
+        devices = ("grp", "chip", "core")
+        one = lax.ppermute(sent, devices, to_first).astype(jnp.float32)
+        two = lax.ppermute(sent, devices, to_second).astype(jnp.float32)
+        shard = jnp.concatenate(
+            [jnp.where(first_core, mine, one), jnp.where(first_core, one, two)], axis=1
+        )
     else:
+        delta = weighted[:, None, :] * slope.reshape(seqs, length, half)
+        delta = delta.astype(jnp.bfloat16).reshape(seqs * length, half)
         grad = lax.dot_general(
             normed, delta, (((0,), (0,)), ((), ())), preferred_element_type=jnp.float32
         )
         copied = passed_on(weights)
         reduced = lax.psum_scatter(grad, "chip", scatter_dimension=0, tiled=True)
         mine, other = [cut(reduced, 0, part * rows, rows) for part in parts]
-    other = from_sibling(other)
-    shard = in_core_order(mine, other, first_core, axis=1)
+        shard = in_core_order(mine, from_sibling(other), first_core, axis=1)
     row_square = jnp.mean(shard * shard, axis=1, keepdims=True)
     normalized = shard * lax.rsqrt(row_square + 1e-06)
     result = jnp.where(trainer, normalized, copied.astype(jnp.float32))

time: 119 us -> 133 us (1.12)
  the two profiles are of different devices: /device:TPU:0 before, /device:TPU:1 now
where the time goes in v15:
time: 133 us
  starting transfers between devices  61.6 us (46%)
  waiting for transfers between devices  36.9 us (28%)
  matrix products  17.5 us (13%)
  Pallas kernels  8.21 us (6%)
  local copies, waits for them, and re-layouts  4.76 us (4%)
  other arithmetic  3.29 us (2%)
    ppermute x28, starting transfers between devices, along_ring(): return lax.ppermute(block, 'chip', pairs)  25.1 us
    ppermute x4, starting transfers between devices, to_refresher(): return lax.ppermute(block, 'grp', [(0, 1)])  15.6 us
    ppermute x28, waiting for transfers between devices, along_ring(): return lax.ppermute(block, 'chip', pairs)  14.3 us
    ppermute x4, waiting for transfers between devices, to_refresher(): return lax.ppermute(block, 'grp', [(0, 1)])  14 us
    ppermute x6, starting transfers between devices, from_sibling(): return lax.ppermute(block, 'core', [(0, 1), (1, 0)])  8.3 us
    dot_general x16, matrix products, term(): lax.dot_general(cut(share, 1, share_starts[offset], rows), delta[:, i * s...  7.96 us
    dot_general x16, matrix products, product(): jnp.dot(columns(offset, i), block, preferred_element_type=jnp.float32)  7.89 us
    pallas_call x2, Pallas kernels, normalize(): pl.pallas_call(functools.partial(normalize_kernel, 16), grid=(seqs,), in_...  7.16 us
  transfers between devices with their start and end apart: 44, of which 14 were waited for; matrix products, arithmetic and copies ran while one was open for 15% of the time, Pallas kernels for 6%

profile of v15, /device:TPU:1, one launch (start us, length us, event | category | flops | bytes accessed | tf_op | source)
XLA Modules:
  0.0 132.9 jit_solution(4715645235712985433)
XLA Ops:
  0.1 1.5 %dynamic-slice_convert_fusion.1 = (bf16[256,512]{1,0:T(8,128)(2,1)S(1)}, bf16[256,512]{1,0:T(8,128)(2,1)S(1)}) fusion(f32[256,1024]{1,0:T(8,128)} %bitcast.41, s32[]{:T(128)S(6)} %mul.321, s32[]{:T(128)S(6)} %mul.322), kind=kLoop, calls=%fused_computation.48 | loop fusion | bytes 1048584 | tf_op jit(solution)/shard_map/convert_element_type | solution.py:215
  2.0 2.4 %collective-permute-start.2 = (bf16[256,512]{1,0:T(8,128)(2,1)S(1)}, bf16[256,512]{1,0:T(8,128)(2,1)S(1)}, u32[]{:S(2)}, u32[]{:S(2)}) collective-permute-start(bf16[256,512]{1,0:T(8,128)(2,1)S(1)} %get-tuple-element.113), channel_id=1, source_target_pairs={{0,4},{4,8},{8,12},{12,14},{14,10},{10,6},{6,2},{2,0},{1,5},{5,9},... | collective-permute-start | bytes 786440 | tf_op jit(solution)/shard_map/ppermute | solution.py:32
  4.4 1.6 %collective-permute-done.1 = bf16[256,512]{1,0:T(8,128)(2,1)S(1)} collective-permute-done((bf16[256,512]{1,0:T(8,128)(2,1)S(1)}, bf16[256,512]{1,0:T(8,128)(2,1)S(1)}, u32[]{:S(2)}, u32[]{:S(2)}) %collective-permute-start.1) | collective-permute-done | bytes 262176 | tf_op jit(solution)/shard_map/ppermute | solution.py:122
  6.0 2.4 %collective-permute-start.5 = (bf16[256,512]{1,0:T(8,128)(2,1)S(1)}, bf16[256,512]{1,0:T(8,128)(2,1)S(1)}, u32[]{:S(2)}, u32[]{:S(2)}) collective-permute-start(bf16[256,512]{1,0:T(8,128)(2,1)S(1)} %collective-permute-done.1), channel_id=1, source_target_pairs={{0,2},{4,0},{8,4},{12,8},{14,12},{10,14},{6,10},{2,6},{1,3},{5,1},... | collective-permute-start | bytes 786440 | tf_op jit(solution)/shard_map/ppermute | solution.py:32
  8.5 2.2 %collective-permute-done.2 = bf16[256,512]{1,0:T(8,128)(2,1)S(1)} collective-permute-done((bf16[256,512]{1,0:T(8,128)(2,1)S(1)}, bf16[256,512]{1,0:T(8,128)(2,1)S(1)}, u32[]{:S(2)}, u32[]{:S(2)}) %collective-permute-start.2) | collective-permute-done | bytes 262176 | tf_op jit(solution)/shard_map/ppermute | solution.py:32
  12.1 1.9 %copy-done = bf16[1,3,128,4096]{3,2,1,0:T(8,128)(2,1)S(1)} copy-done((bf16[1,3,128,4096]{3,2,1,0:T(8,128)(2,1)S(1)}, bf16[1,3,128,4096]{3,2,1,0:T(8,128)(2,1)}, u32[]{:S(2)}) %copy-start) | copy-done | bytes 3145752
  14.7 3.6 %shard_map.64.normed_ref.refs_0_ = bf16[768,4096]{1,0:T(8,128)(2,1)S(1)} custom-call(bf16[3,128,4096]{2,1,0:T(8,128)(2,1)S(1)} %bitcast.37, f32[1,4096]{1,0:T(1,128)S(1)} %bitcast.38), custom_call_target="tpu_custom_call" | custom-call | flops 9437184 | bytes 6291456 | tf_op jit(solution)/shard_map/pallas_call | solution.py:169
  19.0 3.1 %collective-permute-start.17 = (bf16[384,2048]{1,0:T(8,128)(2,1)S(1)}, bf16[384,2048]{1,0:T(8,128)(2,1)S(1)}, u32[]{:S(2)}, u32[]{:S(2)}) collective-permute-start(bf16[384,2048]{1,0:T(8,128)(2,1)S(1)} %shard_map.65), channel_id=1, source_target_pairs={{0,16},{1,17},{2,18},{3,19},{4,20},{5,21},{6,22},{7,23},{8,24},{9,... | collective-permute-start | bytes 4718600 | tf_op jit(solution)/shard_map/ppermute | solution.py:40
  23.7 1.3 collective-permute-start.11
  25.1 3.6 %shard_map.66.normed_ref = bf16[768,4096]{1,0:T(8,128)(2,1)S(1)} custom-call(bf16[3,128,4096]{2,1,0:T(8,128)(2,1)S(1)} %collective-permute-done.states_ref, f32[1,4096]{1,0:T(1,128)S(1)} %bitcast.39, bf16[768,4096]{1,0:T(8,128)(2,1)S(1)} %shard_map.64.normed_ref.refs_0_), custom_call_target="tpu_custom_call", output_to_operand_aliasing={{}: (2, {})} | custom-call | flops 9437184 | bytes 6291456 | tf_op jit(solution)/shard_map/pallas_call | solution.py:169
  32.2 4.2 %collective-permute-start.6 = (s32[3,224]{1,0:T(4,128)S(1)}, s32[3,224]{1,0:T(4,128)S(1)}, u32[]{:S(2)}, u32[]{:S(2)}) collective-permute-start(s32[3,224]{1,0:T(4,128)S(1)} %pad_add_fusion.1), channel_id=1, source_target_pairs={{0,1},{1,0},{2,3},{3,2},{4,5},{5,4},{6,7},{7,6},{8,9},{9,8},{10,11... | collective-permute-start | bytes 8072 | tf_op jit(solution)/shard_map/ppermute | solution.py:122
  40.4 1.4 %collective-permute-start.13 = (bf16[256,512]{1,0:T(8,128)(2,1)S(1)}, bf16[256,512]{1,0:T(8,128)(2,1)S(1)}, u32[]{:S(2)}, u32[]{:S(2)}) collective-permute-start(bf16[256,512]{1,0:T(8,128)(2,1)S(1)} %collective-permute-done.9), channel_id=1, source_target_pairs={{0,4},{4,8},{8,12},{12,14},{14,10},{10,6},{6,2},{2,0},{1,5},{5,9},... | collective-permute-start | bytes 786440 | tf_op jit(solution)/shard_map/ppermute | solution.py:32
  45.6 5.2 %collective-permute-done.13 = bf16[256,512]{1,0:T(8,128)(2,1)S(1)} collective-permute-done((bf16[256,512]{1,0:T(8,128)(2,1)S(1)}, bf16[256,512]{1,0:T(8,128)(2,1)S(1)}, u32[]{:S(2)}, u32[]{:S(2)}) %collective-permute-start.13) | collective-permute-done | bytes 262176 | tf_op jit(solution)/shard_map/ppermute | solution.py:32
  52.9 2.6 %collective-permute-start.19 = (f32[6,512]{1,0:T(8,128)S(1)}, f32[6,512]{1,0:T(8,128)S(1)}, u32[]{:S(2)}, u32[]{:S(2)}) collective-permute-start(f32[6,512]{1,0:T(8,128)S(1)} %broadcast_divide_fusion), channel_id=1, source_target_pairs={{0,1},{1,0},{2,3},{3,2},{4,5},{5,4},{6,7},{7,6},{8,9},{9,8},{10,11... | collective-permute-start | bytes 36872 | tf_op jit(solution)/shard_map/ppermute | solution.py:122
  58.2 1.3 collective-permute-start.22
  59.5 1.3 collective-permute-start.21
  60.8 1.3 collective-permute-start.20
  62.5 7.7 %collective-permute-start.26 = (bf16[768,512]{1,0:T(8,128)(2,1)S(1)}, bf16[768,512]{1,0:T(8,128)(2,1)S(1)}, u32[]{:S(2)}, u32[]{:S(2)}) collective-permute-start(bf16[768,512]{1,0:T(8,128)(2,1)S(1)} %get-tuple-element.123), channel_id=1, source_target_pairs={{0,16},{1,17},{2,18},{3,19},{4,20},{5,21},{6,22},{7,23},{8,24},{9,... | collective-permute-start | bytes 2359304 | tf_op jit(solution)/shard_map/ppermute | solution.py:40
  73.9 14.0 %collective-permute-done.25 = f32[6,512]{1,0:T(8,128)S(1)} collective-permute-done((f32[6,512]{1,0:T(8,128)S(1)}, f32[6,512]{1,0:T(8,128)S(1)}, u32[]{:S(2)}, u32[]{:S(2)}) %collective-permute-start.25) | collective-permute-done | bytes 12320 | tf_op jit(solution)/shard_map/ppermute | solution.py:40
  90.1 1.5 %collective-permute-start.38 = (bf16[256,256]{1,0:T(8,128)(2,1)S(1)}, bf16[256,256]{1,0:T(8,128)(2,1)S(1)}, u32[]{:S(2)}, u32[]{:S(2)}) collective-permute-start(bf16[256,256]{1,0:T(8,128)(2,1)S(1)} %convolution_convert_fusion.2), channel_id=1, source_target_pairs={{0,2},{4,0},{8,4},{12,8},{14,12},{10,14},{6,10},{2,6},{1,3},{5,1},... | collective-permute-start | bytes 393224 | tf_op jit(solution)/shard_map/ppermute | solution.py:32
  92.7 1.5 %collective-permute-start.32 = (bf16[256,256]{1,0:T(8,128)(2,1)S(1)}, bf16[256,256]{1,0:T(8,128)(2,1)S(1)}, u32[]{:S(2)}, u32[]{:S(2)}) collective-permute-start(bf16[256,256]{1,0:T(8,128)(2,1)S(1)} %convolution_convert_fusion.1), channel_id=1, source_target_pairs={{0,2},{4,0},{8,4},{12,8},{14,12},{10,14},{6,10},{2,6},{1,3},{5,1},... | collective-permute-start | bytes 393224 | tf_op jit(solution)/shard_map/ppermute | solution.py:32
  94.5 3.5 %collective-permute-start.28 = (bf16[256,1024]{1,0:T(8,128)(2,1)S(1)}, bf16[256,1024]{1,0:T(8,128)(2,1)S(1)}, u32[]{:S(2)}, u32[]{:S(2)}) collective-permute-start(bf16[256,1024]{1,0:T(8,128)(2,1)S(1)} %convert_element_type.181), channel_id=1, source_target_pairs={{0,16},{1,17},{2,18},{3,19},{4,20},{5,21},{6,22},{7,23},{8,24},{9,... | collective-permute-start | bytes 1572872 | tf_op jit(solution)/shard_map/ppermute | solution.py:40
  99.2 1.5 %collective-permute-start.36 = (bf16[256,256]{1,0:T(8,128)(2,1)S(1)}, bf16[256,256]{1,0:T(8,128)(2,1)S(1)}, u32[]{:S(2)}, u32[]{:S(2)}) collective-permute-start(bf16[256,256]{1,0:T(8,128)(2,1)S(1)} %fusion.8), channel_id=1, source_target_pairs={{0,4},{4,8},{8,12},{12,14},{14,10},{10,6},{6,2},{2,0},{1,5},{5,9},... | collective-permute-start | bytes 393224 | tf_op jit(solution)/shard_map/ppermute | solution.py:32
  101.7 1.5 %collective-permute-start.29 = (bf16[256,256]{1,0:T(8,128)(2,1)S(1)}, bf16[256,256]{1,0:T(8,128)(2,1)S(1)}, u32[]{:S(2)}, u32[]{:S(2)}) collective-permute-start(bf16[256,256]{1,0:T(8,128)(2,1)S(1)} %fusion.5), channel_id=1, source_target_pairs={{0,4},{4,8},{8,12},{12,14},{14,10},{10,6},{6,2},{2,0},{1,5},{5,9},... | collective-permute-start | bytes 393224 | tf_op jit(solution)/shard_map/ppermute | solution.py:32
  104.3 1.5 %collective-permute-start.37 = (bf16[256,256]{1,0:T(8,128)(2,1)S(1)}, bf16[256,256]{1,0:T(8,128)(2,1)S(1)}, u32[]{:S(2)}, u32[]{:S(2)}) collective-permute-start(bf16[256,256]{1,0:T(8,128)(2,1)S(1)} %fusion.7), channel_id=1, source_target_pairs={{0,4},{4,8},{8,12},{12,14},{14,10},{10,6},{6,2},{2,0},{1,5},{5,9},... | collective-permute-start | bytes 393224 | tf_op jit(solution)/shard_map/ppermute | solution.py:32
  107.6 1.6 %collective-permute-start.30 = (bf16[256,256]{1,0:T(8,128)(2,1)S(1)}, bf16[256,256]{1,0:T(8,128)(2,1)S(1)}, u32[]{:S(2)}, u32[]{:S(2)}) collective-permute-start(bf16[256,256]{1,0:T(8,128)(2,1)S(1)} %fusion.4), channel_id=1, source_target_pairs={{0,4},{4,8},{8,12},{12,14},{14,10},{10,6},{6,2},{2,0},{1,5},{5,9},... | collective-permute-start | bytes 393224 | tf_op jit(solution)/shard_map/ppermute | solution.py:32
  110.3 1.5 %collective-permute-done.30 = bf16[256,256]{1,0:T(8,128)(2,1)S(1)} collective-permute-done((bf16[256,256]{1,0:T(8,128)(2,1)S(1)}, bf16[256,256]{1,0:T(8,128)(2,1)S(1)}, u32[]{:S(2)}, u32[]{:S(2)}) %collective-permute-start.30) | collective-permute-done | bytes 131104 | tf_op jit(solution)/shard_map/ppermute | solution.py:32
  113.1 1.5 %collective-permute-start.31 = (bf16[256,256]{1,0:T(8,128)(2,1)S(1)}, bf16[256,256]{1,0:T(8,128)(2,1)S(1)}, u32[]{:S(2)}, u32[]{:S(2)}) collective-permute-start(bf16[256,256]{1,0:T(8,128)(2,1)S(1)} %convolution_add_fusion.10), channel_id=1, source_target_pairs={{0,4},{4,8},{8,12},{12,14},{14,10},{10,6},{6,2},{2,0},{1,5},{5,9},... | collective-permute-start | bytes 393224 | tf_op jit(solution)/shard_map/ppermute | solution.py:32
  115.1 2.4 %collective-permute-done.34 = bf16[256,256]{1,0:T(8,128)(2,1)S(1)} collective-permute-done((bf16[256,256]{1,0:T(8,128)(2,1)S(1)}, bf16[256,256]{1,0:T(8,128)(2,1)S(1)}, u32[]{:S(2)}, u32[]{:S(2)}) %collective-permute-start.34) | collective-permute-done | bytes 131104 | tf_op jit(solution)/shard_map/ppermute | solution.py:32
  118.1 6.2 %collective-permute-start.42 = (bf16[256,512]{1,0:T(8,128)(2,1)S(1)}, bf16[256,512]{1,0:T(8,128)(2,1)S(1)}, u32[]{:S(2)}, u32[]{:S(2)}) collective-permute-start(bf16[256,512]{1,0:T(8,128)(2,1)S(1)} %fusion.16), channel_id=1, source_target_pairs={{1,0},{3,2},{5,4},{7,6},{9,8},{11,10},{13,12},{15,14},{16,1},{18,3... | collective-permute-start | bytes 786440 | tf_op jit(solution)/shard_map/ppermute | solution.py:366
  125.6 2.4 %collective-permute-done.42 = bf16[256,512]{1,0:T(8,128)(2,1)S(1)} collective-permute-done((bf16[256,512]{1,0:T(8,128)(2,1)S(1)}, bf16[256,512]{1,0:T(8,128)(2,1)S(1)}, u32[]{:S(2)}, u32[]{:S(2)}) %collective-permute-start.42) | collective-permute-done | bytes 262176 | tf_op jit(solution)/shard_map/ppermute | solution.py:366
  128.0 3.4 %collective-permute-done.43 = bf16[256,512]{1,0:T(8,128)(2,1)S(1)} collective-permute-done((bf16[256,512]{1,0:T(8,128)(2,1)S(1)}, bf16[256,512]{1,0:T(8,128)(2,1)S(1)}, u32[]{:S(2)}, u32[]{:S(2)}) %collective-permute-start.43) | collective-permute-done | bytes 262176 | tf_op jit(solution)/shard_map/ppermute | solution.py:367
  (143 shorter events, 39.9 us)
Async XLA Ops:
  0.0 25.0 %collective-permute-start = (bf16[3,128,4096]{2,1,0:T(8,128)(2,1)}, bf16[3,128,4096]{2,1,0:T(8,128)(2,1)S(1)}, u32[]{:S(2)}, u32[]{:S(2)}) collective-permute-start(bf16[3,128,4096]{2,1,0:T(8,128)(2,1)} %bitcast.36), channel_id=1, source_target_pairs={{0,1},{1,0},{2,3},{3,2},{4,5},{5,4},{6,7},{7,6},{8,9},{9,8},{10,11... | collective-permute-start | bytes 9437192 | tf_op jit(solution)/shard_map/ppermute | solution.py:122
  2.0 8.6 %collective-permute-start.2 = (bf16[256,512]{1,0:T(8,128)(2,1)S(1)}, bf16[256,512]{1,0:T(8,128)(2,1)S(1)}, u32[]{:S(2)}, u32[]{:S(2)}) collective-permute-start(bf16[256,512]{1,0:T(8,128)(2,1)S(1)} %get-tuple-element.113), channel_id=1, source_target_pairs={{0,4},{4,8},{8,12},{12,14},{14,10},{10,6},{6,2},{2,0},{1,5},{5,9},... | collective-permute-start | bytes 786440 | tf_op jit(solution)/shard_map/ppermute | solution.py:32
  4.4 7.4 %collective-permute-start.3 = (bf16[256,512]{1,0:T(8,128)(2,1)S(1)}, bf16[256,512]{1,0:T(8,128)(2,1)S(1)}, u32[]{:S(2)}, u32[]{:S(2)}) collective-permute-start(bf16[256,512]{1,0:T(8,128)(2,1)S(1)} %get-tuple-element.113), channel_id=1, source_target_pairs={{0,2},{4,0},{8,4},{12,8},{14,12},{10,14},{6,10},{2,6},{1,3},{5,1},... | collective-permute-start | bytes 786440 | tf_op jit(solution)/shard_map/ppermute | solution.py:32
  6.0 13.0 %collective-permute-start.5 = (bf16[256,512]{1,0:T(8,128)(2,1)S(1)}, bf16[256,512]{1,0:T(8,128)(2,1)S(1)}, u32[]{:S(2)}, u32[]{:S(2)}) collective-permute-start(bf16[256,512]{1,0:T(8,128)(2,1)S(1)} %collective-permute-done.1), channel_id=1, source_target_pairs={{0,2},{4,0},{8,4},{12,8},{14,12},{10,14},{6,10},{2,6},{1,3},{5,1},... | collective-permute-start | bytes 786440 | tf_op jit(solution)/shard_map/ppermute | solution.py:32
  8.4 13.7 %collective-permute-start.4 = (bf16[256,512]{1,0:T(8,128)(2,1)S(1)}, bf16[256,512]{1,0:T(8,128)(2,1)S(1)}, u32[]{:S(2)}, u32[]{:S(2)}) collective-permute-start(bf16[256,512]{1,0:T(8,128)(2,1)S(1)} %collective-permute-done.1), channel_id=1, source_target_pairs={{0,4},{4,8},{8,12},{12,14},{14,10},{10,6},{6,2},{2,0},{1,5},{5,9},... | collective-permute-start | bytes 786440 | tf_op jit(solution)/shard_map/ppermute | solution.py:32
  10.7 12.8 %collective-permute-start.7 = (bf16[256,512]{1,0:T(8,128)(2,1)S(1)}, bf16[256,512]{1,0:T(8,128)(2,1)S(1)}, u32[]{:S(2)}, u32[]{:S(2)}) collective-permute-start(bf16[256,512]{1,0:T(8,128)(2,1)S(1)} %collective-permute-done.2), channel_id=1, source_target_pairs={{0,4},{4,8},{8,12},{12,14},{14,10},{10,6},{6,2},{2,0},{1,5},{5,9},... | collective-permute-start | bytes 786440 | tf_op jit(solution)/shard_map/ppermute | solution.py:32
  11.9 11.8 %collective-permute-start.8 = (bf16[256,512]{1,0:T(8,128)(2,1)S(1)}, bf16[256,512]{1,0:T(8,128)(2,1)S(1)}, u32[]{:S(2)}, u32[]{:S(2)}) collective-permute-start(bf16[256,512]{1,0:T(8,128)(2,1)S(1)} %collective-permute-done.3), channel_id=1, source_target_pairs={{0,2},{4,0},{8,4},{12,8},{14,12},{10,14},{6,10},{2,6},{1,3},{5,1},... | collective-permute-start | bytes 786440 | tf_op jit(solution)/shard_map/ppermute | solution.py:32
  19.0 36.7 %collective-permute-start.17 = (bf16[384,2048]{1,0:T(8,128)(2,1)S(1)}, bf16[384,2048]{1,0:T(8,128)(2,1)S(1)}, u32[]{:S(2)}, u32[]{:S(2)}) collective-permute-start(bf16[384,2048]{1,0:T(8,128)(2,1)S(1)} %shard_map.65), channel_id=1, source_target_pairs={{0,16},{1,17},{2,18},{3,19},{4,20},{5,21},{6,22},{7,23},{8,24},{9,... | collective-permute-start | bytes 4718600 | tf_op jit(solution)/shard_map/ppermute | solution.py:40
  22.1 10.1 %collective-permute-start.10 = (bf16[256,512]{1,0:T(8,128)(2,1)S(1)}, bf16[256,512]{1,0:T(8,128)(2,1)S(1)}, u32[]{:S(2)}, u32[]{:S(2)}) collective-permute-start(bf16[256,512]{1,0:T(8,128)(2,1)S(1)} %collective-permute-done.5), channel_id=1, source_target_pairs={{0,2},{4,0},{8,4},{12,8},{14,12},{10,14},{6,10},{2,6},{1,3},{5,1},... | collective-permute-start | bytes 786440 | tf_op jit(solution)/shard_map/ppermute | solution.py:32
  23.4 15.6 %collective-permute-start.9 = (bf16[256,512]{1,0:T(8,128)(2,1)S(1)}, bf16[256,512]{1,0:T(8,128)(2,1)S(1)}, u32[]{:S(2)}, u32[]{:S(2)}) collective-permute-start(bf16[256,512]{1,0:T(8,128)(2,1)S(1)} %collective-permute-done.4), channel_id=1, source_target_pairs={{0,4},{4,8},{8,12},{12,14},{14,10},{10,6},{6,2},{2,0},{1,5},{5,9},... | collective-permute-start | bytes 786440 | tf_op jit(solution)/shard_map/ppermute | solution.py:32
  23.7 12.7 %collective-permute-start.11 = (bf16[256,512]{1,0:T(8,128)(2,1)S(1)}, bf16[256,512]{1,0:T(8,128)(2,1)S(1)}, u32[]{:S(2)}, u32[]{:S(2)}) collective-permute-start(bf16[256,512]{1,0:T(8,128)(2,1)S(1)} %collective-permute-done.7), channel_id=1, source_target_pairs={{0,4},{4,8},{8,12},{12,14},{14,10},{10,6},{6,2},{2,0},{1,5},{5,9},... | collective-permute-start | bytes 786440 | tf_op jit(solution)/shard_map/ppermute | solution.py:32
  25.0 26.7 %collective-permute-start.12 = (bf16[256,512]{1,0:T(8,128)(2,1)S(1)}, bf16[256,512]{1,0:T(8,128)(2,1)S(1)}, u32[]{:S(2)}, u32[]{:S(2)}) collective-permute-start(bf16[256,512]{1,0:T(8,128)(2,1)S(1)} %collective-permute-done.8), channel_id=1, source_target_pairs={{0,2},{4,0},{8,4},{12,8},{14,12},{10,14},{6,10},{2,6},{1,3},{5,1},... | collective-permute-start | bytes 786440 | tf_op jit(solution)/shard_map/ppermute | solution.py:32
  32.2 8.2 %collective-permute-start.6 = (s32[3,224]{1,0:T(4,128)S(1)}, s32[3,224]{1,0:T(4,128)S(1)}, u32[]{:S(2)}, u32[]{:S(2)}) collective-permute-start(s32[3,224]{1,0:T(4,128)S(1)} %pad_add_fusion.1), channel_id=1, source_target_pairs={{0,1},{1,0},{2,3},{3,2},{4,5},{5,4},{6,7},{7,6},{8,9},{9,8},{10,11... | collective-permute-start | bytes 8072 | tf_op jit(solution)/shard_map/ppermute | solution.py:122
  36.4 6.4 %collective-permute-start.14 = (bf16[256,512]{1,0:T(8,128)(2,1)S(1)}, bf16[256,512]{1,0:T(8,128)(2,1)S(1)}, u32[]{:S(2)}, u32[]{:S(2)}) collective-permute-start(bf16[256,512]{1,0:T(8,128)(2,1)S(1)} %collective-permute-done.10), channel_id=1, source_target_pairs={{0,2},{4,0},{8,4},{12,8},{14,12},{10,14},{6,10},{2,6},{1,3},{5,1},... | collective-permute-start | bytes 786440 | tf_op jit(solution)/shard_map/ppermute | solution.py:32
  39.1 6.2 %collective-permute-start.15 = (bf16[256,512]{1,0:T(8,128)(2,1)S(1)}, bf16[256,512]{1,0:T(8,128)(2,1)S(1)}, u32[]{:S(2)}, u32[]{:S(2)}) collective-permute-start(bf16[256,512]{1,0:T(8,128)(2,1)S(1)} %collective-permute-done.11), channel_id=1, source_target_pairs={{0,4},{4,8},{8,12},{12,14},{14,10},{10,6},{6,2},{2,0},{1,5},{5,9},... | collective-permute-start | bytes 786440 | tf_op jit(solution)/shard_map/ppermute | solution.py:32
  40.4 10.4 %collective-permute-start.13 = (bf16[256,512]{1,0:T(8,128)(2,1)S(1)}, bf16[256,512]{1,0:T(8,128)(2,1)S(1)}, u32[]{:S(2)}, u32[]{:S(2)}) collective-permute-start(bf16[256,512]{1,0:T(8,128)(2,1)S(1)} %collective-permute-done.9), channel_id=1, source_target_pairs={{0,4},{4,8},{8,12},{12,14},{14,10},{10,6},{6,2},{2,0},{1,5},{5,9},... | collective-permute-start | bytes 786440 | tf_op jit(solution)/shard_map/ppermute | solution.py:32
  42.8 8.4 %collective-permute-start.16 = (bf16[256,512]{1,0:T(8,128)(2,1)S(1)}, bf16[256,512]{1,0:T(8,128)(2,1)S(1)}, u32[]{:S(2)}, u32[]{:S(2)}) collective-permute-start(bf16[256,512]{1,0:T(8,128)(2,1)S(1)} %collective-permute-done.14), channel_id=1, source_target_pairs={{0,2},{4,0},{8,4},{12,8},{14,12},{10,14},{6,10},{2,6},{1,3},{5,1},... | collective-permute-start | bytes 786440 | tf_op jit(solution)/shard_map/ppermute | solution.py:32
  55.8 32.5 %collective-permute-start.18 = (bf16[384,2048]{1,0:T(8,128)(2,1)S(1)}, bf16[384,2048]{1,0:T(8,128)(2,1)S(1)}, u32[]{:S(2)}, u32[]{:S(2)}) collective-permute-start(bf16[384,2048]{1,0:T(8,128)(2,1)S(1)} %collective-permute-done.17.own_ref), channel_id=1, source_target_pairs={{0,1},{1,0},{2,3},{3,2},{4,5},{5,4},{6,7},{7,6},{8,9},{9,8},{10,11... | collective-permute-start | bytes 4718600 | tf_op jit(solution)/shard_map/ppermute | solution.py:122
  58.2 12.0 %collective-permute-start.22 = (bf16[6,1024]{1,0:T(8,128)(2,1)S(1)}, bf16[6,1024]{1,0:T(8,128)(2,1)S(1)}, u32[]{:S(2)}, u32[]{:S(2)}) collective-permute-start(bf16[6,1024]{1,0:T(8,128)(2,1)S(1)} %maximum_select_fusion.1), channel_id=1, source_target_pairs={{24,0},{23,1},{28,4},{19,5},{30,8},{17,9},{26,12},{21,13},{22,14},... | collective-permute-start | bytes 36872 | tf_op jit(solution)/shard_map/ppermute | solution.py:134
  59.5 10.7 %collective-permute-start.21 = (bf16[6,1024]{1,0:T(8,128)(2,1)S(1)}, bf16[6,1024]{1,0:T(8,128)(2,1)S(1)}, u32[]{:S(2)}, u32[]{:S(2)}) collective-permute-start(bf16[6,1024]{1,0:T(8,128)(2,1)S(1)} %maximum_select_fusion.1), channel_id=1, source_target_pairs={{20,0},{27,1},{24,4},{23,5},{28,8},{19,9},{30,12},{17,13},{26,14},... | collective-permute-start | bytes 36872 | tf_op jit(solution)/shard_map/ppermute | solution.py:134
  60.8 9.4 %collective-permute-start.20 = (bf16[6,1024]{1,0:T(8,128)(2,1)S(1)}, bf16[6,1024]{1,0:T(8,128)(2,1)S(1)}, u32[]{:S(2)}, u32[]{:S(2)}) collective-permute-start(bf16[6,1024]{1,0:T(8,128)(2,1)S(1)} %maximum_select_fusion.1), channel_id=1, source_target_pairs={{16,0},{31,1},{20,4},{27,5},{24,8},{23,9},{28,12},{19,13},{30,14},... | collective-permute-start | bytes 36872 | tf_op jit(solution)/shard_map/ppermute | solution.py:134
  62.5 25.3 %collective-permute-start.26 = (bf16[768,512]{1,0:T(8,128)(2,1)S(1)}, bf16[768,512]{1,0:T(8,128)(2,1)S(1)}, u32[]{:S(2)}, u32[]{:S(2)}) collective-permute-start(bf16[768,512]{1,0:T(8,128)(2,1)S(1)} %get-tuple-element.123), channel_id=1, source_target_pairs={{0,16},{1,17},{2,18},{3,19},{4,20},{5,21},{6,22},{7,23},{8,24},{9,... | collective-permute-start | bytes 2359304 | tf_op jit(solution)/shard_map/ppermute | solution.py:40
  72.6 15.3 %collective-permute-start.25 = (f32[6,512]{1,0:T(8,128)S(1)}, f32[6,512]{1,0:T(8,128)S(1)}, u32[]{:S(2)}, u32[]{:S(2)}) collective-permute-start(f32[6,512]{1,0:T(8,128)S(1)} %fusion.93), channel_id=1, source_target_pairs={{0,16},{1,17},{2,18},{3,19},{4,20},{5,21},{6,22},{7,23},{8,24},{9,... | collective-permute-start | bytes 36872 | tf_op jit(solution)/shard_map/ppermute | solution.py:40
  90.1 8.0 %collective-permute-start.38 = (bf16[256,256]{1,0:T(8,128)(2,1)S(1)}, bf16[256,256]{1,0:T(8,128)(2,1)S(1)}, u32[]{:S(2)}, u32[]{:S(2)}) collective-permute-start(bf16[256,256]{1,0:T(8,128)(2,1)S(1)} %convolution_convert_fusion.2), channel_id=1, source_target_pairs={{0,2},{4,0},{8,4},{12,8},{14,12},{10,14},{6,10},{2,6},{1,3},{5,1},... | collective-permute-start | bytes 393224 | tf_op jit(solution)/shard_map/ppermute | solution.py:32
  92.1 6.5 %collective-permute-start.35 = (bf16[256,256]{1,0:T(8,128)(2,1)S(1)}, bf16[256,256]{1,0:T(8,128)(2,1)S(1)}, u32[]{:S(2)}, u32[]{:S(2)}) collective-permute-start(bf16[256,256]{1,0:T(8,128)(2,1)S(1)} %convolution_convert_fusion), channel_id=1, source_target_pairs={{0,4},{4,8},{8,12},{12,14},{14,10},{10,6},{6,2},{2,0},{1,5},{5,9},... | collective-permute-start | bytes 393224 | tf_op jit(solution)/shard_map/ppermute | solution.py:32
  92.7 8.0 %collective-permute-start.32 = (bf16[256,256]{1,0:T(8,128)(2,1)S(1)}, bf16[256,256]{1,0:T(8,128)(2,1)S(1)}, u32[]{:S(2)}, u32[]{:S(2)}) collective-permute-start(bf16[256,256]{1,0:T(8,128)(2,1)S(1)} %convolution_convert_fusion.1), channel_id=1, source_target_pairs={{0,2},{4,0},{8,4},{12,8},{14,12},{10,14},{6,10},{2,6},{1,3},{5,1},... | collective-permute-start | bytes 393224 | tf_op jit(solution)/shard_map/ppermute | solution.py:32
  94.5 17.8 %collective-permute-start.28 = (bf16[256,1024]{1,0:T(8,128)(2,1)S(1)}, bf16[256,1024]{1,0:T(8,128)(2,1)S(1)}, u32[]{:S(2)}, u32[]{:S(2)}) collective-permute-start(bf16[256,1024]{1,0:T(8,128)(2,1)S(1)} %convert_element_type.181), channel_id=1, source_target_pairs={{0,16},{1,17},{2,18},{3,19},{4,20},{5,21},{6,22},{7,23},{8,24},{9,... | collective-permute-start | bytes 1572872 | tf_op jit(solution)/shard_map/ppermute | solution.py:40
  101.1 8.0 %collective-permute-start.33 = (bf16[256,256]{1,0:T(8,128)(2,1)S(1)}, bf16[256,256]{1,0:T(8,128)(2,1)S(1)}, u32[]{:S(2)}, u32[]{:S(2)}) collective-permute-start(bf16[256,256]{1,0:T(8,128)(2,1)S(1)} %fusion.6), channel_id=1, source_target_pairs={{0,2},{4,0},{8,4},{12,8},{14,12},{10,14},{6,10},{2,6},{1,3},{5,1},... | collective-permute-start | bytes 393224 | tf_op jit(solution)/shard_map/ppermute | solution.py:32
  103.7 5.9 %collective-permute-start.40 = (bf16[256,256]{1,0:T(8,128)(2,1)S(1)}, bf16[256,256]{1,0:T(8,128)(2,1)S(1)}, u32[]{:S(2)}, u32[]{:S(2)}) collective-permute-start(bf16[256,256]{1,0:T(8,128)(2,1)S(1)} %fusion.10), channel_id=1, source_target_pairs={{0,2},{4,0},{8,4},{12,8},{14,12},{10,14},{6,10},{2,6},{1,3},{5,1},... | collective-permute-start | bytes 393224 | tf_op jit(solution)/shard_map/ppermute | solution.py:32
  104.3 10.3 %collective-permute-start.37 = (bf16[256,256]{1,0:T(8,128)(2,1)S(1)}, bf16[256,256]{1,0:T(8,128)(2,1)S(1)}, u32[]{:S(2)}, u32[]{:S(2)}) collective-permute-start(bf16[256,256]{1,0:T(8,128)(2,1)S(1)} %fusion.7), channel_id=1, source_target_pairs={{0,4},{4,8},{8,12},{12,14},{14,10},{10,6},{6,2},{2,0},{1,5},{5,9},... | collective-permute-start | bytes 393224 | tf_op jit(solution)/shard_map/ppermute | solution.py:32
  118.1 9.9 %collective-permute-start.42 = (bf16[256,512]{1,0:T(8,128)(2,1)S(1)}, bf16[256,512]{1,0:T(8,128)(2,1)S(1)}, u32[]{:S(2)}, u32[]{:S(2)}) collective-permute-start(bf16[256,512]{1,0:T(8,128)(2,1)S(1)} %fusion.16), channel_id=1, source_target_pairs={{1,0},{3,2},{5,4},{7,6},{9,8},{11,10},{13,12},{15,14},{16,1},{18,3... | collective-permute-start | bytes 786440 | tf_op jit(solution)/shard_map/ppermute | solution.py:366
  124.3 7.1 %collective-permute-start.43 = (bf16[256,512]{1,0:T(8,128)(2,1)S(1)}, bf16[256,512]{1,0:T(8,128)(2,1)S(1)}, u32[]{:S(2)}, u32[]{:S(2)}) collective-permute-start(bf16[256,512]{1,0:T(8,128)(2,1)S(1)} %fusion.16), channel_id=1, source_target_pairs={{17,1},{19,3},{21,5},{23,7},{25,9},{27,11},{29,13},{31,15}} | collective-permute-start | bytes 786440 | tf_op jit(solution)/shard_map/ppermute | solution.py:367
  (18 other events, 68.7 us)

commit v16 on v14

--- a/solution.py
+++ b/solution.py
@@ -53,16 +53,19 @@
 
 
 def slab_blocks(stored, chips):
-    order = ring_order(chips)
+    quarter = chips // 4
     kept = []
-    for j in range(chips // cores):
+    for j in range(quarter):
         pairs = []
-        for i, chip in enumerate(order):
+        for chip in range(chips):
             for c in range(cores):
-                source = order[(i + j + c * (chips // cores)) % chips]
+                source = 2 * ((chip // 2 + j + c * quarter) % (chips // 2)) + chip % 2
                 pairs.append(((chips + source) * cores + c, chip * cores + c))
         kept.append(lax.ppermute(stored, ("grp", "chip", "core"), pairs))
-    return kept
+    kept = jnp.concatenate(kept)
+    paired = lax.ppermute(kept, "chip", [(chip, chip ^ 1) for chip in range(chips)])
+    kept = jnp.concatenate([kept, paired])
+    return [kept, from_sibling(kept)]
 
 
 def in_core_order(mine, other, first_core, axis=0):
@@ -123,7 +126,7 @@
     seqs = cores * seq_dev
 
     first_core = core == 0
-    shift = place + core * (chips // cores)
+    shift, parity = chip // 2 + core * (chips // 4), chip % 2
     own_columns, given_columns = core * half, (1 - core) * half
     parts = (core, 1 - core)
     span = chips // 2 if chips <= longest_ring else 0
@@ -132,9 +135,9 @@
         for offset in range(-span, span + 1)
         for i in range(2)
     }
-    scalars = [first_core, shift, own_columns, given_columns, trainer, *starts.values()]
+    scalars = [first_core, shift, parity, own_columns, given_columns, trainer, *starts.values()]
     weights, *scalars = lax.optimization_barrier([master[0], *scalars])
-    first_core, shift, own_columns, given_columns, trainer, *firsts = scalars
+    first_core, shift, parity, own_columns, given_columns, trainer, *firsts = scalars
     starts = dict(zip(starts, firsts))
     own = cut(weights, 1, own_columns, half).astype(jnp.bfloat16)
     given = cut(weights, 1, given_columns, half).astype(jnp.bfloat16)
@@ -142,10 +145,10 @@
 
     other_states = from_sibling(states)
     sent = [(0, 1), (0, -1), (1, 1), (1, -1)]
-    normed_own = normalize(states, gain, 0)
-    normed = normalize(other_states, gain, 1, normed_own)
     if chips <= longest_ring:
         moving = {(i, by): along_ring((own, sibling)[i], by) for i, by in sent}
+        states = after((moving[1, 1], moving[1, -1]), states)
+    normed_own = normalize(states, gain, 0)
 
     def columns(offset, i):
         return cut(normed, 1, starts[offset, i], rows)
@@ -154,22 +157,33 @@
         return jnp.dot(columns(offset, i), block, preferred_element_type=jnp.float32)
 
     if chips <= longest_ring:
-        total = product(0, 0, own) + product(0, 1, sibling)
-        sums = {}
+        total, sums = None, {}
+        waiting = [(0, 0, own), (0, 1, sibling)]
         for step in range(1, chips // 2 + 1):
             last = step == chips // 2
             for i, by in [(0, 1), (1, -1)] if last else sent:
                 if step > 1:
                     if last and step > 2:
-                        moving[i, by] = after(sums[1 + i], moving[i, by])
-                    elif step in (2, 3) and i == 1:
-                        moving[i, by] = after((normed_own, normed)[step - 2], moving[i, by])
+                        tie = normed if i == 0 else sums[2]
+                        moving[i, by] = after(tie, moving[i, by])
+                    elif step == 3 and i == 0:
+                        moving[i, by] = after(normed_own, moving[i, by])
                     moving[i, by] = along_ring(moving[i, by], by)
-                total = total + product(-by * step, i, moving[i, by])
+                waiting.append((-by * step, i, moving[i, by]))
+            if step == 1 and not last:
+                continue
+            if step == min(2, chips // 2):
+                other_states = after((moving[1, 1], moving[1, -1]), other_states)
+                normed = normalize(other_states, gain, 1, normed_own)
+            for offset, i, block in waiting:
+                term = product(offset, i, block)
+                total = term if total is None else total + term
+            waiting = []
             sums[step] = total
             if step == chips // 2 - 1:
-                cand_ids, slab_owner = after(sums[1], (cand_ids, slab_owner))
+                cand_ids, slab_owner = after(sums[2], (cand_ids, slab_owner))
     else:
+        normed = normalize(other_states, gain, 1, normed_own)
         both = in_core_order(own, sibling, first_core)
         gathered = lax.all_gather(both, "chip", axis=0, tiled=True)
         total = jnp.dot(normed, gathered, preferred_element_type=jnp.float32)
@@ -197,15 +211,16 @@
     stored = unit.astype(jnp.bfloat16)
     stored = in_core_order(stored[:seq_dev], stored[seq_dev:], first_core)
 
-    kept = slab_blocks(stored, chips)
-    kept = jnp.concatenate(kept)
-    slab = [kept, from_sibling(kept)]
+    slab = slab_blocks(stored, chips)
     earlier = jnp.arange(slab_rows)[:, None] < jnp.arange(slab_rows)[None, :]
     same = slab_owner[:, None] == slab_owner[None, :]
     ranks = jnp.sum((earlier & same).astype(jnp.int32), axis=0)
-    owner_place = ring_place(slab_owner // cores, chips)
-    seen = lax.rem(owner_place - shift + 2 * chips, chips)
-    slots = seen * seqs + lax.rem(slab_owner, cores) * seq_dev + ranks
+    quarter = chips // 4
+    owner_chip = lax.div(slab_owner, cores)
+    seen = lax.rem(lax.div(owner_chip, 2) - shift + chips, chips // 2)
+    paired = (lax.rem(owner_chip, 2) != parity).astype(jnp.int32)
+    block = lax.div(seen, quarter) * 2 * quarter + paired * quarter + lax.rem(seen, quarter)
+    slots = block * seqs + lax.rem(slab_owner, cores) * seq_dev + ranks
     moved = (slots[:, None] == jnp.arange(slab_rows)[None, :]).astype(jnp.float32)
     candidate = jnp.dot(masks[:, :slab_rows], moved)
     positive = jnp.dot(masks[:, slab_rows:], moved)

time: 119 us -> 121 us (1.017)
  waiting for transfers between devices: 45 us -> 47 us
    ppermute x0 -> x1, waiting for transfers between devices: none -> 3.78 us  [slab_blocks(): lax.ppermute(kept, 'chip', [(chip, chip ^ 1) for chip in range(chips)])]
    ppermute x4 -> x2, starting transfers between devices: 5.16 us -> 2.57 us  [slab_blocks(): kept.append(lax.ppermute(stored, ('grp', 'chip', 'core'), pairs))]
    ppermute x4 -> x2, waiting for transfers between devices: 7.31 us -> 5.16 us  [slab_blocks(): kept.append(lax.ppermute(stored, ('grp', 'chip', 'core'), pairs))]
  transfers between devices with their start and end apart: 39 -> 38, of which waited for: 18 -> 16; matrix products, arithmetic and copies ran while one was open for 16% -> 15% of each run, Pallas kernels for 6% -> 6%
where the time goes in v16:
time: 121 us; the launch traced here: 120 us
  waiting for transfers between devices  47 us (39%)
  starting transfers between devices  38.9 us (32%)
  matrix products  18.6 us (15%)
  Pallas kernels  7.16 us (6%)
  local copies, waits for them, and re-layouts  5.08 us (4%)
  other arithmetic  3.26 us (3%)
    ppermute x28, waiting for transfers between devices, along_ring(): return lax.ppermute(block, 'chip', pairs)  35.1 us
    ppermute x28, starting transfers between devices, along_ring(): return lax.ppermute(block, 'chip', pairs)  32.7 us
    dot_general x16, matrix products, term(): lax.dot_general(columns(offset, i), delta, (((0,), (0,)), ((), ())), pref...  9.31 us
    dot_general x16, matrix products, product(): jnp.dot(columns(offset, i), block, preferred_element_type=jnp.float32)  7.68 us
    pallas_call x2, Pallas kernels, normalize(): pl.pallas_call(functools.partial(normalize_kernel, 16), grid=(seqs,), in_...  7.16 us
    ppermute x2, waiting for transfers between devices, slab_blocks(): kept.append(lax.ppermute(stored, ('grp', 'chip', 'core'), pairs))  5.16 us
    ppermute x1, waiting for transfers between devices, slab_blocks(): lax.ppermute(kept, 'chip', [(chip, chip ^ 1) for chip in range(chips)])  3.78 us
    unnamed x11, local copies, waits for them, and re-layouts  3.31 us
  transfers between devices with their start and end apart: 38, of which 16 were waited for; matrix products, arithmetic and copies ran while one was open for 15% of the time, Pallas kernels for 6%

profile of v16, /device:TPU:0, one launch (start us, length us, event | category | flops | bytes accessed | tf_op | source)
XLA Modules:
  0.0 120.4 jit_solution(6760472212823463446)
XLA Ops:
  0.5 1.5 %dynamic-slice_convert_fusion = (bf16[256,512]{1,0:T(8,128)(2,1)S(1)}, bf16[256,512]{1,0:T(8,128)(2,1)S(1)}) fusion(f32[256,1024]{1,0:T(8,128)} %bitcast.58, s32[]{:T(128)S(6)} %mul.287, s32[]{:T(128)S(6)} %mul.288), kind=kLoop, calls=%fused_computation.32 | loop fusion | bytes 1048584 | tf_op jit(solution)/shard_map/convert_element_type | solution.py:142
  2.1 3.0 %collective-permute-start.6 = (bf16[256,512]{1,0:T(8,128)(2,1)S(1)}, bf16[256,512]{1,0:T(8,128)(2,1)S(1)}, u32[]{:S(2)}, u32[]{:S(2)}) collective-permute-start(bf16[256,512]{1,0:T(8,128)(2,1)S(1)} %get-tuple-element.95), channel_id=1, source_target_pairs={{0,4},{4,8},{8,12},{12,14},{14,10},{10,6},{6,2},{2,0},{1,5},{5,9},... | collective-permute-start | bytes 786440 | tf_op jit(solution)/shard_map/ppermute | solution.py:32
  6.1 2.9 %collective-permute-start.3 = (bf16[256,512]{1,0:T(8,128)(2,1)S(1)}, bf16[256,512]{1,0:T(8,128)(2,1)S(1)}, u32[]{:S(2)}, u32[]{:S(2)}) collective-permute-start(bf16[256,512]{1,0:T(8,128)(2,1)S(1)} %collective-permute-done), channel_id=1, source_target_pairs={{0,2},{4,0},{8,4},{12,8},{14,12},{10,14},{6,10},{2,6},{1,3},{5,1},... | collective-permute-start | bytes 786440 | tf_op jit(solution)/shard_map/ppermute | solution.py:32
  9.1 2.7 %collective-permute-done.6 = bf16[256,512]{1,0:T(8,128)(2,1)S(1)} collective-permute-done((bf16[256,512]{1,0:T(8,128)(2,1)S(1)}, bf16[256,512]{1,0:T(8,128)(2,1)S(1)}, u32[]{:S(2)}, u32[]{:S(2)}) %collective-permute-start.6) | collective-permute-done | bytes 262176 | tf_op jit(solution)/shard_map/ppermute | solution.py:32
  11.8 2.5 %collective-permute-start.8 = (bf16[256,512]{1,0:T(8,128)(2,1)S(1)}, bf16[256,512]{1,0:T(8,128)(2,1)S(1)}, u32[]{:S(2)}, u32[]{:S(2)}) collective-permute-start(bf16[256,512]{1,0:T(8,128)(2,1)S(1)} %collective-permute-done.6), channel_id=1, source_target_pairs={{0,4},{4,8},{8,12},{12,14},{14,10},{10,6},{6,2},{2,0},{1,5},{5,9},... | collective-permute-start | bytes 786440 | tf_op jit(solution)/shard_map/ppermute | solution.py:32
  14.3 5.6 %collective-permute-done.3 = bf16[256,512]{1,0:T(8,128)(2,1)S(1)} collective-permute-done((bf16[256,512]{1,0:T(8,128)(2,1)S(1)}, bf16[256,512]{1,0:T(8,128)(2,1)S(1)}, u32[]{:S(2)}, u32[]{:S(2)}) %collective-permute-start.3) | collective-permute-done | bytes 262176 | tf_op jit(solution)/shard_map/ppermute | solution.py:32
  19.9 2.0 %collective-permute-start.2 = (bf16[256,512]{1,0:T(8,128)(2,1)S(1)}, bf16[256,512]{1,0:T(8,128)(2,1)S(1)}, u32[]{:S(2)}, u32[]{:S(2)}) collective-permute-start(bf16[256,512]{1,0:T(8,128)(2,1)S(1)} %collective-permute-done.1), channel_id=1, source_target_pairs={{0,4},{4,8},{8,12},{12,14},{14,10},{10,6},{6,2},{2,0},{1,5},{5,9},... | collective-permute-start | bytes 786440 | tf_op jit(solution)/shard_map/ppermute | solution.py:32
  22.6 1.9 %copy-done = bf16[1,3,128,4096]{3,2,1,0:T(8,128)(2,1)S(1)} copy-done((bf16[1,3,128,4096]{3,2,1,0:T(8,128)(2,1)S(1)}, bf16[1,3,128,4096]{3,2,1,0:T(8,128)(2,1)}, u32[]{:S(2)}) %copy-start) | copy-done | bytes 3145752
  25.2 3.6 %shard_map.64.refs_0_ = bf16[768,4096]{1,0:T(8,128)(2,1)S(1)} custom-call(bf16[3,128,4096]{2,1,0:T(8,128)(2,1)S(1)} %bitcast.54, f32[1,4096]{1,0:T(1,128)S(1)} %bitcast.55), custom_call_target="tpu_custom_call" | custom-call | flops 9437184 | bytes 6291456 | tf_op jit(solution)/shard_map/pallas_call | solution.py:102
  28.8 1.6 %collective-permute-start.11 = (bf16[256,512]{1,0:T(8,128)(2,1)S(1)}, bf16[256,512]{1,0:T(8,128)(2,1)S(1)}, u32[]{:S(2)}, u32[]{:S(2)}) collective-permute-start(bf16[256,512]{1,0:T(8,128)(2,1)S(1)} %collective-permute-done.8), channel_id=1, source_target_pairs={{0,4},{4,8},{8,12},{12,14},{14,10},{10,6},{6,2},{2,0},{1,5},{5,9},... | collective-permute-start | bytes 786440 | tf_op jit(solution)/shard_map/ppermute | solution.py:32
  30.9 2.0 %collective-permute-start.13 = (bf16[256,512]{1,0:T(8,128)(2,1)S(1)}, bf16[256,512]{1,0:T(8,128)(2,1)S(1)}, u32[]{:S(2)}, u32[]{:S(2)}) collective-permute-start(bf16[256,512]{1,0:T(8,128)(2,1)S(1)} %collective-permute-done.2), channel_id=1, source_target_pairs={{0,4},{4,8},{8,12},{12,14},{14,10},{10,6},{6,2},{2,0},{1,5},{5,9},... | collective-permute-start | bytes 786440 | tf_op jit(solution)/shard_map/ppermute | solution.py:32
  32.9 3.6 %shard_map.65 = bf16[768,4096]{1,0:T(8,128)(2,1)S(1)} custom-call(bf16[3,128,4096]{2,1,0:T(8,128)(2,1)S(1)} %collective-permute-done.5.states_ref, f32[1,4096]{1,0:T(1,128)S(1)} %bitcast.56, bf16[768,4096]{1,0:T(8,128)(2,1)S(1)} %shard_map.64.refs_0_), custom_call_target="tpu_custom_call", output_to_operand_aliasing={{}: (2, {})} | custom-call | flops 9437184 | bytes 6291456 | tf_op jit(solution)/shard_map/pallas_call | solution.py:102
  41.8 1.6 %collective-permute-start.15 = (bf16[256,512]{1,0:T(8,128)(2,1)S(1)}, bf16[256,512]{1,0:T(8,128)(2,1)S(1)}, u32[]{:S(2)}, u32[]{:S(2)}) collective-permute-start(bf16[256,512]{1,0:T(8,128)(2,1)S(1)} %collective-permute-done.11), channel_id=1, source_target_pairs={{0,4},{4,8},{8,12},{12,14},{14,10},{10,6},{6,2},{2,0},{1,5},{5,9},... | collective-permute-start | bytes 786440 | tf_op jit(solution)/shard_map/ppermute | solution.py:32
  45.7 4.8 %collective-permute-done.15 = bf16[256,512]{1,0:T(8,128)(2,1)S(1)} collective-permute-done((bf16[256,512]{1,0:T(8,128)(2,1)S(1)}, bf16[256,512]{1,0:T(8,128)(2,1)S(1)}, u32[]{:S(2)}, u32[]{:S(2)}) %collective-permute-start.15) | collective-permute-done | bytes 262176 | tf_op jit(solution)/shard_map/ppermute | solution.py:32
  55.1 1.3 %collective-permute-start.18 = (bf16[6,1024]{1,0:T(8,128)(2,1)S(1)}, bf16[6,1024]{1,0:T(8,128)(2,1)S(1)}, u32[]{:S(2)}, u32[]{:S(2)}) collective-permute-start(bf16[6,1024]{1,0:T(8,128)(2,1)S(1)} %maximum_select_fusion.2), channel_id=1, source_target_pairs={{16,0},{25,1},{18,2},{27,3},{20,4},{29,5},{22,6},{31,7},{24,8},{17... | collective-permute-start | bytes 36872 | tf_op jit(solution)/shard_map/ppermute | solution.py:64
  56.4 1.3 %collective-permute-start.19 = (bf16[6,1024]{1,0:T(8,128)(2,1)S(1)}, bf16[6,1024]{1,0:T(8,128)(2,1)S(1)}, u32[]{:S(2)}, u32[]{:S(2)}) collective-permute-start(bf16[6,1024]{1,0:T(8,128)(2,1)S(1)} %maximum_select_fusion.2), channel_id=1, source_target_pairs={{20,0},{29,1},{22,2},{31,3},{24,4},{17,5},{26,6},{19,7},{28,8},{21... | collective-permute-start | bytes 36872 | tf_op jit(solution)/shard_map/ppermute | solution.py:64
  57.9 2.8 %collective-permute-done.18 = bf16[6,1024]{1,0:T(8,128)(2,1)S(1)} collective-permute-done((bf16[6,1024]{1,0:T(8,128)(2,1)S(1)}, bf16[6,1024]{1,0:T(8,128)(2,1)S(1)}, u32[]{:S(2)}, u32[]{:S(2)}) %collective-permute-start.18) | collective-permute-done | bytes 12320 | tf_op jit(solution)/shard_map/ppermute | solution.py:64
  60.7 2.3 %collective-permute-done.19 = bf16[6,1024]{1,0:T(8,128)(2,1)S(1)} collective-permute-done((bf16[6,1024]{1,0:T(8,128)(2,1)S(1)}, bf16[6,1024]{1,0:T(8,128)(2,1)S(1)}, u32[]{:S(2)}, u32[]{:S(2)}) %collective-permute-start.19) | collective-permute-done | bytes 12320 | tf_op jit(solution)/shard_map/ppermute | solution.py:64
  63.4 3.8 %collective-permute-done.20 = bf16[12,1024]{1,0:T(8,128)(2,1)S(1)} collective-permute-done((bf16[12,1024]{1,0:T(8,128)(2,1)S(1)}, bf16[12,1024]{1,0:T(8,128)(2,1)S(1)}, u32[]{:S(2)}, u32[]{:S(2)}) %collective-permute-start.20) | collective-permute-done | bytes 24608 | tf_op jit(solution)/shard_map/ppermute | solution.py:66
  71.0 1.7 %collective-permute-start.30 = (bf16[256,512]{1,0:T(8,128)(2,1)S(1)}, bf16[256,512]{1,0:T(8,128)(2,1)S(1)}, u32[]{:S(2)}, u32[]{:S(2)}) collective-permute-start(bf16[256,512]{1,0:T(8,128)(2,1)S(1)} %convolution_convert_fusion.1), channel_id=1, source_target_pairs={{0,4},{4,8},{8,12},{12,14},{14,10},{10,6},{6,2},{2,0},{1,5},{5,9},... | collective-permute-start | bytes 786440 | tf_op jit(solution)/shard_map/ppermute | solution.py:32
  73.3 1.3 %collective-permute-start.22 = (bf16[256,512]{1,0:T(8,128)(2,1)S(1)}, bf16[256,512]{1,0:T(8,128)(2,1)S(1)}, u32[]{:S(2)}, u32[]{:S(2)}) collective-permute-start(bf16[256,512]{1,0:T(8,128)(2,1)S(1)} %convolution_convert_fusion.3), channel_id=1, source_target_pairs={{0,4},{4,8},{8,12},{12,14},{14,10},{10,6},{6,2},{2,0},{1,5},{5,9},... | collective-permute-start | bytes 786440 | tf_op jit(solution)/shard_map/ppermute | solution.py:32
  76.4 3.8 %collective-permute-done.30 = bf16[256,512]{1,0:T(8,128)(2,1)S(1)} collective-permute-done((bf16[256,512]{1,0:T(8,128)(2,1)S(1)}, bf16[256,512]{1,0:T(8,128)(2,1)S(1)}, u32[]{:S(2)}, u32[]{:S(2)}) %collective-permute-start.30) | collective-permute-done | bytes 262176 | tf_op jit(solution)/shard_map/ppermute | solution.py:32
  80.8 1.7 %collective-permute-start.31 = (bf16[256,512]{1,0:T(8,128)(2,1)S(1)}, bf16[256,512]{1,0:T(8,128)(2,1)S(1)}, u32[]{:S(2)}, u32[]{:S(2)}) collective-permute-start(bf16[256,512]{1,0:T(8,128)(2,1)S(1)} %add_convert_fusion.4), channel_id=1, source_target_pairs={{0,4},{4,8},{8,12},{12,14},{14,10},{10,6},{6,2},{2,0},{1,5},{5,9},... | collective-permute-start | bytes 786440 | tf_op jit(solution)/shard_map/ppermute | solution.py:32
  82.5 3.3 %collective-permute-done.22 = bf16[256,512]{1,0:T(8,128)(2,1)S(1)} collective-permute-done((bf16[256,512]{1,0:T(8,128)(2,1)S(1)}, bf16[256,512]{1,0:T(8,128)(2,1)S(1)}, u32[]{:S(2)}, u32[]{:S(2)}) %collective-permute-start.22) | collective-permute-done | bytes 262176 | tf_op jit(solution)/shard_map/ppermute | solution.py:32
  88.6 1.8 %collective-permute-start.24 = (bf16[256,512]{1,0:T(8,128)(2,1)S(1)}, bf16[256,512]{1,0:T(8,128)(2,1)S(1)}, u32[]{:S(2)}, u32[]{:S(2)}) collective-permute-start(bf16[256,512]{1,0:T(8,128)(2,1)S(1)} %add_convert_fusion.7), channel_id=1, source_target_pairs={{0,4},{4,8},{8,12},{12,14},{14,10},{10,6},{6,2},{2,0},{1,5},{5,9},... | collective-permute-start | bytes 786440 | tf_op jit(solution)/shard_map/ppermute | solution.py:32
  90.4 2.5 %collective-permute-start.23 = (bf16[256,1024]{1,0:T(8,128)(2,1)S(1)}, bf16[256,1024]{1,0:T(8,128)(2,1)S(1)}, u32[]{:S(2)}, u32[]{:S(2)}) collective-permute-start(bf16[256,1024]{1,0:T(8,128)(2,1)S(1)} %convert_element_type.164), channel_id=1, source_target_pairs={{0,16},{1,17},{2,18},{3,19},{4,20},{5,21},{6,22},{7,23},{8,24},{9,... | collective-permute-start | bytes 1572872 | tf_op jit(solution)/shard_map/ppermute | solution.py:40
  94.0 1.8 %collective-permute-done.34 = bf16[256,512]{1,0:T(8,128)(2,1)S(1)} collective-permute-done((bf16[256,512]{1,0:T(8,128)(2,1)S(1)}, bf16[256,512]{1,0:T(8,128)(2,1)S(1)}, u32[]{:S(2)}, u32[]{:S(2)}) %collective-permute-start.34) | collective-permute-done | bytes 262176 | tf_op jit(solution)/shard_map/ppermute | solution.py:32
  97.1 2.6 %collective-permute-start.32 = (bf16[256,512]{1,0:T(8,128)(2,1)S(1)}, bf16[256,512]{1,0:T(8,128)(2,1)S(1)}, u32[]{:S(2)}, u32[]{:S(2)}) collective-permute-start(bf16[256,512]{1,0:T(8,128)(2,1)S(1)} %add_convert_fusion.3), channel_id=1, source_target_pairs={{0,4},{4,8},{8,12},{12,14},{14,10},{10,6},{6,2},{2,0},{1,5},{5,9},... | collective-permute-start | bytes 786440 | tf_op jit(solution)/shard_map/ppermute | solution.py:32
  100.3 2.0 %collective-permute-start.25 = (bf16[256,512]{1,0:T(8,128)(2,1)S(1)}, bf16[256,512]{1,0:T(8,128)(2,1)S(1)}, u32[]{:S(2)}, u32[]{:S(2)}) collective-permute-start(bf16[256,512]{1,0:T(8,128)(2,1)S(1)} %add_convert_fusion.6), channel_id=1, source_target_pairs={{0,4},{4,8},{8,12},{12,14},{14,10},{10,6},{6,2},{2,0},{1,5},{5,9},... | collective-permute-start | bytes 786440 | tf_op jit(solution)/shard_map/ppermute | solution.py:32
  102.4 3.8 %collective-permute-done.35 = bf16[256,512]{1,0:T(8,128)(2,1)S(1)} collective-permute-done((bf16[256,512]{1,0:T(8,128)(2,1)S(1)}, bf16[256,512]{1,0:T(8,128)(2,1)S(1)}, u32[]{:S(2)}, u32[]{:S(2)}) %collective-permute-start.35) | collective-permute-done | bytes 262176 | tf_op jit(solution)/shard_map/ppermute | solution.py:32
  110.6 5.5 %collective-permute-done.36 = bf16[256,512]{1,0:T(8,128)(2,1)S(1)} collective-permute-done((bf16[256,512]{1,0:T(8,128)(2,1)S(1)}, bf16[256,512]{1,0:T(8,128)(2,1)S(1)}, u32[]{:S(2)}, u32[]{:S(2)}) %collective-permute-start.36) | collective-permute-done | bytes 262176 | tf_op jit(solution)/shard_map/ppermute | solution.py:32
  116.2 2.7 %collective-permute-done.29 = bf16[256,512]{1,0:T(8,128)(2,1)S(1)} collective-permute-done((bf16[256,512]{1,0:T(8,128)(2,1)S(1)}, bf16[256,512]{1,0:T(8,128)(2,1)S(1)}, u32[]{:S(2)}, u32[]{:S(2)}) %collective-permute-start.29) | collective-permute-done | bytes 262176 | tf_op jit(solution)/shard_map/ppermute | solution.py:32
  (127 shorter events, 34.6 us)
Async XLA Ops:
  0.0 32.9 %collective-permute-start.5 = (bf16[3,128,4096]{2,1,0:T(8,128)(2,1)}, bf16[3,128,4096]{2,1,0:T(8,128)(2,1)S(1)}, u32[]{:S(2)}, u32[]{:S(2)}) collective-permute-start(bf16[3,128,4096]{2,1,0:T(8,128)(2,1)} %bitcast.53), channel_id=1, source_target_pairs={{0,1},{1,0},{2,3},{3,2},{4,5},{5,4},{6,7},{7,6},{8,9},{9,8},{10,11... | collective-permute-start | bytes 9437192 | tf_op jit(solution)/shard_map/ppermute | solution.py:52
  2.1 9.7 %collective-permute-start.6 = (bf16[256,512]{1,0:T(8,128)(2,1)S(1)}, bf16[256,512]{1,0:T(8,128)(2,1)S(1)}, u32[]{:S(2)}, u32[]{:S(2)}) collective-permute-start(bf16[256,512]{1,0:T(8,128)(2,1)S(1)} %get-tuple-element.95), channel_id=1, source_target_pairs={{0,4},{4,8},{8,12},{12,14},{14,10},{10,6},{6,2},{2,0},{1,5},{5,9},... | collective-permute-start | bytes 786440 | tf_op jit(solution)/shard_map/ppermute | solution.py:32
  5.1 9.2 %collective-permute-start.7 = (bf16[256,512]{1,0:T(8,128)(2,1)S(1)}, bf16[256,512]{1,0:T(8,128)(2,1)S(1)}, u32[]{:S(2)}, u32[]{:S(2)}) collective-permute-start(bf16[256,512]{1,0:T(8,128)(2,1)S(1)} %get-tuple-element.95), channel_id=1, source_target_pairs={{0,2},{4,0},{8,4},{12,8},{14,12},{10,14},{6,10},{2,6},{1,3},{5,1},... | collective-permute-start | bytes 786440 | tf_op jit(solution)/shard_map/ppermute | solution.py:32
  6.1 13.8 %collective-permute-start.3 = (bf16[256,512]{1,0:T(8,128)(2,1)S(1)}, bf16[256,512]{1,0:T(8,128)(2,1)S(1)}, u32[]{:S(2)}, u32[]{:S(2)}) collective-permute-start(bf16[256,512]{1,0:T(8,128)(2,1)S(1)} %collective-permute-done), channel_id=1, source_target_pairs={{0,2},{4,0},{8,4},{12,8},{14,12},{10,14},{6,10},{2,6},{1,3},{5,1},... | collective-permute-start | bytes 786440 | tf_op jit(solution)/shard_map/ppermute | solution.py:32
  9.0 10.9 %collective-permute-start.1 = (bf16[256,512]{1,0:T(8,128)(2,1)S(1)}, bf16[256,512]{1,0:T(8,128)(2,1)S(1)}, u32[]{:S(2)}, u32[]{:S(2)}) collective-permute-start(bf16[256,512]{1,0:T(8,128)(2,1)S(1)} %collective-permute-done), channel_id=1, source_target_pairs={{0,4},{4,8},{8,12},{12,14},{14,10},{10,6},{6,2},{2,0},{1,5},{5,9},... | collective-permute-start | bytes 786440 | tf_op jit(solution)/shard_map/ppermute | solution.py:32
  11.8 17.0 %collective-permute-start.8 = (bf16[256,512]{1,0:T(8,128)(2,1)S(1)}, bf16[256,512]{1,0:T(8,128)(2,1)S(1)}, u32[]{:S(2)}, u32[]{:S(2)}) collective-permute-start(bf16[256,512]{1,0:T(8,128)(2,1)S(1)} %collective-permute-done.6), channel_id=1, source_target_pairs={{0,4},{4,8},{8,12},{12,14},{14,10},{10,6},{6,2},{2,0},{1,5},{5,9},... | collective-permute-start | bytes 786440 | tf_op jit(solution)/shard_map/ppermute | solution.py:32
  14.3 14.5 %collective-permute-start.9 = (bf16[256,512]{1,0:T(8,128)(2,1)S(1)}, bf16[256,512]{1,0:T(8,128)(2,1)S(1)}, u32[]{:S(2)}, u32[]{:S(2)}) collective-permute-start(bf16[256,512]{1,0:T(8,128)(2,1)S(1)} %collective-permute-done.7), channel_id=1, source_target_pairs={{0,2},{4,0},{8,4},{12,8},{14,12},{10,14},{6,10},{2,6},{1,3},{5,1},... | collective-permute-start | bytes 786440 | tf_op jit(solution)/shard_map/ppermute | solution.py:32
  19.9 11.0 %collective-permute-start.4 = (bf16[256,512]{1,0:T(8,128)(2,1)S(1)}, bf16[256,512]{1,0:T(8,128)(2,1)S(1)}, u32[]{:S(2)}, u32[]{:S(2)}) collective-permute-start(bf16[256,512]{1,0:T(8,128)(2,1)S(1)} %collective-permute-done.3), channel_id=1, source_target_pairs={{0,2},{4,0},{8,4},{12,8},{14,12},{10,14},{6,10},{2,6},{1,3},{5,1},... | collective-permute-start | bytes 786440 | tf_op jit(solution)/shard_map/ppermute | solution.py:32
  19.9 11.0 %collective-permute-start.2 = (bf16[256,512]{1,0:T(8,128)(2,1)S(1)}, bf16[256,512]{1,0:T(8,128)(2,1)S(1)}, u32[]{:S(2)}, u32[]{:S(2)}) collective-permute-start(bf16[256,512]{1,0:T(8,128)(2,1)S(1)} %collective-permute-done.1), channel_id=1, source_target_pairs={{0,4},{4,8},{8,12},{12,14},{14,10},{10,6},{6,2},{2,0},{1,5},{5,9},... | collective-permute-start | bytes 786440 | tf_op jit(solution)/shard_map/ppermute | solution.py:32
  28.8 13.0 %collective-permute-start.11 = (bf16[256,512]{1,0:T(8,128)(2,1)S(1)}, bf16[256,512]{1,0:T(8,128)(2,1)S(1)}, u32[]{:S(2)}, u32[]{:S(2)}) collective-permute-start(bf16[256,512]{1,0:T(8,128)(2,1)S(1)} %collective-permute-done.8), channel_id=1, source_target_pairs={{0,4},{4,8},{8,12},{12,14},{14,10},{10,6},{6,2},{2,0},{1,5},{5,9},... | collective-permute-start | bytes 786440 | tf_op jit(solution)/shard_map/ppermute | solution.py:32
  30.5 14.0 %collective-permute-start.12 = (bf16[256,512]{1,0:T(8,128)(2,1)S(1)}, bf16[256,512]{1,0:T(8,128)(2,1)S(1)}, u32[]{:S(2)}, u32[]{:S(2)}) collective-permute-start(bf16[256,512]{1,0:T(8,128)(2,1)S(1)} %collective-permute-done.9), channel_id=1, source_target_pairs={{0,2},{4,0},{8,4},{12,8},{14,12},{10,14},{6,10},{2,6},{1,3},{5,1},... | collective-permute-start | bytes 786440 | tf_op jit(solution)/shard_map/ppermute | solution.py:32
  30.9 12.7 %collective-permute-start.14 = (bf16[256,512]{1,0:T(8,128)(2,1)S(1)}, bf16[256,512]{1,0:T(8,128)(2,1)S(1)}, u32[]{:S(2)}, u32[]{:S(2)}) collective-permute-start(bf16[256,512]{1,0:T(8,128)(2,1)S(1)} %collective-permute-done.4), channel_id=1, source_target_pairs={{0,2},{4,0},{8,4},{12,8},{14,12},{10,14},{6,10},{2,6},{1,3},{5,1},... | collective-permute-start | bytes 786440 | tf_op jit(solution)/shard_map/ppermute | solution.py:32
  30.9 14.0 %collective-permute-start.13 = (bf16[256,512]{1,0:T(8,128)(2,1)S(1)}, bf16[256,512]{1,0:T(8,128)(2,1)S(1)}, u32[]{:S(2)}, u32[]{:S(2)}) collective-permute-start(bf16[256,512]{1,0:T(8,128)(2,1)S(1)} %collective-permute-done.2), channel_id=1, source_target_pairs={{0,4},{4,8},{8,12},{12,14},{14,10},{10,6},{6,2},{2,0},{1,5},{5,9},... | collective-permute-start | bytes 786440 | tf_op jit(solution)/shard_map/ppermute | solution.py:32
  41.8 8.7 %collective-permute-start.15 = (bf16[256,512]{1,0:T(8,128)(2,1)S(1)}, bf16[256,512]{1,0:T(8,128)(2,1)S(1)}, u32[]{:S(2)}, u32[]{:S(2)}) collective-permute-start(bf16[256,512]{1,0:T(8,128)(2,1)S(1)} %collective-permute-done.11), channel_id=1, source_target_pairs={{0,4},{4,8},{8,12},{12,14},{14,10},{10,6},{6,2},{2,0},{1,5},{5,9},... | collective-permute-start | bytes 786440 | tf_op jit(solution)/shard_map/ppermute | solution.py:32
  43.6 8.4 %collective-permute-start.16 = (bf16[256,512]{1,0:T(8,128)(2,1)S(1)}, bf16[256,512]{1,0:T(8,128)(2,1)S(1)}, u32[]{:S(2)}, u32[]{:S(2)}) collective-permute-start(bf16[256,512]{1,0:T(8,128)(2,1)S(1)} %collective-permute-done.14), channel_id=1, source_target_pairs={{0,2},{4,0},{8,4},{12,8},{14,12},{10,14},{6,10},{2,6},{1,3},{5,1},... | collective-permute-start | bytes 786440 | tf_op jit(solution)/shard_map/ppermute | solution.py:32
  55.1 5.6 %collective-permute-start.18 = (bf16[6,1024]{1,0:T(8,128)(2,1)S(1)}, bf16[6,1024]{1,0:T(8,128)(2,1)S(1)}, u32[]{:S(2)}, u32[]{:S(2)}) collective-permute-start(bf16[6,1024]{1,0:T(8,128)(2,1)S(1)} %maximum_select_fusion.2), channel_id=1, source_target_pairs={{16,0},{25,1},{18,2},{27,3},{20,4},{29,5},{22,6},{31,7},{24,8},{17... | collective-permute-start | bytes 36872 | tf_op jit(solution)/shard_map/ppermute | solution.py:64
  56.4 6.7 %collective-permute-start.19 = (bf16[6,1024]{1,0:T(8,128)(2,1)S(1)}, bf16[6,1024]{1,0:T(8,128)(2,1)S(1)}, u32[]{:S(2)}, u32[]{:S(2)}) collective-permute-start(bf16[6,1024]{1,0:T(8,128)(2,1)S(1)} %maximum_select_fusion.2), channel_id=1, source_target_pairs={{20,0},{29,1},{22,2},{31,3},{24,4},{17,5},{26,6},{19,7},{28,8},{21... | collective-permute-start | bytes 36872 | tf_op jit(solution)/shard_map/ppermute | solution.py:64
  71.0 9.2 %collective-permute-start.30 = (bf16[256,512]{1,0:T(8,128)(2,1)S(1)}, bf16[256,512]{1,0:T(8,128)(2,1)S(1)}, u32[]{:S(2)}, u32[]{:S(2)}) collective-permute-start(bf16[256,512]{1,0:T(8,128)(2,1)S(1)} %convolution_convert_fusion.1), channel_id=1, source_target_pairs={{0,4},{4,8},{8,12},{12,14},{14,10},{10,6},{6,2},{2,0},{1,5},{5,9},... | collective-permute-start | bytes 786440 | tf_op jit(solution)/shard_map/ppermute | solution.py:32
  73.3 12.5 %collective-permute-start.22 = (bf16[256,512]{1,0:T(8,128)(2,1)S(1)}, bf16[256,512]{1,0:T(8,128)(2,1)S(1)}, u32[]{:S(2)}, u32[]{:S(2)}) collective-permute-start(bf16[256,512]{1,0:T(8,128)(2,1)S(1)} %convolution_convert_fusion.3), channel_id=1, source_target_pairs={{0,4},{4,8},{8,12},{12,14},{14,10},{10,6},{6,2},{2,0},{1,5},{5,9},... | collective-permute-start | bytes 786440 | tf_op jit(solution)/shard_map/ppermute | solution.py:32
  75.1 11.9 %collective-permute-start.33 = (bf16[256,512]{1,0:T(8,128)(2,1)S(1)}, bf16[256,512]{1,0:T(8,128)(2,1)S(1)}, u32[]{:S(2)}, u32[]{:S(2)}) collective-permute-start(bf16[256,512]{1,0:T(8,128)(2,1)S(1)} %convolution_convert_fusion), channel_id=1, source_target_pairs={{0,2},{4,0},{8,4},{12,8},{14,12},{10,14},{6,10},{2,6},{1,3},{5,1},... | collective-permute-start | bytes 786440 | tf_op jit(solution)/shard_map/ppermute | solution.py:32
  76.0 16.9 %collective-permute-start.27 = (bf16[256,512]{1,0:T(8,128)(2,1)S(1)}, bf16[256,512]{1,0:T(8,128)(2,1)S(1)}, u32[]{:S(2)}, u32[]{:S(2)}) collective-permute-start(bf16[256,512]{1,0:T(8,128)(2,1)S(1)} %convolution_convert_fusion.2), channel_id=1, source_target_pairs={{0,2},{4,0},{8,4},{12,8},{14,12},{10,14},{6,10},{2,6},{1,3},{5,1},... | collective-permute-start | bytes 786440 | tf_op jit(solution)/shard_map/ppermute | solution.py:32
  80.8 15.7 %collective-permute-start.31 = (bf16[256,512]{1,0:T(8,128)(2,1)S(1)}, bf16[256,512]{1,0:T(8,128)(2,1)S(1)}, u32[]{:S(2)}, u32[]{:S(2)}) collective-permute-start(bf16[256,512]{1,0:T(8,128)(2,1)S(1)} %add_convert_fusion.4), channel_id=1, source_target_pairs={{0,4},{4,8},{8,12},{12,14},{14,10},{10,6},{6,2},{2,0},{1,5},{5,9},... | collective-permute-start | bytes 786440 | tf_op jit(solution)/shard_map/ppermute | solution.py:32
  87.6 8.2 %collective-permute-start.34 = (bf16[256,512]{1,0:T(8,128)(2,1)S(1)}, bf16[256,512]{1,0:T(8,128)(2,1)S(1)}, u32[]{:S(2)}, u32[]{:S(2)}) collective-permute-start(bf16[256,512]{1,0:T(8,128)(2,1)S(1)} %add_convert_fusion.2), channel_id=1, source_target_pairs={{0,2},{4,0},{8,4},{12,8},{14,12},{10,14},{6,10},{2,6},{1,3},{5,1},... | collective-permute-start | bytes 786440 | tf_op jit(solution)/shard_map/ppermute | solution.py:32
  88.6 11.2 %collective-permute-start.24 = (bf16[256,512]{1,0:T(8,128)(2,1)S(1)}, bf16[256,512]{1,0:T(8,128)(2,1)S(1)}, u32[]{:S(2)}, u32[]{:S(2)}) collective-permute-start(bf16[256,512]{1,0:T(8,128)(2,1)S(1)} %add_convert_fusion.7), channel_id=1, source_target_pairs={{0,4},{4,8},{8,12},{12,14},{14,10},{10,6},{6,2},{2,0},{1,5},{5,9},... | collective-permute-start | bytes 786440 | tf_op jit(solution)/shard_map/ppermute | solution.py:32
  90.4 17.1 %collective-permute-start.23 = (bf16[256,1024]{1,0:T(8,128)(2,1)S(1)}, bf16[256,1024]{1,0:T(8,128)(2,1)S(1)}, u32[]{:S(2)}, u32[]{:S(2)}) collective-permute-start(bf16[256,1024]{1,0:T(8,128)(2,1)S(1)} %convert_element_type.164), channel_id=1, source_target_pairs={{0,16},{1,17},{2,18},{3,19},{4,20},{5,21},{6,22},{7,23},{8,24},{9,... | collective-permute-start | bytes 1572872 | tf_op jit(solution)/shard_map/ppermute | solution.py:40
  93.5 13.4 %collective-permute-start.28 = (bf16[256,512]{1,0:T(8,128)(2,1)S(1)}, bf16[256,512]{1,0:T(8,128)(2,1)S(1)}, u32[]{:S(2)}, u32[]{:S(2)}) collective-permute-start(bf16[256,512]{1,0:T(8,128)(2,1)S(1)} %add_convert_fusion.5), channel_id=1, source_target_pairs={{0,2},{4,0},{8,4},{12,8},{14,12},{10,14},{6,10},{2,6},{1,3},{5,1},... | collective-permute-start | bytes 786440 | tf_op jit(solution)/shard_map/ppermute | solution.py:32
  96.4 9.7 %collective-permute-start.35 = (bf16[256,512]{1,0:T(8,128)(2,1)S(1)}, bf16[256,512]{1,0:T(8,128)(2,1)S(1)}, u32[]{:S(2)}, u32[]{:S(2)}) collective-permute-start(bf16[256,512]{1,0:T(8,128)(2,1)S(1)} %add_convert_fusion.1), channel_id=1, source_target_pairs={{0,2},{4,0},{8,4},{12,8},{14,12},{10,14},{6,10},{2,6},{1,3},{5,1},... | collective-permute-start | bytes 786440 | tf_op jit(solution)/shard_map/ppermute | solution.py:32
  97.1 11.7 %collective-permute-start.32 = (bf16[256,512]{1,0:T(8,128)(2,1)S(1)}, bf16[256,512]{1,0:T(8,128)(2,1)S(1)}, u32[]{:S(2)}, u32[]{:S(2)}) collective-permute-start(bf16[256,512]{1,0:T(8,128)(2,1)S(1)} %add_convert_fusion.3), channel_id=1, source_target_pairs={{0,4},{4,8},{8,12},{12,14},{14,10},{10,6},{6,2},{2,0},{1,5},{5,9},... | collective-permute-start | bytes 786440 | tf_op jit(solution)/shard_map/ppermute | solution.py:32
  100.3 8.4 %collective-permute-start.25 = (bf16[256,512]{1,0:T(8,128)(2,1)S(1)}, bf16[256,512]{1,0:T(8,128)(2,1)S(1)}, u32[]{:S(2)}, u32[]{:S(2)}) collective-permute-start(bf16[256,512]{1,0:T(8,128)(2,1)S(1)} %add_convert_fusion.6), channel_id=1, source_target_pairs={{0,4},{4,8},{8,12},{12,14},{14,10},{10,6},{6,2},{2,0},{1,5},{5,9},... | collective-permute-start | bytes 786440 | tf_op jit(solution)/shard_map/ppermute | solution.py:32
  106.7 9.3 %collective-permute-start.36 = (bf16[256,512]{1,0:T(8,128)(2,1)S(1)}, bf16[256,512]{1,0:T(8,128)(2,1)S(1)}, u32[]{:S(2)}, u32[]{:S(2)}) collective-permute-start(bf16[256,512]{1,0:T(8,128)(2,1)S(1)} %add_convert_fusion), channel_id=1, source_target_pairs={{0,2},{4,0},{8,4},{12,8},{14,12},{10,14},{6,10},{2,6},{1,3},{5,1},... | collective-permute-start | bytes 786440 | tf_op jit(solution)/shard_map/ppermute | solution.py:32
  107.5 11.4 %collective-permute-start.29 = (bf16[256,512]{1,0:T(8,128)(2,1)S(1)}, bf16[256,512]{1,0:T(8,128)(2,1)S(1)}, u32[]{:S(2)}, u32[]{:S(2)}) collective-permute-start(bf16[256,512]{1,0:T(8,128)(2,1)S(1)} %convert_add_fusion.2), channel_id=1, source_target_pairs={{0,2},{4,0},{8,4},{12,8},{14,12},{10,14},{6,10},{2,6},{1,3},{5,1},... | collective-permute-start | bytes 786440 | tf_op jit(solution)/shard_map/ppermute | solution.py:32
  109.4 9.6 %collective-permute-start.26 = (bf16[256,512]{1,0:T(8,128)(2,1)S(1)}, bf16[256,512]{1,0:T(8,128)(2,1)S(1)}, u32[]{:S(2)}, u32[]{:S(2)}) collective-permute-start(bf16[256,512]{1,0:T(8,128)(2,1)S(1)} %convert_add_fusion.3), channel_id=1, source_target_pairs={{0,4},{4,8},{8,12},{12,14},{14,10},{10,6},{6,2},{2,0},{1,5},{5,9},... | collective-permute-start | bytes 786440 | tf_op jit(solution)/shard_map/ppermute | solution.py:32
  (11 other events, 27.2 us)

commit v17 on v14

--- a/solution.py
+++ b/solution.py
@@ -246,25 +246,33 @@
         )
 
     if chips <= longest_ring:
-        arrived = {}
-        late = delta
-        early = delta
-        for step in range(chips // 2, 0, -1):
-            for i, by in ((0, 1), (1, -1), (1, 1), (0, -1)):
-                if step == chips // 2 and (i, by) not in ((0, 1), (1, -1)):
-                    continue
-                total = term(by * step, i, delta)
+        four, three = [(0, 1), (1, -1)], [(1, 1), (0, -1)]
+        hops = [(chips // 2, four)]
+        for step in range(chips // 2 - 1, 0, -1):
+            hops += [(step, three), (step, four)]
+        arrived, gates = {}, [delta]
+        for hop, (step, ways) in enumerate(hops):
+            gate = after(gates[max(hop - 2, 0)] if hop > 2 else gates[-1], delta)
+            totals = [term(by * step, i, gate) for i, by in ways]
+            for at, (i, by) in enumerate(ways):
                 if (i, by) in arrived:
-                    total = total + arrived[i, by].astype(jnp.float32)
-                if step == 1 and i == 0:
-                    total = after(copied, total)
-                total = total.astype(jnp.bfloat16)
-                if step == chips // 2:
-                    early = after(total, early)
+                    totals[at], before = lax.optimization_barrier((totals[at], arrived[i, by]))
+                    totals[at] = totals[at] + before.astype(jnp.float32)
+            totals = [total.astype(jnp.bfloat16) for total in totals]
+            if hop == len(hops) - 1:
+                totals = after(copied, totals)
+            for (i, by), total in zip(ways, totals):
                 arrived[i, by] = along_ring(total, by)
-            if step == chips // 2:
-                late, weights = after(arrived[0, 1], (delta, weights))
+            gates.append(totals if hop < 2 else [arrived[way] for way in ways])
+            if hop == 0:
+                first_hop = [arrived[way] for way in ways]
+                weights = after(first_hop, weights)
                 copied = passed_on(weights)
+            if hop == 1:
+                second_hop = [arrived[way] for way in ways]
+            if hop == 2:
+                gates[1:3] = [first_hop, second_hop]
+        late = after(gates[-3], delta)
         owns = [term(0, i, late) for i in range(2)]
         arrived[1, 1] = after(owns, arrived[1, 1])
         arrived[0, -1] = after(owns, arrived[0, -1])

time: 119 us -> 125 us (1.050)
  waiting for transfers between devices: 45 us -> 49.3 us
    ppermute x28, waiting for transfers between devices: 34.8 us -> 39.2 us  [along_ring(): return lax.ppermute(block, 'chip', pairs)]
  transfers between devices with their start and end apart: 39 -> 39, of which waited for: 18 -> 20; matrix products, arithmetic and copies ran while one was open for 16% -> 14% of each run, Pallas kernels for 6% -> 6%
where the time goes in v17:
time: 125 us; the launch traced here: 124 us
  waiting for transfers between devices  49.3 us (39%)
  starting transfers between devices  39.6 us (32%)
  matrix products  18.5 us (15%)
  Pallas kernels  7.18 us (6%)
  local copies, waits for them, and re-layouts  5.08 us (4%)
  other arithmetic  4.02 us (3%)
    ppermute x28, waiting for transfers between devices, along_ring(): return lax.ppermute(block, 'chip', pairs)  39.2 us
    ppermute x28, starting transfers between devices, along_ring(): return lax.ppermute(block, 'chip', pairs)  31.8 us
    dot_general x16, matrix products, term(): lax.dot_general(columns(offset, i), delta, (((0,), (0,)), ((), ())), pref...  9.28 us
    dot_general x16, matrix products, product(): jnp.dot(columns(offset, i), block, preferred_element_type=jnp.float32)  7.67 us
    ppermute x4, waiting for transfers between devices, slab_blocks(): kept.append(lax.ppermute(stored, ('grp', 'chip', 'core'), pairs))  7.31 us
    pallas_call x2, Pallas kernels, normalize(): pl.pallas_call(functools.partial(normalize_kernel, 16), grid=(seqs,), in_...  7.18 us
    ppermute x4, starting transfers between devices, slab_blocks(): kept.append(lax.ppermute(stored, ('grp', 'chip', 'core'), pairs))  5.16 us
    unnamed x11, local copies, waits for them, and re-layouts  3.31 us
  transfers between devices with their start and end apart: 39, of which 20 were waited for; matrix products, arithmetic and copies ran while one was open for 14% of the time, Pallas kernels for 6%

profile of v17, /device:TPU:0, one launch (start us, length us, event | category | flops | bytes accessed | tf_op | source)
XLA Modules:
  0.0 124.3 jit_solution(17284425060484703494)
XLA Ops:
  0.5 1.5 %dynamic-slice_convert_fusion.1 = (bf16[256,512]{1,0:T(8,128)(2,1)S(1)}, bf16[256,512]{1,0:T(8,128)(2,1)S(1)}) fusion(f32[256,1024]{1,0:T(8,128)} %bitcast.58, s32[]{:T(128)S(6)} %mul.280, s32[]{:T(128)S(6)} %mul.281), kind=kLoop, calls=%fused_computation.34 | loop fusion | bytes 1048584 | tf_op jit(solution)/shard_map/convert_element_type | solution.py:139
  2.1 3.0 %collective-permute-start.2 = (bf16[256,512]{1,0:T(8,128)(2,1)S(1)}, bf16[256,512]{1,0:T(8,128)(2,1)S(1)}, u32[]{:S(2)}, u32[]{:S(2)}) collective-permute-start(bf16[256,512]{1,0:T(8,128)(2,1)S(1)} %get-tuple-element.147), channel_id=1, source_target_pairs={{0,4},{4,8},{8,12},{12,14},{14,10},{10,6},{6,2},{2,0},{1,5},{5,9},... | collective-permute-start | bytes 786440 | tf_op jit(solution)/shard_map/ppermute | solution.py:32
  6.1 2.9 %collective-permute-start.5 = (bf16[256,512]{1,0:T(8,128)(2,1)S(1)}, bf16[256,512]{1,0:T(8,128)(2,1)S(1)}, u32[]{:S(2)}, u32[]{:S(2)}) collective-permute-start(bf16[256,512]{1,0:T(8,128)(2,1)S(1)} %collective-permute-done.1), channel_id=1, source_target_pairs={{0,2},{4,0},{8,4},{12,8},{14,12},{10,14},{6,10},{2,6},{1,3},{5,1},... | collective-permute-start | bytes 786440 | tf_op jit(solution)/shard_map/ppermute | solution.py:32
  9.1 2.7 %collective-permute-done.2 = bf16[256,512]{1,0:T(8,128)(2,1)S(1)} collective-permute-done((bf16[256,512]{1,0:T(8,128)(2,1)S(1)}, bf16[256,512]{1,0:T(8,128)(2,1)S(1)}, u32[]{:S(2)}, u32[]{:S(2)}) %collective-permute-start.2) | collective-permute-done | bytes 262176 | tf_op jit(solution)/shard_map/ppermute | solution.py:32
  11.8 2.5 %collective-permute-start.7 = (bf16[256,512]{1,0:T(8,128)(2,1)S(1)}, bf16[256,512]{1,0:T(8,128)(2,1)S(1)}, u32[]{:S(2)}, u32[]{:S(2)}) collective-permute-start(bf16[256,512]{1,0:T(8,128)(2,1)S(1)} %collective-permute-done.2), channel_id=1, source_target_pairs={{0,4},{4,8},{8,12},{12,14},{14,10},{10,6},{6,2},{2,0},{1,5},{5,9},... | collective-permute-start | bytes 786440 | tf_op jit(solution)/shard_map/ppermute | solution.py:32
  15.0 1.9 %copy-done = bf16[1,3,128,4096]{3,2,1,0:T(8,128)(2,1)S(1)} copy-done((bf16[1,3,128,4096]{3,2,1,0:T(8,128)(2,1)S(1)}, bf16[1,3,128,4096]{3,2,1,0:T(8,128)(2,1)}, u32[]{:S(2)}) %copy-start) | copy-done | bytes 3145752
  17.6 3.6 %shard_map.64.refs_0_ = bf16[768,4096]{1,0:T(8,128)(2,1)S(1)} custom-call(bf16[3,128,4096]{2,1,0:T(8,128)(2,1)S(1)} %bitcast.54, f32[1,4096]{1,0:T(1,128)S(1)} %bitcast.55), custom_call_target="tpu_custom_call" | custom-call | flops 9437184 | bytes 6291456 | tf_op jit(solution)/shard_map/pallas_call | solution.py:99
  21.2 2.1 %collective-permute-start.9 = (bf16[256,512]{1,0:T(8,128)(2,1)S(1)}, bf16[256,512]{1,0:T(8,128)(2,1)S(1)}, u32[]{:S(2)}, u32[]{:S(2)}) collective-permute-start(bf16[256,512]{1,0:T(8,128)(2,1)S(1)} %collective-permute-done.4), channel_id=1, source_target_pairs={{0,4},{4,8},{8,12},{12,14},{14,10},{10,6},{6,2},{2,0},{1,5},{5,9},... | collective-permute-start | bytes 786440 | tf_op jit(solution)/shard_map/ppermute | solution.py:32
  23.4 2.1 %collective-permute-start.11 = (bf16[256,512]{1,0:T(8,128)(2,1)S(1)}, bf16[256,512]{1,0:T(8,128)(2,1)S(1)}, u32[]{:S(2)}, u32[]{:S(2)}) collective-permute-start(bf16[256,512]{1,0:T(8,128)(2,1)S(1)} %collective-permute-done.7), channel_id=1, source_target_pairs={{0,4},{4,8},{8,12},{12,14},{14,10},{10,6},{6,2},{2,0},{1,5},{5,9},... | collective-permute-start | bytes 786440 | tf_op jit(solution)/shard_map/ppermute | solution.py:32
  25.5 3.6 %shard_map.65 = bf16[768,4096]{1,0:T(8,128)(2,1)S(1)} custom-call(bf16[3,128,4096]{2,1,0:T(8,128)(2,1)S(1)} %collective-permute-done.states_ref, f32[1,4096]{1,0:T(1,128)S(1)} %bitcast.56, bf16[768,4096]{1,0:T(8,128)(2,1)S(1)} %shard_map.64.refs_0_), custom_call_target="tpu_custom_call", output_to_operand_aliasing={{}: (2, {})} | custom-call | flops 9437184 | bytes 6291456 | tf_op jit(solution)/shard_map/pallas_call | solution.py:99
  32.6 2.1 %collective-permute-start.13 = (bf16[256,512]{1,0:T(8,128)(2,1)S(1)}, bf16[256,512]{1,0:T(8,128)(2,1)S(1)}, u32[]{:S(2)}, u32[]{:S(2)}) collective-permute-start(bf16[256,512]{1,0:T(8,128)(2,1)S(1)} %collective-permute-done.9), channel_id=1, source_target_pairs={{0,4},{4,8},{8,12},{12,14},{14,10},{10,6},{6,2},{2,0},{1,5},{5,9},... | collective-permute-start | bytes 786440 | tf_op jit(solution)/shard_map/ppermute | solution.py:32
  34.7 2.0 %collective-permute-start.15 = (bf16[256,512]{1,0:T(8,128)(2,1)S(1)}, bf16[256,512]{1,0:T(8,128)(2,1)S(1)}, u32[]{:S(2)}, u32[]{:S(2)}) collective-permute-start(bf16[256,512]{1,0:T(8,128)(2,1)S(1)} %collective-permute-done.11), channel_id=1, source_target_pairs={{0,4},{4,8},{8,12},{12,14},{14,10},{10,6},{6,2},{2,0},{1,5},{5,9},... | collective-permute-start | bytes 786440 | tf_op jit(solution)/shard_map/ppermute | solution.py:32
  39.6 3.3 %collective-permute-done.14 = bf16[256,512]{1,0:T(8,128)(2,1)S(1)} collective-permute-done((bf16[256,512]{1,0:T(8,128)(2,1)S(1)}, bf16[256,512]{1,0:T(8,128)(2,1)S(1)}, u32[]{:S(2)}, u32[]{:S(2)}) %collective-permute-start.14) | collective-permute-done | bytes 262176 | tf_op jit(solution)/shard_map/ppermute | solution.py:32
  44.2 2.9 %collective-permute-done.15 = bf16[256,512]{1,0:T(8,128)(2,1)S(1)} collective-permute-done((bf16[256,512]{1,0:T(8,128)(2,1)S(1)}, bf16[256,512]{1,0:T(8,128)(2,1)S(1)}, u32[]{:S(2)}, u32[]{:S(2)}) %collective-permute-start.15) | collective-permute-done | bytes 262176 | tf_op jit(solution)/shard_map/ppermute | solution.py:32
  47.5 3.0 %collective-permute-done.16 = bf16[256,512]{1,0:T(8,128)(2,1)S(1)} collective-permute-done((bf16[256,512]{1,0:T(8,128)(2,1)S(1)}, bf16[256,512]{1,0:T(8,128)(2,1)S(1)}, u32[]{:S(2)}, u32[]{:S(2)}) %collective-permute-start.16) | collective-permute-done | bytes 262176 | tf_op jit(solution)/shard_map/ppermute | solution.py:32
  54.8 1.3 %collective-permute-start.19 = (bf16[6,1024]{1,0:T(8,128)(2,1)S(1)}, bf16[6,1024]{1,0:T(8,128)(2,1)S(1)}, u32[]{:S(2)}, u32[]{:S(2)}) collective-permute-start(bf16[6,1024]{1,0:T(8,128)(2,1)S(1)} %maximum_select_fusion.2), channel_id=1, source_target_pairs={{20,0},{27,1},{24,4},{23,5},{28,8},{19,9},{30,12},{17,13},{26,14},... | collective-permute-start | bytes 36872 | tf_op jit(solution)/shard_map/ppermute | solution.py:64
  56.1 1.3 %collective-permute-start.20 = (bf16[6,1024]{1,0:T(8,128)(2,1)S(1)}, bf16[6,1024]{1,0:T(8,128)(2,1)S(1)}, u32[]{:S(2)}, u32[]{:S(2)}) collective-permute-start(bf16[6,1024]{1,0:T(8,128)(2,1)S(1)} %maximum_select_fusion.2), channel_id=1, source_target_pairs={{24,0},{23,1},{28,4},{19,5},{30,8},{17,9},{26,12},{21,13},{22,14},... | collective-permute-start | bytes 36872 | tf_op jit(solution)/shard_map/ppermute | solution.py:64
  57.4 1.3 %collective-permute-start.21 = (bf16[6,1024]{1,0:T(8,128)(2,1)S(1)}, bf16[6,1024]{1,0:T(8,128)(2,1)S(1)}, u32[]{:S(2)}, u32[]{:S(2)}) collective-permute-start(bf16[6,1024]{1,0:T(8,128)(2,1)S(1)} %maximum_select_fusion.2), channel_id=1, source_target_pairs={{28,0},{19,1},{30,4},{17,5},{26,8},{21,9},{22,12},{25,13},{18,14},... | collective-permute-start | bytes 36872 | tf_op jit(solution)/shard_map/ppermute | solution.py:64
  59.2 2.3 %collective-permute-done.19 = bf16[6,1024]{1,0:T(8,128)(2,1)S(1)} collective-permute-done((bf16[6,1024]{1,0:T(8,128)(2,1)S(1)}, bf16[6,1024]{1,0:T(8,128)(2,1)S(1)}, u32[]{:S(2)}, u32[]{:S(2)}) %collective-permute-start.19) | collective-permute-done | bytes 12320 | tf_op jit(solution)/shard_map/ppermute | solution.py:64
  61.5 2.3 %collective-permute-done.20 = bf16[6,1024]{1,0:T(8,128)(2,1)S(1)} collective-permute-done((bf16[6,1024]{1,0:T(8,128)(2,1)S(1)}, bf16[6,1024]{1,0:T(8,128)(2,1)S(1)}, u32[]{:S(2)}, u32[]{:S(2)}) %collective-permute-start.20) | collective-permute-done | bytes 12320 | tf_op jit(solution)/shard_map/ppermute | solution.py:64
  63.8 2.3 %collective-permute-done.21 = bf16[6,1024]{1,0:T(8,128)(2,1)S(1)} collective-permute-done((bf16[6,1024]{1,0:T(8,128)(2,1)S(1)}, bf16[6,1024]{1,0:T(8,128)(2,1)S(1)}, u32[]{:S(2)}, u32[]{:S(2)}) %collective-permute-start.21) | collective-permute-done | bytes 12320 | tf_op jit(solution)/shard_map/ppermute | solution.py:64
  71.6 1.5 %collective-permute-start.25 = (bf16[256,512]{1,0:T(8,128)(2,1)S(1)}, bf16[256,512]{1,0:T(8,128)(2,1)S(1)}, u32[]{:S(2)}, u32[]{:S(2)}) collective-permute-start(bf16[256,512]{1,0:T(8,128)(2,1)S(1)} %convolution_convert_fusion.3), channel_id=1, source_target_pairs={{0,4},{4,8},{8,12},{12,14},{14,10},{10,6},{6,2},{2,0},{1,5},{5,9},... | collective-permute-start | bytes 786440 | tf_op jit(solution)/shard_map/ppermute | solution.py:32
  73.1 1.5 %collective-permute-start.23 = (bf16[256,512]{1,0:T(8,128)(2,1)S(1)}, bf16[256,512]{1,0:T(8,128)(2,1)S(1)}, u32[]{:S(2)}, u32[]{:S(2)}) collective-permute-start(bf16[256,512]{1,0:T(8,128)(2,1)S(1)} %convolution_convert_fusion.1), channel_id=1, source_target_pairs={{0,4},{4,8},{8,12},{12,14},{14,10},{10,6},{6,2},{2,0},{1,5},{5,9},... | collective-permute-start | bytes 786440 | tf_op jit(solution)/shard_map/ppermute | solution.py:32
  76.3 9.0 %collective-permute-done.23 = bf16[256,512]{1,0:T(8,128)(2,1)S(1)} collective-permute-done((bf16[256,512]{1,0:T(8,128)(2,1)S(1)}, bf16[256,512]{1,0:T(8,128)(2,1)S(1)}, u32[]{:S(2)}, u32[]{:S(2)}) %collective-permute-start.23) | collective-permute-done | bytes 262176 | tf_op jit(solution)/shard_map/ppermute | solution.py:32
  90.0 1.6 %collective-permute-start.32 = (bf16[256,512]{1,0:T(8,128)(2,1)S(1)}, bf16[256,512]{1,0:T(8,128)(2,1)S(1)}, u32[]{:S(2)}, u32[]{:S(2)}) collective-permute-start(bf16[256,512]{1,0:T(8,128)(2,1)S(1)} %add_convert_fusion.5), channel_id=1, source_target_pairs={{0,4},{4,8},{8,12},{12,14},{14,10},{10,6},{6,2},{2,0},{1,5},{5,9},... | collective-permute-start | bytes 786440 | tf_op jit(solution)/shard_map/ppermute | solution.py:32
  92.3 1.8 %collective-permute-start.31 = (bf16[256,1024]{1,0:T(8,128)(2,1)S(1)}, bf16[256,1024]{1,0:T(8,128)(2,1)S(1)}, u32[]{:S(2)}, u32[]{:S(2)}) collective-permute-start(bf16[256,1024]{1,0:T(8,128)(2,1)S(1)} %convert_element_type.174), channel_id=1, source_target_pairs={{0,16},{1,17},{2,18},{3,19},{4,20},{5,21},{6,22},{7,23},{8,24},{9,... | collective-permute-start | bytes 1572872 | tf_op jit(solution)/shard_map/ppermute | solution.py:40
  94.1 2.9 %collective-permute-done.29 = bf16[256,512]{1,0:T(8,128)(2,1)S(1)} collective-permute-done((bf16[256,512]{1,0:T(8,128)(2,1)S(1)}, bf16[256,512]{1,0:T(8,128)(2,1)S(1)}, u32[]{:S(2)}, u32[]{:S(2)}) %collective-permute-start.29) | collective-permute-done | bytes 262176 | tf_op jit(solution)/shard_map/ppermute | solution.py:32
  98.8 3.0 %collective-permute-done.32 = bf16[256,512]{1,0:T(8,128)(2,1)S(1)} collective-permute-done((bf16[256,512]{1,0:T(8,128)(2,1)S(1)}, bf16[256,512]{1,0:T(8,128)(2,1)S(1)}, u32[]{:S(2)}, u32[]{:S(2)}) %collective-permute-start.32) | collective-permute-done | bytes 262176 | tf_op jit(solution)/shard_map/ppermute | solution.py:32
  108.1 3.5 %collective-permute-done.30 = bf16[256,512]{1,0:T(8,128)(2,1)S(1)} collective-permute-done((bf16[256,512]{1,0:T(8,128)(2,1)S(1)}, bf16[256,512]{1,0:T(8,128)(2,1)S(1)}, u32[]{:S(2)}, u32[]{:S(2)}) %collective-permute-start.30) | collective-permute-done | bytes 262176 | tf_op jit(solution)/shard_map/ppermute | solution.py:32
  111.6 2.2 %collective-permute-done.27 = bf16[256,512]{1,0:T(8,128)(2,1)S(1)} collective-permute-done((bf16[256,512]{1,0:T(8,128)(2,1)S(1)}, bf16[256,512]{1,0:T(8,128)(2,1)S(1)}, u32[]{:S(2)}, u32[]{:S(2)}) %collective-permute-start.27) | collective-permute-done | bytes 262176 | tf_op jit(solution)/shard_map/ppermute | solution.py:32
  117.3 3.1 %collective-permute-done.37 = bf16[256,512]{1,0:T(8,128)(2,1)S(1)} collective-permute-done((bf16[256,512]{1,0:T(8,128)(2,1)S(1)}, bf16[256,512]{1,0:T(8,128)(2,1)S(1)}, u32[]{:S(2)}, u32[]{:S(2)}) %collective-permute-start.37) | collective-permute-done | bytes 262176 | tf_op jit(solution)/shard_map/ppermute | solution.py:32
  120.7 2.1 %collective-permute-done.34 = bf16[256,512]{1,0:T(8,128)(2,1)S(1)} collective-permute-done((bf16[256,512]{1,0:T(8,128)(2,1)S(1)}, bf16[256,512]{1,0:T(8,128)(2,1)S(1)}, u32[]{:S(2)}, u32[]{:S(2)}) %collective-permute-start.34) | collective-permute-done | bytes 262176 | tf_op jit(solution)/shard_map/ppermute | solution.py:32
  (137 shorter events, 41.6 us)
Async XLA Ops:
  0.0 25.5 %collective-permute-start = (bf16[3,128,4096]{2,1,0:T(8,128)(2,1)}, bf16[3,128,4096]{2,1,0:T(8,128)(2,1)S(1)}, u32[]{:S(2)}, u32[]{:S(2)}) collective-permute-start(bf16[3,128,4096]{2,1,0:T(8,128)(2,1)} %bitcast.53), channel_id=1, source_target_pairs={{0,1},{1,0},{2,3},{3,2},{4,5},{5,4},{6,7},{7,6},{8,9},{9,8},{10,11... | collective-permute-start | bytes 9437192 | tf_op jit(solution)/shard_map/ppermute | solution.py:52
  2.1 9.7 %collective-permute-start.2 = (bf16[256,512]{1,0:T(8,128)(2,1)S(1)}, bf16[256,512]{1,0:T(8,128)(2,1)S(1)}, u32[]{:S(2)}, u32[]{:S(2)}) collective-permute-start(bf16[256,512]{1,0:T(8,128)(2,1)S(1)} %get-tuple-element.147), channel_id=1, source_target_pairs={{0,4},{4,8},{8,12},{12,14},{14,10},{10,6},{6,2},{2,0},{1,5},{5,9},... | collective-permute-start | bytes 786440 | tf_op jit(solution)/shard_map/ppermute | solution.py:32
  5.1 9.2 %collective-permute-start.3 = (bf16[256,512]{1,0:T(8,128)(2,1)S(1)}, bf16[256,512]{1,0:T(8,128)(2,1)S(1)}, u32[]{:S(2)}, u32[]{:S(2)}) collective-permute-start(bf16[256,512]{1,0:T(8,128)(2,1)S(1)} %get-tuple-element.147), channel_id=1, source_target_pairs={{0,2},{4,0},{8,4},{12,8},{14,12},{10,14},{6,10},{2,6},{1,3},{5,1},... | collective-permute-start | bytes 786440 | tf_op jit(solution)/shard_map/ppermute | solution.py:32
  6.1 15.0 %collective-permute-start.5 = (bf16[256,512]{1,0:T(8,128)(2,1)S(1)}, bf16[256,512]{1,0:T(8,128)(2,1)S(1)}, u32[]{:S(2)}, u32[]{:S(2)}) collective-permute-start(bf16[256,512]{1,0:T(8,128)(2,1)S(1)} %collective-permute-done.1), channel_id=1, source_target_pairs={{0,2},{4,0},{8,4},{12,8},{14,12},{10,14},{6,10},{2,6},{1,3},{5,1},... | collective-permute-start | bytes 786440 | tf_op jit(solution)/shard_map/ppermute | solution.py:32
  9.0 12.2 %collective-permute-start.4 = (bf16[256,512]{1,0:T(8,128)(2,1)S(1)}, bf16[256,512]{1,0:T(8,128)(2,1)S(1)}, u32[]{:S(2)}, u32[]{:S(2)}) collective-permute-start(bf16[256,512]{1,0:T(8,128)(2,1)S(1)} %collective-permute-done.1), channel_id=1, source_target_pairs={{0,4},{4,8},{8,12},{12,14},{14,10},{10,6},{6,2},{2,0},{1,5},{5,9},... | collective-permute-start | bytes 786440 | tf_op jit(solution)/shard_map/ppermute | solution.py:32
  11.8 11.6 %collective-permute-start.7 = (bf16[256,512]{1,0:T(8,128)(2,1)S(1)}, bf16[256,512]{1,0:T(8,128)(2,1)S(1)}, u32[]{:S(2)}, u32[]{:S(2)}) collective-permute-start(bf16[256,512]{1,0:T(8,128)(2,1)S(1)} %collective-permute-done.2), channel_id=1, source_target_pairs={{0,4},{4,8},{8,12},{12,14},{14,10},{10,6},{6,2},{2,0},{1,5},{5,9},... | collective-permute-start | bytes 786440 | tf_op jit(solution)/shard_map/ppermute | solution.py:32
  14.3 11.2 %collective-permute-start.8 = (bf16[256,512]{1,0:T(8,128)(2,1)S(1)}, bf16[256,512]{1,0:T(8,128)(2,1)S(1)}, u32[]{:S(2)}, u32[]{:S(2)}) collective-permute-start(bf16[256,512]{1,0:T(8,128)(2,1)S(1)} %collective-permute-done.3), channel_id=1, source_target_pairs={{0,2},{4,0},{8,4},{12,8},{14,12},{10,14},{6,10},{2,6},{1,3},{5,1},... | collective-permute-start | bytes 786440 | tf_op jit(solution)/shard_map/ppermute | solution.py:32
  21.2 11.4 %collective-permute-start.9 = (bf16[256,512]{1,0:T(8,128)(2,1)S(1)}, bf16[256,512]{1,0:T(8,128)(2,1)S(1)}, u32[]{:S(2)}, u32[]{:S(2)}) collective-permute-start(bf16[256,512]{1,0:T(8,128)(2,1)S(1)} %collective-permute-done.4), channel_id=1, source_target_pairs={{0,4},{4,8},{8,12},{12,14},{14,10},{10,6},{6,2},{2,0},{1,5},{5,9},... | collective-permute-start | bytes 786440 | tf_op jit(solution)/shard_map/ppermute | solution.py:32
  23.3 11.3 %collective-permute-start.10 = (bf16[256,512]{1,0:T(8,128)(2,1)S(1)}, bf16[256,512]{1,0:T(8,128)(2,1)S(1)}, u32[]{:S(2)}, u32[]{:S(2)}) collective-permute-start(bf16[256,512]{1,0:T(8,128)(2,1)S(1)} %collective-permute-done.5), channel_id=1, source_target_pairs={{0,2},{4,0},{8,4},{12,8},{14,12},{10,14},{6,10},{2,6},{1,3},{5,1},... | collective-permute-start | bytes 786440 | tf_op jit(solution)/shard_map/ppermute | solution.py:32
  23.4 11.3 %collective-permute-start.11 = (bf16[256,512]{1,0:T(8,128)(2,1)S(1)}, bf16[256,512]{1,0:T(8,128)(2,1)S(1)}, u32[]{:S(2)}, u32[]{:S(2)}) collective-permute-start(bf16[256,512]{1,0:T(8,128)(2,1)S(1)} %collective-permute-done.7), channel_id=1, source_target_pairs={{0,4},{4,8},{8,12},{12,14},{14,10},{10,6},{6,2},{2,0},{1,5},{5,9},... | collective-permute-start | bytes 786440 | tf_op jit(solution)/shard_map/ppermute | solution.py:32
  25.5 25.5 %collective-permute-start.12 = (bf16[256,512]{1,0:T(8,128)(2,1)S(1)}, bf16[256,512]{1,0:T(8,128)(2,1)S(1)}, u32[]{:S(2)}, u32[]{:S(2)}) collective-permute-start(bf16[256,512]{1,0:T(8,128)(2,1)S(1)} %collective-permute-done.8), channel_id=1, source_target_pairs={{0,2},{4,0},{8,4},{12,8},{14,12},{10,14},{6,10},{2,6},{1,3},{5,1},... | collective-permute-start | bytes 786440 | tf_op jit(solution)/shard_map/ppermute | solution.py:32
  32.5 6.6 %collective-permute-start.6 = (s32[3,224]{1,0:T(4,128)S(1)}, s32[3,224]{1,0:T(4,128)S(1)}, u32[]{:S(2)}, u32[]{:S(2)}) collective-permute-start(s32[3,224]{1,0:T(4,128)S(1)} %pad_add_fusion.1), channel_id=1, source_target_pairs={{0,1},{1,0},{2,3},{3,2},{4,5},{5,4},{6,7},{7,6},{8,9},{9,8},{10,11... | collective-permute-start | bytes 8072 | tf_op jit(solution)/shard_map/ppermute | solution.py:52
  32.6 11.2 %collective-permute-start.13 = (bf16[256,512]{1,0:T(8,128)(2,1)S(1)}, bf16[256,512]{1,0:T(8,128)(2,1)S(1)}, u32[]{:S(2)}, u32[]{:S(2)}) collective-permute-start(bf16[256,512]{1,0:T(8,128)(2,1)S(1)} %collective-permute-done.9), channel_id=1, source_target_pairs={{0,4},{4,8},{8,12},{12,14},{14,10},{10,6},{6,2},{2,0},{1,5},{5,9},... | collective-permute-start | bytes 786440 | tf_op jit(solution)/shard_map/ppermute | solution.py:32
  34.6 8.4 %collective-permute-start.14 = (bf16[256,512]{1,0:T(8,128)(2,1)S(1)}, bf16[256,512]{1,0:T(8,128)(2,1)S(1)}, u32[]{:S(2)}, u32[]{:S(2)}) collective-permute-start(bf16[256,512]{1,0:T(8,128)(2,1)S(1)} %collective-permute-done.10), channel_id=1, source_target_pairs={{0,2},{4,0},{8,4},{12,8},{14,12},{10,14},{6,10},{2,6},{1,3},{5,1},... | collective-permute-start | bytes 786440 | tf_op jit(solution)/shard_map/ppermute | solution.py:32
  34.7 12.3 %collective-permute-start.15 = (bf16[256,512]{1,0:T(8,128)(2,1)S(1)}, bf16[256,512]{1,0:T(8,128)(2,1)S(1)}, u32[]{:S(2)}, u32[]{:S(2)}) collective-permute-start(bf16[256,512]{1,0:T(8,128)(2,1)S(1)} %collective-permute-done.11), channel_id=1, source_target_pairs={{0,4},{4,8},{8,12},{12,14},{14,10},{10,6},{6,2},{2,0},{1,5},{5,9},... | collective-permute-start | bytes 786440 | tf_op jit(solution)/shard_map/ppermute | solution.py:32
  43.0 7.5 %collective-permute-start.16 = (bf16[256,512]{1,0:T(8,128)(2,1)S(1)}, bf16[256,512]{1,0:T(8,128)(2,1)S(1)}, u32[]{:S(2)}, u32[]{:S(2)}) collective-permute-start(bf16[256,512]{1,0:T(8,128)(2,1)S(1)} %collective-permute-done.14), channel_id=1, source_target_pairs={{0,2},{4,0},{8,4},{12,8},{14,12},{10,14},{6,10},{2,6},{1,3},{5,1},... | collective-permute-start | bytes 786440 | tf_op jit(solution)/shard_map/ppermute | solution.py:32
  54.8 6.7 %collective-permute-start.19 = (bf16[6,1024]{1,0:T(8,128)(2,1)S(1)}, bf16[6,1024]{1,0:T(8,128)(2,1)S(1)}, u32[]{:S(2)}, u32[]{:S(2)}) collective-permute-start(bf16[6,1024]{1,0:T(8,128)(2,1)S(1)} %maximum_select_fusion.2), channel_id=1, source_target_pairs={{20,0},{27,1},{24,4},{23,5},{28,8},{19,9},{30,12},{17,13},{26,14},... | collective-permute-start | bytes 36872 | tf_op jit(solution)/shard_map/ppermute | solution.py:64
  56.1 7.6 %collective-permute-start.20 = (bf16[6,1024]{1,0:T(8,128)(2,1)S(1)}, bf16[6,1024]{1,0:T(8,128)(2,1)S(1)}, u32[]{:S(2)}, u32[]{:S(2)}) collective-permute-start(bf16[6,1024]{1,0:T(8,128)(2,1)S(1)} %maximum_select_fusion.2), channel_id=1, source_target_pairs={{24,0},{23,1},{28,4},{19,5},{30,8},{17,9},{26,12},{21,13},{22,14},... | collective-permute-start | bytes 36872 | tf_op jit(solution)/shard_map/ppermute | solution.py:64
  57.4 8.6 %collective-permute-start.21 = (bf16[6,1024]{1,0:T(8,128)(2,1)S(1)}, bf16[6,1024]{1,0:T(8,128)(2,1)S(1)}, u32[]{:S(2)}, u32[]{:S(2)}) collective-permute-start(bf16[6,1024]{1,0:T(8,128)(2,1)S(1)} %maximum_select_fusion.2), channel_id=1, source_target_pairs={{28,0},{19,1},{30,4},{17,5},{26,8},{21,9},{22,12},{25,13},{18,14},... | collective-permute-start | bytes 36872 | tf_op jit(solution)/shard_map/ppermute | solution.py:64
  71.0 15.4 %collective-permute-start.28 = (bf16[256,512]{1,0:T(8,128)(2,1)S(1)}, bf16[256,512]{1,0:T(8,128)(2,1)S(1)}, u32[]{:S(2)}, u32[]{:S(2)}) collective-permute-start(bf16[256,512]{1,0:T(8,128)(2,1)S(1)} %convolution_convert_fusion.2), channel_id=1, source_target_pairs={{0,2},{4,0},{8,4},{12,8},{14,12},{10,14},{6,10},{2,6},{1,3},{5,1},... | collective-permute-start | bytes 786440 | tf_op jit(solution)/shard_map/ppermute | solution.py:32
  71.6 14.9 %collective-permute-start.25 = (bf16[256,512]{1,0:T(8,128)(2,1)S(1)}, bf16[256,512]{1,0:T(8,128)(2,1)S(1)}, u32[]{:S(2)}, u32[]{:S(2)}) collective-permute-start(bf16[256,512]{1,0:T(8,128)(2,1)S(1)} %convolution_convert_fusion.3), channel_id=1, source_target_pairs={{0,4},{4,8},{8,12},{12,14},{14,10},{10,6},{6,2},{2,0},{1,5},{5,9},... | collective-permute-start | bytes 786440 | tf_op jit(solution)/shard_map/ppermute | solution.py:32
  73.1 12.2 %collective-permute-start.23 = (bf16[256,512]{1,0:T(8,128)(2,1)S(1)}, bf16[256,512]{1,0:T(8,128)(2,1)S(1)}, u32[]{:S(2)}, u32[]{:S(2)}) collective-permute-start(bf16[256,512]{1,0:T(8,128)(2,1)S(1)} %convolution_convert_fusion.1), channel_id=1, source_target_pairs={{0,4},{4,8},{8,12},{12,14},{14,10},{10,6},{6,2},{2,0},{1,5},{5,9},... | collective-permute-start | bytes 786440 | tf_op jit(solution)/shard_map/ppermute | solution.py:32
  74.6 10.7 %collective-permute-start.24 = (bf16[256,512]{1,0:T(8,128)(2,1)S(1)}, bf16[256,512]{1,0:T(8,128)(2,1)S(1)}, u32[]{:S(2)}, u32[]{:S(2)}) collective-permute-start(bf16[256,512]{1,0:T(8,128)(2,1)S(1)} %convolution_convert_fusion), channel_id=1, source_target_pairs={{0,2},{4,0},{8,4},{12,8},{14,12},{10,14},{6,10},{2,6},{1,3},{5,1},... | collective-permute-start | bytes 786440 | tf_op jit(solution)/shard_map/ppermute | solution.py:32
  87.7 9.3 %collective-permute-start.29 = (bf16[256,512]{1,0:T(8,128)(2,1)S(1)}, bf16[256,512]{1,0:T(8,128)(2,1)S(1)}, u32[]{:S(2)}, u32[]{:S(2)}) collective-permute-start(bf16[256,512]{1,0:T(8,128)(2,1)S(1)} %add_convert_fusion.7), channel_id=1, source_target_pairs={{0,2},{4,0},{8,4},{12,8},{14,12},{10,14},{6,10},{2,6},{1,3},{5,1},... | collective-permute-start | bytes 786440 | tf_op jit(solution)/shard_map/ppermute | solution.py:32
  88.9 9.3 %collective-permute-start.26 = (bf16[256,512]{1,0:T(8,128)(2,1)S(1)}, bf16[256,512]{1,0:T(8,128)(2,1)S(1)}, u32[]{:S(2)}, u32[]{:S(2)}) collective-permute-start(bf16[256,512]{1,0:T(8,128)(2,1)S(1)} %add_convert_fusion.9), channel_id=1, source_target_pairs={{0,4},{4,8},{8,12},{12,14},{14,10},{10,6},{6,2},{2,0},{1,5},{5,9},... | collective-permute-start | bytes 786440 | tf_op jit(solution)/shard_map/ppermute | solution.py:32
  90.0 11.8 %collective-permute-start.32 = (bf16[256,512]{1,0:T(8,128)(2,1)S(1)}, bf16[256,512]{1,0:T(8,128)(2,1)S(1)}, u32[]{:S(2)}, u32[]{:S(2)}) collective-permute-start(bf16[256,512]{1,0:T(8,128)(2,1)S(1)} %add_convert_fusion.5), channel_id=1, source_target_pairs={{0,4},{4,8},{8,12},{12,14},{14,10},{10,6},{6,2},{2,0},{1,5},{5,9},... | collective-permute-start | bytes 786440 | tf_op jit(solution)/shard_map/ppermute | solution.py:32
  91.7 13.9 %collective-permute-start.33 = (bf16[256,512]{1,0:T(8,128)(2,1)S(1)}, bf16[256,512]{1,0:T(8,128)(2,1)S(1)}, u32[]{:S(2)}, u32[]{:S(2)}) collective-permute-start(bf16[256,512]{1,0:T(8,128)(2,1)S(1)} %add_convert_fusion.4), channel_id=1, source_target_pairs={{0,2},{4,0},{8,4},{12,8},{14,12},{10,14},{6,10},{2,6},{1,3},{5,1},... | collective-permute-start | bytes 786440 | tf_op jit(solution)/shard_map/ppermute | solution.py:32
  92.3 21.7 %collective-permute-start.31 = (bf16[256,1024]{1,0:T(8,128)(2,1)S(1)}, bf16[256,1024]{1,0:T(8,128)(2,1)S(1)}, u32[]{:S(2)}, u32[]{:S(2)}) collective-permute-start(bf16[256,1024]{1,0:T(8,128)(2,1)S(1)} %convert_element_type.174), channel_id=1, source_target_pairs={{0,16},{1,17},{2,18},{3,19},{4,20},{5,21},{6,22},{7,23},{8,24},{9,... | collective-permute-start | bytes 1572872 | tf_op jit(solution)/shard_map/ppermute | solution.py:40
  101.9 14.5 %collective-permute-start.36 = (bf16[256,512]{1,0:T(8,128)(2,1)S(1)}, bf16[256,512]{1,0:T(8,128)(2,1)S(1)}, u32[]{:S(2)}, u32[]{:S(2)}) collective-permute-start(bf16[256,512]{1,0:T(8,128)(2,1)S(1)} %add_convert_fusion), channel_id=1, source_target_pairs={{0,4},{4,8},{8,12},{12,14},{14,10},{10,6},{6,2},{2,0},{1,5},{5,9},... | collective-permute-start | bytes 786440 | tf_op jit(solution)/shard_map/ppermute | solution.py:32
  102.8 8.8 %collective-permute-start.30 = (bf16[256,512]{1,0:T(8,128)(2,1)S(1)}, bf16[256,512]{1,0:T(8,128)(2,1)S(1)}, u32[]{:S(2)}, u32[]{:S(2)}) collective-permute-start(bf16[256,512]{1,0:T(8,128)(2,1)S(1)} %add_convert_fusion.6), channel_id=1, source_target_pairs={{0,2},{4,0},{8,4},{12,8},{14,12},{10,14},{6,10},{2,6},{1,3},{5,1},... | collective-permute-start | bytes 786440 | tf_op jit(solution)/shard_map/ppermute | solution.py:32
  104.2 9.7 %collective-permute-start.27 = (bf16[256,512]{1,0:T(8,128)(2,1)S(1)}, bf16[256,512]{1,0:T(8,128)(2,1)S(1)}, u32[]{:S(2)}, u32[]{:S(2)}) collective-permute-start(bf16[256,512]{1,0:T(8,128)(2,1)S(1)} %add_convert_fusion.8), channel_id=1, source_target_pairs={{0,4},{4,8},{8,12},{12,14},{14,10},{10,6},{6,2},{2,0},{1,5},{5,9},... | collective-permute-start | bytes 786440 | tf_op jit(solution)/shard_map/ppermute | solution.py:32
  106.3 14.4 %collective-permute-start.35 = (bf16[256,512]{1,0:T(8,128)(2,1)S(1)}, bf16[256,512]{1,0:T(8,128)(2,1)S(1)}, u32[]{:S(2)}, u32[]{:S(2)}) collective-permute-start(bf16[256,512]{1,0:T(8,128)(2,1)S(1)} %add_convert_fusion.1), channel_id=1, source_target_pairs={{0,2},{4,0},{8,4},{12,8},{14,12},{10,14},{6,10},{2,6},{1,3},{5,1},... | collective-permute-start | bytes 786440 | tf_op jit(solution)/shard_map/ppermute | solution.py:32
  (12 other events, 38.7 us)

commit v18 on v17

--- a/solution.py
+++ b/solution.py
@@ -250,29 +250,26 @@
         hops = [(chips // 2, four)]
         for step in range(chips // 2 - 1, 0, -1):
             hops += [(step, three), (step, four)]
-        arrived, gates = {}, [delta]
+        arrived, previous, source = {}, delta, delta
         for hop, (step, ways) in enumerate(hops):
-            gate = after(gates[max(hop - 2, 0)] if hop > 2 else gates[-1], delta)
-            totals = [term(by * step, i, gate) for i, by in ways]
-            for at, (i, by) in enumerate(ways):
+            totals = []
+            for i, by in ways:
+                total = term(by * step, i, source)
                 if (i, by) in arrived:
-                    totals[at], before = lax.optimization_barrier((totals[at], arrived[i, by]))
-                    totals[at] = totals[at] + before.astype(jnp.float32)
-            totals = [total.astype(jnp.bfloat16) for total in totals]
+                    before = after(previous, arrived[i, by])
+                    total = total + before.astype(jnp.float32)
+                totals.append(total.astype(jnp.bfloat16))
             if hop == len(hops) - 1:
                 totals = after(copied, totals)
             for (i, by), total in zip(ways, totals):
                 arrived[i, by] = along_ring(total, by)
-            gates.append(totals if hop < 2 else [arrived[way] for way in ways])
+            previous = totals
             if hop == 0:
-                first_hop = [arrived[way] for way in ways]
-                weights = after(first_hop, weights)
+                source = after(totals, delta)
+                late, weights = after(arrived[0, 1], (delta, weights))
                 copied = passed_on(weights)
-            if hop == 1:
-                second_hop = [arrived[way] for way in ways]
-            if hop == 2:
-                gates[1:3] = [first_hop, second_hop]
-        late = after(gates[-3], delta)
+            else:
+                source = late
         owns = [term(0, i, late) for i in range(2)]
         arrived[1, 1] = after(owns, arrived[1, 1])
         arrived[0, -1] = after(owns, arrived[0, -1])

time: 125 us -> 117 us (0.936)
  waiting for transfers between devices: 49.3 us -> 41.2 us
    ppermute x28, waiting for transfers between devices: 39.2 us -> 31.1 us  [along_ring(): return lax.ppermute(block, 'chip', pairs)]
  transfers between devices with their start and end apart: 39 -> 39, of which waited for: 20 -> 21; matrix products, arithmetic and copies ran while one was open for 14% -> 16% of each run, Pallas kernels for 6% -> 6%
where the time goes in v18:
time: 117 us; the launch traced here: 116 us
  waiting for transfers between devices  41.2 us (35%)
  starting transfers between devices  40.5 us (35%)
  matrix products  18.7 us (16%)
  Pallas kernels  7.18 us (6%)
  local copies, waits for them, and re-layouts  5.08 us (4%)
  other arithmetic  3.23 us (3%)
    ppermute x28, starting transfers between devices, along_ring(): return lax.ppermute(block, 'chip', pairs)  32.9 us
    ppermute x28, waiting for transfers between devices, along_ring(): return lax.ppermute(block, 'chip', pairs)  31.1 us
    dot_general x16, matrix products, term(): lax.dot_general(columns(offset, i), delta, (((0,), (0,)), ((), ())), pref...  9.32 us
    dot_general x16, matrix products, product(): jnp.dot(columns(offset, i), block, preferred_element_type=jnp.float32)  7.77 us
    ppermute x4, waiting for transfers between devices, slab_blocks(): kept.append(lax.ppermute(stored, ('grp', 'chip', 'core'), pairs))  7.31 us
    pallas_call x2, Pallas kernels, normalize(): pl.pallas_call(functools.partial(normalize_kernel, 16), grid=(seqs,), in_...  7.18 us
    ppermute x4, starting transfers between devices, slab_blocks(): kept.append(lax.ppermute(stored, ('grp', 'chip', 'core'), pairs))  5.16 us
    unnamed x11, local copies, waits for them, and re-layouts  3.31 us
  transfers between devices with their start and end apart: 39, of which 21 were waited for; matrix products, arithmetic and copies ran while one was open for 16% of the time, Pallas kernels for 6%

profile of v18, /device:TPU:0, one launch (start us, length us, event | category | flops | bytes accessed | tf_op | source)
XLA Modules:
  0.0 116.4 jit_solution(11323148778038584509)
XLA Ops:
  2.1 3.0 %collective-permute-start.2 = (bf16[256,512]{1,0:T(8,128)(2,1)S(1)}, bf16[256,512]{1,0:T(8,128)(2,1)S(1)}, u32[]{:S(2)}, u32[]{:S(2)}) collective-permute-start(bf16[256,512]{1,0:T(8,128)(2,1)S(1)} %get-tuple-element.115), channel_id=1, source_target_pairs={{0,4},{4,8},{8,12},{12,14},{14,10},{10,6},{6,2},{2,0},{1,5},{5,9},... | collective-permute-start | bytes 786440 | tf_op jit(solution)/shard_map/ppermute | solution.py:32
  6.1 2.9 %collective-permute-start.5 = (bf16[256,512]{1,0:T(8,128)(2,1)S(1)}, bf16[256,512]{1,0:T(8,128)(2,1)S(1)}, u32[]{:S(2)}, u32[]{:S(2)}) collective-permute-start(bf16[256,512]{1,0:T(8,128)(2,1)S(1)} %collective-permute-done.1), channel_id=1, source_target_pairs={{0,2},{4,0},{8,4},{12,8},{14,12},{10,14},{6,10},{2,6},{1,3},{5,1},... | collective-permute-start | bytes 786440 | tf_op jit(solution)/shard_map/ppermute | solution.py:32
  9.1 2.7 %collective-permute-done.2 = bf16[256,512]{1,0:T(8,128)(2,1)S(1)} collective-permute-done((bf16[256,512]{1,0:T(8,128)(2,1)S(1)}, bf16[256,512]{1,0:T(8,128)(2,1)S(1)}, u32[]{:S(2)}, u32[]{:S(2)}) %collective-permute-start.2) | collective-permute-done | bytes 262176 | tf_op jit(solution)/shard_map/ppermute | solution.py:32
  11.8 2.5 %collective-permute-start.7 = (bf16[256,512]{1,0:T(8,128)(2,1)S(1)}, bf16[256,512]{1,0:T(8,128)(2,1)S(1)}, u32[]{:S(2)}, u32[]{:S(2)}) collective-permute-start(bf16[256,512]{1,0:T(8,128)(2,1)S(1)} %collective-permute-done.2), channel_id=1, source_target_pairs={{0,4},{4,8},{8,12},{12,14},{14,10},{10,6},{6,2},{2,0},{1,5},{5,9},... | collective-permute-start | bytes 786440 | tf_op jit(solution)/shard_map/ppermute | solution.py:32
  15.0 1.9 %copy-done = bf16[1,3,128,4096]{3,2,1,0:T(8,128)(2,1)S(1)} copy-done((bf16[1,3,128,4096]{3,2,1,0:T(8,128)(2,1)S(1)}, bf16[1,3,128,4096]{3,2,1,0:T(8,128)(2,1)}, u32[]{:S(2)}) %copy-start) | copy-done | bytes 3145752
  17.6 3.6 %shard_map.64.refs_0_ = bf16[768,4096]{1,0:T(8,128)(2,1)S(1)} custom-call(bf16[3,128,4096]{2,1,0:T(8,128)(2,1)S(1)} %bitcast.54, f32[1,4096]{1,0:T(1,128)S(1)} %bitcast.55), custom_call_target="tpu_custom_call" | custom-call | flops 9437184 | bytes 6291456 | tf_op jit(solution)/shard_map/pallas_call | solution.py:99
  21.2 2.1 %collective-permute-start.9 = (bf16[256,512]{1,0:T(8,128)(2,1)S(1)}, bf16[256,512]{1,0:T(8,128)(2,1)S(1)}, u32[]{:S(2)}, u32[]{:S(2)}) collective-permute-start(bf16[256,512]{1,0:T(8,128)(2,1)S(1)} %collective-permute-done.4), channel_id=1, source_target_pairs={{0,4},{4,8},{8,12},{12,14},{14,10},{10,6},{6,2},{2,0},{1,5},{5,9},... | collective-permute-start | bytes 786440 | tf_op jit(solution)/shard_map/ppermute | solution.py:32
  23.4 2.1 %collective-permute-start.11 = (bf16[256,512]{1,0:T(8,128)(2,1)S(1)}, bf16[256,512]{1,0:T(8,128)(2,1)S(1)}, u32[]{:S(2)}, u32[]{:S(2)}) collective-permute-start(bf16[256,512]{1,0:T(8,128)(2,1)S(1)} %collective-permute-done.7), channel_id=1, source_target_pairs={{0,4},{4,8},{8,12},{12,14},{14,10},{10,6},{6,2},{2,0},{1,5},{5,9},... | collective-permute-start | bytes 786440 | tf_op jit(solution)/shard_map/ppermute | solution.py:32
  25.5 3.6 %shard_map.65 = bf16[768,4096]{1,0:T(8,128)(2,1)S(1)} custom-call(bf16[3,128,4096]{2,1,0:T(8,128)(2,1)S(1)} %collective-permute-done.states_ref, f32[1,4096]{1,0:T(1,128)S(1)} %bitcast.56, bf16[768,4096]{1,0:T(8,128)(2,1)S(1)} %shard_map.64.refs_0_), custom_call_target="tpu_custom_call", output_to_operand_aliasing={{}: (2, {})} | custom-call | flops 9437184 | bytes 6291456 | tf_op jit(solution)/shard_map/pallas_call | solution.py:99
  32.6 2.1 %collective-permute-start.13 = (bf16[256,512]{1,0:T(8,128)(2,1)S(1)}, bf16[256,512]{1,0:T(8,128)(2,1)S(1)}, u32[]{:S(2)}, u32[]{:S(2)}) collective-permute-start(bf16[256,512]{1,0:T(8,128)(2,1)S(1)} %collective-permute-done.9), channel_id=1, source_target_pairs={{0,4},{4,8},{8,12},{12,14},{14,10},{10,6},{6,2},{2,0},{1,5},{5,9},... | collective-permute-start | bytes 786440 | tf_op jit(solution)/shard_map/ppermute | solution.py:32
  34.7 2.0 %collective-permute-start.15 = (bf16[256,512]{1,0:T(8,128)(2,1)S(1)}, bf16[256,512]{1,0:T(8,128)(2,1)S(1)}, u32[]{:S(2)}, u32[]{:S(2)}) collective-permute-start(bf16[256,512]{1,0:T(8,128)(2,1)S(1)} %collective-permute-done.11), channel_id=1, source_target_pairs={{0,4},{4,8},{8,12},{12,14},{14,10},{10,6},{6,2},{2,0},{1,5},{5,9},... | collective-permute-start | bytes 786440 | tf_op jit(solution)/shard_map/ppermute | solution.py:32
  39.7 3.3 %collective-permute-done.14 = bf16[256,512]{1,0:T(8,128)(2,1)S(1)} collective-permute-done((bf16[256,512]{1,0:T(8,128)(2,1)S(1)}, bf16[256,512]{1,0:T(8,128)(2,1)S(1)}, u32[]{:S(2)}, u32[]{:S(2)}) %collective-permute-start.14) | collective-permute-done | bytes 262176 | tf_op jit(solution)/shard_map/ppermute | solution.py:32
  44.2 2.9 %collective-permute-done.15 = bf16[256,512]{1,0:T(8,128)(2,1)S(1)} collective-permute-done((bf16[256,512]{1,0:T(8,128)(2,1)S(1)}, bf16[256,512]{1,0:T(8,128)(2,1)S(1)}, u32[]{:S(2)}, u32[]{:S(2)}) %collective-permute-start.15) | collective-permute-done | bytes 262176 | tf_op jit(solution)/shard_map/ppermute | solution.py:32
  47.5 3.0 %collective-permute-done.16 = bf16[256,512]{1,0:T(8,128)(2,1)S(1)} collective-permute-done((bf16[256,512]{1,0:T(8,128)(2,1)S(1)}, bf16[256,512]{1,0:T(8,128)(2,1)S(1)}, u32[]{:S(2)}, u32[]{:S(2)}) %collective-permute-start.16) | collective-permute-done | bytes 262176 | tf_op jit(solution)/shard_map/ppermute | solution.py:32
  59.2 2.3 %collective-permute-done.19 = bf16[6,1024]{1,0:T(8,128)(2,1)S(1)} collective-permute-done((bf16[6,1024]{1,0:T(8,128)(2,1)S(1)}, bf16[6,1024]{1,0:T(8,128)(2,1)S(1)}, u32[]{:S(2)}, u32[]{:S(2)}) %collective-permute-start.19) | collective-permute-done | bytes 12320 | tf_op jit(solution)/shard_map/ppermute | solution.py:64
  61.5 2.3 %collective-permute-done.20 = bf16[6,1024]{1,0:T(8,128)(2,1)S(1)} collective-permute-done((bf16[6,1024]{1,0:T(8,128)(2,1)S(1)}, bf16[6,1024]{1,0:T(8,128)(2,1)S(1)}, u32[]{:S(2)}, u32[]{:S(2)}) %collective-permute-start.20) | collective-permute-done | bytes 12320 | tf_op jit(solution)/shard_map/ppermute | solution.py:64
  63.8 2.3 %collective-permute-done.21 = bf16[6,1024]{1,0:T(8,128)(2,1)S(1)} collective-permute-done((bf16[6,1024]{1,0:T(8,128)(2,1)S(1)}, bf16[6,1024]{1,0:T(8,128)(2,1)S(1)}, u32[]{:S(2)}, u32[]{:S(2)}) %collective-permute-start.21) | collective-permute-done | bytes 12320 | tf_op jit(solution)/shard_map/ppermute | solution.py:64
  70.4 1.5 %collective-permute-start.23 = (bf16[256,512]{1,0:T(8,128)(2,1)S(1)}, bf16[256,512]{1,0:T(8,128)(2,1)S(1)}, u32[]{:S(2)}, u32[]{:S(2)}) collective-permute-start(bf16[256,512]{1,0:T(8,128)(2,1)S(1)} %convolution_convert_fusion.3), channel_id=1, source_target_pairs={{0,4},{4,8},{8,12},{12,14},{14,10},{10,6},{6,2},{2,0},{1,5},{5,9},... | collective-permute-start | bytes 786440 | tf_op jit(solution)/shard_map/ppermute | solution.py:32
  73.7 1.7 %collective-permute-start.26 = (bf16[256,512]{1,0:T(8,128)(2,1)S(1)}, bf16[256,512]{1,0:T(8,128)(2,1)S(1)}, u32[]{:S(2)}, u32[]{:S(2)}) collective-permute-start(bf16[256,512]{1,0:T(8,128)(2,1)S(1)} %convolution_convert_fusion.1), channel_id=1, source_target_pairs={{0,4},{4,8},{8,12},{12,14},{14,10},{10,6},{6,2},{2,0},{1,5},{5,9},... | collective-permute-start | bytes 786440 | tf_op jit(solution)/shard_map/ppermute | solution.py:32
  75.4 3.7 %collective-permute-done.25 = bf16[256,512]{1,0:T(8,128)(2,1)S(1)} collective-permute-done((bf16[256,512]{1,0:T(8,128)(2,1)S(1)}, bf16[256,512]{1,0:T(8,128)(2,1)S(1)}, u32[]{:S(2)}, u32[]{:S(2)}) %collective-permute-start.25) | collective-permute-done | bytes 262176 | tf_op jit(solution)/shard_map/ppermute | solution.py:32
  82.9 1.8 %collective-permute-done.27 = bf16[256,512]{1,0:T(8,128)(2,1)S(1)} collective-permute-done((bf16[256,512]{1,0:T(8,128)(2,1)S(1)}, bf16[256,512]{1,0:T(8,128)(2,1)S(1)}, u32[]{:S(2)}, u32[]{:S(2)}) %collective-permute-start.27) | collective-permute-done | bytes 262176 | tf_op jit(solution)/shard_map/ppermute | solution.py:32
  85.9 1.5 %collective-permute-start.30 = (bf16[256,512]{1,0:T(8,128)(2,1)S(1)}, bf16[256,512]{1,0:T(8,128)(2,1)S(1)}, u32[]{:S(2)}, u32[]{:S(2)}) collective-permute-start(bf16[256,512]{1,0:T(8,128)(2,1)S(1)} %fusion.5), channel_id=1, source_target_pairs={{0,4},{4,8},{8,12},{12,14},{14,10},{10,6},{6,2},{2,0},{1,5},{5,9},... | collective-permute-start | bytes 786440 | tf_op jit(solution)/shard_map/ppermute | solution.py:32
  88.0 1.5 %collective-permute-start.24 = (bf16[256,1024]{1,0:T(8,128)(2,1)S(1)}, bf16[256,1024]{1,0:T(8,128)(2,1)S(1)}, u32[]{:S(2)}, u32[]{:S(2)}) collective-permute-start(bf16[256,1024]{1,0:T(8,128)(2,1)S(1)} %convert_element_type.163), channel_id=1, source_target_pairs={{0,16},{1,17},{2,18},{3,19},{4,20},{5,21},{6,22},{7,23},{8,24},{9,... | collective-permute-start | bytes 1572872 | tf_op jit(solution)/shard_map/ppermute | solution.py:40
  91.5 2.0 %collective-permute-start.33 = (bf16[256,512]{1,0:T(8,128)(2,1)S(1)}, bf16[256,512]{1,0:T(8,128)(2,1)S(1)}, u32[]{:S(2)}, u32[]{:S(2)}) collective-permute-start(bf16[256,512]{1,0:T(8,128)(2,1)S(1)} %fusion.9), channel_id=1, source_target_pairs={{0,2},{4,0},{8,4},{12,8},{14,12},{10,14},{6,10},{2,6},{1,3},{5,1},... | collective-permute-start | bytes 786440 | tf_op jit(solution)/shard_map/ppermute | solution.py:32
  93.6 2.9 %collective-permute-done.30 = bf16[256,512]{1,0:T(8,128)(2,1)S(1)} collective-permute-done((bf16[256,512]{1,0:T(8,128)(2,1)S(1)}, bf16[256,512]{1,0:T(8,128)(2,1)S(1)}, u32[]{:S(2)}, u32[]{:S(2)}) %collective-permute-start.30) | collective-permute-done | bytes 262176 | tf_op jit(solution)/shard_map/ppermute | solution.py:32
  97.1 1.6 %collective-permute-start.36 = (bf16[256,512]{1,0:T(8,128)(2,1)S(1)}, bf16[256,512]{1,0:T(8,128)(2,1)S(1)}, u32[]{:S(2)}, u32[]{:S(2)}) collective-permute-start(bf16[256,512]{1,0:T(8,128)(2,1)S(1)} %fusion.3), channel_id=1, source_target_pairs={{0,4},{4,8},{8,12},{12,14},{14,10},{10,6},{6,2},{2,0},{1,5},{5,9},... | collective-permute-start | bytes 786440 | tf_op jit(solution)/shard_map/ppermute | solution.py:32
  99.2 1.5 %collective-permute-done.33 = bf16[256,512]{1,0:T(8,128)(2,1)S(1)} collective-permute-done((bf16[256,512]{1,0:T(8,128)(2,1)S(1)}, bf16[256,512]{1,0:T(8,128)(2,1)S(1)}, u32[]{:S(2)}, u32[]{:S(2)}) %collective-permute-start.33) | collective-permute-done | bytes 262176 | tf_op jit(solution)/shard_map/ppermute | solution.py:32
  100.8 2.0 %collective-permute-done.32 = bf16[256,512]{1,0:T(8,128)(2,1)S(1)} collective-permute-done((bf16[256,512]{1,0:T(8,128)(2,1)S(1)}, bf16[256,512]{1,0:T(8,128)(2,1)S(1)}, u32[]{:S(2)}, u32[]{:S(2)}) %collective-permute-start.32) | collective-permute-done | bytes 262176 | tf_op jit(solution)/shard_map/ppermute | solution.py:32
  103.9 1.6 %collective-permute-start.37 = (bf16[256,512]{1,0:T(8,128)(2,1)S(1)}, bf16[256,512]{1,0:T(8,128)(2,1)S(1)}, u32[]{:S(2)}, u32[]{:S(2)}) collective-permute-start(bf16[256,512]{1,0:T(8,128)(2,1)S(1)} %fusion.11), channel_id=1, source_target_pairs={{0,2},{4,0},{8,4},{12,8},{14,12},{10,14},{6,10},{2,6},{1,3},{5,1},... | collective-permute-start | bytes 786440 | tf_op jit(solution)/shard_map/ppermute | solution.py:32
  106.7 1.7 %collective-permute-start.35 = (bf16[256,512]{1,0:T(8,128)(2,1)S(1)}, bf16[256,512]{1,0:T(8,128)(2,1)S(1)}, u32[]{:S(2)}, u32[]{:S(2)}) collective-permute-start(bf16[256,512]{1,0:T(8,128)(2,1)S(1)} %fusion.10), channel_id=1, source_target_pairs={{0,2},{4,0},{8,4},{12,8},{14,12},{10,14},{6,10},{2,6},{1,3},{5,1},... | collective-permute-start | bytes 786440 | tf_op jit(solution)/shard_map/ppermute | solution.py:32
  108.8 3.2 %collective-permute-done.37 = bf16[256,512]{1,0:T(8,128)(2,1)S(1)} collective-permute-done((bf16[256,512]{1,0:T(8,128)(2,1)S(1)}, bf16[256,512]{1,0:T(8,128)(2,1)S(1)}, u32[]{:S(2)}, u32[]{:S(2)}) %collective-permute-start.37) | collective-permute-done | bytes 262176 | tf_op jit(solution)/shard_map/ppermute | solution.py:32
  112.2 2.6 %collective-permute-done.35 = bf16[256,512]{1,0:T(8,128)(2,1)S(1)} collective-permute-done((bf16[256,512]{1,0:T(8,128)(2,1)S(1)}, bf16[256,512]{1,0:T(8,128)(2,1)S(1)}, u32[]{:S(2)}, u32[]{:S(2)}) %collective-permute-start.35) | collective-permute-done | bytes 262176 | tf_op jit(solution)/shard_map/ppermute | solution.py:32
  (128 shorter events, 40.4 us)
Async XLA Ops:
  0.0 25.5 %collective-permute-start = (bf16[3,128,4096]{2,1,0:T(8,128)(2,1)}, bf16[3,128,4096]{2,1,0:T(8,128)(2,1)S(1)}, u32[]{:S(2)}, u32[]{:S(2)}) collective-permute-start(bf16[3,128,4096]{2,1,0:T(8,128)(2,1)} %bitcast.53), channel_id=1, source_target_pairs={{0,1},{1,0},{2,3},{3,2},{4,5},{5,4},{6,7},{7,6},{8,9},{9,8},{10,11... | collective-permute-start | bytes 9437192 | tf_op jit(solution)/shard_map/ppermute | solution.py:52
  2.1 9.7 %collective-permute-start.2 = (bf16[256,512]{1,0:T(8,128)(2,1)S(1)}, bf16[256,512]{1,0:T(8,128)(2,1)S(1)}, u32[]{:S(2)}, u32[]{:S(2)}) collective-permute-start(bf16[256,512]{1,0:T(8,128)(2,1)S(1)} %get-tuple-element.115), channel_id=1, source_target_pairs={{0,4},{4,8},{8,12},{12,14},{14,10},{10,6},{6,2},{2,0},{1,5},{5,9},... | collective-permute-start | bytes 786440 | tf_op jit(solution)/shard_map/ppermute | solution.py:32
  5.1 9.2 %collective-permute-start.3 = (bf16[256,512]{1,0:T(8,128)(2,1)S(1)}, bf16[256,512]{1,0:T(8,128)(2,1)S(1)}, u32[]{:S(2)}, u32[]{:S(2)}) collective-permute-start(bf16[256,512]{1,0:T(8,128)(2,1)S(1)} %get-tuple-element.115), channel_id=1, source_target_pairs={{0,2},{4,0},{8,4},{12,8},{14,12},{10,14},{6,10},{2,6},{1,3},{5,1},... | collective-permute-start | bytes 786440 | tf_op jit(solution)/shard_map/ppermute | solution.py:32
  6.1 15.0 %collective-permute-start.5 = (bf16[256,512]{1,0:T(8,128)(2,1)S(1)}, bf16[256,512]{1,0:T(8,128)(2,1)S(1)}, u32[]{:S(2)}, u32[]{:S(2)}) collective-permute-start(bf16[256,512]{1,0:T(8,128)(2,1)S(1)} %collective-permute-done.1), channel_id=1, source_target_pairs={{0,2},{4,0},{8,4},{12,8},{14,12},{10,14},{6,10},{2,6},{1,3},{5,1},... | collective-permute-start | bytes 786440 | tf_op jit(solution)/shard_map/ppermute | solution.py:32
  9.0 12.2 %collective-permute-start.4 = (bf16[256,512]{1,0:T(8,128)(2,1)S(1)}, bf16[256,512]{1,0:T(8,128)(2,1)S(1)}, u32[]{:S(2)}, u32[]{:S(2)}) collective-permute-start(bf16[256,512]{1,0:T(8,128)(2,1)S(1)} %collective-permute-done.1), channel_id=1, source_target_pairs={{0,4},{4,8},{8,12},{12,14},{14,10},{10,6},{6,2},{2,0},{1,5},{5,9},... | collective-permute-start | bytes 786440 | tf_op jit(solution)/shard_map/ppermute | solution.py:32
  11.8 11.6 %collective-permute-start.7 = (bf16[256,512]{1,0:T(8,128)(2,1)S(1)}, bf16[256,512]{1,0:T(8,128)(2,1)S(1)}, u32[]{:S(2)}, u32[]{:S(2)}) collective-permute-start(bf16[256,512]{1,0:T(8,128)(2,1)S(1)} %collective-permute-done.2), channel_id=1, source_target_pairs={{0,4},{4,8},{8,12},{12,14},{14,10},{10,6},{6,2},{2,0},{1,5},{5,9},... | collective-permute-start | bytes 786440 | tf_op jit(solution)/shard_map/ppermute | solution.py:32
  14.3 11.2 %collective-permute-start.8 = (bf16[256,512]{1,0:T(8,128)(2,1)S(1)}, bf16[256,512]{1,0:T(8,128)(2,1)S(1)}, u32[]{:S(2)}, u32[]{:S(2)}) collective-permute-start(bf16[256,512]{1,0:T(8,128)(2,1)S(1)} %collective-permute-done.3), channel_id=1, source_target_pairs={{0,2},{4,0},{8,4},{12,8},{14,12},{10,14},{6,10},{2,6},{1,3},{5,1},... | collective-permute-start | bytes 786440 | tf_op jit(solution)/shard_map/ppermute | solution.py:32
  21.2 11.4 %collective-permute-start.9 = (bf16[256,512]{1,0:T(8,128)(2,1)S(1)}, bf16[256,512]{1,0:T(8,128)(2,1)S(1)}, u32[]{:S(2)}, u32[]{:S(2)}) collective-permute-start(bf16[256,512]{1,0:T(8,128)(2,1)S(1)} %collective-permute-done.4), channel_id=1, source_target_pairs={{0,4},{4,8},{8,12},{12,14},{14,10},{10,6},{6,2},{2,0},{1,5},{5,9},... | collective-permute-start | bytes 786440 | tf_op jit(solution)/shard_map/ppermute | solution.py:32
  23.3 11.3 %collective-permute-start.10 = (bf16[256,512]{1,0:T(8,128)(2,1)S(1)}, bf16[256,512]{1,0:T(8,128)(2,1)S(1)}, u32[]{:S(2)}, u32[]{:S(2)}) collective-permute-start(bf16[256,512]{1,0:T(8,128)(2,1)S(1)} %collective-permute-done.5), channel_id=1, source_target_pairs={{0,2},{4,0},{8,4},{12,8},{14,12},{10,14},{6,10},{2,6},{1,3},{5,1},... | collective-permute-start | bytes 786440 | tf_op jit(solution)/shard_map/ppermute | solution.py:32
  23.4 11.3 %collective-permute-start.11 = (bf16[256,512]{1,0:T(8,128)(2,1)S(1)}, bf16[256,512]{1,0:T(8,128)(2,1)S(1)}, u32[]{:S(2)}, u32[]{:S(2)}) collective-permute-start(bf16[256,512]{1,0:T(8,128)(2,1)S(1)} %collective-permute-done.7), channel_id=1, source_target_pairs={{0,4},{4,8},{8,12},{12,14},{14,10},{10,6},{6,2},{2,0},{1,5},{5,9},... | collective-permute-start | bytes 786440 | tf_op jit(solution)/shard_map/ppermute | solution.py:32
  25.5 25.5 %collective-permute-start.12 = (bf16[256,512]{1,0:T(8,128)(2,1)S(1)}, bf16[256,512]{1,0:T(8,128)(2,1)S(1)}, u32[]{:S(2)}, u32[]{:S(2)}) collective-permute-start(bf16[256,512]{1,0:T(8,128)(2,1)S(1)} %collective-permute-done.8), channel_id=1, source_target_pairs={{0,2},{4,0},{8,4},{12,8},{14,12},{10,14},{6,10},{2,6},{1,3},{5,1},... | collective-permute-start | bytes 786440 | tf_op jit(solution)/shard_map/ppermute | solution.py:32
  32.5 6.7 %collective-permute-start.6 = (s32[3,224]{1,0:T(4,128)S(1)}, s32[3,224]{1,0:T(4,128)S(1)}, u32[]{:S(2)}, u32[]{:S(2)}) collective-permute-start(s32[3,224]{1,0:T(4,128)S(1)} %pad_add_fusion.1), channel_id=1, source_target_pairs={{0,1},{1,0},{2,3},{3,2},{4,5},{5,4},{6,7},{7,6},{8,9},{9,8},{10,11... | collective-permute-start | bytes 8072 | tf_op jit(solution)/shard_map/ppermute | solution.py:52
  32.6 11.2 %collective-permute-start.13 = (bf16[256,512]{1,0:T(8,128)(2,1)S(1)}, bf16[256,512]{1,0:T(8,128)(2,1)S(1)}, u32[]{:S(2)}, u32[]{:S(2)}) collective-permute-start(bf16[256,512]{1,0:T(8,128)(2,1)S(1)} %collective-permute-done.9), channel_id=1, source_target_pairs={{0,4},{4,8},{8,12},{12,14},{14,10},{10,6},{6,2},{2,0},{1,5},{5,9},... | collective-permute-start | bytes 786440 | tf_op jit(solution)/shard_map/ppermute | solution.py:32
  34.6 8.4 %collective-permute-start.14 = (bf16[256,512]{1,0:T(8,128)(2,1)S(1)}, bf16[256,512]{1,0:T(8,128)(2,1)S(1)}, u32[]{:S(2)}, u32[]{:S(2)}) collective-permute-start(bf16[256,512]{1,0:T(8,128)(2,1)S(1)} %collective-permute-done.10), channel_id=1, source_target_pairs={{0,2},{4,0},{8,4},{12,8},{14,12},{10,14},{6,10},{2,6},{1,3},{5,1},... | collective-permute-start | bytes 786440 | tf_op jit(solution)/shard_map/ppermute | solution.py:32
  34.7 12.3 %collective-permute-start.15 = (bf16[256,512]{1,0:T(8,128)(2,1)S(1)}, bf16[256,512]{1,0:T(8,128)(2,1)S(1)}, u32[]{:S(2)}, u32[]{:S(2)}) collective-permute-start(bf16[256,512]{1,0:T(8,128)(2,1)S(1)} %collective-permute-done.11), channel_id=1, source_target_pairs={{0,4},{4,8},{8,12},{12,14},{14,10},{10,6},{6,2},{2,0},{1,5},{5,9},... | collective-permute-start | bytes 786440 | tf_op jit(solution)/shard_map/ppermute | solution.py:32
  43.0 7.5 %collective-permute-start.16 = (bf16[256,512]{1,0:T(8,128)(2,1)S(1)}, bf16[256,512]{1,0:T(8,128)(2,1)S(1)}, u32[]{:S(2)}, u32[]{:S(2)}) collective-permute-start(bf16[256,512]{1,0:T(8,128)(2,1)S(1)} %collective-permute-done.14), channel_id=1, source_target_pairs={{0,2},{4,0},{8,4},{12,8},{14,12},{10,14},{6,10},{2,6},{1,3},{5,1},... | collective-permute-start | bytes 786440 | tf_op jit(solution)/shard_map/ppermute | solution.py:32
  56.2 7.7 %collective-permute-start.20 = (bf16[6,1024]{1,0:T(8,128)(2,1)S(1)}, bf16[6,1024]{1,0:T(8,128)(2,1)S(1)}, u32[]{:S(2)}, u32[]{:S(2)}) collective-permute-start(bf16[6,1024]{1,0:T(8,128)(2,1)S(1)} %maximum_select_fusion.2), channel_id=1, source_target_pairs={{24,0},{23,1},{28,4},{19,5},{30,8},{17,9},{26,12},{21,13},{22,14},... | collective-permute-start | bytes 36872 | tf_op jit(solution)/shard_map/ppermute | solution.py:64
  57.5 8.6 %collective-permute-start.21 = (bf16[6,1024]{1,0:T(8,128)(2,1)S(1)}, bf16[6,1024]{1,0:T(8,128)(2,1)S(1)}, u32[]{:S(2)}, u32[]{:S(2)}) collective-permute-start(bf16[6,1024]{1,0:T(8,128)(2,1)S(1)} %maximum_select_fusion.2), channel_id=1, source_target_pairs={{28,0},{19,1},{30,4},{17,5},{26,8},{21,9},{22,12},{25,13},{18,14},... | collective-permute-start | bytes 36872 | tf_op jit(solution)/shard_map/ppermute | solution.py:64
  69.9 9.2 %collective-permute-start.25 = (bf16[256,512]{1,0:T(8,128)(2,1)S(1)}, bf16[256,512]{1,0:T(8,128)(2,1)S(1)}, u32[]{:S(2)}, u32[]{:S(2)}) collective-permute-start(bf16[256,512]{1,0:T(8,128)(2,1)S(1)} %convolution_convert_fusion.2), channel_id=1, source_target_pairs={{0,2},{4,0},{8,4},{12,8},{14,12},{10,14},{6,10},{2,6},{1,3},{5,1},... | collective-permute-start | bytes 786440 | tf_op jit(solution)/shard_map/ppermute | solution.py:32
  70.4 9.2 %collective-permute-start.23 = (bf16[256,512]{1,0:T(8,128)(2,1)S(1)}, bf16[256,512]{1,0:T(8,128)(2,1)S(1)}, u32[]{:S(2)}, u32[]{:S(2)}) collective-permute-start(bf16[256,512]{1,0:T(8,128)(2,1)S(1)} %convolution_convert_fusion.3), channel_id=1, source_target_pairs={{0,4},{4,8},{8,12},{12,14},{14,10},{10,6},{6,2},{2,0},{1,5},{5,9},... | collective-permute-start | bytes 786440 | tf_op jit(solution)/shard_map/ppermute | solution.py:32
  72.5 12.2 %collective-permute-start.27 = (bf16[256,512]{1,0:T(8,128)(2,1)S(1)}, bf16[256,512]{1,0:T(8,128)(2,1)S(1)}, u32[]{:S(2)}, u32[]{:S(2)}) collective-permute-start(bf16[256,512]{1,0:T(8,128)(2,1)S(1)} %convolution_convert_fusion), channel_id=1, source_target_pairs={{0,2},{4,0},{8,4},{12,8},{14,12},{10,14},{6,10},{2,6},{1,3},{5,1},... | collective-permute-start | bytes 786440 | tf_op jit(solution)/shard_map/ppermute | solution.py:32
  73.7 11.6 %collective-permute-start.26 = (bf16[256,512]{1,0:T(8,128)(2,1)S(1)}, bf16[256,512]{1,0:T(8,128)(2,1)S(1)}, u32[]{:S(2)}, u32[]{:S(2)}) collective-permute-start(bf16[256,512]{1,0:T(8,128)(2,1)S(1)} %convolution_convert_fusion.1), channel_id=1, source_target_pairs={{0,4},{4,8},{8,12},{12,14},{14,10},{10,6},{6,2},{2,0},{1,5},{5,9},... | collective-permute-start | bytes 786440 | tf_op jit(solution)/shard_map/ppermute | solution.py:32
  80.8 9.5 %collective-permute-start.29 = (bf16[256,512]{1,0:T(8,128)(2,1)S(1)}, bf16[256,512]{1,0:T(8,128)(2,1)S(1)}, u32[]{:S(2)}, u32[]{:S(2)}) collective-permute-start(bf16[256,512]{1,0:T(8,128)(2,1)S(1)} %fusion.7), channel_id=1, source_target_pairs={{0,2},{4,0},{8,4},{12,8},{14,12},{10,14},{6,10},{2,6},{1,3},{5,1},... | collective-permute-start | bytes 786440 | tf_op jit(solution)/shard_map/ppermute | solution.py:32
  81.5 9.4 %collective-permute-start.28 = (bf16[256,512]{1,0:T(8,128)(2,1)S(1)}, bf16[256,512]{1,0:T(8,128)(2,1)S(1)}, u32[]{:S(2)}, u32[]{:S(2)}) collective-permute-start(bf16[256,512]{1,0:T(8,128)(2,1)S(1)} %fusion.6), channel_id=1, source_target_pairs={{0,4},{4,8},{8,12},{12,14},{14,10},{10,6},{6,2},{2,0},{1,5},{5,9},... | collective-permute-start | bytes 786440 | tf_op jit(solution)/shard_map/ppermute | solution.py:32
  85.9 10.6 %collective-permute-start.30 = (bf16[256,512]{1,0:T(8,128)(2,1)S(1)}, bf16[256,512]{1,0:T(8,128)(2,1)S(1)}, u32[]{:S(2)}, u32[]{:S(2)}) collective-permute-start(bf16[256,512]{1,0:T(8,128)(2,1)S(1)} %fusion.5), channel_id=1, source_target_pairs={{0,4},{4,8},{8,12},{12,14},{14,10},{10,6},{6,2},{2,0},{1,5},{5,9},... | collective-permute-start | bytes 786440 | tf_op jit(solution)/shard_map/ppermute | solution.py:32
  87.4 11.2 %collective-permute-start.31 = (bf16[256,512]{1,0:T(8,128)(2,1)S(1)}, bf16[256,512]{1,0:T(8,128)(2,1)S(1)}, u32[]{:S(2)}, u32[]{:S(2)}) collective-permute-start(bf16[256,512]{1,0:T(8,128)(2,1)S(1)} %fusion.8), channel_id=1, source_target_pairs={{0,2},{4,0},{8,4},{12,8},{14,12},{10,14},{6,10},{2,6},{1,3},{5,1},... | collective-permute-start | bytes 786440 | tf_op jit(solution)/shard_map/ppermute | solution.py:32
  88.0 15.9 %collective-permute-start.24 = (bf16[256,1024]{1,0:T(8,128)(2,1)S(1)}, bf16[256,1024]{1,0:T(8,128)(2,1)S(1)}, u32[]{:S(2)}, u32[]{:S(2)}) collective-permute-start(bf16[256,1024]{1,0:T(8,128)(2,1)S(1)} %convert_element_type.163), channel_id=1, source_target_pairs={{0,16},{1,17},{2,18},{3,19},{4,20},{5,21},{6,22},{7,23},{8,24},{9,... | collective-permute-start | bytes 1572872 | tf_op jit(solution)/shard_map/ppermute | solution.py:40
  91.5 9.3 %collective-permute-start.33 = (bf16[256,512]{1,0:T(8,128)(2,1)S(1)}, bf16[256,512]{1,0:T(8,128)(2,1)S(1)}, u32[]{:S(2)}, u32[]{:S(2)}) collective-permute-start(bf16[256,512]{1,0:T(8,128)(2,1)S(1)} %fusion.9), channel_id=1, source_target_pairs={{0,2},{4,0},{8,4},{12,8},{14,12},{10,14},{6,10},{2,6},{1,3},{5,1},... | collective-permute-start | bytes 786440 | tf_op jit(solution)/shard_map/ppermute | solution.py:32
  93.5 9.2 %collective-permute-start.32 = (bf16[256,512]{1,0:T(8,128)(2,1)S(1)}, bf16[256,512]{1,0:T(8,128)(2,1)S(1)}, u32[]{:S(2)}, u32[]{:S(2)}) collective-permute-start(bf16[256,512]{1,0:T(8,128)(2,1)S(1)} %fusion.4), channel_id=1, source_target_pairs={{0,4},{4,8},{8,12},{12,14},{14,10},{10,6},{6,2},{2,0},{1,5},{5,9},... | collective-permute-start | bytes 786440 | tf_op jit(solution)/shard_map/ppermute | solution.py:32
  97.1 11.4 %collective-permute-start.36 = (bf16[256,512]{1,0:T(8,128)(2,1)S(1)}, bf16[256,512]{1,0:T(8,128)(2,1)S(1)}, u32[]{:S(2)}, u32[]{:S(2)}) collective-permute-start(bf16[256,512]{1,0:T(8,128)(2,1)S(1)} %fusion.3), channel_id=1, source_target_pairs={{0,4},{4,8},{8,12},{12,14},{14,10},{10,6},{6,2},{2,0},{1,5},{5,9},... | collective-permute-start | bytes 786440 | tf_op jit(solution)/shard_map/ppermute | solution.py:32
  103.9 8.1 %collective-permute-start.37 = (bf16[256,512]{1,0:T(8,128)(2,1)S(1)}, bf16[256,512]{1,0:T(8,128)(2,1)S(1)}, u32[]{:S(2)}, u32[]{:S(2)}) collective-permute-start(bf16[256,512]{1,0:T(8,128)(2,1)S(1)} %fusion.11), channel_id=1, source_target_pairs={{0,2},{4,0},{8,4},{12,8},{14,12},{10,14},{6,10},{2,6},{1,3},{5,1},... | collective-permute-start | bytes 786440 | tf_op jit(solution)/shard_map/ppermute | solution.py:32
  106.7 8.1 %collective-permute-start.35 = (bf16[256,512]{1,0:T(8,128)(2,1)S(1)}, bf16[256,512]{1,0:T(8,128)(2,1)S(1)}, u32[]{:S(2)}, u32[]{:S(2)}) collective-permute-start(bf16[256,512]{1,0:T(8,128)(2,1)S(1)} %fusion.10), channel_id=1, source_target_pairs={{0,2},{4,0},{8,4},{12,8},{14,12},{10,14},{6,10},{2,6},{1,3},{5,1},... | collective-permute-start | bytes 786440 | tf_op jit(solution)/shard_map/ppermute | solution.py:32
  (12 other events, 42.0 us)

commit v19 on v18

--- a/solution.py
+++ b/solution.py
@@ -141,11 +141,14 @@
     sibling = from_sibling(given)
 
     other_states = from_sibling(states)
-    sent = [(0, 1), (0, -1), (1, 1), (1, -1)]
+    four, three = [(0, 1), (1, -1)], [(1, 1), (0, -1)]
     normed_own = normalize(states, gain, 0)
     normed = normalize(other_states, gain, 1, normed_own)
     if chips <= longest_ring:
-        moving = {(i, by): along_ring((own, sibling)[i], by) for i, by in sent}
+        held = [own, sibling, after(sibling, own)]
+        moving = {(i, by): along_ring(held[i], by) for i, by in four}
+        moving[1, 1] = along_ring(held[1], 1)
+        moving[0, -1] = along_ring(held[2], -1)
 
     def columns(offset, i):
         return cut(normed, 1, starts[offset, i], rows)
@@ -158,11 +161,11 @@
         sums = {}
         for step in range(1, chips // 2 + 1):
             last = step == chips // 2
-            for i, by in [(0, 1), (1, -1)] if last else sent:
+            for i, by in four if last else four + three:
                 if step > 1:
                     if last and step > 2:
-                        moving[i, by] = after(sums[1 + i], moving[i, by])
-                    elif step in (2, 3) and i == 1:
+                        moving[i, by] = after(sums[1], moving[i, by])
+                    elif step in (2, 3) and (i, by) in three:
                         moving[i, by] = after((normed_own, normed)[step - 2], moving[i, by])
                     moving[i, by] = along_ring(moving[i, by], by)
                 total = total + product(-by * step, i, moving[i, by])
@@ -246,7 +249,6 @@
         )
 
     if chips <= longest_ring:
-        four, three = [(0, 1), (1, -1)], [(1, 1), (0, -1)]
         hops = [(chips // 2, four)]
         for step in range(chips // 2 - 1, 0, -1):
             hops += [(step, three), (step, four)]

time: 117 us -> 119 us (1.017)
  starting transfers between devices: 40.5 us -> 42.7 us
    ppermute x28, starting transfers between devices: 32.9 us -> 35.1 us  [along_ring(): return lax.ppermute(block, 'chip', pairs)]
  transfers between devices with their start and end apart: 39 -> 39, of which waited for: 21 -> 24; matrix products, arithmetic and copies ran while one was open for 16% -> 16% of each run, Pallas kernels for 6% -> 6%
where the time goes in v19:
time: 119 us
  starting transfers between devices  42.7 us (36%)
  waiting for transfers between devices  41.3 us (35%)
  matrix products  18.5 us (16%)
  Pallas kernels  7.16 us (6%)
  local copies, waits for them, and re-layouts  5.08 us (4%)
  other arithmetic  3.22 us (3%)
    ppermute x28, starting transfers between devices, along_ring(): return lax.ppermute(block, 'chip', pairs)  35.1 us
    ppermute x28, waiting for transfers between devices, along_ring(): return lax.ppermute(block, 'chip', pairs)  30.2 us
    dot_general x16, matrix products, term(): lax.dot_general(columns(offset, i), delta, (((0,), (0,)), ((), ())), pref...  9.32 us
    ppermute x4, waiting for transfers between devices, slab_blocks(): kept.append(lax.ppermute(stored, ('grp', 'chip', 'core'), pairs))  8.26 us
    dot_general x16, matrix products, product(): jnp.dot(columns(offset, i), block, preferred_element_type=jnp.float32)  7.62 us
    pallas_call x2, Pallas kernels, normalize(): pl.pallas_call(functools.partial(normalize_kernel, 16), grid=(seqs,), in_...  7.16 us
    ppermute x4, starting transfers between devices, slab_blocks(): kept.append(lax.ppermute(stored, ('grp', 'chip', 'core'), pairs))  5.16 us
    unnamed x11, local copies, waits for them, and re-layouts  3.31 us
  transfers between devices with their start and end apart: 39, of which 24 were waited for; matrix products, arithmetic and copies ran while one was open for 16% of the time, Pallas kernels for 6%

profile of v19, /device:TPU:0, one launch (start us, length us, event | category | flops | bytes accessed | tf_op | source)
XLA Modules:
  0.0 118.5 jit_solution(10673045052857086023)
XLA Ops:
  2.1 3.0 %collective-permute-start.2 = (bf16[256,512]{1,0:T(8,128)(2,1)S(1)}, bf16[256,512]{1,0:T(8,128)(2,1)S(1)}, u32[]{:S(2)}, u32[]{:S(2)}) collective-permute-start(bf16[256,512]{1,0:T(8,128)(2,1)S(1)} %get-tuple-element.67), channel_id=1, source_target_pairs={{0,4},{4,8},{8,12},{12,14},{14,10},{10,6},{6,2},{2,0},{1,5},{5,9},... | collective-permute-start | bytes 786440 | tf_op jit(solution)/shard_map/ppermute | solution.py:32
  6.1 2.9 %collective-permute-start.3 = (bf16[256,512]{1,0:T(8,128)(2,1)S(1)}, bf16[256,512]{1,0:T(8,128)(2,1)S(1)}, u32[]{:S(2)}, u32[]{:S(2)}) collective-permute-start(bf16[256,512]{1,0:T(8,128)(2,1)S(1)} %collective-permute-done.1), channel_id=1, source_target_pairs={{0,2},{4,0},{8,4},{12,8},{14,12},{10,14},{6,10},{2,6},{1,3},{5,1},... | collective-permute-start | bytes 786440 | tf_op jit(solution)/shard_map/ppermute | solution.py:32
  9.0 1.6 %collective-permute-start.5 = (bf16[256,512]{1,0:T(8,128)(2,1)S(1)}, bf16[256,512]{1,0:T(8,128)(2,1)S(1)}, u32[]{:S(2)}, u32[]{:S(2)}) collective-permute-start(bf16[256,512]{1,0:T(8,128)(2,1)S(1)} %get-tuple-element.67), channel_id=1, source_target_pairs={{0,2},{4,0},{8,4},{12,8},{14,12},{10,14},{6,10},{2,6},{1,3},{5,1},... | collective-permute-start | bytes 786440 | tf_op jit(solution)/shard_map/ppermute | solution.py:32
  11.6 1.9 %collective-permute-start.7 = (bf16[256,512]{1,0:T(8,128)(2,1)S(1)}, bf16[256,512]{1,0:T(8,128)(2,1)S(1)}, u32[]{:S(2)}, u32[]{:S(2)}) collective-permute-start(bf16[256,512]{1,0:T(8,128)(2,1)S(1)} %collective-permute-done.2), channel_id=1, source_target_pairs={{0,4},{4,8},{8,12},{12,14},{14,10},{10,6},{6,2},{2,0},{1,5},{5,9},... | collective-permute-start | bytes 786440 | tf_op jit(solution)/shard_map/ppermute | solution.py:32
  13.4 2.7 %collective-permute-done.3 = bf16[256,512]{1,0:T(8,128)(2,1)S(1)} collective-permute-done((bf16[256,512]{1,0:T(8,128)(2,1)S(1)}, bf16[256,512]{1,0:T(8,128)(2,1)S(1)}, u32[]{:S(2)}, u32[]{:S(2)}) %collective-permute-start.3) | collective-permute-done | bytes 262176 | tf_op jit(solution)/shard_map/ppermute | solution.py:32
  16.1 2.0 %collective-permute-start.8 = (bf16[256,512]{1,0:T(8,128)(2,1)S(1)}, bf16[256,512]{1,0:T(8,128)(2,1)S(1)}, u32[]{:S(2)}, u32[]{:S(2)}) collective-permute-start(bf16[256,512]{1,0:T(8,128)(2,1)S(1)} %collective-permute-done.3), channel_id=1, source_target_pairs={{0,2},{4,0},{8,4},{12,8},{14,12},{10,14},{6,10},{2,6},{1,3},{5,1},... | collective-permute-start | bytes 786440 | tf_op jit(solution)/shard_map/ppermute | solution.py:32
  18.8 1.9 %copy-done = bf16[1,3,128,4096]{3,2,1,0:T(8,128)(2,1)S(1)} copy-done((bf16[1,3,128,4096]{3,2,1,0:T(8,128)(2,1)S(1)}, bf16[1,3,128,4096]{3,2,1,0:T(8,128)(2,1)}, u32[]{:S(2)}) %copy-start) | copy-done | bytes 3145752
  21.4 3.6 %shard_map.64.refs_0_ = bf16[768,4096]{1,0:T(8,128)(2,1)S(1)} custom-call(bf16[3,128,4096]{2,1,0:T(8,128)(2,1)S(1)} %bitcast.54, f32[1,4096]{1,0:T(1,128)S(1)} %bitcast.55), custom_call_target="tpu_custom_call" | custom-call | flops 9437184 | bytes 6291456 | tf_op jit(solution)/shard_map/pallas_call | solution.py:99
  25.1 1.6 %collective-permute-start.10 = (bf16[256,512]{1,0:T(8,128)(2,1)S(1)}, bf16[256,512]{1,0:T(8,128)(2,1)S(1)}, u32[]{:S(2)}, u32[]{:S(2)}) collective-permute-start(bf16[256,512]{1,0:T(8,128)(2,1)S(1)} %collective-permute-done.5), channel_id=1, source_target_pairs={{0,2},{4,0},{8,4},{12,8},{14,12},{10,14},{6,10},{2,6},{1,3},{5,1},... | collective-permute-start | bytes 786440 | tf_op jit(solution)/shard_map/ppermute | solution.py:32
  27.4 2.0 %collective-permute-start.12 = (bf16[256,512]{1,0:T(8,128)(2,1)S(1)}, bf16[256,512]{1,0:T(8,128)(2,1)S(1)}, u32[]{:S(2)}, u32[]{:S(2)}) collective-permute-start(bf16[256,512]{1,0:T(8,128)(2,1)S(1)} %collective-permute-done.8), channel_id=1, source_target_pairs={{0,2},{4,0},{8,4},{12,8},{14,12},{10,14},{6,10},{2,6},{1,3},{5,1},... | collective-permute-start | bytes 786440 | tf_op jit(solution)/shard_map/ppermute | solution.py:32
  29.4 3.6 %shard_map.65 = bf16[768,4096]{1,0:T(8,128)(2,1)S(1)} custom-call(bf16[3,128,4096]{2,1,0:T(8,128)(2,1)S(1)} %collective-permute-done.states_ref, f32[1,4096]{1,0:T(1,128)S(1)} %bitcast.56, bf16[768,4096]{1,0:T(8,128)(2,1)S(1)} %shard_map.64.refs_0_), custom_call_target="tpu_custom_call", output_to_operand_aliasing={{}: (2, {})} | custom-call | flops 9437184 | bytes 6291456 | tf_op jit(solution)/shard_map/pallas_call | solution.py:99
  35.9 2.3 %collective-permute-done.12 = bf16[256,512]{1,0:T(8,128)(2,1)S(1)} collective-permute-done((bf16[256,512]{1,0:T(8,128)(2,1)S(1)}, bf16[256,512]{1,0:T(8,128)(2,1)S(1)}, u32[]{:S(2)}, u32[]{:S(2)}) %collective-permute-start.12) | collective-permute-done | bytes 262176 | tf_op jit(solution)/shard_map/ppermute | solution.py:32
  38.1 1.7 %collective-permute-start.16 = (bf16[256,512]{1,0:T(8,128)(2,1)S(1)}, bf16[256,512]{1,0:T(8,128)(2,1)S(1)}, u32[]{:S(2)}, u32[]{:S(2)}) collective-permute-start(bf16[256,512]{1,0:T(8,128)(2,1)S(1)} %collective-permute-done.12), channel_id=1, source_target_pairs={{0,2},{4,0},{8,4},{12,8},{14,12},{10,14},{6,10},{2,6},{1,3},{5,1},... | collective-permute-start | bytes 786440 | tf_op jit(solution)/shard_map/ppermute | solution.py:32
  40.2 1.7 %collective-permute-start.14 = (bf16[256,512]{1,0:T(8,128)(2,1)S(1)}, bf16[256,512]{1,0:T(8,128)(2,1)S(1)}, u32[]{:S(2)}, u32[]{:S(2)}) collective-permute-start(bf16[256,512]{1,0:T(8,128)(2,1)S(1)} %collective-permute-done.10), channel_id=1, source_target_pairs={{0,2},{4,0},{8,4},{12,8},{14,12},{10,14},{6,10},{2,6},{1,3},{5,1},... | collective-permute-start | bytes 786440 | tf_op jit(solution)/shard_map/ppermute | solution.py:32
  45.5 1.9 %collective-permute-done.16 = bf16[256,512]{1,0:T(8,128)(2,1)S(1)} collective-permute-done((bf16[256,512]{1,0:T(8,128)(2,1)S(1)}, bf16[256,512]{1,0:T(8,128)(2,1)S(1)}, u32[]{:S(2)}, u32[]{:S(2)}) %collective-permute-start.16) | collective-permute-done | bytes 262176 | tf_op jit(solution)/shard_map/ppermute | solution.py:32
  49.4 1.9 %collective-permute-done.14 = bf16[256,512]{1,0:T(8,128)(2,1)S(1)} collective-permute-done((bf16[256,512]{1,0:T(8,128)(2,1)S(1)}, bf16[256,512]{1,0:T(8,128)(2,1)S(1)}, u32[]{:S(2)}, u32[]{:S(2)}) %collective-permute-start.14) | collective-permute-done | bytes 262176 | tf_op jit(solution)/shard_map/ppermute | solution.py:32
  60.1 3.1 %collective-permute-done.21 = bf16[6,1024]{1,0:T(8,128)(2,1)S(1)} collective-permute-done((bf16[6,1024]{1,0:T(8,128)(2,1)S(1)}, bf16[6,1024]{1,0:T(8,128)(2,1)S(1)}, u32[]{:S(2)}, u32[]{:S(2)}) %collective-permute-start.21) | collective-permute-done | bytes 12320 | tf_op jit(solution)/shard_map/ppermute | solution.py:64
  63.2 1.5 %collective-permute-done.20 = bf16[6,1024]{1,0:T(8,128)(2,1)S(1)} collective-permute-done((bf16[6,1024]{1,0:T(8,128)(2,1)S(1)}, bf16[6,1024]{1,0:T(8,128)(2,1)S(1)}, u32[]{:S(2)}, u32[]{:S(2)}) %collective-permute-start.20) | collective-permute-done | bytes 12320 | tf_op jit(solution)/shard_map/ppermute | solution.py:64
  65.9 2.5 %collective-permute-done.18 = bf16[6,1024]{1,0:T(8,128)(2,1)S(1)} collective-permute-done((bf16[6,1024]{1,0:T(8,128)(2,1)S(1)}, bf16[6,1024]{1,0:T(8,128)(2,1)S(1)}, u32[]{:S(2)}, u32[]{:S(2)}) %collective-permute-start.18) | collective-permute-done | bytes 12320 | tf_op jit(solution)/shard_map/ppermute | solution.py:64
  72.2 2.1 %collective-permute-start.25 = (bf16[256,512]{1,0:T(8,128)(2,1)S(1)}, bf16[256,512]{1,0:T(8,128)(2,1)S(1)}, u32[]{:S(2)}, u32[]{:S(2)}) collective-permute-start(bf16[256,512]{1,0:T(8,128)(2,1)S(1)} %convolution_convert_fusion.2), channel_id=1, source_target_pairs={{0,2},{4,0},{8,4},{12,8},{14,12},{10,14},{6,10},{2,6},{1,3},{5,1},... | collective-permute-start | bytes 786440 | tf_op jit(solution)/shard_map/ppermute | solution.py:32
  75.5 2.0 %collective-permute-start.27 = (bf16[256,512]{1,0:T(8,128)(2,1)S(1)}, bf16[256,512]{1,0:T(8,128)(2,1)S(1)}, u32[]{:S(2)}, u32[]{:S(2)}) collective-permute-start(bf16[256,512]{1,0:T(8,128)(2,1)S(1)} %convolution_convert_fusion), channel_id=1, source_target_pairs={{0,2},{4,0},{8,4},{12,8},{14,12},{10,14},{6,10},{2,6},{1,3},{5,1},... | collective-permute-start | bytes 786440 | tf_op jit(solution)/shard_map/ppermute | solution.py:32
  77.5 3.2 %collective-permute-done.23 = bf16[256,512]{1,0:T(8,128)(2,1)S(1)} collective-permute-done((bf16[256,512]{1,0:T(8,128)(2,1)S(1)}, bf16[256,512]{1,0:T(8,128)(2,1)S(1)}, u32[]{:S(2)}, u32[]{:S(2)}) %collective-permute-start.23) | collective-permute-done | bytes 262176 | tf_op jit(solution)/shard_map/ppermute | solution.py:32
  80.8 1.7 %collective-permute-start.24 = (bf16[256,1024]{1,0:T(8,128)(2,1)S(1)}, bf16[256,1024]{1,0:T(8,128)(2,1)S(1)}, u32[]{:S(2)}, u32[]{:S(2)}) collective-permute-start(bf16[256,1024]{1,0:T(8,128)(2,1)S(1)} %convert_element_type.163), channel_id=1, source_target_pairs={{0,16},{1,17},{2,18},{3,19},{4,20},{5,21},{6,22},{7,23},{8,24},{9,... | collective-permute-start | bytes 1572872 | tf_op jit(solution)/shard_map/ppermute | solution.py:40
  83.8 2.0 %collective-permute-start.29 = (bf16[256,512]{1,0:T(8,128)(2,1)S(1)}, bf16[256,512]{1,0:T(8,128)(2,1)S(1)}, u32[]{:S(2)}, u32[]{:S(2)}) collective-permute-start(bf16[256,512]{1,0:T(8,128)(2,1)S(1)} %fusion.7), channel_id=1, source_target_pairs={{0,2},{4,0},{8,4},{12,8},{14,12},{10,14},{6,10},{2,6},{1,3},{5,1},... | collective-permute-start | bytes 786440 | tf_op jit(solution)/shard_map/ppermute | solution.py:32
  87.6 2.1 %collective-permute-start.31 = (bf16[256,512]{1,0:T(8,128)(2,1)S(1)}, bf16[256,512]{1,0:T(8,128)(2,1)S(1)}, u32[]{:S(2)}, u32[]{:S(2)}) collective-permute-start(bf16[256,512]{1,0:T(8,128)(2,1)S(1)} %fusion.8), channel_id=1, source_target_pairs={{0,2},{4,0},{8,4},{12,8},{14,12},{10,14},{6,10},{2,6},{1,3},{5,1},... | collective-permute-start | bytes 786440 | tf_op jit(solution)/shard_map/ppermute | solution.py:32
  89.7 2.6 %collective-permute-done.28 = bf16[256,512]{1,0:T(8,128)(2,1)S(1)} collective-permute-done((bf16[256,512]{1,0:T(8,128)(2,1)S(1)}, bf16[256,512]{1,0:T(8,128)(2,1)S(1)}, u32[]{:S(2)}, u32[]{:S(2)}) %collective-permute-start.28) | collective-permute-done | bytes 262176 | tf_op jit(solution)/shard_map/ppermute | solution.py:32
  93.7 1.5 %collective-permute-start.32 = (bf16[256,512]{1,0:T(8,128)(2,1)S(1)}, bf16[256,512]{1,0:T(8,128)(2,1)S(1)}, u32[]{:S(2)}, u32[]{:S(2)}) collective-permute-start(bf16[256,512]{1,0:T(8,128)(2,1)S(1)} %fusion.4), channel_id=1, source_target_pairs={{0,4},{4,8},{8,12},{12,14},{14,10},{10,6},{6,2},{2,0},{1,5},{5,9},... | collective-permute-start | bytes 786440 | tf_op jit(solution)/shard_map/ppermute | solution.py:32
  95.8 2.9 %collective-permute-done.31 = bf16[256,512]{1,0:T(8,128)(2,1)S(1)} collective-permute-done((bf16[256,512]{1,0:T(8,128)(2,1)S(1)}, bf16[256,512]{1,0:T(8,128)(2,1)S(1)}, u32[]{:S(2)}, u32[]{:S(2)}) %collective-permute-start.31) | collective-permute-done | bytes 262176 | tf_op jit(solution)/shard_map/ppermute | solution.py:32
  101.4 3.2 %collective-permute-done.32 = bf16[256,512]{1,0:T(8,128)(2,1)S(1)} collective-permute-done((bf16[256,512]{1,0:T(8,128)(2,1)S(1)}, bf16[256,512]{1,0:T(8,128)(2,1)S(1)}, u32[]{:S(2)}, u32[]{:S(2)}) %collective-permute-start.32) | collective-permute-done | bytes 262176 | tf_op jit(solution)/shard_map/ppermute | solution.py:32
  108.6 1.5 %collective-permute-start.34 = (bf16[256,512]{1,0:T(8,128)(2,1)S(1)}, bf16[256,512]{1,0:T(8,128)(2,1)S(1)}, u32[]{:S(2)}, u32[]{:S(2)}) collective-permute-start(bf16[256,512]{1,0:T(8,128)(2,1)S(1)} %fusion.2), channel_id=1, source_target_pairs={{0,4},{4,8},{8,12},{12,14},{14,10},{10,6},{6,2},{2,0},{1,5},{5,9},... | collective-permute-start | bytes 786440 | tf_op jit(solution)/shard_map/ppermute | solution.py:32
  110.1 4.1 %collective-permute-done.37 = bf16[256,512]{1,0:T(8,128)(2,1)S(1)} collective-permute-done((bf16[256,512]{1,0:T(8,128)(2,1)S(1)}, bf16[256,512]{1,0:T(8,128)(2,1)S(1)}, u32[]{:S(2)}, u32[]{:S(2)}) %collective-permute-start.37) | collective-permute-done | bytes 262176 | tf_op jit(solution)/shard_map/ppermute | solution.py:32
  114.4 2.6 %collective-permute-done.35 = bf16[256,512]{1,0:T(8,128)(2,1)S(1)} collective-permute-done((bf16[256,512]{1,0:T(8,128)(2,1)S(1)}, bf16[256,512]{1,0:T(8,128)(2,1)S(1)}, u32[]{:S(2)}, u32[]{:S(2)}) %collective-permute-start.35) | collective-permute-done | bytes 262176 | tf_op jit(solution)/shard_map/ppermute | solution.py:32
  (128 shorter events, 43.2 us)
Async XLA Ops:
  0.0 29.4 %collective-permute-start = (bf16[3,128,4096]{2,1,0:T(8,128)(2,1)}, bf16[3,128,4096]{2,1,0:T(8,128)(2,1)S(1)}, u32[]{:S(2)}, u32[]{:S(2)}) collective-permute-start(bf16[3,128,4096]{2,1,0:T(8,128)(2,1)} %bitcast.53), channel_id=1, source_target_pairs={{0,1},{1,0},{2,3},{3,2},{4,5},{5,4},{6,7},{7,6},{8,9},{9,8},{10,11... | collective-permute-start | bytes 9437192 | tf_op jit(solution)/shard_map/ppermute | solution.py:52
  2.1 9.5 %collective-permute-start.2 = (bf16[256,512]{1,0:T(8,128)(2,1)S(1)}, bf16[256,512]{1,0:T(8,128)(2,1)S(1)}, u32[]{:S(2)}, u32[]{:S(2)}) collective-permute-start(bf16[256,512]{1,0:T(8,128)(2,1)S(1)} %get-tuple-element.67), channel_id=1, source_target_pairs={{0,4},{4,8},{8,12},{12,14},{14,10},{10,6},{6,2},{2,0},{1,5},{5,9},... | collective-permute-start | bytes 786440 | tf_op jit(solution)/shard_map/ppermute | solution.py:32
  6.1 10.0 %collective-permute-start.3 = (bf16[256,512]{1,0:T(8,128)(2,1)S(1)}, bf16[256,512]{1,0:T(8,128)(2,1)S(1)}, u32[]{:S(2)}, u32[]{:S(2)}) collective-permute-start(bf16[256,512]{1,0:T(8,128)(2,1)S(1)} %collective-permute-done.1), channel_id=1, source_target_pairs={{0,2},{4,0},{8,4},{12,8},{14,12},{10,14},{6,10},{2,6},{1,3},{5,1},... | collective-permute-start | bytes 786440 | tf_op jit(solution)/shard_map/ppermute | solution.py:32
  9.0 16.0 %collective-permute-start.5 = (bf16[256,512]{1,0:T(8,128)(2,1)S(1)}, bf16[256,512]{1,0:T(8,128)(2,1)S(1)}, u32[]{:S(2)}, u32[]{:S(2)}) collective-permute-start(bf16[256,512]{1,0:T(8,128)(2,1)S(1)} %get-tuple-element.67), channel_id=1, source_target_pairs={{0,2},{4,0},{8,4},{12,8},{14,12},{10,14},{6,10},{2,6},{1,3},{5,1},... | collective-permute-start | bytes 786440 | tf_op jit(solution)/shard_map/ppermute | solution.py:32
  10.6 14.5 %collective-permute-start.4 = (bf16[256,512]{1,0:T(8,128)(2,1)S(1)}, bf16[256,512]{1,0:T(8,128)(2,1)S(1)}, u32[]{:S(2)}, u32[]{:S(2)}) collective-permute-start(bf16[256,512]{1,0:T(8,128)(2,1)S(1)} %collective-permute-done.1), channel_id=1, source_target_pairs={{0,4},{4,8},{8,12},{12,14},{14,10},{10,6},{6,2},{2,0},{1,5},{5,9},... | collective-permute-start | bytes 786440 | tf_op jit(solution)/shard_map/ppermute | solution.py:32
  11.6 15.6 %collective-permute-start.7 = (bf16[256,512]{1,0:T(8,128)(2,1)S(1)}, bf16[256,512]{1,0:T(8,128)(2,1)S(1)}, u32[]{:S(2)}, u32[]{:S(2)}) collective-permute-start(bf16[256,512]{1,0:T(8,128)(2,1)S(1)} %collective-permute-done.2), channel_id=1, source_target_pairs={{0,4},{4,8},{8,12},{12,14},{14,10},{10,6},{6,2},{2,0},{1,5},{5,9},... | collective-permute-start | bytes 786440 | tf_op jit(solution)/shard_map/ppermute | solution.py:32
  16.1 11.2 %collective-permute-start.8 = (bf16[256,512]{1,0:T(8,128)(2,1)S(1)}, bf16[256,512]{1,0:T(8,128)(2,1)S(1)}, u32[]{:S(2)}, u32[]{:S(2)}) collective-permute-start(bf16[256,512]{1,0:T(8,128)(2,1)S(1)} %collective-permute-done.3), channel_id=1, source_target_pairs={{0,2},{4,0},{8,4},{12,8},{14,12},{10,14},{6,10},{2,6},{1,3},{5,1},... | collective-permute-start | bytes 786440 | tf_op jit(solution)/shard_map/ppermute | solution.py:32
  25.1 15.1 %collective-permute-start.10 = (bf16[256,512]{1,0:T(8,128)(2,1)S(1)}, bf16[256,512]{1,0:T(8,128)(2,1)S(1)}, u32[]{:S(2)}, u32[]{:S(2)}) collective-permute-start(bf16[256,512]{1,0:T(8,128)(2,1)S(1)} %collective-permute-done.5), channel_id=1, source_target_pairs={{0,2},{4,0},{8,4},{12,8},{14,12},{10,14},{6,10},{2,6},{1,3},{5,1},... | collective-permute-start | bytes 786440 | tf_op jit(solution)/shard_map/ppermute | solution.py:32
  26.7 15.2 %collective-permute-start.9 = (bf16[256,512]{1,0:T(8,128)(2,1)S(1)}, bf16[256,512]{1,0:T(8,128)(2,1)S(1)}, u32[]{:S(2)}, u32[]{:S(2)}) collective-permute-start(bf16[256,512]{1,0:T(8,128)(2,1)S(1)} %collective-permute-done.4), channel_id=1, source_target_pairs={{0,4},{4,8},{8,12},{12,14},{14,10},{10,6},{6,2},{2,0},{1,5},{5,9},... | collective-permute-start | bytes 786440 | tf_op jit(solution)/shard_map/ppermute | solution.py:32
  27.1 12.7 %collective-permute-start.11 = (bf16[256,512]{1,0:T(8,128)(2,1)S(1)}, bf16[256,512]{1,0:T(8,128)(2,1)S(1)}, u32[]{:S(2)}, u32[]{:S(2)}) collective-permute-start(bf16[256,512]{1,0:T(8,128)(2,1)S(1)} %collective-permute-done.7), channel_id=1, source_target_pairs={{0,4},{4,8},{8,12},{12,14},{14,10},{10,6},{6,2},{2,0},{1,5},{5,9},... | collective-permute-start | bytes 786440 | tf_op jit(solution)/shard_map/ppermute | solution.py:32
  27.4 10.8 %collective-permute-start.12 = (bf16[256,512]{1,0:T(8,128)(2,1)S(1)}, bf16[256,512]{1,0:T(8,128)(2,1)S(1)}, u32[]{:S(2)}, u32[]{:S(2)}) collective-permute-start(bf16[256,512]{1,0:T(8,128)(2,1)S(1)} %collective-permute-done.8), channel_id=1, source_target_pairs={{0,2},{4,0},{8,4},{12,8},{14,12},{10,14},{6,10},{2,6},{1,3},{5,1},... | collective-permute-start | bytes 786440 | tf_op jit(solution)/shard_map/ppermute | solution.py:32
  38.1 9.2 %collective-permute-start.16 = (bf16[256,512]{1,0:T(8,128)(2,1)S(1)}, bf16[256,512]{1,0:T(8,128)(2,1)S(1)}, u32[]{:S(2)}, u32[]{:S(2)}) collective-permute-start(bf16[256,512]{1,0:T(8,128)(2,1)S(1)} %collective-permute-done.12), channel_id=1, source_target_pairs={{0,2},{4,0},{8,4},{12,8},{14,12},{10,14},{6,10},{2,6},{1,3},{5,1},... | collective-permute-start | bytes 786440 | tf_op jit(solution)/shard_map/ppermute | solution.py:32
  39.8 9.1 %collective-permute-start.15 = (bf16[256,512]{1,0:T(8,128)(2,1)S(1)}, bf16[256,512]{1,0:T(8,128)(2,1)S(1)}, u32[]{:S(2)}, u32[]{:S(2)}) collective-permute-start(bf16[256,512]{1,0:T(8,128)(2,1)S(1)} %collective-permute-done.11), channel_id=1, source_target_pairs={{0,4},{4,8},{8,12},{12,14},{14,10},{10,6},{6,2},{2,0},{1,5},{5,9},... | collective-permute-start | bytes 786440 | tf_op jit(solution)/shard_map/ppermute | solution.py:32
  40.2 11.1 %collective-permute-start.14 = (bf16[256,512]{1,0:T(8,128)(2,1)S(1)}, bf16[256,512]{1,0:T(8,128)(2,1)S(1)}, u32[]{:S(2)}, u32[]{:S(2)}) collective-permute-start(bf16[256,512]{1,0:T(8,128)(2,1)S(1)} %collective-permute-done.10), channel_id=1, source_target_pairs={{0,2},{4,0},{8,4},{12,8},{14,12},{10,14},{6,10},{2,6},{1,3},{5,1},... | collective-permute-start | bytes 786440 | tf_op jit(solution)/shard_map/ppermute | solution.py:32
  41.9 9.9 %collective-permute-start.13 = (bf16[256,512]{1,0:T(8,128)(2,1)S(1)}, bf16[256,512]{1,0:T(8,128)(2,1)S(1)}, u32[]{:S(2)}, u32[]{:S(2)}) collective-permute-start(bf16[256,512]{1,0:T(8,128)(2,1)S(1)} %collective-permute-done.9), channel_id=1, source_target_pairs={{0,4},{4,8},{8,12},{12,14},{14,10},{10,6},{6,2},{2,0},{1,5},{5,9},... | collective-permute-start | bytes 786440 | tf_op jit(solution)/shard_map/ppermute | solution.py:32
  56.2 8.5 %collective-permute-start.20 = (bf16[6,1024]{1,0:T(8,128)(2,1)S(1)}, bf16[6,1024]{1,0:T(8,128)(2,1)S(1)}, u32[]{:S(2)}, u32[]{:S(2)}) collective-permute-start(bf16[6,1024]{1,0:T(8,128)(2,1)S(1)} %maximum_select_fusion.2), channel_id=1, source_target_pairs={{24,0},{23,1},{28,4},{19,5},{30,8},{17,9},{26,12},{21,13},{22,14},... | collective-permute-start | bytes 36872 | tf_op jit(solution)/shard_map/ppermute | solution.py:64
  58.8 9.6 %collective-permute-start.18 = (bf16[6,1024]{1,0:T(8,128)(2,1)S(1)}, bf16[6,1024]{1,0:T(8,128)(2,1)S(1)}, u32[]{:S(2)}, u32[]{:S(2)}) collective-permute-start(bf16[6,1024]{1,0:T(8,128)(2,1)S(1)} %maximum_select_fusion.2), channel_id=1, source_target_pairs={{16,0},{31,1},{20,4},{27,5},{24,8},{23,9},{28,12},{19,13},{30,14},... | collective-permute-start | bytes 36872 | tf_op jit(solution)/shard_map/ppermute | solution.py:64
  71.6 9.2 %collective-permute-start.23 = (bf16[256,512]{1,0:T(8,128)(2,1)S(1)}, bf16[256,512]{1,0:T(8,128)(2,1)S(1)}, u32[]{:S(2)}, u32[]{:S(2)}) collective-permute-start(bf16[256,512]{1,0:T(8,128)(2,1)S(1)} %convolution_convert_fusion.3), channel_id=1, source_target_pairs={{0,4},{4,8},{8,12},{12,14},{14,10},{10,6},{6,2},{2,0},{1,5},{5,9},... | collective-permute-start | bytes 786440 | tf_op jit(solution)/shard_map/ppermute | solution.py:32
  72.2 10.9 %collective-permute-start.25 = (bf16[256,512]{1,0:T(8,128)(2,1)S(1)}, bf16[256,512]{1,0:T(8,128)(2,1)S(1)}, u32[]{:S(2)}, u32[]{:S(2)}) collective-permute-start(bf16[256,512]{1,0:T(8,128)(2,1)S(1)} %convolution_convert_fusion.2), channel_id=1, source_target_pairs={{0,2},{4,0},{8,4},{12,8},{14,12},{10,14},{6,10},{2,6},{1,3},{5,1},... | collective-permute-start | bytes 786440 | tf_op jit(solution)/shard_map/ppermute | solution.py:32
  75.5 10.9 %collective-permute-start.26 = (bf16[256,512]{1,0:T(8,128)(2,1)S(1)}, bf16[256,512]{1,0:T(8,128)(2,1)S(1)}, u32[]{:S(2)}, u32[]{:S(2)}) collective-permute-start(bf16[256,512]{1,0:T(8,128)(2,1)S(1)} %convolution_convert_fusion.1), channel_id=1, source_target_pairs={{0,4},{4,8},{8,12},{12,14},{14,10},{10,6},{6,2},{2,0},{1,5},{5,9},... | collective-permute-start | bytes 786440 | tf_op jit(solution)/shard_map/ppermute | solution.py:32
  75.5 11.5 %collective-permute-start.27 = (bf16[256,512]{1,0:T(8,128)(2,1)S(1)}, bf16[256,512]{1,0:T(8,128)(2,1)S(1)}, u32[]{:S(2)}, u32[]{:S(2)}) collective-permute-start(bf16[256,512]{1,0:T(8,128)(2,1)S(1)} %convolution_convert_fusion), channel_id=1, source_target_pairs={{0,2},{4,0},{8,4},{12,8},{14,12},{10,14},{6,10},{2,6},{1,3},{5,1},... | collective-permute-start | bytes 786440 | tf_op jit(solution)/shard_map/ppermute | solution.py:32
  80.8 24.9 %collective-permute-start.24 = (bf16[256,1024]{1,0:T(8,128)(2,1)S(1)}, bf16[256,1024]{1,0:T(8,128)(2,1)S(1)}, u32[]{:S(2)}, u32[]{:S(2)}) collective-permute-start(bf16[256,1024]{1,0:T(8,128)(2,1)S(1)} %convert_element_type.163), channel_id=1, source_target_pairs={{0,16},{1,17},{2,18},{3,19},{4,20},{5,21},{6,22},{7,23},{8,24},{9,... | collective-permute-start | bytes 1572872 | tf_op jit(solution)/shard_map/ppermute | solution.py:40
  83.7 8.7 %collective-permute-start.28 = (bf16[256,512]{1,0:T(8,128)(2,1)S(1)}, bf16[256,512]{1,0:T(8,128)(2,1)S(1)}, u32[]{:S(2)}, u32[]{:S(2)}) collective-permute-start(bf16[256,512]{1,0:T(8,128)(2,1)S(1)} %fusion.6), channel_id=1, source_target_pairs={{0,4},{4,8},{8,12},{12,14},{14,10},{10,6},{6,2},{2,0},{1,5},{5,9},... | collective-permute-start | bytes 786440 | tf_op jit(solution)/shard_map/ppermute | solution.py:32
  83.8 9.3 %collective-permute-start.29 = (bf16[256,512]{1,0:T(8,128)(2,1)S(1)}, bf16[256,512]{1,0:T(8,128)(2,1)S(1)}, u32[]{:S(2)}, u32[]{:S(2)}) collective-permute-start(bf16[256,512]{1,0:T(8,128)(2,1)S(1)} %fusion.7), channel_id=1, source_target_pairs={{0,2},{4,0},{8,4},{12,8},{14,12},{10,14},{6,10},{2,6},{1,3},{5,1},... | collective-permute-start | bytes 786440 | tf_op jit(solution)/shard_map/ppermute | solution.py:32
  87.6 11.1 %collective-permute-start.31 = (bf16[256,512]{1,0:T(8,128)(2,1)S(1)}, bf16[256,512]{1,0:T(8,128)(2,1)S(1)}, u32[]{:S(2)}, u32[]{:S(2)}) collective-permute-start(bf16[256,512]{1,0:T(8,128)(2,1)S(1)} %fusion.8), channel_id=1, source_target_pairs={{0,2},{4,0},{8,4},{12,8},{14,12},{10,14},{6,10},{2,6},{1,3},{5,1},... | collective-permute-start | bytes 786440 | tf_op jit(solution)/shard_map/ppermute | solution.py:32
  89.7 9.6 %collective-permute-start.30 = (bf16[256,512]{1,0:T(8,128)(2,1)S(1)}, bf16[256,512]{1,0:T(8,128)(2,1)S(1)}, u32[]{:S(2)}, u32[]{:S(2)}) collective-permute-start(bf16[256,512]{1,0:T(8,128)(2,1)S(1)} %fusion.5), channel_id=1, source_target_pairs={{0,4},{4,8},{8,12},{12,14},{14,10},{10,6},{6,2},{2,0},{1,5},{5,9},... | collective-permute-start | bytes 786440 | tf_op jit(solution)/shard_map/ppermute | solution.py:32
  93.7 10.9 %collective-permute-start.32 = (bf16[256,512]{1,0:T(8,128)(2,1)S(1)}, bf16[256,512]{1,0:T(8,128)(2,1)S(1)}, u32[]{:S(2)}, u32[]{:S(2)}) collective-permute-start(bf16[256,512]{1,0:T(8,128)(2,1)S(1)} %fusion.4), channel_id=1, source_target_pairs={{0,4},{4,8},{8,12},{12,14},{14,10},{10,6},{6,2},{2,0},{1,5},{5,9},... | collective-permute-start | bytes 786440 | tf_op jit(solution)/shard_map/ppermute | solution.py:32
  95.2 9.4 %collective-permute-start.33 = (bf16[256,512]{1,0:T(8,128)(2,1)S(1)}, bf16[256,512]{1,0:T(8,128)(2,1)S(1)}, u32[]{:S(2)}, u32[]{:S(2)}) collective-permute-start(bf16[256,512]{1,0:T(8,128)(2,1)S(1)} %fusion.9), channel_id=1, source_target_pairs={{0,2},{4,0},{8,4},{12,8},{14,12},{10,14},{6,10},{2,6},{1,3},{5,1},... | collective-permute-start | bytes 786440 | tf_op jit(solution)/shard_map/ppermute | solution.py:32
  99.9 10.2 %collective-permute-start.36 = (bf16[256,512]{1,0:T(8,128)(2,1)S(1)}, bf16[256,512]{1,0:T(8,128)(2,1)S(1)}, u32[]{:S(2)}, u32[]{:S(2)}) collective-permute-start(bf16[256,512]{1,0:T(8,128)(2,1)S(1)} %fusion.3), channel_id=1, source_target_pairs={{0,4},{4,8},{8,12},{12,14},{14,10},{10,6},{6,2},{2,0},{1,5},{5,9},... | collective-permute-start | bytes 786440 | tf_op jit(solution)/shard_map/ppermute | solution.py:32
  105.8 8.4 %collective-permute-start.37 = (bf16[256,512]{1,0:T(8,128)(2,1)S(1)}, bf16[256,512]{1,0:T(8,128)(2,1)S(1)}, u32[]{:S(2)}, u32[]{:S(2)}) collective-permute-start(bf16[256,512]{1,0:T(8,128)(2,1)S(1)} %fusion.11), channel_id=1, source_target_pairs={{0,2},{4,0},{8,4},{12,8},{14,12},{10,14},{6,10},{2,6},{1,3},{5,1},... | collective-permute-start | bytes 786440 | tf_op jit(solution)/shard_map/ppermute | solution.py:32
  108.0 9.0 %collective-permute-start.35 = (bf16[256,512]{1,0:T(8,128)(2,1)S(1)}, bf16[256,512]{1,0:T(8,128)(2,1)S(1)}, u32[]{:S(2)}, u32[]{:S(2)}) collective-permute-start(bf16[256,512]{1,0:T(8,128)(2,1)S(1)} %fusion.10), channel_id=1, source_target_pairs={{0,2},{4,0},{8,4},{12,8},{14,12},{10,14},{6,10},{2,6},{1,3},{5,1},... | collective-permute-start | bytes 786440 | tf_op jit(solution)/shard_map/ppermute | solution.py:32
  108.6 8.4 %collective-permute-start.34 = (bf16[256,512]{1,0:T(8,128)(2,1)S(1)}, bf16[256,512]{1,0:T(8,128)(2,1)S(1)}, u32[]{:S(2)}, u32[]{:S(2)}) collective-permute-start(bf16[256,512]{1,0:T(8,128)(2,1)S(1)} %fusion.2), channel_id=1, source_target_pairs={{0,4},{4,8},{8,12},{12,14},{14,10},{10,6},{6,2},{2,0},{1,5},{5,9},... | collective-permute-start | bytes 786440 | tf_op jit(solution)/shard_map/ppermute | solution.py:32
  (12 other events, 54.3 us)

commit v20 on v18

--- a/solution.py
+++ b/solution.py
@@ -133,9 +133,7 @@
         for i in range(2)
     }
     scalars = [first_core, shift, own_columns, given_columns, trainer, *starts.values()]
-    weights, *scalars = lax.optimization_barrier([master[0], *scalars])
-    first_core, shift, own_columns, given_columns, trainer, *firsts = scalars
-    starts = dict(zip(starts, firsts))
+    weights = after(scalars, master[0])
     own = cut(weights, 1, own_columns, half).astype(jnp.bfloat16)
     given = cut(weights, 1, given_columns, half).astype(jnp.bfloat16)
     sibling = from_sibling(given)

time: 117 us -> 115 us (0.983)
  matrix products: 18.7 us -> 15 us
  waiting for transfers between devices: 41.2 us -> 43.5 us
    dot_general x16, matrix products: 9.32 us -> 6.59 us  [term(): lax.dot_general(columns(offset, i), delta, (((0,), (0,)), ((), ())), pref...]
    ppermute x28, waiting for transfers between devices: 31.1 us -> 33.2 us  [along_ring(): return lax.ppermute(block, 'chip', pairs)]
  transfers between devices with their start and end apart: 39 -> 39, of which waited for: 21 -> 23; matrix products, arithmetic and copies ran while one was open for 16% -> 14% of each run, Pallas kernels for 6% -> 6%
where the time goes in v20:
time: 115 us
  waiting for transfers between devices  43.5 us (38%)
  starting transfers between devices  40.9 us (36%)
  matrix products  15 us (13%)
  Pallas kernels  7.16 us (6%)
  local copies, waits for them, and re-layouts  4.88 us (4%)
  other arithmetic  3.22 us (3%)
    ppermute x28, waiting for transfers between devices, along_ring(): return lax.ppermute(block, 'chip', pairs)  33.2 us
    ppermute x28, starting transfers between devices, along_ring(): return lax.ppermute(block, 'chip', pairs)  33.1 us
    ppermute x4, waiting for transfers between devices, slab_blocks(): kept.append(lax.ppermute(stored, ('grp', 'chip', 'core'), pairs))  7.28 us
    pallas_call x2, Pallas kernels, normalize(): pl.pallas_call(functools.partial(normalize_kernel, 16), grid=(seqs,), in_...  7.16 us
    dot_general x16, matrix products, product(): jnp.dot(columns(offset, i), block, preferred_element_type=jnp.float32)  6.81 us
    dot_general x16, matrix products, term(): lax.dot_general(columns(offset, i), delta, (((0,), (0,)), ((), ())), pref...  6.59 us
    ppermute x4, starting transfers between devices, slab_blocks(): kept.append(lax.ppermute(stored, ('grp', 'chip', 'core'), pairs))  5.16 us
    unnamed x11, local copies, waits for them, and re-layouts  3.31 us
  transfers between devices with their start and end apart: 39, of which 23 were waited for; matrix products, arithmetic and copies ran while one was open for 14% of the time, Pallas kernels for 6%

profile of v20, /device:TPU:0, one launch (start us, length us, event | category | flops | bytes accessed | tf_op | source)
XLA Modules:
  0.0 115.1 jit_solution(4919105103247573895)
XLA Ops:
  1.8 3.0 %collective-permute-start.2 = (bf16[256,512]{1,0:T(8,128)(2,1)S(1)}, bf16[256,512]{1,0:T(8,128)(2,1)S(1)}, u32[]{:S(2)}, u32[]{:S(2)}) collective-permute-start(bf16[256,512]{1,0:T(8,128)(2,1)S(1)} %get-tuple-element.69), channel_id=1, source_target_pairs={{0,4},{4,8},{8,12},{12,14},{14,10},{10,6},{6,2},{2,0},{1,5},{5,9},... | collective-permute-start | bytes 786440 | tf_op jit(solution)/shard_map/ppermute | solution.py:32
  6.1 2.9 %collective-permute-start.5 = (bf16[256,512]{1,0:T(8,128)(2,1)S(1)}, bf16[256,512]{1,0:T(8,128)(2,1)S(1)}, u32[]{:S(2)}, u32[]{:S(2)}) collective-permute-start(bf16[256,512]{1,0:T(8,128)(2,1)S(1)} %collective-permute-done.1), channel_id=1, source_target_pairs={{0,2},{4,0},{8,4},{12,8},{14,12},{10,14},{6,10},{2,6},{1,3},{5,1},... | collective-permute-start | bytes 786440 | tf_op jit(solution)/shard_map/ppermute | solution.py:32
  9.1 2.5 %collective-permute-done.2 = bf16[256,512]{1,0:T(8,128)(2,1)S(1)} collective-permute-done((bf16[256,512]{1,0:T(8,128)(2,1)S(1)}, bf16[256,512]{1,0:T(8,128)(2,1)S(1)}, u32[]{:S(2)}, u32[]{:S(2)}) %collective-permute-start.2) | collective-permute-done | bytes 262176 | tf_op jit(solution)/shard_map/ppermute | solution.py:32
  11.5 2.5 %collective-permute-start.7 = (bf16[256,512]{1,0:T(8,128)(2,1)S(1)}, bf16[256,512]{1,0:T(8,128)(2,1)S(1)}, u32[]{:S(2)}, u32[]{:S(2)}) collective-permute-start(bf16[256,512]{1,0:T(8,128)(2,1)S(1)} %collective-permute-done.2), channel_id=1, source_target_pairs={{0,4},{4,8},{8,12},{12,14},{14,10},{10,6},{6,2},{2,0},{1,5},{5,9},... | collective-permute-start | bytes 786440 | tf_op jit(solution)/shard_map/ppermute | solution.py:32
  14.8 1.9 %copy-done = bf16[1,3,128,4096]{3,2,1,0:T(8,128)(2,1)S(1)} copy-done((bf16[1,3,128,4096]{3,2,1,0:T(8,128)(2,1)S(1)}, bf16[1,3,128,4096]{3,2,1,0:T(8,128)(2,1)}, u32[]{:S(2)}) %copy-start) | copy-done | bytes 3145752
  17.4 3.6 %shard_map.64.refs_0_ = bf16[768,4096]{1,0:T(8,128)(2,1)S(1)} custom-call(bf16[3,128,4096]{2,1,0:T(8,128)(2,1)S(1)} %bitcast.54, f32[1,4096]{1,0:T(1,128)S(1)} %bitcast.55), custom_call_target="tpu_custom_call" | custom-call | flops 9437184 | bytes 6291456 | tf_op jit(solution)/shard_map/pallas_call | solution.py:99
  21.0 2.1 %collective-permute-start.9 = (bf16[256,512]{1,0:T(8,128)(2,1)S(1)}, bf16[256,512]{1,0:T(8,128)(2,1)S(1)}, u32[]{:S(2)}, u32[]{:S(2)}) collective-permute-start(bf16[256,512]{1,0:T(8,128)(2,1)S(1)} %collective-permute-done.4), channel_id=1, source_target_pairs={{0,4},{4,8},{8,12},{12,14},{14,10},{10,6},{6,2},{2,0},{1,5},{5,9},... | collective-permute-start | bytes 786440 | tf_op jit(solution)/shard_map/ppermute | solution.py:32
  23.4 1.9 %collective-permute-start.11 = (bf16[256,512]{1,0:T(8,128)(2,1)S(1)}, bf16[256,512]{1,0:T(8,128)(2,1)S(1)}, u32[]{:S(2)}, u32[]{:S(2)}) collective-permute-start(bf16[256,512]{1,0:T(8,128)(2,1)S(1)} %collective-permute-done.7), channel_id=1, source_target_pairs={{0,4},{4,8},{8,12},{12,14},{14,10},{10,6},{6,2},{2,0},{1,5},{5,9},... | collective-permute-start | bytes 786440 | tf_op jit(solution)/shard_map/ppermute | solution.py:32
  25.4 3.6 %shard_map.65 = bf16[768,4096]{1,0:T(8,128)(2,1)S(1)} custom-call(bf16[3,128,4096]{2,1,0:T(8,128)(2,1)S(1)} %collective-permute-done.states_ref, f32[1,4096]{1,0:T(1,128)S(1)} %bitcast.56, bf16[768,4096]{1,0:T(8,128)(2,1)S(1)} %shard_map.64.refs_0_), custom_call_target="tpu_custom_call", output_to_operand_aliasing={{}: (2, {})} | custom-call | flops 9437184 | bytes 6291456 | tf_op jit(solution)/shard_map/pallas_call | solution.py:99
  32.2 1.9 %collective-permute-start.13 = (bf16[256,512]{1,0:T(8,128)(2,1)S(1)}, bf16[256,512]{1,0:T(8,128)(2,1)S(1)}, u32[]{:S(2)}, u32[]{:S(2)}) collective-permute-start(bf16[256,512]{1,0:T(8,128)(2,1)S(1)} %collective-permute-done.9), channel_id=1, source_target_pairs={{0,4},{4,8},{8,12},{12,14},{14,10},{10,6},{6,2},{2,0},{1,5},{5,9},... | collective-permute-start | bytes 786440 | tf_op jit(solution)/shard_map/ppermute | solution.py:32
  34.4 1.9 %collective-permute-start.15 = (bf16[256,512]{1,0:T(8,128)(2,1)S(1)}, bf16[256,512]{1,0:T(8,128)(2,1)S(1)}, u32[]{:S(2)}, u32[]{:S(2)}) collective-permute-start(bf16[256,512]{1,0:T(8,128)(2,1)S(1)} %collective-permute-done.11), channel_id=1, source_target_pairs={{0,4},{4,8},{8,12},{12,14},{14,10},{10,6},{6,2},{2,0},{1,5},{5,9},... | collective-permute-start | bytes 786440 | tf_op jit(solution)/shard_map/ppermute | solution.py:32
  38.8 3.7 %collective-permute-done.14 = bf16[256,512]{1,0:T(8,128)(2,1)S(1)} collective-permute-done((bf16[256,512]{1,0:T(8,128)(2,1)S(1)}, bf16[256,512]{1,0:T(8,128)(2,1)S(1)}, u32[]{:S(2)}, u32[]{:S(2)}) %collective-permute-start.14) | collective-permute-done | bytes 262176 | tf_op jit(solution)/shard_map/ppermute | solution.py:32
  43.6 3.1 %collective-permute-done.15 = bf16[256,512]{1,0:T(8,128)(2,1)S(1)} collective-permute-done((bf16[256,512]{1,0:T(8,128)(2,1)S(1)}, bf16[256,512]{1,0:T(8,128)(2,1)S(1)}, u32[]{:S(2)}, u32[]{:S(2)}) %collective-permute-start.15) | collective-permute-done | bytes 262176 | tf_op jit(solution)/shard_map/ppermute | solution.py:32
  47.0 3.0 %collective-permute-done.16 = bf16[256,512]{1,0:T(8,128)(2,1)S(1)} collective-permute-done((bf16[256,512]{1,0:T(8,128)(2,1)S(1)}, bf16[256,512]{1,0:T(8,128)(2,1)S(1)}, u32[]{:S(2)}, u32[]{:S(2)}) %collective-permute-start.16) | collective-permute-done | bytes 262176 | tf_op jit(solution)/shard_map/ppermute | solution.py:32
  58.7 2.3 %collective-permute-done.19 = bf16[6,1024]{1,0:T(8,128)(2,1)S(1)} collective-permute-done((bf16[6,1024]{1,0:T(8,128)(2,1)S(1)}, bf16[6,1024]{1,0:T(8,128)(2,1)S(1)}, u32[]{:S(2)}, u32[]{:S(2)}) %collective-permute-start.19) | collective-permute-done | bytes 12320 | tf_op jit(solution)/shard_map/ppermute | solution.py:64
  61.0 2.3 %collective-permute-done.20 = bf16[6,1024]{1,0:T(8,128)(2,1)S(1)} collective-permute-done((bf16[6,1024]{1,0:T(8,128)(2,1)S(1)}, bf16[6,1024]{1,0:T(8,128)(2,1)S(1)}, u32[]{:S(2)}, u32[]{:S(2)}) %collective-permute-start.20) | collective-permute-done | bytes 12320 | tf_op jit(solution)/shard_map/ppermute | solution.py:64
  63.3 2.3 %collective-permute-done.21 = bf16[6,1024]{1,0:T(8,128)(2,1)S(1)} collective-permute-done((bf16[6,1024]{1,0:T(8,128)(2,1)S(1)}, bf16[6,1024]{1,0:T(8,128)(2,1)S(1)}, u32[]{:S(2)}, u32[]{:S(2)}) %collective-permute-start.21) | collective-permute-done | bytes 12320 | tf_op jit(solution)/shard_map/ppermute | solution.py:64
  69.5 1.5 %collective-permute-start.23 = (bf16[256,512]{1,0:T(8,128)(2,1)S(1)}, bf16[256,512]{1,0:T(8,128)(2,1)S(1)}, u32[]{:S(2)}, u32[]{:S(2)}) collective-permute-start(bf16[256,512]{1,0:T(8,128)(2,1)S(1)} %convolution_convert_fusion.3), channel_id=1, source_target_pairs={{0,4},{4,8},{8,12},{12,14},{14,10},{10,6},{6,2},{2,0},{1,5},{5,9},... | collective-permute-start | bytes 786440 | tf_op jit(solution)/shard_map/ppermute | solution.py:32
  72.4 1.6 %collective-permute-start.26 = (bf16[256,512]{1,0:T(8,128)(2,1)S(1)}, bf16[256,512]{1,0:T(8,128)(2,1)S(1)}, u32[]{:S(2)}, u32[]{:S(2)}) collective-permute-start(bf16[256,512]{1,0:T(8,128)(2,1)S(1)} %convolution_convert_fusion.1), channel_id=1, source_target_pairs={{0,4},{4,8},{8,12},{12,14},{14,10},{10,6},{6,2},{2,0},{1,5},{5,9},... | collective-permute-start | bytes 786440 | tf_op jit(solution)/shard_map/ppermute | solution.py:32
  74.0 4.2 %collective-permute-done.25 = bf16[256,512]{1,0:T(8,128)(2,1)S(1)} collective-permute-done((bf16[256,512]{1,0:T(8,128)(2,1)S(1)}, bf16[256,512]{1,0:T(8,128)(2,1)S(1)}, u32[]{:S(2)}, u32[]{:S(2)}) %collective-permute-start.25) | collective-permute-done | bytes 262176 | tf_op jit(solution)/shard_map/ppermute | solution.py:32
  81.6 2.1 %collective-permute-done.27 = bf16[256,512]{1,0:T(8,128)(2,1)S(1)} collective-permute-done((bf16[256,512]{1,0:T(8,128)(2,1)S(1)}, bf16[256,512]{1,0:T(8,128)(2,1)S(1)}, u32[]{:S(2)}, u32[]{:S(2)}) %collective-permute-start.27) | collective-permute-done | bytes 262176 | tf_op jit(solution)/shard_map/ppermute | solution.py:32
  84.7 1.6 %collective-permute-start.30 = (bf16[256,512]{1,0:T(8,128)(2,1)S(1)}, bf16[256,512]{1,0:T(8,128)(2,1)S(1)}, u32[]{:S(2)}, u32[]{:S(2)}) collective-permute-start(bf16[256,512]{1,0:T(8,128)(2,1)S(1)} %fusion.5), channel_id=1, source_target_pairs={{0,4},{4,8},{8,12},{12,14},{14,10},{10,6},{6,2},{2,0},{1,5},{5,9},... | collective-permute-start | bytes 786440 | tf_op jit(solution)/shard_map/ppermute | solution.py:32
  86.9 1.8 %collective-permute-start.24 = (bf16[256,1024]{1,0:T(8,128)(2,1)S(1)}, bf16[256,1024]{1,0:T(8,128)(2,1)S(1)}, u32[]{:S(2)}, u32[]{:S(2)}) collective-permute-start(bf16[256,1024]{1,0:T(8,128)(2,1)S(1)} %convert_element_type.163), channel_id=1, source_target_pairs={{0,16},{1,17},{2,18},{3,19},{4,20},{5,21},{6,22},{7,23},{8,24},{9,... | collective-permute-start | bytes 1572872 | tf_op jit(solution)/shard_map/ppermute | solution.py:40
  90.3 1.8 %collective-permute-start.33 = (bf16[256,512]{1,0:T(8,128)(2,1)S(1)}, bf16[256,512]{1,0:T(8,128)(2,1)S(1)}, u32[]{:S(2)}, u32[]{:S(2)}) collective-permute-start(bf16[256,512]{1,0:T(8,128)(2,1)S(1)} %fusion.9), channel_id=1, source_target_pairs={{0,2},{4,0},{8,4},{12,8},{14,12},{10,14},{6,10},{2,6},{1,3},{5,1},... | collective-permute-start | bytes 786440 | tf_op jit(solution)/shard_map/ppermute | solution.py:32
  92.4 3.1 %collective-permute-done.30 = bf16[256,512]{1,0:T(8,128)(2,1)S(1)} collective-permute-done((bf16[256,512]{1,0:T(8,128)(2,1)S(1)}, bf16[256,512]{1,0:T(8,128)(2,1)S(1)}, u32[]{:S(2)}, u32[]{:S(2)}) %collective-permute-start.30) | collective-permute-done | bytes 262176 | tf_op jit(solution)/shard_map/ppermute | solution.py:32
  96.0 1.6 %collective-permute-start.36 = (bf16[256,512]{1,0:T(8,128)(2,1)S(1)}, bf16[256,512]{1,0:T(8,128)(2,1)S(1)}, u32[]{:S(2)}, u32[]{:S(2)}) collective-permute-start(bf16[256,512]{1,0:T(8,128)(2,1)S(1)} %fusion.3), channel_id=1, source_target_pairs={{0,4},{4,8},{8,12},{12,14},{14,10},{10,6},{6,2},{2,0},{1,5},{5,9},... | collective-permute-start | bytes 786440 | tf_op jit(solution)/shard_map/ppermute | solution.py:32
  98.0 1.9 %collective-permute-done.33 = bf16[256,512]{1,0:T(8,128)(2,1)S(1)} collective-permute-done((bf16[256,512]{1,0:T(8,128)(2,1)S(1)}, bf16[256,512]{1,0:T(8,128)(2,1)S(1)}, u32[]{:S(2)}, u32[]{:S(2)}) %collective-permute-start.33) | collective-permute-done | bytes 262176 | tf_op jit(solution)/shard_map/ppermute | solution.py:32
  99.8 1.5 %collective-permute-done.32 = bf16[256,512]{1,0:T(8,128)(2,1)S(1)} collective-permute-done((bf16[256,512]{1,0:T(8,128)(2,1)S(1)}, bf16[256,512]{1,0:T(8,128)(2,1)S(1)}, u32[]{:S(2)}, u32[]{:S(2)}) %collective-permute-start.32) | collective-permute-done | bytes 262176 | tf_op jit(solution)/shard_map/ppermute | solution.py:32
  102.2 1.6 %collective-permute-start.37 = (bf16[256,512]{1,0:T(8,128)(2,1)S(1)}, bf16[256,512]{1,0:T(8,128)(2,1)S(1)}, u32[]{:S(2)}, u32[]{:S(2)}) collective-permute-start(bf16[256,512]{1,0:T(8,128)(2,1)S(1)} %fusion.11), channel_id=1, source_target_pairs={{0,2},{4,0},{8,4},{12,8},{14,12},{10,14},{6,10},{2,6},{1,3},{5,1},... | collective-permute-start | bytes 786440 | tf_op jit(solution)/shard_map/ppermute | solution.py:32
  104.6 1.7 %collective-permute-start.35 = (bf16[256,512]{1,0:T(8,128)(2,1)S(1)}, bf16[256,512]{1,0:T(8,128)(2,1)S(1)}, u32[]{:S(2)}, u32[]{:S(2)}) collective-permute-start(bf16[256,512]{1,0:T(8,128)(2,1)S(1)} %fusion.10), channel_id=1, source_target_pairs={{0,2},{4,0},{8,4},{12,8},{14,12},{10,14},{6,10},{2,6},{1,3},{5,1},... | collective-permute-start | bytes 786440 | tf_op jit(solution)/shard_map/ppermute | solution.py:32
  107.2 3.6 %collective-permute-done.37 = bf16[256,512]{1,0:T(8,128)(2,1)S(1)} collective-permute-done((bf16[256,512]{1,0:T(8,128)(2,1)S(1)}, bf16[256,512]{1,0:T(8,128)(2,1)S(1)}, u32[]{:S(2)}, u32[]{:S(2)}) %collective-permute-start.37) | collective-permute-done | bytes 262176 | tf_op jit(solution)/shard_map/ppermute | solution.py:32
  111.0 2.6 %collective-permute-done.35 = bf16[256,512]{1,0:T(8,128)(2,1)S(1)} collective-permute-done((bf16[256,512]{1,0:T(8,128)(2,1)S(1)}, bf16[256,512]{1,0:T(8,128)(2,1)S(1)}, u32[]{:S(2)}, u32[]{:S(2)}) %collective-permute-start.35) | collective-permute-done | bytes 262176 | tf_op jit(solution)/shard_map/ppermute | solution.py:32
  (128 shorter events, 38.0 us)
Async XLA Ops:
  0.0 25.4 %collective-permute-start = (bf16[3,128,4096]{2,1,0:T(8,128)(2,1)}, bf16[3,128,4096]{2,1,0:T(8,128)(2,1)S(1)}, u32[]{:S(2)}, u32[]{:S(2)}) collective-permute-start(bf16[3,128,4096]{2,1,0:T(8,128)(2,1)} %bitcast.53), channel_id=1, source_target_pairs={{0,1},{1,0},{2,3},{3,2},{4,5},{5,4},{6,7},{7,6},{8,9},{9,8},{10,11... | collective-permute-start | bytes 9437192 | tf_op jit(solution)/shard_map/ppermute | solution.py:52
  1.8 9.7 %collective-permute-start.2 = (bf16[256,512]{1,0:T(8,128)(2,1)S(1)}, bf16[256,512]{1,0:T(8,128)(2,1)S(1)}, u32[]{:S(2)}, u32[]{:S(2)}) collective-permute-start(bf16[256,512]{1,0:T(8,128)(2,1)S(1)} %get-tuple-element.69), channel_id=1, source_target_pairs={{0,4},{4,8},{8,12},{12,14},{14,10},{10,6},{6,2},{2,0},{1,5},{5,9},... | collective-permute-start | bytes 786440 | tf_op jit(solution)/shard_map/ppermute | solution.py:32
  4.9 9.2 %collective-permute-start.3 = (bf16[256,512]{1,0:T(8,128)(2,1)S(1)}, bf16[256,512]{1,0:T(8,128)(2,1)S(1)}, u32[]{:S(2)}, u32[]{:S(2)}) collective-permute-start(bf16[256,512]{1,0:T(8,128)(2,1)S(1)} %get-tuple-element.69), channel_id=1, source_target_pairs={{0,2},{4,0},{8,4},{12,8},{14,12},{10,14},{6,10},{2,6},{1,3},{5,1},... | collective-permute-start | bytes 786440 | tf_op jit(solution)/shard_map/ppermute | solution.py:32
  6.1 14.8 %collective-permute-start.5 = (bf16[256,512]{1,0:T(8,128)(2,1)S(1)}, bf16[256,512]{1,0:T(8,128)(2,1)S(1)}, u32[]{:S(2)}, u32[]{:S(2)}) collective-permute-start(bf16[256,512]{1,0:T(8,128)(2,1)S(1)} %collective-permute-done.1), channel_id=1, source_target_pairs={{0,2},{4,0},{8,4},{12,8},{14,12},{10,14},{6,10},{2,6},{1,3},{5,1},... | collective-permute-start | bytes 786440 | tf_op jit(solution)/shard_map/ppermute | solution.py:32
  9.0 12.0 %collective-permute-start.4 = (bf16[256,512]{1,0:T(8,128)(2,1)S(1)}, bf16[256,512]{1,0:T(8,128)(2,1)S(1)}, u32[]{:S(2)}, u32[]{:S(2)}) collective-permute-start(bf16[256,512]{1,0:T(8,128)(2,1)S(1)} %collective-permute-done.1), channel_id=1, source_target_pairs={{0,4},{4,8},{8,12},{12,14},{14,10},{10,6},{6,2},{2,0},{1,5},{5,9},... | collective-permute-start | bytes 786440 | tf_op jit(solution)/shard_map/ppermute | solution.py:32
  11.5 11.9 %collective-permute-start.7 = (bf16[256,512]{1,0:T(8,128)(2,1)S(1)}, bf16[256,512]{1,0:T(8,128)(2,1)S(1)}, u32[]{:S(2)}, u32[]{:S(2)}) collective-permute-start(bf16[256,512]{1,0:T(8,128)(2,1)S(1)} %collective-permute-done.2), channel_id=1, source_target_pairs={{0,4},{4,8},{8,12},{12,14},{14,10},{10,6},{6,2},{2,0},{1,5},{5,9},... | collective-permute-start | bytes 786440 | tf_op jit(solution)/shard_map/ppermute | solution.py:32
  14.1 11.2 %collective-permute-start.8 = (bf16[256,512]{1,0:T(8,128)(2,1)S(1)}, bf16[256,512]{1,0:T(8,128)(2,1)S(1)}, u32[]{:S(2)}, u32[]{:S(2)}) collective-permute-start(bf16[256,512]{1,0:T(8,128)(2,1)S(1)} %collective-permute-done.3), channel_id=1, source_target_pairs={{0,2},{4,0},{8,4},{12,8},{14,12},{10,14},{6,10},{2,6},{1,3},{5,1},... | collective-permute-start | bytes 786440 | tf_op jit(solution)/shard_map/ppermute | solution.py:32
  21.0 11.3 %collective-permute-start.9 = (bf16[256,512]{1,0:T(8,128)(2,1)S(1)}, bf16[256,512]{1,0:T(8,128)(2,1)S(1)}, u32[]{:S(2)}, u32[]{:S(2)}) collective-permute-start(bf16[256,512]{1,0:T(8,128)(2,1)S(1)} %collective-permute-done.4), channel_id=1, source_target_pairs={{0,4},{4,8},{8,12},{12,14},{14,10},{10,6},{6,2},{2,0},{1,5},{5,9},... | collective-permute-start | bytes 786440 | tf_op jit(solution)/shard_map/ppermute | solution.py:32
  23.0 11.1 %collective-permute-start.10 = (bf16[256,512]{1,0:T(8,128)(2,1)S(1)}, bf16[256,512]{1,0:T(8,128)(2,1)S(1)}, u32[]{:S(2)}, u32[]{:S(2)}) collective-permute-start(bf16[256,512]{1,0:T(8,128)(2,1)S(1)} %collective-permute-done.5), channel_id=1, source_target_pairs={{0,2},{4,0},{8,4},{12,8},{14,12},{10,14},{6,10},{2,6},{1,3},{5,1},... | collective-permute-start | bytes 786440 | tf_op jit(solution)/shard_map/ppermute | solution.py:32
  23.4 10.9 %collective-permute-start.11 = (bf16[256,512]{1,0:T(8,128)(2,1)S(1)}, bf16[256,512]{1,0:T(8,128)(2,1)S(1)}, u32[]{:S(2)}, u32[]{:S(2)}) collective-permute-start(bf16[256,512]{1,0:T(8,128)(2,1)S(1)} %collective-permute-done.7), channel_id=1, source_target_pairs={{0,4},{4,8},{8,12},{12,14},{14,10},{10,6},{6,2},{2,0},{1,5},{5,9},... | collective-permute-start | bytes 786440 | tf_op jit(solution)/shard_map/ppermute | solution.py:32
  25.3 25.2 %collective-permute-start.12 = (bf16[256,512]{1,0:T(8,128)(2,1)S(1)}, bf16[256,512]{1,0:T(8,128)(2,1)S(1)}, u32[]{:S(2)}, u32[]{:S(2)}) collective-permute-start(bf16[256,512]{1,0:T(8,128)(2,1)S(1)} %collective-permute-done.8), channel_id=1, source_target_pairs={{0,2},{4,0},{8,4},{12,8},{14,12},{10,14},{6,10},{2,6},{1,3},{5,1},... | collective-permute-start | bytes 786440 | tf_op jit(solution)/shard_map/ppermute | solution.py:32
  32.2 11.0 %collective-permute-start.13 = (bf16[256,512]{1,0:T(8,128)(2,1)S(1)}, bf16[256,512]{1,0:T(8,128)(2,1)S(1)}, u32[]{:S(2)}, u32[]{:S(2)}) collective-permute-start(bf16[256,512]{1,0:T(8,128)(2,1)S(1)} %collective-permute-done.9), channel_id=1, source_target_pairs={{0,4},{4,8},{8,12},{12,14},{14,10},{10,6},{6,2},{2,0},{1,5},{5,9},... | collective-permute-start | bytes 786440 | tf_op jit(solution)/shard_map/ppermute | solution.py:32
  34.2 8.4 %collective-permute-start.14 = (bf16[256,512]{1,0:T(8,128)(2,1)S(1)}, bf16[256,512]{1,0:T(8,128)(2,1)S(1)}, u32[]{:S(2)}, u32[]{:S(2)}) collective-permute-start(bf16[256,512]{1,0:T(8,128)(2,1)S(1)} %collective-permute-done.10), channel_id=1, source_target_pairs={{0,2},{4,0},{8,4},{12,8},{14,12},{10,14},{6,10},{2,6},{1,3},{5,1},... | collective-permute-start | bytes 786440 | tf_op jit(solution)/shard_map/ppermute | solution.py:32
  34.4 12.3 %collective-permute-start.15 = (bf16[256,512]{1,0:T(8,128)(2,1)S(1)}, bf16[256,512]{1,0:T(8,128)(2,1)S(1)}, u32[]{:S(2)}, u32[]{:S(2)}) collective-permute-start(bf16[256,512]{1,0:T(8,128)(2,1)S(1)} %collective-permute-done.11), channel_id=1, source_target_pairs={{0,4},{4,8},{8,12},{12,14},{14,10},{10,6},{6,2},{2,0},{1,5},{5,9},... | collective-permute-start | bytes 786440 | tf_op jit(solution)/shard_map/ppermute | solution.py:32
  42.5 7.5 %collective-permute-start.16 = (bf16[256,512]{1,0:T(8,128)(2,1)S(1)}, bf16[256,512]{1,0:T(8,128)(2,1)S(1)}, u32[]{:S(2)}, u32[]{:S(2)}) collective-permute-start(bf16[256,512]{1,0:T(8,128)(2,1)S(1)} %collective-permute-done.14), channel_id=1, source_target_pairs={{0,2},{4,0},{8,4},{12,8},{14,12},{10,14},{6,10},{2,6},{1,3},{5,1},... | collective-permute-start | bytes 786440 | tf_op jit(solution)/shard_map/ppermute | solution.py:32
  55.6 7.6 %collective-permute-start.20 = (bf16[6,1024]{1,0:T(8,128)(2,1)S(1)}, bf16[6,1024]{1,0:T(8,128)(2,1)S(1)}, u32[]{:S(2)}, u32[]{:S(2)}) collective-permute-start(bf16[6,1024]{1,0:T(8,128)(2,1)S(1)} %maximum_select_fusion.2), channel_id=1, source_target_pairs={{24,0},{23,1},{28,4},{19,5},{30,8},{17,9},{26,12},{21,13},{22,14},... | collective-permute-start | bytes 36872 | tf_op jit(solution)/shard_map/ppermute | solution.py:64
  56.9 8.6 %collective-permute-start.21 = (bf16[6,1024]{1,0:T(8,128)(2,1)S(1)}, bf16[6,1024]{1,0:T(8,128)(2,1)S(1)}, u32[]{:S(2)}, u32[]{:S(2)}) collective-permute-start(bf16[6,1024]{1,0:T(8,128)(2,1)S(1)} %maximum_select_fusion.2), channel_id=1, source_target_pairs={{28,0},{19,1},{30,4},{17,5},{26,8},{21,9},{22,12},{25,13},{18,14},... | collective-permute-start | bytes 36872 | tf_op jit(solution)/shard_map/ppermute | solution.py:64
  68.9 9.2 %collective-permute-start.25 = (bf16[256,512]{1,0:T(8,128)(2,1)S(1)}, bf16[256,512]{1,0:T(8,128)(2,1)S(1)}, u32[]{:S(2)}, u32[]{:S(2)}) collective-permute-start(bf16[256,512]{1,0:T(8,128)(2,1)S(1)} %convolution_convert_fusion.2), channel_id=1, source_target_pairs={{0,2},{4,0},{8,4},{12,8},{14,12},{10,14},{6,10},{2,6},{1,3},{5,1},... | collective-permute-start | bytes 786440 | tf_op jit(solution)/shard_map/ppermute | solution.py:32
  69.5 9.2 %collective-permute-start.23 = (bf16[256,512]{1,0:T(8,128)(2,1)S(1)}, bf16[256,512]{1,0:T(8,128)(2,1)S(1)}, u32[]{:S(2)}, u32[]{:S(2)}) collective-permute-start(bf16[256,512]{1,0:T(8,128)(2,1)S(1)} %convolution_convert_fusion.3), channel_id=1, source_target_pairs={{0,4},{4,8},{8,12},{12,14},{14,10},{10,6},{6,2},{2,0},{1,5},{5,9},... | collective-permute-start | bytes 786440 | tf_op jit(solution)/shard_map/ppermute | solution.py:32
  71.4 12.3 %collective-permute-start.27 = (bf16[256,512]{1,0:T(8,128)(2,1)S(1)}, bf16[256,512]{1,0:T(8,128)(2,1)S(1)}, u32[]{:S(2)}, u32[]{:S(2)}) collective-permute-start(bf16[256,512]{1,0:T(8,128)(2,1)S(1)} %convolution_convert_fusion), channel_id=1, source_target_pairs={{0,2},{4,0},{8,4},{12,8},{14,12},{10,14},{6,10},{2,6},{1,3},{5,1},... | collective-permute-start | bytes 786440 | tf_op jit(solution)/shard_map/ppermute | solution.py:32
  72.4 11.9 %collective-permute-start.26 = (bf16[256,512]{1,0:T(8,128)(2,1)S(1)}, bf16[256,512]{1,0:T(8,128)(2,1)S(1)}, u32[]{:S(2)}, u32[]{:S(2)}) collective-permute-start(bf16[256,512]{1,0:T(8,128)(2,1)S(1)} %convolution_convert_fusion.1), channel_id=1, source_target_pairs={{0,4},{4,8},{8,12},{12,14},{14,10},{10,6},{6,2},{2,0},{1,5},{5,9},... | collective-permute-start | bytes 786440 | tf_op jit(solution)/shard_map/ppermute | solution.py:32
  79.5 9.8 %collective-permute-start.29 = (bf16[256,512]{1,0:T(8,128)(2,1)S(1)}, bf16[256,512]{1,0:T(8,128)(2,1)S(1)}, u32[]{:S(2)}, u32[]{:S(2)}) collective-permute-start(bf16[256,512]{1,0:T(8,128)(2,1)S(1)} %fusion.7), channel_id=1, source_target_pairs={{0,2},{4,0},{8,4},{12,8},{14,12},{10,14},{6,10},{2,6},{1,3},{5,1},... | collective-permute-start | bytes 786440 | tf_op jit(solution)/shard_map/ppermute | solution.py:32
  80.3 9.6 %collective-permute-start.28 = (bf16[256,512]{1,0:T(8,128)(2,1)S(1)}, bf16[256,512]{1,0:T(8,128)(2,1)S(1)}, u32[]{:S(2)}, u32[]{:S(2)}) collective-permute-start(bf16[256,512]{1,0:T(8,128)(2,1)S(1)} %fusion.6), channel_id=1, source_target_pairs={{0,4},{4,8},{8,12},{12,14},{14,10},{10,6},{6,2},{2,0},{1,5},{5,9},... | collective-permute-start | bytes 786440 | tf_op jit(solution)/shard_map/ppermute | solution.py:32
  84.7 10.8 %collective-permute-start.30 = (bf16[256,512]{1,0:T(8,128)(2,1)S(1)}, bf16[256,512]{1,0:T(8,128)(2,1)S(1)}, u32[]{:S(2)}, u32[]{:S(2)}) collective-permute-start(bf16[256,512]{1,0:T(8,128)(2,1)S(1)} %fusion.5), channel_id=1, source_target_pairs={{0,4},{4,8},{8,12},{12,14},{14,10},{10,6},{6,2},{2,0},{1,5},{5,9},... | collective-permute-start | bytes 786440 | tf_op jit(solution)/shard_map/ppermute | solution.py:32
  86.3 11.2 %collective-permute-start.31 = (bf16[256,512]{1,0:T(8,128)(2,1)S(1)}, bf16[256,512]{1,0:T(8,128)(2,1)S(1)}, u32[]{:S(2)}, u32[]{:S(2)}) collective-permute-start(bf16[256,512]{1,0:T(8,128)(2,1)S(1)} %fusion.8), channel_id=1, source_target_pairs={{0,2},{4,0},{8,4},{12,8},{14,12},{10,14},{6,10},{2,6},{1,3},{5,1},... | collective-permute-start | bytes 786440 | tf_op jit(solution)/shard_map/ppermute | solution.py:32
  86.9 15.3 %collective-permute-start.24 = (bf16[256,1024]{1,0:T(8,128)(2,1)S(1)}, bf16[256,1024]{1,0:T(8,128)(2,1)S(1)}, u32[]{:S(2)}, u32[]{:S(2)}) collective-permute-start(bf16[256,1024]{1,0:T(8,128)(2,1)S(1)} %convert_element_type.163), channel_id=1, source_target_pairs={{0,16},{1,17},{2,18},{3,19},{4,20},{5,21},{6,22},{7,23},{8,24},{9,... | collective-permute-start | bytes 1572872 | tf_op jit(solution)/shard_map/ppermute | solution.py:40
  90.3 9.5 %collective-permute-start.33 = (bf16[256,512]{1,0:T(8,128)(2,1)S(1)}, bf16[256,512]{1,0:T(8,128)(2,1)S(1)}, u32[]{:S(2)}, u32[]{:S(2)}) collective-permute-start(bf16[256,512]{1,0:T(8,128)(2,1)S(1)} %fusion.9), channel_id=1, source_target_pairs={{0,2},{4,0},{8,4},{12,8},{14,12},{10,14},{6,10},{2,6},{1,3},{5,1},... | collective-permute-start | bytes 786440 | tf_op jit(solution)/shard_map/ppermute | solution.py:32
  92.1 9.2 %collective-permute-start.32 = (bf16[256,512]{1,0:T(8,128)(2,1)S(1)}, bf16[256,512]{1,0:T(8,128)(2,1)S(1)}, u32[]{:S(2)}, u32[]{:S(2)}) collective-permute-start(bf16[256,512]{1,0:T(8,128)(2,1)S(1)} %fusion.4), channel_id=1, source_target_pairs={{0,4},{4,8},{8,12},{12,14},{14,10},{10,6},{6,2},{2,0},{1,5},{5,9},... | collective-permute-start | bytes 786440 | tf_op jit(solution)/shard_map/ppermute | solution.py:32
  96.0 10.4 %collective-permute-start.36 = (bf16[256,512]{1,0:T(8,128)(2,1)S(1)}, bf16[256,512]{1,0:T(8,128)(2,1)S(1)}, u32[]{:S(2)}, u32[]{:S(2)}) collective-permute-start(bf16[256,512]{1,0:T(8,128)(2,1)S(1)} %fusion.3), channel_id=1, source_target_pairs={{0,4},{4,8},{8,12},{12,14},{14,10},{10,6},{6,2},{2,0},{1,5},{5,9},... | collective-permute-start | bytes 786440 | tf_op jit(solution)/shard_map/ppermute | solution.py:32
  102.2 8.6 %collective-permute-start.37 = (bf16[256,512]{1,0:T(8,128)(2,1)S(1)}, bf16[256,512]{1,0:T(8,128)(2,1)S(1)}, u32[]{:S(2)}, u32[]{:S(2)}) collective-permute-start(bf16[256,512]{1,0:T(8,128)(2,1)S(1)} %fusion.11), channel_id=1, source_target_pairs={{0,2},{4,0},{8,4},{12,8},{14,12},{10,14},{6,10},{2,6},{1,3},{5,1},... | collective-permute-start | bytes 786440 | tf_op jit(solution)/shard_map/ppermute | solution.py:32
  104.6 9.0 %collective-permute-start.35 = (bf16[256,512]{1,0:T(8,128)(2,1)S(1)}, bf16[256,512]{1,0:T(8,128)(2,1)S(1)}, u32[]{:S(2)}, u32[]{:S(2)}) collective-permute-start(bf16[256,512]{1,0:T(8,128)(2,1)S(1)} %fusion.10), channel_id=1, source_target_pairs={{0,2},{4,0},{8,4},{12,8},{14,12},{10,14},{6,10},{2,6},{1,3},{5,1},... | collective-permute-start | bytes 786440 | tf_op jit(solution)/shard_map/ppermute | solution.py:32
  106.3 7.3 %collective-permute-start.34 = (bf16[256,512]{1,0:T(8,128)(2,1)S(1)}, bf16[256,512]{1,0:T(8,128)(2,1)S(1)}, u32[]{:S(2)}, u32[]{:S(2)}) collective-permute-start(bf16[256,512]{1,0:T(8,128)(2,1)S(1)} %fusion.2), channel_id=1, source_target_pairs={{0,4},{4,8},{8,12},{12,14},{14,10},{10,6},{6,2},{2,0},{1,5},{5,9},... | collective-permute-start | bytes 786440 | tf_op jit(solution)/shard_map/ppermute | solution.py:32
  (12 other events, 39.9 us)

commit v21 on v19

--- a/solution.py
+++ b/solution.py
@@ -133,9 +133,7 @@
         for i in range(2)
     }
     scalars = [first_core, shift, own_columns, given_columns, trainer, *starts.values()]
-    weights, *scalars = lax.optimization_barrier([master[0], *scalars])
-    first_core, shift, own_columns, given_columns, trainer, *firsts = scalars
-    starts = dict(zip(starts, firsts))
+    weights = after(scalars, master[0])
     own = cut(weights, 1, own_columns, half).astype(jnp.bfloat16)
     given = cut(weights, 1, given_columns, half).astype(jnp.bfloat16)
     sibling = from_sibling(given)
@@ -164,9 +162,9 @@
             for i, by in four if last else four + three:
                 if step > 1:
                     if last and step > 2:
-                        moving[i, by] = after(sums[1], moving[i, by])
-                    elif step in (2, 3) and (i, by) in three:
-                        moving[i, by] = after((normed_own, normed)[step - 2], moving[i, by])
+                        moving[i, by] = after(normed, moving[i, by])
+                    elif step == 3 and (i, by) in four:
+                        moving[i, by] = after(normed_own, moving[i, by])
                     moving[i, by] = along_ring(moving[i, by], by)
                 total = total + product(-by * step, i, moving[i, by])
             sums[step] = total
@@ -272,6 +270,7 @@
                 copied = passed_on(weights)
             else:
                 source = late
+        late = after([arrived[way] for way in three], delta)
         owns = [term(0, i, late) for i in range(2)]
         arrived[1, 1] = after(owns, arrived[1, 1])
         arrived[0, -1] = after(owns, arrived[0, -1])

time: 119 us -> 123 us (1.034)
  waiting for transfers between devices: 41.3 us -> 50 us
  matrix products: 18.5 us -> 14.8 us
    ppermute x28, waiting for transfers between devices: 30.2 us -> 37.8 us  [along_ring(): return lax.ppermute(block, 'chip', pairs)]
    dot_general x16, matrix products: 9.32 us -> 6.6 us  [term(): lax.dot_general(columns(offset, i), delta, (((0,), (0,)), ((), ())), pref...]
  transfers between devices with their start and end apart: 39 -> 39, of which waited for: 24 -> 25; matrix products, arithmetic and copies ran while one was open for 16% -> 13% of each run, Pallas kernels for 6% -> 6%
where the time goes in v21:
time: 123 us
  waiting for transfers between devices  50 us (41%)
  starting transfers between devices  42 us (34%)
  matrix products  14.8 us (12%)
  Pallas kernels  7.16 us (6%)
  local copies, waits for them, and re-layouts  4.88 us (4%)
  other arithmetic  3.22 us (3%)
    ppermute x28, waiting for transfers between devices, along_ring(): return lax.ppermute(block, 'chip', pairs)  37.8 us
    ppermute x28, starting transfers between devices, along_ring(): return lax.ppermute(block, 'chip', pairs)  34.7 us
    ppermute x4, waiting for transfers between devices, slab_blocks(): kept.append(lax.ppermute(stored, ('grp', 'chip', 'core'), pairs))  7.39 us
    pallas_call x2, Pallas kernels, normalize(): pl.pallas_call(functools.partial(normalize_kernel, 16), grid=(seqs,), in_...  7.16 us
    dot_general x16, matrix products, product(): jnp.dot(columns(offset, i), block, preferred_element_type=jnp.float32)  6.65 us
    dot_general x16, matrix products, term(): lax.dot_general(columns(offset, i), delta, (((0,), (0,)), ((), ())), pref...  6.6 us
    ppermute x4, starting transfers between devices, slab_blocks(): kept.append(lax.ppermute(stored, ('grp', 'chip', 'core'), pairs))  5.16 us
    ppermute x6, waiting for transfers between devices, from_sibling(): return lax.ppermute(block, 'core', [(0, 1), (1, 0)])  3.68 us
  transfers between devices with their start and end apart: 39, of which 25 were waited for; matrix products, arithmetic and copies ran while one was open for 13% of the time, Pallas kernels for 6%

profile of v21, /device:TPU:0, one launch (start us, length us, event | category | flops | bytes accessed | tf_op | source)
XLA Modules:
  0.0 122.6 jit_solution(1237038090745199679)
XLA Ops:
  1.8 3.0 %collective-permute-start.2 = (bf16[256,512]{1,0:T(8,128)(2,1)S(1)}, bf16[256,512]{1,0:T(8,128)(2,1)S(1)}, u32[]{:S(2)}, u32[]{:S(2)}) collective-permute-start(bf16[256,512]{1,0:T(8,128)(2,1)S(1)} %get-tuple-element.32), channel_id=1, source_target_pairs={{0,4},{4,8},{8,12},{12,14},{14,10},{10,6},{6,2},{2,0},{1,5},{5,9},... | collective-permute-start | bytes 786440 | tf_op jit(solution)/shard_map/ppermute | solution.py:32
  6.1 2.9 %collective-permute-start.3 = (bf16[256,512]{1,0:T(8,128)(2,1)S(1)}, bf16[256,512]{1,0:T(8,128)(2,1)S(1)}, u32[]{:S(2)}, u32[]{:S(2)}) collective-permute-start(bf16[256,512]{1,0:T(8,128)(2,1)S(1)} %collective-permute-done.1), channel_id=1, source_target_pairs={{0,2},{4,0},{8,4},{12,8},{14,12},{10,14},{6,10},{2,6},{1,3},{5,1},... | collective-permute-start | bytes 786440 | tf_op jit(solution)/shard_map/ppermute | solution.py:32
  9.0 1.6 %collective-permute-start.5 = (bf16[256,512]{1,0:T(8,128)(2,1)S(1)}, bf16[256,512]{1,0:T(8,128)(2,1)S(1)}, u32[]{:S(2)}, u32[]{:S(2)}) collective-permute-start(bf16[256,512]{1,0:T(8,128)(2,1)S(1)} %get-tuple-element.32), channel_id=1, source_target_pairs={{0,2},{4,0},{8,4},{12,8},{14,12},{10,14},{6,10},{2,6},{1,3},{5,1},... | collective-permute-start | bytes 786440 | tf_op jit(solution)/shard_map/ppermute | solution.py:32
  11.3 1.8 %collective-permute-start.7 = (bf16[256,512]{1,0:T(8,128)(2,1)S(1)}, bf16[256,512]{1,0:T(8,128)(2,1)S(1)}, u32[]{:S(2)}, u32[]{:S(2)}) collective-permute-start(bf16[256,512]{1,0:T(8,128)(2,1)S(1)} %collective-permute-done.2), channel_id=1, source_target_pairs={{0,4},{4,8},{8,12},{12,14},{14,10},{10,6},{6,2},{2,0},{1,5},{5,9},... | collective-permute-start | bytes 786440 | tf_op jit(solution)/shard_map/ppermute | solution.py:32
  13.1 3.0 %collective-permute-done.3 = bf16[256,512]{1,0:T(8,128)(2,1)S(1)} collective-permute-done((bf16[256,512]{1,0:T(8,128)(2,1)S(1)}, bf16[256,512]{1,0:T(8,128)(2,1)S(1)}, u32[]{:S(2)}, u32[]{:S(2)}) %collective-permute-start.3) | collective-permute-done | bytes 262176 | tf_op jit(solution)/shard_map/ppermute | solution.py:32
  16.1 2.0 %collective-permute-start.8 = (bf16[256,512]{1,0:T(8,128)(2,1)S(1)}, bf16[256,512]{1,0:T(8,128)(2,1)S(1)}, u32[]{:S(2)}, u32[]{:S(2)}) collective-permute-start(bf16[256,512]{1,0:T(8,128)(2,1)S(1)} %collective-permute-done.3), channel_id=1, source_target_pairs={{0,2},{4,0},{8,4},{12,8},{14,12},{10,14},{6,10},{2,6},{1,3},{5,1},... | collective-permute-start | bytes 786440 | tf_op jit(solution)/shard_map/ppermute | solution.py:32
  18.2 3.6 %collective-permute-done.5 = bf16[256,512]{1,0:T(8,128)(2,1)S(1)} collective-permute-done((bf16[256,512]{1,0:T(8,128)(2,1)S(1)}, bf16[256,512]{1,0:T(8,128)(2,1)S(1)}, u32[]{:S(2)}, u32[]{:S(2)}) %collective-permute-start.5) | collective-permute-done | bytes 262176 | tf_op jit(solution)/shard_map/ppermute | solution.py:32
  21.8 2.0 %collective-permute-start.10 = (bf16[256,512]{1,0:T(8,128)(2,1)S(1)}, bf16[256,512]{1,0:T(8,128)(2,1)S(1)}, u32[]{:S(2)}, u32[]{:S(2)}) collective-permute-start(bf16[256,512]{1,0:T(8,128)(2,1)S(1)} %collective-permute-done.5), channel_id=1, source_target_pairs={{0,2},{4,0},{8,4},{12,8},{14,12},{10,14},{6,10},{2,6},{1,3},{5,1},... | collective-permute-start | bytes 786440 | tf_op jit(solution)/shard_map/ppermute | solution.py:32
  24.5 1.9 %copy-done = bf16[1,3,128,4096]{3,2,1,0:T(8,128)(2,1)S(1)} copy-done((bf16[1,3,128,4096]{3,2,1,0:T(8,128)(2,1)S(1)}, bf16[1,3,128,4096]{3,2,1,0:T(8,128)(2,1)}, u32[]{:S(2)}) %copy-start) | copy-done | bytes 3145752
  27.1 3.6 %shard_map.64.refs_0_ = bf16[768,4096]{1,0:T(8,128)(2,1)S(1)} custom-call(bf16[3,128,4096]{2,1,0:T(8,128)(2,1)S(1)} %bitcast.54, f32[1,4096]{1,0:T(1,128)S(1)} %bitcast.55), custom_call_target="tpu_custom_call" | custom-call | flops 9437184 | bytes 6291456 | tf_op jit(solution)/shard_map/pallas_call | solution.py:99
  30.7 2.1 %collective-permute-start.11 = (bf16[256,512]{1,0:T(8,128)(2,1)S(1)}, bf16[256,512]{1,0:T(8,128)(2,1)S(1)}, u32[]{:S(2)}, u32[]{:S(2)}) collective-permute-start(bf16[256,512]{1,0:T(8,128)(2,1)S(1)} %collective-permute-done.7), channel_id=1, source_target_pairs={{0,4},{4,8},{8,12},{12,14},{14,10},{10,6},{6,2},{2,0},{1,5},{5,9},... | collective-permute-start | bytes 786440 | tf_op jit(solution)/shard_map/ppermute | solution.py:32
  32.8 2.0 %collective-permute-start.14 = (bf16[256,512]{1,0:T(8,128)(2,1)S(1)}, bf16[256,512]{1,0:T(8,128)(2,1)S(1)}, u32[]{:S(2)}, u32[]{:S(2)}) collective-permute-start(bf16[256,512]{1,0:T(8,128)(2,1)S(1)} %collective-permute-done.10), channel_id=1, source_target_pairs={{0,2},{4,0},{8,4},{12,8},{14,12},{10,14},{6,10},{2,6},{1,3},{5,1},... | collective-permute-start | bytes 786440 | tf_op jit(solution)/shard_map/ppermute | solution.py:32
  34.9 3.6 %shard_map.65 = bf16[768,4096]{1,0:T(8,128)(2,1)S(1)} custom-call(bf16[3,128,4096]{2,1,0:T(8,128)(2,1)S(1)} %collective-permute-done.states_ref, f32[1,4096]{1,0:T(1,128)S(1)} %bitcast.56, bf16[768,4096]{1,0:T(8,128)(2,1)S(1)} %shard_map.64.refs_0_), custom_call_target="tpu_custom_call", output_to_operand_aliasing={{}: (2, {})} | custom-call | flops 9437184 | bytes 6291456 | tf_op jit(solution)/shard_map/pallas_call | solution.py:99
  41.7 2.0 %collective-permute-start.15 = (bf16[256,512]{1,0:T(8,128)(2,1)S(1)}, bf16[256,512]{1,0:T(8,128)(2,1)S(1)}, u32[]{:S(2)}, u32[]{:S(2)}) collective-permute-start(bf16[256,512]{1,0:T(8,128)(2,1)S(1)} %collective-permute-done.11), channel_id=1, source_target_pairs={{0,4},{4,8},{8,12},{12,14},{14,10},{10,6},{6,2},{2,0},{1,5},{5,9},... | collective-permute-start | bytes 786440 | tf_op jit(solution)/shard_map/ppermute | solution.py:32
  46.9 3.6 %collective-permute-done.15 = bf16[256,512]{1,0:T(8,128)(2,1)S(1)} collective-permute-done((bf16[256,512]{1,0:T(8,128)(2,1)S(1)}, bf16[256,512]{1,0:T(8,128)(2,1)S(1)}, u32[]{:S(2)}, u32[]{:S(2)}) %collective-permute-start.15) | collective-permute-done | bytes 262176 | tf_op jit(solution)/shard_map/ppermute | solution.py:32
  56.5 1.3 %collective-permute-start.19 = (bf16[6,1024]{1,0:T(8,128)(2,1)S(1)}, bf16[6,1024]{1,0:T(8,128)(2,1)S(1)}, u32[]{:S(2)}, u32[]{:S(2)}) collective-permute-start(bf16[6,1024]{1,0:T(8,128)(2,1)S(1)} %maximum_select_fusion.2), channel_id=1, source_target_pairs={{20,0},{27,1},{24,4},{23,5},{28,8},{19,9},{30,12},{17,13},{26,14},... | collective-permute-start | bytes 36872 | tf_op jit(solution)/shard_map/ppermute | solution.py:64
  60.9 2.3 %collective-permute-done.19 = bf16[6,1024]{1,0:T(8,128)(2,1)S(1)} collective-permute-done((bf16[6,1024]{1,0:T(8,128)(2,1)S(1)}, bf16[6,1024]{1,0:T(8,128)(2,1)S(1)}, u32[]{:S(2)}, u32[]{:S(2)}) %collective-permute-start.19) | collective-permute-done | bytes 12320 | tf_op jit(solution)/shard_map/ppermute | solution.py:64
  63.2 2.3 %collective-permute-done.20 = bf16[6,1024]{1,0:T(8,128)(2,1)S(1)} collective-permute-done((bf16[6,1024]{1,0:T(8,128)(2,1)S(1)}, bf16[6,1024]{1,0:T(8,128)(2,1)S(1)}, u32[]{:S(2)}, u32[]{:S(2)}) %collective-permute-start.20) | collective-permute-done | bytes 12320 | tf_op jit(solution)/shard_map/ppermute | solution.py:64
  65.5 2.4 %collective-permute-done.21 = bf16[6,1024]{1,0:T(8,128)(2,1)S(1)} collective-permute-done((bf16[6,1024]{1,0:T(8,128)(2,1)S(1)}, bf16[6,1024]{1,0:T(8,128)(2,1)S(1)}, u32[]{:S(2)}, u32[]{:S(2)}) %collective-permute-start.21) | collective-permute-done | bytes 12320 | tf_op jit(solution)/shard_map/ppermute | solution.py:64
  71.7 1.6 %collective-permute-start.23 = (bf16[256,512]{1,0:T(8,128)(2,1)S(1)}, bf16[256,512]{1,0:T(8,128)(2,1)S(1)}, u32[]{:S(2)}, u32[]{:S(2)}) collective-permute-start(bf16[256,512]{1,0:T(8,128)(2,1)S(1)} %convolution_convert_fusion.3), channel_id=1, source_target_pairs={{0,4},{4,8},{8,12},{12,14},{14,10},{10,6},{6,2},{2,0},{1,5},{5,9},... | collective-permute-start | bytes 786440 | tf_op jit(solution)/shard_map/ppermute | solution.py:32
  74.6 1.7 %collective-permute-start.25 = (bf16[256,512]{1,0:T(8,128)(2,1)S(1)}, bf16[256,512]{1,0:T(8,128)(2,1)S(1)}, u32[]{:S(2)}, u32[]{:S(2)}) collective-permute-start(bf16[256,512]{1,0:T(8,128)(2,1)S(1)} %convolution_convert_fusion.1), channel_id=1, source_target_pairs={{0,4},{4,8},{8,12},{12,14},{14,10},{10,6},{6,2},{2,0},{1,5},{5,9},... | collective-permute-start | bytes 786440 | tf_op jit(solution)/shard_map/ppermute | solution.py:32
  76.3 4.2 %collective-permute-done.24 = bf16[256,512]{1,0:T(8,128)(2,1)S(1)} collective-permute-done((bf16[256,512]{1,0:T(8,128)(2,1)S(1)}, bf16[256,512]{1,0:T(8,128)(2,1)S(1)}, u32[]{:S(2)}, u32[]{:S(2)}) %collective-permute-start.24) | collective-permute-done | bytes 262176 | tf_op jit(solution)/shard_map/ppermute | solution.py:32
  83.8 2.2 %collective-permute-done.26 = bf16[256,512]{1,0:T(8,128)(2,1)S(1)} collective-permute-done((bf16[256,512]{1,0:T(8,128)(2,1)S(1)}, bf16[256,512]{1,0:T(8,128)(2,1)S(1)}, u32[]{:S(2)}, u32[]{:S(2)}) %collective-permute-start.26) | collective-permute-done | bytes 262176 | tf_op jit(solution)/shard_map/ppermute | solution.py:32
  89.0 2.7 %collective-permute-done.28 = bf16[256,512]{1,0:T(8,128)(2,1)S(1)} collective-permute-done((bf16[256,512]{1,0:T(8,128)(2,1)S(1)}, bf16[256,512]{1,0:T(8,128)(2,1)S(1)}, u32[]{:S(2)}, u32[]{:S(2)}) %collective-permute-start.28) | collective-permute-done | bytes 262176 | tf_op jit(solution)/shard_map/ppermute | solution.py:32
  92.6 4.0 %collective-permute-done.31 = bf16[256,512]{1,0:T(8,128)(2,1)S(1)} collective-permute-done((bf16[256,512]{1,0:T(8,128)(2,1)S(1)}, bf16[256,512]{1,0:T(8,128)(2,1)S(1)}, u32[]{:S(2)}, u32[]{:S(2)}) %collective-permute-start.31) | collective-permute-done | bytes 262176 | tf_op jit(solution)/shard_map/ppermute | solution.py:32
  97.8 1.7 %collective-permute-start.30 = (bf16[256,512]{1,0:T(8,128)(2,1)S(1)}, bf16[256,512]{1,0:T(8,128)(2,1)S(1)}, u32[]{:S(2)}, u32[]{:S(2)}) collective-permute-start(bf16[256,512]{1,0:T(8,128)(2,1)S(1)} %fusion.2), channel_id=1, source_target_pairs={{0,4},{4,8},{8,12},{12,14},{14,10},{10,6},{6,2},{2,0},{1,5},{5,9},... | collective-permute-start | bytes 786440 | tf_op jit(solution)/shard_map/ppermute | solution.py:32
  99.9 1.6 %collective-permute-start.34 = (bf16[256,512]{1,0:T(8,128)(2,1)S(1)}, bf16[256,512]{1,0:T(8,128)(2,1)S(1)}, u32[]{:S(2)}, u32[]{:S(2)}) collective-permute-start(bf16[256,512]{1,0:T(8,128)(2,1)S(1)} %fusion.3), channel_id=1, source_target_pairs={{0,4},{4,8},{8,12},{12,14},{14,10},{10,6},{6,2},{2,0},{1,5},{5,9},... | collective-permute-start | bytes 786440 | tf_op jit(solution)/shard_map/ppermute | solution.py:32
  101.6 1.3 %collective-permute-start.33 = (bf16[256,1024]{1,0:T(8,128)(2,1)S(1)}, bf16[256,1024]{1,0:T(8,128)(2,1)S(1)}, u32[]{:S(2)}, u32[]{:S(2)}) collective-permute-start(bf16[256,1024]{1,0:T(8,128)(2,1)S(1)} %convert_element_type.182), channel_id=1, source_target_pairs={{0,16},{1,17},{2,18},{3,19},{4,20},{5,21},{6,22},{7,23},{8,24},{9,... | collective-permute-start | bytes 1572872 | tf_op jit(solution)/shard_map/ppermute | solution.py:40
  102.9 3.3 %collective-permute-done.32 = bf16[256,512]{1,0:T(8,128)(2,1)S(1)} collective-permute-done((bf16[256,512]{1,0:T(8,128)(2,1)S(1)}, bf16[256,512]{1,0:T(8,128)(2,1)S(1)}, u32[]{:S(2)}, u32[]{:S(2)}) %collective-permute-start.32) | collective-permute-done | bytes 262176 | tf_op jit(solution)/shard_map/ppermute | solution.py:32
  107.1 3.0 %collective-permute-done.35 = bf16[256,512]{1,0:T(8,128)(2,1)S(1)} collective-permute-done((bf16[256,512]{1,0:T(8,128)(2,1)S(1)}, bf16[256,512]{1,0:T(8,128)(2,1)S(1)}, u32[]{:S(2)}, u32[]{:S(2)}) %collective-permute-start.35) | collective-permute-done | bytes 262176 | tf_op jit(solution)/shard_map/ppermute | solution.py:32
  114.0 1.7 %collective-permute-start.36 = (bf16[256,512]{1,0:T(8,128)(2,1)S(1)}, bf16[256,512]{1,0:T(8,128)(2,1)S(1)}, u32[]{:S(2)}, u32[]{:S(2)}) collective-permute-start(bf16[256,512]{1,0:T(8,128)(2,1)S(1)} %fusion.10), channel_id=1, source_target_pairs={{0,4},{4,8},{8,12},{12,14},{14,10},{10,6},{6,2},{2,0},{1,5},{5,9},... | collective-permute-start | bytes 786440 | tf_op jit(solution)/shard_map/ppermute | solution.py:32
  115.6 3.5 %collective-permute-done.37 = bf16[256,512]{1,0:T(8,128)(2,1)S(1)} collective-permute-done((bf16[256,512]{1,0:T(8,128)(2,1)S(1)}, bf16[256,512]{1,0:T(8,128)(2,1)S(1)}, u32[]{:S(2)}, u32[]{:S(2)}) %collective-permute-start.37) | collective-permute-done | bytes 262176 | tf_op jit(solution)/shard_map/ppermute | solution.py:32
  (128 shorter events, 42.8 us)
Async XLA Ops:
  0.0 34.9 %collective-permute-start = (bf16[3,128,4096]{2,1,0:T(8,128)(2,1)}, bf16[3,128,4096]{2,1,0:T(8,128)(2,1)S(1)}, u32[]{:S(2)}, u32[]{:S(2)}) collective-permute-start(bf16[3,128,4096]{2,1,0:T(8,128)(2,1)} %bitcast.53), channel_id=1, source_target_pairs={{0,1},{1,0},{2,3},{3,2},{4,5},{5,4},{6,7},{7,6},{8,9},{9,8},{10,11... | collective-permute-start | bytes 9437192 | tf_op jit(solution)/shard_map/ppermute | solution.py:52
  1.8 9.5 %collective-permute-start.2 = (bf16[256,512]{1,0:T(8,128)(2,1)S(1)}, bf16[256,512]{1,0:T(8,128)(2,1)S(1)}, u32[]{:S(2)}, u32[]{:S(2)}) collective-permute-start(bf16[256,512]{1,0:T(8,128)(2,1)S(1)} %get-tuple-element.32), channel_id=1, source_target_pairs={{0,4},{4,8},{8,12},{12,14},{14,10},{10,6},{6,2},{2,0},{1,5},{5,9},... | collective-permute-start | bytes 786440 | tf_op jit(solution)/shard_map/ppermute | solution.py:32
  6.1 10.0 %collective-permute-start.3 = (bf16[256,512]{1,0:T(8,128)(2,1)S(1)}, bf16[256,512]{1,0:T(8,128)(2,1)S(1)}, u32[]{:S(2)}, u32[]{:S(2)}) collective-permute-start(bf16[256,512]{1,0:T(8,128)(2,1)S(1)} %collective-permute-done.1), channel_id=1, source_target_pairs={{0,2},{4,0},{8,4},{12,8},{14,12},{10,14},{6,10},{2,6},{1,3},{5,1},... | collective-permute-start | bytes 786440 | tf_op jit(solution)/shard_map/ppermute | solution.py:32
  9.0 12.8 %collective-permute-start.5 = (bf16[256,512]{1,0:T(8,128)(2,1)S(1)}, bf16[256,512]{1,0:T(8,128)(2,1)S(1)}, u32[]{:S(2)}, u32[]{:S(2)}) collective-permute-start(bf16[256,512]{1,0:T(8,128)(2,1)S(1)} %get-tuple-element.32), channel_id=1, source_target_pairs={{0,2},{4,0},{8,4},{12,8},{14,12},{10,14},{6,10},{2,6},{1,3},{5,1},... | collective-permute-start | bytes 786440 | tf_op jit(solution)/shard_map/ppermute | solution.py:32
  10.6 13.2 %collective-permute-start.4 = (bf16[256,512]{1,0:T(8,128)(2,1)S(1)}, bf16[256,512]{1,0:T(8,128)(2,1)S(1)}, u32[]{:S(2)}, u32[]{:S(2)}) collective-permute-start(bf16[256,512]{1,0:T(8,128)(2,1)S(1)} %collective-permute-done.1), channel_id=1, source_target_pairs={{0,4},{4,8},{8,12},{12,14},{14,10},{10,6},{6,2},{2,0},{1,5},{5,9},... | collective-permute-start | bytes 786440 | tf_op jit(solution)/shard_map/ppermute | solution.py:32
  11.3 19.4 %collective-permute-start.7 = (bf16[256,512]{1,0:T(8,128)(2,1)S(1)}, bf16[256,512]{1,0:T(8,128)(2,1)S(1)}, u32[]{:S(2)}, u32[]{:S(2)}) collective-permute-start(bf16[256,512]{1,0:T(8,128)(2,1)S(1)} %collective-permute-done.2), channel_id=1, source_target_pairs={{0,4},{4,8},{8,12},{12,14},{14,10},{10,6},{6,2},{2,0},{1,5},{5,9},... | collective-permute-start | bytes 786440 | tf_op jit(solution)/shard_map/ppermute | solution.py:32
  16.1 16.7 %collective-permute-start.8 = (bf16[256,512]{1,0:T(8,128)(2,1)S(1)}, bf16[256,512]{1,0:T(8,128)(2,1)S(1)}, u32[]{:S(2)}, u32[]{:S(2)}) collective-permute-start(bf16[256,512]{1,0:T(8,128)(2,1)S(1)} %collective-permute-done.3), channel_id=1, source_target_pairs={{0,2},{4,0},{8,4},{12,8},{14,12},{10,14},{6,10},{2,6},{1,3},{5,1},... | collective-permute-start | bytes 786440 | tf_op jit(solution)/shard_map/ppermute | solution.py:32
  21.8 11.1 %collective-permute-start.10 = (bf16[256,512]{1,0:T(8,128)(2,1)S(1)}, bf16[256,512]{1,0:T(8,128)(2,1)S(1)}, u32[]{:S(2)}, u32[]{:S(2)}) collective-permute-start(bf16[256,512]{1,0:T(8,128)(2,1)S(1)} %collective-permute-done.5), channel_id=1, source_target_pairs={{0,2},{4,0},{8,4},{12,8},{14,12},{10,14},{6,10},{2,6},{1,3},{5,1},... | collective-permute-start | bytes 786440 | tf_op jit(solution)/shard_map/ppermute | solution.py:32
  23.8 11.0 %collective-permute-start.9 = (bf16[256,512]{1,0:T(8,128)(2,1)S(1)}, bf16[256,512]{1,0:T(8,128)(2,1)S(1)}, u32[]{:S(2)}, u32[]{:S(2)}) collective-permute-start(bf16[256,512]{1,0:T(8,128)(2,1)S(1)} %collective-permute-done.4), channel_id=1, source_target_pairs={{0,4},{4,8},{8,12},{12,14},{14,10},{10,6},{6,2},{2,0},{1,5},{5,9},... | collective-permute-start | bytes 786440 | tf_op jit(solution)/shard_map/ppermute | solution.py:32
  30.7 11.0 %collective-permute-start.11 = (bf16[256,512]{1,0:T(8,128)(2,1)S(1)}, bf16[256,512]{1,0:T(8,128)(2,1)S(1)}, u32[]{:S(2)}, u32[]{:S(2)}) collective-permute-start(bf16[256,512]{1,0:T(8,128)(2,1)S(1)} %collective-permute-done.7), channel_id=1, source_target_pairs={{0,4},{4,8},{8,12},{12,14},{14,10},{10,6},{6,2},{2,0},{1,5},{5,9},... | collective-permute-start | bytes 786440 | tf_op jit(solution)/shard_map/ppermute | solution.py:32
  32.8 11.0 %collective-permute-start.12 = (bf16[256,512]{1,0:T(8,128)(2,1)S(1)}, bf16[256,512]{1,0:T(8,128)(2,1)S(1)}, u32[]{:S(2)}, u32[]{:S(2)}) collective-permute-start(bf16[256,512]{1,0:T(8,128)(2,1)S(1)} %collective-permute-done.8), channel_id=1, source_target_pairs={{0,2},{4,0},{8,4},{12,8},{14,12},{10,14},{6,10},{2,6},{1,3},{5,1},... | collective-permute-start | bytes 786440 | tf_op jit(solution)/shard_map/ppermute | solution.py:32
  32.8 13.3 %collective-permute-start.14 = (bf16[256,512]{1,0:T(8,128)(2,1)S(1)}, bf16[256,512]{1,0:T(8,128)(2,1)S(1)}, u32[]{:S(2)}, u32[]{:S(2)}) collective-permute-start(bf16[256,512]{1,0:T(8,128)(2,1)S(1)} %collective-permute-done.10), channel_id=1, source_target_pairs={{0,2},{4,0},{8,4},{12,8},{14,12},{10,14},{6,10},{2,6},{1,3},{5,1},... | collective-permute-start | bytes 786440 | tf_op jit(solution)/shard_map/ppermute | solution.py:32
  34.8 17.8 %collective-permute-start.13 = (bf16[256,512]{1,0:T(8,128)(2,1)S(1)}, bf16[256,512]{1,0:T(8,128)(2,1)S(1)}, u32[]{:S(2)}, u32[]{:S(2)}) collective-permute-start(bf16[256,512]{1,0:T(8,128)(2,1)S(1)} %collective-permute-done.9), channel_id=1, source_target_pairs={{0,4},{4,8},{8,12},{12,14},{14,10},{10,6},{6,2},{2,0},{1,5},{5,9},... | collective-permute-start | bytes 786440 | tf_op jit(solution)/shard_map/ppermute | solution.py:32
  41.7 8.9 %collective-permute-start.15 = (bf16[256,512]{1,0:T(8,128)(2,1)S(1)}, bf16[256,512]{1,0:T(8,128)(2,1)S(1)}, u32[]{:S(2)}, u32[]{:S(2)}) collective-permute-start(bf16[256,512]{1,0:T(8,128)(2,1)S(1)} %collective-permute-done.11), channel_id=1, source_target_pairs={{0,4},{4,8},{8,12},{12,14},{14,10},{10,6},{6,2},{2,0},{1,5},{5,9},... | collective-permute-start | bytes 786440 | tf_op jit(solution)/shard_map/ppermute | solution.py:32
  43.8 8.4 %collective-permute-start.16 = (bf16[256,512]{1,0:T(8,128)(2,1)S(1)}, bf16[256,512]{1,0:T(8,128)(2,1)S(1)}, u32[]{:S(2)}, u32[]{:S(2)}) collective-permute-start(bf16[256,512]{1,0:T(8,128)(2,1)S(1)} %collective-permute-done.12), channel_id=1, source_target_pairs={{0,2},{4,0},{8,4},{12,8},{14,12},{10,14},{6,10},{2,6},{1,3},{5,1},... | collective-permute-start | bytes 786440 | tf_op jit(solution)/shard_map/ppermute | solution.py:32
  56.5 6.6 %collective-permute-start.19 = (bf16[6,1024]{1,0:T(8,128)(2,1)S(1)}, bf16[6,1024]{1,0:T(8,128)(2,1)S(1)}, u32[]{:S(2)}, u32[]{:S(2)}) collective-permute-start(bf16[6,1024]{1,0:T(8,128)(2,1)S(1)} %maximum_select_fusion.2), channel_id=1, source_target_pairs={{20,0},{27,1},{24,4},{23,5},{28,8},{19,9},{30,12},{17,13},{26,14},... | collective-permute-start | bytes 36872 | tf_op jit(solution)/shard_map/ppermute | solution.py:64
  57.8 7.7 %collective-permute-start.20 = (bf16[6,1024]{1,0:T(8,128)(2,1)S(1)}, bf16[6,1024]{1,0:T(8,128)(2,1)S(1)}, u32[]{:S(2)}, u32[]{:S(2)}) collective-permute-start(bf16[6,1024]{1,0:T(8,128)(2,1)S(1)} %maximum_select_fusion.2), channel_id=1, source_target_pairs={{24,0},{23,1},{28,4},{19,5},{30,8},{17,9},{26,12},{21,13},{22,14},... | collective-permute-start | bytes 36872 | tf_op jit(solution)/shard_map/ppermute | solution.py:64
  59.1 8.7 %collective-permute-start.21 = (bf16[6,1024]{1,0:T(8,128)(2,1)S(1)}, bf16[6,1024]{1,0:T(8,128)(2,1)S(1)}, u32[]{:S(2)}, u32[]{:S(2)}) collective-permute-start(bf16[6,1024]{1,0:T(8,128)(2,1)S(1)} %maximum_select_fusion.2), channel_id=1, source_target_pairs={{28,0},{19,1},{30,4},{17,5},{26,8},{21,9},{22,12},{25,13},{18,14},... | collective-permute-start | bytes 36872 | tf_op jit(solution)/shard_map/ppermute | solution.py:64
  71.2 9.2 %collective-permute-start.24 = (bf16[256,512]{1,0:T(8,128)(2,1)S(1)}, bf16[256,512]{1,0:T(8,128)(2,1)S(1)}, u32[]{:S(2)}, u32[]{:S(2)}) collective-permute-start(bf16[256,512]{1,0:T(8,128)(2,1)S(1)} %convolution_convert_fusion.2), channel_id=1, source_target_pairs={{0,2},{4,0},{8,4},{12,8},{14,12},{10,14},{6,10},{2,6},{1,3},{5,1},... | collective-permute-start | bytes 786440 | tf_op jit(solution)/shard_map/ppermute | solution.py:32
  71.7 9.2 %collective-permute-start.23 = (bf16[256,512]{1,0:T(8,128)(2,1)S(1)}, bf16[256,512]{1,0:T(8,128)(2,1)S(1)}, u32[]{:S(2)}, u32[]{:S(2)}) collective-permute-start(bf16[256,512]{1,0:T(8,128)(2,1)S(1)} %convolution_convert_fusion.3), channel_id=1, source_target_pairs={{0,4},{4,8},{8,12},{12,14},{14,10},{10,6},{6,2},{2,0},{1,5},{5,9},... | collective-permute-start | bytes 786440 | tf_op jit(solution)/shard_map/ppermute | solution.py:32
  73.7 12.3 %collective-permute-start.26 = (bf16[256,512]{1,0:T(8,128)(2,1)S(1)}, bf16[256,512]{1,0:T(8,128)(2,1)S(1)}, u32[]{:S(2)}, u32[]{:S(2)}) collective-permute-start(bf16[256,512]{1,0:T(8,128)(2,1)S(1)} %convolution_convert_fusion), channel_id=1, source_target_pairs={{0,2},{4,0},{8,4},{12,8},{14,12},{10,14},{6,10},{2,6},{1,3},{5,1},... | collective-permute-start | bytes 786440 | tf_op jit(solution)/shard_map/ppermute | solution.py:32
  74.6 11.9 %collective-permute-start.25 = (bf16[256,512]{1,0:T(8,128)(2,1)S(1)}, bf16[256,512]{1,0:T(8,128)(2,1)S(1)}, u32[]{:S(2)}, u32[]{:S(2)}) collective-permute-start(bf16[256,512]{1,0:T(8,128)(2,1)S(1)} %convolution_convert_fusion.1), channel_id=1, source_target_pairs={{0,4},{4,8},{8,12},{12,14},{14,10},{10,6},{6,2},{2,0},{1,5},{5,9},... | collective-permute-start | bytes 786440 | tf_op jit(solution)/shard_map/ppermute | solution.py:32
  81.7 9.9 %collective-permute-start.28 = (bf16[256,512]{1,0:T(8,128)(2,1)S(1)}, bf16[256,512]{1,0:T(8,128)(2,1)S(1)}, u32[]{:S(2)}, u32[]{:S(2)}) collective-permute-start(bf16[256,512]{1,0:T(8,128)(2,1)S(1)} %fusion.6), channel_id=1, source_target_pairs={{0,2},{4,0},{8,4},{12,8},{14,12},{10,14},{6,10},{2,6},{1,3},{5,1},... | collective-permute-start | bytes 786440 | tf_op jit(solution)/shard_map/ppermute | solution.py:32
  82.7 9.4 %collective-permute-start.27 = (bf16[256,512]{1,0:T(8,128)(2,1)S(1)}, bf16[256,512]{1,0:T(8,128)(2,1)S(1)}, u32[]{:S(2)}, u32[]{:S(2)}) collective-permute-start(bf16[256,512]{1,0:T(8,128)(2,1)S(1)} %fusion.5), channel_id=1, source_target_pairs={{0,4},{4,8},{8,12},{12,14},{14,10},{10,6},{6,2},{2,0},{1,5},{5,9},... | collective-permute-start | bytes 786440 | tf_op jit(solution)/shard_map/ppermute | solution.py:32
  86.9 9.6 %collective-permute-start.31 = (bf16[256,512]{1,0:T(8,128)(2,1)S(1)}, bf16[256,512]{1,0:T(8,128)(2,1)S(1)}, u32[]{:S(2)}, u32[]{:S(2)}) collective-permute-start(bf16[256,512]{1,0:T(8,128)(2,1)S(1)} %fusion.7), channel_id=1, source_target_pairs={{0,2},{4,0},{8,4},{12,8},{14,12},{10,14},{6,10},{2,6},{1,3},{5,1},... | collective-permute-start | bytes 786440 | tf_op jit(solution)/shard_map/ppermute | solution.py:32
  87.9 9.5 %collective-permute-start.29 = (bf16[256,512]{1,0:T(8,128)(2,1)S(1)}, bf16[256,512]{1,0:T(8,128)(2,1)S(1)}, u32[]{:S(2)}, u32[]{:S(2)}) collective-permute-start(bf16[256,512]{1,0:T(8,128)(2,1)S(1)} %fusion.4), channel_id=1, source_target_pairs={{0,4},{4,8},{8,12},{12,14},{14,10},{10,6},{6,2},{2,0},{1,5},{5,9},... | collective-permute-start | bytes 786440 | tf_op jit(solution)/shard_map/ppermute | solution.py:32
  96.9 9.3 %collective-permute-start.32 = (bf16[256,512]{1,0:T(8,128)(2,1)S(1)}, bf16[256,512]{1,0:T(8,128)(2,1)S(1)}, u32[]{:S(2)}, u32[]{:S(2)}) collective-permute-start(bf16[256,512]{1,0:T(8,128)(2,1)S(1)} %fusion.9), channel_id=1, source_target_pairs={{0,2},{4,0},{8,4},{12,8},{14,12},{10,14},{6,10},{2,6},{1,3},{5,1},... | collective-permute-start | bytes 786440 | tf_op jit(solution)/shard_map/ppermute | solution.py:32
  97.8 9.3 %collective-permute-start.30 = (bf16[256,512]{1,0:T(8,128)(2,1)S(1)}, bf16[256,512]{1,0:T(8,128)(2,1)S(1)}, u32[]{:S(2)}, u32[]{:S(2)}) collective-permute-start(bf16[256,512]{1,0:T(8,128)(2,1)S(1)} %fusion.2), channel_id=1, source_target_pairs={{0,4},{4,8},{8,12},{12,14},{14,10},{10,6},{6,2},{2,0},{1,5},{5,9},... | collective-permute-start | bytes 786440 | tf_op jit(solution)/shard_map/ppermute | solution.py:32
  99.5 10.7 %collective-permute-start.35 = (bf16[256,512]{1,0:T(8,128)(2,1)S(1)}, bf16[256,512]{1,0:T(8,128)(2,1)S(1)}, u32[]{:S(2)}, u32[]{:S(2)}) collective-permute-start(bf16[256,512]{1,0:T(8,128)(2,1)S(1)} %fusion.8), channel_id=1, source_target_pairs={{0,2},{4,0},{8,4},{12,8},{14,12},{10,14},{6,10},{2,6},{1,3},{5,1},... | collective-permute-start | bytes 786440 | tf_op jit(solution)/shard_map/ppermute | solution.py:32
  99.9 10.8 %collective-permute-start.34 = (bf16[256,512]{1,0:T(8,128)(2,1)S(1)}, bf16[256,512]{1,0:T(8,128)(2,1)S(1)}, u32[]{:S(2)}, u32[]{:S(2)}) collective-permute-start(bf16[256,512]{1,0:T(8,128)(2,1)S(1)} %fusion.3), channel_id=1, source_target_pairs={{0,4},{4,8},{8,12},{12,14},{14,10},{10,6},{6,2},{2,0},{1,5},{5,9},... | collective-permute-start | bytes 786440 | tf_op jit(solution)/shard_map/ppermute | solution.py:32
  101.6 11.1 %collective-permute-start.33 = (bf16[256,1024]{1,0:T(8,128)(2,1)S(1)}, bf16[256,1024]{1,0:T(8,128)(2,1)S(1)}, u32[]{:S(2)}, u32[]{:S(2)}) collective-permute-start(bf16[256,1024]{1,0:T(8,128)(2,1)S(1)} %convert_element_type.182), channel_id=1, source_target_pairs={{0,16},{1,17},{2,18},{3,19},{4,20},{5,21},{6,22},{7,23},{8,24},{9,... | collective-permute-start | bytes 1572872 | tf_op jit(solution)/shard_map/ppermute | solution.py:40
  114.0 6.4 %collective-permute-start.36 = (bf16[256,512]{1,0:T(8,128)(2,1)S(1)}, bf16[256,512]{1,0:T(8,128)(2,1)S(1)}, u32[]{:S(2)}, u32[]{:S(2)}) collective-permute-start(bf16[256,512]{1,0:T(8,128)(2,1)S(1)} %fusion.10), channel_id=1, source_target_pairs={{0,4},{4,8},{8,12},{12,14},{14,10},{10,6},{6,2},{2,0},{1,5},{5,9},... | collective-permute-start | bytes 786440 | tf_op jit(solution)/shard_map/ppermute | solution.py:32
  (12 other events, 39.1 us)

commit v22 on v20

--- a/solution.py
+++ b/solution.py
@@ -248,20 +248,20 @@
         hops = [(chips // 2, four)]
         for step in range(chips // 2 - 1, 0, -1):
             hops += [(step, three), (step, four)]
-        arrived, previous, source = {}, delta, delta
+        arrived, previous, source = {}, {}, delta
         for hop, (step, ways) in enumerate(hops):
             totals = []
             for i, by in ways:
                 total = term(by * step, i, source)
                 if (i, by) in arrived:
-                    before = after(previous, arrived[i, by])
+                    before = after(previous[by], arrived[i, by])
                     total = total + before.astype(jnp.float32)
                 totals.append(total.astype(jnp.bfloat16))
             if hop == len(hops) - 1:
                 totals = after(copied, totals)
             for (i, by), total in zip(ways, totals):
                 arrived[i, by] = along_ring(total, by)
-            previous = totals
+            previous = {by: total for (i, by), total in zip(ways, totals)}
             if hop == 0:
                 source = after(totals, delta)
                 late, weights = after(arrived[0, 1], (delta, weights))

time: 115 us -> 118 us (1.026)
  waiting for transfers between devices: 43.5 us -> 48.2 us
  starting transfers between devices: 40.9 us -> 39 us
    ppermute x28, waiting for transfers between devices: 33.2 us -> 37.9 us  [along_ring(): return lax.ppermute(block, 'chip', pairs)]
    ppermute x28, starting transfers between devices: 33.1 us -> 31.1 us  [along_ring(): return lax.ppermute(block, 'chip', pairs)]
  transfers between devices with their start and end apart: 39 -> 39, of which waited for: 23 -> 19; matrix products, arithmetic and copies ran while one was open for 14% -> 13% of each run, Pallas kernels for 6% -> 6%
where the time goes in v22:
time: 118 us
  waiting for transfers between devices  48.2 us (41%)
  starting transfers between devices  39 us (33%)
  matrix products  15 us (13%)
  Pallas kernels  7.16 us (6%)
  local copies, waits for them, and re-layouts  4.88 us (4%)
  other arithmetic  3.22 us (3%)
    ppermute x28, waiting for transfers between devices, along_ring(): return lax.ppermute(block, 'chip', pairs)  37.9 us
    ppermute x28, starting transfers between devices, along_ring(): return lax.ppermute(block, 'chip', pairs)  31.1 us
    ppermute x4, waiting for transfers between devices, slab_blocks(): kept.append(lax.ppermute(stored, ('grp', 'chip', 'core'), pairs))  7.28 us
    pallas_call x2, Pallas kernels, normalize(): pl.pallas_call(functools.partial(normalize_kernel, 16), grid=(seqs,), in_...  7.16 us
    dot_general x16, matrix products, product(): jnp.dot(columns(offset, i), block, preferred_element_type=jnp.float32)  6.81 us
    dot_general x16, matrix products, term(): lax.dot_general(columns(offset, i), delta, (((0,), (0,)), ((), ())), pref...  6.58 us
    ppermute x4, starting transfers between devices, slab_blocks(): kept.append(lax.ppermute(stored, ('grp', 'chip', 'core'), pairs))  5.16 us
    unnamed x11, local copies, waits for them, and re-layouts  3.31 us
  transfers between devices with their start and end apart: 39, of which 19 were waited for; matrix products, arithmetic and copies ran while one was open for 13% of the time, Pallas kernels for 6%

profile of v22, /device:TPU:0, one launch (start us, length us, event | category | flops | bytes accessed | tf_op | source)
XLA Modules:
  0.0 118.0 jit_solution(9504459944102501374)
XLA Ops:
  1.8 3.0 %collective-permute-start.2 = (bf16[256,512]{1,0:T(8,128)(2,1)S(1)}, bf16[256,512]{1,0:T(8,128)(2,1)S(1)}, u32[]{:S(2)}, u32[]{:S(2)}) collective-permute-start(bf16[256,512]{1,0:T(8,128)(2,1)S(1)} %get-tuple-element.69), channel_id=1, source_target_pairs={{0,4},{4,8},{8,12},{12,14},{14,10},{10,6},{6,2},{2,0},{1,5},{5,9},... | collective-permute-start | bytes 786440 | tf_op jit(solution)/shard_map/ppermute | solution.py:32
  6.1 2.9 %collective-permute-start.5 = (bf16[256,512]{1,0:T(8,128)(2,1)S(1)}, bf16[256,512]{1,0:T(8,128)(2,1)S(1)}, u32[]{:S(2)}, u32[]{:S(2)}) collective-permute-start(bf16[256,512]{1,0:T(8,128)(2,1)S(1)} %collective-permute-done.1), channel_id=1, source_target_pairs={{0,2},{4,0},{8,4},{12,8},{14,12},{10,14},{6,10},{2,6},{1,3},{5,1},... | collective-permute-start | bytes 786440 | tf_op jit(solution)/shard_map/ppermute | solution.py:32
  9.1 2.5 %collective-permute-done.2 = bf16[256,512]{1,0:T(8,128)(2,1)S(1)} collective-permute-done((bf16[256,512]{1,0:T(8,128)(2,1)S(1)}, bf16[256,512]{1,0:T(8,128)(2,1)S(1)}, u32[]{:S(2)}, u32[]{:S(2)}) %collective-permute-start.2) | collective-permute-done | bytes 262176 | tf_op jit(solution)/shard_map/ppermute | solution.py:32
  11.5 2.5 %collective-permute-start.7 = (bf16[256,512]{1,0:T(8,128)(2,1)S(1)}, bf16[256,512]{1,0:T(8,128)(2,1)S(1)}, u32[]{:S(2)}, u32[]{:S(2)}) collective-permute-start(bf16[256,512]{1,0:T(8,128)(2,1)S(1)} %collective-permute-done.2), channel_id=1, source_target_pairs={{0,4},{4,8},{8,12},{12,14},{14,10},{10,6},{6,2},{2,0},{1,5},{5,9},... | collective-permute-start | bytes 786440 | tf_op jit(solution)/shard_map/ppermute | solution.py:32
  14.8 1.9 %copy-done = bf16[1,3,128,4096]{3,2,1,0:T(8,128)(2,1)S(1)} copy-done((bf16[1,3,128,4096]{3,2,1,0:T(8,128)(2,1)S(1)}, bf16[1,3,128,4096]{3,2,1,0:T(8,128)(2,1)}, u32[]{:S(2)}) %copy-start) | copy-done | bytes 3145752
  17.4 3.6 %shard_map.64.refs_0_ = bf16[768,4096]{1,0:T(8,128)(2,1)S(1)} custom-call(bf16[3,128,4096]{2,1,0:T(8,128)(2,1)S(1)} %bitcast.54, f32[1,4096]{1,0:T(1,128)S(1)} %bitcast.55), custom_call_target="tpu_custom_call" | custom-call | flops 9437184 | bytes 6291456 | tf_op jit(solution)/shard_map/pallas_call | solution.py:99
  21.0 2.1 %collective-permute-start.9 = (bf16[256,512]{1,0:T(8,128)(2,1)S(1)}, bf16[256,512]{1,0:T(8,128)(2,1)S(1)}, u32[]{:S(2)}, u32[]{:S(2)}) collective-permute-start(bf16[256,512]{1,0:T(8,128)(2,1)S(1)} %collective-permute-done.4), channel_id=1, source_target_pairs={{0,4},{4,8},{8,12},{12,14},{14,10},{10,6},{6,2},{2,0},{1,5},{5,9},... | collective-permute-start | bytes 786440 | tf_op jit(solution)/shard_map/ppermute | solution.py:32
  23.4 1.9 %collective-permute-start.11 = (bf16[256,512]{1,0:T(8,128)(2,1)S(1)}, bf16[256,512]{1,0:T(8,128)(2,1)S(1)}, u32[]{:S(2)}, u32[]{:S(2)}) collective-permute-start(bf16[256,512]{1,0:T(8,128)(2,1)S(1)} %collective-permute-done.7), channel_id=1, source_target_pairs={{0,4},{4,8},{8,12},{12,14},{14,10},{10,6},{6,2},{2,0},{1,5},{5,9},... | collective-permute-start | bytes 786440 | tf_op jit(solution)/shard_map/ppermute | solution.py:32
  25.4 3.6 %shard_map.65 = bf16[768,4096]{1,0:T(8,128)(2,1)S(1)} custom-call(bf16[3,128,4096]{2,1,0:T(8,128)(2,1)S(1)} %collective-permute-done.states_ref, f32[1,4096]{1,0:T(1,128)S(1)} %bitcast.56, bf16[768,4096]{1,0:T(8,128)(2,1)S(1)} %shard_map.64.refs_0_), custom_call_target="tpu_custom_call", output_to_operand_aliasing={{}: (2, {})} | custom-call | flops 9437184 | bytes 6291456 | tf_op jit(solution)/shard_map/pallas_call | solution.py:99
  32.2 1.9 %collective-permute-start.13 = (bf16[256,512]{1,0:T(8,128)(2,1)S(1)}, bf16[256,512]{1,0:T(8,128)(2,1)S(1)}, u32[]{:S(2)}, u32[]{:S(2)}) collective-permute-start(bf16[256,512]{1,0:T(8,128)(2,1)S(1)} %collective-permute-done.9), channel_id=1, source_target_pairs={{0,4},{4,8},{8,12},{12,14},{14,10},{10,6},{6,2},{2,0},{1,5},{5,9},... | collective-permute-start | bytes 786440 | tf_op jit(solution)/shard_map/ppermute | solution.py:32
  34.4 1.9 %collective-permute-start.15 = (bf16[256,512]{1,0:T(8,128)(2,1)S(1)}, bf16[256,512]{1,0:T(8,128)(2,1)S(1)}, u32[]{:S(2)}, u32[]{:S(2)}) collective-permute-start(bf16[256,512]{1,0:T(8,128)(2,1)S(1)} %collective-permute-done.11), channel_id=1, source_target_pairs={{0,4},{4,8},{8,12},{12,14},{14,10},{10,6},{6,2},{2,0},{1,5},{5,9},... | collective-permute-start | bytes 786440 | tf_op jit(solution)/shard_map/ppermute | solution.py:32
  38.8 3.7 %collective-permute-done.14 = bf16[256,512]{1,0:T(8,128)(2,1)S(1)} collective-permute-done((bf16[256,512]{1,0:T(8,128)(2,1)S(1)}, bf16[256,512]{1,0:T(8,128)(2,1)S(1)}, u32[]{:S(2)}, u32[]{:S(2)}) %collective-permute-start.14) | collective-permute-done | bytes 262176 | tf_op jit(solution)/shard_map/ppermute | solution.py:32
  43.6 3.1 %collective-permute-done.15 = bf16[256,512]{1,0:T(8,128)(2,1)S(1)} collective-permute-done((bf16[256,512]{1,0:T(8,128)(2,1)S(1)}, bf16[256,512]{1,0:T(8,128)(2,1)S(1)}, u32[]{:S(2)}, u32[]{:S(2)}) %collective-permute-start.15) | collective-permute-done | bytes 262176 | tf_op jit(solution)/shard_map/ppermute | solution.py:32
  47.0 3.0 %collective-permute-done.16 = bf16[256,512]{1,0:T(8,128)(2,1)S(1)} collective-permute-done((bf16[256,512]{1,0:T(8,128)(2,1)S(1)}, bf16[256,512]{1,0:T(8,128)(2,1)S(1)}, u32[]{:S(2)}, u32[]{:S(2)}) %collective-permute-start.16) | collective-permute-done | bytes 262176 | tf_op jit(solution)/shard_map/ppermute | solution.py:32
  53.0 1.3 %collective-permute-start.18 = (bf16[6,1024]{1,0:T(8,128)(2,1)S(1)}, bf16[6,1024]{1,0:T(8,128)(2,1)S(1)}, u32[]{:S(2)}, u32[]{:S(2)}) collective-permute-start(bf16[6,1024]{1,0:T(8,128)(2,1)S(1)} %maximum_select_fusion.2), channel_id=1, source_target_pairs={{16,0},{31,1},{20,4},{27,5},{24,8},{23,9},{28,12},{19,13},{30,14},... | collective-permute-start | bytes 36872 | tf_op jit(solution)/shard_map/ppermute | solution.py:64
  54.3 1.3 %collective-permute-start.19 = (bf16[6,1024]{1,0:T(8,128)(2,1)S(1)}, bf16[6,1024]{1,0:T(8,128)(2,1)S(1)}, u32[]{:S(2)}, u32[]{:S(2)}) collective-permute-start(bf16[6,1024]{1,0:T(8,128)(2,1)S(1)} %maximum_select_fusion.2), channel_id=1, source_target_pairs={{20,0},{27,1},{24,4},{23,5},{28,8},{19,9},{30,12},{17,13},{26,14},... | collective-permute-start | bytes 36872 | tf_op jit(solution)/shard_map/ppermute | solution.py:64
  55.6 1.3 %collective-permute-start.20 = (bf16[6,1024]{1,0:T(8,128)(2,1)S(1)}, bf16[6,1024]{1,0:T(8,128)(2,1)S(1)}, u32[]{:S(2)}, u32[]{:S(2)}) collective-permute-start(bf16[6,1024]{1,0:T(8,128)(2,1)S(1)} %maximum_select_fusion.2), channel_id=1, source_target_pairs={{24,0},{23,1},{28,4},{19,5},{30,8},{17,9},{26,12},{21,13},{22,14},... | collective-permute-start | bytes 36872 | tf_op jit(solution)/shard_map/ppermute | solution.py:64
  56.9 1.3 %collective-permute-start.21 = (bf16[6,1024]{1,0:T(8,128)(2,1)S(1)}, bf16[6,1024]{1,0:T(8,128)(2,1)S(1)}, u32[]{:S(2)}, u32[]{:S(2)}) collective-permute-start(bf16[6,1024]{1,0:T(8,128)(2,1)S(1)} %maximum_select_fusion.2), channel_id=1, source_target_pairs={{28,0},{19,1},{30,4},{17,5},{26,8},{21,9},{22,12},{25,13},{18,14},... | collective-permute-start | bytes 36872 | tf_op jit(solution)/shard_map/ppermute | solution.py:64
  58.7 2.3 %collective-permute-done.19 = bf16[6,1024]{1,0:T(8,128)(2,1)S(1)} collective-permute-done((bf16[6,1024]{1,0:T(8,128)(2,1)S(1)}, bf16[6,1024]{1,0:T(8,128)(2,1)S(1)}, u32[]{:S(2)}, u32[]{:S(2)}) %collective-permute-start.19) | collective-permute-done | bytes 12320 | tf_op jit(solution)/shard_map/ppermute | solution.py:64
  61.0 2.3 %collective-permute-done.20 = bf16[6,1024]{1,0:T(8,128)(2,1)S(1)} collective-permute-done((bf16[6,1024]{1,0:T(8,128)(2,1)S(1)}, bf16[6,1024]{1,0:T(8,128)(2,1)S(1)}, u32[]{:S(2)}, u32[]{:S(2)}) %collective-permute-start.20) | collective-permute-done | bytes 12320 | tf_op jit(solution)/shard_map/ppermute | solution.py:64
  63.3 2.3 %collective-permute-done.21 = bf16[6,1024]{1,0:T(8,128)(2,1)S(1)} collective-permute-done((bf16[6,1024]{1,0:T(8,128)(2,1)S(1)}, bf16[6,1024]{1,0:T(8,128)(2,1)S(1)}, u32[]{:S(2)}, u32[]{:S(2)}) %collective-permute-start.21) | collective-permute-done | bytes 12320 | tf_op jit(solution)/shard_map/ppermute | solution.py:64
  68.9 1.5 %collective-permute-start.23 = (bf16[256,512]{1,0:T(8,128)(2,1)S(1)}, bf16[256,512]{1,0:T(8,128)(2,1)S(1)}, u32[]{:S(2)}, u32[]{:S(2)}) collective-permute-start(bf16[256,512]{1,0:T(8,128)(2,1)S(1)} %convolution_convert_fusion.3), channel_id=1, source_target_pairs={{0,4},{4,8},{8,12},{12,14},{14,10},{10,6},{6,2},{2,0},{1,5},{5,9},... | collective-permute-start | bytes 786440 | tf_op jit(solution)/shard_map/ppermute | solution.py:32
  71.4 1.5 %collective-permute-start.25 = (bf16[256,512]{1,0:T(8,128)(2,1)S(1)}, bf16[256,512]{1,0:T(8,128)(2,1)S(1)}, u32[]{:S(2)}, u32[]{:S(2)}) collective-permute-start(bf16[256,512]{1,0:T(8,128)(2,1)S(1)} %convolution_convert_fusion.1), channel_id=1, source_target_pairs={{0,4},{4,8},{8,12},{12,14},{14,10},{10,6},{6,2},{2,0},{1,5},{5,9},... | collective-permute-start | bytes 786440 | tf_op jit(solution)/shard_map/ppermute | solution.py:32
  74.0 4.2 %collective-permute-done.23 = bf16[256,512]{1,0:T(8,128)(2,1)S(1)} collective-permute-done((bf16[256,512]{1,0:T(8,128)(2,1)S(1)}, bf16[256,512]{1,0:T(8,128)(2,1)S(1)}, u32[]{:S(2)}, u32[]{:S(2)}) %collective-permute-start.23) | collective-permute-done | bytes 262176 | tf_op jit(solution)/shard_map/ppermute | solution.py:32
  78.6 1.5 %collective-permute-start.26 = (bf16[256,512]{1,0:T(8,128)(2,1)S(1)}, bf16[256,512]{1,0:T(8,128)(2,1)S(1)}, u32[]{:S(2)}, u32[]{:S(2)}) collective-permute-start(bf16[256,512]{1,0:T(8,128)(2,1)S(1)} %fusion.6), channel_id=1, source_target_pairs={{0,4},{4,8},{8,12},{12,14},{14,10},{10,6},{6,2},{2,0},{1,5},{5,9},... | collective-permute-start | bytes 786440 | tf_op jit(solution)/shard_map/ppermute | solution.py:32
  80.1 3.7 %collective-permute-done.25 = bf16[256,512]{1,0:T(8,128)(2,1)S(1)} collective-permute-done((bf16[256,512]{1,0:T(8,128)(2,1)S(1)}, bf16[256,512]{1,0:T(8,128)(2,1)S(1)}, u32[]{:S(2)}, u32[]{:S(2)}) %collective-permute-start.25) | collective-permute-done | bytes 262176 | tf_op jit(solution)/shard_map/ppermute | solution.py:32
  84.2 1.5 %collective-permute-start.27 = (bf16[256,512]{1,0:T(8,128)(2,1)S(1)}, bf16[256,512]{1,0:T(8,128)(2,1)S(1)}, u32[]{:S(2)}, u32[]{:S(2)}) collective-permute-start(bf16[256,512]{1,0:T(8,128)(2,1)S(1)} %fusion.5), channel_id=1, source_target_pairs={{0,4},{4,8},{8,12},{12,14},{14,10},{10,6},{6,2},{2,0},{1,5},{5,9},... | collective-permute-start | bytes 786440 | tf_op jit(solution)/shard_map/ppermute | solution.py:32
  87.8 1.8 %collective-permute-start.24 = (bf16[256,1024]{1,0:T(8,128)(2,1)S(1)}, bf16[256,1024]{1,0:T(8,128)(2,1)S(1)}, u32[]{:S(2)}, u32[]{:S(2)}) collective-permute-start(bf16[256,1024]{1,0:T(8,128)(2,1)S(1)} %convert_element_type.163), channel_id=1, source_target_pairs={{0,16},{1,17},{2,18},{3,19},{4,20},{5,21},{6,22},{7,23},{8,24},{9,... | collective-permute-start | bytes 1572872 | tf_op jit(solution)/shard_map/ppermute | solution.py:40
  90.1 5.4 %collective-permute-done.31 = bf16[256,512]{1,0:T(8,128)(2,1)S(1)} collective-permute-done((bf16[256,512]{1,0:T(8,128)(2,1)S(1)}, bf16[256,512]{1,0:T(8,128)(2,1)S(1)}, u32[]{:S(2)}, u32[]{:S(2)}) %collective-permute-start.31) | collective-permute-done | bytes 262176 | tf_op jit(solution)/shard_map/ppermute | solution.py:32
  100.7 3.2 %collective-permute-done.33 = bf16[256,512]{1,0:T(8,128)(2,1)S(1)} collective-permute-done((bf16[256,512]{1,0:T(8,128)(2,1)S(1)}, bf16[256,512]{1,0:T(8,128)(2,1)S(1)}, u32[]{:S(2)}, u32[]{:S(2)}) %collective-permute-start.33) | collective-permute-done | bytes 262176 | tf_op jit(solution)/shard_map/ppermute | solution.py:32
  108.3 5.4 %collective-permute-done.37 = bf16[256,512]{1,0:T(8,128)(2,1)S(1)} collective-permute-done((bf16[256,512]{1,0:T(8,128)(2,1)S(1)}, bf16[256,512]{1,0:T(8,128)(2,1)S(1)}, u32[]{:S(2)}, u32[]{:S(2)}) %collective-permute-start.37) | collective-permute-done | bytes 262176 | tf_op jit(solution)/shard_map/ppermute | solution.py:32
  113.8 2.6 %collective-permute-done.35 = bf16[256,512]{1,0:T(8,128)(2,1)S(1)} collective-permute-done((bf16[256,512]{1,0:T(8,128)(2,1)S(1)}, bf16[256,512]{1,0:T(8,128)(2,1)S(1)}, u32[]{:S(2)}, u32[]{:S(2)}) %collective-permute-start.35) | collective-permute-done | bytes 262176 | tf_op jit(solution)/shard_map/ppermute | solution.py:32
  (128 shorter events, 35.7 us)
Async XLA Ops:
  0.0 25.4 %collective-permute-start = (bf16[3,128,4096]{2,1,0:T(8,128)(2,1)}, bf16[3,128,4096]{2,1,0:T(8,128)(2,1)S(1)}, u32[]{:S(2)}, u32[]{:S(2)}) collective-permute-start(bf16[3,128,4096]{2,1,0:T(8,128)(2,1)} %bitcast.53), channel_id=1, source_target_pairs={{0,1},{1,0},{2,3},{3,2},{4,5},{5,4},{6,7},{7,6},{8,9},{9,8},{10,11... | collective-permute-start | bytes 9437192 | tf_op jit(solution)/shard_map/ppermute | solution.py:52
  1.8 9.7 %collective-permute-start.2 = (bf16[256,512]{1,0:T(8,128)(2,1)S(1)}, bf16[256,512]{1,0:T(8,128)(2,1)S(1)}, u32[]{:S(2)}, u32[]{:S(2)}) collective-permute-start(bf16[256,512]{1,0:T(8,128)(2,1)S(1)} %get-tuple-element.69), channel_id=1, source_target_pairs={{0,4},{4,8},{8,12},{12,14},{14,10},{10,6},{6,2},{2,0},{1,5},{5,9},... | collective-permute-start | bytes 786440 | tf_op jit(solution)/shard_map/ppermute | solution.py:32
  4.9 9.2 %collective-permute-start.3 = (bf16[256,512]{1,0:T(8,128)(2,1)S(1)}, bf16[256,512]{1,0:T(8,128)(2,1)S(1)}, u32[]{:S(2)}, u32[]{:S(2)}) collective-permute-start(bf16[256,512]{1,0:T(8,128)(2,1)S(1)} %get-tuple-element.69), channel_id=1, source_target_pairs={{0,2},{4,0},{8,4},{12,8},{14,12},{10,14},{6,10},{2,6},{1,3},{5,1},... | collective-permute-start | bytes 786440 | tf_op jit(solution)/shard_map/ppermute | solution.py:32
  6.1 14.8 %collective-permute-start.5 = (bf16[256,512]{1,0:T(8,128)(2,1)S(1)}, bf16[256,512]{1,0:T(8,128)(2,1)S(1)}, u32[]{:S(2)}, u32[]{:S(2)}) collective-permute-start(bf16[256,512]{1,0:T(8,128)(2,1)S(1)} %collective-permute-done.1), channel_id=1, source_target_pairs={{0,2},{4,0},{8,4},{12,8},{14,12},{10,14},{6,10},{2,6},{1,3},{5,1},... | collective-permute-start | bytes 786440 | tf_op jit(solution)/shard_map/ppermute | solution.py:32
  9.0 12.0 %collective-permute-start.4 = (bf16[256,512]{1,0:T(8,128)(2,1)S(1)}, bf16[256,512]{1,0:T(8,128)(2,1)S(1)}, u32[]{:S(2)}, u32[]{:S(2)}) collective-permute-start(bf16[256,512]{1,0:T(8,128)(2,1)S(1)} %collective-permute-done.1), channel_id=1, source_target_pairs={{0,4},{4,8},{8,12},{12,14},{14,10},{10,6},{6,2},{2,0},{1,5},{5,9},... | collective-permute-start | bytes 786440 | tf_op jit(solution)/shard_map/ppermute | solution.py:32
  11.5 11.9 %collective-permute-start.7 = (bf16[256,512]{1,0:T(8,128)(2,1)S(1)}, bf16[256,512]{1,0:T(8,128)(2,1)S(1)}, u32[]{:S(2)}, u32[]{:S(2)}) collective-permute-start(bf16[256,512]{1,0:T(8,128)(2,1)S(1)} %collective-permute-done.2), channel_id=1, source_target_pairs={{0,4},{4,8},{8,12},{12,14},{14,10},{10,6},{6,2},{2,0},{1,5},{5,9},... | collective-permute-start | bytes 786440 | tf_op jit(solution)/shard_map/ppermute | solution.py:32
  14.1 11.2 %collective-permute-start.8 = (bf16[256,512]{1,0:T(8,128)(2,1)S(1)}, bf16[256,512]{1,0:T(8,128)(2,1)S(1)}, u32[]{:S(2)}, u32[]{:S(2)}) collective-permute-start(bf16[256,512]{1,0:T(8,128)(2,1)S(1)} %collective-permute-done.3), channel_id=1, source_target_pairs={{0,2},{4,0},{8,4},{12,8},{14,12},{10,14},{6,10},{2,6},{1,3},{5,1},... | collective-permute-start | bytes 786440 | tf_op jit(solution)/shard_map/ppermute | solution.py:32
  21.0 11.3 %collective-permute-start.9 = (bf16[256,512]{1,0:T(8,128)(2,1)S(1)}, bf16[256,512]{1,0:T(8,128)(2,1)S(1)}, u32[]{:S(2)}, u32[]{:S(2)}) collective-permute-start(bf16[256,512]{1,0:T(8,128)(2,1)S(1)} %collective-permute-done.4), channel_id=1, source_target_pairs={{0,4},{4,8},{8,12},{12,14},{14,10},{10,6},{6,2},{2,0},{1,5},{5,9},... | collective-permute-start | bytes 786440 | tf_op jit(solution)/shard_map/ppermute | solution.py:32
  23.0 11.1 %collective-permute-start.10 = (bf16[256,512]{1,0:T(8,128)(2,1)S(1)}, bf16[256,512]{1,0:T(8,128)(2,1)S(1)}, u32[]{:S(2)}, u32[]{:S(2)}) collective-permute-start(bf16[256,512]{1,0:T(8,128)(2,1)S(1)} %collective-permute-done.5), channel_id=1, source_target_pairs={{0,2},{4,0},{8,4},{12,8},{14,12},{10,14},{6,10},{2,6},{1,3},{5,1},... | collective-permute-start | bytes 786440 | tf_op jit(solution)/shard_map/ppermute | solution.py:32
  23.4 10.9 %collective-permute-start.11 = (bf16[256,512]{1,0:T(8,128)(2,1)S(1)}, bf16[256,512]{1,0:T(8,128)(2,1)S(1)}, u32[]{:S(2)}, u32[]{:S(2)}) collective-permute-start(bf16[256,512]{1,0:T(8,128)(2,1)S(1)} %collective-permute-done.7), channel_id=1, source_target_pairs={{0,4},{4,8},{8,12},{12,14},{14,10},{10,6},{6,2},{2,0},{1,5},{5,9},... | collective-permute-start | bytes 786440 | tf_op jit(solution)/shard_map/ppermute | solution.py:32
  25.3 25.2 %collective-permute-start.12 = (bf16[256,512]{1,0:T(8,128)(2,1)S(1)}, bf16[256,512]{1,0:T(8,128)(2,1)S(1)}, u32[]{:S(2)}, u32[]{:S(2)}) collective-permute-start(bf16[256,512]{1,0:T(8,128)(2,1)S(1)} %collective-permute-done.8), channel_id=1, source_target_pairs={{0,2},{4,0},{8,4},{12,8},{14,12},{10,14},{6,10},{2,6},{1,3},{5,1},... | collective-permute-start | bytes 786440 | tf_op jit(solution)/shard_map/ppermute | solution.py:32
  32.2 11.0 %collective-permute-start.13 = (bf16[256,512]{1,0:T(8,128)(2,1)S(1)}, bf16[256,512]{1,0:T(8,128)(2,1)S(1)}, u32[]{:S(2)}, u32[]{:S(2)}) collective-permute-start(bf16[256,512]{1,0:T(8,128)(2,1)S(1)} %collective-permute-done.9), channel_id=1, source_target_pairs={{0,4},{4,8},{8,12},{12,14},{14,10},{10,6},{6,2},{2,0},{1,5},{5,9},... | collective-permute-start | bytes 786440 | tf_op jit(solution)/shard_map/ppermute | solution.py:32
  34.2 8.4 %collective-permute-start.14 = (bf16[256,512]{1,0:T(8,128)(2,1)S(1)}, bf16[256,512]{1,0:T(8,128)(2,1)S(1)}, u32[]{:S(2)}, u32[]{:S(2)}) collective-permute-start(bf16[256,512]{1,0:T(8,128)(2,1)S(1)} %collective-permute-done.10), channel_id=1, source_target_pairs={{0,2},{4,0},{8,4},{12,8},{14,12},{10,14},{6,10},{2,6},{1,3},{5,1},... | collective-permute-start | bytes 786440 | tf_op jit(solution)/shard_map/ppermute | solution.py:32
  34.4 12.3 %collective-permute-start.15 = (bf16[256,512]{1,0:T(8,128)(2,1)S(1)}, bf16[256,512]{1,0:T(8,128)(2,1)S(1)}, u32[]{:S(2)}, u32[]{:S(2)}) collective-permute-start(bf16[256,512]{1,0:T(8,128)(2,1)S(1)} %collective-permute-done.11), channel_id=1, source_target_pairs={{0,4},{4,8},{8,12},{12,14},{14,10},{10,6},{6,2},{2,0},{1,5},{5,9},... | collective-permute-start | bytes 786440 | tf_op jit(solution)/shard_map/ppermute | solution.py:32
  42.5 7.5 %collective-permute-start.16 = (bf16[256,512]{1,0:T(8,128)(2,1)S(1)}, bf16[256,512]{1,0:T(8,128)(2,1)S(1)}, u32[]{:S(2)}, u32[]{:S(2)}) collective-permute-start(bf16[256,512]{1,0:T(8,128)(2,1)S(1)} %collective-permute-done.14), channel_id=1, source_target_pairs={{0,2},{4,0},{8,4},{12,8},{14,12},{10,14},{6,10},{2,6},{1,3},{5,1},... | collective-permute-start | bytes 786440 | tf_op jit(solution)/shard_map/ppermute | solution.py:32
  55.6 7.6 %collective-permute-start.20 = (bf16[6,1024]{1,0:T(8,128)(2,1)S(1)}, bf16[6,1024]{1,0:T(8,128)(2,1)S(1)}, u32[]{:S(2)}, u32[]{:S(2)}) collective-permute-start(bf16[6,1024]{1,0:T(8,128)(2,1)S(1)} %maximum_select_fusion.2), channel_id=1, source_target_pairs={{24,0},{23,1},{28,4},{19,5},{30,8},{17,9},{26,12},{21,13},{22,14},... | collective-permute-start | bytes 36872 | tf_op jit(solution)/shard_map/ppermute | solution.py:64
  56.9 8.6 %collective-permute-start.21 = (bf16[6,1024]{1,0:T(8,128)(2,1)S(1)}, bf16[6,1024]{1,0:T(8,128)(2,1)S(1)}, u32[]{:S(2)}, u32[]{:S(2)}) collective-permute-start(bf16[6,1024]{1,0:T(8,128)(2,1)S(1)} %maximum_select_fusion.2), channel_id=1, source_target_pairs={{28,0},{19,1},{30,4},{17,5},{26,8},{21,9},{22,12},{25,13},{18,14},... | collective-permute-start | bytes 36872 | tf_op jit(solution)/shard_map/ppermute | solution.py:64
  68.9 9.2 %collective-permute-start.23 = (bf16[256,512]{1,0:T(8,128)(2,1)S(1)}, bf16[256,512]{1,0:T(8,128)(2,1)S(1)}, u32[]{:S(2)}, u32[]{:S(2)}) collective-permute-start(bf16[256,512]{1,0:T(8,128)(2,1)S(1)} %convolution_convert_fusion.3), channel_id=1, source_target_pairs={{0,4},{4,8},{8,12},{12,14},{14,10},{10,6},{6,2},{2,0},{1,5},{5,9},... | collective-permute-start | bytes 786440 | tf_op jit(solution)/shard_map/ppermute | solution.py:32
  70.5 15.3 %collective-permute-start.29 = (bf16[256,512]{1,0:T(8,128)(2,1)S(1)}, bf16[256,512]{1,0:T(8,128)(2,1)S(1)}, u32[]{:S(2)}, u32[]{:S(2)}) collective-permute-start(bf16[256,512]{1,0:T(8,128)(2,1)S(1)} %convolution_convert_fusion.2), channel_id=1, source_target_pairs={{0,2},{4,0},{8,4},{12,8},{14,12},{10,14},{6,10},{2,6},{1,3},{5,1},... | collective-permute-start | bytes 786440 | tf_op jit(solution)/shard_map/ppermute | solution.py:32
  71.4 12.3 %collective-permute-start.25 = (bf16[256,512]{1,0:T(8,128)(2,1)S(1)}, bf16[256,512]{1,0:T(8,128)(2,1)S(1)}, u32[]{:S(2)}, u32[]{:S(2)}) collective-permute-start(bf16[256,512]{1,0:T(8,128)(2,1)S(1)} %convolution_convert_fusion.1), channel_id=1, source_target_pairs={{0,4},{4,8},{8,12},{12,14},{14,10},{10,6},{6,2},{2,0},{1,5},{5,9},... | collective-permute-start | bytes 786440 | tf_op jit(solution)/shard_map/ppermute | solution.py:32
  73.4 13.4 %collective-permute-start.30 = (bf16[256,512]{1,0:T(8,128)(2,1)S(1)}, bf16[256,512]{1,0:T(8,128)(2,1)S(1)}, u32[]{:S(2)}, u32[]{:S(2)}) collective-permute-start(bf16[256,512]{1,0:T(8,128)(2,1)S(1)} %convolution_convert_fusion), channel_id=1, source_target_pairs={{0,2},{4,0},{8,4},{12,8},{14,12},{10,14},{6,10},{2,6},{1,3},{5,1},... | collective-permute-start | bytes 786440 | tf_op jit(solution)/shard_map/ppermute | solution.py:32
  78.6 11.1 %collective-permute-start.26 = (bf16[256,512]{1,0:T(8,128)(2,1)S(1)}, bf16[256,512]{1,0:T(8,128)(2,1)S(1)}, u32[]{:S(2)}, u32[]{:S(2)}) collective-permute-start(bf16[256,512]{1,0:T(8,128)(2,1)S(1)} %fusion.6), channel_id=1, source_target_pairs={{0,4},{4,8},{8,12},{12,14},{14,10},{10,6},{6,2},{2,0},{1,5},{5,9},... | collective-permute-start | bytes 786440 | tf_op jit(solution)/shard_map/ppermute | solution.py:32
  84.2 12.7 %collective-permute-start.27 = (bf16[256,512]{1,0:T(8,128)(2,1)S(1)}, bf16[256,512]{1,0:T(8,128)(2,1)S(1)}, u32[]{:S(2)}, u32[]{:S(2)}) collective-permute-start(bf16[256,512]{1,0:T(8,128)(2,1)S(1)} %fusion.5), channel_id=1, source_target_pairs={{0,4},{4,8},{8,12},{12,14},{14,10},{10,6},{6,2},{2,0},{1,5},{5,9},... | collective-permute-start | bytes 786440 | tf_op jit(solution)/shard_map/ppermute | solution.py:32
  86.1 9.3 %collective-permute-start.31 = (bf16[256,512]{1,0:T(8,128)(2,1)S(1)}, bf16[256,512]{1,0:T(8,128)(2,1)S(1)}, u32[]{:S(2)}, u32[]{:S(2)}) collective-permute-start(bf16[256,512]{1,0:T(8,128)(2,1)S(1)} %fusion.11), channel_id=1, source_target_pairs={{0,2},{4,0},{8,4},{12,8},{14,12},{10,14},{6,10},{2,6},{1,3},{5,1},... | collective-permute-start | bytes 786440 | tf_op jit(solution)/shard_map/ppermute | solution.py:32
  87.2 13.1 %collective-permute-start.32 = (bf16[256,512]{1,0:T(8,128)(2,1)S(1)}, bf16[256,512]{1,0:T(8,128)(2,1)S(1)}, u32[]{:S(2)}, u32[]{:S(2)}) collective-permute-start(bf16[256,512]{1,0:T(8,128)(2,1)S(1)} %fusion.10), channel_id=1, source_target_pairs={{0,2},{4,0},{8,4},{12,8},{14,12},{10,14},{6,10},{2,6},{1,3},{5,1},... | collective-permute-start | bytes 786440 | tf_op jit(solution)/shard_map/ppermute | solution.py:32
  87.8 16.9 %collective-permute-start.24 = (bf16[256,1024]{1,0:T(8,128)(2,1)S(1)}, bf16[256,1024]{1,0:T(8,128)(2,1)S(1)}, u32[]{:S(2)}, u32[]{:S(2)}) collective-permute-start(bf16[256,1024]{1,0:T(8,128)(2,1)S(1)} %convert_element_type.163), channel_id=1, source_target_pairs={{0,16},{1,17},{2,18},{3,19},{4,20},{5,21},{6,22},{7,23},{8,24},{9,... | collective-permute-start | bytes 1572872 | tf_op jit(solution)/shard_map/ppermute | solution.py:40
  95.9 8.0 %collective-permute-start.28 = (bf16[256,512]{1,0:T(8,128)(2,1)S(1)}, bf16[256,512]{1,0:T(8,128)(2,1)S(1)}, u32[]{:S(2)}, u32[]{:S(2)}) collective-permute-start(bf16[256,512]{1,0:T(8,128)(2,1)S(1)} %fusion.4), channel_id=1, source_target_pairs={{0,4},{4,8},{8,12},{12,14},{14,10},{10,6},{6,2},{2,0},{1,5},{5,9},... | collective-permute-start | bytes 786440 | tf_op jit(solution)/shard_map/ppermute | solution.py:32
  96.9 7.0 %collective-permute-start.33 = (bf16[256,512]{1,0:T(8,128)(2,1)S(1)}, bf16[256,512]{1,0:T(8,128)(2,1)S(1)}, u32[]{:S(2)}, u32[]{:S(2)}) collective-permute-start(bf16[256,512]{1,0:T(8,128)(2,1)S(1)} %fusion.9), channel_id=1, source_target_pairs={{0,2},{4,0},{8,4},{12,8},{14,12},{10,14},{6,10},{2,6},{1,3},{5,1},... | collective-permute-start | bytes 786440 | tf_op jit(solution)/shard_map/ppermute | solution.py:32
  98.4 8.7 %collective-permute-start.36 = (bf16[256,512]{1,0:T(8,128)(2,1)S(1)}, bf16[256,512]{1,0:T(8,128)(2,1)S(1)}, u32[]{:S(2)}, u32[]{:S(2)}) collective-permute-start(bf16[256,512]{1,0:T(8,128)(2,1)S(1)} %fusion.3), channel_id=1, source_target_pairs={{0,4},{4,8},{8,12},{12,14},{14,10},{10,6},{6,2},{2,0},{1,5},{5,9},... | collective-permute-start | bytes 786440 | tf_op jit(solution)/shard_map/ppermute | solution.py:32
  104.7 8.9 %collective-permute-start.37 = (bf16[256,512]{1,0:T(8,128)(2,1)S(1)}, bf16[256,512]{1,0:T(8,128)(2,1)S(1)}, u32[]{:S(2)}, u32[]{:S(2)}) collective-permute-start(bf16[256,512]{1,0:T(8,128)(2,1)S(1)} %fusion.7), channel_id=1, source_target_pairs={{0,2},{4,0},{8,4},{12,8},{14,12},{10,14},{6,10},{2,6},{1,3},{5,1},... | collective-permute-start | bytes 786440 | tf_op jit(solution)/shard_map/ppermute | solution.py:32
  106.2 10.3 %collective-permute-start.35 = (bf16[256,512]{1,0:T(8,128)(2,1)S(1)}, bf16[256,512]{1,0:T(8,128)(2,1)S(1)}, u32[]{:S(2)}, u32[]{:S(2)}) collective-permute-start(bf16[256,512]{1,0:T(8,128)(2,1)S(1)} %fusion.8), channel_id=1, source_target_pairs={{0,2},{4,0},{8,4},{12,8},{14,12},{10,14},{6,10},{2,6},{1,3},{5,1},... | collective-permute-start | bytes 786440 | tf_op jit(solution)/shard_map/ppermute | solution.py:32
  107.1 9.4 %collective-permute-start.34 = (bf16[256,512]{1,0:T(8,128)(2,1)S(1)}, bf16[256,512]{1,0:T(8,128)(2,1)S(1)}, u32[]{:S(2)}, u32[]{:S(2)}) collective-permute-start(bf16[256,512]{1,0:T(8,128)(2,1)S(1)} %fusion.2), channel_id=1, source_target_pairs={{0,4},{4,8},{8,12},{12,14},{14,10},{10,6},{6,2},{2,0},{1,5},{5,9},... | collective-permute-start | bytes 786440 | tf_op jit(solution)/shard_map/ppermute | solution.py:32
  (12 other events, 36.1 us)

commit v23 on v20

--- a/solution.py
+++ b/solution.py
@@ -250,6 +250,9 @@
             hops += [(step, three), (step, four)]
         arrived, previous, source = {}, delta, delta
         for hop, (step, ways) in enumerate(hops):
+            if hop == max(len(hops) - 3, 1):
+                owns = [term(0, i, late) for i in range(2)]
+                previous = after(owns, previous)
             totals = []
             for i, by in ways:
                 total = term(by * step, i, source)
@@ -268,9 +271,6 @@
                 copied = passed_on(weights)
             else:
                 source = late
-        owns = [term(0, i, late) for i in range(2)]
-        arrived[1, 1] = after(owns, arrived[1, 1])
-        arrived[0, -1] = after(owns, arrived[0, -1])
         mine, other = [
             owns[i] + arrived[i, 1].astype(jnp.float32) + arrived[i, -1].astype(jnp.float32)
             for i in range(2)

time: 115 us -> 115 us (level)
  no operation moved by 1% of the time
where the time goes in v23:
time: 115 us
  waiting for transfers between devices  44 us (38%)
  starting transfers between devices  40.1 us (35%)
  matrix products  15 us (13%)
  Pallas kernels  7.16 us (6%)
  local copies, waits for them, and re-layouts  4.88 us (4%)
  other arithmetic  3.22 us (3%)
    ppermute x28, waiting for transfers between devices, along_ring(): return lax.ppermute(block, 'chip', pairs)  33.7 us
    ppermute x28, starting transfers between devices, along_ring(): return lax.ppermute(block, 'chip', pairs)  32.2 us
    ppermute x4, waiting for transfers between devices, slab_blocks(): kept.append(lax.ppermute(stored, ('grp', 'chip', 'core'), pairs))  7.28 us
    pallas_call x2, Pallas kernels, normalize(): pl.pallas_call(functools.partial(normalize_kernel, 16), grid=(seqs,), in_...  7.16 us
    dot_general x16, matrix products, product(): jnp.dot(columns(offset, i), block, preferred_element_type=jnp.float32)  6.81 us
    dot_general x16, matrix products, term(): lax.dot_general(columns(offset, i), delta, (((0,), (0,)), ((), ())), pref...  6.59 us
    ppermute x4, starting transfers between devices, slab_blocks(): kept.append(lax.ppermute(stored, ('grp', 'chip', 'core'), pairs))  5.16 us
    unnamed x11, local copies, waits for them, and re-layouts  3.31 us
  transfers between devices with their start and end apart: 39, of which 23 were waited for; matrix products, arithmetic and copies ran while one was open for 14% of the time, Pallas kernels for 6%

profile of v23, /device:TPU:0, one launch (start us, length us, event | category | flops | bytes accessed | tf_op | source)
XLA Modules:
  0.0 114.9 jit_solution(7910910882311922914)
XLA Ops:
  1.8 3.0 %collective-permute-start.2 = (bf16[256,512]{1,0:T(8,128)(2,1)S(1)}, bf16[256,512]{1,0:T(8,128)(2,1)S(1)}, u32[]{:S(2)}, u32[]{:S(2)}) collective-permute-start(bf16[256,512]{1,0:T(8,128)(2,1)S(1)} %get-tuple-element.69), channel_id=1, source_target_pairs={{0,4},{4,8},{8,12},{12,14},{14,10},{10,6},{6,2},{2,0},{1,5},{5,9},... | collective-permute-start | bytes 786440 | tf_op jit(solution)/shard_map/ppermute | solution.py:32
  6.1 2.9 %collective-permute-start.5 = (bf16[256,512]{1,0:T(8,128)(2,1)S(1)}, bf16[256,512]{1,0:T(8,128)(2,1)S(1)}, u32[]{:S(2)}, u32[]{:S(2)}) collective-permute-start(bf16[256,512]{1,0:T(8,128)(2,1)S(1)} %collective-permute-done.1), channel_id=1, source_target_pairs={{0,2},{4,0},{8,4},{12,8},{14,12},{10,14},{6,10},{2,6},{1,3},{5,1},... | collective-permute-start | bytes 786440 | tf_op jit(solution)/shard_map/ppermute | solution.py:32
  9.1 2.5 %collective-permute-done.2 = bf16[256,512]{1,0:T(8,128)(2,1)S(1)} collective-permute-done((bf16[256,512]{1,0:T(8,128)(2,1)S(1)}, bf16[256,512]{1,0:T(8,128)(2,1)S(1)}, u32[]{:S(2)}, u32[]{:S(2)}) %collective-permute-start.2) | collective-permute-done | bytes 262176 | tf_op jit(solution)/shard_map/ppermute | solution.py:32
  11.5 2.5 %collective-permute-start.7 = (bf16[256,512]{1,0:T(8,128)(2,1)S(1)}, bf16[256,512]{1,0:T(8,128)(2,1)S(1)}, u32[]{:S(2)}, u32[]{:S(2)}) collective-permute-start(bf16[256,512]{1,0:T(8,128)(2,1)S(1)} %collective-permute-done.2), channel_id=1, source_target_pairs={{0,4},{4,8},{8,12},{12,14},{14,10},{10,6},{6,2},{2,0},{1,5},{5,9},... | collective-permute-start | bytes 786440 | tf_op jit(solution)/shard_map/ppermute | solution.py:32
  14.8 1.9 %copy-done = bf16[1,3,128,4096]{3,2,1,0:T(8,128)(2,1)S(1)} copy-done((bf16[1,3,128,4096]{3,2,1,0:T(8,128)(2,1)S(1)}, bf16[1,3,128,4096]{3,2,1,0:T(8,128)(2,1)}, u32[]{:S(2)}) %copy-start) | copy-done | bytes 3145752
  17.4 3.6 %shard_map.64.refs_0_ = bf16[768,4096]{1,0:T(8,128)(2,1)S(1)} custom-call(bf16[3,128,4096]{2,1,0:T(8,128)(2,1)S(1)} %bitcast.54, f32[1,4096]{1,0:T(1,128)S(1)} %bitcast.55), custom_call_target="tpu_custom_call" | custom-call | flops 9437184 | bytes 6291456 | tf_op jit(solution)/shard_map/pallas_call | solution.py:99
  21.0 2.1 %collective-permute-start.9 = (bf16[256,512]{1,0:T(8,128)(2,1)S(1)}, bf16[256,512]{1,0:T(8,128)(2,1)S(1)}, u32[]{:S(2)}, u32[]{:S(2)}) collective-permute-start(bf16[256,512]{1,0:T(8,128)(2,1)S(1)} %collective-permute-done.4), channel_id=1, source_target_pairs={{0,4},{4,8},{8,12},{12,14},{14,10},{10,6},{6,2},{2,0},{1,5},{5,9},... | collective-permute-start | bytes 786440 | tf_op jit(solution)/shard_map/ppermute | solution.py:32
  23.4 1.9 %collective-permute-start.11 = (bf16[256,512]{1,0:T(8,128)(2,1)S(1)}, bf16[256,512]{1,0:T(8,128)(2,1)S(1)}, u32[]{:S(2)}, u32[]{:S(2)}) collective-permute-start(bf16[256,512]{1,0:T(8,128)(2,1)S(1)} %collective-permute-done.7), channel_id=1, source_target_pairs={{0,4},{4,8},{8,12},{12,14},{14,10},{10,6},{6,2},{2,0},{1,5},{5,9},... | collective-permute-start | bytes 786440 | tf_op jit(solution)/shard_map/ppermute | solution.py:32
  25.4 3.6 %shard_map.65 = bf16[768,4096]{1,0:T(8,128)(2,1)S(1)} custom-call(bf16[3,128,4096]{2,1,0:T(8,128)(2,1)S(1)} %collective-permute-done.states_ref, f32[1,4096]{1,0:T(1,128)S(1)} %bitcast.56, bf16[768,4096]{1,0:T(8,128)(2,1)S(1)} %shard_map.64.refs_0_), custom_call_target="tpu_custom_call", output_to_operand_aliasing={{}: (2, {})} | custom-call | flops 9437184 | bytes 6291456 | tf_op jit(solution)/shard_map/pallas_call | solution.py:99
  32.2 1.9 %collective-permute-start.13 = (bf16[256,512]{1,0:T(8,128)(2,1)S(1)}, bf16[256,512]{1,0:T(8,128)(2,1)S(1)}, u32[]{:S(2)}, u32[]{:S(2)}) collective-permute-start(bf16[256,512]{1,0:T(8,128)(2,1)S(1)} %collective-permute-done.9), channel_id=1, source_target_pairs={{0,4},{4,8},{8,12},{12,14},{14,10},{10,6},{6,2},{2,0},{1,5},{5,9},... | collective-permute-start | bytes 786440 | tf_op jit(solution)/shard_map/ppermute | solution.py:32
  34.4 1.9 %collective-permute-start.15 = (bf16[256,512]{1,0:T(8,128)(2,1)S(1)}, bf16[256,512]{1,0:T(8,128)(2,1)S(1)}, u32[]{:S(2)}, u32[]{:S(2)}) collective-permute-start(bf16[256,512]{1,0:T(8,128)(2,1)S(1)} %collective-permute-done.11), channel_id=1, source_target_pairs={{0,4},{4,8},{8,12},{12,14},{14,10},{10,6},{6,2},{2,0},{1,5},{5,9},... | collective-permute-start | bytes 786440 | tf_op jit(solution)/shard_map/ppermute | solution.py:32
  38.8 3.7 %collective-permute-done.14 = bf16[256,512]{1,0:T(8,128)(2,1)S(1)} collective-permute-done((bf16[256,512]{1,0:T(8,128)(2,1)S(1)}, bf16[256,512]{1,0:T(8,128)(2,1)S(1)}, u32[]{:S(2)}, u32[]{:S(2)}) %collective-permute-start.14) | collective-permute-done | bytes 262176 | tf_op jit(solution)/shard_map/ppermute | solution.py:32
  43.6 3.1 %collective-permute-done.15 = bf16[256,512]{1,0:T(8,128)(2,1)S(1)} collective-permute-done((bf16[256,512]{1,0:T(8,128)(2,1)S(1)}, bf16[256,512]{1,0:T(8,128)(2,1)S(1)}, u32[]{:S(2)}, u32[]{:S(2)}) %collective-permute-start.15) | collective-permute-done | bytes 262176 | tf_op jit(solution)/shard_map/ppermute | solution.py:32
  47.0 3.0 %collective-permute-done.16 = bf16[256,512]{1,0:T(8,128)(2,1)S(1)} collective-permute-done((bf16[256,512]{1,0:T(8,128)(2,1)S(1)}, bf16[256,512]{1,0:T(8,128)(2,1)S(1)}, u32[]{:S(2)}, u32[]{:S(2)}) %collective-permute-start.16) | collective-permute-done | bytes 262176 | tf_op jit(solution)/shard_map/ppermute | solution.py:32
  58.7 2.3 %collective-permute-done.19 = bf16[6,1024]{1,0:T(8,128)(2,1)S(1)} collective-permute-done((bf16[6,1024]{1,0:T(8,128)(2,1)S(1)}, bf16[6,1024]{1,0:T(8,128)(2,1)S(1)}, u32[]{:S(2)}, u32[]{:S(2)}) %collective-permute-start.19) | collective-permute-done | bytes 12320 | tf_op jit(solution)/shard_map/ppermute | solution.py:64
  61.0 2.3 %collective-permute-done.20 = bf16[6,1024]{1,0:T(8,128)(2,1)S(1)} collective-permute-done((bf16[6,1024]{1,0:T(8,128)(2,1)S(1)}, bf16[6,1024]{1,0:T(8,128)(2,1)S(1)}, u32[]{:S(2)}, u32[]{:S(2)}) %collective-permute-start.20) | collective-permute-done | bytes 12320 | tf_op jit(solution)/shard_map/ppermute | solution.py:64
  63.3 2.3 %collective-permute-done.21 = bf16[6,1024]{1,0:T(8,128)(2,1)S(1)} collective-permute-done((bf16[6,1024]{1,0:T(8,128)(2,1)S(1)}, bf16[6,1024]{1,0:T(8,128)(2,1)S(1)}, u32[]{:S(2)}, u32[]{:S(2)}) %collective-permute-start.21) | collective-permute-done | bytes 12320 | tf_op jit(solution)/shard_map/ppermute | solution.py:64
  69.5 1.5 %collective-permute-start.23 = (bf16[256,512]{1,0:T(8,128)(2,1)S(1)}, bf16[256,512]{1,0:T(8,128)(2,1)S(1)}, u32[]{:S(2)}, u32[]{:S(2)}) collective-permute-start(bf16[256,512]{1,0:T(8,128)(2,1)S(1)} %convolution_convert_fusion.3), channel_id=1, source_target_pairs={{0,4},{4,8},{8,12},{12,14},{14,10},{10,6},{6,2},{2,0},{1,5},{5,9},... | collective-permute-start | bytes 786440 | tf_op jit(solution)/shard_map/ppermute | solution.py:32
  72.4 1.6 %collective-permute-start.26 = (bf16[256,512]{1,0:T(8,128)(2,1)S(1)}, bf16[256,512]{1,0:T(8,128)(2,1)S(1)}, u32[]{:S(2)}, u32[]{:S(2)}) collective-permute-start(bf16[256,512]{1,0:T(8,128)(2,1)S(1)} %convolution_convert_fusion.1), channel_id=1, source_target_pairs={{0,4},{4,8},{8,12},{12,14},{14,10},{10,6},{6,2},{2,0},{1,5},{5,9},... | collective-permute-start | bytes 786440 | tf_op jit(solution)/shard_map/ppermute | solution.py:32
  74.0 4.7 %collective-permute-done.23 = bf16[256,512]{1,0:T(8,128)(2,1)S(1)} collective-permute-done((bf16[256,512]{1,0:T(8,128)(2,1)S(1)}, bf16[256,512]{1,0:T(8,128)(2,1)S(1)}, u32[]{:S(2)}, u32[]{:S(2)}) %collective-permute-start.23) | collective-permute-done | bytes 262176 | tf_op jit(solution)/shard_map/ppermute | solution.py:32
  82.5 1.3 %collective-permute-done.27 = bf16[256,512]{1,0:T(8,128)(2,1)S(1)} collective-permute-done((bf16[256,512]{1,0:T(8,128)(2,1)S(1)}, bf16[256,512]{1,0:T(8,128)(2,1)S(1)}, u32[]{:S(2)}, u32[]{:S(2)}) %collective-permute-start.27) | collective-permute-done | bytes 262176 | tf_op jit(solution)/shard_map/ppermute | solution.py:32
  84.7 1.6 %collective-permute-start.30 = (bf16[256,512]{1,0:T(8,128)(2,1)S(1)}, bf16[256,512]{1,0:T(8,128)(2,1)S(1)}, u32[]{:S(2)}, u32[]{:S(2)}) collective-permute-start(bf16[256,512]{1,0:T(8,128)(2,1)S(1)} %fusion.5), channel_id=1, source_target_pairs={{0,4},{4,8},{8,12},{12,14},{14,10},{10,6},{6,2},{2,0},{1,5},{5,9},... | collective-permute-start | bytes 786440 | tf_op jit(solution)/shard_map/ppermute | solution.py:32
  86.9 1.8 %collective-permute-start.24 = (bf16[256,1024]{1,0:T(8,128)(2,1)S(1)}, bf16[256,1024]{1,0:T(8,128)(2,1)S(1)}, u32[]{:S(2)}, u32[]{:S(2)}) collective-permute-start(bf16[256,1024]{1,0:T(8,128)(2,1)S(1)} %convert_element_type.163), channel_id=1, source_target_pairs={{0,16},{1,17},{2,18},{3,19},{4,20},{5,21},{6,22},{7,23},{8,24},{9,... | collective-permute-start | bytes 1572872 | tf_op jit(solution)/shard_map/ppermute | solution.py:40
  90.9 2.1 %collective-permute-start.33 = (bf16[256,512]{1,0:T(8,128)(2,1)S(1)}, bf16[256,512]{1,0:T(8,128)(2,1)S(1)}, u32[]{:S(2)}, u32[]{:S(2)}) collective-permute-start(bf16[256,512]{1,0:T(8,128)(2,1)S(1)} %fusion.9), channel_id=1, source_target_pairs={{0,2},{4,0},{8,4},{12,8},{14,12},{10,14},{6,10},{2,6},{1,3},{5,1},... | collective-permute-start | bytes 786440 | tf_op jit(solution)/shard_map/ppermute | solution.py:32
  93.0 3.1 %collective-permute-done.30 = bf16[256,512]{1,0:T(8,128)(2,1)S(1)} collective-permute-done((bf16[256,512]{1,0:T(8,128)(2,1)S(1)}, bf16[256,512]{1,0:T(8,128)(2,1)S(1)}, u32[]{:S(2)}, u32[]{:S(2)}) %collective-permute-start.30) | collective-permute-done | bytes 262176 | tf_op jit(solution)/shard_map/ppermute | solution.py:32
  96.9 1.3 %collective-permute-start.36 = (bf16[256,512]{1,0:T(8,128)(2,1)S(1)}, bf16[256,512]{1,0:T(8,128)(2,1)S(1)}, u32[]{:S(2)}, u32[]{:S(2)}) collective-permute-start(bf16[256,512]{1,0:T(8,128)(2,1)S(1)} %fusion.3), channel_id=1, source_target_pairs={{0,4},{4,8},{8,12},{12,14},{14,10},{10,6},{6,2},{2,0},{1,5},{5,9},... | collective-permute-start | bytes 786440 | tf_op jit(solution)/shard_map/ppermute | solution.py:32
  98.2 1.6 %collective-permute-done.33 = bf16[256,512]{1,0:T(8,128)(2,1)S(1)} collective-permute-done((bf16[256,512]{1,0:T(8,128)(2,1)S(1)}, bf16[256,512]{1,0:T(8,128)(2,1)S(1)}, u32[]{:S(2)}, u32[]{:S(2)}) %collective-permute-start.33) | collective-permute-done | bytes 262176 | tf_op jit(solution)/shard_map/ppermute | solution.py:32
  99.8 2.4 %collective-permute-done.32 = bf16[256,512]{1,0:T(8,128)(2,1)S(1)} collective-permute-done((bf16[256,512]{1,0:T(8,128)(2,1)S(1)}, bf16[256,512]{1,0:T(8,128)(2,1)S(1)}, u32[]{:S(2)}, u32[]{:S(2)}) %collective-permute-start.32) | collective-permute-done | bytes 262176 | tf_op jit(solution)/shard_map/ppermute | solution.py:32
  103.1 1.6 %collective-permute-start.37 = (bf16[256,512]{1,0:T(8,128)(2,1)S(1)}, bf16[256,512]{1,0:T(8,128)(2,1)S(1)}, u32[]{:S(2)}, u32[]{:S(2)}) collective-permute-start(bf16[256,512]{1,0:T(8,128)(2,1)S(1)} %fusion.11), channel_id=1, source_target_pairs={{0,2},{4,0},{8,4},{12,8},{14,12},{10,14},{6,10},{2,6},{1,3},{5,1},... | collective-permute-start | bytes 786440 | tf_op jit(solution)/shard_map/ppermute | solution.py:32
  104.6 1.7 %collective-permute-start.35 = (bf16[256,512]{1,0:T(8,128)(2,1)S(1)}, bf16[256,512]{1,0:T(8,128)(2,1)S(1)}, u32[]{:S(2)}, u32[]{:S(2)}) collective-permute-start(bf16[256,512]{1,0:T(8,128)(2,1)S(1)} %fusion.10), channel_id=1, source_target_pairs={{0,2},{4,0},{8,4},{12,8},{14,12},{10,14},{6,10},{2,6},{1,3},{5,1},... | collective-permute-start | bytes 786440 | tf_op jit(solution)/shard_map/ppermute | solution.py:32
  107.6 2.9 %collective-permute-done.37 = bf16[256,512]{1,0:T(8,128)(2,1)S(1)} collective-permute-done((bf16[256,512]{1,0:T(8,128)(2,1)S(1)}, bf16[256,512]{1,0:T(8,128)(2,1)S(1)}, u32[]{:S(2)}, u32[]{:S(2)}) %collective-permute-start.37) | collective-permute-done | bytes 262176 | tf_op jit(solution)/shard_map/ppermute | solution.py:32
  110.7 2.6 %collective-permute-done.35 = bf16[256,512]{1,0:T(8,128)(2,1)S(1)} collective-permute-done((bf16[256,512]{1,0:T(8,128)(2,1)S(1)}, bf16[256,512]{1,0:T(8,128)(2,1)S(1)}, u32[]{:S(2)}, u32[]{:S(2)}) %collective-permute-start.35) | collective-permute-done | bytes 262176 | tf_op jit(solution)/shard_map/ppermute | solution.py:32
  (128 shorter events, 38.2 us)
Async XLA Ops:
  0.0 25.4 %collective-permute-start = (bf16[3,128,4096]{2,1,0:T(8,128)(2,1)}, bf16[3,128,4096]{2,1,0:T(8,128)(2,1)S(1)}, u32[]{:S(2)}, u32[]{:S(2)}) collective-permute-start(bf16[3,128,4096]{2,1,0:T(8,128)(2,1)} %bitcast.53), channel_id=1, source_target_pairs={{0,1},{1,0},{2,3},{3,2},{4,5},{5,4},{6,7},{7,6},{8,9},{9,8},{10,11... | collective-permute-start | bytes 9437192 | tf_op jit(solution)/shard_map/ppermute | solution.py:52
  1.8 9.7 %collective-permute-start.2 = (bf16[256,512]{1,0:T(8,128)(2,1)S(1)}, bf16[256,512]{1,0:T(8,128)(2,1)S(1)}, u32[]{:S(2)}, u32[]{:S(2)}) collective-permute-start(bf16[256,512]{1,0:T(8,128)(2,1)S(1)} %get-tuple-element.69), channel_id=1, source_target_pairs={{0,4},{4,8},{8,12},{12,14},{14,10},{10,6},{6,2},{2,0},{1,5},{5,9},... | collective-permute-start | bytes 786440 | tf_op jit(solution)/shard_map/ppermute | solution.py:32
  4.9 9.2 %collective-permute-start.3 = (bf16[256,512]{1,0:T(8,128)(2,1)S(1)}, bf16[256,512]{1,0:T(8,128)(2,1)S(1)}, u32[]{:S(2)}, u32[]{:S(2)}) collective-permute-start(bf16[256,512]{1,0:T(8,128)(2,1)S(1)} %get-tuple-element.69), channel_id=1, source_target_pairs={{0,2},{4,0},{8,4},{12,8},{14,12},{10,14},{6,10},{2,6},{1,3},{5,1},... | collective-permute-start | bytes 786440 | tf_op jit(solution)/shard_map/ppermute | solution.py:32
  6.1 14.8 %collective-permute-start.5 = (bf16[256,512]{1,0:T(8,128)(2,1)S(1)}, bf16[256,512]{1,0:T(8,128)(2,1)S(1)}, u32[]{:S(2)}, u32[]{:S(2)}) collective-permute-start(bf16[256,512]{1,0:T(8,128)(2,1)S(1)} %collective-permute-done.1), channel_id=1, source_target_pairs={{0,2},{4,0},{8,4},{12,8},{14,12},{10,14},{6,10},{2,6},{1,3},{5,1},... | collective-permute-start | bytes 786440 | tf_op jit(solution)/shard_map/ppermute | solution.py:32
  9.0 12.0 %collective-permute-start.4 = (bf16[256,512]{1,0:T(8,128)(2,1)S(1)}, bf16[256,512]{1,0:T(8,128)(2,1)S(1)}, u32[]{:S(2)}, u32[]{:S(2)}) collective-permute-start(bf16[256,512]{1,0:T(8,128)(2,1)S(1)} %collective-permute-done.1), channel_id=1, source_target_pairs={{0,4},{4,8},{8,12},{12,14},{14,10},{10,6},{6,2},{2,0},{1,5},{5,9},... | collective-permute-start | bytes 786440 | tf_op jit(solution)/shard_map/ppermute | solution.py:32
  11.5 11.9 %collective-permute-start.7 = (bf16[256,512]{1,0:T(8,128)(2,1)S(1)}, bf16[256,512]{1,0:T(8,128)(2,1)S(1)}, u32[]{:S(2)}, u32[]{:S(2)}) collective-permute-start(bf16[256,512]{1,0:T(8,128)(2,1)S(1)} %collective-permute-done.2), channel_id=1, source_target_pairs={{0,4},{4,8},{8,12},{12,14},{14,10},{10,6},{6,2},{2,0},{1,5},{5,9},... | collective-permute-start | bytes 786440 | tf_op jit(solution)/shard_map/ppermute | solution.py:32
  14.1 11.2 %collective-permute-start.8 = (bf16[256,512]{1,0:T(8,128)(2,1)S(1)}, bf16[256,512]{1,0:T(8,128)(2,1)S(1)}, u32[]{:S(2)}, u32[]{:S(2)}) collective-permute-start(bf16[256,512]{1,0:T(8,128)(2,1)S(1)} %collective-permute-done.3), channel_id=1, source_target_pairs={{0,2},{4,0},{8,4},{12,8},{14,12},{10,14},{6,10},{2,6},{1,3},{5,1},... | collective-permute-start | bytes 786440 | tf_op jit(solution)/shard_map/ppermute | solution.py:32
  21.0 11.3 %collective-permute-start.9 = (bf16[256,512]{1,0:T(8,128)(2,1)S(1)}, bf16[256,512]{1,0:T(8,128)(2,1)S(1)}, u32[]{:S(2)}, u32[]{:S(2)}) collective-permute-start(bf16[256,512]{1,0:T(8,128)(2,1)S(1)} %collective-permute-done.4), channel_id=1, source_target_pairs={{0,4},{4,8},{8,12},{12,14},{14,10},{10,6},{6,2},{2,0},{1,5},{5,9},... | collective-permute-start | bytes 786440 | tf_op jit(solution)/shard_map/ppermute | solution.py:32
  23.0 11.1 %collective-permute-start.10 = (bf16[256,512]{1,0:T(8,128)(2,1)S(1)}, bf16[256,512]{1,0:T(8,128)(2,1)S(1)}, u32[]{:S(2)}, u32[]{:S(2)}) collective-permute-start(bf16[256,512]{1,0:T(8,128)(2,1)S(1)} %collective-permute-done.5), channel_id=1, source_target_pairs={{0,2},{4,0},{8,4},{12,8},{14,12},{10,14},{6,10},{2,6},{1,3},{5,1},... | collective-permute-start | bytes 786440 | tf_op jit(solution)/shard_map/ppermute | solution.py:32
  23.4 10.9 %collective-permute-start.11 = (bf16[256,512]{1,0:T(8,128)(2,1)S(1)}, bf16[256,512]{1,0:T(8,128)(2,1)S(1)}, u32[]{:S(2)}, u32[]{:S(2)}) collective-permute-start(bf16[256,512]{1,0:T(8,128)(2,1)S(1)} %collective-permute-done.7), channel_id=1, source_target_pairs={{0,4},{4,8},{8,12},{12,14},{14,10},{10,6},{6,2},{2,0},{1,5},{5,9},... | collective-permute-start | bytes 786440 | tf_op jit(solution)/shard_map/ppermute | solution.py:32
  25.3 25.2 %collective-permute-start.12 = (bf16[256,512]{1,0:T(8,128)(2,1)S(1)}, bf16[256,512]{1,0:T(8,128)(2,1)S(1)}, u32[]{:S(2)}, u32[]{:S(2)}) collective-permute-start(bf16[256,512]{1,0:T(8,128)(2,1)S(1)} %collective-permute-done.8), channel_id=1, source_target_pairs={{0,2},{4,0},{8,4},{12,8},{14,12},{10,14},{6,10},{2,6},{1,3},{5,1},... | collective-permute-start | bytes 786440 | tf_op jit(solution)/shard_map/ppermute | solution.py:32
  32.2 11.0 %collective-permute-start.13 = (bf16[256,512]{1,0:T(8,128)(2,1)S(1)}, bf16[256,512]{1,0:T(8,128)(2,1)S(1)}, u32[]{:S(2)}, u32[]{:S(2)}) collective-permute-start(bf16[256,512]{1,0:T(8,128)(2,1)S(1)} %collective-permute-done.9), channel_id=1, source_target_pairs={{0,4},{4,8},{8,12},{12,14},{14,10},{10,6},{6,2},{2,0},{1,5},{5,9},... | collective-permute-start | bytes 786440 | tf_op jit(solution)/shard_map/ppermute | solution.py:32
  34.2 8.4 %collective-permute-start.14 = (bf16[256,512]{1,0:T(8,128)(2,1)S(1)}, bf16[256,512]{1,0:T(8,128)(2,1)S(1)}, u32[]{:S(2)}, u32[]{:S(2)}) collective-permute-start(bf16[256,512]{1,0:T(8,128)(2,1)S(1)} %collective-permute-done.10), channel_id=1, source_target_pairs={{0,2},{4,0},{8,4},{12,8},{14,12},{10,14},{6,10},{2,6},{1,3},{5,1},... | collective-permute-start | bytes 786440 | tf_op jit(solution)/shard_map/ppermute | solution.py:32
  34.4 12.3 %collective-permute-start.15 = (bf16[256,512]{1,0:T(8,128)(2,1)S(1)}, bf16[256,512]{1,0:T(8,128)(2,1)S(1)}, u32[]{:S(2)}, u32[]{:S(2)}) collective-permute-start(bf16[256,512]{1,0:T(8,128)(2,1)S(1)} %collective-permute-done.11), channel_id=1, source_target_pairs={{0,4},{4,8},{8,12},{12,14},{14,10},{10,6},{6,2},{2,0},{1,5},{5,9},... | collective-permute-start | bytes 786440 | tf_op jit(solution)/shard_map/ppermute | solution.py:32
  42.5 7.5 %collective-permute-start.16 = (bf16[256,512]{1,0:T(8,128)(2,1)S(1)}, bf16[256,512]{1,0:T(8,128)(2,1)S(1)}, u32[]{:S(2)}, u32[]{:S(2)}) collective-permute-start(bf16[256,512]{1,0:T(8,128)(2,1)S(1)} %collective-permute-done.14), channel_id=1, source_target_pairs={{0,2},{4,0},{8,4},{12,8},{14,12},{10,14},{6,10},{2,6},{1,3},{5,1},... | collective-permute-start | bytes 786440 | tf_op jit(solution)/shard_map/ppermute | solution.py:32
  55.6 7.6 %collective-permute-start.20 = (bf16[6,1024]{1,0:T(8,128)(2,1)S(1)}, bf16[6,1024]{1,0:T(8,128)(2,1)S(1)}, u32[]{:S(2)}, u32[]{:S(2)}) collective-permute-start(bf16[6,1024]{1,0:T(8,128)(2,1)S(1)} %maximum_select_fusion.2), channel_id=1, source_target_pairs={{24,0},{23,1},{28,4},{19,5},{30,8},{17,9},{26,12},{21,13},{22,14},... | collective-permute-start | bytes 36872 | tf_op jit(solution)/shard_map/ppermute | solution.py:64
  56.9 8.6 %collective-permute-start.21 = (bf16[6,1024]{1,0:T(8,128)(2,1)S(1)}, bf16[6,1024]{1,0:T(8,128)(2,1)S(1)}, u32[]{:S(2)}, u32[]{:S(2)}) collective-permute-start(bf16[6,1024]{1,0:T(8,128)(2,1)S(1)} %maximum_select_fusion.2), channel_id=1, source_target_pairs={{28,0},{19,1},{30,4},{17,5},{26,8},{21,9},{22,12},{25,13},{18,14},... | collective-permute-start | bytes 36872 | tf_op jit(solution)/shard_map/ppermute | solution.py:64
  68.9 10.6 %collective-permute-start.25 = (bf16[256,512]{1,0:T(8,128)(2,1)S(1)}, bf16[256,512]{1,0:T(8,128)(2,1)S(1)}, u32[]{:S(2)}, u32[]{:S(2)}) collective-permute-start(bf16[256,512]{1,0:T(8,128)(2,1)S(1)} %convolution_convert_fusion.2), channel_id=1, source_target_pairs={{0,2},{4,0},{8,4},{12,8},{14,12},{10,14},{6,10},{2,6},{1,3},{5,1},... | collective-permute-start | bytes 786440 | tf_op jit(solution)/shard_map/ppermute | solution.py:32
  69.5 9.2 %collective-permute-start.23 = (bf16[256,512]{1,0:T(8,128)(2,1)S(1)}, bf16[256,512]{1,0:T(8,128)(2,1)S(1)}, u32[]{:S(2)}, u32[]{:S(2)}) collective-permute-start(bf16[256,512]{1,0:T(8,128)(2,1)S(1)} %convolution_convert_fusion.3), channel_id=1, source_target_pairs={{0,4},{4,8},{8,12},{12,14},{14,10},{10,6},{6,2},{2,0},{1,5},{5,9},... | collective-permute-start | bytes 786440 | tf_op jit(solution)/shard_map/ppermute | solution.py:32
  71.4 12.3 %collective-permute-start.27 = (bf16[256,512]{1,0:T(8,128)(2,1)S(1)}, bf16[256,512]{1,0:T(8,128)(2,1)S(1)}, u32[]{:S(2)}, u32[]{:S(2)}) collective-permute-start(bf16[256,512]{1,0:T(8,128)(2,1)S(1)} %convolution_convert_fusion), channel_id=1, source_target_pairs={{0,2},{4,0},{8,4},{12,8},{14,12},{10,14},{6,10},{2,6},{1,3},{5,1},... | collective-permute-start | bytes 786440 | tf_op jit(solution)/shard_map/ppermute | solution.py:32
  72.4 11.9 %collective-permute-start.26 = (bf16[256,512]{1,0:T(8,128)(2,1)S(1)}, bf16[256,512]{1,0:T(8,128)(2,1)S(1)}, u32[]{:S(2)}, u32[]{:S(2)}) collective-permute-start(bf16[256,512]{1,0:T(8,128)(2,1)S(1)} %convolution_convert_fusion.1), channel_id=1, source_target_pairs={{0,4},{4,8},{8,12},{12,14},{14,10},{10,6},{6,2},{2,0},{1,5},{5,9},... | collective-permute-start | bytes 786440 | tf_op jit(solution)/shard_map/ppermute | solution.py:32
  80.4 9.3 %collective-permute-start.29 = (bf16[256,512]{1,0:T(8,128)(2,1)S(1)}, bf16[256,512]{1,0:T(8,128)(2,1)S(1)}, u32[]{:S(2)}, u32[]{:S(2)}) collective-permute-start(bf16[256,512]{1,0:T(8,128)(2,1)S(1)} %fusion.7), channel_id=1, source_target_pairs={{0,2},{4,0},{8,4},{12,8},{14,12},{10,14},{6,10},{2,6},{1,3},{5,1},... | collective-permute-start | bytes 786440 | tf_op jit(solution)/shard_map/ppermute | solution.py:32
  81.2 9.3 %collective-permute-start.28 = (bf16[256,512]{1,0:T(8,128)(2,1)S(1)}, bf16[256,512]{1,0:T(8,128)(2,1)S(1)}, u32[]{:S(2)}, u32[]{:S(2)}) collective-permute-start(bf16[256,512]{1,0:T(8,128)(2,1)S(1)} %fusion.6), channel_id=1, source_target_pairs={{0,4},{4,8},{8,12},{12,14},{14,10},{10,6},{6,2},{2,0},{1,5},{5,9},... | collective-permute-start | bytes 786440 | tf_op jit(solution)/shard_map/ppermute | solution.py:32
  84.7 11.4 %collective-permute-start.30 = (bf16[256,512]{1,0:T(8,128)(2,1)S(1)}, bf16[256,512]{1,0:T(8,128)(2,1)S(1)}, u32[]{:S(2)}, u32[]{:S(2)}) collective-permute-start(bf16[256,512]{1,0:T(8,128)(2,1)S(1)} %fusion.5), channel_id=1, source_target_pairs={{0,4},{4,8},{8,12},{12,14},{14,10},{10,6},{6,2},{2,0},{1,5},{5,9},... | collective-permute-start | bytes 786440 | tf_op jit(solution)/shard_map/ppermute | solution.py:32
  86.3 10.2 %collective-permute-start.31 = (bf16[256,512]{1,0:T(8,128)(2,1)S(1)}, bf16[256,512]{1,0:T(8,128)(2,1)S(1)}, u32[]{:S(2)}, u32[]{:S(2)}) collective-permute-start(bf16[256,512]{1,0:T(8,128)(2,1)S(1)} %fusion.8), channel_id=1, source_target_pairs={{0,2},{4,0},{8,4},{12,8},{14,12},{10,14},{6,10},{2,6},{1,3},{5,1},... | collective-permute-start | bytes 786440 | tf_op jit(solution)/shard_map/ppermute | solution.py:32
  86.9 16.2 %collective-permute-start.24 = (bf16[256,1024]{1,0:T(8,128)(2,1)S(1)}, bf16[256,1024]{1,0:T(8,128)(2,1)S(1)}, u32[]{:S(2)}, u32[]{:S(2)}) collective-permute-start(bf16[256,1024]{1,0:T(8,128)(2,1)S(1)} %convert_element_type.163), channel_id=1, source_target_pairs={{0,16},{1,17},{2,18},{3,19},{4,20},{5,21},{6,22},{7,23},{8,24},{9,... | collective-permute-start | bytes 1572872 | tf_op jit(solution)/shard_map/ppermute | solution.py:40
  90.9 9.0 %collective-permute-start.33 = (bf16[256,512]{1,0:T(8,128)(2,1)S(1)}, bf16[256,512]{1,0:T(8,128)(2,1)S(1)}, u32[]{:S(2)}, u32[]{:S(2)}) collective-permute-start(bf16[256,512]{1,0:T(8,128)(2,1)S(1)} %fusion.9), channel_id=1, source_target_pairs={{0,2},{4,0},{8,4},{12,8},{14,12},{10,14},{6,10},{2,6},{1,3},{5,1},... | collective-permute-start | bytes 786440 | tf_op jit(solution)/shard_map/ppermute | solution.py:32
  93.0 9.2 %collective-permute-start.32 = (bf16[256,512]{1,0:T(8,128)(2,1)S(1)}, bf16[256,512]{1,0:T(8,128)(2,1)S(1)}, u32[]{:S(2)}, u32[]{:S(2)}) collective-permute-start(bf16[256,512]{1,0:T(8,128)(2,1)S(1)} %fusion.4), channel_id=1, source_target_pairs={{0,4},{4,8},{8,12},{12,14},{14,10},{10,6},{6,2},{2,0},{1,5},{5,9},... | collective-permute-start | bytes 786440 | tf_op jit(solution)/shard_map/ppermute | solution.py:32
  96.9 10.7 %collective-permute-start.36 = (bf16[256,512]{1,0:T(8,128)(2,1)S(1)}, bf16[256,512]{1,0:T(8,128)(2,1)S(1)}, u32[]{:S(2)}, u32[]{:S(2)}) collective-permute-start(bf16[256,512]{1,0:T(8,128)(2,1)S(1)} %fusion.3), channel_id=1, source_target_pairs={{0,4},{4,8},{8,12},{12,14},{14,10},{10,6},{6,2},{2,0},{1,5},{5,9},... | collective-permute-start | bytes 786440 | tf_op jit(solution)/shard_map/ppermute | solution.py:32
  103.1 7.5 %collective-permute-start.37 = (bf16[256,512]{1,0:T(8,128)(2,1)S(1)}, bf16[256,512]{1,0:T(8,128)(2,1)S(1)}, u32[]{:S(2)}, u32[]{:S(2)}) collective-permute-start(bf16[256,512]{1,0:T(8,128)(2,1)S(1)} %fusion.11), channel_id=1, source_target_pairs={{0,2},{4,0},{8,4},{12,8},{14,12},{10,14},{6,10},{2,6},{1,3},{5,1},... | collective-permute-start | bytes 786440 | tf_op jit(solution)/shard_map/ppermute | solution.py:32
  104.6 8.7 %collective-permute-start.35 = (bf16[256,512]{1,0:T(8,128)(2,1)S(1)}, bf16[256,512]{1,0:T(8,128)(2,1)S(1)}, u32[]{:S(2)}, u32[]{:S(2)}) collective-permute-start(bf16[256,512]{1,0:T(8,128)(2,1)S(1)} %fusion.10), channel_id=1, source_target_pairs={{0,2},{4,0},{8,4},{12,8},{14,12},{10,14},{6,10},{2,6},{1,3},{5,1},... | collective-permute-start | bytes 786440 | tf_op jit(solution)/shard_map/ppermute | solution.py:32
  106.3 7.1 %collective-permute-start.34 = (bf16[256,512]{1,0:T(8,128)(2,1)S(1)}, bf16[256,512]{1,0:T(8,128)(2,1)S(1)}, u32[]{:S(2)}, u32[]{:S(2)}) collective-permute-start(bf16[256,512]{1,0:T(8,128)(2,1)S(1)} %fusion.2), channel_id=1, source_target_pairs={{0,4},{4,8},{8,12},{12,14},{14,10},{10,6},{6,2},{2,0},{1,5},{5,9},... | collective-permute-start | bytes 786440 | tf_op jit(solution)/shard_map/ppermute | solution.py:32
  (12 other events, 39.0 us)

commit v24 on v23

--- a/solution.py
+++ b/solution.py
@@ -250,8 +250,9 @@
             hops += [(step, three), (step, four)]
         arrived, previous, source = {}, delta, delta
         for hop, (step, ways) in enumerate(hops):
-            if hop == max(len(hops) - 3, 1):
-                owns = [term(0, i, late) for i in range(2)]
+            if hop == max(len(hops) - 2, 1):
+                released = after(previous, delta)
+                owns = [term(0, i, released) for i in range(2)]
                 previous = after(owns, previous)
             totals = []
             for i, by in ways:

time: 115 us -> 115 us (level)
  transfers between devices with their start and end apart: 39 -> 39, of which waited for: 23 -> 24; matrix products, arithmetic and copies ran while one was open for 14% -> 14% of each run, Pallas kernels for 6% -> 6%
where the time goes in v24:
time: 115 us
  waiting for transfers between devices  44 us (38%)
  starting transfers between devices  40.4 us (35%)
  matrix products  15 us (13%)
  Pallas kernels  7.16 us (6%)
  local copies, waits for them, and re-layouts  4.88 us (4%)
  other arithmetic  3.22 us (3%)
    ppermute x28, waiting for transfers between devices, along_ring(): return lax.ppermute(block, 'chip', pairs)  33.7 us
    ppermute x28, starting transfers between devices, along_ring(): return lax.ppermute(block, 'chip', pairs)  32.6 us
    ppermute x4, waiting for transfers between devices, slab_blocks(): kept.append(lax.ppermute(stored, ('grp', 'chip', 'core'), pairs))  7.28 us
    pallas_call x2, Pallas kernels, normalize(): pl.pallas_call(functools.partial(normalize_kernel, 16), grid=(seqs,), in_...  7.16 us
    dot_general x16, matrix products, product(): jnp.dot(columns(offset, i), block, preferred_element_type=jnp.float32)  6.81 us
    dot_general x16, matrix products, term(): lax.dot_general(columns(offset, i), delta, (((0,), (0,)), ((), ())), pref...  6.6 us
    ppermute x4, starting transfers between devices, slab_blocks(): kept.append(lax.ppermute(stored, ('grp', 'chip', 'core'), pairs))  5.16 us
    unnamed x11, local copies, waits for them, and re-layouts  3.31 us
  transfers between devices with their start and end apart: 39, of which 24 were waited for; matrix products, arithmetic and copies ran while one was open for 14% of the time, Pallas kernels for 6%

profile of v24, /device:TPU:0, one launch (start us, length us, event | category | flops | bytes accessed | tf_op | source)
XLA Modules:
  0.0 115.1 jit_solution(10299247056656827682)
XLA Ops:
  1.8 3.0 %collective-permute-start.2 = (bf16[256,512]{1,0:T(8,128)(2,1)S(1)}, bf16[256,512]{1,0:T(8,128)(2,1)S(1)}, u32[]{:S(2)}, u32[]{:S(2)}) collective-permute-start(bf16[256,512]{1,0:T(8,128)(2,1)S(1)} %get-tuple-element.71), channel_id=1, source_target_pairs={{0,4},{4,8},{8,12},{12,14},{14,10},{10,6},{6,2},{2,0},{1,5},{5,9},... | collective-permute-start | bytes 786440 | tf_op jit(solution)/shard_map/ppermute | solution.py:32
  6.1 2.9 %collective-permute-start.5 = (bf16[256,512]{1,0:T(8,128)(2,1)S(1)}, bf16[256,512]{1,0:T(8,128)(2,1)S(1)}, u32[]{:S(2)}, u32[]{:S(2)}) collective-permute-start(bf16[256,512]{1,0:T(8,128)(2,1)S(1)} %collective-permute-done.1), channel_id=1, source_target_pairs={{0,2},{4,0},{8,4},{12,8},{14,12},{10,14},{6,10},{2,6},{1,3},{5,1},... | collective-permute-start | bytes 786440 | tf_op jit(solution)/shard_map/ppermute | solution.py:32
  9.1 2.5 %collective-permute-done.2 = bf16[256,512]{1,0:T(8,128)(2,1)S(1)} collective-permute-done((bf16[256,512]{1,0:T(8,128)(2,1)S(1)}, bf16[256,512]{1,0:T(8,128)(2,1)S(1)}, u32[]{:S(2)}, u32[]{:S(2)}) %collective-permute-start.2) | collective-permute-done | bytes 262176 | tf_op jit(solution)/shard_map/ppermute | solution.py:32
  11.5 2.5 %collective-permute-start.7 = (bf16[256,512]{1,0:T(8,128)(2,1)S(1)}, bf16[256,512]{1,0:T(8,128)(2,1)S(1)}, u32[]{:S(2)}, u32[]{:S(2)}) collective-permute-start(bf16[256,512]{1,0:T(8,128)(2,1)S(1)} %collective-permute-done.2), channel_id=1, source_target_pairs={{0,4},{4,8},{8,12},{12,14},{14,10},{10,6},{6,2},{2,0},{1,5},{5,9},... | collective-permute-start | bytes 786440 | tf_op jit(solution)/shard_map/ppermute | solution.py:32
  14.8 1.9 %copy-done = bf16[1,3,128,4096]{3,2,1,0:T(8,128)(2,1)S(1)} copy-done((bf16[1,3,128,4096]{3,2,1,0:T(8,128)(2,1)S(1)}, bf16[1,3,128,4096]{3,2,1,0:T(8,128)(2,1)}, u32[]{:S(2)}) %copy-start) | copy-done | bytes 3145752
  17.4 3.6 %shard_map.64.refs_0_ = bf16[768,4096]{1,0:T(8,128)(2,1)S(1)} custom-call(bf16[3,128,4096]{2,1,0:T(8,128)(2,1)S(1)} %bitcast.54, f32[1,4096]{1,0:T(1,128)S(1)} %bitcast.55), custom_call_target="tpu_custom_call" | custom-call | flops 9437184 | bytes 6291456 | tf_op jit(solution)/shard_map/pallas_call | solution.py:99
  21.0 2.1 %collective-permute-start.9 = (bf16[256,512]{1,0:T(8,128)(2,1)S(1)}, bf16[256,512]{1,0:T(8,128)(2,1)S(1)}, u32[]{:S(2)}, u32[]{:S(2)}) collective-permute-start(bf16[256,512]{1,0:T(8,128)(2,1)S(1)} %collective-permute-done.4), channel_id=1, source_target_pairs={{0,4},{4,8},{8,12},{12,14},{14,10},{10,6},{6,2},{2,0},{1,5},{5,9},... | collective-permute-start | bytes 786440 | tf_op jit(solution)/shard_map/ppermute | solution.py:32
  23.4 1.9 %collective-permute-start.11 = (bf16[256,512]{1,0:T(8,128)(2,1)S(1)}, bf16[256,512]{1,0:T(8,128)(2,1)S(1)}, u32[]{:S(2)}, u32[]{:S(2)}) collective-permute-start(bf16[256,512]{1,0:T(8,128)(2,1)S(1)} %collective-permute-done.7), channel_id=1, source_target_pairs={{0,4},{4,8},{8,12},{12,14},{14,10},{10,6},{6,2},{2,0},{1,5},{5,9},... | collective-permute-start | bytes 786440 | tf_op jit(solution)/shard_map/ppermute | solution.py:32
  25.4 3.6 %shard_map.65 = bf16[768,4096]{1,0:T(8,128)(2,1)S(1)} custom-call(bf16[3,128,4096]{2,1,0:T(8,128)(2,1)S(1)} %collective-permute-done.states_ref, f32[1,4096]{1,0:T(1,128)S(1)} %bitcast.56, bf16[768,4096]{1,0:T(8,128)(2,1)S(1)} %shard_map.64.refs_0_), custom_call_target="tpu_custom_call", output_to_operand_aliasing={{}: (2, {})} | custom-call | flops 9437184 | bytes 6291456 | tf_op jit(solution)/shard_map/pallas_call | solution.py:99
  32.2 1.9 %collective-permute-start.13 = (bf16[256,512]{1,0:T(8,128)(2,1)S(1)}, bf16[256,512]{1,0:T(8,128)(2,1)S(1)}, u32[]{:S(2)}, u32[]{:S(2)}) collective-permute-start(bf16[256,512]{1,0:T(8,128)(2,1)S(1)} %collective-permute-done.9), channel_id=1, source_target_pairs={{0,4},{4,8},{8,12},{12,14},{14,10},{10,6},{6,2},{2,0},{1,5},{5,9},... | collective-permute-start | bytes 786440 | tf_op jit(solution)/shard_map/ppermute | solution.py:32
  34.4 1.9 %collective-permute-start.15 = (bf16[256,512]{1,0:T(8,128)(2,1)S(1)}, bf16[256,512]{1,0:T(8,128)(2,1)S(1)}, u32[]{:S(2)}, u32[]{:S(2)}) collective-permute-start(bf16[256,512]{1,0:T(8,128)(2,1)S(1)} %collective-permute-done.11), channel_id=1, source_target_pairs={{0,4},{4,8},{8,12},{12,14},{14,10},{10,6},{6,2},{2,0},{1,5},{5,9},... | collective-permute-start | bytes 786440 | tf_op jit(solution)/shard_map/ppermute | solution.py:32
  38.8 3.7 %collective-permute-done.14 = bf16[256,512]{1,0:T(8,128)(2,1)S(1)} collective-permute-done((bf16[256,512]{1,0:T(8,128)(2,1)S(1)}, bf16[256,512]{1,0:T(8,128)(2,1)S(1)}, u32[]{:S(2)}, u32[]{:S(2)}) %collective-permute-start.14) | collective-permute-done | bytes 262176 | tf_op jit(solution)/shard_map/ppermute | solution.py:32
  43.6 3.1 %collective-permute-done.15 = bf16[256,512]{1,0:T(8,128)(2,1)S(1)} collective-permute-done((bf16[256,512]{1,0:T(8,128)(2,1)S(1)}, bf16[256,512]{1,0:T(8,128)(2,1)S(1)}, u32[]{:S(2)}, u32[]{:S(2)}) %collective-permute-start.15) | collective-permute-done | bytes 262176 | tf_op jit(solution)/shard_map/ppermute | solution.py:32
  47.0 3.0 %collective-permute-done.16 = bf16[256,512]{1,0:T(8,128)(2,1)S(1)} collective-permute-done((bf16[256,512]{1,0:T(8,128)(2,1)S(1)}, bf16[256,512]{1,0:T(8,128)(2,1)S(1)}, u32[]{:S(2)}, u32[]{:S(2)}) %collective-permute-start.16) | collective-permute-done | bytes 262176 | tf_op jit(solution)/shard_map/ppermute | solution.py:32
  58.7 2.3 %collective-permute-done.19 = bf16[6,1024]{1,0:T(8,128)(2,1)S(1)} collective-permute-done((bf16[6,1024]{1,0:T(8,128)(2,1)S(1)}, bf16[6,1024]{1,0:T(8,128)(2,1)S(1)}, u32[]{:S(2)}, u32[]{:S(2)}) %collective-permute-start.19) | collective-permute-done | bytes 12320 | tf_op jit(solution)/shard_map/ppermute | solution.py:64
  61.0 2.3 %collective-permute-done.20 = bf16[6,1024]{1,0:T(8,128)(2,1)S(1)} collective-permute-done((bf16[6,1024]{1,0:T(8,128)(2,1)S(1)}, bf16[6,1024]{1,0:T(8,128)(2,1)S(1)}, u32[]{:S(2)}, u32[]{:S(2)}) %collective-permute-start.20) | collective-permute-done | bytes 12320 | tf_op jit(solution)/shard_map/ppermute | solution.py:64
  63.3 2.3 %collective-permute-done.21 = bf16[6,1024]{1,0:T(8,128)(2,1)S(1)} collective-permute-done((bf16[6,1024]{1,0:T(8,128)(2,1)S(1)}, bf16[6,1024]{1,0:T(8,128)(2,1)S(1)}, u32[]{:S(2)}, u32[]{:S(2)}) %collective-permute-start.21) | collective-permute-done | bytes 12320 | tf_op jit(solution)/shard_map/ppermute | solution.py:64
  69.5 1.5 %collective-permute-start.23 = (bf16[256,512]{1,0:T(8,128)(2,1)S(1)}, bf16[256,512]{1,0:T(8,128)(2,1)S(1)}, u32[]{:S(2)}, u32[]{:S(2)}) collective-permute-start(bf16[256,512]{1,0:T(8,128)(2,1)S(1)} %convolution_convert_fusion.3), channel_id=1, source_target_pairs={{0,4},{4,8},{8,12},{12,14},{14,10},{10,6},{6,2},{2,0},{1,5},{5,9},... | collective-permute-start | bytes 786440 | tf_op jit(solution)/shard_map/ppermute | solution.py:32
  72.4 1.6 %collective-permute-start.25 = (bf16[256,512]{1,0:T(8,128)(2,1)S(1)}, bf16[256,512]{1,0:T(8,128)(2,1)S(1)}, u32[]{:S(2)}, u32[]{:S(2)}) collective-permute-start(bf16[256,512]{1,0:T(8,128)(2,1)S(1)} %convolution_convert_fusion.1), channel_id=1, source_target_pairs={{0,4},{4,8},{8,12},{12,14},{14,10},{10,6},{6,2},{2,0},{1,5},{5,9},... | collective-permute-start | bytes 786440 | tf_op jit(solution)/shard_map/ppermute | solution.py:32
  74.0 4.2 %collective-permute-done.24 = bf16[256,512]{1,0:T(8,128)(2,1)S(1)} collective-permute-done((bf16[256,512]{1,0:T(8,128)(2,1)S(1)}, bf16[256,512]{1,0:T(8,128)(2,1)S(1)}, u32[]{:S(2)}, u32[]{:S(2)}) %collective-permute-start.24) | collective-permute-done | bytes 262176 | tf_op jit(solution)/shard_map/ppermute | solution.py:32
  81.6 2.1 %collective-permute-done.26 = bf16[256,512]{1,0:T(8,128)(2,1)S(1)} collective-permute-done((bf16[256,512]{1,0:T(8,128)(2,1)S(1)}, bf16[256,512]{1,0:T(8,128)(2,1)S(1)}, u32[]{:S(2)}, u32[]{:S(2)}) %collective-permute-start.26) | collective-permute-done | bytes 262176 | tf_op jit(solution)/shard_map/ppermute | solution.py:32
  84.7 1.6 %collective-permute-start.30 = (bf16[256,512]{1,0:T(8,128)(2,1)S(1)}, bf16[256,512]{1,0:T(8,128)(2,1)S(1)}, u32[]{:S(2)}, u32[]{:S(2)}) collective-permute-start(bf16[256,512]{1,0:T(8,128)(2,1)S(1)} %fusion.3), channel_id=1, source_target_pairs={{0,4},{4,8},{8,12},{12,14},{14,10},{10,6},{6,2},{2,0},{1,5},{5,9},... | collective-permute-start | bytes 786440 | tf_op jit(solution)/shard_map/ppermute | solution.py:32
  86.9 1.8 %collective-permute-start.29 = (bf16[256,1024]{1,0:T(8,128)(2,1)S(1)}, bf16[256,1024]{1,0:T(8,128)(2,1)S(1)}, u32[]{:S(2)}, u32[]{:S(2)}) collective-permute-start(bf16[256,1024]{1,0:T(8,128)(2,1)S(1)} %convert_element_type.178), channel_id=1, source_target_pairs={{0,16},{1,17},{2,18},{3,19},{4,20},{5,21},{6,22},{7,23},{8,24},{9,... | collective-permute-start | bytes 1572872 | tf_op jit(solution)/shard_map/ppermute | solution.py:40
  91.2 1.8 %collective-permute-start.33 = (bf16[256,512]{1,0:T(8,128)(2,1)S(1)}, bf16[256,512]{1,0:T(8,128)(2,1)S(1)}, u32[]{:S(2)}, u32[]{:S(2)}) collective-permute-start(bf16[256,512]{1,0:T(8,128)(2,1)S(1)} %fusion.7), channel_id=1, source_target_pairs={{0,2},{4,0},{8,4},{12,8},{14,12},{10,14},{6,10},{2,6},{1,3},{5,1},... | collective-permute-start | bytes 786440 | tf_op jit(solution)/shard_map/ppermute | solution.py:32
  93.3 2.3 %collective-permute-done.30 = bf16[256,512]{1,0:T(8,128)(2,1)S(1)} collective-permute-done((bf16[256,512]{1,0:T(8,128)(2,1)S(1)}, bf16[256,512]{1,0:T(8,128)(2,1)S(1)}, u32[]{:S(2)}, u32[]{:S(2)}) %collective-permute-start.30) | collective-permute-done | bytes 262176 | tf_op jit(solution)/shard_map/ppermute | solution.py:32
  96.4 1.6 %collective-permute-start.36 = (bf16[256,512]{1,0:T(8,128)(2,1)S(1)}, bf16[256,512]{1,0:T(8,128)(2,1)S(1)}, u32[]{:S(2)}, u32[]{:S(2)}) collective-permute-start(bf16[256,512]{1,0:T(8,128)(2,1)S(1)} %fusion.9), channel_id=1, source_target_pairs={{0,4},{4,8},{8,12},{12,14},{14,10},{10,6},{6,2},{2,0},{1,5},{5,9},... | collective-permute-start | bytes 786440 | tf_op jit(solution)/shard_map/ppermute | solution.py:32
  98.0 1.9 %collective-permute-done.33 = bf16[256,512]{1,0:T(8,128)(2,1)S(1)} collective-permute-done((bf16[256,512]{1,0:T(8,128)(2,1)S(1)}, bf16[256,512]{1,0:T(8,128)(2,1)S(1)}, u32[]{:S(2)}, u32[]{:S(2)}) %collective-permute-start.33) | collective-permute-done | bytes 262176 | tf_op jit(solution)/shard_map/ppermute | solution.py:32
  99.8 2.4 %collective-permute-done.32 = bf16[256,512]{1,0:T(8,128)(2,1)S(1)} collective-permute-done((bf16[256,512]{1,0:T(8,128)(2,1)S(1)}, bf16[256,512]{1,0:T(8,128)(2,1)S(1)}, u32[]{:S(2)}, u32[]{:S(2)}) %collective-permute-start.32) | collective-permute-done | bytes 262176 | tf_op jit(solution)/shard_map/ppermute | solution.py:32
  103.0 1.6 %collective-permute-start.37 = (bf16[256,512]{1,0:T(8,128)(2,1)S(1)}, bf16[256,512]{1,0:T(8,128)(2,1)S(1)}, u32[]{:S(2)}, u32[]{:S(2)}) collective-permute-start(bf16[256,512]{1,0:T(8,128)(2,1)S(1)} %fusion.11), channel_id=1, source_target_pairs={{0,2},{4,0},{8,4},{12,8},{14,12},{10,14},{6,10},{2,6},{1,3},{5,1},... | collective-permute-start | bytes 786440 | tf_op jit(solution)/shard_map/ppermute | solution.py:32
  104.7 1.6 %collective-permute-start.35 = (bf16[256,512]{1,0:T(8,128)(2,1)S(1)}, bf16[256,512]{1,0:T(8,128)(2,1)S(1)}, u32[]{:S(2)}, u32[]{:S(2)}) collective-permute-start(bf16[256,512]{1,0:T(8,128)(2,1)S(1)} %fusion.10), channel_id=1, source_target_pairs={{0,2},{4,0},{8,4},{12,8},{14,12},{10,14},{6,10},{2,6},{1,3},{5,1},... | collective-permute-start | bytes 786440 | tf_op jit(solution)/shard_map/ppermute | solution.py:32
  107.6 3.2 %collective-permute-done.37 = bf16[256,512]{1,0:T(8,128)(2,1)S(1)} collective-permute-done((bf16[256,512]{1,0:T(8,128)(2,1)S(1)}, bf16[256,512]{1,0:T(8,128)(2,1)S(1)}, u32[]{:S(2)}, u32[]{:S(2)}) %collective-permute-start.37) | collective-permute-done | bytes 262176 | tf_op jit(solution)/shard_map/ppermute | solution.py:32
  111.0 2.6 %collective-permute-done.35 = bf16[256,512]{1,0:T(8,128)(2,1)S(1)} collective-permute-done((bf16[256,512]{1,0:T(8,128)(2,1)S(1)}, bf16[256,512]{1,0:T(8,128)(2,1)S(1)}, u32[]{:S(2)}, u32[]{:S(2)}) %collective-permute-start.35) | collective-permute-done | bytes 262176 | tf_op jit(solution)/shard_map/ppermute | solution.py:32
  (128 shorter events, 38.5 us)
Async XLA Ops:
  0.0 25.4 %collective-permute-start = (bf16[3,128,4096]{2,1,0:T(8,128)(2,1)}, bf16[3,128,4096]{2,1,0:T(8,128)(2,1)S(1)}, u32[]{:S(2)}, u32[]{:S(2)}) collective-permute-start(bf16[3,128,4096]{2,1,0:T(8,128)(2,1)} %bitcast.53), channel_id=1, source_target_pairs={{0,1},{1,0},{2,3},{3,2},{4,5},{5,4},{6,7},{7,6},{8,9},{9,8},{10,11... | collective-permute-start | bytes 9437192 | tf_op jit(solution)/shard_map/ppermute | solution.py:52
  1.8 9.7 %collective-permute-start.2 = (bf16[256,512]{1,0:T(8,128)(2,1)S(1)}, bf16[256,512]{1,0:T(8,128)(2,1)S(1)}, u32[]{:S(2)}, u32[]{:S(2)}) collective-permute-start(bf16[256,512]{1,0:T(8,128)(2,1)S(1)} %get-tuple-element.71), channel_id=1, source_target_pairs={{0,4},{4,8},{8,12},{12,14},{14,10},{10,6},{6,2},{2,0},{1,5},{5,9},... | collective-permute-start | bytes 786440 | tf_op jit(solution)/shard_map/ppermute | solution.py:32
  4.9 9.2 %collective-permute-start.3 = (bf16[256,512]{1,0:T(8,128)(2,1)S(1)}, bf16[256,512]{1,0:T(8,128)(2,1)S(1)}, u32[]{:S(2)}, u32[]{:S(2)}) collective-permute-start(bf16[256,512]{1,0:T(8,128)(2,1)S(1)} %get-tuple-element.71), channel_id=1, source_target_pairs={{0,2},{4,0},{8,4},{12,8},{14,12},{10,14},{6,10},{2,6},{1,3},{5,1},... | collective-permute-start | bytes 786440 | tf_op jit(solution)/shard_map/ppermute | solution.py:32
  6.1 14.8 %collective-permute-start.5 = (bf16[256,512]{1,0:T(8,128)(2,1)S(1)}, bf16[256,512]{1,0:T(8,128)(2,1)S(1)}, u32[]{:S(2)}, u32[]{:S(2)}) collective-permute-start(bf16[256,512]{1,0:T(8,128)(2,1)S(1)} %collective-permute-done.1), channel_id=1, source_target_pairs={{0,2},{4,0},{8,4},{12,8},{14,12},{10,14},{6,10},{2,6},{1,3},{5,1},... | collective-permute-start | bytes 786440 | tf_op jit(solution)/shard_map/ppermute | solution.py:32
  9.0 12.0 %collective-permute-start.4 = (bf16[256,512]{1,0:T(8,128)(2,1)S(1)}, bf16[256,512]{1,0:T(8,128)(2,1)S(1)}, u32[]{:S(2)}, u32[]{:S(2)}) collective-permute-start(bf16[256,512]{1,0:T(8,128)(2,1)S(1)} %collective-permute-done.1), channel_id=1, source_target_pairs={{0,4},{4,8},{8,12},{12,14},{14,10},{10,6},{6,2},{2,0},{1,5},{5,9},... | collective-permute-start | bytes 786440 | tf_op jit(solution)/shard_map/ppermute | solution.py:32
  11.5 11.9 %collective-permute-start.7 = (bf16[256,512]{1,0:T(8,128)(2,1)S(1)}, bf16[256,512]{1,0:T(8,128)(2,1)S(1)}, u32[]{:S(2)}, u32[]{:S(2)}) collective-permute-start(bf16[256,512]{1,0:T(8,128)(2,1)S(1)} %collective-permute-done.2), channel_id=1, source_target_pairs={{0,4},{4,8},{8,12},{12,14},{14,10},{10,6},{6,2},{2,0},{1,5},{5,9},... | collective-permute-start | bytes 786440 | tf_op jit(solution)/shard_map/ppermute | solution.py:32
  14.1 11.2 %collective-permute-start.8 = (bf16[256,512]{1,0:T(8,128)(2,1)S(1)}, bf16[256,512]{1,0:T(8,128)(2,1)S(1)}, u32[]{:S(2)}, u32[]{:S(2)}) collective-permute-start(bf16[256,512]{1,0:T(8,128)(2,1)S(1)} %collective-permute-done.3), channel_id=1, source_target_pairs={{0,2},{4,0},{8,4},{12,8},{14,12},{10,14},{6,10},{2,6},{1,3},{5,1},... | collective-permute-start | bytes 786440 | tf_op jit(solution)/shard_map/ppermute | solution.py:32
  21.0 11.3 %collective-permute-start.9 = (bf16[256,512]{1,0:T(8,128)(2,1)S(1)}, bf16[256,512]{1,0:T(8,128)(2,1)S(1)}, u32[]{:S(2)}, u32[]{:S(2)}) collective-permute-start(bf16[256,512]{1,0:T(8,128)(2,1)S(1)} %collective-permute-done.4), channel_id=1, source_target_pairs={{0,4},{4,8},{8,12},{12,14},{14,10},{10,6},{6,2},{2,0},{1,5},{5,9},... | collective-permute-start | bytes 786440 | tf_op jit(solution)/shard_map/ppermute | solution.py:32
  23.0 11.1 %collective-permute-start.10 = (bf16[256,512]{1,0:T(8,128)(2,1)S(1)}, bf16[256,512]{1,0:T(8,128)(2,1)S(1)}, u32[]{:S(2)}, u32[]{:S(2)}) collective-permute-start(bf16[256,512]{1,0:T(8,128)(2,1)S(1)} %collective-permute-done.5), channel_id=1, source_target_pairs={{0,2},{4,0},{8,4},{12,8},{14,12},{10,14},{6,10},{2,6},{1,3},{5,1},... | collective-permute-start | bytes 786440 | tf_op jit(solution)/shard_map/ppermute | solution.py:32
  23.4 10.9 %collective-permute-start.11 = (bf16[256,512]{1,0:T(8,128)(2,1)S(1)}, bf16[256,512]{1,0:T(8,128)(2,1)S(1)}, u32[]{:S(2)}, u32[]{:S(2)}) collective-permute-start(bf16[256,512]{1,0:T(8,128)(2,1)S(1)} %collective-permute-done.7), channel_id=1, source_target_pairs={{0,4},{4,8},{8,12},{12,14},{14,10},{10,6},{6,2},{2,0},{1,5},{5,9},... | collective-permute-start | bytes 786440 | tf_op jit(solution)/shard_map/ppermute | solution.py:32
  25.3 25.2 %collective-permute-start.12 = (bf16[256,512]{1,0:T(8,128)(2,1)S(1)}, bf16[256,512]{1,0:T(8,128)(2,1)S(1)}, u32[]{:S(2)}, u32[]{:S(2)}) collective-permute-start(bf16[256,512]{1,0:T(8,128)(2,1)S(1)} %collective-permute-done.8), channel_id=1, source_target_pairs={{0,2},{4,0},{8,4},{12,8},{14,12},{10,14},{6,10},{2,6},{1,3},{5,1},... | collective-permute-start | bytes 786440 | tf_op jit(solution)/shard_map/ppermute | solution.py:32
  32.2 11.0 %collective-permute-start.13 = (bf16[256,512]{1,0:T(8,128)(2,1)S(1)}, bf16[256,512]{1,0:T(8,128)(2,1)S(1)}, u32[]{:S(2)}, u32[]{:S(2)}) collective-permute-start(bf16[256,512]{1,0:T(8,128)(2,1)S(1)} %collective-permute-done.9), channel_id=1, source_target_pairs={{0,4},{4,8},{8,12},{12,14},{14,10},{10,6},{6,2},{2,0},{1,5},{5,9},... | collective-permute-start | bytes 786440 | tf_op jit(solution)/shard_map/ppermute | solution.py:32
  34.2 8.4 %collective-permute-start.14 = (bf16[256,512]{1,0:T(8,128)(2,1)S(1)}, bf16[256,512]{1,0:T(8,128)(2,1)S(1)}, u32[]{:S(2)}, u32[]{:S(2)}) collective-permute-start(bf16[256,512]{1,0:T(8,128)(2,1)S(1)} %collective-permute-done.10), channel_id=1, source_target_pairs={{0,2},{4,0},{8,4},{12,8},{14,12},{10,14},{6,10},{2,6},{1,3},{5,1},... | collective-permute-start | bytes 786440 | tf_op jit(solution)/shard_map/ppermute | solution.py:32
  34.4 12.3 %collective-permute-start.15 = (bf16[256,512]{1,0:T(8,128)(2,1)S(1)}, bf16[256,512]{1,0:T(8,128)(2,1)S(1)}, u32[]{:S(2)}, u32[]{:S(2)}) collective-permute-start(bf16[256,512]{1,0:T(8,128)(2,1)S(1)} %collective-permute-done.11), channel_id=1, source_target_pairs={{0,4},{4,8},{8,12},{12,14},{14,10},{10,6},{6,2},{2,0},{1,5},{5,9},... | collective-permute-start | bytes 786440 | tf_op jit(solution)/shard_map/ppermute | solution.py:32
  42.5 7.5 %collective-permute-start.16 = (bf16[256,512]{1,0:T(8,128)(2,1)S(1)}, bf16[256,512]{1,0:T(8,128)(2,1)S(1)}, u32[]{:S(2)}, u32[]{:S(2)}) collective-permute-start(bf16[256,512]{1,0:T(8,128)(2,1)S(1)} %collective-permute-done.14), channel_id=1, source_target_pairs={{0,2},{4,0},{8,4},{12,8},{14,12},{10,14},{6,10},{2,6},{1,3},{5,1},... | collective-permute-start | bytes 786440 | tf_op jit(solution)/shard_map/ppermute | solution.py:32
  55.6 7.6 %collective-permute-start.20 = (bf16[6,1024]{1,0:T(8,128)(2,1)S(1)}, bf16[6,1024]{1,0:T(8,128)(2,1)S(1)}, u32[]{:S(2)}, u32[]{:S(2)}) collective-permute-start(bf16[6,1024]{1,0:T(8,128)(2,1)S(1)} %maximum_select_fusion.2), channel_id=1, source_target_pairs={{24,0},{23,1},{28,4},{19,5},{30,8},{17,9},{26,12},{21,13},{22,14},... | collective-permute-start | bytes 36872 | tf_op jit(solution)/shard_map/ppermute | solution.py:64
  56.9 8.6 %collective-permute-start.21 = (bf16[6,1024]{1,0:T(8,128)(2,1)S(1)}, bf16[6,1024]{1,0:T(8,128)(2,1)S(1)}, u32[]{:S(2)}, u32[]{:S(2)}) collective-permute-start(bf16[6,1024]{1,0:T(8,128)(2,1)S(1)} %maximum_select_fusion.2), channel_id=1, source_target_pairs={{28,0},{19,1},{30,4},{17,5},{26,8},{21,9},{22,12},{25,13},{18,14},... | collective-permute-start | bytes 36872 | tf_op jit(solution)/shard_map/ppermute | solution.py:64
  68.9 9.2 %collective-permute-start.24 = (bf16[256,512]{1,0:T(8,128)(2,1)S(1)}, bf16[256,512]{1,0:T(8,128)(2,1)S(1)}, u32[]{:S(2)}, u32[]{:S(2)}) collective-permute-start(bf16[256,512]{1,0:T(8,128)(2,1)S(1)} %convolution_convert_fusion.2), channel_id=1, source_target_pairs={{0,2},{4,0},{8,4},{12,8},{14,12},{10,14},{6,10},{2,6},{1,3},{5,1},... | collective-permute-start | bytes 786440 | tf_op jit(solution)/shard_map/ppermute | solution.py:32
  69.5 9.2 %collective-permute-start.23 = (bf16[256,512]{1,0:T(8,128)(2,1)S(1)}, bf16[256,512]{1,0:T(8,128)(2,1)S(1)}, u32[]{:S(2)}, u32[]{:S(2)}) collective-permute-start(bf16[256,512]{1,0:T(8,128)(2,1)S(1)} %convolution_convert_fusion.3), channel_id=1, source_target_pairs={{0,4},{4,8},{8,12},{12,14},{14,10},{10,6},{6,2},{2,0},{1,5},{5,9},... | collective-permute-start | bytes 786440 | tf_op jit(solution)/shard_map/ppermute | solution.py:32
  71.4 12.3 %collective-permute-start.26 = (bf16[256,512]{1,0:T(8,128)(2,1)S(1)}, bf16[256,512]{1,0:T(8,128)(2,1)S(1)}, u32[]{:S(2)}, u32[]{:S(2)}) collective-permute-start(bf16[256,512]{1,0:T(8,128)(2,1)S(1)} %convolution_convert_fusion), channel_id=1, source_target_pairs={{0,2},{4,0},{8,4},{12,8},{14,12},{10,14},{6,10},{2,6},{1,3},{5,1},... | collective-permute-start | bytes 786440 | tf_op jit(solution)/shard_map/ppermute | solution.py:32
  72.4 11.9 %collective-permute-start.25 = (bf16[256,512]{1,0:T(8,128)(2,1)S(1)}, bf16[256,512]{1,0:T(8,128)(2,1)S(1)}, u32[]{:S(2)}, u32[]{:S(2)}) collective-permute-start(bf16[256,512]{1,0:T(8,128)(2,1)S(1)} %convolution_convert_fusion.1), channel_id=1, source_target_pairs={{0,4},{4,8},{8,12},{12,14},{14,10},{10,6},{6,2},{2,0},{1,5},{5,9},... | collective-permute-start | bytes 786440 | tf_op jit(solution)/shard_map/ppermute | solution.py:32
  79.5 9.8 %collective-permute-start.28 = (bf16[256,512]{1,0:T(8,128)(2,1)S(1)}, bf16[256,512]{1,0:T(8,128)(2,1)S(1)}, u32[]{:S(2)}, u32[]{:S(2)}) collective-permute-start(bf16[256,512]{1,0:T(8,128)(2,1)S(1)} %fusion.5), channel_id=1, source_target_pairs={{0,2},{4,0},{8,4},{12,8},{14,12},{10,14},{6,10},{2,6},{1,3},{5,1},... | collective-permute-start | bytes 786440 | tf_op jit(solution)/shard_map/ppermute | solution.py:32
  80.3 9.6 %collective-permute-start.27 = (bf16[256,512]{1,0:T(8,128)(2,1)S(1)}, bf16[256,512]{1,0:T(8,128)(2,1)S(1)}, u32[]{:S(2)}, u32[]{:S(2)}) collective-permute-start(bf16[256,512]{1,0:T(8,128)(2,1)S(1)} %fusion.4), channel_id=1, source_target_pairs={{0,4},{4,8},{8,12},{12,14},{14,10},{10,6},{6,2},{2,0},{1,5},{5,9},... | collective-permute-start | bytes 786440 | tf_op jit(solution)/shard_map/ppermute | solution.py:32
  84.7 10.8 %collective-permute-start.30 = (bf16[256,512]{1,0:T(8,128)(2,1)S(1)}, bf16[256,512]{1,0:T(8,128)(2,1)S(1)}, u32[]{:S(2)}, u32[]{:S(2)}) collective-permute-start(bf16[256,512]{1,0:T(8,128)(2,1)S(1)} %fusion.3), channel_id=1, source_target_pairs={{0,4},{4,8},{8,12},{12,14},{14,10},{10,6},{6,2},{2,0},{1,5},{5,9},... | collective-permute-start | bytes 786440 | tf_op jit(solution)/shard_map/ppermute | solution.py:32
  86.3 9.7 %collective-permute-start.31 = (bf16[256,512]{1,0:T(8,128)(2,1)S(1)}, bf16[256,512]{1,0:T(8,128)(2,1)S(1)}, u32[]{:S(2)}, u32[]{:S(2)}) collective-permute-start(bf16[256,512]{1,0:T(8,128)(2,1)S(1)} %fusion.6), channel_id=1, source_target_pairs={{0,2},{4,0},{8,4},{12,8},{14,12},{10,14},{6,10},{2,6},{1,3},{5,1},... | collective-permute-start | bytes 786440 | tf_op jit(solution)/shard_map/ppermute | solution.py:32
  86.9 16.1 %collective-permute-start.29 = (bf16[256,1024]{1,0:T(8,128)(2,1)S(1)}, bf16[256,1024]{1,0:T(8,128)(2,1)S(1)}, u32[]{:S(2)}, u32[]{:S(2)}) collective-permute-start(bf16[256,1024]{1,0:T(8,128)(2,1)S(1)} %convert_element_type.178), channel_id=1, source_target_pairs={{0,16},{1,17},{2,18},{3,19},{4,20},{5,21},{6,22},{7,23},{8,24},{9,... | collective-permute-start | bytes 1572872 | tf_op jit(solution)/shard_map/ppermute | solution.py:40
  91.2 8.7 %collective-permute-start.33 = (bf16[256,512]{1,0:T(8,128)(2,1)S(1)}, bf16[256,512]{1,0:T(8,128)(2,1)S(1)}, u32[]{:S(2)}, u32[]{:S(2)}) collective-permute-start(bf16[256,512]{1,0:T(8,128)(2,1)S(1)} %fusion.7), channel_id=1, source_target_pairs={{0,2},{4,0},{8,4},{12,8},{14,12},{10,14},{6,10},{2,6},{1,3},{5,1},... | collective-permute-start | bytes 786440 | tf_op jit(solution)/shard_map/ppermute | solution.py:32
  93.0 9.2 %collective-permute-start.32 = (bf16[256,512]{1,0:T(8,128)(2,1)S(1)}, bf16[256,512]{1,0:T(8,128)(2,1)S(1)}, u32[]{:S(2)}, u32[]{:S(2)}) collective-permute-start(bf16[256,512]{1,0:T(8,128)(2,1)S(1)} %fusion.2), channel_id=1, source_target_pairs={{0,4},{4,8},{8,12},{12,14},{14,10},{10,6},{6,2},{2,0},{1,5},{5,9},... | collective-permute-start | bytes 786440 | tf_op jit(solution)/shard_map/ppermute | solution.py:32
  96.4 11.2 %collective-permute-start.36 = (bf16[256,512]{1,0:T(8,128)(2,1)S(1)}, bf16[256,512]{1,0:T(8,128)(2,1)S(1)}, u32[]{:S(2)}, u32[]{:S(2)}) collective-permute-start(bf16[256,512]{1,0:T(8,128)(2,1)S(1)} %fusion.9), channel_id=1, source_target_pairs={{0,4},{4,8},{8,12},{12,14},{14,10},{10,6},{6,2},{2,0},{1,5},{5,9},... | collective-permute-start | bytes 786440 | tf_op jit(solution)/shard_map/ppermute | solution.py:32
  103.0 7.7 %collective-permute-start.37 = (bf16[256,512]{1,0:T(8,128)(2,1)S(1)}, bf16[256,512]{1,0:T(8,128)(2,1)S(1)}, u32[]{:S(2)}, u32[]{:S(2)}) collective-permute-start(bf16[256,512]{1,0:T(8,128)(2,1)S(1)} %fusion.11), channel_id=1, source_target_pairs={{0,2},{4,0},{8,4},{12,8},{14,12},{10,14},{6,10},{2,6},{1,3},{5,1},... | collective-permute-start | bytes 786440 | tf_op jit(solution)/shard_map/ppermute | solution.py:32
  104.7 8.9 %collective-permute-start.35 = (bf16[256,512]{1,0:T(8,128)(2,1)S(1)}, bf16[256,512]{1,0:T(8,128)(2,1)S(1)}, u32[]{:S(2)}, u32[]{:S(2)}) collective-permute-start(bf16[256,512]{1,0:T(8,128)(2,1)S(1)} %fusion.10), channel_id=1, source_target_pairs={{0,2},{4,0},{8,4},{12,8},{14,12},{10,14},{6,10},{2,6},{1,3},{5,1},... | collective-permute-start | bytes 786440 | tf_op jit(solution)/shard_map/ppermute | solution.py:32
  106.3 7.3 %collective-permute-start.34 = (bf16[256,512]{1,0:T(8,128)(2,1)S(1)}, bf16[256,512]{1,0:T(8,128)(2,1)S(1)}, u32[]{:S(2)}, u32[]{:S(2)}) collective-permute-start(bf16[256,512]{1,0:T(8,128)(2,1)S(1)} %fusion.8), channel_id=1, source_target_pairs={{0,4},{4,8},{8,12},{12,14},{14,10},{10,6},{6,2},{2,0},{1,5},{5,9},... | collective-permute-start | bytes 786440 | tf_op jit(solution)/shard_map/ppermute | solution.py:32
  (12 other events, 39.9 us)

commit v25 on v20

--- a/solution.py
+++ b/solution.py
@@ -138,7 +138,7 @@
     given = cut(weights, 1, given_columns, half).astype(jnp.bfloat16)
     sibling = from_sibling(given)
 
-    other_states = from_sibling(states)
+    other_states = from_sibling(after(own, states))
     sent = [(0, 1), (0, -1), (1, 1), (1, -1)]
     normed_own = normalize(states, gain, 0)
     normed = normalize(other_states, gain, 1, normed_own)

time: 115 us -> 116 us (level)
  waiting for transfers between devices: 43.5 us -> 45.6 us
  starting transfers between devices: 40.9 us -> 39.2 us
    ppermute x28, starting transfers between devices: 33.1 us -> 31 us  [along_ring(): return lax.ppermute(block, 'chip', pairs)]
    ppermute x6, waiting for transfers between devices: 3.01 us -> 4.27 us  [from_sibling(): return lax.ppermute(block, 'core', [(0, 1), (1, 0)])]
  transfers between devices with their start and end apart: 39 -> 39, of which waited for: 23 -> 23; matrix products, arithmetic and copies ran while one was open for 14% -> 12% of each run, Pallas kernels for 6% -> 6%
where the time goes in v25:
time: 116 us; the launch traced here: 115 us
  waiting for transfers between devices  45.6 us (39%)
  starting transfers between devices  39.2 us (34%)
  matrix products  14.7 us (13%)
  Pallas kernels  7.16 us (6%)
  local copies, waits for them, and re-layouts  4.98 us (4%)
  other arithmetic  3.24 us (3%)
    ppermute x28, waiting for transfers between devices, along_ring(): return lax.ppermute(block, 'chip', pairs)  33.8 us
    ppermute x28, starting transfers between devices, along_ring(): return lax.ppermute(block, 'chip', pairs)  31 us
    ppermute x4, waiting for transfers between devices, slab_blocks(): kept.append(lax.ppermute(stored, ('grp', 'chip', 'core'), pairs))  7.51 us
    pallas_call x2, Pallas kernels, normalize(): pl.pallas_call(functools.partial(normalize_kernel, 16), grid=(seqs,), in_...  7.16 us
    dot_general x16, matrix products, term(): lax.dot_general(columns(offset, i), delta, (((0,), (0,)), ((), ())), pref...  6.58 us
    dot_general x16, matrix products, product(): jnp.dot(columns(offset, i), block, preferred_element_type=jnp.float32)  6.53 us
    ppermute x4, starting transfers between devices, slab_blocks(): kept.append(lax.ppermute(stored, ('grp', 'chip', 'core'), pairs))  5.16 us
    ppermute x6, waiting for transfers between devices, from_sibling(): return lax.ppermute(block, 'core', [(0, 1), (1, 0)])  4.27 us
  transfers between devices with their start and end apart: 39, of which 23 were waited for; matrix products, arithmetic and copies ran while one was open for 12% of the time, Pallas kernels for 6%

profile of v25, /device:TPU:0, one launch (start us, length us, event | category | flops | bytes accessed | tf_op | source)
XLA Modules:
  0.0 115.4 jit_solution(4338686916235665184)
XLA Ops:
  1.9 3.0 %collective-permute-start.2 = (bf16[256,512]{1,0:T(8,128)(2,1)S(1)}, bf16[256,512]{1,0:T(8,128)(2,1)S(1)}, u32[]{:S(2)}, u32[]{:S(2)}) collective-permute-start(bf16[256,512]{1,0:T(8,128)(2,1)S(1)} %get-tuple-element.71), channel_id=1, source_target_pairs={{0,4},{4,8},{8,12},{12,14},{14,10},{10,6},{6,2},{2,0},{1,5},{5,9},... | collective-permute-start | bytes 786440 | tf_op jit(solution)/shard_map/ppermute | solution.py:32
  4.9 2.5 %collective-permute-done.1 = bf16[256,512]{1,0:T(8,128)(2,1)S(1)} collective-permute-done((bf16[256,512]{1,0:T(8,128)(2,1)S(1)}, bf16[256,512]{1,0:T(8,128)(2,1)S(1)}, u32[]{:S(2)}, u32[]{:S(2)}) %collective-permute-start.1) | collective-permute-done | bytes 262176 | tf_op jit(solution)/shard_map/ppermute | solution.py:52
  7.4 2.6 %collective-permute-start.5 = (bf16[256,512]{1,0:T(8,128)(2,1)S(1)}, bf16[256,512]{1,0:T(8,128)(2,1)S(1)}, u32[]{:S(2)}, u32[]{:S(2)}) collective-permute-start(bf16[256,512]{1,0:T(8,128)(2,1)S(1)} %collective-permute-done.1), channel_id=1, source_target_pairs={{0,2},{4,0},{8,4},{12,8},{14,12},{10,14},{6,10},{2,6},{1,3},{5,1},... | collective-permute-start | bytes 786440 | tf_op jit(solution)/shard_map/ppermute | solution.py:32
  10.0 1.3 %collective-permute-done.2 = bf16[256,512]{1,0:T(8,128)(2,1)S(1)} collective-permute-done((bf16[256,512]{1,0:T(8,128)(2,1)S(1)}, bf16[256,512]{1,0:T(8,128)(2,1)S(1)}, u32[]{:S(2)}, u32[]{:S(2)}) %collective-permute-start.2) | collective-permute-done | bytes 262176 | tf_op jit(solution)/shard_map/ppermute | solution.py:32
  11.4 1.9 %collective-permute-start.7 = (bf16[256,512]{1,0:T(8,128)(2,1)S(1)}, bf16[256,512]{1,0:T(8,128)(2,1)S(1)}, u32[]{:S(2)}, u32[]{:S(2)}) collective-permute-start(bf16[256,512]{1,0:T(8,128)(2,1)S(1)} %collective-permute-done.2), channel_id=1, source_target_pairs={{0,4},{4,8},{8,12},{12,14},{14,10},{10,6},{6,2},{2,0},{1,5},{5,9},... | collective-permute-start | bytes 786440 | tf_op jit(solution)/shard_map/ppermute | solution.py:32
  14.8 1.9 %copy-done = bf16[1,3,128,4096]{3,2,1,0:T(8,128)(2,1)S(1)} copy-done((bf16[1,3,128,4096]{3,2,1,0:T(8,128)(2,1)S(1)}, bf16[1,3,128,4096]{3,2,1,0:T(8,128)(2,1)}, u32[]{:S(2)}) %copy-start) | copy-done | bytes 3145752
  17.4 3.6 %shard_map.64.refs_0_ = bf16[768,4096]{1,0:T(8,128)(2,1)S(1)} custom-call(bf16[3,128,4096]{2,1,0:T(8,128)(2,1)S(1)} %bitcast.54, f32[1,4096]{1,0:T(1,128)S(1)} %bitcast.55), custom_call_target="tpu_custom_call" | custom-call | flops 9437184 | bytes 6291456 | tf_op jit(solution)/shard_map/pallas_call | solution.py:99
  21.0 2.1 %collective-permute-start.9 = (bf16[256,512]{1,0:T(8,128)(2,1)S(1)}, bf16[256,512]{1,0:T(8,128)(2,1)S(1)}, u32[]{:S(2)}, u32[]{:S(2)}) collective-permute-start(bf16[256,512]{1,0:T(8,128)(2,1)S(1)} %collective-permute-done.4), channel_id=1, source_target_pairs={{0,4},{4,8},{8,12},{12,14},{14,10},{10,6},{6,2},{2,0},{1,5},{5,9},... | collective-permute-start | bytes 786440 | tf_op jit(solution)/shard_map/ppermute | solution.py:32
  23.1 1.7 %collective-permute-done.7 = bf16[256,512]{1,0:T(8,128)(2,1)S(1)} collective-permute-done((bf16[256,512]{1,0:T(8,128)(2,1)S(1)}, bf16[256,512]{1,0:T(8,128)(2,1)S(1)}, u32[]{:S(2)}, u32[]{:S(2)}) %collective-permute-start.7) | collective-permute-done | bytes 262176 | tf_op jit(solution)/shard_map/ppermute | solution.py:32
  25.1 1.7 %collective-permute-start.12 = (bf16[256,512]{1,0:T(8,128)(2,1)S(1)}, bf16[256,512]{1,0:T(8,128)(2,1)S(1)}, u32[]{:S(2)}, u32[]{:S(2)}) collective-permute-start(bf16[256,512]{1,0:T(8,128)(2,1)S(1)} %collective-permute-done.8), channel_id=1, source_target_pairs={{0,2},{4,0},{8,4},{12,8},{14,12},{10,14},{6,10},{2,6},{1,3},{5,1},... | collective-permute-start | bytes 786440 | tf_op jit(solution)/shard_map/ppermute | solution.py:32
  26.8 3.6 %shard_map.65 = bf16[768,4096]{1,0:T(8,128)(2,1)S(1)} custom-call(bf16[3,128,4096]{2,1,0:T(8,128)(2,1)S(1)} %collective-permute-done.states_ref, f32[1,4096]{1,0:T(1,128)S(1)} %bitcast.56, bf16[768,4096]{1,0:T(8,128)(2,1)S(1)} %shard_map.64.refs_0_), custom_call_target="tpu_custom_call", output_to_operand_aliasing={{}: (2, {})} | custom-call | flops 9437184 | bytes 6291456 | tf_op jit(solution)/shard_map/pallas_call | solution.py:99
  33.9 1.7 %collective-permute-start.14 = (bf16[256,512]{1,0:T(8,128)(2,1)S(1)}, bf16[256,512]{1,0:T(8,128)(2,1)S(1)}, u32[]{:S(2)}, u32[]{:S(2)}) collective-permute-start(bf16[256,512]{1,0:T(8,128)(2,1)S(1)} %collective-permute-done.10), channel_id=1, source_target_pairs={{0,2},{4,0},{8,4},{12,8},{14,12},{10,14},{6,10},{2,6},{1,3},{5,1},... | collective-permute-start | bytes 786440 | tf_op jit(solution)/shard_map/ppermute | solution.py:32
  38.6 3.7 %collective-permute-done.14 = bf16[256,512]{1,0:T(8,128)(2,1)S(1)} collective-permute-done((bf16[256,512]{1,0:T(8,128)(2,1)S(1)}, bf16[256,512]{1,0:T(8,128)(2,1)S(1)}, u32[]{:S(2)}, u32[]{:S(2)}) %collective-permute-start.14) | collective-permute-done | bytes 262176 | tf_op jit(solution)/shard_map/ppermute | solution.py:32
  42.3 1.7 %collective-permute-start.16 = (bf16[256,512]{1,0:T(8,128)(2,1)S(1)}, bf16[256,512]{1,0:T(8,128)(2,1)S(1)}, u32[]{:S(2)}, u32[]{:S(2)}) collective-permute-start(bf16[256,512]{1,0:T(8,128)(2,1)S(1)} %collective-permute-done.14), channel_id=1, source_target_pairs={{0,2},{4,0},{8,4},{12,8},{14,12},{10,14},{6,10},{2,6},{1,3},{5,1},... | collective-permute-start | bytes 786440 | tf_op jit(solution)/shard_map/ppermute | solution.py:32
  44.8 3.1 %collective-permute-done.15 = bf16[256,512]{1,0:T(8,128)(2,1)S(1)} collective-permute-done((bf16[256,512]{1,0:T(8,128)(2,1)S(1)}, bf16[256,512]{1,0:T(8,128)(2,1)S(1)}, u32[]{:S(2)}, u32[]{:S(2)}) %collective-permute-start.15) | collective-permute-done | bytes 262176 | tf_op jit(solution)/shard_map/ppermute | solution.py:32
  48.3 1.7 %collective-permute-done.16 = bf16[256,512]{1,0:T(8,128)(2,1)S(1)} collective-permute-done((bf16[256,512]{1,0:T(8,128)(2,1)S(1)}, bf16[256,512]{1,0:T(8,128)(2,1)S(1)}, u32[]{:S(2)}, u32[]{:S(2)}) %collective-permute-start.16) | collective-permute-done | bytes 262176 | tf_op jit(solution)/shard_map/ppermute | solution.py:32
  54.1 1.3 %collective-permute-start.19 = (bf16[6,1024]{1,0:T(8,128)(2,1)S(1)}, bf16[6,1024]{1,0:T(8,128)(2,1)S(1)}, u32[]{:S(2)}, u32[]{:S(2)}) collective-permute-start(bf16[6,1024]{1,0:T(8,128)(2,1)S(1)} %maximum_select_fusion.2), channel_id=1, source_target_pairs={{20,0},{27,1},{24,4},{23,5},{28,8},{19,9},{30,12},{17,13},{26,14},... | collective-permute-start | bytes 36872 | tf_op jit(solution)/shard_map/ppermute | solution.py:64
  55.4 1.3 %collective-permute-start.20 = (bf16[6,1024]{1,0:T(8,128)(2,1)S(1)}, bf16[6,1024]{1,0:T(8,128)(2,1)S(1)}, u32[]{:S(2)}, u32[]{:S(2)}) collective-permute-start(bf16[6,1024]{1,0:T(8,128)(2,1)S(1)} %maximum_select_fusion.2), channel_id=1, source_target_pairs={{24,0},{23,1},{28,4},{19,5},{30,8},{17,9},{26,12},{21,13},{22,14},... | collective-permute-start | bytes 36872 | tf_op jit(solution)/shard_map/ppermute | solution.py:64
  58.4 2.6 %collective-permute-done.19 = bf16[6,1024]{1,0:T(8,128)(2,1)S(1)} collective-permute-done((bf16[6,1024]{1,0:T(8,128)(2,1)S(1)}, bf16[6,1024]{1,0:T(8,128)(2,1)S(1)}, u32[]{:S(2)}, u32[]{:S(2)}) %collective-permute-start.19) | collective-permute-done | bytes 12320 | tf_op jit(solution)/shard_map/ppermute | solution.py:64
  60.9 2.2 %collective-permute-done.20 = bf16[6,1024]{1,0:T(8,128)(2,1)S(1)} collective-permute-done((bf16[6,1024]{1,0:T(8,128)(2,1)S(1)}, bf16[6,1024]{1,0:T(8,128)(2,1)S(1)}, u32[]{:S(2)}, u32[]{:S(2)}) %collective-permute-start.20) | collective-permute-done | bytes 12320 | tf_op jit(solution)/shard_map/ppermute | solution.py:64
  63.2 2.3 %collective-permute-done.21 = bf16[6,1024]{1,0:T(8,128)(2,1)S(1)} collective-permute-done((bf16[6,1024]{1,0:T(8,128)(2,1)S(1)}, bf16[6,1024]{1,0:T(8,128)(2,1)S(1)}, u32[]{:S(2)}, u32[]{:S(2)}) %collective-permute-start.21) | collective-permute-done | bytes 12320 | tf_op jit(solution)/shard_map/ppermute | solution.py:64
  73.9 4.2 %collective-permute-done.25 = bf16[256,512]{1,0:T(8,128)(2,1)S(1)} collective-permute-done((bf16[256,512]{1,0:T(8,128)(2,1)S(1)}, bf16[256,512]{1,0:T(8,128)(2,1)S(1)}, u32[]{:S(2)}, u32[]{:S(2)}) %collective-permute-start.25) | collective-permute-done | bytes 262176 | tf_op jit(solution)/shard_map/ppermute | solution.py:32
  82.2 1.5 %collective-permute-done.27 = bf16[256,512]{1,0:T(8,128)(2,1)S(1)} collective-permute-done((bf16[256,512]{1,0:T(8,128)(2,1)S(1)}, bf16[256,512]{1,0:T(8,128)(2,1)S(1)}, u32[]{:S(2)}, u32[]{:S(2)}) %collective-permute-start.27) | collective-permute-done | bytes 262176 | tf_op jit(solution)/shard_map/ppermute | solution.py:32
  87.5 2.2 %collective-permute-start.24 = (bf16[256,1024]{1,0:T(8,128)(2,1)S(1)}, bf16[256,1024]{1,0:T(8,128)(2,1)S(1)}, u32[]{:S(2)}, u32[]{:S(2)}) collective-permute-start(bf16[256,1024]{1,0:T(8,128)(2,1)S(1)} %convert_element_type.163), channel_id=1, source_target_pairs={{0,16},{1,17},{2,18},{3,19},{4,20},{5,21},{6,22},{7,23},{8,24},{9,... | collective-permute-start | bytes 1572872 | tf_op jit(solution)/shard_map/ppermute | solution.py:40
  91.0 2.1 %collective-permute-start.33 = (bf16[256,512]{1,0:T(8,128)(2,1)S(1)}, bf16[256,512]{1,0:T(8,128)(2,1)S(1)}, u32[]{:S(2)}, u32[]{:S(2)}) collective-permute-start(bf16[256,512]{1,0:T(8,128)(2,1)S(1)} %fusion.9), channel_id=1, source_target_pairs={{0,2},{4,0},{8,4},{12,8},{14,12},{10,14},{6,10},{2,6},{1,3},{5,1},... | collective-permute-start | bytes 786440 | tf_op jit(solution)/shard_map/ppermute | solution.py:32
  93.1 3.1 %collective-permute-done.30 = bf16[256,512]{1,0:T(8,128)(2,1)S(1)} collective-permute-done((bf16[256,512]{1,0:T(8,128)(2,1)S(1)}, bf16[256,512]{1,0:T(8,128)(2,1)S(1)}, u32[]{:S(2)}, u32[]{:S(2)}) %collective-permute-start.30) | collective-permute-done | bytes 262176 | tf_op jit(solution)/shard_map/ppermute | solution.py:32
  98.0 1.8 %collective-permute-done.33 = bf16[256,512]{1,0:T(8,128)(2,1)S(1)} collective-permute-done((bf16[256,512]{1,0:T(8,128)(2,1)S(1)}, bf16[256,512]{1,0:T(8,128)(2,1)S(1)}, u32[]{:S(2)}, u32[]{:S(2)}) %collective-permute-start.33) | collective-permute-done | bytes 262176 | tf_op jit(solution)/shard_map/ppermute | solution.py:32
  99.8 2.5 %collective-permute-done.32 = bf16[256,512]{1,0:T(8,128)(2,1)S(1)} collective-permute-done((bf16[256,512]{1,0:T(8,128)(2,1)S(1)}, bf16[256,512]{1,0:T(8,128)(2,1)S(1)}, u32[]{:S(2)}, u32[]{:S(2)}) %collective-permute-start.32) | collective-permute-done | bytes 262176 | tf_op jit(solution)/shard_map/ppermute | solution.py:32
  103.2 1.6 %collective-permute-start.37 = (bf16[256,512]{1,0:T(8,128)(2,1)S(1)}, bf16[256,512]{1,0:T(8,128)(2,1)S(1)}, u32[]{:S(2)}, u32[]{:S(2)}) collective-permute-start(bf16[256,512]{1,0:T(8,128)(2,1)S(1)} %fusion.11), channel_id=1, source_target_pairs={{0,2},{4,0},{8,4},{12,8},{14,12},{10,14},{6,10},{2,6},{1,3},{5,1},... | collective-permute-start | bytes 786440 | tf_op jit(solution)/shard_map/ppermute | solution.py:32
  105.7 1.6 %collective-permute-start.35 = (bf16[256,512]{1,0:T(8,128)(2,1)S(1)}, bf16[256,512]{1,0:T(8,128)(2,1)S(1)}, u32[]{:S(2)}, u32[]{:S(2)}) collective-permute-start(bf16[256,512]{1,0:T(8,128)(2,1)S(1)} %fusion.10), channel_id=1, source_target_pairs={{0,2},{4,0},{8,4},{12,8},{14,12},{10,14},{6,10},{2,6},{1,3},{5,1},... | collective-permute-start | bytes 786440 | tf_op jit(solution)/shard_map/ppermute | solution.py:32
  107.7 3.3 %collective-permute-done.37 = bf16[256,512]{1,0:T(8,128)(2,1)S(1)} collective-permute-done((bf16[256,512]{1,0:T(8,128)(2,1)S(1)}, bf16[256,512]{1,0:T(8,128)(2,1)S(1)}, u32[]{:S(2)}, u32[]{:S(2)}) %collective-permute-start.37) | collective-permute-done | bytes 262176 | tf_op jit(solution)/shard_map/ppermute | solution.py:32
  111.3 2.6 %collective-permute-done.35 = bf16[256,512]{1,0:T(8,128)(2,1)S(1)} collective-permute-done((bf16[256,512]{1,0:T(8,128)(2,1)S(1)}, bf16[256,512]{1,0:T(8,128)(2,1)S(1)}, u32[]{:S(2)}, u32[]{:S(2)}) %collective-permute-start.35) | collective-permute-done | bytes 262176 | tf_op jit(solution)/shard_map/ppermute | solution.py:32
  (128 shorter events, 40.9 us)
Async XLA Ops:
  1.3 25.5 %collective-permute-start = (bf16[3,128,4096]{2,1,0:T(8,128)(2,1)}, bf16[3,128,4096]{2,1,0:T(8,128)(2,1)S(1)}, u32[]{:S(2)}, u32[]{:S(2)}) collective-permute-start(bf16[3,128,4096]{2,1,0:T(8,128)(2,1)} %bitcast.53), channel_id=1, source_target_pairs={{0,1},{1,0},{2,3},{3,2},{4,5},{5,4},{6,7},{7,6},{8,9},{9,8},{10,11... | collective-permute-start | bytes 9437192 | tf_op jit(solution)/shard_map/ppermute | solution.py:52
  1.9 9.5 %collective-permute-start.2 = (bf16[256,512]{1,0:T(8,128)(2,1)S(1)}, bf16[256,512]{1,0:T(8,128)(2,1)S(1)}, u32[]{:S(2)}, u32[]{:S(2)}) collective-permute-start(bf16[256,512]{1,0:T(8,128)(2,1)S(1)} %get-tuple-element.71), channel_id=1, source_target_pairs={{0,4},{4,8},{8,12},{12,14},{14,10},{10,6},{6,2},{2,0},{1,5},{5,9},... | collective-permute-start | bytes 786440 | tf_op jit(solution)/shard_map/ppermute | solution.py:32
  4.9 9.2 %collective-permute-start.3 = (bf16[256,512]{1,0:T(8,128)(2,1)S(1)}, bf16[256,512]{1,0:T(8,128)(2,1)S(1)}, u32[]{:S(2)}, u32[]{:S(2)}) collective-permute-start(bf16[256,512]{1,0:T(8,128)(2,1)S(1)} %get-tuple-element.71), channel_id=1, source_target_pairs={{0,2},{4,0},{8,4},{12,8},{14,12},{10,14},{6,10},{2,6},{1,3},{5,1},... | collective-permute-start | bytes 786440 | tf_op jit(solution)/shard_map/ppermute | solution.py:32
  7.4 13.6 %collective-permute-start.5 = (bf16[256,512]{1,0:T(8,128)(2,1)S(1)}, bf16[256,512]{1,0:T(8,128)(2,1)S(1)}, u32[]{:S(2)}, u32[]{:S(2)}) collective-permute-start(bf16[256,512]{1,0:T(8,128)(2,1)S(1)} %collective-permute-done.1), channel_id=1, source_target_pairs={{0,2},{4,0},{8,4},{12,8},{14,12},{10,14},{6,10},{2,6},{1,3},{5,1},... | collective-permute-start | bytes 786440 | tf_op jit(solution)/shard_map/ppermute | solution.py:32
  10.0 11.0 %collective-permute-start.4 = (bf16[256,512]{1,0:T(8,128)(2,1)S(1)}, bf16[256,512]{1,0:T(8,128)(2,1)S(1)}, u32[]{:S(2)}, u32[]{:S(2)}) collective-permute-start(bf16[256,512]{1,0:T(8,128)(2,1)S(1)} %collective-permute-done.1), channel_id=1, source_target_pairs={{0,4},{4,8},{8,12},{12,14},{14,10},{10,6},{6,2},{2,0},{1,5},{5,9},... | collective-permute-start | bytes 786440 | tf_op jit(solution)/shard_map/ppermute | solution.py:32
  11.4 13.4 %collective-permute-start.7 = (bf16[256,512]{1,0:T(8,128)(2,1)S(1)}, bf16[256,512]{1,0:T(8,128)(2,1)S(1)}, u32[]{:S(2)}, u32[]{:S(2)}) collective-permute-start(bf16[256,512]{1,0:T(8,128)(2,1)S(1)} %collective-permute-done.2), channel_id=1, source_target_pairs={{0,4},{4,8},{8,12},{12,14},{14,10},{10,6},{6,2},{2,0},{1,5},{5,9},... | collective-permute-start | bytes 786440 | tf_op jit(solution)/shard_map/ppermute | solution.py:32
  14.1 11.0 %collective-permute-start.8 = (bf16[256,512]{1,0:T(8,128)(2,1)S(1)}, bf16[256,512]{1,0:T(8,128)(2,1)S(1)}, u32[]{:S(2)}, u32[]{:S(2)}) collective-permute-start(bf16[256,512]{1,0:T(8,128)(2,1)S(1)} %collective-permute-done.3), channel_id=1, source_target_pairs={{0,2},{4,0},{8,4},{12,8},{14,12},{10,14},{6,10},{2,6},{1,3},{5,1},... | collective-permute-start | bytes 786440 | tf_op jit(solution)/shard_map/ppermute | solution.py:32
  21.0 12.6 %collective-permute-start.9 = (bf16[256,512]{1,0:T(8,128)(2,1)S(1)}, bf16[256,512]{1,0:T(8,128)(2,1)S(1)}, u32[]{:S(2)}, u32[]{:S(2)}) collective-permute-start(bf16[256,512]{1,0:T(8,128)(2,1)S(1)} %collective-permute-done.4), channel_id=1, source_target_pairs={{0,4},{4,8},{8,12},{12,14},{14,10},{10,6},{6,2},{2,0},{1,5},{5,9},... | collective-permute-start | bytes 786440 | tf_op jit(solution)/shard_map/ppermute | solution.py:32
  23.1 10.9 %collective-permute-start.10 = (bf16[256,512]{1,0:T(8,128)(2,1)S(1)}, bf16[256,512]{1,0:T(8,128)(2,1)S(1)}, u32[]{:S(2)}, u32[]{:S(2)}) collective-permute-start(bf16[256,512]{1,0:T(8,128)(2,1)S(1)} %collective-permute-done.5), channel_id=1, source_target_pairs={{0,2},{4,0},{8,4},{12,8},{14,12},{10,14},{6,10},{2,6},{1,3},{5,1},... | collective-permute-start | bytes 786440 | tf_op jit(solution)/shard_map/ppermute | solution.py:32
  24.8 10.9 %collective-permute-start.11 = (bf16[256,512]{1,0:T(8,128)(2,1)S(1)}, bf16[256,512]{1,0:T(8,128)(2,1)S(1)}, u32[]{:S(2)}, u32[]{:S(2)}) collective-permute-start(bf16[256,512]{1,0:T(8,128)(2,1)S(1)} %collective-permute-done.7), channel_id=1, source_target_pairs={{0,4},{4,8},{8,12},{12,14},{14,10},{10,6},{6,2},{2,0},{1,5},{5,9},... | collective-permute-start | bytes 786440 | tf_op jit(solution)/shard_map/ppermute | solution.py:32
  25.1 25.2 %collective-permute-start.12 = (bf16[256,512]{1,0:T(8,128)(2,1)S(1)}, bf16[256,512]{1,0:T(8,128)(2,1)S(1)}, u32[]{:S(2)}, u32[]{:S(2)}) collective-permute-start(bf16[256,512]{1,0:T(8,128)(2,1)S(1)} %collective-permute-done.8), channel_id=1, source_target_pairs={{0,2},{4,0},{8,4},{12,8},{14,12},{10,14},{6,10},{2,6},{1,3},{5,1},... | collective-permute-start | bytes 786440 | tf_op jit(solution)/shard_map/ppermute | solution.py:32
  33.6 10.8 %collective-permute-start.13 = (bf16[256,512]{1,0:T(8,128)(2,1)S(1)}, bf16[256,512]{1,0:T(8,128)(2,1)S(1)}, u32[]{:S(2)}, u32[]{:S(2)}) collective-permute-start(bf16[256,512]{1,0:T(8,128)(2,1)S(1)} %collective-permute-done.9), channel_id=1, source_target_pairs={{0,4},{4,8},{8,12},{12,14},{14,10},{10,6},{6,2},{2,0},{1,5},{5,9},... | collective-permute-start | bytes 786440 | tf_op jit(solution)/shard_map/ppermute | solution.py:32
  33.9 8.4 %collective-permute-start.14 = (bf16[256,512]{1,0:T(8,128)(2,1)S(1)}, bf16[256,512]{1,0:T(8,128)(2,1)S(1)}, u32[]{:S(2)}, u32[]{:S(2)}) collective-permute-start(bf16[256,512]{1,0:T(8,128)(2,1)S(1)} %collective-permute-done.10), channel_id=1, source_target_pairs={{0,2},{4,0},{8,4},{12,8},{14,12},{10,14},{6,10},{2,6},{1,3},{5,1},... | collective-permute-start | bytes 786440 | tf_op jit(solution)/shard_map/ppermute | solution.py:32
  35.7 12.2 %collective-permute-start.15 = (bf16[256,512]{1,0:T(8,128)(2,1)S(1)}, bf16[256,512]{1,0:T(8,128)(2,1)S(1)}, u32[]{:S(2)}, u32[]{:S(2)}) collective-permute-start(bf16[256,512]{1,0:T(8,128)(2,1)S(1)} %collective-permute-done.11), channel_id=1, source_target_pairs={{0,4},{4,8},{8,12},{12,14},{14,10},{10,6},{6,2},{2,0},{1,5},{5,9},... | collective-permute-start | bytes 786440 | tf_op jit(solution)/shard_map/ppermute | solution.py:32
  42.3 7.6 %collective-permute-start.16 = (bf16[256,512]{1,0:T(8,128)(2,1)S(1)}, bf16[256,512]{1,0:T(8,128)(2,1)S(1)}, u32[]{:S(2)}, u32[]{:S(2)}) collective-permute-start(bf16[256,512]{1,0:T(8,128)(2,1)S(1)} %collective-permute-done.14), channel_id=1, source_target_pairs={{0,2},{4,0},{8,4},{12,8},{14,12},{10,14},{6,10},{2,6},{1,3},{5,1},... | collective-permute-start | bytes 786440 | tf_op jit(solution)/shard_map/ppermute | solution.py:32
  54.1 6.9 %collective-permute-start.19 = (bf16[6,1024]{1,0:T(8,128)(2,1)S(1)}, bf16[6,1024]{1,0:T(8,128)(2,1)S(1)}, u32[]{:S(2)}, u32[]{:S(2)}) collective-permute-start(bf16[6,1024]{1,0:T(8,128)(2,1)S(1)} %maximum_select_fusion.2), channel_id=1, source_target_pairs={{20,0},{27,1},{24,4},{23,5},{28,8},{19,9},{30,12},{17,13},{26,14},... | collective-permute-start | bytes 36872 | tf_op jit(solution)/shard_map/ppermute | solution.py:64
  55.4 7.8 %collective-permute-start.20 = (bf16[6,1024]{1,0:T(8,128)(2,1)S(1)}, bf16[6,1024]{1,0:T(8,128)(2,1)S(1)}, u32[]{:S(2)}, u32[]{:S(2)}) collective-permute-start(bf16[6,1024]{1,0:T(8,128)(2,1)S(1)} %maximum_select_fusion.2), channel_id=1, source_target_pairs={{24,0},{23,1},{28,4},{19,5},{30,8},{17,9},{26,12},{21,13},{22,14},... | collective-permute-start | bytes 36872 | tf_op jit(solution)/shard_map/ppermute | solution.py:64
  56.7 8.8 %collective-permute-start.21 = (bf16[6,1024]{1,0:T(8,128)(2,1)S(1)}, bf16[6,1024]{1,0:T(8,128)(2,1)S(1)}, u32[]{:S(2)}, u32[]{:S(2)}) collective-permute-start(bf16[6,1024]{1,0:T(8,128)(2,1)S(1)} %maximum_select_fusion.2), channel_id=1, source_target_pairs={{28,0},{19,1},{30,4},{17,5},{26,8},{21,9},{22,12},{25,13},{18,14},... | collective-permute-start | bytes 36872 | tf_op jit(solution)/shard_map/ppermute | solution.py:64
  68.9 9.2 %collective-permute-start.25 = (bf16[256,512]{1,0:T(8,128)(2,1)S(1)}, bf16[256,512]{1,0:T(8,128)(2,1)S(1)}, u32[]{:S(2)}, u32[]{:S(2)}) collective-permute-start(bf16[256,512]{1,0:T(8,128)(2,1)S(1)} %convolution_convert_fusion.2), channel_id=1, source_target_pairs={{0,2},{4,0},{8,4},{12,8},{14,12},{10,14},{6,10},{2,6},{1,3},{5,1},... | collective-permute-start | bytes 786440 | tf_op jit(solution)/shard_map/ppermute | solution.py:32
  70.1 9.2 %collective-permute-start.23 = (bf16[256,512]{1,0:T(8,128)(2,1)S(1)}, bf16[256,512]{1,0:T(8,128)(2,1)S(1)}, u32[]{:S(2)}, u32[]{:S(2)}) collective-permute-start(bf16[256,512]{1,0:T(8,128)(2,1)S(1)} %convolution_convert_fusion.3), channel_id=1, source_target_pairs={{0,4},{4,8},{8,12},{12,14},{14,10},{10,6},{6,2},{2,0},{1,5},{5,9},... | collective-permute-start | bytes 786440 | tf_op jit(solution)/shard_map/ppermute | solution.py:32
  71.4 12.3 %collective-permute-start.27 = (bf16[256,512]{1,0:T(8,128)(2,1)S(1)}, bf16[256,512]{1,0:T(8,128)(2,1)S(1)}, u32[]{:S(2)}, u32[]{:S(2)}) collective-permute-start(bf16[256,512]{1,0:T(8,128)(2,1)S(1)} %convolution_convert_fusion), channel_id=1, source_target_pairs={{0,2},{4,0},{8,4},{12,8},{14,12},{10,14},{6,10},{2,6},{1,3},{5,1},... | collective-permute-start | bytes 786440 | tf_op jit(solution)/shard_map/ppermute | solution.py:32
  73.0 11.9 %collective-permute-start.26 = (bf16[256,512]{1,0:T(8,128)(2,1)S(1)}, bf16[256,512]{1,0:T(8,128)(2,1)S(1)}, u32[]{:S(2)}, u32[]{:S(2)}) collective-permute-start(bf16[256,512]{1,0:T(8,128)(2,1)S(1)} %convolution_convert_fusion.1), channel_id=1, source_target_pairs={{0,4},{4,8},{8,12},{12,14},{14,10},{10,6},{6,2},{2,0},{1,5},{5,9},... | collective-permute-start | bytes 786440 | tf_op jit(solution)/shard_map/ppermute | solution.py:32
  80.2 9.6 %collective-permute-start.29 = (bf16[256,512]{1,0:T(8,128)(2,1)S(1)}, bf16[256,512]{1,0:T(8,128)(2,1)S(1)}, u32[]{:S(2)}, u32[]{:S(2)}) collective-permute-start(bf16[256,512]{1,0:T(8,128)(2,1)S(1)} %fusion.7), channel_id=1, source_target_pairs={{0,2},{4,0},{8,4},{12,8},{14,12},{10,14},{6,10},{2,6},{1,3},{5,1},... | collective-permute-start | bytes 786440 | tf_op jit(solution)/shard_map/ppermute | solution.py:32
  81.3 9.2 %collective-permute-start.28 = (bf16[256,512]{1,0:T(8,128)(2,1)S(1)}, bf16[256,512]{1,0:T(8,128)(2,1)S(1)}, u32[]{:S(2)}, u32[]{:S(2)}) collective-permute-start(bf16[256,512]{1,0:T(8,128)(2,1)S(1)} %fusion.6), channel_id=1, source_target_pairs={{0,4},{4,8},{8,12},{12,14},{14,10},{10,6},{6,2},{2,0},{1,5},{5,9},... | collective-permute-start | bytes 786440 | tf_op jit(solution)/shard_map/ppermute | solution.py:32
  85.3 10.8 %collective-permute-start.30 = (bf16[256,512]{1,0:T(8,128)(2,1)S(1)}, bf16[256,512]{1,0:T(8,128)(2,1)S(1)}, u32[]{:S(2)}, u32[]{:S(2)}) collective-permute-start(bf16[256,512]{1,0:T(8,128)(2,1)S(1)} %fusion.5), channel_id=1, source_target_pairs={{0,4},{4,8},{8,12},{12,14},{14,10},{10,6},{6,2},{2,0},{1,5},{5,9},... | collective-permute-start | bytes 786440 | tf_op jit(solution)/shard_map/ppermute | solution.py:32
  86.3 11.3 %collective-permute-start.31 = (bf16[256,512]{1,0:T(8,128)(2,1)S(1)}, bf16[256,512]{1,0:T(8,128)(2,1)S(1)}, u32[]{:S(2)}, u32[]{:S(2)}) collective-permute-start(bf16[256,512]{1,0:T(8,128)(2,1)S(1)} %fusion.8), channel_id=1, source_target_pairs={{0,2},{4,0},{8,4},{12,8},{14,12},{10,14},{6,10},{2,6},{1,3},{5,1},... | collective-permute-start | bytes 786440 | tf_op jit(solution)/shard_map/ppermute | solution.py:32
  87.5 15.7 %collective-permute-start.24 = (bf16[256,1024]{1,0:T(8,128)(2,1)S(1)}, bf16[256,1024]{1,0:T(8,128)(2,1)S(1)}, u32[]{:S(2)}, u32[]{:S(2)}) collective-permute-start(bf16[256,1024]{1,0:T(8,128)(2,1)S(1)} %convert_element_type.163), channel_id=1, source_target_pairs={{0,16},{1,17},{2,18},{3,19},{4,20},{5,21},{6,22},{7,23},{8,24},{9,... | collective-permute-start | bytes 1572872 | tf_op jit(solution)/shard_map/ppermute | solution.py:40
  91.0 8.8 %collective-permute-start.33 = (bf16[256,512]{1,0:T(8,128)(2,1)S(1)}, bf16[256,512]{1,0:T(8,128)(2,1)S(1)}, u32[]{:S(2)}, u32[]{:S(2)}) collective-permute-start(bf16[256,512]{1,0:T(8,128)(2,1)S(1)} %fusion.9), channel_id=1, source_target_pairs={{0,2},{4,0},{8,4},{12,8},{14,12},{10,14},{6,10},{2,6},{1,3},{5,1},... | collective-permute-start | bytes 786440 | tf_op jit(solution)/shard_map/ppermute | solution.py:32
  93.1 9.2 %collective-permute-start.32 = (bf16[256,512]{1,0:T(8,128)(2,1)S(1)}, bf16[256,512]{1,0:T(8,128)(2,1)S(1)}, u32[]{:S(2)}, u32[]{:S(2)}) collective-permute-start(bf16[256,512]{1,0:T(8,128)(2,1)S(1)} %fusion.4), channel_id=1, source_target_pairs={{0,4},{4,8},{8,12},{12,14},{14,10},{10,6},{6,2},{2,0},{1,5},{5,9},... | collective-permute-start | bytes 786440 | tf_op jit(solution)/shard_map/ppermute | solution.py:32
  96.6 10.7 %collective-permute-start.36 = (bf16[256,512]{1,0:T(8,128)(2,1)S(1)}, bf16[256,512]{1,0:T(8,128)(2,1)S(1)}, u32[]{:S(2)}, u32[]{:S(2)}) collective-permute-start(bf16[256,512]{1,0:T(8,128)(2,1)S(1)} %fusion.3), channel_id=1, source_target_pairs={{0,4},{4,8},{8,12},{12,14},{14,10},{10,6},{6,2},{2,0},{1,5},{5,9},... | collective-permute-start | bytes 786440 | tf_op jit(solution)/shard_map/ppermute | solution.py:32
  103.2 7.9 %collective-permute-start.37 = (bf16[256,512]{1,0:T(8,128)(2,1)S(1)}, bf16[256,512]{1,0:T(8,128)(2,1)S(1)}, u32[]{:S(2)}, u32[]{:S(2)}) collective-permute-start(bf16[256,512]{1,0:T(8,128)(2,1)S(1)} %fusion.11), channel_id=1, source_target_pairs={{0,2},{4,0},{8,4},{12,8},{14,12},{10,14},{6,10},{2,6},{1,3},{5,1},... | collective-permute-start | bytes 786440 | tf_op jit(solution)/shard_map/ppermute | solution.py:32
  105.7 8.2 %collective-permute-start.35 = (bf16[256,512]{1,0:T(8,128)(2,1)S(1)}, bf16[256,512]{1,0:T(8,128)(2,1)S(1)}, u32[]{:S(2)}, u32[]{:S(2)}) collective-permute-start(bf16[256,512]{1,0:T(8,128)(2,1)S(1)} %fusion.10), channel_id=1, source_target_pairs={{0,2},{4,0},{8,4},{12,8},{14,12},{10,14},{6,10},{2,6},{1,3},{5,1},... | collective-permute-start | bytes 786440 | tf_op jit(solution)/shard_map/ppermute | solution.py:32
  (12 other events, 39.4 us)
